TPU v7x, 32 devices: a whole 2x2x4 slice. The times are simulated.
32 devices in a mesh: seq: 8 (over z, y), chan: 4 (over x, core).
Axes of the slice: x: 2, y: 2, z: 4, core: 2. Of those that a mesh axis runs over, the one named last changes fastest.
Arguments:
- query_proj: bfloat16 [2048, 4096], P('seq', 'chan'), may hold values from -6 to 6
- key_proj: bfloat16 [2048, 4096], P('seq', 'chan'), may hold values from -6 to 6
- value_proj: bfloat16 [2048, 4096], P('seq', 'chan'), may hold values from -6 to 6
- out_grad: bfloat16 [2048, 4096], P('seq', 'chan'), may hold values from -6 to 6
- residues: float32 [256, 16], replicated, may hold values from -2.1 to 2.1
- decay_rate: float32 [256, 16], replicated, as said below
- skip_gain: float32 [4096], P('chan'), may hold values from -3 to 3
Outputs:
- layer_out: bfloat16 [2048, 4096], P('seq', 'chan')
- key_grad: bfloat16 [2048, 4096], P('seq', 'chan')
- value_grad: bfloat16 [2048, 4096], P('seq', 'chan')
- filter_grad: float32 [2048, 256], P('seq', 'chan')
Inputs may be any that keep to these rules, and one draw needn't show every extreme that they name: `decay_rate`: every rate is positive.
All inputs are finite; a program needn't handle non-finite values.
Results may differ from a plain program's by a relative error of at most 0.022.
Values may be sent and summed in bfloat16 or wider, within the bound.
No kernel may reach another device: no remote copies, remote signals or barrier semaphores. Data moves between devices by JAX's collectives and lax.ppermute only.
A program may use at most 192 MiB of HBM per device.

v0:
```python
import functools
import math

import jax
import jax.numpy as jnp
from jax import lax
from jax.experimental import pallas as pl
from jax.experimental.pallas import tpu as pltpu
from jax.sharding import PartitionSpec as P

CHANNELS = 4096
FILTERS = 256
LANES = 128
SUBLANES = 8
VMEM_BYTES = 48 * 1024 * 1024
F32 = jnp.float32
BF16 = jnp.bfloat16


def product(first, second):
    return (first.astype(F32) * second.astype(F32)).astype(BF16)


def one_hot(rows, cols, column_of):
    row = lax.broadcasted_iota(jnp.int32, (rows, cols), 0)
    col = lax.broadcasted_iota(jnp.int32, (rows, cols), 1)
    return (col == column_of(row)).astype(F32).astype(BF16)


def pack_kernel(shards, chans, owned, q_ref, k_ref, v_ref, o_ref, send_ref):
    per_chan = FILTERS // chans

    def owned_filter(row):
        seq = row // (chans * owned)
        chan = row // owned % chans
        return chan * per_chan + seq * owned + row % owned

    order = one_hot(FILTERS, FILTERS, owned_filter)
    width = k_ref.shape[1]
    groups = width // FILTERS
    for which, (a_ref, b_ref) in enumerate(((k_ref, v_ref), (o_ref, q_ref))):
        signal = product(a_ref[...], b_ref[...])
        parts = []
        for group in range(groups):
            part = lax.dot_general(
                order,
                signal[:, group * FILTERS : (group + 1) * FILTERS],
                (((1,), (1,)), ((), ())),
                preferred_element_type=F32,
            )
            if owned % SUBLANES:
                send_ref[which, group] = part.astype(BF16)
            else:
                parts.append(part.reshape(shards * chans, owned, part.shape[1]))
        if parts:
            rows = groups * owned
            send_ref[:, which * rows : (which + 1) * rows, :] = jnp.concatenate(
                parts, axis=1
            ).astype(BF16)


def pack_signals(shards, chans, owned, query_proj, key_proj, value_proj, out_grad):
    tok_rows, width = key_proj.shape
    groups = width // FILTERS
    dests = shards * chans
    steps = tok_rows // LANES
    block = pl.BlockSpec((LANES, width), lambda i: (i, 0))
    if owned % SUBLANES:
        shape = (2, groups, FILTERS, tok_rows)
        out_spec = pl.BlockSpec((2, groups, FILTERS, LANES), lambda i: (0, 0, 0, i))
    else:
        shape = (dests, 2 * groups * owned, tok_rows)
        out_spec = pl.BlockSpec((dests, 2 * groups * owned, LANES), lambda i: (0, 0, i))
    send = pl.pallas_call(
        functools.partial(pack_kernel, shards, chans, owned),
        grid=(steps,),
        in_specs=[block] * 4,
        out_specs=out_spec,
        out_shape=jax.ShapeDtypeStruct(shape, BF16),
        compiler_params=pltpu.CompilerParams(vmem_limit_bytes=VMEM_BYTES),
        name="pack_signals",
    )(query_proj, key_proj, value_proj, out_grad)
    if owned % SUBLANES:
        send = send.reshape(2, groups, dests, owned, tok_rows)
        send = send.transpose(2, 0, 1, 3, 4).reshape(dests, 2 * groups * owned, tok_rows)
    return send


def state_kernel(q_ref, k_ref, v_ref, o_ref, coef_ref, state_ref, x_ref, g_ref):
    tok_rows, width = k_ref.shape
    tiles = width // LANES
    modes = coef_ref.shape[1]
    spread_tokens(k_ref, v_ref, x_ref)
    spread_tokens(o_ref, q_ref, g_ref)

    def step(t, carry):
        x = x_ref[pl.ds(t, tiles, stride=tok_rows), :]
        g = g_ref[pl.ds(tok_rows - 1 - t, tiles, stride=tok_rows), :]
        ahead = tuple(coef_ref[0, m] * carry[0][m] + x for m in range(modes))
        behind = tuple(coef_ref[0, m] * carry[1][m] + g for m in range(modes))
        return (ahead, behind)

    zero = tuple(jnp.zeros((tiles, LANES), F32) for _ in range(modes))
    ahead, behind = lax.fori_loop(0, tok_rows, step, (zero, zero), unroll=8)
    for m in range(modes):
        state_ref[0, m] = ahead[m]
        state_ref[1, m] = behind[m]


def spread_tokens(a_ref, b_ref, x_ref):
    tok_rows, width = a_ref.shape
    for tile in range(width // LANES):
        cols = slice(tile * LANES, (tile + 1) * LANES)
        x_ref[tile * tok_rows : (tile + 1) * tok_rows, :] = product(
            a_ref[:, cols], b_ref[:, cols]
        ).astype(F32)


def block_states(query_proj, key_proj, value_proj, out_grad, coefs):
    tok_rows, width = key_proj.shape
    tiles = width // LANES
    modes = coefs.shape[1]
    return pl.pallas_call(
        state_kernel,
        out_shape=jax.ShapeDtypeStruct((2, modes, tiles, LANES), F32),
        scratch_shapes=[pltpu.VMEM((tok_rows * tiles, LANES), F32)] * 2,
        compiler_params=pltpu.CompilerParams(vmem_limit_bytes=VMEM_BYTES),
        cost_estimate=pl.CostEstimate(
            flops=4 * modes * tok_rows * width, bytes_accessed=8 * tok_rows * width, transcendentals=0
        ),
        name="block_states",
    )(query_proj, key_proj, value_proj, out_grad, coefs)


def output_kernel(
    seq_ref, q_ref, k_ref, v_ref, o_ref, coef_ref, gain_ref, all_ref,
    layer_ref, key_ref, value_ref, x_ref, g_ref,
):
    tok_rows, width = k_ref.shape
    tiles = width // LANES
    modes = coef_ref.shape[1]
    shards = all_ref.shape[0]
    seq = seq_ref[0]
    spread_tokens(k_ref, v_ref, x_ref)
    spread_tokens(o_ref, q_ref, g_ref)
    zero = tuple(jnp.zeros((tiles, LANES), F32) for _ in range(modes))

    def join_ahead(s, held):
        return tuple(coef_ref[1, m] * held[m] + all_ref[s, 0, m] for m in range(modes))

    def join_behind(i, held):
        s = shards - 1 - i
        return tuple(coef_ref[1, m] * held[m] + all_ref[s, 1, m] for m in range(modes))

    def total(held):
        terms = [coef_ref[2, m] * held[m] for m in range(modes)]
        while len(terms) > 1:
            terms = [sum(terms[i : i + 2][1:], terms[i]) for i in range(0, len(terms), 2)]
        return terms[0]

    def walk(ref, start, move):
        def step(t, held):
            rows = pl.ds(start + move * t, tiles, stride=tok_rows)
            x = ref[rows, :]
            held = tuple(coef_ref[0, m] * held[m] + x for m in range(modes))
            ref[rows, :] = total(held)
            return held

        return step

    held = lax.fori_loop(0, seq, join_ahead, zero)
    lax.fori_loop(0, tok_rows, walk(x_ref, 0, 1), held, unroll=8)
    held = lax.fori_loop(0, shards - 1 - seq, join_behind, zero)
    lax.fori_loop(0, tok_rows, walk(g_ref, tok_rows - 1, -1), held, unroll=8)
    for tile in range(tiles):
        cols = slice(tile * LANES, (tile + 1) * LANES)
        rows = slice(tile * tok_rows, (tile + 1) * tok_rows)
        q = q_ref[:, cols].astype(F32)
        k = k_ref[:, cols].astype(F32)
        v = v_ref[:, cols].astype(F32)
        gain = gain_ref[:, cols]
        conv_in = (k * v).astype(BF16).astype(F32)
        mid_grad = (o_ref[:, cols].astype(F32) * q).astype(BF16).astype(F32)
        layer_ref[:, cols] = (q * (x_ref[rows, :] + gain * conv_in)).astype(BF16)
        conv_grad = g_ref[rows, :] + gain * mid_grad
        key_ref[:, cols] = (conv_grad * v).astype(BF16)
        value_ref[:, cols] = (conv_grad * k).astype(BF16)


def local_outputs(seq_index, query_proj, key_proj, value_proj, out_grad, coefs, gain, states):
    tok_rows, width = key_proj.shape
    tiles = width // LANES
    modes = coefs.shape[1]
    whole = pl.BlockSpec(memory_space=pltpu.VMEM)
    return pl.pallas_call(
        output_kernel,
        in_specs=[pl.BlockSpec(memory_space=pltpu.SMEM)] + [whole] * 7,
        out_specs=[whole] * 3,
        out_shape=[jax.ShapeDtypeStruct((tok_rows, width), BF16)] * 3,
        scratch_shapes=[pltpu.VMEM((tok_rows * tiles, LANES), F32)] * 2,
        compiler_params=pltpu.CompilerParams(vmem_limit_bytes=VMEM_BYTES),
        cost_estimate=pl.CostEstimate(
            flops=8 * modes * tok_rows * width, bytes_accessed=14 * tok_rows * width, transcendentals=0
        ),
        name="local_outputs",
    )(seq_index.reshape(1), query_proj, key_proj, value_proj, out_grad, coefs, gain, states)


def lag_kernel(shards, chans, groups, owned, scale, *refs):
    in_refs, out_ref, u_all, g_all = refs[:-3], refs[-3], refs[-2], refs[-1]
    tok_rows = out_ref.shape[2]
    halves = tok_rows // LANES
    blocks = shards * halves
    depth = chans * groups
    full = blocks * depth
    if len(in_refs) == 1:
        take = chans * groups * owned

        def by_filter(row):
            return row % depth * owned + row // depth

        order = one_hot(take, take, by_filter)
        for which, kept in enumerate((u_all, g_all)):
            rows = slice(which * groups * owned, (which + 1) * groups * owned)
            for s in range(shards):
                piece = in_refs[0][s * chans : (s + 1) * chans, rows, :].reshape(take, tok_rows)
                piece = jnp.dot(order, piece, preferred_element_type=F32).astype(BF16)
                piece = piece.reshape(owned, depth, tok_rows)
                for h in range(halves):
                    first = (s * halves + h) * depth
                    kept[:, first : first + depth, :] = piece[:, :, h * LANES : (h + 1) * LANES]
    else:
        u_all[...] = in_refs[0][...]
        g_all[:, :full, :] = in_refs[1][...]
    g_all[:, full:, :] = jnp.zeros((owned, g_all.shape[1] - full, LANES), BF16)
    mirror = one_hot(LANES, LANES, lambda row: LANES - 1 - row)
    row = lax.broadcasted_iota(jnp.int32, (LANES, LANES), 0)
    col = lax.broadcasted_iota(jnp.int32, (LANES, LANES), 1)
    same_block = row + col >= LANES - 1
    filter_row = lax.broadcasted_iota(jnp.int32, (owned, LANES), 0)
    batch = min(blocks, 16)

    def one_filter(f, _):
        turned = lax.dot_general(
            mirror, u_all[f], (((1,), (1,)), ((), ())), preferred_element_type=F32
        ).astype(BF16)

        def some_lags(first):
            tables = []
            for d in range(0, batch, 2):
                pair = jnp.concatenate(
                    [
                        g_all[f, pl.ds(pl.multiple_of((first + d + e) * depth, depth), full), :]
                        for e in range(2)
                    ],
                    axis=1,
                )
                table = jnp.dot(turned, pair, preferred_element_type=F32)
                tables += [table[:, :LANES], table[:, LANES:]]
            last = g_all[f, pl.ds(pl.multiple_of((first + batch) * depth, depth), full), :]
            if batch < blocks:
                tables.append(jnp.dot(turned, last, preferred_element_type=F32))
            else:
                tables.append(jnp.zeros((LANES, LANES), F32))
            for d in range(batch):
                joined = jnp.where(same_block, tables[d], tables[d + 1])
                skewed = pltpu.roll(joined, 1, 1, stride=1, stride_axis=0)
                sums = jnp.sum(skewed, axis=0, keepdims=True) * scale
                lane = d % halves * LANES
                place = ((first + d) // halves, slice(None), slice(lane, lane + LANES))
                out_ref[place] = jnp.where(filter_row == f, sums, out_ref[place])

        if batch == blocks:
            some_lags(0)
        else:
            lax.fori_loop(0, blocks // batch, lambda i, c: (some_lags(i * batch), c)[1], 0)
        return 0

    lax.fori_loop(0, owned, one_filter, 0)


def filter_lags(received, shards, chans, owned, scale):
    tok_rows = received.shape[2]
    groups = received.shape[1] // (2 * owned)
    halves = tok_rows // LANES
    depth = chans * groups
    full = shards * halves * depth
    args = (received,)
    if owned % SUBLANES:
        split = received.reshape(shards, chans, 2, groups, owned, halves, LANES)
        split = split.transpose(2, 4, 0, 5, 1, 3, 6).reshape(2, owned, full, LANES)
        args = (split[0], split[1])
    return pl.pallas_call(
        functools.partial(lag_kernel, shards, chans, groups, owned, scale),
        out_shape=jax.ShapeDtypeStruct((shards, owned, tok_rows), F32),
        scratch_shapes=[
            pltpu.VMEM((owned, full, LANES), BF16),
            pltpu.VMEM((owned, 2 * full + depth, LANES), BF16),
        ],
        compiler_params=pltpu.CompilerParams(vmem_limit_bytes=VMEM_BYTES),
        name="filter_lags",
    )(*args)


def per_device(query_proj, key_proj, value_proj, out_grad, residues, decay_rate, skip_gain):
    tok_rows, width = key_proj.shape
    shards = lax.axis_size("seq")
    chans = lax.axis_size("chan")
    seq_index = lax.axis_index("seq")
    length = shards * tok_rows
    owned = FILTERS // (shards * chans)
    modes = residues.shape[1]
    signals = (query_proj, key_proj, value_proj, out_grad)

    send = pack_signals(shards, chans, owned, *signals)
    received = lax.all_to_all(send, ("seq", "chan"), split_axis=0, concat_axis=0, tiled=True)

    coefs = jnp.stack(
        [
            jnp.exp(-decay_rate),
            jnp.exp(-(decay_rate * float(tok_rows))),
            residues * jnp.sqrt(decay_rate),
        ]
    )
    coefs = coefs.transpose(0, 2, 1).reshape(3, modes, 1, FILTERS // LANES, LANES)
    coefs = jnp.broadcast_to(coefs, (3, modes, width // FILTERS, FILTERS // LANES, LANES))
    coefs = coefs.reshape(3, modes, width // LANES, LANES)
    states = block_states(*signals, coefs)
    states = lax.all_gather(states, "seq", axis=0)
    layer_out, key_grad, value_grad = local_outputs(
        seq_index, *signals, coefs, skip_gain[None, :], states
    )

    scale = 1.0 / math.sqrt(length * (CHANNELS // FILTERS))
    lags = filter_lags(received, shards, chans, owned, scale)
    lags = lax.all_to_all(lags, "seq", split_axis=0, concat_axis=0, tiled=True)
    filter_grad = lags.reshape(shards * owned, tok_rows).T
    return (layer_out, key_grad, value_grad, filter_grad)


def solution(mesh):
    split = P("seq", "chan")
    return jax.shard_map(
        per_device,
        mesh=mesh,
        in_specs=(split, split, split, split, P(), P(), P("chan")),
        out_specs=(split, split, split, split),
        check_vma=False,
    )
```

profile of v0, /device:TPU:0, one launch (start us, length us, event | category | flops | bytes accessed | tf_op | source)
XLA Modules:
  0.0 89.9 jit_solution(12434390936740752293)
XLA Ops:
  7.2 0.0 copy-start
  7.2 1.0 %copy-done = bf16[256,1024]{1,0:T(8,128)(2,1)S(1)} copy-done((bf16[256,1024]{1,0:T(8,128)(2,1)S(1)}, bf16[256,1024]{1,0:T(8,128)(2,1)}, u32[]{:S(2)}) %copy-start) | copy-done | bytes 524312
  8.2 0.0 copy-start.2
  8.2 1.0 %copy-done.2 = bf16[256,1024]{1,0:T(8,128)(2,1)S(1)} copy-done((bf16[256,1024]{1,0:T(8,128)(2,1)S(1)}, bf16[256,1024]{1,0:T(8,128)(2,1)}, u32[]{:S(2)}) %copy-start.2) | copy-done | bytes 524312
  9.3 0.0 copy-start.4
  9.3 1.0 %copy-done.4 = bf16[256,1024]{1,0:T(8,128)(2,1)S(1)} copy-done((bf16[256,1024]{1,0:T(8,128)(2,1)S(1)}, bf16[256,1024]{1,0:T(8,128)(2,1)}, u32[]{:S(2)}) %copy-start.4) | copy-done | bytes 524312
  10.3 0.0 copy-start.6
  10.3 1.0 %copy-done.6 = bf16[256,1024]{1,0:T(8,128)(2,1)S(1)} copy-done((bf16[256,1024]{1,0:T(8,128)(2,1)S(1)}, bf16[256,1024]{1,0:T(8,128)(2,1)}, u32[]{:S(2)}) %copy-start.6) | copy-done | bytes 524312
  11.3 1.8 %pack_signals.1 = bf16[32,64,256]{2,1,0:T(8,128)(2,1)} custom-call(bf16[256,1024]{1,0:T(8,128)(2,1)S(1)} %copy-done, bf16[256,1024]{1,0:T(8,128)(2,1)S(1)} %copy-done.2, bf16[256,1024]{1,0:T(8,128)(2,1)S(1)} %copy-done.4, bf16[256,1024]{1,0:T(8,128)(2,1)S(1)} %copy-done.6), custom_call_target="tpu_custom_call" | custom-call | tf_op jit(solution)/shard_map/pack_signals/pallas_call | solution.py:74
  13.1 0.0 copy-start.10
  13.1 0.0 copy-start.11
  13.1 0.0 copy-start.3
  13.1 0.0 copy-start.5
  13.1 0.0 copy-start.7
  13.1 7.3 %all-to-all-start = ((bf16[32,64,256]{2,1,0:T(8,128)(2,1)}), bf16[32,64,256]{2,1,0:T(8,128)(2,1)S(1)}, u32[]{:S(2)}, u32[]{:S(2)}) async-start(bf16[32,64,256]{2,1,0:T(8,128)(2,1)} %pack_signals.1), calls=%async_computation | async-start | bytes 2097152 | tf_op jit(solution)/shard_map/all_to_all | solution.py:316
  20.5 0.0 copy-start.1
  20.5 0.0 all-gather.3.cloned.1.call-start
  20.5 0.0 copy-done.10
  20.5 0.0 copy-done.11
  20.6 0.1 broadcast_in_dim.11
  20.7 0.0 copy-done.3
  20.7 0.0 copy-done.5
  20.7 0.0 copy-done.7
  20.7 0.8 copy-done.1
  21.5 4.2 %block_states.1 = f32[2,16,8,128]{3,2,1,0:T(8,128)} custom-call(bf16[256,1024]{1,0:T(8,128)(2,1)S(1)} %copy-done.1, bf16[256,1024]{1,0:T(8,128)(2,1)S(1)} %copy-done.3, bf16[256,1024]{1,0:T(8,128)(2,1)S(1)} %copy-done.5, bf16[256,1024]{1,0:T(8,128)(2,1)S(1)} %copy-done.7, f32[3,16,8,128]{3,2,1,0:T(8,128)S(1)} %bitcast.15), custom_call_target="tpu_custom_call" | custom-call | flops 16777216 | bytes 2097152 | tf_op jit(solution)/shard_map/block_states/pallas_call | solution.py:123
  25.7 0.0 all-gather.3.cloned.1.call-update
  25.7 25.2 %all-to-all-done.refs_0_ = bf16[32,64,256]{2,1,0:T(8,128)(2,1)S(1)} async-done(((bf16[32,64,256]{2,1,0:T(8,128)(2,1)}), bf16[32,64,256]{2,1,0:T(8,128)(2,1)S(1)}, u32[]{:S(2)}, u32[]{:S(2)}) %all-to-all-start) | async-done | bytes 1048608 | tf_op jit(solution)/shard_map/all_to_all | solution.py:316
  50.9 6.3 %filter_lags.1 = f32[8,8,256]{2,1,0:T(8,128)} custom-call(bf16[32,64,256]{2,1,0:T(8,128)(2,1)S(1)} %all-to-all-done.refs_0_), custom_call_target="tpu_custom_call" | custom-call | tf_op jit(solution)/shard_map/filter_lags/pallas_call | solution.py:293
  57.2 3.7 %all-to-all-start.1 = ((f32[8,8,256]{2,1,0:T(8,128)}), f32[8,8,256]{2,1,0:T(8,128)S(1)}, u32[]{:S(2)}, u32[]{:S(2)}) async-start(f32[8,8,256]{2,1,0:T(8,128)} %filter_lags.1), calls=%async_computation.1 | async-start | bytes 131072 | tf_op jit(solution)/shard_map/all_to_all | solution.py:336
  60.9 0.0 copy-start.9
  60.9 9.7 %all-gather.3.cloned.1.call-done = f32[16,16,8,128]{3,2,1,0:T(8,128)} async-done(((f32[2,16,8,128]{3,2,1,0:T(8,128)}), f32[16,16,8,128]{3,2,1,0:T(8,128)}) %all-gather.3.cloned.1.call-update) | async-done | bytes 1048592 | tf_op jit(solution)/shard_map/all_gather | solution.py:329
  70.6 0.0 copy-done.9
  70.6 0.0 copy-start.8
  70.6 1.2 %copy-done.8 = f32[16,16,8,128]{3,2,1,0:T(8,128)S(1)} copy-done((f32[16,16,8,128]{3,2,1,0:T(8,128)S(1)}, f32[16,16,8,128]{3,2,1,0:T(8,128)}, u32[]{:S(2)}) %copy-start.8) | copy-done | bytes 1048600
  71.9 10.6 %local_outputs.1 = (bf16[256,1024]{1,0:T(8,128)(2,1)}, bf16[256,1024]{1,0:T(8,128)(2,1)}, bf16[256,1024]{1,0:T(8,128)(2,1)}) custom-call(s32[1]{0:T(128)} %bitcast.seq_ref, bf16[256,1024]{1,0:T(8,128)(2,1)S(1)} %copy-done.1, bf16[256,1024]{1,0:T(8,128)(2,1)S(1)} %copy-done.3, bf16[256,1024]{1,0:T(8,128)(2,1)S(1)} %copy-done.5, ...), custom_call_target="tpu_custom_call" | custom-call | flops 33554432 | bytes 3670016 | tf_op jit(solution)/shard_map/local_outputs/pallas_call | solution.py:195
  82.4 0.0 all-to-all-done.1
  82.4 0.6 copy.12
  (3 shorter events, 0.1 us)
Async XLA Ops:
  7.2 1.0 %copy-start = (bf16[256,1024]{1,0:T(8,128)(2,1)S(1)}, bf16[256,1024]{1,0:T(8,128)(2,1)}, u32[]{:S(2)}) copy-start(bf16[256,1024]{1,0:T(8,128)(2,1)} %q_ref.5) | copy-start | bytes 1572868
  8.2 1.0 %copy-start.2 = (bf16[256,1024]{1,0:T(8,128)(2,1)S(1)}, bf16[256,1024]{1,0:T(8,128)(2,1)}, u32[]{:S(2)}) copy-start(bf16[256,1024]{1,0:T(8,128)(2,1)} %k_ref.5) | copy-start | bytes 1572868
  9.3 1.0 %copy-start.4 = (bf16[256,1024]{1,0:T(8,128)(2,1)S(1)}, bf16[256,1024]{1,0:T(8,128)(2,1)}, u32[]{:S(2)}) copy-start(bf16[256,1024]{1,0:T(8,128)(2,1)} %v_ref.5) | copy-start | bytes 1572868
  10.3 1.0 %copy-start.6 = (bf16[256,1024]{1,0:T(8,128)(2,1)S(1)}, bf16[256,1024]{1,0:T(8,128)(2,1)}, u32[]{:S(2)}) copy-start(bf16[256,1024]{1,0:T(8,128)(2,1)} %o_ref.5) | copy-start | bytes 1572868
  13.1 7.4 %copy-start.10 = (f32[256,16]{0,1:T(8,128)S(1)}, f32[256,16]{0,1:T(8,128)}, u32[]{:S(2)}) copy-start(f32[256,16]{0,1:T(8,128)} %param.12) | copy-start | bytes 49156
  13.1 7.4 %copy-start.11 = (f32[256,16]{0,1:T(8,128)S(1)}, f32[256,16]{0,1:T(8,128)}, u32[]{:S(2)}) copy-start(f32[256,16]{0,1:T(8,128)} %param.11) | copy-start | bytes 49156
  13.1 7.5 %copy-start.3 = (bf16[256,1024]{1,0:T(8,128)(2,1)S(1)}, bf16[256,1024]{1,0:T(8,128)(2,1)}, u32[]{:S(2)}) copy-start(bf16[256,1024]{1,0:T(8,128)(2,1)} %k_ref.5) | copy-start | bytes 1572868
  13.1 7.6 %copy-start.5 = (bf16[256,1024]{1,0:T(8,128)(2,1)S(1)}, bf16[256,1024]{1,0:T(8,128)(2,1)}, u32[]{:S(2)}) copy-start(bf16[256,1024]{1,0:T(8,128)(2,1)} %v_ref.5) | copy-start | bytes 1572868
  13.1 7.6 %copy-start.7 = (bf16[256,1024]{1,0:T(8,128)(2,1)S(1)}, bf16[256,1024]{1,0:T(8,128)(2,1)}, u32[]{:S(2)}) copy-start(bf16[256,1024]{1,0:T(8,128)(2,1)} %o_ref.5) | copy-start | bytes 1572868
  13.1 37.8 %all-to-all-start = ((bf16[32,64,256]{2,1,0:T(8,128)(2,1)}), bf16[32,64,256]{2,1,0:T(8,128)(2,1)S(1)}, u32[]{:S(2)}, u32[]{:S(2)}) async-start(bf16[32,64,256]{2,1,0:T(8,128)(2,1)} %pack_signals.1), calls=%async_computation | async-start | bytes 2097152 | tf_op jit(solution)/shard_map/all_to_all | solution.py:316
  20.5 1.0 %copy-start.1 = (bf16[256,1024]{1,0:T(8,128)(2,1)S(1)}, bf16[256,1024]{1,0:T(8,128)(2,1)}, u32[]{:S(2)}) copy-start(bf16[256,1024]{1,0:T(8,128)(2,1)} %q_ref.5) | copy-start | bytes 1572868
  20.5 50.2 %all-gather.3.cloned.1.call-start = ((), (), s32[]{:S(2)}) async-start(), calls=%async_computation.2 | async-start | bytes 1179648 | tf_op jit(solution)/shard_map/all_gather | solution.py:329
  57.2 25.2 %all-to-all-start.1 = ((f32[8,8,256]{2,1,0:T(8,128)}), f32[8,8,256]{2,1,0:T(8,128)S(1)}, u32[]{:S(2)}, u32[]{:S(2)}) async-start(f32[8,8,256]{2,1,0:T(8,128)} %filter_lags.1), calls=%async_computation.1 | async-start | bytes 131072 | tf_op jit(solution)/shard_map/all_to_all | solution.py:336
  60.9 9.7 %copy-start.9 = (f32[1024]{0:T(1024)S(1)}, f32[1024]{0:T(1024)}, u32[]{:S(2)}) copy-start(f32[1024]{0:T(1024)} %param.13) | copy-start | bytes 12292
  70.6 1.2 %copy-start.8 = (f32[16,16,8,128]{3,2,1,0:T(8,128)S(1)}, f32[16,16,8,128]{3,2,1,0:T(8,128)}, u32[]{:S(2)}) copy-start(f32[16,16,8,128]{3,2,1,0:T(8,128)} %all-gather.3.cloned.1.call-done) | copy-start | bytes 3145732
Sparse Core Ops, SparseCore 0:
  25.9 44.7 all-gather.2
where the time goes:
time: 90.4 us; the launch traced here: 89.9 us
  waiting for transfers between devices  34.9 us (39%)
  Pallas kernels  22.9 us (25%)
  between operations  14.1 us (16%)
  starting transfers between devices  11 us (12%)
  local copies, waits for them, and re-layouts  6.92 us (8%)
    all_to_all x1, waiting for transfers between devices, per_device(): lax.all_to_all(send, ('seq', 'chan'), split_axis=0, concat_axis=0, tiled=...  25.2 us
    pallas_call x1, Pallas kernels, local_outputs(): pl.pallas_call(output_kernel, in_specs=[pl.BlockSpec(memory_space=pltpu.S...  10.6 us
    all_gather x1, waiting for transfers between devices, per_device(): states = lax.all_gather(states, 'seq', axis=0)  9.74 us
    all_to_all x1, starting transfers between devices, per_device(): lax.all_to_all(send, ('seq', 'chan'), split_axis=0, concat_axis=0, tiled=...  7.3 us
    unnamed x25, local copies, waits for them, and re-layouts  6.84 us
    pallas_call x1, Pallas kernels, filter_lags(): pl.pallas_call(functools.partial(lag_kernel, shards, chans, groups, owned...  6.28 us
    pallas_call x1, Pallas kernels, block_states(): pl.pallas_call(state_kernel, out_shape=jax.ShapeDtypeStruct((2, modes, ti...  4.22 us
    all_to_all x1, starting transfers between devices, per_device(): lags = lax.all_to_all(lags, 'seq', split_axis=0, concat_axis=0, tiled=True)  3.68 us
  transfers between devices with their start and end apart: 3, of which 2 were waited for; matrix products, arithmetic and copies ran while one was open for 0% of the time, Pallas kernels for 23%

commit v1 on v0

--- a/solution.py
+++ b/solution.py
@@ -13,6 +13,7 @@
 LANES = 128
 SUBLANES = 8
 VMEM_BYTES = 48 * 1024 * 1024
+PACK_VMEM_BYTES = 62 * 1024 * 1024
 F32 = jnp.float32
 BF16 = jnp.bfloat16
 
@@ -77,7 +78,7 @@
         in_specs=[block] * 4,
         out_specs=out_spec,
         out_shape=jax.ShapeDtypeStruct(shape, BF16),
-        compiler_params=pltpu.CompilerParams(vmem_limit_bytes=VMEM_BYTES),
+        compiler_params=pltpu.CompilerParams(vmem_limit_bytes=PACK_VMEM_BYTES),
         name="pack_signals",
     )(query_proj, key_proj, value_proj, out_grad)
     if owned % SUBLANES:
@@ -86,25 +87,38 @@
     return send
 
 
-def state_kernel(q_ref, k_ref, v_ref, o_ref, coef_ref, state_ref, x_ref, g_ref):
+def state_kernel(seq_ref, q_ref, k_ref, v_ref, o_ref, coef_ref, state_ref, x_ref, g_ref):
     tok_rows, width = k_ref.shape
     tiles = width // LANES
     modes = coef_ref.shape[1]
     spread_tokens(k_ref, v_ref, x_ref)
     spread_tokens(o_ref, q_ref, g_ref)
+    decay = [coef_ref[0, m] for m in range(modes)]
 
     def step(t, carry):
         x = x_ref[pl.ds(t, tiles, stride=tok_rows), :]
         g = g_ref[pl.ds(tok_rows - 1 - t, tiles, stride=tok_rows), :]
-        ahead = tuple(coef_ref[0, m] * carry[0][m] + x for m in range(modes))
-        behind = tuple(coef_ref[0, m] * carry[1][m] + g for m in range(modes))
+        ahead = tuple(decay[m] * carry[0][m] + x for m in range(modes))
+        behind = tuple(decay[m] * carry[1][m] + g for m in range(modes))
         return (ahead, behind)
 
     zero = tuple(jnp.zeros((tiles, LANES), F32) for _ in range(modes))
     ahead, behind = lax.fori_loop(0, tok_rows, step, (zero, zero), unroll=8)
-    for m in range(modes):
-        state_ref[0, m] = ahead[m]
-        state_ref[1, m] = behind[m]
+    ahead = jnp.concatenate(ahead, axis=0).astype(BF16)
+    behind = jnp.concatenate(behind, axis=0).astype(BF16)
+
+    def fill(s, _):
+        @pl.when(s > seq_ref[0])
+        def _():
+            state_ref[s] = ahead
+
+        @pl.when(s <= seq_ref[0])
+        def _():
+            state_ref[s] = behind
+
+        return 0
+
+    lax.fori_loop(0, state_ref.shape[0], fill, 0)
 
 
 def spread_tokens(a_ref, b_ref, x_ref):
@@ -116,20 +130,23 @@
         ).astype(F32)
 
 
-def block_states(query_proj, key_proj, value_proj, out_grad, coefs):
+def block_states(seq_index, shards, query_proj, key_proj, value_proj, out_grad, coefs):
     tok_rows, width = key_proj.shape
     tiles = width // LANES
     modes = coefs.shape[1]
+    whole = pl.BlockSpec(memory_space=pltpu.VMEM)
     return pl.pallas_call(
         state_kernel,
-        out_shape=jax.ShapeDtypeStruct((2, modes, tiles, LANES), F32),
+        in_specs=[pl.BlockSpec(memory_space=pltpu.SMEM)] + [whole] * 5,
+        out_specs=whole,
+        out_shape=jax.ShapeDtypeStruct((shards, modes * tiles, LANES), BF16),
         scratch_shapes=[pltpu.VMEM((tok_rows * tiles, LANES), F32)] * 2,
         compiler_params=pltpu.CompilerParams(vmem_limit_bytes=VMEM_BYTES),
         cost_estimate=pl.CostEstimate(
             flops=4 * modes * tok_rows * width, bytes_accessed=8 * tok_rows * width, transcendentals=0
         ),
         name="block_states",
-    )(query_proj, key_proj, value_proj, out_grad, coefs)
+    )(seq_index, query_proj, key_proj, value_proj, out_grad, coefs)
 
 
 def output_kernel(
@@ -145,15 +162,14 @@
     spread_tokens(o_ref, q_ref, g_ref)
     zero = tuple(jnp.zeros((tiles, LANES), F32) for _ in range(modes))
 
-    def join_ahead(s, held):
-        return tuple(coef_ref[1, m] * held[m] + all_ref[s, 0, m] for m in range(modes))
-
-    def join_behind(i, held):
-        s = shards - 1 - i
-        return tuple(coef_ref[1, m] * held[m] + all_ref[s, 1, m] for m in range(modes))
+    def join(s, held):
+        block = all_ref[s].astype(F32)
+        return tuple(
+            coef_ref[1, m] * held[m] + block[m * tiles : (m + 1) * tiles] for m in range(modes)
+        )
 
     def total(held):
-        terms = [coef_ref[2, m] * held[m] for m in range(modes)]
+        terms = [weight[m] * held[m] for m in range(modes)]
         while len(terms) > 1:
             terms = [sum(terms[i : i + 2][1:], terms[i]) for i in range(0, len(terms), 2)]
         return terms[0]
@@ -162,16 +178,18 @@
         def step(t, held):
             rows = pl.ds(start + move * t, tiles, stride=tok_rows)
             x = ref[rows, :]
-            held = tuple(coef_ref[0, m] * held[m] + x for m in range(modes))
+            held = tuple(decay[m] * held[m] + x for m in range(modes))
             ref[rows, :] = total(held)
             return held
 
         return step
 
-    held = lax.fori_loop(0, seq, join_ahead, zero)
-    lax.fori_loop(0, tok_rows, walk(x_ref, 0, 1), held, unroll=8)
-    held = lax.fori_loop(0, shards - 1 - seq, join_behind, zero)
-    lax.fori_loop(0, tok_rows, walk(g_ref, tok_rows - 1, -1), held, unroll=8)
+    before = lax.fori_loop(0, seq, join, zero)
+    after = lax.fori_loop(0, shards - 1 - seq, lambda i, held: join(shards - 1 - i, held), zero)
+    decay = [coef_ref[0, m] for m in range(modes)]
+    weight = [coef_ref[2, m] for m in range(modes)]
+    lax.fori_loop(0, tok_rows, walk(x_ref, 0, 1), before, unroll=8)
+    lax.fori_loop(0, tok_rows, walk(g_ref, tok_rows - 1, -1), after, unroll=8)
     for tile in range(tiles):
         cols = slice(tile * LANES, (tile + 1) * LANES)
         rows = slice(tile * tok_rows, (tile + 1) * tok_rows)
@@ -203,7 +221,7 @@
             flops=8 * modes * tok_rows * width, bytes_accessed=14 * tok_rows * width, transcendentals=0
         ),
         name="local_outputs",
-    )(seq_index.reshape(1), query_proj, key_proj, value_proj, out_grad, coefs, gain, states)
+    )(seq_index, query_proj, key_proj, value_proj, out_grad, coefs, gain, states)
 
 
 def lag_kernel(shards, chans, groups, owned, scale, *refs):
@@ -306,13 +324,14 @@
     tok_rows, width = key_proj.shape
     shards = lax.axis_size("seq")
     chans = lax.axis_size("chan")
-    seq_index = lax.axis_index("seq")
+    seq_index = lax.axis_index("seq").reshape(1)
     length = shards * tok_rows
     owned = FILTERS // (shards * chans)
     modes = residues.shape[1]
     signals = (query_proj, key_proj, value_proj, out_grad)
 
     send = pack_signals(shards, chans, owned, *signals)
+    send, *signals = lax.optimization_barrier((send, *signals))
     received = lax.all_to_all(send, ("seq", "chan"), split_axis=0, concat_axis=0, tiled=True)
 
     coefs = jnp.stack(
@@ -325,11 +344,10 @@
     coefs = coefs.transpose(0, 2, 1).reshape(3, modes, 1, FILTERS // LANES, LANES)
     coefs = jnp.broadcast_to(coefs, (3, modes, width // FILTERS, FILTERS // LANES, LANES))
     coefs = coefs.reshape(3, modes, width // LANES, LANES)
-    states = block_states(*signals, coefs)
-    states = lax.all_gather(states, "seq", axis=0)
-    layer_out, key_grad, value_grad = local_outputs(
-        seq_index, *signals, coefs, skip_gain[None, :], states
-    )
+    states = block_states(seq_index, shards, *signals, coefs)
+    states = lax.all_to_all(states, "seq", split_axis=0, concat_axis=0, tiled=True)
+    local = local_outputs(seq_index, *signals, coefs, skip_gain[None, :], states)
+    received, layer_out, key_grad, value_grad = lax.optimization_barrier((received, *local))
 
     scale = 1.0 / math.sqrt(length * (CHANNELS // FILTERS))
     lags = filter_lags(received, shards, chans, owned, scale)

time: 90.4 us -> 74 us (0.82)
  blocking collectives: 0 us -> 26.4 us
  waiting for transfers between devices: 34.9 us -> 15.9 us
  between operations: 14.1 us -> 0.76 us
  starting transfers between devices: 11 us -> 3.73 us
  local copies, waits for them, and re-layouts: 6.92 us -> 1.77 us
  Pallas kernels: 22.9 us -> 24.3 us
    all_to_all x0 -> x2, blocking collectives: none -> 26.4 us  [the longest x1 16 us: per_device(): lax.all_to_all(states, 'seq', split_axis=0, concat_axis=0, tiled=True)]
    all_gather x1 -> x0, waiting for transfers between devices: 9.74 us -> none  [per_device(): states = lax.all_gather(states, 'seq', axis=0)]
    all_to_all x1, waiting for transfers between devices: 25.2 us -> 15.9 us  [per_device(): lax.all_to_all(send, ('seq', 'chan'), split_axis=0, concat_axis=0, tiled=...]
    unnamed x25 -> x13, local copies, waits for them, and re-layouts: 6.84 us -> 1.69 us
    all_to_all x1 -> x0, starting transfers between devices: 3.68 us -> none  [per_device(): lags = lax.all_to_all(lags, 'seq', split_axis=0, concat_axis=0, tiled=True)]
    all_to_all x1, starting transfers between devices: 7.3 us -> 3.73 us  [per_device(): lax.all_to_all(send, ('seq', 'chan'), split_axis=0, concat_axis=0, tiled=...]
    pallas_call x1, Pallas kernels: 1.79 us -> 3.11 us  [pack_signals(): pl.pallas_call(functools.partial(pack_kernel, shards, chans, owned), grid...]
  transfers between devices with their start and end apart: 3 -> 1, of which waited for: 2 -> 1; matrix products, arithmetic and copies ran while one was open for 0% -> 0% of each run, Pallas kernels for 23% -> 14%
where the time goes in v1:
time: 74 us; the launch traced here: 73.6 us
  blocking collectives  26.4 us (36%)
  Pallas kernels  24.3 us (33%)
  waiting for transfers between devices  15.9 us (21%)
  starting transfers between devices  3.73 us (5%)
  local copies, waits for them, and re-layouts  1.77 us (2%)
  other arithmetic  0.76 us (1%)
  between operations  0.76 us (1%)
    all_to_all x1, blocking collectives, per_device(): lax.all_to_all(states, 'seq', split_axis=0, concat_axis=0, tiled=True)  16 us
    all_to_all x1, waiting for transfers between devices, per_device(): lax.all_to_all(send, ('seq', 'chan'), split_axis=0, concat_axis=0, tiled=...  15.9 us
    all_to_all x1, blocking collectives, per_device(): lags = lax.all_to_all(lags, 'seq', split_axis=0, concat_axis=0, tiled=True)  10.4 us
    pallas_call x1, Pallas kernels, local_outputs(): pl.pallas_call(output_kernel, in_specs=[pl.BlockSpec(memory_space=pltpu.S...  10.3 us
    pallas_call x1, Pallas kernels, filter_lags(): pl.pallas_call(functools.partial(lag_kernel, shards, chans, groups, owned...  6.88 us
    pallas_call x1, Pallas kernels, block_states(): pl.pallas_call(state_kernel, in_specs=[pl.BlockSpec(memory_space=pltpu.SM...  4.01 us
    all_to_all x1, starting transfers between devices, per_device(): lax.all_to_all(send, ('seq', 'chan'), split_axis=0, concat_axis=0, tiled=...  3.73 us
    pallas_call x1, Pallas kernels, pack_signals(): pl.pallas_call(functools.partial(pack_kernel, shards, chans, owned), grid...  3.11 us
  transfers between devices with their start and end apart: 1, of which 1 were waited for; matrix products, arithmetic and copies ran while one was open for 0% of the time, Pallas kernels for 14%

profile of v1, /device:TPU:0, one launch (start us, length us, event | category | flops | bytes accessed | tf_op | source)
XLA Modules:
  0.0 73.6 jit_solution(3556471379105119908)
XLA Ops:
  0.6 0.8 %exponential_bitcast_fusion.1 = (f32[1,256,16]{1,2,0:T(8,128)S(1)}, f32[1,256,16]{1,2,0:T(8,128)S(1)}, f32[1,256,16]{1,2,0:T(8,128)S(1)}) fusion(f32[256,16]{0,1:T(8,128)} %param.12, f32[256,16]{0,1:T(8,128)} %param.11), kind=kLoop, calls=%fused_computation.3 | loop fusion | flops 16384 | bytes 81920 | tf_op jit(solution)/shard_map/stack | solution.py:337
  1.4 0.0 copy-start
  1.5 0.0 copy-start.1
  1.5 0.0 copy-start.2
  1.5 3.1 %pack_signals.1 = bf16[32,64,256]{2,1,0:T(8,128)(2,1)} custom-call(bf16[256,1024]{1,0:T(8,128)(2,1)} %q_ref.3, bf16[256,1024]{1,0:T(8,128)(2,1)} %k_ref.3, bf16[256,1024]{1,0:T(8,128)(2,1)} %v_ref.3, bf16[256,1024]{1,0:T(8,128)(2,1)} %o_ref.3), custom_call_target="tpu_custom_call" | custom-call | tf_op jit(solution)/shard_map/pack_signals/pallas_call | solution.py:75
  4.6 0.1 broadcast_in_dim.11
  4.6 0.0 copy-done
  4.7 0.0 copy-done.1
  4.7 0.0 copy-done.2
  4.7 0.0 copy-start.3
  4.7 1.0 %copy-done.3 = bf16[256,1024]{1,0:T(8,128)(2,1)S(1)} copy-done((bf16[256,1024]{1,0:T(8,128)(2,1)S(1)}, bf16[256,1024]{1,0:T(8,128)(2,1)}, u32[]{:S(2)}) %copy-start.3) | copy-done | bytes 524312
  5.7 4.0 %block_states.1 = bf16[8,128,128]{2,1,0:T(8,128)(2,1)S(1)} custom-call(s32[1]{0:T(128)} %bitcast.seq_ref, bf16[256,1024]{1,0:T(8,128)(2,1)S(1)} %copy-done, bf16[256,1024]{1,0:T(8,128)(2,1)S(1)} %copy-done.1, bf16[256,1024]{1,0:T(8,128)(2,1)S(1)} %copy-done.2, bf16[256,1024]{1,0:T(8,128)(2,1)S(1)} %copy-done.3, f32[3,16,8,128]{3,2,1,0:T(8,128)S(1)} %bitcast.14), custom_call_target="tpu_custom_call" | custom-call | flops 16777216 | bytes 2097152 | tf_op jit(solution)/shard_map/block_states/pallas_call | solution.py:138
  9.7 16.0 %all_to_all.15.all_ref = bf16[8,128,128]{2,1,0:T(8,128)(2,1)S(1)} all-to-all(bf16[8,128,128]{2,1,0:T(8,128)(2,1)S(1)} %block_states.1), channel_id=1, replica_groups=mesh['seq'=8,'chan'=4] {'seq'}, dimensions={0} | all-to-all | bytes 524288 | tf_op jit(solution)/shard_map/all_to_all | solution.py:348
  25.7 0.0 copy-start.4
  25.7 0.0 copy-start.5
  25.7 3.7 %all-to-all-start = ((bf16[32,64,256]{2,1,0:T(8,128)(2,1)}), bf16[32,64,256]{2,1,0:T(8,128)(2,1)}, u32[]{:S(2)}, u32[]{:S(2)}) async-start(bf16[32,64,256]{2,1,0:T(8,128)(2,1)} %pack_signals.1), calls=%async_computation | async-start | bytes 2097152 | tf_op jit(solution)/shard_map/all_to_all | solution.py:335
  29.5 0.0 copy-done.4
  29.5 0.0 copy-done.5
  29.5 10.3 %local_outputs.1 = (bf16[256,1024]{1,0:T(8,128)(2,1)}, bf16[256,1024]{1,0:T(8,128)(2,1)}, bf16[256,1024]{1,0:T(8,128)(2,1)}) custom-call(s32[1]{0:T(128)} %bitcast.seq_ref, bf16[256,1024]{1,0:T(8,128)(2,1)S(1)} %copy-done, bf16[256,1024]{1,0:T(8,128)(2,1)S(1)} %copy-done.1, bf16[256,1024]{1,0:T(8,128)(2,1)S(1)} %copy-done.2, ...), custom_call_target="tpu_custom_call" | custom-call | flops 33554432 | bytes 3670016 | tf_op jit(solution)/shard_map/local_outputs/pallas_call | solution.py:213
  39.8 15.9 %all-to-all-done.refs_0_ = bf16[32,64,256]{2,1,0:T(8,128)(2,1)} async-done(((bf16[32,64,256]{2,1,0:T(8,128)(2,1)}), bf16[32,64,256]{2,1,0:T(8,128)(2,1)}, u32[]{:S(2)}, u32[]{:S(2)}) %all-to-all-start) | async-done | bytes 1048608 | tf_op jit(solution)/shard_map/all_to_all | solution.py:335
  55.7 6.9 %filter_lags.1 = f32[8,8,256]{2,1,0:T(8,128)S(1)} custom-call(bf16[32,64,256]{2,1,0:T(8,128)(2,1)} %all-to-all-done.refs_0_), custom_call_target="tpu_custom_call" | custom-call | tf_op jit(solution)/shard_map/filter_lags/pallas_call | solution.py:311
  62.6 10.4 %all_to_all.16 = f32[8,8,256]{2,1,0:T(8,128)S(1)} all-to-all(f32[8,8,256]{2,1,0:T(8,128)S(1)} %filter_lags.1), channel_id=1, replica_groups=mesh['seq'=8,'chan'=4] {'seq'}, dimensions={0} | all-to-all | bytes 131072 | tf_op jit(solution)/shard_map/all_to_all | solution.py:354
  73.0 0.6 copy.12
  (2 shorter events, 0.0 us)
Async XLA Ops:
  1.4 3.2 %copy-start = (bf16[256,1024]{1,0:T(8,128)(2,1)S(1)}, bf16[256,1024]{1,0:T(8,128)(2,1)}, u32[]{:S(2)}) copy-start(bf16[256,1024]{1,0:T(8,128)(2,1)} %q_ref.3) | copy-start | bytes 1572868
  1.5 3.2 %copy-start.1 = (bf16[256,1024]{1,0:T(8,128)(2,1)S(1)}, bf16[256,1024]{1,0:T(8,128)(2,1)}, u32[]{:S(2)}) copy-start(bf16[256,1024]{1,0:T(8,128)(2,1)} %k_ref.3) | copy-start | bytes 1572868
  1.5 3.2 %copy-start.2 = (bf16[256,1024]{1,0:T(8,128)(2,1)S(1)}, bf16[256,1024]{1,0:T(8,128)(2,1)}, u32[]{:S(2)}) copy-start(bf16[256,1024]{1,0:T(8,128)(2,1)} %v_ref.3) | copy-start | bytes 1572868
  4.7 1.0 %copy-start.3 = (bf16[256,1024]{1,0:T(8,128)(2,1)S(1)}, bf16[256,1024]{1,0:T(8,128)(2,1)}, u32[]{:S(2)}) copy-start(bf16[256,1024]{1,0:T(8,128)(2,1)} %o_ref.3) | copy-start | bytes 1572868
  25.7 3.7 %copy-start.4 = (bf16[256,1024]{1,0:T(8,128)(2,1)S(1)}, bf16[256,1024]{1,0:T(8,128)(2,1)}, u32[]{:S(2)}) copy-start(bf16[256,1024]{1,0:T(8,128)(2,1)} %o_ref.3) | copy-start | bytes 1572868
  25.7 3.8 %copy-start.5 = (f32[1024]{0:T(1024)S(1)}, f32[1024]{0:T(1024)}, u32[]{:S(2)}) copy-start(f32[1024]{0:T(1024)} %param.13) | copy-start | bytes 12292
  25.7 30.0 %all-to-all-start = ((bf16[32,64,256]{2,1,0:T(8,128)(2,1)}), bf16[32,64,256]{2,1,0:T(8,128)(2,1)}, u32[]{:S(2)}, u32[]{:S(2)}) async-start(bf16[32,64,256]{2,1,0:T(8,128)(2,1)} %pack_signals.1), calls=%async_computation | async-start | bytes 2097152 | tf_op jit(solution)/shard_map/all_to_all | solution.py:335

commit v2 on v0

--- a/solution.py
+++ b/solution.py
@@ -13,8 +13,10 @@
 LANES = 128
 SUBLANES = 8
 VMEM_BYTES = 48 * 1024 * 1024
+PACK_VMEM_BYTES = 24 * 1024 * 1024
 F32 = jnp.float32
 BF16 = jnp.bfloat16
+LINK = jnp.bfloat16
 
 
 def product(first, second):
@@ -27,8 +29,16 @@
     return (col == column_of(row)).astype(F32).astype(BF16)
 
 
-def pack_kernel(shards, chans, owned, q_ref, k_ref, v_ref, o_ref, send_ref):
+def pack_kernel(shards, chans, owned, *refs):
+    hbm_refs, send_ref, held, sems = refs[:4], refs[4], refs[5], refs[6]
+    tok_rows, width = held.shape[1:]
+    groups = width // FILTERS
     per_chan = FILTERS // chans
+    copies = [
+        pltpu.make_async_copy(hbm_refs[i], held.at[i], sems.at[i]) for i in range(len(hbm_refs))
+    ]
+    for copy in copies:
+        copy.start()
 
     def owned_filter(row):
         seq = row // (chans * owned)
@@ -36,10 +46,10 @@
         return chan * per_chan + seq * owned + row % owned
 
     order = one_hot(FILTERS, FILTERS, owned_filter)
-    width = k_ref.shape[1]
-    groups = width // FILTERS
-    for which, (a_ref, b_ref) in enumerate(((k_ref, v_ref), (o_ref, q_ref))):
-        signal = product(a_ref[...], b_ref[...])
+    for which in range(2):
+        copies[2 * which].wait()
+        copies[2 * which + 1].wait()
+        signal = product(held[2 * which], held[2 * which + 1])
         parts = []
         for group in range(groups):
             part = lax.dot_general(
@@ -51,7 +61,7 @@
             if owned % SUBLANES:
                 send_ref[which, group] = part.astype(BF16)
             else:
-                parts.append(part.reshape(shards * chans, owned, part.shape[1]))
+                parts.append(part.reshape(shards * chans, owned, tok_rows))
         if parts:
             rows = groups * owned
             send_ref[:, which * rows : (which + 1) * rows, :] = jnp.concatenate(
@@ -63,48 +73,48 @@
     tok_rows, width = key_proj.shape
     groups = width // FILTERS
     dests = shards * chans
-    steps = tok_rows // LANES
-    block = pl.BlockSpec((LANES, width), lambda i: (i, 0))
     if owned % SUBLANES:
         shape = (2, groups, FILTERS, tok_rows)
-        out_spec = pl.BlockSpec((2, groups, FILTERS, LANES), lambda i: (0, 0, 0, i))
     else:
         shape = (dests, 2 * groups * owned, tok_rows)
-        out_spec = pl.BlockSpec((dests, 2 * groups * owned, LANES), lambda i: (0, 0, i))
     send = pl.pallas_call(
         functools.partial(pack_kernel, shards, chans, owned),
-        grid=(steps,),
-        in_specs=[block] * 4,
-        out_specs=out_spec,
+        in_specs=[pl.BlockSpec(memory_space=pltpu.HBM)] * 4,
+        out_specs=pl.BlockSpec(memory_space=pltpu.VMEM),
         out_shape=jax.ShapeDtypeStruct(shape, BF16),
-        compiler_params=pltpu.CompilerParams(vmem_limit_bytes=VMEM_BYTES),
+        scratch_shapes=[
+            pltpu.VMEM((4, tok_rows, width), BF16),
+            pltpu.SemaphoreType.DMA((4,)),
+        ],
+        compiler_params=pltpu.CompilerParams(vmem_limit_bytes=PACK_VMEM_BYTES),
         name="pack_signals",
-    )(query_proj, key_proj, value_proj, out_grad)
+    )(key_proj, value_proj, out_grad, query_proj)
     if owned % SUBLANES:
         send = send.reshape(2, groups, dests, owned, tok_rows)
         send = send.transpose(2, 0, 1, 3, 4).reshape(dests, 2 * groups * owned, tok_rows)
     return send
 
 
-def state_kernel(q_ref, k_ref, v_ref, o_ref, coef_ref, state_ref, x_ref, g_ref):
+def state_kernel(q_ref, k_ref, v_ref, o_ref, coef_ref, ahead_ref, behind_ref, x_ref, g_ref):
     tok_rows, width = k_ref.shape
     tiles = width // LANES
     modes = coef_ref.shape[1]
     spread_tokens(k_ref, v_ref, x_ref)
     spread_tokens(o_ref, q_ref, g_ref)
+    decay = [coef_ref[0, m] for m in range(modes)]
 
     def step(t, carry):
         x = x_ref[pl.ds(t, tiles, stride=tok_rows), :]
         g = g_ref[pl.ds(tok_rows - 1 - t, tiles, stride=tok_rows), :]
-        ahead = tuple(coef_ref[0, m] * carry[0][m] + x for m in range(modes))
-        behind = tuple(coef_ref[0, m] * carry[1][m] + g for m in range(modes))
+        ahead = tuple(decay[m] * carry[0][m] + x for m in range(modes))
+        behind = tuple(decay[m] * carry[1][m] + g for m in range(modes))
         return (ahead, behind)
 
     zero = tuple(jnp.zeros((tiles, LANES), F32) for _ in range(modes))
     ahead, behind = lax.fori_loop(0, tok_rows, step, (zero, zero), unroll=8)
     for m in range(modes):
-        state_ref[0, m] = ahead[m]
-        state_ref[1, m] = behind[m]
+        ahead_ref[m] = ahead[m].astype(ahead_ref.dtype)
+        behind_ref[m] = behind[m].astype(behind_ref.dtype)
 
 
 def spread_tokens(a_ref, b_ref, x_ref):
@@ -122,7 +132,7 @@
     modes = coefs.shape[1]
     return pl.pallas_call(
         state_kernel,
-        out_shape=jax.ShapeDtypeStruct((2, modes, tiles, LANES), F32),
+        out_shape=[jax.ShapeDtypeStruct((modes, tiles, LANES), F32)] * 2,
         scratch_shapes=[pltpu.VMEM((tok_rows * tiles, LANES), F32)] * 2,
         compiler_params=pltpu.CompilerParams(vmem_limit_bytes=VMEM_BYTES),
         cost_estimate=pl.CostEstimate(
@@ -132,78 +142,87 @@
     )(query_proj, key_proj, value_proj, out_grad, coefs)
 
 
-def output_kernel(
-    seq_ref, q_ref, k_ref, v_ref, o_ref, coef_ref, gain_ref, all_ref,
-    layer_ref, key_ref, value_ref, x_ref, g_ref,
+def blocks_before(state, block_decay, move):
+    shards = lax.axis_size("seq")
+
+    def shift(value, count):
+        route = [
+            (i, i + move * count) for i in range(shards) if 0 <= i + move * count < shards
+        ]
+        if not route:
+            return jnp.zeros_like(value)
+        return lax.ppermute(value, "seq", route)
+
+    sent = state.astype(LINK)
+    total = shift(sent, 1).astype(F32) + block_decay * shift(sent, 2).astype(F32)
+    span = 2
+    while span < shards - 1:
+        block_decay = block_decay * block_decay
+        total = total + block_decay * shift(total.astype(LINK), span).astype(F32)
+        span *= 2
+    return total
+
+
+def walk_tokens(ref, held, coef_ref, tok_rows, tiles, start, move):
+    modes = coef_ref.shape[1]
+    decay = [coef_ref[0, m] for m in range(modes)]
+    weight = [coef_ref[2, m] for m in range(modes)]
+
+    def step(t, held):
+        rows = pl.ds(start + move * t, tiles, stride=tok_rows)
+        x = ref[rows, :]
+        held = tuple(decay[m] * held[m] + x for m in range(modes))
+        terms = [weight[m] * held[m] for m in range(modes)]
+        while len(terms) > 1:
+            terms = [sum(terms[i : i + 2][1:], terms[i]) for i in range(0, len(terms), 2)]
+        ref[rows, :] = terms[0]
+        return held
+
+    lax.fori_loop(0, tok_rows, step, tuple(held[m] for m in range(modes)), unroll=8)
+
+
+def conv_kernel(q_ref, k_ref, v_ref, coef_ref, gain_ref, before_ref, layer_ref, x_ref):
+    tok_rows, width = k_ref.shape
+    tiles = width // LANES
+    spread_tokens(k_ref, v_ref, x_ref)
+    walk_tokens(x_ref, before_ref, coef_ref, tok_rows, tiles, 0, 1)
+    for tile in range(tiles):
+        cols = slice(tile * LANES, (tile + 1) * LANES)
+        rows = slice(tile * tok_rows, (tile + 1) * tok_rows)
+        conv_in = product(k_ref[:, cols], v_ref[:, cols]).astype(F32)
+        long_conv = x_ref[rows, :] + gain_ref[:, cols] * conv_in
+        layer_ref[:, cols] = (q_ref[:, cols].astype(F32) * long_conv).astype(BF16)
+
+
+def grad_kernel(
+    q_ref, k_ref, v_ref, o_ref, coef_ref, gain_ref, after_ref, key_ref, value_ref, g_ref
 ):
     tok_rows, width = k_ref.shape
     tiles = width // LANES
-    modes = coef_ref.shape[1]
-    shards = all_ref.shape[0]
-    seq = seq_ref[0]
-    spread_tokens(k_ref, v_ref, x_ref)
     spread_tokens(o_ref, q_ref, g_ref)
-    zero = tuple(jnp.zeros((tiles, LANES), F32) for _ in range(modes))
-
-    def join_ahead(s, held):
-        return tuple(coef_ref[1, m] * held[m] + all_ref[s, 0, m] for m in range(modes))
-
-    def join_behind(i, held):
-        s = shards - 1 - i
-        return tuple(coef_ref[1, m] * held[m] + all_ref[s, 1, m] for m in range(modes))
-
-    def total(held):
-        terms = [coef_ref[2, m] * held[m] for m in range(modes)]
-        while len(terms) > 1:
-            terms = [sum(terms[i : i + 2][1:], terms[i]) for i in range(0, len(terms), 2)]
-        return terms[0]
-
-    def walk(ref, start, move):
-        def step(t, held):
-            rows = pl.ds(start + move * t, tiles, stride=tok_rows)
-            x = ref[rows, :]
-            held = tuple(coef_ref[0, m] * held[m] + x for m in range(modes))
-            ref[rows, :] = total(held)
-            return held
-
-        return step
-
-    held = lax.fori_loop(0, seq, join_ahead, zero)
-    lax.fori_loop(0, tok_rows, walk(x_ref, 0, 1), held, unroll=8)
-    held = lax.fori_loop(0, shards - 1 - seq, join_behind, zero)
-    lax.fori_loop(0, tok_rows, walk(g_ref, tok_rows - 1, -1), held, unroll=8)
+    walk_tokens(g_ref, after_ref, coef_ref, tok_rows, tiles, tok_rows - 1, -1)
     for tile in range(tiles):
         cols = slice(tile * LANES, (tile + 1) * LANES)
         rows = slice(tile * tok_rows, (tile + 1) * tok_rows)
-        q = q_ref[:, cols].astype(F32)
-        k = k_ref[:, cols].astype(F32)
-        v = v_ref[:, cols].astype(F32)
-        gain = gain_ref[:, cols]
-        conv_in = (k * v).astype(BF16).astype(F32)
-        mid_grad = (o_ref[:, cols].astype(F32) * q).astype(BF16).astype(F32)
-        layer_ref[:, cols] = (q * (x_ref[rows, :] + gain * conv_in)).astype(BF16)
-        conv_grad = g_ref[rows, :] + gain * mid_grad
-        key_ref[:, cols] = (conv_grad * v).astype(BF16)
-        value_ref[:, cols] = (conv_grad * k).astype(BF16)
-
-
-def local_outputs(seq_index, query_proj, key_proj, value_proj, out_grad, coefs, gain, states):
-    tok_rows, width = key_proj.shape
-    tiles = width // LANES
-    modes = coefs.shape[1]
-    whole = pl.BlockSpec(memory_space=pltpu.VMEM)
+        mid_grad = product(o_ref[:, cols], q_ref[:, cols]).astype(F32)
+        conv_grad = g_ref[rows, :] + gain_ref[:, cols] * mid_grad
+        key_ref[:, cols] = (conv_grad * v_ref[:, cols].astype(F32)).astype(BF16)
+        value_ref[:, cols] = (conv_grad * k_ref[:, cols].astype(F32)).astype(BF16)
+
+
+def local_outputs(kernel, count, name, *args):
+    tok_rows, width = args[0].shape
+    modes, tiles = args[-1].shape[:2]
     return pl.pallas_call(
-        output_kernel,
-        in_specs=[pl.BlockSpec(memory_space=pltpu.SMEM)] + [whole] * 7,
-        out_specs=[whole] * 3,
-        out_shape=[jax.ShapeDtypeStruct((tok_rows, width), BF16)] * 3,
-        scratch_shapes=[pltpu.VMEM((tok_rows * tiles, LANES), F32)] * 2,
+        kernel,
+        out_shape=[jax.ShapeDtypeStruct((tok_rows, width), BF16)] * count,
+        scratch_shapes=[pltpu.VMEM((tok_rows * tiles, LANES), F32)],
         compiler_params=pltpu.CompilerParams(vmem_limit_bytes=VMEM_BYTES),
         cost_estimate=pl.CostEstimate(
-            flops=8 * modes * tok_rows * width, bytes_accessed=14 * tok_rows * width, transcendentals=0
+            flops=4 * modes * tok_rows * width, bytes_accessed=8 * tok_rows * width, transcendentals=0
         ),
-        name="local_outputs",
-    )(seq_index.reshape(1), query_proj, key_proj, value_proj, out_grad, coefs, gain, states)
+        name=name,
+    )(*args)
 
 
 def lag_kernel(shards, chans, groups, owned, scale, *refs):
@@ -306,13 +325,15 @@
     tok_rows, width = key_proj.shape
     shards = lax.axis_size("seq")
     chans = lax.axis_size("chan")
-    seq_index = lax.axis_index("seq")
     length = shards * tok_rows
     owned = FILTERS // (shards * chans)
     modes = residues.shape[1]
     signals = (query_proj, key_proj, value_proj, out_grad)
 
     send = pack_signals(shards, chans, owned, *signals)
+    send, *signals, residues, decay_rate = lax.optimization_barrier(
+        (send, *signals, residues, decay_rate)
+    )
     received = lax.all_to_all(send, ("seq", "chan"), split_axis=0, concat_axis=0, tiled=True)
 
     coefs = jnp.stack(
@@ -325,10 +346,17 @@
     coefs = coefs.transpose(0, 2, 1).reshape(3, modes, 1, FILTERS // LANES, LANES)
     coefs = jnp.broadcast_to(coefs, (3, modes, width // FILTERS, FILTERS // LANES, LANES))
     coefs = coefs.reshape(3, modes, width // LANES, LANES)
-    states = block_states(*signals, coefs)
-    states = lax.all_gather(states, "seq", axis=0)
-    layer_out, key_grad, value_grad = local_outputs(
-        seq_index, *signals, coefs, skip_gain[None, :], states
+    ahead, behind = block_states(*signals, coefs)
+    before = blocks_before(ahead, coefs[1], 1)
+    after = blocks_before(behind, coefs[1], -1)
+    query_proj, key_proj, value_proj, out_grad = signals
+    gain = skip_gain[None, :]
+    (layer_out,) = local_outputs(
+        conv_kernel, 1, "conv_outputs", query_proj, key_proj, value_proj, coefs, gain, before
+    )
+    received, layer_out = lax.optimization_barrier((received, layer_out))
+    key_grad, value_grad = local_outputs(
+        grad_kernel, 2, "grad_outputs", *signals, coefs, gain, after
     )
 
     scale = 1.0 / math.sqrt(length * (CHANNELS // FILTERS))

time: 90.4 us -> 82.9 us (0.917)
  starting transfers between devices: 11 us -> 45.2 us
  waiting for transfers between devices: 34.9 us -> 5.13 us
  between operations: 14.1 us -> 0.91 us
  other arithmetic: 0.02 us -> 1.39 us
    ppermute x0 -> x8, starting transfers between devices: none -> 30.6 us  [shift(): return lax.ppermute(value, 'seq', route)]
    all_to_all x1, waiting for transfers between devices: 25.2 us -> 0.01 us  [per_device(): lax.all_to_all(send, ('seq', 'chan'), split_axis=0, concat_axis=0, tiled=...]
    all_gather x1 -> x0, waiting for transfers between devices: 9.74 us -> none  [per_device(): states = lax.all_gather(states, 'seq', axis=0)]
    ppermute x0 -> x8, waiting for transfers between devices: none -> 4.99 us  [shift(): return lax.ppermute(value, 'seq', route)]
    all_to_all x1, starting transfers between devices: 3.68 us -> 7.25 us  [per_device(): lags = lax.all_to_all(lags, 'seq', split_axis=0, concat_axis=0, tiled=True)]
    convert_element_type x0 -> x4, other arithmetic: none -> 1.31 us  [the longest x2 1.24 us: blocks_before(): sent = state.astype(LINK)]
    unnamed x25 -> x23, local copies, waits for them, and re-layouts: 6.84 us -> 6.33 us
    pallas_call x3 -> x4, Pallas kernels: 16.6 us -> 16.8 us  [the longest x2 11.1 us: local_outputs(): pl.pallas_call(kernel, out_shape=[jax.ShapeDtypeStruct((tok_rows, width),...]
  transfers between devices with their start and end apart: 3 -> 10, of which waited for: 2 -> 5; matrix products, arithmetic and copies ran while one was open for 0% -> 2% of each run, Pallas kernels for 23% -> 18%
where the time goes in v2:
time: 82.9 us; the launch traced here: 82.2 us
  starting transfers between devices  45.2 us (55%)
  Pallas kernels  23.1 us (28%)
  local copies, waits for them, and re-layouts  6.44 us (8%)
  waiting for transfers between devices  5.13 us (6%)
  other arithmetic  1.39 us (2%)
  between operations  0.91 us (1%)
    ppermute x8, starting transfers between devices, shift(): return lax.ppermute(value, 'seq', route)  30.6 us
    pallas_call x2, Pallas kernels, local_outputs(): pl.pallas_call(kernel, out_shape=[jax.ShapeDtypeStruct((tok_rows, width),...  11.1 us
    all_to_all x1, starting transfers between devices, per_device(): lax.all_to_all(send, ('seq', 'chan'), split_axis=0, concat_axis=0, tiled=...  7.3 us
    all_to_all x1, starting transfers between devices, per_device(): lags = lax.all_to_all(lags, 'seq', split_axis=0, concat_axis=0, tiled=True)  7.25 us
    unnamed x23, local copies, waits for them, and re-layouts  6.33 us
    pallas_call x1, Pallas kernels, filter_lags(): pl.pallas_call(functools.partial(lag_kernel, shards, chans, groups, owned...  6.29 us
    ppermute x8, waiting for transfers between devices, shift(): return lax.ppermute(value, 'seq', route)  4.99 us
    pallas_call x1, Pallas kernels, block_states(): pl.pallas_call(state_kernel, out_shape=[jax.ShapeDtypeStruct((modes, tile...  3.77 us
  transfers between devices with their start and end apart: 10, of which 5 were waited for; matrix products, arithmetic and copies ran while one was open for 2% of the time, Pallas kernels for 18%

profile of v2, /device:TPU:0, one launch (start us, length us, event | category | flops | bytes accessed | tf_op | source)
XLA Modules:
  0.0 82.2 jit_solution(8473073876965498745)
XLA Ops:
  0.6 0.0 copy-start
  0.6 1.0 %copy-done = bf16[256,1024]{1,0:T(8,128)(2,1)S(1)} copy-done((bf16[256,1024]{1,0:T(8,128)(2,1)S(1)}, bf16[256,1024]{1,0:T(8,128)(2,1)}, u32[]{:S(2)}) %copy-start) | copy-done | bytes 524312
  1.7 0.0 copy-start.2
  1.7 1.0 %copy-done.2 = bf16[256,1024]{1,0:T(8,128)(2,1)S(1)} copy-done((bf16[256,1024]{1,0:T(8,128)(2,1)S(1)}, bf16[256,1024]{1,0:T(8,128)(2,1)}, u32[]{:S(2)}) %copy-start.2) | copy-done | bytes 524312
  2.7 0.0 copy-start.4
  2.7 1.0 %copy-done.4 = bf16[256,1024]{1,0:T(8,128)(2,1)S(1)} copy-done((bf16[256,1024]{1,0:T(8,128)(2,1)S(1)}, bf16[256,1024]{1,0:T(8,128)(2,1)}, u32[]{:S(2)}) %copy-start.4) | copy-done | bytes 524312
  3.8 0.0 copy-start.6
  3.8 1.0 %copy-done.6 = bf16[256,1024]{1,0:T(8,128)(2,1)S(1)} copy-done((bf16[256,1024]{1,0:T(8,128)(2,1)S(1)}, bf16[256,1024]{1,0:T(8,128)(2,1)}, u32[]{:S(2)}) %copy-start.6) | copy-done | bytes 524312
  4.8 1.9 %pack_signals.1 = bf16[32,64,256]{2,1,0:T(8,128)(2,1)} custom-call(bf16[256,1024]{1,0:T(8,128)(2,1)S(1)} %copy-done.2, bf16[256,1024]{1,0:T(8,128)(2,1)S(1)} %copy-done.4, bf16[256,1024]{1,0:T(8,128)(2,1)S(1)} %copy-done.6, bf16[256,1024]{1,0:T(8,128)(2,1)S(1)} %copy-done), custom_call_target="tpu_custom_call" | custom-call | tf_op jit(solution)/shard_map/pack_signals/pallas_call | solution.py:80
  6.8 0.0 copy-start.9
  6.8 0.0 copy-start.10
  6.8 0.0 copy-start.3
  6.8 0.0 copy-start.5
  6.8 0.0 copy-start.7
  6.8 7.3 %all-to-all-start = ((bf16[32,64,256]{2,1,0:T(8,128)(2,1)}), bf16[32,64,256]{2,1,0:T(8,128)(2,1)S(1)}, u32[]{:S(2)}, u32[]{:S(2)}) async-start(bf16[32,64,256]{2,1,0:T(8,128)(2,1)} %pack_signals.1), calls=%async_computation | async-start | bytes 2097152 | tf_op jit(solution)/shard_map/all_to_all | solution.py:337
  14.1 0.0 copy-done.9
  14.1 0.0 copy-done.10
  14.1 0.0 copy-start.1
  14.2 0.1 broadcast_in_dim.15
  14.3 0.0 copy-done.3
  14.3 0.0 copy-done.5
  14.3 0.0 copy-done.7
  14.3 0.9 %copy-done.1 = bf16[256,1024]{1,0:T(8,128)(2,1)S(1)} copy-done((bf16[256,1024]{1,0:T(8,128)(2,1)S(1)}, bf16[256,1024]{1,0:T(8,128)(2,1)}, u32[]{:S(2)}) %copy-start.1) | copy-done | bytes 524312
  15.2 3.8 %block_states.1 = (f32[16,8,128]{2,1,0:T(8,128)S(1)}, f32[16,8,128]{2,1,0:T(8,128)S(1)}) custom-call(bf16[256,1024]{1,0:T(8,128)(2,1)S(1)} %copy-done.1, bf16[256,1024]{1,0:T(8,128)(2,1)S(1)} %copy-done.3, bf16[256,1024]{1,0:T(8,128)(2,1)S(1)} %copy-done.5, bf16[256,1024]{1,0:T(8,128)(2,1)S(1)} %copy-done.7, f32[3,16,8,128]{3,2,1,0:T(8,128)S(1)} %bitcast.14), custom_call_target="tpu_custom_call" | custom-call | flops 16777216 | bytes 2097152 | tf_op jit(solution)/shard_map/block_states/pallas_call | solution.py:133
  19.0 0.6 convert_element_type.49
  19.6 1.3 %collective-permute-start.5 = (bf16[16,8,128]{2,1,0:T(8,128)(2,1)}, bf16[16,8,128]{2,1,0:T(8,128)(2,1)S(1)}, u32[]{:S(2)}, u32[]{:S(2)}) collective-permute-start(bf16[16,8,128]{2,1,0:T(8,128)(2,1)} %convert_element_type.49), channel_id=1, source_target_pairs={{8,0},{12,4},{16,8},{20,12},{24,16},{28,20},{9,1},{13,5},{17,9},{2... | collective-permute-start | bytes 98312 | tf_op jit(solution)/shard_map/ppermute | solution.py:154
  20.9 1.3 %collective-permute-start.4 = (bf16[16,8,128]{2,1,0:T(8,128)(2,1)}, bf16[16,8,128]{2,1,0:T(8,128)(2,1)S(1)}, u32[]{:S(2)}, u32[]{:S(2)}) collective-permute-start(bf16[16,8,128]{2,1,0:T(8,128)(2,1)} %convert_element_type.49), channel_id=1, source_target_pairs={{4,0},{8,4},{12,8},{16,12},{20,16},{24,20},{28,24},{5,1},{9,5},{13... | collective-permute-start | bytes 98312 | tf_op jit(solution)/shard_map/ppermute | solution.py:154
  22.2 0.6 convert_element_type.42
  22.8 5.7 %collective-permute-start.1 = (bf16[16,8,128]{2,1,0:T(8,128)(2,1)}, bf16[16,8,128]{2,1,0:T(8,128)(2,1)S(1)}, u32[]{:S(2)}, u32[]{:S(2)}) collective-permute-start(bf16[16,8,128]{2,1,0:T(8,128)(2,1)} %convert_element_type.42), channel_id=1, source_target_pairs={{0,8},{4,12},{8,16},{12,20},{16,24},{20,28},{1,9},{5,13},{9,17},{1... | collective-permute-start | bytes 98312 | tf_op jit(solution)/shard_map/ppermute | solution.py:154
  28.5 3.3 %collective-permute-start = (bf16[16,8,128]{2,1,0:T(8,128)(2,1)}, bf16[16,8,128]{2,1,0:T(8,128)(2,1)S(1)}, u32[]{:S(2)}, u32[]{:S(2)}) collective-permute-start(bf16[16,8,128]{2,1,0:T(8,128)(2,1)} %convert_element_type.42), channel_id=1, source_target_pairs={{0,4},{4,8},{8,12},{12,16},{16,20},{20,24},{24,28},{1,5},{5,9},{9,... | collective-permute-start | bytes 98312 | tf_op jit(solution)/shard_map/ppermute | solution.py:154
  31.9 0.0 collective-permute-done.5
  31.9 0.0 collective-permute-done.4
  31.9 0.6 collective-permute-done.1
  32.6 1.2 %collective-permute-done = bf16[16,8,128]{2,1,0:T(8,128)(2,1)S(1)} collective-permute-done((bf16[16,8,128]{2,1,0:T(8,128)(2,1)}, bf16[16,8,128]{2,1,0:T(8,128)(2,1)S(1)}, u32[]{:S(2)}, u32[]{:S(2)}) %collective-permute-start) | collective-permute-done | bytes 32800 | tf_op jit(solution)/shard_map/ppermute | solution.py:154
  33.8 1.3 %collective-permute-start.6 = (bf16[16,8,128]{2,1,0:T(8,128)(2,1)S(1)}, bf16[16,8,128]{2,1,0:T(8,128)(2,1)S(1)}, u32[]{:S(2)}, u32[]{:S(2)}) collective-permute-start(bf16[16,8,128]{2,1,0:T(8,128)(2,1)S(1)} %get-tuple-element.34), channel_id=1, source_target_pairs={{8,0},{12,4},{16,8},{20,12},{24,16},{28,20},{9,1},{13,5},{17,9},{2... | collective-permute-start | bytes 98312 | tf_op jit(solution)/shard_map/ppermute | solution.py:154
  35.1 10.7 %collective-permute-start.2 = (bf16[16,8,128]{2,1,0:T(8,128)(2,1)S(1)}, bf16[16,8,128]{2,1,0:T(8,128)(2,1)S(1)}, u32[]{:S(2)}, u32[]{:S(2)}) collective-permute-start(bf16[16,8,128]{2,1,0:T(8,128)(2,1)S(1)} %get-tuple-element.35), channel_id=1, source_target_pairs={{0,8},{4,12},{8,16},{12,20},{16,24},{20,28},{1,9},{5,13},{9,17},{1... | collective-permute-start | bytes 98312 | tf_op jit(solution)/shard_map/ppermute | solution.py:154
  45.9 0.0 collective-permute-done.6
  45.9 1.6 %collective-permute-done.2 = bf16[16,8,128]{2,1,0:T(8,128)(2,1)S(1)} collective-permute-done((bf16[16,8,128]{2,1,0:T(8,128)(2,1)S(1)}, bf16[16,8,128]{2,1,0:T(8,128)(2,1)S(1)}, u32[]{:S(2)}, u32[]{:S(2)}) %collective-permute-start.2) | collective-permute-done | bytes 32800 | tf_op jit(solution)/shard_map/ppermute | solution.py:154
  47.5 1.3 %collective-permute-start.7 = (bf16[16,8,128]{2,1,0:T(8,128)(2,1)S(1)}, bf16[16,8,128]{2,1,0:T(8,128)(2,1)S(1)}, u32[]{:S(2)}, u32[]{:S(2)}) collective-permute-start(bf16[16,8,128]{2,1,0:T(8,128)(2,1)S(1)} %get-tuple-element.32), channel_id=1, source_target_pairs={{16,0},{20,4},{24,8},{28,12},{17,1},{21,5},{25,9},{29,13},{18,2},{... | collective-permute-start | bytes 98312 | tf_op jit(solution)/shard_map/ppermute | solution.py:154
  48.8 5.7 %collective-permute-start.3 = (bf16[16,8,128]{2,1,0:T(8,128)(2,1)S(1)}, bf16[16,8,128]{2,1,0:T(8,128)(2,1)S(1)}, u32[]{:S(2)}, u32[]{:S(2)}) collective-permute-start(bf16[16,8,128]{2,1,0:T(8,128)(2,1)S(1)} %get-tuple-element.33), channel_id=1, source_target_pairs={{0,16},{4,20},{8,24},{12,28},{1,17},{5,21},{9,25},{13,29},{2,18},{... | collective-permute-start | bytes 98312 | tf_op jit(solution)/shard_map/ppermute | solution.py:154
  54.5 0.0 collective-permute-done.7
  54.5 1.6 %collective-permute-done.3 = bf16[16,8,128]{2,1,0:T(8,128)(2,1)S(1)} collective-permute-done((bf16[16,8,128]{2,1,0:T(8,128)(2,1)S(1)}, bf16[16,8,128]{2,1,0:T(8,128)(2,1)S(1)}, u32[]{:S(2)}, u32[]{:S(2)}) %collective-permute-start.3) | collective-permute-done | bytes 32800 | tf_op jit(solution)/shard_map/ppermute | solution.py:154
  56.1 0.0 copy-start.8
  56.1 0.1 multiply_add_fusion
  56.1 0.6 copy-done.8
  56.8 4.4 %conv_outputs.1 = bf16[256,1024]{1,0:T(8,128)(2,1)} custom-call(bf16[256,1024]{1,0:T(8,128)(2,1)S(1)} %copy-done.1, bf16[256,1024]{1,0:T(8,128)(2,1)S(1)} %copy-done.3, bf16[256,1024]{1,0:T(8,128)(2,1)S(1)} %copy-done.5, f32[3,16,8,128]{3,2,1,0:T(8,128)S(1)} %bitcast.15, f32[1,1024]{1,0:T(1,128)S(1)} %bitcast.17, f32[16,8,128]{2,1,0:T(8,128)S(1)} %get-tuple-element.31.before_ref), custom_call_target="tpu_custom_call" | custom-call | flops 16777216 | bytes 2097152 | tf_op jit(solution)/shard_map/conv_outputs/pallas_call | solution.py:216
  61.1 0.0 all-to-all-done.refs_0_
  61.1 6.3 %filter_lags.1 = f32[8,8,256]{2,1,0:T(8,128)} custom-call(bf16[32,64,256]{2,1,0:T(8,128)(2,1)S(1)} %all-to-all-done.refs_0_), custom_call_target="tpu_custom_call" | custom-call | tf_op jit(solution)/shard_map/filter_lags/pallas_call | solution.py:312
  67.4 7.3 %all-to-all-start.1 = ((f32[8,8,256]{2,1,0:T(8,128)}), f32[8,8,256]{2,1,0:T(8,128)S(1)}, u32[]{:S(2)}, u32[]{:S(2)}) async-start(f32[8,8,256]{2,1,0:T(8,128)} %filter_lags.1), calls=%async_computation.1 | async-start | bytes 131072 | tf_op jit(solution)/shard_map/all_to_all | solution.py:364
  74.7 6.8 %grad_outputs.1 = (bf16[256,1024]{1,0:T(8,128)(2,1)}, bf16[256,1024]{1,0:T(8,128)(2,1)}) custom-call(bf16[256,1024]{1,0:T(8,128)(2,1)S(1)} %copy-done.1, bf16[256,1024]{1,0:T(8,128)(2,1)S(1)} %copy-done.3, bf16[256,1024]{1,0:T(8,128)(2,1)S(1)} %copy-done.5, bf16[256,1024]{1,0:T(8,128)(2,1)S(1)} %copy-done.7, f32[3,16,8,128]{3,2,1,0:T(8,128)S(1)} %bitcast.16, ...), custom_call_target="tpu_custom_call" | custom-call | flops 16777216 | bytes 2097152 | tf_op jit(solution)/shard_map/grad_outputs/pallas_call | solution.py:216
  81.4 0.1 all-to-all-done.1
  81.6 0.6 copy.12
  (8 shorter events, 0.2 us)
Async XLA Ops:
  0.6 1.0 %copy-start = (bf16[256,1024]{1,0:T(8,128)(2,1)S(1)}, bf16[256,1024]{1,0:T(8,128)(2,1)}, u32[]{:S(2)}) copy-start(bf16[256,1024]{1,0:T(8,128)(2,1)} %q_ref.2) | copy-start | bytes 1572868
  1.7 1.0 %copy-start.2 = (bf16[256,1024]{1,0:T(8,128)(2,1)S(1)}, bf16[256,1024]{1,0:T(8,128)(2,1)}, u32[]{:S(2)}) copy-start(bf16[256,1024]{1,0:T(8,128)(2,1)} %k_ref.2) | copy-start | bytes 1572868
  2.7 1.0 %copy-start.4 = (bf16[256,1024]{1,0:T(8,128)(2,1)S(1)}, bf16[256,1024]{1,0:T(8,128)(2,1)}, u32[]{:S(2)}) copy-start(bf16[256,1024]{1,0:T(8,128)(2,1)} %v_ref.2) | copy-start | bytes 1572868
  3.8 1.0 %copy-start.6 = (bf16[256,1024]{1,0:T(8,128)(2,1)S(1)}, bf16[256,1024]{1,0:T(8,128)(2,1)}, u32[]{:S(2)}) copy-start(bf16[256,1024]{1,0:T(8,128)(2,1)} %o_ref.1) | copy-start | bytes 1572868
  6.8 7.4 %copy-start.9 = (f32[256,16]{0,1:T(8,128)S(1)}, f32[256,16]{0,1:T(8,128)}, u32[]{:S(2)}) copy-start(f32[256,16]{0,1:T(8,128)} %param.12) | copy-start | bytes 49156
  6.8 7.4 %copy-start.10 = (f32[256,16]{0,1:T(8,128)S(1)}, f32[256,16]{0,1:T(8,128)}, u32[]{:S(2)}) copy-start(f32[256,16]{0,1:T(8,128)} %param.11) | copy-start | bytes 49156
  6.8 7.5 %copy-start.3 = (bf16[256,1024]{1,0:T(8,128)(2,1)S(1)}, bf16[256,1024]{1,0:T(8,128)(2,1)}, u32[]{:S(2)}) copy-start(bf16[256,1024]{1,0:T(8,128)(2,1)} %k_ref.2) | copy-start | bytes 1572868
  6.8 7.5 %copy-start.5 = (bf16[256,1024]{1,0:T(8,128)(2,1)S(1)}, bf16[256,1024]{1,0:T(8,128)(2,1)}, u32[]{:S(2)}) copy-start(bf16[256,1024]{1,0:T(8,128)(2,1)} %v_ref.2) | copy-start | bytes 1572868
  6.8 7.5 %copy-start.7 = (bf16[256,1024]{1,0:T(8,128)(2,1)S(1)}, bf16[256,1024]{1,0:T(8,128)(2,1)}, u32[]{:S(2)}) copy-start(bf16[256,1024]{1,0:T(8,128)(2,1)} %o_ref.1) | copy-start | bytes 1572868
  6.8 54.3 %all-to-all-start = ((bf16[32,64,256]{2,1,0:T(8,128)(2,1)}), bf16[32,64,256]{2,1,0:T(8,128)(2,1)S(1)}, u32[]{:S(2)}, u32[]{:S(2)}) async-start(bf16[32,64,256]{2,1,0:T(8,128)(2,1)} %pack_signals.1), calls=%async_computation | async-start | bytes 2097152 | tf_op jit(solution)/shard_map/all_to_all | solution.py:337
  14.1 1.0 %copy-start.1 = (bf16[256,1024]{1,0:T(8,128)(2,1)S(1)}, bf16[256,1024]{1,0:T(8,128)(2,1)}, u32[]{:S(2)}) copy-start(bf16[256,1024]{1,0:T(8,128)(2,1)} %q_ref.2) | copy-start | bytes 1572868
  19.6 12.3 %collective-permute-start.5 = (bf16[16,8,128]{2,1,0:T(8,128)(2,1)}, bf16[16,8,128]{2,1,0:T(8,128)(2,1)S(1)}, u32[]{:S(2)}, u32[]{:S(2)}) collective-permute-start(bf16[16,8,128]{2,1,0:T(8,128)(2,1)} %convert_element_type.49), channel_id=1, source_target_pairs={{8,0},{12,4},{16,8},{20,12},{24,16},{28,20},{9,1},{13,5},{17,9},{2... | collective-permute-start | bytes 98312 | tf_op jit(solution)/shard_map/ppermute | solution.py:154
  20.9 11.1 %collective-permute-start.4 = (bf16[16,8,128]{2,1,0:T(8,128)(2,1)}, bf16[16,8,128]{2,1,0:T(8,128)(2,1)S(1)}, u32[]{:S(2)}, u32[]{:S(2)}) collective-permute-start(bf16[16,8,128]{2,1,0:T(8,128)(2,1)} %convert_element_type.49), channel_id=1, source_target_pairs={{4,0},{8,4},{12,8},{16,12},{20,16},{24,20},{28,24},{5,1},{9,5},{13... | collective-permute-start | bytes 98312 | tf_op jit(solution)/shard_map/ppermute | solution.py:154
  22.8 9.8 %collective-permute-start.1 = (bf16[16,8,128]{2,1,0:T(8,128)(2,1)}, bf16[16,8,128]{2,1,0:T(8,128)(2,1)S(1)}, u32[]{:S(2)}, u32[]{:S(2)}) collective-permute-start(bf16[16,8,128]{2,1,0:T(8,128)(2,1)} %convert_element_type.42), channel_id=1, source_target_pairs={{0,8},{4,12},{8,16},{12,20},{16,24},{20,28},{1,9},{5,13},{9,17},{1... | collective-permute-start | bytes 98312 | tf_op jit(solution)/shard_map/ppermute | solution.py:154
  28.5 5.2 %collective-permute-start = (bf16[16,8,128]{2,1,0:T(8,128)(2,1)}, bf16[16,8,128]{2,1,0:T(8,128)(2,1)S(1)}, u32[]{:S(2)}, u32[]{:S(2)}) collective-permute-start(bf16[16,8,128]{2,1,0:T(8,128)(2,1)} %convert_element_type.42), channel_id=1, source_target_pairs={{0,4},{4,8},{8,12},{12,16},{16,20},{20,24},{24,28},{1,5},{5,9},{9,... | collective-permute-start | bytes 98312 | tf_op jit(solution)/shard_map/ppermute | solution.py:154
  33.8 12.1 %collective-permute-start.6 = (bf16[16,8,128]{2,1,0:T(8,128)(2,1)S(1)}, bf16[16,8,128]{2,1,0:T(8,128)(2,1)S(1)}, u32[]{:S(2)}, u32[]{:S(2)}) collective-permute-start(bf16[16,8,128]{2,1,0:T(8,128)(2,1)S(1)} %get-tuple-element.34), channel_id=1, source_target_pairs={{8,0},{12,4},{16,8},{20,12},{24,16},{28,20},{9,1},{13,5},{17,9},{2... | collective-permute-start | bytes 98312 | tf_op jit(solution)/shard_map/ppermute | solution.py:154
  35.1 12.3 %collective-permute-start.2 = (bf16[16,8,128]{2,1,0:T(8,128)(2,1)S(1)}, bf16[16,8,128]{2,1,0:T(8,128)(2,1)S(1)}, u32[]{:S(2)}, u32[]{:S(2)}) collective-permute-start(bf16[16,8,128]{2,1,0:T(8,128)(2,1)S(1)} %get-tuple-element.35), channel_id=1, source_target_pairs={{0,8},{4,12},{8,16},{12,20},{16,24},{20,28},{1,9},{5,13},{9,17},{1... | collective-permute-start | bytes 98312 | tf_op jit(solution)/shard_map/ppermute | solution.py:154
  47.5 7.0 %collective-permute-start.7 = (bf16[16,8,128]{2,1,0:T(8,128)(2,1)S(1)}, bf16[16,8,128]{2,1,0:T(8,128)(2,1)S(1)}, u32[]{:S(2)}, u32[]{:S(2)}) collective-permute-start(bf16[16,8,128]{2,1,0:T(8,128)(2,1)S(1)} %get-tuple-element.32), channel_id=1, source_target_pairs={{16,0},{20,4},{24,8},{28,12},{17,1},{21,5},{25,9},{29,13},{18,2},{... | collective-permute-start | bytes 98312 | tf_op jit(solution)/shard_map/ppermute | solution.py:154
  48.8 7.3 %collective-permute-start.3 = (bf16[16,8,128]{2,1,0:T(8,128)(2,1)S(1)}, bf16[16,8,128]{2,1,0:T(8,128)(2,1)S(1)}, u32[]{:S(2)}, u32[]{:S(2)}) collective-permute-start(bf16[16,8,128]{2,1,0:T(8,128)(2,1)S(1)} %get-tuple-element.33), channel_id=1, source_target_pairs={{0,16},{4,20},{8,24},{12,28},{1,17},{5,21},{9,25},{13,29},{2,18},{... | collective-permute-start | bytes 98312 | tf_op jit(solution)/shard_map/ppermute | solution.py:154
  56.1 0.7 copy-start.8
  67.4 14.2 %all-to-all-start.1 = ((f32[8,8,256]{2,1,0:T(8,128)}), f32[8,8,256]{2,1,0:T(8,128)S(1)}, u32[]{:S(2)}, u32[]{:S(2)}) async-start(f32[8,8,256]{2,1,0:T(8,128)} %filter_lags.1), calls=%async_computation.1 | async-start | bytes 131072 | tf_op jit(solution)/shard_map/all_to_all | solution.py:364

commit v3 on v2

--- a/solution.py
+++ b/solution.py
@@ -13,7 +13,7 @@
 LANES = 128
 SUBLANES = 8
 VMEM_BYTES = 48 * 1024 * 1024
-PACK_VMEM_BYTES = 24 * 1024 * 1024
+PACK_VMEM_BYTES = 62 * 1024 * 1024
 F32 = jnp.float32
 BF16 = jnp.bfloat16
 LINK = jnp.bfloat16
@@ -30,15 +30,33 @@
 
 
 def pack_kernel(shards, chans, owned, *refs):
-    hbm_refs, send_ref, held, sems = refs[:4], refs[4], refs[5], refs[6]
+    hbm_refs, send_ref, held, packed, in_sems, out_sems = refs[:4], *refs[4:]
     tok_rows, width = held.shape[1:]
     groups = width // FILTERS
     per_chan = FILTERS // chans
-    copies = [
-        pltpu.make_async_copy(hbm_refs[i], held.at[i], sems.at[i]) for i in range(len(hbm_refs))
-    ]
-    for copy in copies:
-        copy.start()
+    parts = tok_rows // LANES
+    rows = groups * owned
+
+    def arrival(i, part):
+        place = pl.ds(part * LANES, LANES)
+        return pltpu.make_async_copy(
+            hbm_refs[i].at[place, :], held.at[i, place, :], in_sems.at[i, part]
+        )
+
+    def departure(which, part):
+        lanes = pl.ds(part * LANES, LANES)
+        if owned % SUBLANES:
+            place = (which, slice(None), slice(None), lanes)
+        else:
+            place = (slice(None), pl.ds(which * rows, rows), lanes)
+        return pltpu.make_async_copy(
+            packed.at[place], send_ref.at[place], out_sems.at[which, part]
+        )
+
+    units = [(which, part) for which in range(2) for part in range(parts)]
+    for which, part in units:
+        for i in (2 * which, 2 * which + 1):
+            arrival(i, part).start()
 
     def owned_filter(row):
         seq = row // (chans * owned)
@@ -46,45 +64,51 @@
         return chan * per_chan + seq * owned + row % owned
 
     order = one_hot(FILTERS, FILTERS, owned_filter)
-    for which in range(2):
-        copies[2 * which].wait()
-        copies[2 * which + 1].wait()
-        signal = product(held[2 * which], held[2 * which + 1])
-        parts = []
+    for which, part in units:
+        for i in (2 * which, 2 * which + 1):
+            arrival(i, part).wait()
+        place = slice(part * LANES, (part + 1) * LANES)
+        signal = product(held[2 * which, place, :], held[2 * which + 1, place, :])
+        pieces = []
         for group in range(groups):
-            part = lax.dot_general(
+            piece = lax.dot_general(
                 order,
                 signal[:, group * FILTERS : (group + 1) * FILTERS],
                 (((1,), (1,)), ((), ())),
                 preferred_element_type=F32,
             )
             if owned % SUBLANES:
-                send_ref[which, group] = part.astype(BF16)
+                packed[which, group, :, place] = piece.astype(BF16)
             else:
-                parts.append(part.reshape(shards * chans, owned, tok_rows))
-        if parts:
-            rows = groups * owned
-            send_ref[:, which * rows : (which + 1) * rows, :] = jnp.concatenate(
-                parts, axis=1
+                pieces.append(piece.reshape(shards * chans, owned, LANES))
+        if pieces:
+            packed[:, which * rows : (which + 1) * rows, place] = jnp.concatenate(
+                pieces, axis=1
             ).astype(BF16)
+        departure(which, part).start()
+    for which, part in units:
+        departure(which, part).wait()
 
 
 def pack_signals(shards, chans, owned, query_proj, key_proj, value_proj, out_grad):
     tok_rows, width = key_proj.shape
     groups = width // FILTERS
     dests = shards * chans
+    parts = tok_rows // LANES
     if owned % SUBLANES:
         shape = (2, groups, FILTERS, tok_rows)
     else:
         shape = (dests, 2 * groups * owned, tok_rows)
     send = pl.pallas_call(
         functools.partial(pack_kernel, shards, chans, owned),
-        in_specs=[pl.BlockSpec(memory_space=pltpu.HBM)] * 4,
-        out_specs=pl.BlockSpec(memory_space=pltpu.VMEM),
+        in_specs=[pl.BlockSpec(memory_space=pl.ANY)] * 4,
+        out_specs=pl.BlockSpec(memory_space=pl.ANY),
         out_shape=jax.ShapeDtypeStruct(shape, BF16),
         scratch_shapes=[
             pltpu.VMEM((4, tok_rows, width), BF16),
-            pltpu.SemaphoreType.DMA((4,)),
+            pltpu.VMEM(shape, BF16),
+            pltpu.SemaphoreType.DMA((4, parts)),
+            pltpu.SemaphoreType.DMA((2, parts)),
         ],
         compiler_params=pltpu.CompilerParams(vmem_limit_bytes=PACK_VMEM_BYTES),
         name="pack_signals",
@@ -95,10 +119,12 @@
     return send
 
 
-def state_kernel(q_ref, k_ref, v_ref, o_ref, coef_ref, ahead_ref, behind_ref, x_ref, g_ref):
+def state_kernel(seq_ref, q_ref, k_ref, v_ref, o_ref, coef_ref, *refs):
+    state_refs, x_ref, g_ref = refs[:-2], refs[-2], refs[-1]
     tok_rows, width = k_ref.shape
     tiles = width // LANES
     modes = coef_ref.shape[1]
+    shards = len(state_refs) + 1
     spread_tokens(k_ref, v_ref, x_ref)
     spread_tokens(o_ref, q_ref, g_ref)
     decay = [coef_ref[0, m] for m in range(modes)]
@@ -112,9 +138,18 @@
 
     zero = tuple(jnp.zeros((tiles, LANES), F32) for _ in range(modes))
     ahead, behind = lax.fori_loop(0, tok_rows, step, (zero, zero), unroll=8)
-    for m in range(modes):
-        ahead_ref[m] = ahead[m].astype(ahead_ref.dtype)
-        behind_ref[m] = behind[m].astype(behind_ref.dtype)
+    ahead = jnp.concatenate(ahead, axis=0).astype(LINK)
+    behind = jnp.concatenate(behind, axis=0).astype(LINK)
+    for k in range(1, shards):
+        stays = seq_ref[0] + k < shards
+
+        @pl.when(stays)
+        def _():
+            state_refs[k - 1][...] = ahead
+
+        @pl.when(jnp.logical_not(stays))
+        def _():
+            state_refs[k - 1][...] = behind
 
 
 def spread_tokens(a_ref, b_ref, x_ref):
@@ -126,41 +161,45 @@
         ).astype(F32)
 
 
-def block_states(query_proj, key_proj, value_proj, out_grad, coefs):
+def block_states(seq_index, shards, query_proj, key_proj, value_proj, out_grad, coefs):
     tok_rows, width = key_proj.shape
     tiles = width // LANES
     modes = coefs.shape[1]
+    whole = pl.BlockSpec(memory_space=pltpu.VMEM)
     return pl.pallas_call(
         state_kernel,
-        out_shape=[jax.ShapeDtypeStruct((modes, tiles, LANES), F32)] * 2,
+        in_specs=[pl.BlockSpec(memory_space=pltpu.SMEM)] + [whole] * 5,
+        out_specs=[whole] * (shards - 1),
+        out_shape=[jax.ShapeDtypeStruct((modes * tiles, LANES), LINK)] * (shards - 1),
         scratch_shapes=[pltpu.VMEM((tok_rows * tiles, LANES), F32)] * 2,
         compiler_params=pltpu.CompilerParams(vmem_limit_bytes=VMEM_BYTES),
         cost_estimate=pl.CostEstimate(
             flops=4 * modes * tok_rows * width, bytes_accessed=8 * tok_rows * width, transcendentals=0
         ),
         name="block_states",
-    )(query_proj, key_proj, value_proj, out_grad, coefs)
-
-
-def blocks_before(state, block_decay, move):
-    shards = lax.axis_size("seq")
-
-    def shift(value, count):
-        route = [
-            (i, i + move * count) for i in range(shards) if 0 <= i + move * count < shards
+    )(seq_index, query_proj, key_proj, value_proj, out_grad, coefs)
+
+
+def exchange_states(states):
+    shards = len(states) + 1
+    return [
+        lax.ppermute(states[k - 1], "seq", [(i, (i + k) % shards) for i in range(shards)])
+        for k in range(1, shards)
+    ]
+
+
+def edge_states(seq, state_refs, coef_ref, later):
+    shards = len(state_refs) + 1
+    modes, tiles = coef_ref.shape[1:3]
+    held = [jnp.zeros((tiles, LANES), F32) for _ in range(modes)]
+    count = shards - 1 - seq if later else seq
+    for k in range(shards - 1, 0, -1):
+        ref = state_refs[shards - k - 1 if later else k - 1]
+        block = jnp.where(k <= count, ref[...].astype(F32), 0.0)
+        held = [
+            coef_ref[1, m] * held[m] + block[m * tiles : (m + 1) * tiles] for m in range(modes)
         ]
-        if not route:
-            return jnp.zeros_like(value)
-        return lax.ppermute(value, "seq", route)
-
-    sent = state.astype(LINK)
-    total = shift(sent, 1).astype(F32) + block_decay * shift(sent, 2).astype(F32)
-    span = 2
-    while span < shards - 1:
-        block_decay = block_decay * block_decay
-        total = total + block_decay * shift(total.astype(LINK), span).astype(F32)
-        span *= 2
-    return total
+    return held
 
 
 def walk_tokens(ref, held, coef_ref, tok_rows, tiles, start, move):
@@ -178,14 +217,16 @@
         ref[rows, :] = terms[0]
         return held
 
-    lax.fori_loop(0, tok_rows, step, tuple(held[m] for m in range(modes)), unroll=8)
-
-
-def conv_kernel(q_ref, k_ref, v_ref, coef_ref, gain_ref, before_ref, layer_ref, x_ref):
+    lax.fori_loop(0, tok_rows, step, tuple(held), unroll=8)
+
+
+def conv_kernel(seq_ref, q_ref, k_ref, v_ref, coef_ref, gain_ref, *refs):
+    state_refs, layer_ref, x_ref = refs[:-2], refs[-2], refs[-1]
     tok_rows, width = k_ref.shape
     tiles = width // LANES
     spread_tokens(k_ref, v_ref, x_ref)
-    walk_tokens(x_ref, before_ref, coef_ref, tok_rows, tiles, 0, 1)
+    held = edge_states(seq_ref[0], state_refs, coef_ref, False)
+    walk_tokens(x_ref, held, coef_ref, tok_rows, tiles, 0, 1)
     for tile in range(tiles):
         cols = slice(tile * LANES, (tile + 1) * LANES)
         rows = slice(tile * tok_rows, (tile + 1) * tok_rows)
@@ -194,13 +235,13 @@
         layer_ref[:, cols] = (q_ref[:, cols].astype(F32) * long_conv).astype(BF16)
 
 
-def grad_kernel(
-    q_ref, k_ref, v_ref, o_ref, coef_ref, gain_ref, after_ref, key_ref, value_ref, g_ref
-):
+def grad_kernel(seq_ref, q_ref, k_ref, v_ref, o_ref, coef_ref, gain_ref, *refs):
+    state_refs, key_ref, value_ref, g_ref = refs[:-3], *refs[-3:]
     tok_rows, width = k_ref.shape
     tiles = width // LANES
     spread_tokens(o_ref, q_ref, g_ref)
-    walk_tokens(g_ref, after_ref, coef_ref, tok_rows, tiles, tok_rows - 1, -1)
+    held = edge_states(seq_ref[0], state_refs, coef_ref, True)
+    walk_tokens(g_ref, held, coef_ref, tok_rows, tiles, tok_rows - 1, -1)
     for tile in range(tiles):
         cols = slice(tile * LANES, (tile + 1) * LANES)
         rows = slice(tile * tok_rows, (tile + 1) * tok_rows)
@@ -210,11 +251,15 @@
         value_ref[:, cols] = (conv_grad * k_ref[:, cols].astype(F32)).astype(BF16)
 
 
-def local_outputs(kernel, count, name, *args):
-    tok_rows, width = args[0].shape
-    modes, tiles = args[-1].shape[:2]
+def local_outputs(kernel, count, name, seq_index, signals, coefs, gain, states):
+    tok_rows, width = signals[0].shape
+    modes, tiles = coefs.shape[1:3]
+    args = (*signals, coefs, gain, *states)
+    whole = pl.BlockSpec(memory_space=pltpu.VMEM)
     return pl.pallas_call(
         kernel,
+        in_specs=[pl.BlockSpec(memory_space=pltpu.SMEM)] + [whole] * len(args),
+        out_specs=[whole] * count,
         out_shape=[jax.ShapeDtypeStruct((tok_rows, width), BF16)] * count,
         scratch_shapes=[pltpu.VMEM((tok_rows * tiles, LANES), F32)],
         compiler_params=pltpu.CompilerParams(vmem_limit_bytes=VMEM_BYTES),
@@ -222,11 +267,11 @@
             flops=4 * modes * tok_rows * width, bytes_accessed=8 * tok_rows * width, transcendentals=0
         ),
         name=name,
-    )(*args)
+    )(seq_index, *args)
 
 
 def lag_kernel(shards, chans, groups, owned, scale, *refs):
-    in_refs, out_ref, u_all, g_all = refs[:-3], refs[-3], refs[-2], refs[-1]
+    in_refs, out_ref, u_all, g_all, turned_all = refs[:-4], *refs[-4:]
     tok_rows = out_ref.shape[2]
     halves = tok_rows // LANES
     blocks = shards * halves
@@ -260,21 +305,22 @@
     batch = min(blocks, 16)
 
     def one_filter(f, _):
-        turned = lax.dot_general(
-            mirror, u_all[f], (((1,), (1,)), ((), ())), preferred_element_type=F32
-        ).astype(BF16)
+        turned = turned_all[f]
 
         def some_lags(first):
             tables = []
             for d in range(0, batch, 2):
+                live = full
+                if batch == blocks:
+                    live = min(full, -(-(blocks - d) * depth // LANES) * LANES)
                 pair = jnp.concatenate(
                     [
-                        g_all[f, pl.ds(pl.multiple_of((first + d + e) * depth, depth), full), :]
+                        g_all[f, pl.ds(pl.multiple_of((first + d + e) * depth, depth), live), :]
                         for e in range(2)
                     ],
                     axis=1,
                 )
-                table = jnp.dot(turned, pair, preferred_element_type=F32)
+                table = jnp.dot(turned[:, :live], pair, preferred_element_type=F32)
                 tables += [table[:, :LANES], table[:, LANES:]]
             last = g_all[f, pl.ds(pl.multiple_of((first + batch) * depth, depth), full), :]
             if batch < blocks:
@@ -295,7 +341,11 @@
             lax.fori_loop(0, blocks // batch, lambda i, c: (some_lags(i * batch), c)[1], 0)
         return 0
 
-    lax.fori_loop(0, owned, one_filter, 0)
+    for f in range(owned):
+        turned_all[f] = lax.dot_general(
+            mirror, u_all[f], (((1,), (1,)), ((), ())), preferred_element_type=F32
+        ).astype(BF16)
+    lax.fori_loop(0, owned, one_filter, 0, unroll=min(owned, 2))
 
 
 def filter_lags(received, shards, chans, owned, scale):
@@ -315,6 +365,7 @@
         scratch_shapes=[
             pltpu.VMEM((owned, full, LANES), BF16),
             pltpu.VMEM((owned, 2 * full + depth, LANES), BF16),
+            pltpu.VMEM((owned, LANES, full), BF16),
         ],
         compiler_params=pltpu.CompilerParams(vmem_limit_bytes=VMEM_BYTES),
         name="filter_lags",
@@ -346,17 +397,15 @@
     coefs = coefs.transpose(0, 2, 1).reshape(3, modes, 1, FILTERS // LANES, LANES)
     coefs = jnp.broadcast_to(coefs, (3, modes, width // FILTERS, FILTERS // LANES, LANES))
     coefs = coefs.reshape(3, modes, width // LANES, LANES)
-    ahead, behind = block_states(*signals, coefs)
-    before = blocks_before(ahead, coefs[1], 1)
-    after = blocks_before(behind, coefs[1], -1)
-    query_proj, key_proj, value_proj, out_grad = signals
+    seq_index = lax.axis_index("seq").reshape(1)
+    states = exchange_states(block_states(seq_index, shards, *signals, coefs))
     gain = skip_gain[None, :]
     (layer_out,) = local_outputs(
-        conv_kernel, 1, "conv_outputs", query_proj, key_proj, value_proj, coefs, gain, before
+        conv_kernel, 1, "conv_outputs", seq_index, signals[:3], coefs, gain, states
     )
     received, layer_out = lax.optimization_barrier((received, layer_out))
     key_grad, value_grad = local_outputs(
-        grad_kernel, 2, "grad_outputs", *signals, coefs, gain, after
+        grad_kernel, 2, "grad_outputs", seq_index, signals, coefs, gain, states
     )
 
     scale = 1.0 / math.sqrt(length * (CHANNELS // FILTERS))

time: 82.9 us -> 66.8 us (0.81)
  starting transfers between devices: 45.2 us -> 24.1 us
  waiting for transfers between devices: 5.13 us -> 16.5 us
  local copies, waits for them, and re-layouts: 6.44 us -> 2.21 us
  other arithmetic: 1.39 us -> 0.02 us
    ppermute x8 -> x7, starting transfers between devices: 30.6 us -> 9.79 us  [exchange_states(): lax.ppermute(states[k - 1], 'seq', [(i, (i + k) % shards) for i in range(...]
    ppermute x8 -> x7, waiting for transfers between devices: 4.99 us -> 16.4 us  [exchange_states(): lax.ppermute(states[k - 1], 'seq', [(i, (i + k) % shards) for i in range(...]
    unnamed x23 -> x19, local copies, waits for them, and re-layouts: 6.33 us -> 2.13 us
    pallas_call x1, Pallas kernels: 6.29 us -> 4.53 us  [filter_lags(): pl.pallas_call(functools.partial(lag_kernel, shards, chans, groups, owned...]
    convert_element_type x4 -> x0, other arithmetic: 1.31 us -> none  [the longest x2 1.24 us: blocks_before(): sent = state.astype(LINK)]
    pallas_call x1, Pallas kernels: 1.94 us -> 3.11 us  [pack_signals(): pl.pallas_call(functools.partial(pack_kernel, shards, chans, owned), in_s...]
  transfers between devices with their start and end apart: 10 -> 9, of which waited for: 5 -> 3; matrix products, arithmetic and copies ran while one was open for 2% -> 0% of each run, Pallas kernels for 18% -> 23%
where the time goes in v3:
time: 66.8 us; the launch traced here: 66.4 us
  starting transfers between devices  24.1 us (36%)
  Pallas kernels  22.8 us (34%)
  waiting for transfers between devices  16.5 us (25%)
  local copies, waits for them, and re-layouts  2.21 us (3%)
  between operations  0.81 us (1%)
    ppermute x7, waiting for transfers between devices, exchange_states(): lax.ppermute(states[k - 1], 'seq', [(i, (i + k) % shards) for i in range(...  16.4 us
    pallas_call x2, Pallas kernels, local_outputs(): pl.pallas_call(kernel, in_specs=[pl.BlockSpec(memory_space=pltpu.SMEM)] +...  11.2 us
    ppermute x7, starting transfers between devices, exchange_states(): lax.ppermute(states[k - 1], 'seq', [(i, (i + k) % shards) for i in range(...  9.79 us
    all_to_all x1, starting transfers between devices, per_device(): lax.all_to_all(send, ('seq', 'chan'), split_axis=0, concat_axis=0, tiled=...  7.3 us
    all_to_all x1, starting transfers between devices, per_device(): lags = lax.all_to_all(lags, 'seq', split_axis=0, concat_axis=0, tiled=True)  7.05 us
    pallas_call x1, Pallas kernels, filter_lags(): pl.pallas_call(functools.partial(lag_kernel, shards, chans, groups, owned...  4.53 us
    pallas_call x1, Pallas kernels, block_states(): pl.pallas_call(state_kernel, in_specs=[pl.BlockSpec(memory_space=pltpu.SM...  3.92 us
    pallas_call x1, Pallas kernels, pack_signals(): pl.pallas_call(functools.partial(pack_kernel, shards, chans, owned), in_s...  3.11 us
  transfers between devices with their start and end apart: 9, of which 3 were waited for; matrix products, arithmetic and copies ran while one was open for 0% of the time, Pallas kernels for 23%

profile of v3, /device:TPU:0, one launch (start us, length us, event | category | flops | bytes accessed | tf_op | source)
XLA Modules:
  0.0 66.4 jit_solution(2815151990797413668)
XLA Ops:
  0.6 3.1 %pack_signals.1 = bf16[32,64,256]{2,1,0:T(8,128)(2,1)} custom-call(bf16[256,1024]{1,0:T(8,128)(2,1)} %k_ref.2, bf16[256,1024]{1,0:T(8,128)(2,1)} %v_ref.2, bf16[256,1024]{1,0:T(8,128)(2,1)} %o_ref.1, bf16[256,1024]{1,0:T(8,128)(2,1)} %q_ref.2), custom_call_target="tpu_custom_call" | custom-call | tf_op jit(solution)/shard_map/pack_signals/pallas_call | solution.py:102
  3.7 0.0 copy-start.7
  3.8 0.0 copy-start.8
  3.8 0.0 copy-start.1
  3.8 0.0 copy-start.2
  3.8 0.0 copy-start.3
  3.8 7.3 %all-to-all-start = ((bf16[32,64,256]{2,1,0:T(8,128)(2,1)}), bf16[32,64,256]{2,1,0:T(8,128)(2,1)S(1)}, u32[]{:S(2)}, u32[]{:S(2)}) async-start(bf16[32,64,256]{2,1,0:T(8,128)(2,1)} %pack_signals.1), calls=%async_computation | async-start | bytes 2097152 | tf_op jit(solution)/shard_map/all_to_all | solution.py:388
  11.1 0.0 copy-start
  11.1 0.0 copy-done.7
  11.1 0.0 copy-done.8
  11.2 0.1 broadcast_in_dim.11
  11.3 0.0 copy-done.1
  11.3 0.0 copy-done.2
  11.3 0.0 copy-done.3
  11.3 0.8 %copy-done = bf16[256,1024]{1,0:T(8,128)(2,1)S(1)} copy-done((bf16[256,1024]{1,0:T(8,128)(2,1)S(1)}, bf16[256,1024]{1,0:T(8,128)(2,1)}, u32[]{:S(2)}) %copy-start) | copy-done | bytes 524312
  12.2 3.9 %block_states.1 = (bf16[128,128]{1,0:T(8,128)(2,1)S(1)}, bf16[128,128]{1,0:T(8,128)(2,1)S(1)}, bf16[128,128]{1,0:T(8,128)(2,1)S(1)}, bf16[128,128]{1,0:T(8,128)(...) custom-call(s32[1]{0:T(128)} %bitcast.seq_ref, ...), custom_call_target="tpu_custom_call" | custom-call | flops 16777216 | bytes 2097152 | tf_op jit(solution)/shard_map/block_states/pallas_call | solution.py:169
  16.1 1.8 %collective-permute-start = (bf16[128,128]{1,0:T(8,128)(2,1)S(1)}, bf16[128,128]{1,0:T(8,128)(2,1)S(1)}, u32[]{:S(2)}, u32[]{:S(2)}) collective-permute-start(bf16[128,128]{1,0:T(8,128)(2,1)S(1)} %get-tuple-element.29), channel_id=1, source_target_pairs={{0,4},{4,8},{8,12},{12,16},{16,20},{20,24},{24,28},{28,0},{1,5},{5... | collective-permute-start | bytes 98312 | tf_op jit(solution)/shard_map/ppermute | solution.py:186
  17.9 1.5 %collective-permute-start.1 = (bf16[128,128]{1,0:T(8,128)(2,1)S(1)}, bf16[128,128]{1,0:T(8,128)(2,1)S(1)}, u32[]{:S(2)}, u32[]{:S(2)}) collective-permute-start(bf16[128,128]{1,0:T(8,128)(2,1)S(1)} %get-tuple-element.30), channel_id=1, source_target_pairs={{0,8},{4,12},{8,16},{12,20},{16,24},{20,28},{24,0},{28,4},{1,9},{5... | collective-permute-start | bytes 98312 | tf_op jit(solution)/shard_map/ppermute | solution.py:186
  19.4 2.4 %collective-permute-start.2 = (bf16[128,128]{1,0:T(8,128)(2,1)S(1)}, bf16[128,128]{1,0:T(8,128)(2,1)S(1)}, u32[]{:S(2)}, u32[]{:S(2)}) collective-permute-start(bf16[128,128]{1,0:T(8,128)(2,1)S(1)} %get-tuple-element.31), channel_id=1, source_target_pairs={{0,12},{4,16},{8,20},{12,24},{16,28},{20,0},{24,4},{28,8},{1,13},{... | collective-permute-start | bytes 98312 | tf_op jit(solution)/shard_map/ppermute | solution.py:186
  21.8 0.0 copy-start.6
  21.8 1.4 %collective-permute-start.3 = (bf16[128,128]{1,0:T(8,128)(2,1)S(1)}, bf16[128,128]{1,0:T(8,128)(2,1)S(1)}, u32[]{:S(2)}, u32[]{:S(2)}) collective-permute-start(bf16[128,128]{1,0:T(8,128)(2,1)S(1)} %get-tuple-element.32), channel_id=1, source_target_pairs={{0,16},{4,20},{8,24},{12,28},{16,0},{20,4},{24,8},{28,12},{1,17},{... | collective-permute-start | bytes 98312 | tf_op jit(solution)/shard_map/ppermute | solution.py:186
  23.2 2.4 %collective-permute-start.4 = (bf16[128,128]{1,0:T(8,128)(2,1)S(1)}, bf16[128,128]{1,0:T(8,128)(2,1)S(1)}, u32[]{:S(2)}, u32[]{:S(2)}) collective-permute-start(bf16[128,128]{1,0:T(8,128)(2,1)S(1)} %get-tuple-element.33), channel_id=1, source_target_pairs={{0,20},{4,24},{8,28},{12,0},{16,4},{20,8},{24,12},{28,16},{1,21},{... | collective-permute-start | bytes 98312 | tf_op jit(solution)/shard_map/ppermute | solution.py:186
  25.7 9.1 %collective-permute-done.refs_0_ = bf16[128,128]{1,0:T(8,128)(2,1)S(1)} collective-permute-done((bf16[128,128]{1,0:T(8,128)(2,1)S(1)}, bf16[128,128]{1,0:T(8,128)(2,1)S(1)}, u32[]{:S(2)}, u32[]{:S(2)}) %collective-permute-start) | collective-permute-done | bytes 32800 | tf_op jit(solution)/shard_map/ppermute | solution.py:186
  34.8 0.0 collective-permute-start.5
  34.8 0.0 collective-permute-done.1.refs_1_
  34.8 0.2 collective-permute-start.6
  35.0 7.2 %collective-permute-done.2.refs_2_ = bf16[128,128]{1,0:T(8,128)(2,1)S(1)} collective-permute-done((bf16[128,128]{1,0:T(8,128)(2,1)S(1)}, bf16[128,128]{1,0:T(8,128)(2,1)S(1)}, u32[]{:S(2)}, u32[]{:S(2)}) %collective-permute-start.2) | collective-permute-done | bytes 32800 | tf_op jit(solution)/shard_map/ppermute | solution.py:186
  42.2 0.0 collective-permute-done.3.refs_3_
  42.3 0.0 collective-permute-done.4.refs_4_
  42.3 0.0 collective-permute-done.5.refs_5_
  42.3 0.0 collective-permute-done.6.refs_6_
  42.3 0.0 copy-done.6
  42.3 4.4 %conv_outputs.1 = bf16[256,1024]{1,0:T(8,128)(2,1)} custom-call(s32[1]{0:T(128)} %bitcast.seq_ref, bf16[256,1024]{1,0:T(8,128)(2,1)S(1)} %copy-done, bf16[256,1024]{1,0:T(8,128)(2,1)S(1)} %copy-done.1, bf16[256,1024]{1,0:T(8,128)(2,1)S(1)} %copy-done.2, f32[3,16,8,128]{3,2,1,0:T(8,128)S(1)} %bitcast.15, f32[1,1024]{1,0:T(1,128)S(1)} %bitcast.17, ...), custom_call_target="tpu_custom_call" | custom-call | flops 16777216 | bytes 2097152 | tf_op jit(solution)/shard_map/conv_outputs/pallas_call | solution.py:259
  46.7 0.0 copy-start.4
  46.7 0.6 copy-done.4
  47.3 0.0 all-to-all-done.refs_0_
  47.3 4.5 %filter_lags.1 = f32[8,8,256]{2,1,0:T(8,128)} custom-call(bf16[32,64,256]{2,1,0:T(8,128)(2,1)S(1)} %all-to-all-done.refs_0_), custom_call_target="tpu_custom_call" | custom-call | tf_op jit(solution)/shard_map/filter_lags/pallas_call | solution.py:362
  51.8 0.0 copy-start.5
  51.8 7.1 %all-to-all-start.1 = ((f32[8,8,256]{2,1,0:T(8,128)}), f32[8,8,256]{2,1,0:T(8,128)S(1)}, u32[]{:S(2)}, u32[]{:S(2)}) async-start(f32[8,8,256]{2,1,0:T(8,128)} %filter_lags.1), calls=%async_computation.1 | async-start | bytes 131072 | tf_op jit(solution)/shard_map/all_to_all | solution.py:413
  58.9 0.0 copy-done.5
  58.9 6.8 %grad_outputs.1 = (bf16[256,1024]{1,0:T(8,128)(2,1)}, bf16[256,1024]{1,0:T(8,128)(2,1)}) custom-call(s32[1]{0:T(128)} %bitcast.seq_ref, bf16[256,1024]{1,0:T(8,128)(2,1)S(1)} %copy-done, bf16[256,1024]{1,0:T(8,128)(2,1)S(1)} %copy-done.1, bf16[256,1024]{1,0:T(8,128)(2,1)S(1)} %copy-done.2, bf16[256,1024]{1,0:T(8,128)(2,1)S(1)} %copy-done.3, ...), custom_call_target="tpu_custom_call" | custom-call | flops 16777216 | bytes 2097152 | tf_op jit(solution)/shard_map/grad_outputs/pallas_call | solution.py:259
  65.7 0.1 all-to-all-done.1
  65.8 0.6 copy.12
  (3 shorter events, 0.1 us)
Async XLA Ops:
  3.7 7.4 %copy-start.7 = (f32[256,16]{0,1:T(8,128)S(1)}, f32[256,16]{0,1:T(8,128)}, u32[]{:S(2)}) copy-start(f32[256,16]{0,1:T(8,128)} %param.12) | copy-start | bytes 49156
  3.8 7.4 %copy-start.8 = (f32[256,16]{0,1:T(8,128)S(1)}, f32[256,16]{0,1:T(8,128)}, u32[]{:S(2)}) copy-start(f32[256,16]{0,1:T(8,128)} %param.11) | copy-start | bytes 49156
  3.8 7.5 %copy-start.1 = (bf16[256,1024]{1,0:T(8,128)(2,1)S(1)}, bf16[256,1024]{1,0:T(8,128)(2,1)}, u32[]{:S(2)}) copy-start(bf16[256,1024]{1,0:T(8,128)(2,1)} %k_ref.2) | copy-start | bytes 1572868
  3.8 7.5 %copy-start.2 = (bf16[256,1024]{1,0:T(8,128)(2,1)S(1)}, bf16[256,1024]{1,0:T(8,128)(2,1)}, u32[]{:S(2)}) copy-start(bf16[256,1024]{1,0:T(8,128)(2,1)} %v_ref.2) | copy-start | bytes 1572868
  3.8 7.5 %copy-start.3 = (bf16[256,1024]{1,0:T(8,128)(2,1)S(1)}, bf16[256,1024]{1,0:T(8,128)(2,1)}, u32[]{:S(2)}) copy-start(bf16[256,1024]{1,0:T(8,128)(2,1)} %o_ref.1) | copy-start | bytes 1572868
  3.8 43.5 %all-to-all-start = ((bf16[32,64,256]{2,1,0:T(8,128)(2,1)}), bf16[32,64,256]{2,1,0:T(8,128)(2,1)S(1)}, u32[]{:S(2)}, u32[]{:S(2)}) async-start(bf16[32,64,256]{2,1,0:T(8,128)(2,1)} %pack_signals.1), calls=%async_computation | async-start | bytes 2097152 | tf_op jit(solution)/shard_map/all_to_all | solution.py:388
  11.1 1.0 %copy-start = (bf16[256,1024]{1,0:T(8,128)(2,1)S(1)}, bf16[256,1024]{1,0:T(8,128)(2,1)}, u32[]{:S(2)}) copy-start(bf16[256,1024]{1,0:T(8,128)(2,1)} %q_ref.2) | copy-start | bytes 1572868
  16.1 18.7 %collective-permute-start = (bf16[128,128]{1,0:T(8,128)(2,1)S(1)}, bf16[128,128]{1,0:T(8,128)(2,1)S(1)}, u32[]{:S(2)}, u32[]{:S(2)}) collective-permute-start(bf16[128,128]{1,0:T(8,128)(2,1)S(1)} %get-tuple-element.29), channel_id=1, source_target_pairs={{0,4},{4,8},{8,12},{12,16},{16,20},{20,24},{24,28},{28,0},{1,5},{5... | collective-permute-start | bytes 98312 | tf_op jit(solution)/shard_map/ppermute | solution.py:186
  17.9 16.9 %collective-permute-start.1 = (bf16[128,128]{1,0:T(8,128)(2,1)S(1)}, bf16[128,128]{1,0:T(8,128)(2,1)S(1)}, u32[]{:S(2)}, u32[]{:S(2)}) collective-permute-start(bf16[128,128]{1,0:T(8,128)(2,1)S(1)} %get-tuple-element.30), channel_id=1, source_target_pairs={{0,8},{4,12},{8,16},{12,20},{16,24},{20,28},{24,0},{28,4},{1,9},{5... | collective-permute-start | bytes 98312 | tf_op jit(solution)/shard_map/ppermute | solution.py:186
  19.4 22.9 %collective-permute-start.2 = (bf16[128,128]{1,0:T(8,128)(2,1)S(1)}, bf16[128,128]{1,0:T(8,128)(2,1)S(1)}, u32[]{:S(2)}, u32[]{:S(2)}) collective-permute-start(bf16[128,128]{1,0:T(8,128)(2,1)S(1)} %get-tuple-element.31), channel_id=1, source_target_pairs={{0,12},{4,16},{8,20},{12,24},{16,28},{20,0},{24,4},{28,8},{1,13},{... | collective-permute-start | bytes 98312 | tf_op jit(solution)/shard_map/ppermute | solution.py:186
  21.8 20.5 %copy-start.6 = (f32[1024]{0:T(1024)S(1)}, f32[1024]{0:T(1024)}, u32[]{:S(2)}) copy-start(f32[1024]{0:T(1024)} %param.13) | copy-start | bytes 12292
  21.8 20.5 %collective-permute-start.3 = (bf16[128,128]{1,0:T(8,128)(2,1)S(1)}, bf16[128,128]{1,0:T(8,128)(2,1)S(1)}, u32[]{:S(2)}, u32[]{:S(2)}) collective-permute-start(bf16[128,128]{1,0:T(8,128)(2,1)S(1)} %get-tuple-element.32), channel_id=1, source_target_pairs={{0,16},{4,20},{8,24},{12,28},{16,0},{20,4},{24,8},{28,12},{1,17},{... | collective-permute-start | bytes 98312 | tf_op jit(solution)/shard_map/ppermute | solution.py:186
  23.2 19.0 %collective-permute-start.4 = (bf16[128,128]{1,0:T(8,128)(2,1)S(1)}, bf16[128,128]{1,0:T(8,128)(2,1)S(1)}, u32[]{:S(2)}, u32[]{:S(2)}) collective-permute-start(bf16[128,128]{1,0:T(8,128)(2,1)S(1)} %get-tuple-element.33), channel_id=1, source_target_pairs={{0,20},{4,24},{8,28},{12,0},{16,4},{20,8},{24,12},{28,16},{1,21},{... | collective-permute-start | bytes 98312 | tf_op jit(solution)/shard_map/ppermute | solution.py:186
  34.8 7.5 %collective-permute-start.5 = (bf16[128,128]{1,0:T(8,128)(2,1)S(1)}, bf16[128,128]{1,0:T(8,128)(2,1)S(1)}, u32[]{:S(2)}, u32[]{:S(2)}) collective-permute-start(bf16[128,128]{1,0:T(8,128)(2,1)S(1)} %get-tuple-element.34), channel_id=1, source_target_pairs={{0,24},{4,28},{8,0},{12,4},{16,8},{20,12},{24,16},{28,20},{1,25},{... | collective-permute-start | bytes 98312 | tf_op jit(solution)/shard_map/ppermute | solution.py:186
  34.8 7.5 %collective-permute-start.6 = (bf16[128,128]{1,0:T(8,128)(2,1)S(1)}, bf16[128,128]{1,0:T(8,128)(2,1)S(1)}, u32[]{:S(2)}, u32[]{:S(2)}) collective-permute-start(bf16[128,128]{1,0:T(8,128)(2,1)S(1)} %get-tuple-element.35), channel_id=1, source_target_pairs={{0,28},{4,0},{8,4},{12,8},{16,12},{20,16},{24,20},{28,24},{1,29},{... | collective-permute-start | bytes 98312 | tf_op jit(solution)/shard_map/ppermute | solution.py:186
  46.7 0.6 copy-start.4
  51.8 7.1 %copy-start.5 = (bf16[128,128]{1,0:T(8,128)(2,1)S(1)}, bf16[128,128]{1,0:T(8,128)(2,1)}, u32[]{:S(2)}) copy-start(bf16[128,128]{1,0:T(8,128)(2,1)} %copy-done.4) | copy-start | bytes 98308
  51.8 14.0 %all-to-all-start.1 = ((f32[8,8,256]{2,1,0:T(8,128)}), f32[8,8,256]{2,1,0:T(8,128)S(1)}, u32[]{:S(2)}, u32[]{:S(2)}) async-start(f32[8,8,256]{2,1,0:T(8,128)} %filter_lags.1), calls=%async_computation.1 | async-start | bytes 131072 | tf_op jit(solution)/shard_map/all_to_all | solution.py:413

commit v4 on v3

--- a/solution.py
+++ b/solution.py
@@ -119,39 +119,6 @@
     return send
 
 
-def state_kernel(seq_ref, q_ref, k_ref, v_ref, o_ref, coef_ref, *refs):
-    state_refs, x_ref, g_ref = refs[:-2], refs[-2], refs[-1]
-    tok_rows, width = k_ref.shape
-    tiles = width // LANES
-    modes = coef_ref.shape[1]
-    shards = len(state_refs) + 1
-    spread_tokens(k_ref, v_ref, x_ref)
-    spread_tokens(o_ref, q_ref, g_ref)
-    decay = [coef_ref[0, m] for m in range(modes)]
-
-    def step(t, carry):
-        x = x_ref[pl.ds(t, tiles, stride=tok_rows), :]
-        g = g_ref[pl.ds(tok_rows - 1 - t, tiles, stride=tok_rows), :]
-        ahead = tuple(decay[m] * carry[0][m] + x for m in range(modes))
-        behind = tuple(decay[m] * carry[1][m] + g for m in range(modes))
-        return (ahead, behind)
-
-    zero = tuple(jnp.zeros((tiles, LANES), F32) for _ in range(modes))
-    ahead, behind = lax.fori_loop(0, tok_rows, step, (zero, zero), unroll=8)
-    ahead = jnp.concatenate(ahead, axis=0).astype(LINK)
-    behind = jnp.concatenate(behind, axis=0).astype(LINK)
-    for k in range(1, shards):
-        stays = seq_ref[0] + k < shards
-
-        @pl.when(stays)
-        def _():
-            state_refs[k - 1][...] = ahead
-
-        @pl.when(jnp.logical_not(stays))
-        def _():
-            state_refs[k - 1][...] = behind
-
-
 def spread_tokens(a_ref, b_ref, x_ref):
     tok_rows, width = a_ref.shape
     for tile in range(width // LANES):
@@ -161,31 +128,71 @@
         ).astype(F32)
 
 
-def block_states(seq_index, shards, query_proj, key_proj, value_proj, out_grad, coefs):
+def walk_tokens(ref, coef_ref, tok_rows, tiles, start, move):
+    modes = coef_ref.shape[1]
+    decay = [coef_ref[0, m] for m in range(modes)]
+    weight = [coef_ref[2, m] for m in range(modes)]
+
+    def step(t, held):
+        rows = pl.ds(start + move * t, tiles, stride=tok_rows)
+        x = ref[rows, :]
+        held = tuple(decay[m] * held[m] + x for m in range(modes))
+        ref[rows, :] = tree_sum([weight[m] * held[m] for m in range(modes)])
+        return held
+
+    zero = tuple(jnp.zeros((tiles, LANES), F32) for _ in range(modes))
+    return lax.fori_loop(0, tok_rows, step, zero, unroll=8)
+
+
+def tree_sum(terms):
+    while len(terms) > 1:
+        terms = [sum(terms[i : i + 2][1:], terms[i]) for i in range(0, len(terms), 2)]
+    return terms[0]
+
+
+def local_kernel(seq_ref, q_ref, k_ref, v_ref, o_ref, coef_ref, conv_ref, grad_ref, *state_refs):
+    tok_rows, width = k_ref.shape
+    tiles = width // LANES
+    shards = len(state_refs) + 1
+    spread_tokens(k_ref, v_ref, conv_ref)
+    spread_tokens(o_ref, q_ref, grad_ref)
+    ahead = walk_tokens(conv_ref, coef_ref, tok_rows, tiles, 0, 1)
+    behind = walk_tokens(grad_ref, coef_ref, tok_rows, tiles, tok_rows - 1, -1)
+    ahead = jnp.concatenate(ahead, axis=0).astype(LINK)
+    behind = jnp.concatenate(behind, axis=0).astype(LINK)
+    for k in range(1, shards):
+        stays = seq_ref[0] + k < shards
+
+        @pl.when(stays)
+        def _():
+            state_refs[k - 1][...] = ahead
+
+        @pl.when(jnp.logical_not(stays))
+        def _():
+            state_refs[k - 1][...] = behind
+
+
+def local_parts(seq_index, shards, query_proj, key_proj, value_proj, out_grad, coefs):
     tok_rows, width = key_proj.shape
-    tiles = width // LANES
-    modes = coefs.shape[1]
+    modes, tiles = coefs.shape[1:3]
     whole = pl.BlockSpec(memory_space=pltpu.VMEM)
-    return pl.pallas_call(
-        state_kernel,
+    outs = pl.pallas_call(
+        local_kernel,
         in_specs=[pl.BlockSpec(memory_space=pltpu.SMEM)] + [whole] * 5,
-        out_specs=[whole] * (shards - 1),
-        out_shape=[jax.ShapeDtypeStruct((modes * tiles, LANES), LINK)] * (shards - 1),
-        scratch_shapes=[pltpu.VMEM((tok_rows * tiles, LANES), F32)] * 2,
+        out_specs=[whole] * (shards + 1),
+        out_shape=[jax.ShapeDtypeStruct((tok_rows * tiles, LANES), F32)] * 2
+        + [jax.ShapeDtypeStruct((modes * tiles, LANES), LINK)] * (shards - 1),
         compiler_params=pltpu.CompilerParams(vmem_limit_bytes=VMEM_BYTES),
         cost_estimate=pl.CostEstimate(
-            flops=4 * modes * tok_rows * width, bytes_accessed=8 * tok_rows * width, transcendentals=0
+            flops=8 * modes * tok_rows * width, bytes_accessed=8 * tok_rows * width, transcendentals=0
         ),
-        name="block_states",
+        name="local_parts",
     )(seq_index, query_proj, key_proj, value_proj, out_grad, coefs)
-
-
-def exchange_states(states):
-    shards = len(states) + 1
-    return [
-        lax.ppermute(states[k - 1], "seq", [(i, (i + k) % shards) for i in range(shards)])
-        for k in range(1, shards)
-    ]
+    return outs[:2], outs[2:]
+
+
+def send_state(state, shards, k):
+    return lax.ppermute(state, "seq", [(i, (i + k) % shards) for i in range(shards)])
 
 
 def edge_states(seq, state_refs, coef_ref, later):
@@ -202,71 +209,74 @@
     return held
 
 
-def walk_tokens(ref, held, coef_ref, tok_rows, tiles, start, move):
+def add_edge(ref, held, coef_ref, tok_rows, tiles, start, move):
     modes = coef_ref.shape[1]
     decay = [coef_ref[0, m] for m in range(modes)]
-    weight = [coef_ref[2, m] for m in range(modes)]
 
     def step(t, held):
         rows = pl.ds(start + move * t, tiles, stride=tok_rows)
-        x = ref[rows, :]
-        held = tuple(decay[m] * held[m] + x for m in range(modes))
-        terms = [weight[m] * held[m] for m in range(modes)]
-        while len(terms) > 1:
-            terms = [sum(terms[i : i + 2][1:], terms[i]) for i in range(0, len(terms), 2)]
-        ref[rows, :] = terms[0]
+        held = tuple(decay[m] * held[m] for m in range(modes))
+        ref[rows, :] = ref[rows, :] + tree_sum(list(held))
         return held
 
-    lax.fori_loop(0, tok_rows, step, tuple(held), unroll=8)
-
-
-def conv_kernel(seq_ref, q_ref, k_ref, v_ref, coef_ref, gain_ref, *refs):
-    state_refs, layer_ref, x_ref = refs[:-2], refs[-2], refs[-1]
+    held = tuple(coef_ref[2, m] * held[m] for m in range(modes))
+    lax.fori_loop(0, tok_rows, step, held, unroll=8)
+
+
+def final_kernel(seq_ref, q_ref, k_ref, v_ref, o_ref, coef_ref, gain_ref, x_ref, g_ref, *refs):
+    state_refs, hbm_refs, held_refs, sems = refs[:-7], refs[-7:-4], refs[-4:-1], refs[-1]
+    layer_ref, key_ref, value_ref = held_refs
     tok_rows, width = k_ref.shape
     tiles = width // LANES
-    spread_tokens(k_ref, v_ref, x_ref)
-    held = edge_states(seq_ref[0], state_refs, coef_ref, False)
-    walk_tokens(x_ref, held, coef_ref, tok_rows, tiles, 0, 1)
+
+    def departure(i, tile):
+        place = (slice(None), pl.ds(tile * LANES, LANES))
+        return pltpu.make_async_copy(
+            held_refs[i].at[place], hbm_refs[i].at[place], sems.at[i, tile]
+        )
+
+    edge = edge_states(seq_ref[0], state_refs, coef_ref, False)
+    add_edge(x_ref, edge, coef_ref, tok_rows, tiles, 0, 1)
     for tile in range(tiles):
         cols = slice(tile * LANES, (tile + 1) * LANES)
         rows = slice(tile * tok_rows, (tile + 1) * tok_rows)
         conv_in = product(k_ref[:, cols], v_ref[:, cols]).astype(F32)
         long_conv = x_ref[rows, :] + gain_ref[:, cols] * conv_in
         layer_ref[:, cols] = (q_ref[:, cols].astype(F32) * long_conv).astype(BF16)
-
-
-def grad_kernel(seq_ref, q_ref, k_ref, v_ref, o_ref, coef_ref, gain_ref, *refs):
-    state_refs, key_ref, value_ref, g_ref = refs[:-3], *refs[-3:]
-    tok_rows, width = k_ref.shape
-    tiles = width // LANES
-    spread_tokens(o_ref, q_ref, g_ref)
-    held = edge_states(seq_ref[0], state_refs, coef_ref, True)
-    walk_tokens(g_ref, held, coef_ref, tok_rows, tiles, tok_rows - 1, -1)
+        departure(0, tile).start()
+    edge = edge_states(seq_ref[0], state_refs, coef_ref, True)
+    add_edge(g_ref, edge, coef_ref, tok_rows, tiles, tok_rows - 1, -1)
     for tile in range(tiles):
         cols = slice(tile * LANES, (tile + 1) * LANES)
         rows = slice(tile * tok_rows, (tile + 1) * tok_rows)
         mid_grad = product(o_ref[:, cols], q_ref[:, cols]).astype(F32)
         conv_grad = g_ref[rows, :] + gain_ref[:, cols] * mid_grad
         key_ref[:, cols] = (conv_grad * v_ref[:, cols].astype(F32)).astype(BF16)
+        departure(1, tile).start()
         value_ref[:, cols] = (conv_grad * k_ref[:, cols].astype(F32)).astype(BF16)
-
-
-def local_outputs(kernel, count, name, seq_index, signals, coefs, gain, states):
+        departure(2, tile).start()
+    for i in range(3):
+        for tile in range(tiles):
+            departure(i, tile).wait()
+
+
+def final_outputs(seq_index, signals, coefs, gain, parts, states):
     tok_rows, width = signals[0].shape
     modes, tiles = coefs.shape[1:3]
-    args = (*signals, coefs, gain, *states)
+    args = (*signals, coefs, gain, *parts, *states)
     whole = pl.BlockSpec(memory_space=pltpu.VMEM)
     return pl.pallas_call(
-        kernel,
+        final_kernel,
         in_specs=[pl.BlockSpec(memory_space=pltpu.SMEM)] + [whole] * len(args),
-        out_specs=[whole] * count,
-        out_shape=[jax.ShapeDtypeStruct((tok_rows, width), BF16)] * count,
-        scratch_shapes=[pltpu.VMEM((tok_rows * tiles, LANES), F32)],
+        out_specs=[pl.BlockSpec(memory_space=pl.ANY)] * 3,
+        out_shape=[jax.ShapeDtypeStruct((tok_rows, width), BF16)] * 3,
+        scratch_shapes=[pltpu.VMEM((tok_rows, width), BF16)] * 3
+        + [pltpu.SemaphoreType.DMA((3, tiles))],
         compiler_params=pltpu.CompilerParams(vmem_limit_bytes=VMEM_BYTES),
         cost_estimate=pl.CostEstimate(
-            flops=4 * modes * tok_rows * width, bytes_accessed=8 * tok_rows * width, transcendentals=0
+            flops=8 * modes * tok_rows * width, bytes_accessed=14 * tok_rows * width, transcendentals=0
         ),
-        name=name,
+        name="final_outputs",
     )(seq_index, *args)
 
 
@@ -398,20 +408,19 @@
     coefs = jnp.broadcast_to(coefs, (3, modes, width // FILTERS, FILTERS // LANES, LANES))
     coefs = coefs.reshape(3, modes, width // LANES, LANES)
     seq_index = lax.axis_index("seq").reshape(1)
-    states = exchange_states(block_states(seq_index, shards, *signals, coefs))
-    gain = skip_gain[None, :]
-    (layer_out,) = local_outputs(
-        conv_kernel, 1, "conv_outputs", seq_index, signals[:3], coefs, gain, states
-    )
-    received, layer_out = lax.optimization_barrier((received, layer_out))
-    key_grad, value_grad = local_outputs(
-        grad_kernel, 2, "grad_outputs", seq_index, signals, coefs, gain, states
-    )
+    parts, states = local_parts(seq_index, shards, *signals, coefs)
+    early = [send_state(states[k - 1], shards, k) for k in range(1, min(shards, 6))]
+    received, *parts = lax.optimization_barrier((received, *parts))
 
     scale = 1.0 / math.sqrt(length * (CHANNELS // FILTERS))
     lags = filter_lags(received, shards, chans, owned, scale)
+    lags, *late = lax.optimization_barrier((lags, *states[5:]))
+    late = [send_state(state, shards, 6 + i) for i, state in enumerate(late)]
     lags = lax.all_to_all(lags, "seq", split_axis=0, concat_axis=0, tiled=True)
     filter_grad = lags.reshape(shards * owned, tok_rows).T
+    layer_out, key_grad, value_grad = final_outputs(
+        seq_index, signals, coefs, skip_gain[None, :], parts, early + late
+    )
     return (layer_out, key_grad, value_grad, filter_grad)
 
 

time: 66.8 us -> 71.3 us (1.067)
  local copies, waits for them, and re-layouts: 2.21 us -> 6.6 us
    ppermute x7, waiting for transfers between devices: 16.4 us -> 2.45 us  [send_state(): lax.ppermute(state, 'seq', [(i, (i + k) % shards) for i in range(shards)])]
    all_to_all x1, waiting for transfers between devices: 0.01 us -> 13.9 us  [per_device(): lax.all_to_all(send, ('seq', 'chan'), split_axis=0, concat_axis=0, tiled=...]
    unnamed x19 -> x27, local copies, waits for them, and re-layouts: 2.13 us -> 6.52 us
    all_to_all x1, starting transfers between devices: 7.05 us -> 3.81 us  [per_device(): lags = lax.all_to_all(lags, 'seq', split_axis=0, concat_axis=0, tiled=True)]
    ppermute x7, starting transfers between devices: 9.79 us -> 12.6 us  [send_state(): lax.ppermute(state, 'seq', [(i, (i + k) % shards) for i in range(shards)])]
    pallas_call x3 -> x2, Pallas kernels: 15.1 us -> 15.7 us  [the longest x1 8.75 us: local_parts(): pl.pallas_call(local_kernel, in_specs=[pl.BlockSpec(memory_space=pltpu.SM...]
  transfers between devices with their start and end apart: 9 -> 9, of which waited for: 3 -> 3; matrix products, arithmetic and copies ran while one was open for 0% -> 0% of each run, Pallas kernels for 23% -> 22%
where the time goes in v4:
time: 71.3 us; the launch traced here: 70.8 us
  starting transfers between devices  23.7 us (33%)
  Pallas kernels  23.3 us (33%)
  waiting for transfers between devices  16.3 us (23%)
  local copies, waits for them, and re-layouts  6.6 us (9%)
  between operations  0.82 us (1%)
    all_to_all x1, waiting for transfers between devices, per_device(): lax.all_to_all(send, ('seq', 'chan'), split_axis=0, concat_axis=0, tiled=...  13.9 us
    ppermute x7, starting transfers between devices, send_state(): lax.ppermute(state, 'seq', [(i, (i + k) % shards) for i in range(shards)])  12.6 us
    pallas_call x1, Pallas kernels, local_parts(): pl.pallas_call(local_kernel, in_specs=[pl.BlockSpec(memory_space=pltpu.SM...  8.75 us
    all_to_all x1, starting transfers between devices, per_device(): lax.all_to_all(send, ('seq', 'chan'), split_axis=0, concat_axis=0, tiled=...  7.3 us
    pallas_call x1, Pallas kernels, final_outputs(): pl.pallas_call(final_kernel, in_specs=[pl.BlockSpec(memory_space=pltpu.SM...  6.94 us
    unnamed x27, local copies, waits for them, and re-layouts  6.52 us
    pallas_call x1, Pallas kernels, filter_lags(): pl.pallas_call(functools.partial(lag_kernel, shards, chans, groups, owned...  4.52 us
    all_to_all x1, starting transfers between devices, per_device(): lags = lax.all_to_all(lags, 'seq', split_axis=0, concat_axis=0, tiled=True)  3.81 us
  transfers between devices with their start and end apart: 9, of which 3 were waited for; matrix products, arithmetic and copies ran while one was open for 0% of the time, Pallas kernels for 22%

profile of v4, /device:TPU:0, one launch (start us, length us, event | category | flops | bytes accessed | tf_op | source)
XLA Modules:
  0.0 70.8 jit_solution(7513100237158930904)
XLA Ops:
  0.6 3.1 %pack_signals.1 = bf16[32,64,256]{2,1,0:T(8,128)(2,1)} custom-call(bf16[256,1024]{1,0:T(8,128)(2,1)} %k_ref.1, bf16[256,1024]{1,0:T(8,128)(2,1)} %v_ref.1, bf16[256,1024]{1,0:T(8,128)(2,1)} %o_ref.1, bf16[256,1024]{1,0:T(8,128)(2,1)} %q_ref.1), custom_call_target="tpu_custom_call" | custom-call | tf_op jit(solution)/shard_map/pack_signals/pallas_call | solution.py:102
  3.8 0.0 copy-start.11
  3.8 0.0 copy-start.12
  3.8 0.0 copy-start.1
  3.8 0.0 copy-start.2
  3.8 0.0 copy-start.3
  3.8 7.3 %all-to-all-start = ((bf16[32,64,256]{2,1,0:T(8,128)(2,1)}), bf16[32,64,256]{2,1,0:T(8,128)(2,1)S(1)}, u32[]{:S(2)}, u32[]{:S(2)}) async-start(bf16[32,64,256]{2,1,0:T(8,128)(2,1)} %pack_signals.1), calls=%async_computation | async-start | bytes 2097152 | tf_op jit(solution)/shard_map/all_to_all | solution.py:398
  11.1 0.0 copy-start
  11.1 0.0 copy-done.11
  11.2 0.0 copy-done.12
  11.2 0.1 broadcast_in_dim.11
  11.3 0.0 copy-done.1
  11.3 0.0 copy-done.2
  11.3 0.0 copy-done.3
  11.3 0.8 %copy-done = bf16[256,1024]{1,0:T(8,128)(2,1)S(1)} copy-done((bf16[256,1024]{1,0:T(8,128)(2,1)S(1)}, bf16[256,1024]{1,0:T(8,128)(2,1)}, u32[]{:S(2)}) %copy-start) | copy-done | bytes 524312
  12.2 8.8 %local_parts.1 = (f32[2048,128]{1,0:T(8,128)S(1)}, f32[2048,128]{1,0:T(8,128)S(1)}, bf16[128,128]{1,0:T(8,128)(2,1)S(1)}, bf16[128,128]{1,0:T(8,128)(2,1)S(1)}, ...) custom-call(s32[1]{0:T(128)} %bitcast.seq_ref, ...), custom_call_target="tpu_custom_call" | custom-call | flops 33554432 | bytes 2097152 | tf_op jit(solution)/shard_map/local_parts/pallas_call | solution.py:179
  20.9 0.0 copy-start.4
  20.9 1.0 %copy-done.4 = f32[2048,128]{1,0:T(8,128)} copy-done((f32[2048,128]{1,0:T(8,128)}, f32[2048,128]{1,0:T(8,128)S(1)}, u32[]{:S(2)}) %copy-start.4) | copy-done | bytes 1048600
  21.9 0.0 copy-start.6
  21.9 1.0 %copy-done.6 = f32[2048,128]{1,0:T(8,128)} copy-done((f32[2048,128]{1,0:T(8,128)}, f32[2048,128]{1,0:T(8,128)S(1)}, u32[]{:S(2)}) %copy-start.6) | copy-done | bytes 1048600
  22.9 0.0 copy-start.9
  22.9 0.6 copy-done.9
  23.5 13.9 %all-to-all-done.refs_0_ = bf16[32,64,256]{2,1,0:T(8,128)(2,1)S(1)} async-done(((bf16[32,64,256]{2,1,0:T(8,128)(2,1)}), bf16[32,64,256]{2,1,0:T(8,128)(2,1)S(1)}, u32[]{:S(2)}, u32[]{:S(2)}) %all-to-all-start) | async-done | bytes 1048608 | tf_op jit(solution)/shard_map/all_to_all | solution.py:398
  37.4 4.5 %filter_lags.1 = f32[8,8,256]{2,1,0:T(8,128)} custom-call(bf16[32,64,256]{2,1,0:T(8,128)(2,1)S(1)} %all-to-all-done.refs_0_), custom_call_target="tpu_custom_call" | custom-call | tf_op jit(solution)/shard_map/filter_lags/pallas_call | solution.py:372
  41.9 0.0 copy-start.10
  41.9 3.8 %all-to-all-start.1 = ((f32[8,8,256]{2,1,0:T(8,128)}), f32[8,8,256]{2,1,0:T(8,128)S(1)}, u32[]{:S(2)}, u32[]{:S(2)}) async-start(f32[8,8,256]{2,1,0:T(8,128)} %filter_lags.1), calls=%async_computation.1 | async-start | bytes 131072 | tf_op jit(solution)/shard_map/all_to_all | solution.py:419
  45.7 0.0 copy-done.10
  45.7 2.0 %collective-permute-start = (bf16[128,128]{1,0:T(8,128)(2,1)S(1)}, bf16[128,128]{1,0:T(8,128)(2,1)S(1)}, u32[]{:S(2)}, u32[]{:S(2)}) collective-permute-start(bf16[128,128]{1,0:T(8,128)(2,1)S(1)} %copy-done.10), channel_id=1, source_target_pairs={{0,4},{4,8},{8,12},{12,16},{16,20},{20,24},{24,28},{28,0},{1,5},{5... | collective-permute-start | bytes 98312 | tf_op jit(solution)/shard_map/ppermute | solution.py:195
  47.7 0.0 copy-start.8
  47.7 1.5 %collective-permute-start.1 = (bf16[128,128]{1,0:T(8,128)(2,1)S(1)}, bf16[128,128]{1,0:T(8,128)(2,1)S(1)}, u32[]{:S(2)}, u32[]{:S(2)}) collective-permute-start(bf16[128,128]{1,0:T(8,128)(2,1)S(1)} %get-tuple-element.41), channel_id=1, source_target_pairs={{0,8},{4,12},{8,16},{12,20},{16,24},{20,28},{24,0},{28,4},{1,9},{5... | collective-permute-start | bytes 98312 | tf_op jit(solution)/shard_map/ppermute | solution.py:195
  49.2 2.4 %collective-permute-start.2 = (bf16[128,128]{1,0:T(8,128)(2,1)S(1)}, bf16[128,128]{1,0:T(8,128)(2,1)S(1)}, u32[]{:S(2)}, u32[]{:S(2)}) collective-permute-start(bf16[128,128]{1,0:T(8,128)(2,1)S(1)} %get-tuple-element.42), channel_id=1, source_target_pairs={{0,12},{4,16},{8,20},{12,24},{16,28},{20,0},{24,4},{28,8},{1,13},{... | collective-permute-start | bytes 98312 | tf_op jit(solution)/shard_map/ppermute | solution.py:195
  51.6 1.5 %collective-permute-start.3 = (bf16[128,128]{1,0:T(8,128)(2,1)S(1)}, bf16[128,128]{1,0:T(8,128)(2,1)S(1)}, u32[]{:S(2)}, u32[]{:S(2)}) collective-permute-start(bf16[128,128]{1,0:T(8,128)(2,1)S(1)} %get-tuple-element.43), channel_id=1, source_target_pairs={{0,16},{4,20},{8,24},{12,28},{16,0},{20,4},{24,8},{28,12},{1,17},{... | collective-permute-start | bytes 98312 | tf_op jit(solution)/shard_map/ppermute | solution.py:195
  53.0 2.4 %collective-permute-start.4 = (bf16[128,128]{1,0:T(8,128)(2,1)S(1)}, bf16[128,128]{1,0:T(8,128)(2,1)S(1)}, u32[]{:S(2)}, u32[]{:S(2)}) collective-permute-start(bf16[128,128]{1,0:T(8,128)(2,1)S(1)} %get-tuple-element.44), channel_id=1, source_target_pairs={{0,20},{4,24},{8,28},{12,0},{16,4},{20,8},{24,12},{28,16},{1,21},{... | collective-permute-start | bytes 98312 | tf_op jit(solution)/shard_map/ppermute | solution.py:195
  55.4 0.0 collective-permute-done.refs_0_
  55.4 1.5 %collective-permute-start.5 = (bf16[128,128]{1,0:T(8,128)(2,1)S(1)}, bf16[128,128]{1,0:T(8,128)(2,1)S(1)}, u32[]{:S(2)}, u32[]{:S(2)}) collective-permute-start(bf16[128,128]{1,0:T(8,128)(2,1)S(1)} %get-tuple-element.48), channel_id=1, source_target_pairs={{0,24},{4,28},{8,0},{12,4},{16,8},{20,12},{24,16},{28,20},{1,25},{... | collective-permute-start | bytes 98312 | tf_op jit(solution)/shard_map/ppermute | solution.py:195
  56.8 0.0 collective-permute-done.1.refs_1_
  56.8 1.5 %collective-permute-start.6 = (bf16[128,128]{1,0:T(8,128)(2,1)S(1)}, bf16[128,128]{1,0:T(8,128)(2,1)S(1)}, u32[]{:S(2)}, u32[]{:S(2)}) collective-permute-start(bf16[128,128]{1,0:T(8,128)(2,1)S(1)} %get-tuple-element.49), channel_id=1, source_target_pairs={{0,28},{4,0},{8,4},{12,8},{16,12},{20,16},{24,20},{28,24},{1,29},{... | collective-permute-start | bytes 98312 | tf_op jit(solution)/shard_map/ppermute | solution.py:195
  58.3 0.0 collective-permute-done.2.refs_2_
  58.3 0.0 collective-permute-done.3.refs_3_
  58.3 0.0 collective-permute-done.4.refs_4_
  58.3 1.0 %collective-permute-done.5.refs_5_ = bf16[128,128]{1,0:T(8,128)(2,1)S(1)} collective-permute-done((bf16[128,128]{1,0:T(8,128)(2,1)S(1)}, bf16[128,128]{1,0:T(8,128)(2,1)S(1)}, u32[]{:S(2)}, u32[]{:S(2)}) %collective-permute-start.5) | collective-permute-done | bytes 32800 | tf_op jit(solution)/shard_map/ppermute | solution.py:195
  59.3 1.5 %collective-permute-done.6.refs_6_ = bf16[128,128]{1,0:T(8,128)(2,1)S(1)} collective-permute-done((bf16[128,128]{1,0:T(8,128)(2,1)S(1)}, bf16[128,128]{1,0:T(8,128)(2,1)S(1)}, u32[]{:S(2)}, u32[]{:S(2)}) %collective-permute-start.6) | collective-permute-done | bytes 32800 | tf_op jit(solution)/shard_map/ppermute | solution.py:195
  60.8 0.0 copy-done.8
  60.8 0.0 copy-start.5
  60.8 1.2 %copy-done.5 = f32[2048,128]{1,0:T(8,128)S(1)} copy-done((f32[2048,128]{1,0:T(8,128)S(1)}, f32[2048,128]{1,0:T(8,128)}, u32[]{:S(2)}) %copy-start.5) | copy-done | bytes 1048600
  62.0 0.0 copy-start.7
  62.0 1.2 %copy-done.7 = f32[2048,128]{1,0:T(8,128)S(1)} copy-done((f32[2048,128]{1,0:T(8,128)S(1)}, f32[2048,128]{1,0:T(8,128)}, u32[]{:S(2)}) %copy-start.7) | copy-done | bytes 1048600
  63.2 6.9 %final_outputs.1 = (bf16[256,1024]{1,0:T(8,128)(2,1)}, bf16[256,1024]{1,0:T(8,128)(2,1)}, bf16[256,1024]{1,0:T(8,128)(2,1)}) custom-call(s32[1]{0:T(128)} %bitcast.seq_ref, bf16[256,1024]{1,0:T(8,128)(2,1)S(1)} %copy-done, bf16[256,1024]{1,0:T(8,128)(2,1)S(1)} %copy-done.1, bf16[256,1024]{1,0:T(8,128)(2,1)S(1)} %copy-done.2, ...), custom_call_target="tpu_custom_call" | custom-call | flops 33554432 | bytes 3670016 | tf_op jit(solution)/shard_map/final_outputs/pallas_call | solution.py:268
  70.2 0.0 all-to-all-done.1
  70.2 0.6 copy.12
  (3 shorter events, 0.1 us)
Async XLA Ops:
  3.8 7.4 %copy-start.11 = (f32[256,16]{0,1:T(8,128)S(1)}, f32[256,16]{0,1:T(8,128)}, u32[]{:S(2)}) copy-start(f32[256,16]{0,1:T(8,128)} %param.12) | copy-start | bytes 49156
  3.8 7.4 %copy-start.12 = (f32[256,16]{0,1:T(8,128)S(1)}, f32[256,16]{0,1:T(8,128)}, u32[]{:S(2)}) copy-start(f32[256,16]{0,1:T(8,128)} %param.11) | copy-start | bytes 49156
  3.8 7.5 %copy-start.1 = (bf16[256,1024]{1,0:T(8,128)(2,1)S(1)}, bf16[256,1024]{1,0:T(8,128)(2,1)}, u32[]{:S(2)}) copy-start(bf16[256,1024]{1,0:T(8,128)(2,1)} %k_ref.1) | copy-start | bytes 1572868
  3.8 7.5 %copy-start.2 = (bf16[256,1024]{1,0:T(8,128)(2,1)S(1)}, bf16[256,1024]{1,0:T(8,128)(2,1)}, u32[]{:S(2)}) copy-start(bf16[256,1024]{1,0:T(8,128)(2,1)} %v_ref.1) | copy-start | bytes 1572868
  3.8 7.5 %copy-start.3 = (bf16[256,1024]{1,0:T(8,128)(2,1)S(1)}, bf16[256,1024]{1,0:T(8,128)(2,1)}, u32[]{:S(2)}) copy-start(bf16[256,1024]{1,0:T(8,128)(2,1)} %o_ref.1) | copy-start | bytes 1572868
  3.8 33.5 %all-to-all-start = ((bf16[32,64,256]{2,1,0:T(8,128)(2,1)}), bf16[32,64,256]{2,1,0:T(8,128)(2,1)S(1)}, u32[]{:S(2)}, u32[]{:S(2)}) async-start(bf16[32,64,256]{2,1,0:T(8,128)(2,1)} %pack_signals.1), calls=%async_computation | async-start | bytes 2097152 | tf_op jit(solution)/shard_map/all_to_all | solution.py:398
  11.1 1.0 %copy-start = (bf16[256,1024]{1,0:T(8,128)(2,1)S(1)}, bf16[256,1024]{1,0:T(8,128)(2,1)}, u32[]{:S(2)}) copy-start(bf16[256,1024]{1,0:T(8,128)(2,1)} %q_ref.1) | copy-start | bytes 1572868
  20.9 1.0 %copy-start.4 = (f32[2048,128]{1,0:T(8,128)}, f32[2048,128]{1,0:T(8,128)S(1)}, u32[]{:S(2)}) copy-start(f32[2048,128]{1,0:T(8,128)S(1)} %get-tuple-element.38.x_ref) | copy-start | bytes 3145732
  21.9 1.0 %copy-start.6 = (f32[2048,128]{1,0:T(8,128)}, f32[2048,128]{1,0:T(8,128)S(1)}, u32[]{:S(2)}) copy-start(f32[2048,128]{1,0:T(8,128)S(1)} %get-tuple-element.39.g_ref) | copy-start | bytes 3145732
  22.9 0.6 copy-start.9
  41.9 3.8 %copy-start.10 = (bf16[128,128]{1,0:T(8,128)(2,1)S(1)}, bf16[128,128]{1,0:T(8,128)(2,1)}, u32[]{:S(2)}) copy-start(bf16[128,128]{1,0:T(8,128)(2,1)} %copy-done.9) | copy-start | bytes 98308
  41.9 28.3 %all-to-all-start.1 = ((f32[8,8,256]{2,1,0:T(8,128)}), f32[8,8,256]{2,1,0:T(8,128)S(1)}, u32[]{:S(2)}, u32[]{:S(2)}) async-start(f32[8,8,256]{2,1,0:T(8,128)} %filter_lags.1), calls=%async_computation.1 | async-start | bytes 131072 | tf_op jit(solution)/shard_map/all_to_all | solution.py:419
  45.7 9.7 %collective-permute-start = (bf16[128,128]{1,0:T(8,128)(2,1)S(1)}, bf16[128,128]{1,0:T(8,128)(2,1)S(1)}, u32[]{:S(2)}, u32[]{:S(2)}) collective-permute-start(bf16[128,128]{1,0:T(8,128)(2,1)S(1)} %copy-done.10), channel_id=1, source_target_pairs={{0,4},{4,8},{8,12},{12,16},{16,20},{20,24},{24,28},{28,0},{1,5},{5... | collective-permute-start | bytes 98312 | tf_op jit(solution)/shard_map/ppermute | solution.py:195
  47.7 13.0 %copy-start.8 = (f32[1024]{0:T(1024)S(1)}, f32[1024]{0:T(1024)}, u32[]{:S(2)}) copy-start(f32[1024]{0:T(1024)} %param.13) | copy-start | bytes 12292
  47.7 9.1 %collective-permute-start.1 = (bf16[128,128]{1,0:T(8,128)(2,1)S(1)}, bf16[128,128]{1,0:T(8,128)(2,1)S(1)}, u32[]{:S(2)}, u32[]{:S(2)}) collective-permute-start(bf16[128,128]{1,0:T(8,128)(2,1)S(1)} %get-tuple-element.41), channel_id=1, source_target_pairs={{0,8},{4,12},{8,16},{12,20},{16,24},{20,28},{24,0},{28,4},{1,9},{5... | collective-permute-start | bytes 98312 | tf_op jit(solution)/shard_map/ppermute | solution.py:195
  49.2 9.1 %collective-permute-start.2 = (bf16[128,128]{1,0:T(8,128)(2,1)S(1)}, bf16[128,128]{1,0:T(8,128)(2,1)S(1)}, u32[]{:S(2)}, u32[]{:S(2)}) collective-permute-start(bf16[128,128]{1,0:T(8,128)(2,1)S(1)} %get-tuple-element.42), channel_id=1, source_target_pairs={{0,12},{4,16},{8,20},{12,24},{16,28},{20,0},{24,4},{28,8},{1,13},{... | collective-permute-start | bytes 98312 | tf_op jit(solution)/shard_map/ppermute | solution.py:195
  51.6 6.8 %collective-permute-start.3 = (bf16[128,128]{1,0:T(8,128)(2,1)S(1)}, bf16[128,128]{1,0:T(8,128)(2,1)S(1)}, u32[]{:S(2)}, u32[]{:S(2)}) collective-permute-start(bf16[128,128]{1,0:T(8,128)(2,1)S(1)} %get-tuple-element.43), channel_id=1, source_target_pairs={{0,16},{4,20},{8,24},{12,28},{16,0},{20,4},{24,8},{28,12},{1,17},{... | collective-permute-start | bytes 98312 | tf_op jit(solution)/shard_map/ppermute | solution.py:195
  53.0 5.3 %collective-permute-start.4 = (bf16[128,128]{1,0:T(8,128)(2,1)S(1)}, bf16[128,128]{1,0:T(8,128)(2,1)S(1)}, u32[]{:S(2)}, u32[]{:S(2)}) collective-permute-start(bf16[128,128]{1,0:T(8,128)(2,1)S(1)} %get-tuple-element.44), channel_id=1, source_target_pairs={{0,20},{4,24},{8,28},{12,0},{16,4},{20,8},{24,12},{28,16},{1,21},{... | collective-permute-start | bytes 98312 | tf_op jit(solution)/shard_map/ppermute | solution.py:195
  55.4 3.9 %collective-permute-start.5 = (bf16[128,128]{1,0:T(8,128)(2,1)S(1)}, bf16[128,128]{1,0:T(8,128)(2,1)S(1)}, u32[]{:S(2)}, u32[]{:S(2)}) collective-permute-start(bf16[128,128]{1,0:T(8,128)(2,1)S(1)} %get-tuple-element.48), channel_id=1, source_target_pairs={{0,24},{4,28},{8,0},{12,4},{16,8},{20,12},{24,16},{28,20},{1,25},{... | collective-permute-start | bytes 98312 | tf_op jit(solution)/shard_map/ppermute | solution.py:195
  56.8 3.9 %collective-permute-start.6 = (bf16[128,128]{1,0:T(8,128)(2,1)S(1)}, bf16[128,128]{1,0:T(8,128)(2,1)S(1)}, u32[]{:S(2)}, u32[]{:S(2)}) collective-permute-start(bf16[128,128]{1,0:T(8,128)(2,1)S(1)} %get-tuple-element.49), channel_id=1, source_target_pairs={{0,28},{4,0},{8,4},{12,8},{16,12},{20,16},{24,20},{28,24},{1,29},{... | collective-permute-start | bytes 98312 | tf_op jit(solution)/shard_map/ppermute | solution.py:195
  60.8 1.2 %copy-start.5 = (f32[2048,128]{1,0:T(8,128)S(1)}, f32[2048,128]{1,0:T(8,128)}, u32[]{:S(2)}) copy-start(f32[2048,128]{1,0:T(8,128)} %copy-done.4) | copy-start | bytes 3145732
  62.0 1.2 %copy-start.7 = (f32[2048,128]{1,0:T(8,128)S(1)}, f32[2048,128]{1,0:T(8,128)}, u32[]{:S(2)}) copy-start(f32[2048,128]{1,0:T(8,128)} %copy-done.6) | copy-start | bytes 3145732

commit v5 on v4

--- a/solution.py
+++ b/solution.py
@@ -150,14 +150,25 @@
     return terms[0]
 
 
-def local_kernel(seq_ref, q_ref, k_ref, v_ref, o_ref, coef_ref, conv_ref, grad_ref, *state_refs):
+def state_kernel(seq_ref, q_ref, k_ref, v_ref, o_ref, coef_ref, *refs):
+    state_refs, x_ref, g_ref = refs[:-2], refs[-2], refs[-1]
     tok_rows, width = k_ref.shape
     tiles = width // LANES
+    modes = coef_ref.shape[1]
     shards = len(state_refs) + 1
-    spread_tokens(k_ref, v_ref, conv_ref)
-    spread_tokens(o_ref, q_ref, grad_ref)
-    ahead = walk_tokens(conv_ref, coef_ref, tok_rows, tiles, 0, 1)
-    behind = walk_tokens(grad_ref, coef_ref, tok_rows, tiles, tok_rows - 1, -1)
+    spread_tokens(k_ref, v_ref, x_ref)
+    spread_tokens(o_ref, q_ref, g_ref)
+    decay = [coef_ref[0, m] for m in range(modes)]
+
+    def step(t, carry):
+        x = x_ref[pl.ds(t, tiles, stride=tok_rows), :]
+        g = g_ref[pl.ds(tok_rows - 1 - t, tiles, stride=tok_rows), :]
+        ahead = tuple(decay[m] * carry[0][m] + x for m in range(modes))
+        behind = tuple(decay[m] * carry[1][m] + g for m in range(modes))
+        return (ahead, behind)
+
+    zero = tuple(jnp.zeros((tiles, LANES), F32) for _ in range(modes))
+    ahead, behind = lax.fori_loop(0, tok_rows, step, (zero, zero), unroll=8)
     ahead = jnp.concatenate(ahead, axis=0).astype(LINK)
     behind = jnp.concatenate(behind, axis=0).astype(LINK)
     for k in range(1, shards):
@@ -172,23 +183,45 @@
             state_refs[k - 1][...] = behind
 
 
-def local_parts(seq_index, shards, query_proj, key_proj, value_proj, out_grad, coefs):
+def block_states(seq_index, shards, query_proj, key_proj, value_proj, out_grad, coefs):
     tok_rows, width = key_proj.shape
     modes, tiles = coefs.shape[1:3]
     whole = pl.BlockSpec(memory_space=pltpu.VMEM)
-    outs = pl.pallas_call(
+    return pl.pallas_call(
+        state_kernel,
+        in_specs=[pl.BlockSpec(memory_space=pltpu.SMEM)] + [whole] * 5,
+        out_specs=[whole] * (shards - 1),
+        out_shape=[jax.ShapeDtypeStruct((modes * tiles, LANES), LINK)] * (shards - 1),
+        scratch_shapes=[pltpu.VMEM((tok_rows * tiles, LANES), F32)] * 2,
+        compiler_params=pltpu.CompilerParams(vmem_limit_bytes=VMEM_BYTES),
+        cost_estimate=pl.CostEstimate(
+            flops=4 * modes * tok_rows * width, bytes_accessed=8 * tok_rows * width, transcendentals=0
+        ),
+        name="block_states",
+    )(seq_index, query_proj, key_proj, value_proj, out_grad, coefs)
+
+
+def local_kernel(q_ref, k_ref, v_ref, o_ref, coef_ref, conv_ref, grad_ref):
+    tok_rows, width = k_ref.shape
+    tiles = width // LANES
+    spread_tokens(k_ref, v_ref, conv_ref)
+    spread_tokens(o_ref, q_ref, grad_ref)
+    walk_tokens(conv_ref, coef_ref, tok_rows, tiles, 0, 1)
+    walk_tokens(grad_ref, coef_ref, tok_rows, tiles, tok_rows - 1, -1)
+
+
+def local_parts(query_proj, key_proj, value_proj, out_grad, coefs):
+    tok_rows, width = key_proj.shape
+    modes, tiles = coefs.shape[1:3]
+    return pl.pallas_call(
         local_kernel,
-        in_specs=[pl.BlockSpec(memory_space=pltpu.SMEM)] + [whole] * 5,
-        out_specs=[whole] * (shards + 1),
-        out_shape=[jax.ShapeDtypeStruct((tok_rows * tiles, LANES), F32)] * 2
-        + [jax.ShapeDtypeStruct((modes * tiles, LANES), LINK)] * (shards - 1),
+        out_shape=[jax.ShapeDtypeStruct((tok_rows * tiles, LANES), F32)] * 2,
         compiler_params=pltpu.CompilerParams(vmem_limit_bytes=VMEM_BYTES),
         cost_estimate=pl.CostEstimate(
             flops=8 * modes * tok_rows * width, bytes_accessed=8 * tok_rows * width, transcendentals=0
         ),
         name="local_parts",
-    )(seq_index, query_proj, key_proj, value_proj, out_grad, coefs)
-    return outs[:2], outs[2:]
+    )(query_proj, key_proj, value_proj, out_grad, coefs)
 
 
 def send_state(state, shards, k):
@@ -408,18 +441,19 @@
     coefs = jnp.broadcast_to(coefs, (3, modes, width // FILTERS, FILTERS // LANES, LANES))
     coefs = coefs.reshape(3, modes, width // LANES, LANES)
     seq_index = lax.axis_index("seq").reshape(1)
-    parts, states = local_parts(seq_index, shards, *signals, coefs)
-    early = [send_state(states[k - 1], shards, k) for k in range(1, min(shards, 6))]
-    received, *parts = lax.optimization_barrier((received, *parts))
+    states = block_states(seq_index, shards, *signals, coefs)
+    *states, coefs = lax.optimization_barrier((*states, coefs))
+    states = [send_state(state, shards, 1 + i) for i, state in enumerate(states)]
+    parts = local_parts(*signals, coefs)
+    received, *parts = lax.optimization_barrier((received, *parts, *states))
+    parts, states = parts[:2], parts[2:]
 
     scale = 1.0 / math.sqrt(length * (CHANNELS // FILTERS))
     lags = filter_lags(received, shards, chans, owned, scale)
-    lags, *late = lax.optimization_barrier((lags, *states[5:]))
-    late = [send_state(state, shards, 6 + i) for i, state in enumerate(late)]
     lags = lax.all_to_all(lags, "seq", split_axis=0, concat_axis=0, tiled=True)
     filter_grad = lags.reshape(shards * owned, tok_rows).T
     layer_out, key_grad, value_grad = final_outputs(
-        seq_index, signals, coefs, skip_gain[None, :], parts, early + late
+        seq_index, signals, coefs, skip_gain[None, :], parts, states
     )
     return (layer_out, key_grad, value_grad, filter_grad)
 

time: 71.3 us -> 73.7 us (1.034)
  waiting for transfers between devices: 16.3 us -> 9.16 us
  starting transfers between devices: 23.7 us -> 28.8 us
  Pallas kernels: 23.3 us -> 27 us
  local copies, waits for them, and re-layouts: 6.6 us -> 7.34 us
    all_to_all x1, waiting for transfers between devices: 13.9 us -> 0.01 us  [per_device(): lax.all_to_all(send, ('seq', 'chan'), split_axis=0, concat_axis=0, tiled=...]
    all_to_all x1, starting transfers between devices: 3.81 us -> 11.7 us  [per_device(): lags = lax.all_to_all(lags, 'seq', split_axis=0, concat_axis=0, tiled=True)]
    ppermute x7, waiting for transfers between devices: 2.45 us -> 9.16 us  [send_state(): lax.ppermute(state, 'seq', [(i, (i + k) % shards) for i in range(shards)])]
    pallas_call x1 -> x2, Pallas kernels: 8.75 us -> 12.5 us  [the longest x1 8.54 us: local_parts(): pl.pallas_call(local_kernel, out_shape=[jax.ShapeDtypeStruct((tok_rows *...]
    ppermute x7, starting transfers between devices: 12.6 us -> 9.79 us  [send_state(): lax.ppermute(state, 'seq', [(i, (i + k) % shards) for i in range(shards)])]
  transfers between devices with their start and end apart: 9 -> 9, of which waited for: 3 -> 1; matrix products, arithmetic and copies ran while one was open for 0% -> 0% of each run, Pallas kernels for 22% -> 26%
where the time goes in v5:
time: 73.7 us; the launch traced here: 73.2 us
  starting transfers between devices  28.8 us (39%)
  Pallas kernels  27 us (37%)
  waiting for transfers between devices  9.16 us (12%)
  local copies, waits for them, and re-layouts  7.34 us (10%)
  between operations  0.86 us (1%)
    all_to_all x1, starting transfers between devices, per_device(): lags = lax.all_to_all(lags, 'seq', split_axis=0, concat_axis=0, tiled=True)  11.7 us
    ppermute x7, starting transfers between devices, send_state(): lax.ppermute(state, 'seq', [(i, (i + k) % shards) for i in range(shards)])  9.79 us
    ppermute x7, waiting for transfers between devices, send_state(): lax.ppermute(state, 'seq', [(i, (i + k) % shards) for i in range(shards)])  9.16 us
    pallas_call x1, Pallas kernels, local_parts(): pl.pallas_call(local_kernel, out_shape=[jax.ShapeDtypeStruct((tok_rows *...  8.54 us
    all_to_all x1, starting transfers between devices, per_device(): lax.all_to_all(send, ('seq', 'chan'), split_axis=0, concat_axis=0, tiled=...  7.3 us
    unnamed x27, local copies, waits for them, and re-layouts  7.26 us
    pallas_call x1, Pallas kernels, final_outputs(): pl.pallas_call(final_kernel, in_specs=[pl.BlockSpec(memory_space=pltpu.SM...  6.88 us
    pallas_call x1, Pallas kernels, filter_lags(): pl.pallas_call(functools.partial(lag_kernel, shards, chans, groups, owned...  4.53 us
  transfers between devices with their start and end apart: 9, of which 1 were waited for; matrix products, arithmetic and copies ran while one was open for 0% of the time, Pallas kernels for 26%

profile of v5, /device:TPU:0, one launch (start us, length us, event | category | flops | bytes accessed | tf_op | source)
XLA Modules:
  0.0 73.2 jit_solution(13276928687223810775)
XLA Ops:
  0.6 3.1 %pack_signals.1 = bf16[32,64,256]{2,1,0:T(8,128)(2,1)} custom-call(bf16[256,1024]{1,0:T(8,128)(2,1)} %k_ref.2, bf16[256,1024]{1,0:T(8,128)(2,1)} %v_ref.2, bf16[256,1024]{1,0:T(8,128)(2,1)} %o_ref.2, bf16[256,1024]{1,0:T(8,128)(2,1)} %q_ref.2), custom_call_target="tpu_custom_call" | custom-call | tf_op jit(solution)/shard_map/pack_signals/pallas_call | solution.py:102
  3.7 0.0 copy-start.11
  3.7 0.0 copy-start.12
  3.8 0.0 copy-start.1
  3.8 0.0 copy-start.2
  3.8 0.0 copy-start.3
  3.8 7.3 %all-to-all-start = ((bf16[32,64,256]{2,1,0:T(8,128)(2,1)}), bf16[32,64,256]{2,1,0:T(8,128)(2,1)S(1)}, u32[]{:S(2)}, u32[]{:S(2)}) async-start(bf16[32,64,256]{2,1,0:T(8,128)(2,1)} %pack_signals.1), calls=%async_computation | async-start | bytes 2097152 | tf_op jit(solution)/shard_map/all_to_all | solution.py:431
  11.1 0.0 copy-start
  11.1 0.0 copy-done.11
  11.1 0.0 copy-done.12
  11.2 0.1 broadcast_in_dim.11
  11.3 0.0 copy-done.1
  11.3 0.0 copy-done.2
  11.3 0.0 copy-done.3
  11.3 0.8 %copy-done = bf16[256,1024]{1,0:T(8,128)(2,1)S(1)} copy-done((bf16[256,1024]{1,0:T(8,128)(2,1)S(1)}, bf16[256,1024]{1,0:T(8,128)(2,1)}, u32[]{:S(2)}) %copy-start) | copy-done | bytes 524312
  12.1 3.9 %block_states.1 = (bf16[128,128]{1,0:T(8,128)(2,1)S(1)}, bf16[128,128]{1,0:T(8,128)(2,1)S(1)}, bf16[128,128]{1,0:T(8,128)(2,1)S(1)}, bf16[128,128]{1,0:T(8,128)(...) custom-call(s32[1]{0:T(128)} %bitcast.seq_ref, ...), custom_call_target="tpu_custom_call" | custom-call | flops 16777216 | bytes 2097152 | tf_op jit(solution)/shard_map/block_states/pallas_call | solution.py:190
  16.1 1.8 %collective-permute-start = (bf16[128,128]{1,0:T(8,128)(2,1)S(1)}, bf16[128,128]{1,0:T(8,128)(2,1)S(1)}, u32[]{:S(2)}, u32[]{:S(2)}) collective-permute-start(bf16[128,128]{1,0:T(8,128)(2,1)S(1)} %get-tuple-element.58), channel_id=1, source_target_pairs={{0,4},{4,8},{8,12},{12,16},{16,20},{20,24},{24,28},{28,0},{1,5},{5... | collective-permute-start | bytes 98312 | tf_op jit(solution)/shard_map/ppermute | solution.py:228
  17.9 1.5 %collective-permute-start.1 = (bf16[128,128]{1,0:T(8,128)(2,1)S(1)}, bf16[128,128]{1,0:T(8,128)(2,1)S(1)}, u32[]{:S(2)}, u32[]{:S(2)}) collective-permute-start(bf16[128,128]{1,0:T(8,128)(2,1)S(1)} %get-tuple-element.59), channel_id=1, source_target_pairs={{0,8},{4,12},{8,16},{12,20},{16,24},{20,28},{24,0},{28,4},{1,9},{5... | collective-permute-start | bytes 98312 | tf_op jit(solution)/shard_map/ppermute | solution.py:228
  19.4 2.4 %collective-permute-start.2 = (bf16[128,128]{1,0:T(8,128)(2,1)S(1)}, bf16[128,128]{1,0:T(8,128)(2,1)S(1)}, u32[]{:S(2)}, u32[]{:S(2)}) collective-permute-start(bf16[128,128]{1,0:T(8,128)(2,1)S(1)} %get-tuple-element.60), channel_id=1, source_target_pairs={{0,12},{4,16},{8,20},{12,24},{16,28},{20,0},{24,4},{28,8},{1,13},{... | collective-permute-start | bytes 98312 | tf_op jit(solution)/shard_map/ppermute | solution.py:228
  21.8 1.4 %collective-permute-start.3 = (bf16[128,128]{1,0:T(8,128)(2,1)S(1)}, bf16[128,128]{1,0:T(8,128)(2,1)S(1)}, u32[]{:S(2)}, u32[]{:S(2)}) collective-permute-start(bf16[128,128]{1,0:T(8,128)(2,1)S(1)} %get-tuple-element.61), channel_id=1, source_target_pairs={{0,16},{4,20},{8,24},{12,28},{16,0},{20,4},{24,8},{28,12},{1,17},{... | collective-permute-start | bytes 98312 | tf_op jit(solution)/shard_map/ppermute | solution.py:228
  23.2 2.4 %collective-permute-start.4 = (bf16[128,128]{1,0:T(8,128)(2,1)S(1)}, bf16[128,128]{1,0:T(8,128)(2,1)S(1)}, u32[]{:S(2)}, u32[]{:S(2)}) collective-permute-start(bf16[128,128]{1,0:T(8,128)(2,1)S(1)} %get-tuple-element.62), channel_id=1, source_target_pairs={{0,20},{4,24},{8,28},{12,0},{16,4},{20,8},{24,12},{28,16},{1,21},{... | collective-permute-start | bytes 98312 | tf_op jit(solution)/shard_map/ppermute | solution.py:228
  25.6 9.1 %collective-permute-done.refs_0_ = bf16[128,128]{1,0:T(8,128)(2,1)S(1)} collective-permute-done((bf16[128,128]{1,0:T(8,128)(2,1)S(1)}, bf16[128,128]{1,0:T(8,128)(2,1)S(1)}, u32[]{:S(2)}, u32[]{:S(2)}) %collective-permute-start) | collective-permute-done | bytes 32800 | tf_op jit(solution)/shard_map/ppermute | solution.py:228
  34.8 0.0 collective-permute-start.5
  34.8 0.0 collective-permute-done.1.refs_1_
  34.8 0.2 collective-permute-start.6
  35.0 8.5 %local_parts.1 = (f32[2048,128]{1,0:T(8,128)S(1)}, f32[2048,128]{1,0:T(8,128)S(1)}) custom-call(bf16[256,1024]{1,0:T(8,128)(2,1)S(1)} %copy-done, bf16[256,1024]{1,0:T(8,128)(2,1)S(1)} %copy-done.1, bf16[256,1024]{1,0:T(8,128)(2,1)S(1)} %copy-done.2, bf16[256,1024]{1,0:T(8,128)(2,1)S(1)} %copy-done.3, f32[3,16,8,128]{3,2,1,0:T(8,128)S(1)} %bitcast.15), custom_call_target="tpu_custom_call" | custom-call | flops 33554432 | bytes 2097152 | tf_op jit(solution)/shard_map/local_parts/pallas_call | solution.py:216
  43.6 0.0 copy-start.4
  43.6 0.9 %copy-done.4 = f32[2048,128]{1,0:T(8,128)} copy-done((f32[2048,128]{1,0:T(8,128)}, f32[2048,128]{1,0:T(8,128)S(1)}, u32[]{:S(2)}) %copy-start.4) | copy-done | bytes 1048600
  44.5 0.0 copy-start.6
  44.5 1.0 %copy-done.6 = f32[2048,128]{1,0:T(8,128)} copy-done((f32[2048,128]{1,0:T(8,128)}, f32[2048,128]{1,0:T(8,128)S(1)}, u32[]{:S(2)}) %copy-start.6) | copy-done | bytes 1048600
  45.5 0.0 collective-permute-done.2.refs_2_
  45.5 0.0 collective-permute-done.3.refs_3_
  45.5 0.0 collective-permute-done.4.refs_4_
  45.5 0.0 collective-permute-done.5.refs_5_
  45.5 0.0 collective-permute-done.6.refs_6_
  45.5 0.0 copy-start.8
  45.6 0.6 copy-done.8
  46.2 0.0 all-to-all-done.refs_0_
  46.2 4.5 %filter_lags.1 = f32[8,8,256]{2,1,0:T(8,128)} custom-call(bf16[32,64,256]{2,1,0:T(8,128)(2,1)S(1)} %all-to-all-done.refs_0_), custom_call_target="tpu_custom_call" | custom-call | tf_op jit(solution)/shard_map/filter_lags/pallas_call | solution.py:405
  50.7 0.0 copy-start.10
  50.7 11.7 %all-to-all-start.1 = ((f32[8,8,256]{2,1,0:T(8,128)}), f32[8,8,256]{2,1,0:T(8,128)S(1)}, u32[]{:S(2)}, u32[]{:S(2)}) async-start(f32[8,8,256]{2,1,0:T(8,128)} %filter_lags.1), calls=%async_computation.1 | async-start | bytes 131072 | tf_op jit(solution)/shard_map/all_to_all | solution.py:453
  62.4 0.0 copy-done.10
  62.4 0.0 copy-start.5
  62.5 1.2 %copy-done.5 = f32[2048,128]{1,0:T(8,128)S(1)} copy-done((f32[2048,128]{1,0:T(8,128)S(1)}, f32[2048,128]{1,0:T(8,128)}, u32[]{:S(2)}) %copy-start.5) | copy-done | bytes 1048600
  63.7 0.0 copy-start.7
  63.7 1.2 %copy-done.7 = f32[2048,128]{1,0:T(8,128)S(1)} copy-done((f32[2048,128]{1,0:T(8,128)S(1)}, f32[2048,128]{1,0:T(8,128)}, u32[]{:S(2)}) %copy-start.7) | copy-done | bytes 1048600
  64.9 0.0 copy-start.9
  64.9 0.8 %copy-done.9 = bf16[128,128]{1,0:T(8,128)(2,1)S(1)} copy-done((bf16[128,128]{1,0:T(8,128)(2,1)S(1)}, bf16[128,128]{1,0:T(8,128)(2,1)}, u32[]{:S(2)}) %copy-start.9) | copy-done | bytes 32792
  65.7 6.9 %final_outputs.1 = (bf16[256,1024]{1,0:T(8,128)(2,1)}, bf16[256,1024]{1,0:T(8,128)(2,1)}, bf16[256,1024]{1,0:T(8,128)(2,1)}) custom-call(s32[1]{0:T(128)} %bitcast.seq_ref, bf16[256,1024]{1,0:T(8,128)(2,1)S(1)} %copy-done, bf16[256,1024]{1,0:T(8,128)(2,1)S(1)} %copy-done.1, bf16[256,1024]{1,0:T(8,128)(2,1)S(1)} %copy-done.2, ...), custom_call_target="tpu_custom_call" | custom-call | flops 33554432 | bytes 3670016 | tf_op jit(solution)/shard_map/final_outputs/pallas_call | solution.py:301
  72.5 0.0 all-to-all-done.1
  72.6 0.6 copy.12
  (3 shorter events, 0.1 us)
Async XLA Ops:
  3.7 7.4 %copy-start.11 = (f32[256,16]{0,1:T(8,128)S(1)}, f32[256,16]{0,1:T(8,128)}, u32[]{:S(2)}) copy-start(f32[256,16]{0,1:T(8,128)} %param.12) | copy-start | bytes 49156
  3.7 7.4 %copy-start.12 = (f32[256,16]{0,1:T(8,128)S(1)}, f32[256,16]{0,1:T(8,128)}, u32[]{:S(2)}) copy-start(f32[256,16]{0,1:T(8,128)} %param.11) | copy-start | bytes 49156
  3.8 7.5 %copy-start.1 = (bf16[256,1024]{1,0:T(8,128)(2,1)S(1)}, bf16[256,1024]{1,0:T(8,128)(2,1)}, u32[]{:S(2)}) copy-start(bf16[256,1024]{1,0:T(8,128)(2,1)} %k_ref.2) | copy-start | bytes 1572868
  3.8 7.5 %copy-start.2 = (bf16[256,1024]{1,0:T(8,128)(2,1)S(1)}, bf16[256,1024]{1,0:T(8,128)(2,1)}, u32[]{:S(2)}) copy-start(bf16[256,1024]{1,0:T(8,128)(2,1)} %v_ref.2) | copy-start | bytes 1572868
  3.8 7.5 %copy-start.3 = (bf16[256,1024]{1,0:T(8,128)(2,1)S(1)}, bf16[256,1024]{1,0:T(8,128)(2,1)}, u32[]{:S(2)}) copy-start(bf16[256,1024]{1,0:T(8,128)(2,1)} %o_ref.2) | copy-start | bytes 1572868
  3.8 42.4 %all-to-all-start = ((bf16[32,64,256]{2,1,0:T(8,128)(2,1)}), bf16[32,64,256]{2,1,0:T(8,128)(2,1)S(1)}, u32[]{:S(2)}, u32[]{:S(2)}) async-start(bf16[32,64,256]{2,1,0:T(8,128)(2,1)} %pack_signals.1), calls=%async_computation | async-start | bytes 2097152 | tf_op jit(solution)/shard_map/all_to_all | solution.py:431
  11.1 1.0 %copy-start = (bf16[256,1024]{1,0:T(8,128)(2,1)S(1)}, bf16[256,1024]{1,0:T(8,128)(2,1)}, u32[]{:S(2)}) copy-start(bf16[256,1024]{1,0:T(8,128)(2,1)} %q_ref.2) | copy-start | bytes 1572868
  16.1 18.7 %collective-permute-start = (bf16[128,128]{1,0:T(8,128)(2,1)S(1)}, bf16[128,128]{1,0:T(8,128)(2,1)S(1)}, u32[]{:S(2)}, u32[]{:S(2)}) collective-permute-start(bf16[128,128]{1,0:T(8,128)(2,1)S(1)} %get-tuple-element.58), channel_id=1, source_target_pairs={{0,4},{4,8},{8,12},{12,16},{16,20},{20,24},{24,28},{28,0},{1,5},{5... | collective-permute-start | bytes 98312 | tf_op jit(solution)/shard_map/ppermute | solution.py:228
  17.9 16.9 %collective-permute-start.1 = (bf16[128,128]{1,0:T(8,128)(2,1)S(1)}, bf16[128,128]{1,0:T(8,128)(2,1)S(1)}, u32[]{:S(2)}, u32[]{:S(2)}) collective-permute-start(bf16[128,128]{1,0:T(8,128)(2,1)S(1)} %get-tuple-element.59), channel_id=1, source_target_pairs={{0,8},{4,12},{8,16},{12,20},{16,24},{20,28},{24,0},{28,4},{1,9},{5... | collective-permute-start | bytes 98312 | tf_op jit(solution)/shard_map/ppermute | solution.py:228
  19.4 26.1 %collective-permute-start.2 = (bf16[128,128]{1,0:T(8,128)(2,1)S(1)}, bf16[128,128]{1,0:T(8,128)(2,1)S(1)}, u32[]{:S(2)}, u32[]{:S(2)}) collective-permute-start(bf16[128,128]{1,0:T(8,128)(2,1)S(1)} %get-tuple-element.60), channel_id=1, source_target_pairs={{0,12},{4,16},{8,20},{12,24},{16,28},{20,0},{24,4},{28,8},{1,13},{... | collective-permute-start | bytes 98312 | tf_op jit(solution)/shard_map/ppermute | solution.py:228
  21.8 23.7 %collective-permute-start.3 = (bf16[128,128]{1,0:T(8,128)(2,1)S(1)}, bf16[128,128]{1,0:T(8,128)(2,1)S(1)}, u32[]{:S(2)}, u32[]{:S(2)}) collective-permute-start(bf16[128,128]{1,0:T(8,128)(2,1)S(1)} %get-tuple-element.61), channel_id=1, source_target_pairs={{0,16},{4,20},{8,24},{12,28},{16,0},{20,4},{24,8},{28,12},{1,17},{... | collective-permute-start | bytes 98312 | tf_op jit(solution)/shard_map/ppermute | solution.py:228
  23.2 22.3 %collective-permute-start.4 = (bf16[128,128]{1,0:T(8,128)(2,1)S(1)}, bf16[128,128]{1,0:T(8,128)(2,1)S(1)}, u32[]{:S(2)}, u32[]{:S(2)}) collective-permute-start(bf16[128,128]{1,0:T(8,128)(2,1)S(1)} %get-tuple-element.62), channel_id=1, source_target_pairs={{0,20},{4,24},{8,28},{12,0},{16,4},{20,8},{24,12},{28,16},{1,21},{... | collective-permute-start | bytes 98312 | tf_op jit(solution)/shard_map/ppermute | solution.py:228
  34.8 10.7 %collective-permute-start.5 = (bf16[128,128]{1,0:T(8,128)(2,1)S(1)}, bf16[128,128]{1,0:T(8,128)(2,1)S(1)}, u32[]{:S(2)}, u32[]{:S(2)}) collective-permute-start(bf16[128,128]{1,0:T(8,128)(2,1)S(1)} %get-tuple-element.63), channel_id=1, source_target_pairs={{0,24},{4,28},{8,0},{12,4},{16,8},{20,12},{24,16},{28,20},{1,25},{... | collective-permute-start | bytes 98312 | tf_op jit(solution)/shard_map/ppermute | solution.py:228
  34.8 10.8 %collective-permute-start.6 = (bf16[128,128]{1,0:T(8,128)(2,1)S(1)}, bf16[128,128]{1,0:T(8,128)(2,1)S(1)}, u32[]{:S(2)}, u32[]{:S(2)}) collective-permute-start(bf16[128,128]{1,0:T(8,128)(2,1)S(1)} %get-tuple-element.64), channel_id=1, source_target_pairs={{0,28},{4,0},{8,4},{12,8},{16,12},{20,16},{24,20},{28,24},{1,29},{... | collective-permute-start | bytes 98312 | tf_op jit(solution)/shard_map/ppermute | solution.py:228
  43.6 0.9 %copy-start.4 = (f32[2048,128]{1,0:T(8,128)}, f32[2048,128]{1,0:T(8,128)S(1)}, u32[]{:S(2)}) copy-start(f32[2048,128]{1,0:T(8,128)S(1)} %get-tuple-element.65.x_ref) | copy-start | bytes 3145732
  44.5 1.0 %copy-start.6 = (f32[2048,128]{1,0:T(8,128)}, f32[2048,128]{1,0:T(8,128)S(1)}, u32[]{:S(2)}) copy-start(f32[2048,128]{1,0:T(8,128)S(1)} %get-tuple-element.66.g_ref) | copy-start | bytes 3145732
  45.5 0.6 copy-start.8
  50.7 11.7 %copy-start.10 = (f32[1024]{0:T(1024)S(1)}, f32[1024]{0:T(1024)}, u32[]{:S(2)}) copy-start(f32[1024]{0:T(1024)} %param.13) | copy-start | bytes 12292
  50.7 21.8 %all-to-all-start.1 = ((f32[8,8,256]{2,1,0:T(8,128)}), f32[8,8,256]{2,1,0:T(8,128)S(1)}, u32[]{:S(2)}, u32[]{:S(2)}) async-start(f32[8,8,256]{2,1,0:T(8,128)} %filter_lags.1), calls=%async_computation.1 | async-start | bytes 131072 | tf_op jit(solution)/shard_map/all_to_all | solution.py:453
  62.4 1.2 %copy-start.5 = (f32[2048,128]{1,0:T(8,128)S(1)}, f32[2048,128]{1,0:T(8,128)}, u32[]{:S(2)}) copy-start(f32[2048,128]{1,0:T(8,128)} %copy-done.4) | copy-start | bytes 3145732
  63.7 1.2 %copy-start.7 = (f32[2048,128]{1,0:T(8,128)S(1)}, f32[2048,128]{1,0:T(8,128)}, u32[]{:S(2)}) copy-start(f32[2048,128]{1,0:T(8,128)} %copy-done.6) | copy-start | bytes 3145732
  64.9 0.8 %copy-start.9 = (bf16[128,128]{1,0:T(8,128)(2,1)S(1)}, bf16[128,128]{1,0:T(8,128)(2,1)}, u32[]{:S(2)}) copy-start(bf16[128,128]{1,0:T(8,128)(2,1)} %copy-done.8) | copy-start | bytes 98308

commit v6 on v5

--- a/solution.py
+++ b/solution.py
@@ -12,7 +12,7 @@
 FILTERS = 256
 LANES = 128
 SUBLANES = 8
-VMEM_BYTES = 48 * 1024 * 1024
+VMEM_BYTES = 16 * 1024 * 1024
 PACK_VMEM_BYTES = 62 * 1024 * 1024
 F32 = jnp.float32
 BF16 = jnp.bfloat16
@@ -151,11 +151,11 @@
 
 
 def state_kernel(seq_ref, q_ref, k_ref, v_ref, o_ref, coef_ref, *refs):
-    state_refs, x_ref, g_ref = refs[:-2], refs[-2], refs[-1]
+    state_refs, own_ref, x_ref, g_ref = refs[:-3], *refs[-3:]
     tok_rows, width = k_ref.shape
     tiles = width // LANES
     modes = coef_ref.shape[1]
-    shards = len(state_refs) + 1
+    pairs = len(state_refs) + 1
     spread_tokens(k_ref, v_ref, x_ref)
     spread_tokens(o_ref, q_ref, g_ref)
     decay = [coef_ref[0, m] for m in range(modes)]
@@ -169,29 +169,32 @@
 
     zero = tuple(jnp.zeros((tiles, LANES), F32) for _ in range(modes))
     ahead, behind = lax.fori_loop(0, tok_rows, step, (zero, zero), unroll=8)
-    ahead = jnp.concatenate(ahead, axis=0).astype(LINK)
-    behind = jnp.concatenate(behind, axis=0).astype(LINK)
-    for k in range(1, shards):
-        stays = seq_ref[0] + k < shards
+    ahead = jnp.concatenate(ahead, axis=0)
+    behind = jnp.concatenate(behind, axis=0)
+    own_ref[0] = ahead
+    own_ref[1] = behind
+    for k in range(1, pairs):
+        stays = seq_ref[0] // 2 + k < pairs
 
         @pl.when(stays)
         def _():
-            state_refs[k - 1][...] = ahead
+            state_refs[k - 1][...] = ahead.astype(LINK)
 
         @pl.when(jnp.logical_not(stays))
         def _():
-            state_refs[k - 1][...] = behind
-
-
-def block_states(seq_index, shards, query_proj, key_proj, value_proj, out_grad, coefs):
+            state_refs[k - 1][...] = behind.astype(LINK)
+
+
+def block_states(seq_index, pairs, query_proj, key_proj, value_proj, out_grad, coefs):
     tok_rows, width = key_proj.shape
     modes, tiles = coefs.shape[1:3]
     whole = pl.BlockSpec(memory_space=pltpu.VMEM)
-    return pl.pallas_call(
+    *states, own = pl.pallas_call(
         state_kernel,
         in_specs=[pl.BlockSpec(memory_space=pltpu.SMEM)] + [whole] * 5,
-        out_specs=[whole] * (shards - 1),
-        out_shape=[jax.ShapeDtypeStruct((modes * tiles, LANES), LINK)] * (shards - 1),
+        out_specs=[whole] * pairs,
+        out_shape=[jax.ShapeDtypeStruct((modes * tiles, LANES), LINK)] * (pairs - 1)
+        + [jax.ShapeDtypeStruct((2, modes * tiles, LANES), F32)],
         scratch_shapes=[pltpu.VMEM((tok_rows * tiles, LANES), F32)] * 2,
         compiler_params=pltpu.CompilerParams(vmem_limit_bytes=VMEM_BYTES),
         cost_estimate=pl.CostEstimate(
@@ -199,6 +202,49 @@
         ),
         name="block_states",
     )(seq_index, query_proj, key_proj, value_proj, out_grad, coefs)
+    return states, own
+
+
+def pair_kernel(seq_ref, coef_ref, own_ref, *refs):
+    state_refs, kept_ref, given_ref = refs[:-2], *refs[-2:]
+    pairs = len(state_refs) + 1
+    modes, tiles = coef_ref.shape[1:3]
+    pair = seq_ref[0] // 2
+    second = seq_ref[0] % 2 == 1
+    for m in range(modes):
+        rows = slice(m * tiles, (m + 1) * tiles)
+        decay = coef_ref[1, m]
+        both = decay * decay
+        before = jnp.zeros((tiles, LANES), F32)
+        after = jnp.zeros((tiles, LANES), F32)
+        for k in range(pairs - 1, 0, -1):
+            block = state_refs[k - 1][...].astype(F32)[rows]
+            before = both * before + jnp.where(k <= pair, block, 0.0)
+            block = state_refs[pairs - k - 1][...].astype(F32)[rows]
+            after = both * after + jnp.where(k <= pairs - 1 - pair, block, 0.0)
+        before = jnp.where(second, before, decay * before)
+        after = jnp.where(second, decay * after, after)
+        kept_ref[0, rows] = jnp.where(second, decay * before, before)
+        kept_ref[1, rows] = jnp.where(second, after, decay * after)
+        own = own_ref[0, rows]
+        given_ref[0, rows] = jnp.where(second, before, decay * before + own).astype(LINK)
+        own = own_ref[1, rows]
+        given_ref[1, rows] = jnp.where(second, decay * after + own, after).astype(LINK)
+
+
+def pair_states(seq_index, coefs, own, states):
+    whole = pl.BlockSpec(memory_space=pltpu.VMEM)
+    return pl.pallas_call(
+        pair_kernel,
+        in_specs=[pl.BlockSpec(memory_space=pltpu.SMEM)] + [whole] * (2 + len(states)),
+        out_specs=[whole] * 2,
+        out_shape=[
+            jax.ShapeDtypeStruct(own.shape, F32),
+            jax.ShapeDtypeStruct(own.shape, LINK),
+        ],
+        compiler_params=pltpu.CompilerParams(vmem_limit_bytes=VMEM_BYTES),
+        name="pair_states",
+    )(seq_index, coefs, own, *states)
 
 
 def local_kernel(q_ref, k_ref, v_ref, o_ref, coef_ref, conv_ref, grad_ref):
@@ -224,22 +270,13 @@
     )(query_proj, key_proj, value_proj, out_grad, coefs)
 
 
-def send_state(state, shards, k):
-    return lax.ppermute(state, "seq", [(i, (i + k) % shards) for i in range(shards)])
-
-
-def edge_states(seq, state_refs, coef_ref, later):
-    shards = len(state_refs) + 1
-    modes, tiles = coef_ref.shape[1:3]
-    held = [jnp.zeros((tiles, LANES), F32) for _ in range(modes)]
-    count = shards - 1 - seq if later else seq
-    for k in range(shards - 1, 0, -1):
-        ref = state_refs[shards - k - 1 if later else k - 1]
-        block = jnp.where(k <= count, ref[...].astype(F32), 0.0)
-        held = [
-            coef_ref[1, m] * held[m] + block[m * tiles : (m + 1) * tiles] for m in range(modes)
-        ]
-    return held
+def along_column(state, pairs, k):
+    route = [(2 * p + b, 2 * ((p + k) % pairs) + b) for p in range(pairs) for b in range(2)]
+    return lax.ppermute(state, "seq", route)
+
+
+def inside_pair(state, pairs):
+    return lax.ppermute(state, "seq", [(i, i ^ 1) for i in range(2 * pairs)])
 
 
 def add_edge(ref, held, coef_ref, tok_rows, tiles, start, move):
@@ -256,11 +293,18 @@
     lax.fori_loop(0, tok_rows, step, held, unroll=8)
 
 
-def final_kernel(seq_ref, q_ref, k_ref, v_ref, o_ref, coef_ref, gain_ref, x_ref, g_ref, *refs):
-    state_refs, hbm_refs, held_refs, sems = refs[:-7], refs[-7:-4], refs[-4:-1], refs[-1]
+def final_kernel(
+    q_ref, k_ref, v_ref, o_ref, coef_ref, gain_ref, x_ref, g_ref, kept_ref, given_ref, *refs
+):
+    hbm_refs, held_refs, sems = refs[:3], refs[3:6], refs[6]
     layer_ref, key_ref, value_ref = held_refs
     tok_rows, width = k_ref.shape
     tiles = width // LANES
+    modes = coef_ref.shape[1]
+
+    def edge(side):
+        total = kept_ref[side] + given_ref[side].astype(F32)
+        return [total[m * tiles : (m + 1) * tiles] for m in range(modes)]
 
     def departure(i, tile):
         place = (slice(None), pl.ds(tile * LANES, LANES))
@@ -268,8 +312,7 @@
             held_refs[i].at[place], hbm_refs[i].at[place], sems.at[i, tile]
         )
 
-    edge = edge_states(seq_ref[0], state_refs, coef_ref, False)
-    add_edge(x_ref, edge, coef_ref, tok_rows, tiles, 0, 1)
+    add_edge(x_ref, edge(0), coef_ref, tok_rows, tiles, 0, 1)
     for tile in range(tiles):
         cols = slice(tile * LANES, (tile + 1) * LANES)
         rows = slice(tile * tok_rows, (tile + 1) * tok_rows)
@@ -277,8 +320,7 @@
         long_conv = x_ref[rows, :] + gain_ref[:, cols] * conv_in
         layer_ref[:, cols] = (q_ref[:, cols].astype(F32) * long_conv).astype(BF16)
         departure(0, tile).start()
-    edge = edge_states(seq_ref[0], state_refs, coef_ref, True)
-    add_edge(g_ref, edge, coef_ref, tok_rows, tiles, tok_rows - 1, -1)
+    add_edge(g_ref, edge(1), coef_ref, tok_rows, tiles, tok_rows - 1, -1)
     for tile in range(tiles):
         cols = slice(tile * LANES, (tile + 1) * LANES)
         rows = slice(tile * tok_rows, (tile + 1) * tok_rows)
@@ -293,14 +335,14 @@
             departure(i, tile).wait()
 
 
-def final_outputs(seq_index, signals, coefs, gain, parts, states):
+def final_outputs(signals, coefs, gain, parts, kept, given):
     tok_rows, width = signals[0].shape
     modes, tiles = coefs.shape[1:3]
-    args = (*signals, coefs, gain, *parts, *states)
+    args = (*signals, coefs, gain, *parts, kept, given)
     whole = pl.BlockSpec(memory_space=pltpu.VMEM)
     return pl.pallas_call(
         final_kernel,
-        in_specs=[pl.BlockSpec(memory_space=pltpu.SMEM)] + [whole] * len(args),
+        in_specs=[whole] * len(args),
         out_specs=[pl.BlockSpec(memory_space=pl.ANY)] * 3,
         out_shape=[jax.ShapeDtypeStruct((tok_rows, width), BF16)] * 3,
         scratch_shapes=[pltpu.VMEM((tok_rows, width), BF16)] * 3
@@ -310,7 +352,7 @@
             flops=8 * modes * tok_rows * width, bytes_accessed=14 * tok_rows * width, transcendentals=0
         ),
         name="final_outputs",
-    )(seq_index, *args)
+    )(*args)
 
 
 def lag_kernel(shards, chans, groups, owned, scale, *refs):
@@ -441,19 +483,21 @@
     coefs = jnp.broadcast_to(coefs, (3, modes, width // FILTERS, FILTERS // LANES, LANES))
     coefs = coefs.reshape(3, modes, width // LANES, LANES)
     seq_index = lax.axis_index("seq").reshape(1)
-    states = block_states(seq_index, shards, *signals, coefs)
+    pairs = shards // 2
+    states, own = block_states(seq_index, pairs, *signals, coefs)
     *states, coefs = lax.optimization_barrier((*states, coefs))
-    states = [send_state(state, shards, 1 + i) for i, state in enumerate(states)]
+    states = [along_column(state, pairs, 1 + i) for i, state in enumerate(states)]
     parts = local_parts(*signals, coefs)
-    received, *parts = lax.optimization_barrier((received, *parts, *states))
-    parts, states = parts[:2], parts[2:]
+    kept, given = pair_states(seq_index, coefs, own, states)
+    received, kept, given, *parts = lax.optimization_barrier((received, kept, given, *parts))
+    given = inside_pair(given, pairs)
 
     scale = 1.0 / math.sqrt(length * (CHANNELS // FILTERS))
     lags = filter_lags(received, shards, chans, owned, scale)
     lags = lax.all_to_all(lags, "seq", split_axis=0, concat_axis=0, tiled=True)
     filter_grad = lags.reshape(shards * owned, tok_rows).T
     layer_out, key_grad, value_grad = final_outputs(
-        seq_index, signals, coefs, skip_gain[None, :], parts, states
+        signals, coefs, skip_gain[None, :], parts, kept, given
     )
     return (layer_out, key_grad, value_grad, filter_grad)
 

time: 73.7 us -> 63.5 us (0.86)
  starting transfers between devices: 28.8 us -> 19.1 us
  local copies, waits for them, and re-layouts: 7.34 us -> 6 us
  waiting for transfers between devices: 9.16 us -> 10.2 us
    all_to_all x1, starting transfers between devices: 11.7 us -> 4.17 us  [per_device(): lags = lax.all_to_all(lags, 'seq', split_axis=0, concat_axis=0, tiled=True)]
    ppermute x7 -> x4, starting transfers between devices: 9.79 us -> 7.67 us  [the longest x3 5.65 us: along_column(): return lax.ppermute(state, 'seq', route)]
    unnamed x27 -> x23, local copies, waits for them, and re-layouts: 7.26 us -> 5.92 us
    ppermute x7 -> x4, waiting for transfers between devices: 9.16 us -> 10.2 us  [the longest x3 7.59 us: along_column(): return lax.ppermute(state, 'seq', route)]
    pallas_call x1 -> x2, Pallas kernels: 6.88 us -> 6.81 us  [the longest x1 6.72 us: final_outputs(): pl.pallas_call(final_kernel, in_specs=[whole] * len(args), out_specs=[pl....]
  transfers between devices with their start and end apart: 9 -> 6, of which waited for: 1 -> 3; matrix products, arithmetic and copies ran while one was open for 0% -> 0% of each run, Pallas kernels for 26% -> 30%
where the time goes in v6:
time: 63.5 us; the launch traced here: 63.1 us
  Pallas kernels  26.9 us (42%)
  starting transfers between devices  19.1 us (30%)
  waiting for transfers between devices  10.2 us (16%)
  local copies, waits for them, and re-layouts  6 us (9%)
  between operations  0.83 us (1%)
    pallas_call x1, Pallas kernels, local_parts(): pl.pallas_call(local_kernel, out_shape=[jax.ShapeDtypeStruct((tok_rows *...  8.54 us
    ppermute x3, waiting for transfers between devices, along_column(): return lax.ppermute(state, 'seq', route)  7.59 us
    all_to_all x1, starting transfers between devices, per_device(): lax.all_to_all(send, ('seq', 'chan'), split_axis=0, concat_axis=0, tiled=...  7.3 us
    pallas_call x1, Pallas kernels, final_outputs(): pl.pallas_call(final_kernel, in_specs=[whole] * len(args), out_specs=[pl....  6.72 us
    unnamed x23, local copies, waits for them, and re-layouts  5.92 us
    ppermute x3, starting transfers between devices, along_column(): return lax.ppermute(state, 'seq', route)  5.65 us
    pallas_call x1, Pallas kernels, filter_lags(): pl.pallas_call(functools.partial(lag_kernel, shards, chans, groups, owned...  4.52 us
    all_to_all x1, starting transfers between devices, per_device(): lags = lax.all_to_all(lags, 'seq', split_axis=0, concat_axis=0, tiled=True)  4.17 us
  transfers between devices with their start and end apart: 6, of which 3 were waited for; matrix products, arithmetic and copies ran while one was open for 0% of the time, Pallas kernels for 30%

profile of v6, /device:TPU:0, one launch (start us, length us, event | category | flops | bytes accessed | tf_op | source)
XLA Modules:
  0.0 63.1 jit_solution(16636272061091142642)
XLA Ops:
  0.6 3.1 %pack_signals.1 = bf16[32,64,256]{2,1,0:T(8,128)(2,1)} custom-call(bf16[256,1024]{1,0:T(8,128)(2,1)} %k_ref.2, bf16[256,1024]{1,0:T(8,128)(2,1)} %v_ref.2, bf16[256,1024]{1,0:T(8,128)(2,1)} %o_ref.2, bf16[256,1024]{1,0:T(8,128)(2,1)} %q_ref.2), custom_call_target="tpu_custom_call" | custom-call | tf_op jit(solution)/shard_map/pack_signals/pallas_call | solution.py:102
  3.7 0.0 copy-start.9
  3.7 0.0 copy-start.10
  3.8 0.0 copy-start.1
  3.8 0.0 copy-start.2
  3.8 0.0 copy-start.3
  3.8 7.3 %all-to-all-start = ((bf16[32,64,256]{2,1,0:T(8,128)(2,1)}), bf16[32,64,256]{2,1,0:T(8,128)(2,1)S(1)}, u32[]{:S(2)}, u32[]{:S(2)}) async-start(bf16[32,64,256]{2,1,0:T(8,128)(2,1)} %pack_signals.1), calls=%async_computation | async-start | bytes 2097152 | tf_op jit(solution)/shard_map/all_to_all | solution.py:473
  11.1 0.0 copy-start
  11.1 0.0 copy-done.9
  11.1 0.0 copy-done.10
  11.2 0.1 broadcast_in_dim.11
  11.3 0.0 copy-done.1
  11.3 0.0 copy-done.2
  11.3 0.0 copy-done.3
  11.3 0.8 %copy-done = bf16[256,1024]{1,0:T(8,128)(2,1)S(1)} copy-done((bf16[256,1024]{1,0:T(8,128)(2,1)S(1)}, bf16[256,1024]{1,0:T(8,128)(2,1)}, u32[]{:S(2)}) %copy-start) | copy-done | bytes 524312
  12.2 3.9 %block_states.1 = (bf16[128,128]{1,0:T(8,128)(2,1)S(1)}, bf16[128,128]{1,0:T(8,128)(2,1)S(1)}, bf16[128,128]{1,0:T(8,128)(2,1)S(1)}, f32[2,128,128]{2,1,0:T(8,128)S(1)}) custom-call(s32[1]{0:T(128)} %bitcast.seq_ref, bf16[256,1024]{1,0:T(8,128)(2,1)S(1)} %copy-done, bf16[256,1024]{1,0:T(8,128)(2,1)S(1)} %copy-done.1, bf16[256,1024]{1,0:T(8,128)(2,1)S(1)} %copy-done.2, ...), custom_call_target="tpu_custom_call" | custom-call | flops 16777216 | bytes 2097152 | tf_op jit(solution)/shard_map/block_states/pallas_call | solution.py:192
  16.0 1.8 %collective-permute-start = (bf16[128,128]{1,0:T(8,128)(2,1)S(1)}, bf16[128,128]{1,0:T(8,128)(2,1)S(1)}, u32[]{:S(2)}, u32[]{:S(2)}) collective-permute-start(bf16[128,128]{1,0:T(8,128)(2,1)S(1)} %get-tuple-element.43), channel_id=1, source_target_pairs={{0,8},{4,12},{8,16},{12,20},{16,24},{20,28},{24,0},{28,4},{1,9},{5... | collective-permute-start | bytes 98312 | tf_op jit(solution)/shard_map/ppermute | solution.py:275
  17.9 2.4 %collective-permute-start.1 = (bf16[128,128]{1,0:T(8,128)(2,1)S(1)}, bf16[128,128]{1,0:T(8,128)(2,1)S(1)}, u32[]{:S(2)}, u32[]{:S(2)}) collective-permute-start(bf16[128,128]{1,0:T(8,128)(2,1)S(1)} %get-tuple-element.44), channel_id=1, source_target_pairs={{0,16},{4,20},{8,24},{12,28},{16,0},{20,4},{24,8},{28,12},{1,17},{... | collective-permute-start | bytes 98312 | tf_op jit(solution)/shard_map/ppermute | solution.py:275
  20.3 1.4 %collective-permute-start.2 = (bf16[128,128]{1,0:T(8,128)(2,1)S(1)}, bf16[128,128]{1,0:T(8,128)(2,1)S(1)}, u32[]{:S(2)}, u32[]{:S(2)}) collective-permute-start(bf16[128,128]{1,0:T(8,128)(2,1)S(1)} %get-tuple-element.45), channel_id=1, source_target_pairs={{0,24},{4,28},{8,0},{12,4},{16,8},{20,12},{24,16},{28,20},{1,25},{... | collective-permute-start | bytes 98312 | tf_op jit(solution)/shard_map/ppermute | solution.py:275
  21.7 8.5 %local_parts.1 = (f32[2048,128]{1,0:T(8,128)S(1)}, f32[2048,128]{1,0:T(8,128)S(1)}) custom-call(bf16[256,1024]{1,0:T(8,128)(2,1)S(1)} %copy-done, bf16[256,1024]{1,0:T(8,128)(2,1)S(1)} %copy-done.1, bf16[256,1024]{1,0:T(8,128)(2,1)S(1)} %copy-done.2, bf16[256,1024]{1,0:T(8,128)(2,1)S(1)} %copy-done.3, f32[3,16,8,128]{3,2,1,0:T(8,128)S(1)} %bitcast.15), custom_call_target="tpu_custom_call" | custom-call | flops 33554432 | bytes 2097152 | tf_op jit(solution)/shard_map/local_parts/pallas_call | solution.py:262
  30.2 0.0 copy-start.4
  30.3 1.0 %copy-done.4 = f32[2048,128]{1,0:T(8,128)} copy-done((f32[2048,128]{1,0:T(8,128)}, f32[2048,128]{1,0:T(8,128)S(1)}, u32[]{:S(2)}) %copy-start.4) | copy-done | bytes 1048600
  31.2 0.0 copy-start.6
  31.2 1.0 %copy-done.6 = f32[2048,128]{1,0:T(8,128)} copy-done((f32[2048,128]{1,0:T(8,128)}, f32[2048,128]{1,0:T(8,128)S(1)}, u32[]{:S(2)}) %copy-start.6) | copy-done | bytes 1048600
  32.2 1.6 %collective-permute-done.refs_0_ = bf16[128,128]{1,0:T(8,128)(2,1)S(1)} collective-permute-done((bf16[128,128]{1,0:T(8,128)(2,1)S(1)}, bf16[128,128]{1,0:T(8,128)(2,1)S(1)}, u32[]{:S(2)}, u32[]{:S(2)}) %collective-permute-start) | collective-permute-done | bytes 32800 | tf_op jit(solution)/shard_map/ppermute | solution.py:275
  33.8 6.0 %collective-permute-done.1.refs_1_ = bf16[128,128]{1,0:T(8,128)(2,1)S(1)} collective-permute-done((bf16[128,128]{1,0:T(8,128)(2,1)S(1)}, bf16[128,128]{1,0:T(8,128)(2,1)S(1)}, u32[]{:S(2)}, u32[]{:S(2)}) %collective-permute-start.1) | collective-permute-done | bytes 32800 | tf_op jit(solution)/shard_map/ppermute | solution.py:275
  39.8 0.0 collective-permute-done.2.refs_2_
  39.8 0.1 pair_states.1
  39.9 0.0 all-to-all-done.refs_0_
  39.9 4.5 %filter_lags.1 = f32[8,8,256]{2,1,0:T(8,128)} custom-call(bf16[32,64,256]{2,1,0:T(8,128)(2,1)S(1)} %all-to-all-done.refs_0_), custom_call_target="tpu_custom_call" | custom-call | tf_op jit(solution)/shard_map/filter_lags/pallas_call | solution.py:447
  44.4 0.0 copy-start.8
  44.4 4.2 %all-to-all-start.1 = ((f32[8,8,256]{2,1,0:T(8,128)}), f32[8,8,256]{2,1,0:T(8,128)S(1)}, u32[]{:S(2)}, u32[]{:S(2)}) async-start(f32[8,8,256]{2,1,0:T(8,128)} %filter_lags.1), calls=%async_computation.1 | async-start | bytes 131072 | tf_op jit(solution)/shard_map/all_to_all | solution.py:497
  48.6 2.0 %collective-permute-start.3 = (bf16[2,128,128]{2,1,0:T(8,128)(2,1)S(1)}, bf16[2,128,128]{2,1,0:T(8,128)(2,1)S(1)}, u32[]{:S(2)}, u32[]{:S(2)}) collective-permute-start(bf16[2,128,128]{2,1,0:T(8,128)(2,1)S(1)} %get-tuple-element.53), channel_id=1, source_target_pairs={{0,4},{4,0},{8,12},{12,8},{16,20},{20,16},{24,28},{28,24},{1,5},{5... | collective-permute-start | bytes 196616 | tf_op jit(solution)/shard_map/ppermute | solution.py:279
  50.6 2.6 %collective-permute-done.3.given_ref = bf16[2,128,128]{2,1,0:T(8,128)(2,1)S(1)} collective-permute-done((bf16[2,128,128]{2,1,0:T(8,128)(2,1)S(1)}, bf16[2,128,128]{2,1,0:T(8,128)(2,1)S(1)}, u32[]{:S(2)}, u32[]{:S(2)}) %collective-permute-start.3) | collective-permute-done | bytes 65568 | tf_op jit(solution)/shard_map/ppermute | solution.py:279
  53.2 0.0 copy-done.8
  53.3 0.0 copy-start.5
  53.3 1.2 %copy-done.5 = f32[2048,128]{1,0:T(8,128)S(1)} copy-done((f32[2048,128]{1,0:T(8,128)S(1)}, f32[2048,128]{1,0:T(8,128)}, u32[]{:S(2)}) %copy-start.5) | copy-done | bytes 1048600
  54.5 0.0 copy-start.7
  54.5 1.2 %copy-done.7 = f32[2048,128]{1,0:T(8,128)S(1)} copy-done((f32[2048,128]{1,0:T(8,128)S(1)}, f32[2048,128]{1,0:T(8,128)}, u32[]{:S(2)}) %copy-start.7) | copy-done | bytes 1048600
  55.7 6.7 %final_outputs.1 = (bf16[256,1024]{1,0:T(8,128)(2,1)}, bf16[256,1024]{1,0:T(8,128)(2,1)}, bf16[256,1024]{1,0:T(8,128)(2,1)}) custom-call(bf16[256,1024]{1,0:T(8,128)(2,1)S(1)} %copy-done, bf16[256,1024]{1,0:T(8,128)(2,1)S(1)} %copy-done.1, bf16[256,1024]{1,0:T(8,128)(2,1)S(1)} %copy-done.2, bf16[256,1024]{1,0:T(8,128)(2,1)S(1)} %copy-done.3, ...), custom_call_target="tpu_custom_call" | custom-call | flops 33554432 | bytes 3670016 | tf_op jit(solution)/shard_map/final_outputs/pallas_call | solution.py:343
  62.4 0.0 all-to-all-done.1
  62.4 0.6 %copy.12 = f32[256,64]{0,1:T(8,128)} copy(f32[256,64]{0,1:T(8,128)S(1)} %bitcast.19) | data formatting | bytes 131072
  (3 shorter events, 0.1 us)
Async XLA Ops:
  3.7 7.4 %copy-start.9 = (f32[256,16]{0,1:T(8,128)S(1)}, f32[256,16]{0,1:T(8,128)}, u32[]{:S(2)}) copy-start(f32[256,16]{0,1:T(8,128)} %param.12) | copy-start | bytes 49156
  3.7 7.4 %copy-start.10 = (f32[256,16]{0,1:T(8,128)S(1)}, f32[256,16]{0,1:T(8,128)}, u32[]{:S(2)}) copy-start(f32[256,16]{0,1:T(8,128)} %param.11) | copy-start | bytes 49156
  3.8 7.5 %copy-start.1 = (bf16[256,1024]{1,0:T(8,128)(2,1)S(1)}, bf16[256,1024]{1,0:T(8,128)(2,1)}, u32[]{:S(2)}) copy-start(bf16[256,1024]{1,0:T(8,128)(2,1)} %k_ref.2) | copy-start | bytes 1572868
  3.8 7.5 %copy-start.2 = (bf16[256,1024]{1,0:T(8,128)(2,1)S(1)}, bf16[256,1024]{1,0:T(8,128)(2,1)}, u32[]{:S(2)}) copy-start(bf16[256,1024]{1,0:T(8,128)(2,1)} %v_ref.2) | copy-start | bytes 1572868
  3.8 7.5 %copy-start.3 = (bf16[256,1024]{1,0:T(8,128)(2,1)S(1)}, bf16[256,1024]{1,0:T(8,128)(2,1)}, u32[]{:S(2)}) copy-start(bf16[256,1024]{1,0:T(8,128)(2,1)} %o_ref.2) | copy-start | bytes 1572868
  3.8 36.1 %all-to-all-start = ((bf16[32,64,256]{2,1,0:T(8,128)(2,1)}), bf16[32,64,256]{2,1,0:T(8,128)(2,1)S(1)}, u32[]{:S(2)}, u32[]{:S(2)}) async-start(bf16[32,64,256]{2,1,0:T(8,128)(2,1)} %pack_signals.1), calls=%async_computation | async-start | bytes 2097152 | tf_op jit(solution)/shard_map/all_to_all | solution.py:473
  11.1 1.0 %copy-start = (bf16[256,1024]{1,0:T(8,128)(2,1)S(1)}, bf16[256,1024]{1,0:T(8,128)(2,1)}, u32[]{:S(2)}) copy-start(bf16[256,1024]{1,0:T(8,128)(2,1)} %q_ref.2) | copy-start | bytes 1572868
  16.0 17.8 %collective-permute-start = (bf16[128,128]{1,0:T(8,128)(2,1)S(1)}, bf16[128,128]{1,0:T(8,128)(2,1)S(1)}, u32[]{:S(2)}, u32[]{:S(2)}) collective-permute-start(bf16[128,128]{1,0:T(8,128)(2,1)S(1)} %get-tuple-element.43), channel_id=1, source_target_pairs={{0,8},{4,12},{8,16},{12,20},{16,24},{20,28},{24,0},{28,4},{1,9},{5... | collective-permute-start | bytes 98312 | tf_op jit(solution)/shard_map/ppermute | solution.py:275
  17.9 21.9 %collective-permute-start.1 = (bf16[128,128]{1,0:T(8,128)(2,1)S(1)}, bf16[128,128]{1,0:T(8,128)(2,1)S(1)}, u32[]{:S(2)}, u32[]{:S(2)}) collective-permute-start(bf16[128,128]{1,0:T(8,128)(2,1)S(1)} %get-tuple-element.44), channel_id=1, source_target_pairs={{0,16},{4,20},{8,24},{12,28},{16,0},{20,4},{24,8},{28,12},{1,17},{... | collective-permute-start | bytes 98312 | tf_op jit(solution)/shard_map/ppermute | solution.py:275
  20.3 19.5 %collective-permute-start.2 = (bf16[128,128]{1,0:T(8,128)(2,1)S(1)}, bf16[128,128]{1,0:T(8,128)(2,1)S(1)}, u32[]{:S(2)}, u32[]{:S(2)}) collective-permute-start(bf16[128,128]{1,0:T(8,128)(2,1)S(1)} %get-tuple-element.45), channel_id=1, source_target_pairs={{0,24},{4,28},{8,0},{12,4},{16,8},{20,12},{24,16},{28,20},{1,25},{... | collective-permute-start | bytes 98312 | tf_op jit(solution)/shard_map/ppermute | solution.py:275
  30.2 1.0 %copy-start.4 = (f32[2048,128]{1,0:T(8,128)}, f32[2048,128]{1,0:T(8,128)S(1)}, u32[]{:S(2)}) copy-start(f32[2048,128]{1,0:T(8,128)S(1)} %get-tuple-element.50.x_ref) | copy-start | bytes 3145732
  31.2 1.0 %copy-start.6 = (f32[2048,128]{1,0:T(8,128)}, f32[2048,128]{1,0:T(8,128)S(1)}, u32[]{:S(2)}) copy-start(f32[2048,128]{1,0:T(8,128)S(1)} %get-tuple-element.51.g_ref) | copy-start | bytes 3145732
  44.4 8.8 %copy-start.8 = (f32[1024]{0:T(1024)S(1)}, f32[1024]{0:T(1024)}, u32[]{:S(2)}) copy-start(f32[1024]{0:T(1024)} %param.13) | copy-start | bytes 12292
  44.4 18.0 %all-to-all-start.1 = ((f32[8,8,256]{2,1,0:T(8,128)}), f32[8,8,256]{2,1,0:T(8,128)S(1)}, u32[]{:S(2)}, u32[]{:S(2)}) async-start(f32[8,8,256]{2,1,0:T(8,128)} %filter_lags.1), calls=%async_computation.1 | async-start | bytes 131072 | tf_op jit(solution)/shard_map/all_to_all | solution.py:497
  48.6 4.6 %collective-permute-start.3 = (bf16[2,128,128]{2,1,0:T(8,128)(2,1)S(1)}, bf16[2,128,128]{2,1,0:T(8,128)(2,1)S(1)}, u32[]{:S(2)}, u32[]{:S(2)}) collective-permute-start(bf16[2,128,128]{2,1,0:T(8,128)(2,1)S(1)} %get-tuple-element.53), channel_id=1, source_target_pairs={{0,4},{4,0},{8,12},{12,8},{16,20},{20,16},{24,28},{28,24},{1,5},{5... | collective-permute-start | bytes 196616 | tf_op jit(solution)/shard_map/ppermute | solution.py:279
  53.3 1.2 %copy-start.5 = (f32[2048,128]{1,0:T(8,128)S(1)}, f32[2048,128]{1,0:T(8,128)}, u32[]{:S(2)}) copy-start(f32[2048,128]{1,0:T(8,128)} %copy-done.4) | copy-start | bytes 3145732
  54.5 1.2 %copy-start.7 = (f32[2048,128]{1,0:T(8,128)S(1)}, f32[2048,128]{1,0:T(8,128)}, u32[]{:S(2)}) copy-start(f32[2048,128]{1,0:T(8,128)} %copy-done.6) | copy-start | bytes 3145732

commit v7 on v6

--- a/solution.py
+++ b/solution.py
@@ -12,6 +12,7 @@
 FILTERS = 256
 LANES = 128
 SUBLANES = 8
+GAP = 8
 VMEM_BYTES = 16 * 1024 * 1024
 PACK_VMEM_BYTES = 62 * 1024 * 1024
 F32 = jnp.float32
@@ -34,29 +35,26 @@
     tok_rows, width = held.shape[1:]
     groups = width // FILTERS
     per_chan = FILTERS // chans
-    parts = tok_rows // LANES
-    rows = groups * owned
-
-    def arrival(i, part):
-        place = pl.ds(part * LANES, LANES)
+    units = [(which, first) for which in range(2) for first in range(0, groups, 2)]
+
+    def arrival(i, first):
+        place = (slice(None), pl.ds(first * FILTERS, 2 * FILTERS))
         return pltpu.make_async_copy(
-            hbm_refs[i].at[place, :], held.at[i, place, :], in_sems.at[i, part]
+            hbm_refs[i].at[place], held.at[(i, *place)], in_sems.at[i, first // 2]
         )
 
-    def departure(which, part):
-        lanes = pl.ds(part * LANES, LANES)
+    def departure(which, first):
         if owned % SUBLANES:
-            place = (which, slice(None), slice(None), lanes)
+            place = (which, pl.ds(first, 2))
         else:
-            place = (slice(None), pl.ds(which * rows, rows), lanes)
+            place = (slice(None), pl.ds((which * groups + first) * owned, 2 * owned))
         return pltpu.make_async_copy(
-            packed.at[place], send_ref.at[place], out_sems.at[which, part]
+            packed.at[place], send_ref.at[place], out_sems.at[which, first // 2]
         )
 
-    units = [(which, part) for which in range(2) for part in range(parts)]
-    for which, part in units:
+    for which, first in units:
         for i in (2 * which, 2 * which + 1):
-            arrival(i, part).start()
+            arrival(i, first).start()
 
     def owned_filter(row):
         seq = row // (chans * owned)
@@ -64,37 +62,34 @@
         return chan * per_chan + seq * owned + row % owned
 
     order = one_hot(FILTERS, FILTERS, owned_filter)
-    for which, part in units:
+    for which, first in units:
         for i in (2 * which, 2 * which + 1):
-            arrival(i, part).wait()
-        place = slice(part * LANES, (part + 1) * LANES)
-        signal = product(held[2 * which, place, :], held[2 * which + 1, place, :])
+            arrival(i, first).wait()
         pieces = []
-        for group in range(groups):
+        for group in (first, first + 1):
+            cols = slice(group * FILTERS, (group + 1) * FILTERS)
             piece = lax.dot_general(
                 order,
-                signal[:, group * FILTERS : (group + 1) * FILTERS],
+                product(held[2 * which, :, cols], held[2 * which + 1, :, cols]),
                 (((1,), (1,)), ((), ())),
                 preferred_element_type=F32,
             )
             if owned % SUBLANES:
-                packed[which, group, :, place] = piece.astype(BF16)
+                packed[which, group] = piece.astype(BF16)
             else:
-                pieces.append(piece.reshape(shards * chans, owned, LANES))
+                pieces.append(piece.reshape(shards * chans, owned, tok_rows))
         if pieces:
-            packed[:, which * rows : (which + 1) * rows, place] = jnp.concatenate(
-                pieces, axis=1
-            ).astype(BF16)
-        departure(which, part).start()
-    for which, part in units:
-        departure(which, part).wait()
+            row = (which * groups + first) * owned
+            packed[:, row : row + 2 * owned, :] = jnp.concatenate(pieces, axis=1).astype(BF16)
+        departure(which, first).start()
+    for which, first in units:
+        departure(which, first).wait()
 
 
 def pack_signals(shards, chans, owned, query_proj, key_proj, value_proj, out_grad):
     tok_rows, width = key_proj.shape
     groups = width // FILTERS
     dests = shards * chans
-    parts = tok_rows // LANES
     if owned % SUBLANES:
         shape = (2, groups, FILTERS, tok_rows)
     else:
@@ -107,8 +102,8 @@
         scratch_shapes=[
             pltpu.VMEM((4, tok_rows, width), BF16),
             pltpu.VMEM(shape, BF16),
-            pltpu.SemaphoreType.DMA((4, parts)),
-            pltpu.SemaphoreType.DMA((2, parts)),
+            pltpu.SemaphoreType.DMA((4, groups // 2)),
+            pltpu.SemaphoreType.DMA((2, groups // 2)),
         ],
         compiler_params=pltpu.CompilerParams(vmem_limit_bytes=PACK_VMEM_BYTES),
         name="pack_signals",
@@ -119,13 +114,24 @@
     return send
 
 
+def tile_rows(tok_rows, tile):
+    first = tile * (tok_rows + GAP)
+    return slice(first, first + tok_rows)
+
+
+def token_shape(tok_rows, tiles):
+    return (tiles * (tok_rows + GAP), LANES)
+
+
+def token_place(t, tok_rows, tiles):
+    return (pl.ds(t, tiles, stride=tok_rows + GAP), slice(None))
+
+
 def spread_tokens(a_ref, b_ref, x_ref):
     tok_rows, width = a_ref.shape
     for tile in range(width // LANES):
         cols = slice(tile * LANES, (tile + 1) * LANES)
-        x_ref[tile * tok_rows : (tile + 1) * tok_rows, :] = product(
-            a_ref[:, cols], b_ref[:, cols]
-        ).astype(F32)
+        x_ref[tile_rows(tok_rows, tile), :] = product(a_ref[:, cols], b_ref[:, cols]).astype(F32)
 
 
 def walk_tokens(ref, coef_ref, tok_rows, tiles, start, move):
@@ -134,10 +140,10 @@
     weight = [coef_ref[2, m] for m in range(modes)]
 
     def step(t, held):
-        rows = pl.ds(start + move * t, tiles, stride=tok_rows)
-        x = ref[rows, :]
+        place = token_place(start + move * t, tok_rows, tiles)
+        x = ref[place]
         held = tuple(decay[m] * held[m] + x for m in range(modes))
-        ref[rows, :] = tree_sum([weight[m] * held[m] for m in range(modes)])
+        ref[place] = tree_sum([weight[m] * held[m] for m in range(modes)])
         return held
 
     zero = tuple(jnp.zeros((tiles, LANES), F32) for _ in range(modes))
@@ -161,8 +167,8 @@
     decay = [coef_ref[0, m] for m in range(modes)]
 
     def step(t, carry):
-        x = x_ref[pl.ds(t, tiles, stride=tok_rows), :]
-        g = g_ref[pl.ds(tok_rows - 1 - t, tiles, stride=tok_rows), :]
+        x = x_ref[token_place(t, tok_rows, tiles)]
+        g = g_ref[token_place(tok_rows - 1 - t, tok_rows, tiles)]
         ahead = tuple(decay[m] * carry[0][m] + x for m in range(modes))
         behind = tuple(decay[m] * carry[1][m] + g for m in range(modes))
         return (ahead, behind)
@@ -195,7 +201,7 @@
         out_specs=[whole] * pairs,
         out_shape=[jax.ShapeDtypeStruct((modes * tiles, LANES), LINK)] * (pairs - 1)
         + [jax.ShapeDtypeStruct((2, modes * tiles, LANES), F32)],
-        scratch_shapes=[pltpu.VMEM((tok_rows * tiles, LANES), F32)] * 2,
+        scratch_shapes=[pltpu.VMEM(token_shape(tok_rows, tiles), F32)] * 2,
         compiler_params=pltpu.CompilerParams(vmem_limit_bytes=VMEM_BYTES),
         cost_estimate=pl.CostEstimate(
             flops=4 * modes * tok_rows * width, bytes_accessed=8 * tok_rows * width, transcendentals=0
@@ -261,7 +267,7 @@
     modes, tiles = coefs.shape[1:3]
     return pl.pallas_call(
         local_kernel,
-        out_shape=[jax.ShapeDtypeStruct((tok_rows * tiles, LANES), F32)] * 2,
+        out_shape=[jax.ShapeDtypeStruct(token_shape(tok_rows, tiles), F32)] * 2,
         compiler_params=pltpu.CompilerParams(vmem_limit_bytes=VMEM_BYTES),
         cost_estimate=pl.CostEstimate(
             flops=8 * modes * tok_rows * width, bytes_accessed=8 * tok_rows * width, transcendentals=0
@@ -279,14 +285,13 @@
     return lax.ppermute(state, "seq", [(i, i ^ 1) for i in range(2 * pairs)])
 
 
-def add_edge(ref, held, coef_ref, tok_rows, tiles, start, move):
+def fill_edge(ref, held, coef_ref, tok_rows, tiles, start, move):
     modes = coef_ref.shape[1]
     decay = [coef_ref[0, m] for m in range(modes)]
 
     def step(t, held):
-        rows = pl.ds(start + move * t, tiles, stride=tok_rows)
         held = tuple(decay[m] * held[m] for m in range(modes))
-        ref[rows, :] = ref[rows, :] + tree_sum(list(held))
+        ref[token_place(start + move * t, tok_rows, tiles)] = tree_sum(list(held))
         return held
 
     held = tuple(coef_ref[2, m] * held[m] for m in range(modes))
@@ -294,38 +299,51 @@
 
 
 def final_kernel(
-    q_ref, k_ref, v_ref, o_ref, coef_ref, gain_ref, x_ref, g_ref, kept_ref, given_ref, *refs
+    q_ref, k_ref, v_ref, o_ref, coef_ref, gain_ref, kept_ref, given_ref, *refs
 ):
-    hbm_refs, held_refs, sems = refs[:3], refs[3:6], refs[6]
-    layer_ref, key_ref, value_ref = held_refs
+    part_refs, hbm_refs, refs = refs[:2], refs[2:5], refs[5:]
+    x_ref, g_ref, edge_ref, layer_ref, key_ref, value_ref, in_sems, out_sems = refs
     tok_rows, width = k_ref.shape
     tiles = width // LANES
     modes = coef_ref.shape[1]
 
+    def arrival(i, tile):
+        rows = pl.ds(tile * (tok_rows + GAP), tok_rows)
+        return pltpu.make_async_copy(
+            part_refs[i].at[rows, :], (x_ref, g_ref)[i].at[rows, :], in_sems.at[i, tile]
+        )
+
+    def departure(i, tile):
+        place = (slice(None), pl.ds(tile * LANES, LANES))
+        return pltpu.make_async_copy(
+            (layer_ref, key_ref, value_ref)[i].at[place], hbm_refs[i].at[place], out_sems.at[i, tile]
+        )
+
     def edge(side):
         total = kept_ref[side] + given_ref[side].astype(F32)
         return [total[m * tiles : (m + 1) * tiles] for m in range(modes)]
 
-    def departure(i, tile):
-        place = (slice(None), pl.ds(tile * LANES, LANES))
-        return pltpu.make_async_copy(
-            held_refs[i].at[place], hbm_refs[i].at[place], sems.at[i, tile]
-        )
-
-    add_edge(x_ref, edge(0), coef_ref, tok_rows, tiles, 0, 1)
+    for i in range(2):
+        for tile in range(tiles):
+            arrival(i, tile).start()
+    fill_edge(edge_ref, edge(0), coef_ref, tok_rows, tiles, 0, 1)
+    for tile in range(tiles):
+        arrival(0, tile).wait()
     for tile in range(tiles):
         cols = slice(tile * LANES, (tile + 1) * LANES)
-        rows = slice(tile * tok_rows, (tile + 1) * tok_rows)
+        rows = tile_rows(tok_rows, tile)
         conv_in = product(k_ref[:, cols], v_ref[:, cols]).astype(F32)
-        long_conv = x_ref[rows, :] + gain_ref[:, cols] * conv_in
+        long_conv = x_ref[rows, :] + edge_ref[rows, :] + gain_ref[:, cols] * conv_in
         layer_ref[:, cols] = (q_ref[:, cols].astype(F32) * long_conv).astype(BF16)
         departure(0, tile).start()
-    add_edge(g_ref, edge(1), coef_ref, tok_rows, tiles, tok_rows - 1, -1)
+    fill_edge(edge_ref, edge(1), coef_ref, tok_rows, tiles, tok_rows - 1, -1)
+    for tile in range(tiles):
+        arrival(1, tile).wait()
     for tile in range(tiles):
         cols = slice(tile * LANES, (tile + 1) * LANES)
-        rows = slice(tile * tok_rows, (tile + 1) * tok_rows)
+        rows = tile_rows(tok_rows, tile)
         mid_grad = product(o_ref[:, cols], q_ref[:, cols]).astype(F32)
-        conv_grad = g_ref[rows, :] + gain_ref[:, cols] * mid_grad
+        conv_grad = g_ref[rows, :] + edge_ref[rows, :] + gain_ref[:, cols] * mid_grad
         key_ref[:, cols] = (conv_grad * v_ref[:, cols].astype(F32)).astype(BF16)
         departure(1, tile).start()
         value_ref[:, cols] = (conv_grad * k_ref[:, cols].astype(F32)).astype(BF16)
@@ -335,24 +353,26 @@
             departure(i, tile).wait()
 
 
-def final_outputs(signals, coefs, gain, parts, kept, given):
+def final_outputs(signals, coefs, gain, kept, given, parts):
     tok_rows, width = signals[0].shape
     modes, tiles = coefs.shape[1:3]
-    args = (*signals, coefs, gain, *parts, kept, given)
+    args = (*signals, coefs, gain, kept, given)
     whole = pl.BlockSpec(memory_space=pltpu.VMEM)
+    away = pl.BlockSpec(memory_space=pl.ANY)
     return pl.pallas_call(
         final_kernel,
-        in_specs=[whole] * len(args),
-        out_specs=[pl.BlockSpec(memory_space=pl.ANY)] * 3,
+        in_specs=[whole] * len(args) + [away] * len(parts),
+        out_specs=[away] * 3,
         out_shape=[jax.ShapeDtypeStruct((tok_rows, width), BF16)] * 3,
-        scratch_shapes=[pltpu.VMEM((tok_rows, width), BF16)] * 3
-        + [pltpu.SemaphoreType.DMA((3, tiles))],
+        scratch_shapes=[pltpu.VMEM(token_shape(tok_rows, tiles), F32)] * 3
+        + [pltpu.VMEM((tok_rows, width), BF16)] * 3
+        + [pltpu.SemaphoreType.DMA((2, tiles)), pltpu.SemaphoreType.DMA((3, tiles))],
         compiler_params=pltpu.CompilerParams(vmem_limit_bytes=VMEM_BYTES),
         cost_estimate=pl.CostEstimate(
             flops=8 * modes * tok_rows * width, bytes_accessed=14 * tok_rows * width, transcendentals=0
         ),
         name="final_outputs",
-    )(*args)
+    )(*args, *parts)
 
 
 def lag_kernel(shards, chans, groups, owned, scale, *refs):
@@ -453,6 +473,9 @@
             pltpu.VMEM((owned, LANES, full), BF16),
         ],
         compiler_params=pltpu.CompilerParams(vmem_limit_bytes=VMEM_BYTES),
+        cost_estimate=pl.CostEstimate(
+            flops=4 * owned * LANES * full * full, bytes_accessed=8 * owned * full * LANES, transcendentals=0
+        ),
         name="filter_lags",
     )(*args)
 
@@ -494,10 +517,11 @@
 
     scale = 1.0 / math.sqrt(length * (CHANNELS // FILTERS))
     lags = filter_lags(received, shards, chans, owned, scale)
+    lags, given = lax.optimization_barrier((lags, given))
     lags = lax.all_to_all(lags, "seq", split_axis=0, concat_axis=0, tiled=True)
     filter_grad = lags.reshape(shards * owned, tok_rows).T
     layer_out, key_grad, value_grad = final_outputs(
-        signals, coefs, skip_gain[None, :], parts, kept, given
+        signals, coefs, skip_gain[None, :], kept, given, parts
     )
     return (layer_out, key_grad, value_grad, filter_grad)
 

time: 63.5 us -> 60.4 us (0.951)
  Pallas kernels: 26.9 us -> 23.6 us
  waiting for transfers between devices: 10.2 us -> 12 us
  starting transfers between devices: 19.1 us -> 17.8 us
    ppermute x3, waiting for transfers between devices: 7.59 us -> 12 us  [along_column(): return lax.ppermute(state, 'seq', route)]
    ppermute x1, waiting for transfers between devices: 2.62 us -> 0.01 us  [inside_pair(): return lax.ppermute(state, 'seq', [(i, i ^ 1) for i in range(2 * pairs)])]
    pallas_call x2, Pallas kernels: 15.3 us -> 13 us  [the longest x1 7.17 us: final_outputs(): pl.pallas_call(final_kernel, in_specs=[whole] * len(args) + [away] * len(...]
    pallas_call x1, Pallas kernels: 3.89 us -> 3.02 us  [block_states(): pl.pallas_call(state_kernel, in_specs=[pl.BlockSpec(memory_space=pltpu.SM...]
    all_to_all x1, starting transfers between devices: 4.17 us -> 3.35 us  [per_device(): lags = lax.all_to_all(lags, 'seq', split_axis=0, concat_axis=0, tiled=True)]
    unnamed x23 -> x25, local copies, waits for them, and re-layouts: 5.92 us -> 5.76 us
  transfers between devices with their start and end apart: 6 -> 6, of which waited for: 3 -> 2; matrix products, arithmetic and copies ran while one was open for 0% -> 0% of each run, Pallas kernels for 30% -> 34%
where the time goes in v7:
time: 60.4 us; the launch traced here: 60.1 us
  Pallas kernels  23.6 us (39%)
  starting transfers between devices  17.8 us (29%)
  waiting for transfers between devices  12 us (20%)
  local copies, waits for them, and re-layouts  5.84 us (10%)
  between operations  0.86 us (1%)
    ppermute x3, waiting for transfers between devices, along_column(): return lax.ppermute(state, 'seq', route)  12 us
    all_to_all x1, starting transfers between devices, per_device(): lax.all_to_all(send, ('seq', 'chan'), split_axis=0, concat_axis=0, tiled=...  7.3 us
    pallas_call x1, Pallas kernels, final_outputs(): pl.pallas_call(final_kernel, in_specs=[whole] * len(args) + [away] * len(...  7.17 us
    pallas_call x1, Pallas kernels, local_parts(): pl.pallas_call(local_kernel, out_shape=[jax.ShapeDtypeStruct(token_shape(...  5.79 us
    unnamed x25, local copies, waits for them, and re-layouts  5.76 us
    ppermute x3, starting transfers between devices, along_column(): return lax.ppermute(state, 'seq', route)  5.65 us
    pallas_call x1, Pallas kernels, filter_lags(): pl.pallas_call(functools.partial(lag_kernel, shards, chans, groups, owned...  4.52 us
    all_to_all x1, starting transfers between devices, per_device(): lags = lax.all_to_all(lags, 'seq', split_axis=0, concat_axis=0, tiled=True)  3.35 us
  transfers between devices with their start and end apart: 6, of which 2 were waited for; matrix products, arithmetic and copies ran while one was open for 0% of the time, Pallas kernels for 34%

profile of v7, /device:TPU:0, one launch (start us, length us, event | category | flops | bytes accessed | tf_op | source)
XLA Modules:
  0.0 60.1 jit_solution(5692851701500659168)
XLA Ops:
  0.6 0.0 copy-start.10
  0.6 0.0 copy-start.11
  0.7 3.0 %pack_signals.1 = bf16[32,64,256]{2,1,0:T(8,128)(2,1)} custom-call(bf16[256,1024]{1,0:T(8,128)(2,1)} %k_ref.2, bf16[256,1024]{1,0:T(8,128)(2,1)} %v_ref.2, bf16[256,1024]{1,0:T(8,128)(2,1)} %o_ref.2, bf16[256,1024]{1,0:T(8,128)(2,1)} %q_ref.2), custom_call_target="tpu_custom_call" | custom-call | tf_op jit(solution)/shard_map/pack_signals/pallas_call | solution.py:97
  3.6 0.0 copy-start
  3.6 0.0 copy-start.1
  3.6 0.0 copy-start.2
  3.6 0.0 copy-start.3
  3.7 7.3 %all-to-all-start = ((bf16[32,64,256]{2,1,0:T(8,128)(2,1)}), bf16[32,64,256]{2,1,0:T(8,128)(2,1)S(1)}, u32[]{:S(2)}, u32[]{:S(2)}) async-start(bf16[32,64,256]{2,1,0:T(8,128)(2,1)} %pack_signals.1), calls=%async_computation | async-start | bytes 2097152 | tf_op jit(solution)/shard_map/all_to_all | solution.py:496
  11.0 0.0 copy-done.10
  11.0 0.0 copy-done.11
  11.1 0.1 broadcast_in_dim.11
  11.1 0.0 copy-done
  11.1 0.0 copy-done.1
  11.2 0.0 copy-done.2
  11.2 0.0 copy-done.3
  11.2 3.0 %block_states.1 = (bf16[128,128]{1,0:T(8,128)(2,1)S(1)}, bf16[128,128]{1,0:T(8,128)(2,1)S(1)}, bf16[128,128]{1,0:T(8,128)(2,1)S(1)}, f32[2,128,128]{2,1,0:T(8,128)S(1)}) custom-call(s32[1]{0:T(128)} %bitcast.seq_ref, bf16[256,1024]{1,0:T(8,128)(2,1)S(1)} %copy-done, bf16[256,1024]{1,0:T(8,128)(2,1)S(1)} %copy-done.1, bf16[256,1024]{1,0:T(8,128)(2,1)S(1)} %copy-done.2, ...), custom_call_target="tpu_custom_call" | custom-call | flops 16777216 | bytes 2097152 | tf_op jit(solution)/shard_map/block_states/pallas_call | solution.py:198
  14.2 1.8 %collective-permute-start = (bf16[128,128]{1,0:T(8,128)(2,1)S(1)}, bf16[128,128]{1,0:T(8,128)(2,1)S(1)}, u32[]{:S(2)}, u32[]{:S(2)}) collective-permute-start(bf16[128,128]{1,0:T(8,128)(2,1)S(1)} %get-tuple-element.45), channel_id=1, source_target_pairs={{0,8},{4,12},{8,16},{12,20},{16,24},{20,28},{24,0},{28,4},{1,9},{5... | collective-permute-start | bytes 98312 | tf_op jit(solution)/shard_map/ppermute | solution.py:281
  16.0 2.4 %collective-permute-start.1 = (bf16[128,128]{1,0:T(8,128)(2,1)S(1)}, bf16[128,128]{1,0:T(8,128)(2,1)S(1)}, u32[]{:S(2)}, u32[]{:S(2)}) collective-permute-start(bf16[128,128]{1,0:T(8,128)(2,1)S(1)} %get-tuple-element.46), channel_id=1, source_target_pairs={{0,16},{4,20},{8,24},{12,28},{16,0},{20,4},{24,8},{28,12},{1,17},{... | collective-permute-start | bytes 98312 | tf_op jit(solution)/shard_map/ppermute | solution.py:281
  18.4 1.4 %collective-permute-start.2 = (bf16[128,128]{1,0:T(8,128)(2,1)S(1)}, bf16[128,128]{1,0:T(8,128)(2,1)S(1)}, u32[]{:S(2)}, u32[]{:S(2)}) collective-permute-start(bf16[128,128]{1,0:T(8,128)(2,1)S(1)} %get-tuple-element.47), channel_id=1, source_target_pairs={{0,24},{4,28},{8,0},{12,4},{16,8},{20,12},{24,16},{28,20},{1,25},{... | collective-permute-start | bytes 98312 | tf_op jit(solution)/shard_map/ppermute | solution.py:281
  19.9 5.8 %local_parts.1 = (f32[2112,128]{1,0:T(8,128)S(1)}, f32[2112,128]{1,0:T(8,128)S(1)}) custom-call(bf16[256,1024]{1,0:T(8,128)(2,1)S(1)} %copy-done, bf16[256,1024]{1,0:T(8,128)(2,1)S(1)} %copy-done.1, bf16[256,1024]{1,0:T(8,128)(2,1)S(1)} %copy-done.2, bf16[256,1024]{1,0:T(8,128)(2,1)S(1)} %copy-done.3, f32[3,16,8,128]{3,2,1,0:T(8,128)S(1)} %bitcast.15), custom_call_target="tpu_custom_call" | custom-call | flops 33554432 | bytes 2097152 | tf_op jit(solution)/shard_map/local_parts/pallas_call | solution.py:268
  25.6 0.0 copy-start.4
  25.7 1.0 %copy-done.4 = f32[2112,128]{1,0:T(8,128)} copy-done((f32[2112,128]{1,0:T(8,128)}, f32[2112,128]{1,0:T(8,128)S(1)}, u32[]{:S(2)}) %copy-start.4) | copy-done | bytes 1081368
  26.7 0.0 copy-start.6
  26.7 1.0 %copy-done.6 = f32[2112,128]{1,0:T(8,128)} copy-done((f32[2112,128]{1,0:T(8,128)}, f32[2112,128]{1,0:T(8,128)S(1)}, u32[]{:S(2)}) %copy-start.6) | copy-done | bytes 1081368
  27.7 0.0 copy-start.8
  27.7 6.1 %collective-permute-done.refs_0_ = bf16[128,128]{1,0:T(8,128)(2,1)S(1)} collective-permute-done((bf16[128,128]{1,0:T(8,128)(2,1)S(1)}, bf16[128,128]{1,0:T(8,128)(2,1)S(1)}, u32[]{:S(2)}, u32[]{:S(2)}) %collective-permute-start) | collective-permute-done | bytes 32800 | tf_op jit(solution)/shard_map/ppermute | solution.py:281
  33.7 6.0 %collective-permute-done.1.refs_1_ = bf16[128,128]{1,0:T(8,128)(2,1)S(1)} collective-permute-done((bf16[128,128]{1,0:T(8,128)(2,1)S(1)}, bf16[128,128]{1,0:T(8,128)(2,1)S(1)}, u32[]{:S(2)}, u32[]{:S(2)}) %collective-permute-start.1) | collective-permute-done | bytes 32800 | tf_op jit(solution)/shard_map/ppermute | solution.py:281
  39.7 0.0 collective-permute-done.2.refs_2_
  39.7 0.1 pair_states.1
  39.8 0.0 copy-start.9
  39.8 0.6 %copy-done.9 = bf16[2,128,128]{2,1,0:T(8,128)(2,1)} copy-done((bf16[2,128,128]{2,1,0:T(8,128)(2,1)}, bf16[2,128,128]{2,1,0:T(8,128)(2,1)S(1)}, u32[]{:S(2)}) %copy-start.9) | copy-done | bytes 65560
  40.4 0.0 all-to-all-done.refs_0_
  40.4 1.5 %collective-permute-start.3 = (bf16[2,128,128]{2,1,0:T(8,128)(2,1)}, bf16[2,128,128]{2,1,0:T(8,128)(2,1)S(1)}, u32[]{:S(2)}, u32[]{:S(2)}) collective-permute-start(bf16[2,128,128]{2,1,0:T(8,128)(2,1)} %copy-done.9), channel_id=1, source_target_pairs={{0,4},{4,0},{8,12},{12,8},{16,20},{20,16},{24,28},{28,24},{1,5},{5... | collective-permute-start | bytes 196616 | tf_op jit(solution)/shard_map/ppermute | solution.py:285
  41.9 4.5 %filter_lags.1 = f32[8,8,256]{2,1,0:T(8,128)} custom-call(bf16[32,64,256]{2,1,0:T(8,128)(2,1)S(1)} %all-to-all-done.refs_0_), custom_call_target="tpu_custom_call" | custom-call | flops 268435456 | bytes 2097152 | tf_op jit(solution)/shard_map/filter_lags/pallas_call | solution.py:467
  46.4 0.0 collective-permute-done.3.given_ref
  46.4 3.4 %all-to-all-start.1 = ((f32[8,8,256]{2,1,0:T(8,128)}), f32[8,8,256]{2,1,0:T(8,128)S(1)}, u32[]{:S(2)}, u32[]{:S(2)}) async-start(f32[8,8,256]{2,1,0:T(8,128)} %filter_lags.1), calls=%async_computation.1 | async-start | bytes 131072 | tf_op jit(solution)/shard_map/all_to_all | solution.py:521
  49.8 0.0 copy-done.8
  49.8 0.0 copy-start.5
  49.8 1.2 %copy-done.5 = f32[2112,128]{1,0:T(8,128)S(1)} copy-done((f32[2112,128]{1,0:T(8,128)S(1)}, f32[2112,128]{1,0:T(8,128)}, u32[]{:S(2)}) %copy-start.5) | copy-done | bytes 1081368
  51.0 0.0 copy-start.7
  51.0 1.2 %copy-done.7 = f32[2112,128]{1,0:T(8,128)S(1)} copy-done((f32[2112,128]{1,0:T(8,128)S(1)}, f32[2112,128]{1,0:T(8,128)}, u32[]{:S(2)}) %copy-start.7) | copy-done | bytes 1081368
  52.3 7.2 %final_outputs.1 = (bf16[256,1024]{1,0:T(8,128)(2,1)}, bf16[256,1024]{1,0:T(8,128)(2,1)}, bf16[256,1024]{1,0:T(8,128)(2,1)}) custom-call(bf16[256,1024]{1,0:T(8,128)(2,1)S(1)} %copy-done, bf16[256,1024]{1,0:T(8,128)(2,1)S(1)} %copy-done.1, bf16[256,1024]{1,0:T(8,128)(2,1)S(1)} %copy-done.2, bf16[256,1024]{1,0:T(8,128)(2,1)S(1)} %copy-done.3, ...), custom_call_target="tpu_custom_call" | custom-call | flops 33554432 | bytes 3670016 | tf_op jit(solution)/shard_map/final_outputs/pallas_call | solution.py:362
  59.4 0.0 all-to-all-done.1
  59.4 0.6 %copy.12 = f32[256,64]{0,1:T(8,128)} copy(f32[256,64]{0,1:T(8,128)S(1)} %bitcast.19) | data formatting | bytes 131072
  (3 shorter events, 0.1 us)
Async XLA Ops:
  0.6 10.3 %copy-start.10 = (f32[256,16]{0,1:T(8,128)S(1)}, f32[256,16]{0,1:T(8,128)}, u32[]{:S(2)}) copy-start(f32[256,16]{0,1:T(8,128)} %param.12) | copy-start | bytes 49156
  0.6 10.3 %copy-start.11 = (f32[256,16]{0,1:T(8,128)S(1)}, f32[256,16]{0,1:T(8,128)}, u32[]{:S(2)}) copy-start(f32[256,16]{0,1:T(8,128)} %param.11) | copy-start | bytes 49156
  3.6 7.5 %copy-start = (bf16[256,1024]{1,0:T(8,128)(2,1)S(1)}, bf16[256,1024]{1,0:T(8,128)(2,1)}, u32[]{:S(2)}) copy-start(bf16[256,1024]{1,0:T(8,128)(2,1)} %q_ref.2) | copy-start | bytes 1572868
  3.6 7.5 %copy-start.1 = (bf16[256,1024]{1,0:T(8,128)(2,1)S(1)}, bf16[256,1024]{1,0:T(8,128)(2,1)}, u32[]{:S(2)}) copy-start(bf16[256,1024]{1,0:T(8,128)(2,1)} %k_ref.2) | copy-start | bytes 1572868
  3.6 7.5 %copy-start.2 = (bf16[256,1024]{1,0:T(8,128)(2,1)S(1)}, bf16[256,1024]{1,0:T(8,128)(2,1)}, u32[]{:S(2)}) copy-start(bf16[256,1024]{1,0:T(8,128)(2,1)} %v_ref.2) | copy-start | bytes 1572868
  3.6 7.5 %copy-start.3 = (bf16[256,1024]{1,0:T(8,128)(2,1)S(1)}, bf16[256,1024]{1,0:T(8,128)(2,1)}, u32[]{:S(2)}) copy-start(bf16[256,1024]{1,0:T(8,128)(2,1)} %o_ref.2) | copy-start | bytes 1572868
  3.7 36.7 %all-to-all-start = ((bf16[32,64,256]{2,1,0:T(8,128)(2,1)}), bf16[32,64,256]{2,1,0:T(8,128)(2,1)S(1)}, u32[]{:S(2)}, u32[]{:S(2)}) async-start(bf16[32,64,256]{2,1,0:T(8,128)(2,1)} %pack_signals.1), calls=%async_computation | async-start | bytes 2097152 | tf_op jit(solution)/shard_map/all_to_all | solution.py:496
  14.2 19.5 %collective-permute-start = (bf16[128,128]{1,0:T(8,128)(2,1)S(1)}, bf16[128,128]{1,0:T(8,128)(2,1)S(1)}, u32[]{:S(2)}, u32[]{:S(2)}) collective-permute-start(bf16[128,128]{1,0:T(8,128)(2,1)S(1)} %get-tuple-element.45), channel_id=1, source_target_pairs={{0,8},{4,12},{8,16},{12,20},{16,24},{20,28},{24,0},{28,4},{1,9},{5... | collective-permute-start | bytes 98312 | tf_op jit(solution)/shard_map/ppermute | solution.py:281
  16.0 23.6 %collective-permute-start.1 = (bf16[128,128]{1,0:T(8,128)(2,1)S(1)}, bf16[128,128]{1,0:T(8,128)(2,1)S(1)}, u32[]{:S(2)}, u32[]{:S(2)}) collective-permute-start(bf16[128,128]{1,0:T(8,128)(2,1)S(1)} %get-tuple-element.46), channel_id=1, source_target_pairs={{0,16},{4,20},{8,24},{12,28},{16,0},{20,4},{24,8},{28,12},{1,17},{... | collective-permute-start | bytes 98312 | tf_op jit(solution)/shard_map/ppermute | solution.py:281
  18.4 21.2 %collective-permute-start.2 = (bf16[128,128]{1,0:T(8,128)(2,1)S(1)}, bf16[128,128]{1,0:T(8,128)(2,1)S(1)}, u32[]{:S(2)}, u32[]{:S(2)}) collective-permute-start(bf16[128,128]{1,0:T(8,128)(2,1)S(1)} %get-tuple-element.47), channel_id=1, source_target_pairs={{0,24},{4,28},{8,0},{12,4},{16,8},{20,12},{24,16},{28,20},{1,25},{... | collective-permute-start | bytes 98312 | tf_op jit(solution)/shard_map/ppermute | solution.py:281
  25.6 1.0 %copy-start.4 = (f32[2112,128]{1,0:T(8,128)}, f32[2112,128]{1,0:T(8,128)S(1)}, u32[]{:S(2)}) copy-start(f32[2112,128]{1,0:T(8,128)S(1)} %get-tuple-element.56.refs_0_) | copy-start | bytes 3244036
  26.7 1.0 %copy-start.6 = (f32[2112,128]{1,0:T(8,128)}, f32[2112,128]{1,0:T(8,128)S(1)}, u32[]{:S(2)}) copy-start(f32[2112,128]{1,0:T(8,128)S(1)} %get-tuple-element.57.refs_1_) | copy-start | bytes 3244036
  27.7 22.1 %copy-start.8 = (f32[1024]{0:T(1024)S(1)}, f32[1024]{0:T(1024)}, u32[]{:S(2)}) copy-start(f32[1024]{0:T(1024)} %param.13) | copy-start | bytes 12292
  39.8 0.6 %copy-start.9 = (bf16[2,128,128]{2,1,0:T(8,128)(2,1)}, bf16[2,128,128]{2,1,0:T(8,128)(2,1)S(1)}, u32[]{:S(2)}) copy-start(bf16[2,128,128]{2,1,0:T(8,128)(2,1)S(1)} %get-tuple-element.54) | copy-start | bytes 196612
  40.4 6.0 %collective-permute-start.3 = (bf16[2,128,128]{2,1,0:T(8,128)(2,1)}, bf16[2,128,128]{2,1,0:T(8,128)(2,1)S(1)}, u32[]{:S(2)}, u32[]{:S(2)}) collective-permute-start(bf16[2,128,128]{2,1,0:T(8,128)(2,1)} %copy-done.9), channel_id=1, source_target_pairs={{0,4},{4,0},{8,12},{12,8},{16,20},{20,16},{24,28},{28,24},{1,5},{5... | collective-permute-start | bytes 196616 | tf_op jit(solution)/shard_map/ppermute | solution.py:285
  46.4 13.0 %all-to-all-start.1 = ((f32[8,8,256]{2,1,0:T(8,128)}), f32[8,8,256]{2,1,0:T(8,128)S(1)}, u32[]{:S(2)}, u32[]{:S(2)}) async-start(f32[8,8,256]{2,1,0:T(8,128)} %filter_lags.1), calls=%async_computation.1 | async-start | bytes 131072 | tf_op jit(solution)/shard_map/all_to_all | solution.py:521
  49.8 1.2 %copy-start.5 = (f32[2112,128]{1,0:T(8,128)S(1)}, f32[2112,128]{1,0:T(8,128)}, u32[]{:S(2)}) copy-start(f32[2112,128]{1,0:T(8,128)} %copy-done.4) | copy-start | bytes 3244036
  51.0 1.2 %copy-start.7 = (f32[2112,128]{1,0:T(8,128)S(1)}, f32[2112,128]{1,0:T(8,128)}, u32[]{:S(2)}) copy-start(f32[2112,128]{1,0:T(8,128)} %copy-done.6) | copy-start | bytes 3244036

commit v8 on v7

--- a/solution.py
+++ b/solution.py
@@ -253,16 +253,24 @@
     )(seq_index, coefs, own, *states)
 
 
-def local_kernel(q_ref, k_ref, v_ref, o_ref, coef_ref, conv_ref, grad_ref):
+def local_kernel(q_ref, k_ref, v_ref, o_ref, coef_ref, gain_ref, conv_ref, grad_ref):
     tok_rows, width = k_ref.shape
     tiles = width // LANES
     spread_tokens(k_ref, v_ref, conv_ref)
     spread_tokens(o_ref, q_ref, grad_ref)
     walk_tokens(conv_ref, coef_ref, tok_rows, tiles, 0, 1)
     walk_tokens(grad_ref, coef_ref, tok_rows, tiles, tok_rows - 1, -1)
-
-
-def local_parts(query_proj, key_proj, value_proj, out_grad, coefs):
+    for tile in range(tiles):
+        cols = slice(tile * LANES, (tile + 1) * LANES)
+        rows = tile_rows(tok_rows, tile)
+        gain = gain_ref[:, cols]
+        conv_in = product(k_ref[:, cols], v_ref[:, cols]).astype(F32)
+        conv_ref[rows, :] = conv_ref[rows, :] + gain * conv_in
+        mid_grad = product(o_ref[:, cols], q_ref[:, cols]).astype(F32)
+        grad_ref[rows, :] = grad_ref[rows, :] + gain * mid_grad
+
+
+def local_parts(query_proj, key_proj, value_proj, out_grad, coefs, gain):
     tok_rows, width = key_proj.shape
     modes, tiles = coefs.shape[1:3]
     return pl.pallas_call(
@@ -273,7 +281,7 @@
             flops=8 * modes * tok_rows * width, bytes_accessed=8 * tok_rows * width, transcendentals=0
         ),
         name="local_parts",
-    )(query_proj, key_proj, value_proj, out_grad, coefs)
+    )(query_proj, key_proj, value_proj, out_grad, coefs, gain)
 
 
 def along_column(state, pairs, k):
@@ -299,51 +307,35 @@
 
 
 def final_kernel(
-    q_ref, k_ref, v_ref, o_ref, coef_ref, gain_ref, kept_ref, given_ref, *refs
+    q_ref, k_ref, v_ref, coef_ref, x_ref, g_ref, kept_ref, given_ref, *refs
 ):
-    part_refs, hbm_refs, refs = refs[:2], refs[2:5], refs[5:]
-    x_ref, g_ref, edge_ref, layer_ref, key_ref, value_ref, in_sems, out_sems = refs
+    hbm_refs, (edge_ref, layer_ref, key_ref, value_ref, sems) = refs[:3], refs[3:]
     tok_rows, width = k_ref.shape
     tiles = width // LANES
     modes = coef_ref.shape[1]
 
-    def arrival(i, tile):
-        rows = pl.ds(tile * (tok_rows + GAP), tok_rows)
-        return pltpu.make_async_copy(
-            part_refs[i].at[rows, :], (x_ref, g_ref)[i].at[rows, :], in_sems.at[i, tile]
-        )
-
     def departure(i, tile):
         place = (slice(None), pl.ds(tile * LANES, LANES))
         return pltpu.make_async_copy(
-            (layer_ref, key_ref, value_ref)[i].at[place], hbm_refs[i].at[place], out_sems.at[i, tile]
+            (layer_ref, key_ref, value_ref)[i].at[place], hbm_refs[i].at[place], sems.at[i, tile]
         )
 
     def edge(side):
         total = kept_ref[side] + given_ref[side].astype(F32)
         return [total[m * tiles : (m + 1) * tiles] for m in range(modes)]
 
-    for i in range(2):
-        for tile in range(tiles):
-            arrival(i, tile).start()
     fill_edge(edge_ref, edge(0), coef_ref, tok_rows, tiles, 0, 1)
-    for tile in range(tiles):
-        arrival(0, tile).wait()
     for tile in range(tiles):
         cols = slice(tile * LANES, (tile + 1) * LANES)
         rows = tile_rows(tok_rows, tile)
-        conv_in = product(k_ref[:, cols], v_ref[:, cols]).astype(F32)
-        long_conv = x_ref[rows, :] + edge_ref[rows, :] + gain_ref[:, cols] * conv_in
+        long_conv = x_ref[rows, :] + edge_ref[rows, :]
         layer_ref[:, cols] = (q_ref[:, cols].astype(F32) * long_conv).astype(BF16)
         departure(0, tile).start()
     fill_edge(edge_ref, edge(1), coef_ref, tok_rows, tiles, tok_rows - 1, -1)
     for tile in range(tiles):
-        arrival(1, tile).wait()
-    for tile in range(tiles):
         cols = slice(tile * LANES, (tile + 1) * LANES)
         rows = tile_rows(tok_rows, tile)
-        mid_grad = product(o_ref[:, cols], q_ref[:, cols]).astype(F32)
-        conv_grad = g_ref[rows, :] + edge_ref[rows, :] + gain_ref[:, cols] * mid_grad
+        conv_grad = g_ref[rows, :] + edge_ref[rows, :]
         key_ref[:, cols] = (conv_grad * v_ref[:, cols].astype(F32)).astype(BF16)
         departure(1, tile).start()
         value_ref[:, cols] = (conv_grad * k_ref[:, cols].astype(F32)).astype(BF16)
@@ -353,30 +345,29 @@
             departure(i, tile).wait()
 
 
-def final_outputs(signals, coefs, gain, kept, given, parts):
+def final_outputs(signals, coefs, parts, kept, given):
     tok_rows, width = signals[0].shape
     modes, tiles = coefs.shape[1:3]
-    args = (*signals, coefs, gain, kept, given)
+    args = (*signals, coefs, *parts, kept, given)
     whole = pl.BlockSpec(memory_space=pltpu.VMEM)
-    away = pl.BlockSpec(memory_space=pl.ANY)
     return pl.pallas_call(
         final_kernel,
-        in_specs=[whole] * len(args) + [away] * len(parts),
-        out_specs=[away] * 3,
+        in_specs=[whole] * len(args),
+        out_specs=[pl.BlockSpec(memory_space=pl.ANY)] * 3,
         out_shape=[jax.ShapeDtypeStruct((tok_rows, width), BF16)] * 3,
-        scratch_shapes=[pltpu.VMEM(token_shape(tok_rows, tiles), F32)] * 3
+        scratch_shapes=[pltpu.VMEM(token_shape(tok_rows, tiles), F32)]
         + [pltpu.VMEM((tok_rows, width), BF16)] * 3
-        + [pltpu.SemaphoreType.DMA((2, tiles)), pltpu.SemaphoreType.DMA((3, tiles))],
+        + [pltpu.SemaphoreType.DMA((3, tiles))],
         compiler_params=pltpu.CompilerParams(vmem_limit_bytes=VMEM_BYTES),
         cost_estimate=pl.CostEstimate(
             flops=8 * modes * tok_rows * width, bytes_accessed=14 * tok_rows * width, transcendentals=0
         ),
         name="final_outputs",
-    )(*args, *parts)
-
-
-def lag_kernel(shards, chans, groups, owned, scale, *refs):
-    in_refs, out_ref, u_all, g_all, turned_all = refs[:-4], *refs[-4:]
+    )(*args)
+
+
+def lag_kernel(shards, chans, groups, owned, scale, count, *refs):
+    in_refs, (out_ref, u_all, g_all, turned_all) = refs[:count], refs[-4:]
     tok_rows = out_ref.shape[2]
     halves = tok_rows // LANES
     blocks = shards * halves
@@ -450,10 +441,10 @@
         turned_all[f] = lax.dot_general(
             mirror, u_all[f], (((1,), (1,)), ((), ())), preferred_element_type=F32
         ).astype(BF16)
-    lax.fori_loop(0, owned, one_filter, 0, unroll=min(owned, 2))
-
-
-def filter_lags(received, shards, chans, owned, scale):
+    lax.fori_loop(0, owned, one_filter, 0, unroll=min(owned, 4))
+
+
+def filter_lags(received, held, shards, chans, owned, scale):
     tok_rows = received.shape[2]
     groups = received.shape[1] // (2 * owned)
     halves = tok_rows // LANES
@@ -465,7 +456,10 @@
         split = split.transpose(2, 4, 0, 5, 1, 3, 6).reshape(2, owned, full, LANES)
         args = (split[0], split[1])
     return pl.pallas_call(
-        functools.partial(lag_kernel, shards, chans, groups, owned, scale),
+        functools.partial(lag_kernel, shards, chans, groups, owned, scale, len(args)),
+        in_specs=[pl.BlockSpec(memory_space=pltpu.VMEM)] * len(args)
+        + [pl.BlockSpec(memory_space=pl.ANY)] * len(held),
+        out_specs=pl.BlockSpec(memory_space=pltpu.VMEM),
         out_shape=jax.ShapeDtypeStruct((shards, owned, tok_rows), F32),
         scratch_shapes=[
             pltpu.VMEM((owned, full, LANES), BF16),
@@ -477,7 +471,7 @@
             flops=4 * owned * LANES * full * full, bytes_accessed=8 * owned * full * LANES, transcendentals=0
         ),
         name="filter_lags",
-    )(*args)
+    )(*args, *held)
 
 
 def per_device(query_proj, key_proj, value_proj, out_grad, residues, decay_rate, skip_gain):
@@ -510,18 +504,18 @@
     states, own = block_states(seq_index, pairs, *signals, coefs)
     *states, coefs = lax.optimization_barrier((*states, coefs))
     states = [along_column(state, pairs, 1 + i) for i, state in enumerate(states)]
-    parts = local_parts(*signals, coefs)
+    parts = local_parts(*signals, coefs, skip_gain[None, :])
     kept, given = pair_states(seq_index, coefs, own, states)
-    received, kept, given, *parts = lax.optimization_barrier((received, kept, given, *parts))
+    received, kept, given = lax.optimization_barrier((received, kept, given))
     given = inside_pair(given, pairs)
 
     scale = 1.0 / math.sqrt(length * (CHANNELS // FILTERS))
-    lags = filter_lags(received, shards, chans, owned, scale)
+    lags = filter_lags(received, parts, shards, chans, owned, scale)
     lags, given = lax.optimization_barrier((lags, given))
     lags = lax.all_to_all(lags, "seq", split_axis=0, concat_axis=0, tiled=True)
     filter_grad = lags.reshape(shards * owned, tok_rows).T
     layer_out, key_grad, value_grad = final_outputs(
-        signals, coefs, skip_gain[None, :], kept, given, parts
+        signals[:3], coefs, parts, kept, given
     )
     return (layer_out, key_grad, value_grad, filter_grad)
 

time: 60.4 us -> 65 us (1.076)
  waiting for transfers between devices: 12 us -> 20.8 us
  Pallas kernels: 23.6 us -> 20.2 us
  local copies, waits for them, and re-layouts: 5.84 us -> 5.04 us
    ppermute x3, waiting for transfers between devices: 12 us -> 19.8 us  [along_column(): return lax.ppermute(state, 'seq', route)]
    pallas_call x1, Pallas kernels: 7.17 us -> 3.81 us  [final_outputs(): pl.pallas_call(final_kernel, in_specs=[whole] * len(args), out_specs=[pl....]
    all_to_all x1, waiting for transfers between devices: 0.01 us -> 0.94 us  [per_device(): lags = lax.all_to_all(lags, 'seq', split_axis=0, concat_axis=0, tiled=True)]
    unnamed x25 -> x29, local copies, waits for them, and re-layouts: 5.76 us -> 4.96 us
  transfers between devices with their start and end apart: 6 -> 6, of which waited for: 2 -> 3; matrix products, arithmetic and copies ran while one was open for 0% -> 0% of each run, Pallas kernels for 34% -> 27%
where the time goes in v8:
time: 65 us; the launch traced here: 64.7 us
  waiting for transfers between devices  20.8 us (32%)
  Pallas kernels  20.2 us (31%)
  starting transfers between devices  17.8 us (27%)
  local copies, waits for them, and re-layouts  5.04 us (8%)
  between operations  0.86 us (1%)
    ppermute x3, waiting for transfers between devices, along_column(): return lax.ppermute(state, 'seq', route)  19.8 us
    all_to_all x1, starting transfers between devices, per_device(): lax.all_to_all(send, ('seq', 'chan'), split_axis=0, concat_axis=0, tiled=...  7.3 us
    pallas_call x1, Pallas kernels, local_parts(): pl.pallas_call(local_kernel, out_shape=[jax.ShapeDtypeStruct(token_shape(...  6.34 us
    ppermute x3, starting transfers between devices, along_column(): return lax.ppermute(state, 'seq', route)  5.65 us
    unnamed x29, local copies, waits for them, and re-layouts  4.96 us
    pallas_call x1, Pallas kernels, filter_lags(): pl.pallas_call(functools.partial(lag_kernel, shards, chans, groups, owned...  4.02 us
    pallas_call x1, Pallas kernels, final_outputs(): pl.pallas_call(final_kernel, in_specs=[whole] * len(args), out_specs=[pl....  3.81 us
    all_to_all x1, starting transfers between devices, per_device(): lags = lax.all_to_all(lags, 'seq', split_axis=0, concat_axis=0, tiled=True)  3.35 us
  transfers between devices with their start and end apart: 6, of which 3 were waited for; matrix products, arithmetic and copies ran while one was open for 0% of the time, Pallas kernels for 27%

profile of v8, /device:TPU:0, one launch (start us, length us, event | category | flops | bytes accessed | tf_op | source)
XLA Modules:
  0.0 64.7 jit_solution(13660260253056207638)
XLA Ops:
  0.6 0.0 copy-start.12
  0.6 0.0 copy-start.13
  0.7 3.0 %pack_signals.1 = bf16[32,64,256]{2,1,0:T(8,128)(2,1)} custom-call(bf16[256,1024]{1,0:T(8,128)(2,1)} %k_ref.2, bf16[256,1024]{1,0:T(8,128)(2,1)} %v_ref.2, bf16[256,1024]{1,0:T(8,128)(2,1)} %o_ref.1, bf16[256,1024]{1,0:T(8,128)(2,1)} %q_ref.2), custom_call_target="tpu_custom_call" | custom-call | tf_op jit(solution)/shard_map/pack_signals/pallas_call | solution.py:97
  3.6 0.0 copy-start
  3.6 0.0 copy-start.1
  3.6 0.0 copy-start.2
  3.6 0.0 copy-start.3
  3.7 7.3 %all-to-all-start = ((bf16[32,64,256]{2,1,0:T(8,128)(2,1)}), bf16[32,64,256]{2,1,0:T(8,128)(2,1)S(1)}, u32[]{:S(2)}, u32[]{:S(2)}) async-start(bf16[32,64,256]{2,1,0:T(8,128)(2,1)} %pack_signals.1), calls=%async_computation | async-start | bytes 2097152 | tf_op jit(solution)/shard_map/all_to_all | solution.py:490
  11.0 0.0 copy-done.12
  11.0 0.0 copy-done.13
  11.1 0.1 broadcast_in_dim.11
  11.1 0.0 copy-done
  11.1 0.0 copy-done.1
  11.2 0.0 copy-done.2
  11.2 0.0 copy-done.3
  11.2 0.0 copy-start.10
  11.2 3.0 %block_states.1 = (bf16[128,128]{1,0:T(8,128)(2,1)S(1)}, bf16[128,128]{1,0:T(8,128)(2,1)S(1)}, bf16[128,128]{1,0:T(8,128)(2,1)S(1)}, f32[2,128,128]{2,1,0:T(8,128)S(1)}) custom-call(s32[1]{0:T(128)} %bitcast.seq_ref, bf16[256,1024]{1,0:T(8,128)(2,1)S(1)} %copy-done, bf16[256,1024]{1,0:T(8,128)(2,1)S(1)} %copy-done.1, bf16[256,1024]{1,0:T(8,128)(2,1)S(1)} %copy-done.2, ...), custom_call_target="tpu_custom_call" | custom-call | flops 16777216 | bytes 2097152 | tf_op jit(solution)/shard_map/block_states/pallas_call | solution.py:198
  14.2 1.8 %collective-permute-start = (bf16[128,128]{1,0:T(8,128)(2,1)S(1)}, bf16[128,128]{1,0:T(8,128)(2,1)S(1)}, u32[]{:S(2)}, u32[]{:S(2)}) collective-permute-start(bf16[128,128]{1,0:T(8,128)(2,1)S(1)} %get-tuple-element.45), channel_id=1, source_target_pairs={{0,8},{4,12},{8,16},{12,20},{16,24},{20,28},{24,0},{28,4},{1,9},{5... | collective-permute-start | bytes 98312 | tf_op jit(solution)/shard_map/ppermute | solution.py:289
  16.0 2.4 %collective-permute-start.1 = (bf16[128,128]{1,0:T(8,128)(2,1)S(1)}, bf16[128,128]{1,0:T(8,128)(2,1)S(1)}, u32[]{:S(2)}, u32[]{:S(2)}) collective-permute-start(bf16[128,128]{1,0:T(8,128)(2,1)S(1)} %get-tuple-element.46), channel_id=1, source_target_pairs={{0,16},{4,20},{8,24},{12,28},{16,0},{20,4},{24,8},{28,12},{1,17},{... | collective-permute-start | bytes 98312 | tf_op jit(solution)/shard_map/ppermute | solution.py:289
  18.5 1.4 %collective-permute-start.2 = (bf16[128,128]{1,0:T(8,128)(2,1)S(1)}, bf16[128,128]{1,0:T(8,128)(2,1)S(1)}, u32[]{:S(2)}, u32[]{:S(2)}) collective-permute-start(bf16[128,128]{1,0:T(8,128)(2,1)S(1)} %get-tuple-element.47), channel_id=1, source_target_pairs={{0,24},{4,28},{8,0},{12,4},{16,8},{20,12},{24,16},{28,20},{1,25},{... | collective-permute-start | bytes 98312 | tf_op jit(solution)/shard_map/ppermute | solution.py:289
  19.9 13.8 %collective-permute-done.refs_0_ = bf16[128,128]{1,0:T(8,128)(2,1)S(1)} collective-permute-done((bf16[128,128]{1,0:T(8,128)(2,1)S(1)}, bf16[128,128]{1,0:T(8,128)(2,1)S(1)}, u32[]{:S(2)}, u32[]{:S(2)}) %collective-permute-start) | collective-permute-done | bytes 32800 | tf_op jit(solution)/shard_map/ppermute | solution.py:289
  33.7 6.0 %collective-permute-done.1.refs_1_ = bf16[128,128]{1,0:T(8,128)(2,1)S(1)} collective-permute-done((bf16[128,128]{1,0:T(8,128)(2,1)S(1)}, bf16[128,128]{1,0:T(8,128)(2,1)S(1)}, u32[]{:S(2)}, u32[]{:S(2)}) %collective-permute-start.1) | collective-permute-done | bytes 32800 | tf_op jit(solution)/shard_map/ppermute | solution.py:289
  39.7 0.0 collective-permute-done.2.refs_2_
  39.7 0.1 pair_states.1
  39.8 0.0 copy-start.11
  39.8 0.6 copy-done.11
  40.4 0.0 all-to-all-done.refs_0_
  40.4 0.0 copy-start.6
  40.4 1.0 %copy-done.6 = bf16[32,64,256]{2,1,0:T(8,128)(2,1)} copy-done((bf16[32,64,256]{2,1,0:T(8,128)(2,1)}, bf16[32,64,256]{2,1,0:T(8,128)(2,1)S(1)}, u32[]{:S(2)}) %copy-start.6) | copy-done | bytes 1048600
  41.4 1.5 %collective-permute-start.3 = (bf16[2,128,128]{2,1,0:T(8,128)(2,1)}, bf16[2,128,128]{2,1,0:T(8,128)(2,1)S(1)}, u32[]{:S(2)}, u32[]{:S(2)}) collective-permute-start(bf16[2,128,128]{2,1,0:T(8,128)(2,1)} %copy-done.11), channel_id=1, source_target_pairs={{0,4},{4,0},{8,12},{12,8},{16,20},{20,16},{24,28},{28,24},{1,5},{5... | collective-permute-start | bytes 196616 | tf_op jit(solution)/shard_map/ppermute | solution.py:293
  42.8 0.0 copy-done.10
  42.8 0.0 copy-start.7
  42.8 6.3 %local_parts.1 = (f32[2112,128]{1,0:T(8,128)S(1)}, f32[2112,128]{1,0:T(8,128)S(1)}) custom-call(bf16[256,1024]{1,0:T(8,128)(2,1)S(1)} %copy-done, bf16[256,1024]{1,0:T(8,128)(2,1)S(1)} %copy-done.1, bf16[256,1024]{1,0:T(8,128)(2,1)S(1)} %copy-done.2, bf16[256,1024]{1,0:T(8,128)(2,1)S(1)} %copy-done.3, f32[3,16,8,128]{3,2,1,0:T(8,128)S(1)} %bitcast.16, ...), custom_call_target="tpu_custom_call" | custom-call | flops 33554432 | bytes 2097152 | tf_op jit(solution)/shard_map/local_parts/pallas_call | solution.py:276
  49.2 0.0 copy-start.4
  49.2 0.0 copy-done.7
  49.2 4.0 %filter_lags.1 = f32[8,8,256]{2,1,0:T(8,128)} custom-call(bf16[32,64,256]{2,1,0:T(8,128)(2,1)S(1)} %copy-done.7, f32[2112,128]{1,0:T(8,128)S(1)} %get-tuple-element.41.refs_1_.x_ref, f32[2112,128]{1,0:T(8,128)S(1)} %get-tuple-element.42.refs_2_.g_ref), custom_call_target="tpu_custom_call" | custom-call | flops 268435456 | bytes 2097152 | tf_op jit(solution)/shard_map/filter_lags/pallas_call | solution.py:458
  53.2 0.0 copy-done.4
  53.2 0.0 collective-permute-done.3.given_ref
  53.2 0.0 copy-start.8
  53.2 0.6 copy-done.8
  53.9 3.3 %all-to-all-start.1 = ((f32[8,8,256]{2,1,0:T(8,128)}), f32[8,8,256]{2,1,0:T(8,128)S(1)}, u32[]{:S(2)}, u32[]{:S(2)}) async-start(f32[8,8,256]{2,1,0:T(8,128)} %filter_lags.1), calls=%async_computation.1 | async-start | bytes 131072 | tf_op jit(solution)/shard_map/all_to_all | solution.py:515
  57.2 0.0 copy-start.5
  57.2 1.2 %copy-done.5 = f32[2112,128]{1,0:T(8,128)S(1)} copy-done((f32[2112,128]{1,0:T(8,128)S(1)}, f32[2112,128]{1,0:T(8,128)}, u32[]{:S(2)}) %copy-start.5) | copy-done | bytes 1081368
  58.5 0.0 copy-start.9
  58.5 0.8 %copy-done.9 = bf16[2,128,128]{2,1,0:T(8,128)(2,1)S(1)} copy-done((bf16[2,128,128]{2,1,0:T(8,128)(2,1)S(1)}, bf16[2,128,128]{2,1,0:T(8,128)(2,1)}, u32[]{:S(2)}) %copy-start.9) | copy-done | bytes 65560
  59.3 3.8 %final_outputs.1 = (bf16[256,1024]{1,0:T(8,128)(2,1)}, bf16[256,1024]{1,0:T(8,128)(2,1)}, bf16[256,1024]{1,0:T(8,128)(2,1)}) custom-call(bf16[256,1024]{1,0:T(8,128)(2,1)S(1)} %copy-done, bf16[256,1024]{1,0:T(8,128)(2,1)S(1)} %copy-done.1, bf16[256,1024]{1,0:T(8,128)(2,1)S(1)} %copy-done.2, f32[3,16,8,128]{3,2,1,0:T(8,128)S(1)} %bitcast.17, ...), custom_call_target="tpu_custom_call" | custom-call | flops 33554432 | bytes 3670016 | tf_op jit(solution)/shard_map/final_outputs/pallas_call | solution.py:353
  63.1 0.9 %all-to-all-done.1 = f32[8,8,256]{2,1,0:T(8,128)S(1)} async-done(((f32[8,8,256]{2,1,0:T(8,128)}), f32[8,8,256]{2,1,0:T(8,128)S(1)}, u32[]{:S(2)}, u32[]{:S(2)}) %all-to-all-start.1) | async-done | bytes 65568 | tf_op jit(solution)/shard_map/all_to_all | solution.py:515
  64.1 0.6 copy.12
  (3 shorter events, 0.1 us)
Async XLA Ops:
  0.6 10.3 %copy-start.12 = (f32[256,16]{0,1:T(8,128)S(1)}, f32[256,16]{0,1:T(8,128)}, u32[]{:S(2)}) copy-start(f32[256,16]{0,1:T(8,128)} %param.12) | copy-start | bytes 49156
  0.6 10.3 %copy-start.13 = (f32[256,16]{0,1:T(8,128)S(1)}, f32[256,16]{0,1:T(8,128)}, u32[]{:S(2)}) copy-start(f32[256,16]{0,1:T(8,128)} %param.11) | copy-start | bytes 49156
  3.6 7.5 %copy-start = (bf16[256,1024]{1,0:T(8,128)(2,1)S(1)}, bf16[256,1024]{1,0:T(8,128)(2,1)}, u32[]{:S(2)}) copy-start(bf16[256,1024]{1,0:T(8,128)(2,1)} %q_ref.2) | copy-start | bytes 1572868
  3.6 7.5 %copy-start.1 = (bf16[256,1024]{1,0:T(8,128)(2,1)S(1)}, bf16[256,1024]{1,0:T(8,128)(2,1)}, u32[]{:S(2)}) copy-start(bf16[256,1024]{1,0:T(8,128)(2,1)} %k_ref.2) | copy-start | bytes 1572868
  3.6 7.5 %copy-start.2 = (bf16[256,1024]{1,0:T(8,128)(2,1)S(1)}, bf16[256,1024]{1,0:T(8,128)(2,1)}, u32[]{:S(2)}) copy-start(bf16[256,1024]{1,0:T(8,128)(2,1)} %v_ref.2) | copy-start | bytes 1572868
  3.6 7.5 %copy-start.3 = (bf16[256,1024]{1,0:T(8,128)(2,1)S(1)}, bf16[256,1024]{1,0:T(8,128)(2,1)}, u32[]{:S(2)}) copy-start(bf16[256,1024]{1,0:T(8,128)(2,1)} %o_ref.1) | copy-start | bytes 1572868
  3.7 36.7 %all-to-all-start = ((bf16[32,64,256]{2,1,0:T(8,128)(2,1)}), bf16[32,64,256]{2,1,0:T(8,128)(2,1)S(1)}, u32[]{:S(2)}, u32[]{:S(2)}) async-start(bf16[32,64,256]{2,1,0:T(8,128)(2,1)} %pack_signals.1), calls=%async_computation | async-start | bytes 2097152 | tf_op jit(solution)/shard_map/all_to_all | solution.py:490
  11.2 31.7 %copy-start.10 = (f32[1024]{0:T(1024)S(1)}, f32[1024]{0:T(1024)}, u32[]{:S(2)}) copy-start(f32[1024]{0:T(1024)} %param.13) | copy-start | bytes 12292
  14.2 19.5 %collective-permute-start = (bf16[128,128]{1,0:T(8,128)(2,1)S(1)}, bf16[128,128]{1,0:T(8,128)(2,1)S(1)}, u32[]{:S(2)}, u32[]{:S(2)}) collective-permute-start(bf16[128,128]{1,0:T(8,128)(2,1)S(1)} %get-tuple-element.45), channel_id=1, source_target_pairs={{0,8},{4,12},{8,16},{12,20},{16,24},{20,28},{24,0},{28,4},{1,9},{5... | collective-permute-start | bytes 98312 | tf_op jit(solution)/shard_map/ppermute | solution.py:289
  16.0 23.6 %collective-permute-start.1 = (bf16[128,128]{1,0:T(8,128)(2,1)S(1)}, bf16[128,128]{1,0:T(8,128)(2,1)S(1)}, u32[]{:S(2)}, u32[]{:S(2)}) collective-permute-start(bf16[128,128]{1,0:T(8,128)(2,1)S(1)} %get-tuple-element.46), channel_id=1, source_target_pairs={{0,16},{4,20},{8,24},{12,28},{16,0},{20,4},{24,8},{28,12},{1,17},{... | collective-permute-start | bytes 98312 | tf_op jit(solution)/shard_map/ppermute | solution.py:289
  18.5 21.2 %collective-permute-start.2 = (bf16[128,128]{1,0:T(8,128)(2,1)S(1)}, bf16[128,128]{1,0:T(8,128)(2,1)S(1)}, u32[]{:S(2)}, u32[]{:S(2)}) collective-permute-start(bf16[128,128]{1,0:T(8,128)(2,1)S(1)} %get-tuple-element.47), channel_id=1, source_target_pairs={{0,24},{4,28},{8,0},{12,4},{16,8},{20,12},{24,16},{28,20},{1,25},{... | collective-permute-start | bytes 98312 | tf_op jit(solution)/shard_map/ppermute | solution.py:289
  39.8 0.6 copy-start.11
  40.4 1.0 %copy-start.6 = (bf16[32,64,256]{2,1,0:T(8,128)(2,1)}, bf16[32,64,256]{2,1,0:T(8,128)(2,1)S(1)}, u32[]{:S(2)}) copy-start(bf16[32,64,256]{2,1,0:T(8,128)(2,1)S(1)} %all-to-all-done.refs_0_) | copy-start | bytes 3145732
  41.4 11.9 %collective-permute-start.3 = (bf16[2,128,128]{2,1,0:T(8,128)(2,1)}, bf16[2,128,128]{2,1,0:T(8,128)(2,1)S(1)}, u32[]{:S(2)}, u32[]{:S(2)}) collective-permute-start(bf16[2,128,128]{2,1,0:T(8,128)(2,1)} %copy-done.11), channel_id=1, source_target_pairs={{0,4},{4,0},{8,12},{12,8},{16,20},{20,16},{24,28},{28,24},{1,5},{5... | collective-permute-start | bytes 196616 | tf_op jit(solution)/shard_map/ppermute | solution.py:293
  42.8 6.4 %copy-start.7 = (bf16[32,64,256]{2,1,0:T(8,128)(2,1)S(1)}, bf16[32,64,256]{2,1,0:T(8,128)(2,1)}, u32[]{:S(2)}) copy-start(bf16[32,64,256]{2,1,0:T(8,128)(2,1)} %copy-done.6) | copy-start | bytes 3145732
  49.2 4.0 %copy-start.4 = (f32[2112,128]{1,0:T(8,128)}, f32[2112,128]{1,0:T(8,128)S(1)}, u32[]{:S(2)}) copy-start(f32[2112,128]{1,0:T(8,128)S(1)} %get-tuple-element.42.refs_2_.g_ref) | copy-start | bytes 3244036
  53.2 0.6 copy-start.8
  53.9 10.2 %all-to-all-start.1 = ((f32[8,8,256]{2,1,0:T(8,128)}), f32[8,8,256]{2,1,0:T(8,128)S(1)}, u32[]{:S(2)}, u32[]{:S(2)}) async-start(f32[8,8,256]{2,1,0:T(8,128)} %filter_lags.1), calls=%async_computation.1 | async-start | bytes 131072 | tf_op jit(solution)/shard_map/all_to_all | solution.py:515
  57.2 1.2 %copy-start.5 = (f32[2112,128]{1,0:T(8,128)S(1)}, f32[2112,128]{1,0:T(8,128)}, u32[]{:S(2)}) copy-start(f32[2112,128]{1,0:T(8,128)} %copy-done.4) | copy-start | bytes 3244036
  58.5 0.8 %copy-start.9 = (bf16[2,128,128]{2,1,0:T(8,128)(2,1)S(1)}, bf16[2,128,128]{2,1,0:T(8,128)(2,1)}, u32[]{:S(2)}) copy-start(bf16[2,128,128]{2,1,0:T(8,128)(2,1)} %copy-done.8) | copy-start | bytes 196612

commit v9 on v8

--- a/solution.py
+++ b/solution.py
@@ -14,6 +14,7 @@
 SUBLANES = 8
 GAP = 8
 VMEM_BYTES = 16 * 1024 * 1024
+FINAL_VMEM_BYTES = 60 * 1024 * 1024
 PACK_VMEM_BYTES = 62 * 1024 * 1024
 F32 = jnp.float32
 BF16 = jnp.bfloat16
@@ -211,7 +212,7 @@
     return states, own
 
 
-def pair_kernel(seq_ref, coef_ref, own_ref, *refs):
+def pair_kernel(seq_ref, coef_ref, own_ref, _, *refs):
     state_refs, kept_ref, given_ref = refs[:-2], *refs[-2:]
     pairs = len(state_refs) + 1
     modes, tiles = coef_ref.shape[1:3]
@@ -238,11 +239,13 @@
         given_ref[1, rows] = jnp.where(second, decay * after + own, after).astype(LINK)
 
 
-def pair_states(seq_index, coefs, own, states):
+def pair_states(seq_index, coefs, own, parts, states):
     whole = pl.BlockSpec(memory_space=pltpu.VMEM)
     return pl.pallas_call(
         pair_kernel,
-        in_specs=[pl.BlockSpec(memory_space=pltpu.SMEM)] + [whole] * (2 + len(states)),
+        in_specs=[pl.BlockSpec(memory_space=pltpu.SMEM), whole, whole]
+        + [pl.BlockSpec(memory_space=pl.ANY)]
+        + [whole] * len(states),
         out_specs=[whole] * 2,
         out_shape=[
             jax.ShapeDtypeStruct(own.shape, F32),
@@ -250,10 +253,11 @@
         ],
         compiler_params=pltpu.CompilerParams(vmem_limit_bytes=VMEM_BYTES),
         name="pair_states",
-    )(seq_index, coefs, own, *states)
-
-
-def local_kernel(q_ref, k_ref, v_ref, o_ref, coef_ref, gain_ref, conv_ref, grad_ref):
+    )(seq_index, coefs, own, parts, *states)
+
+
+def local_kernel(q_ref, k_ref, v_ref, o_ref, coef_ref, gain_ref, part_ref):
+    conv_ref, grad_ref = part_ref.at[0], part_ref.at[1]
     tok_rows, width = k_ref.shape
     tiles = width // LANES
     spread_tokens(k_ref, v_ref, conv_ref)
@@ -275,7 +279,7 @@
     modes, tiles = coefs.shape[1:3]
     return pl.pallas_call(
         local_kernel,
-        out_shape=[jax.ShapeDtypeStruct(token_shape(tok_rows, tiles), F32)] * 2,
+        out_shape=jax.ShapeDtypeStruct((2, *token_shape(tok_rows, tiles)), F32),
         compiler_params=pltpu.CompilerParams(vmem_limit_bytes=VMEM_BYTES),
         cost_estimate=pl.CostEstimate(
             flops=8 * modes * tok_rows * width, bytes_accessed=8 * tok_rows * width, transcendentals=0
@@ -306,13 +310,19 @@
     lax.fori_loop(0, tok_rows, step, held, unroll=8)
 
 
-def final_kernel(
-    q_ref, k_ref, v_ref, coef_ref, x_ref, g_ref, kept_ref, given_ref, *refs
-):
-    hbm_refs, (edge_ref, layer_ref, key_ref, value_ref, sems) = refs[:3], refs[3:]
+def final_kernel(q_ref, k_ref, v_ref, coef_ref, kept_ref, given_ref, part_ref, *refs):
+    hbm_refs, refs = refs[:3], refs[3:]
+    held_ref, edge_ref, layer_ref, key_ref, value_ref, in_sems, sems = refs
+    x_ref, g_ref = held_ref.at[0], held_ref.at[1]
     tok_rows, width = k_ref.shape
     tiles = width // LANES
     modes = coef_ref.shape[1]
+
+    def arrival(i, half):
+        rows = pl.ds(half * (part_ref.shape[1] // 2), part_ref.shape[1] // 2)
+        return pltpu.make_async_copy(
+            part_ref.at[i, rows, :], held_ref.at[i, rows, :], in_sems.at[i, half]
+        )
 
     def departure(i, tile):
         place = (slice(None), pl.ds(tile * LANES, LANES))
@@ -324,7 +334,12 @@
         total = kept_ref[side] + given_ref[side].astype(F32)
         return [total[m * tiles : (m + 1) * tiles] for m in range(modes)]
 
+    for i in range(2):
+        for half in range(2):
+            arrival(i, half).start()
     fill_edge(edge_ref, edge(0), coef_ref, tok_rows, tiles, 0, 1)
+    for half in range(2):
+        arrival(0, half).wait()
     for tile in range(tiles):
         cols = slice(tile * LANES, (tile + 1) * LANES)
         rows = tile_rows(tok_rows, tile)
@@ -332,6 +347,8 @@
         layer_ref[:, cols] = (q_ref[:, cols].astype(F32) * long_conv).astype(BF16)
         departure(0, tile).start()
     fill_edge(edge_ref, edge(1), coef_ref, tok_rows, tiles, tok_rows - 1, -1)
+    for half in range(2):
+        arrival(1, half).wait()
     for tile in range(tiles):
         cols = slice(tile * LANES, (tile + 1) * LANES)
         rows = tile_rows(tok_rows, tile)
@@ -345,29 +362,36 @@
             departure(i, tile).wait()
 
 
-def final_outputs(signals, coefs, parts, kept, given):
+def final_outputs(signals, coefs, kept, given, parts):
     tok_rows, width = signals[0].shape
     modes, tiles = coefs.shape[1:3]
-    args = (*signals, coefs, *parts, kept, given)
+    args = (*signals, coefs, kept, given)
     whole = pl.BlockSpec(memory_space=pltpu.VMEM)
+    away = pl.BlockSpec(memory_space=pl.ANY)
     return pl.pallas_call(
         final_kernel,
-        in_specs=[whole] * len(args),
-        out_specs=[pl.BlockSpec(memory_space=pl.ANY)] * 3,
+        in_specs=[whole] * len(args) + [away],
+        out_specs=[away] * 3,
         out_shape=[jax.ShapeDtypeStruct((tok_rows, width), BF16)] * 3,
-        scratch_shapes=[pltpu.VMEM(token_shape(tok_rows, tiles), F32)]
-        + [pltpu.VMEM((tok_rows, width), BF16)] * 3
-        + [pltpu.SemaphoreType.DMA((3, tiles))],
-        compiler_params=pltpu.CompilerParams(vmem_limit_bytes=VMEM_BYTES),
+        scratch_shapes=[
+            pltpu.VMEM(parts.shape, F32),
+            pltpu.VMEM(parts.shape[1:], F32),
+            pltpu.VMEM((tok_rows, width), BF16),
+            pltpu.VMEM((tok_rows, width), BF16),
+            pltpu.VMEM((tok_rows, width), BF16),
+            pltpu.SemaphoreType.DMA((2, 2)),
+            pltpu.SemaphoreType.DMA((3, tiles)),
+        ],
+        compiler_params=pltpu.CompilerParams(vmem_limit_bytes=FINAL_VMEM_BYTES),
         cost_estimate=pl.CostEstimate(
             flops=8 * modes * tok_rows * width, bytes_accessed=14 * tok_rows * width, transcendentals=0
         ),
         name="final_outputs",
-    )(*args)
-
-
-def lag_kernel(shards, chans, groups, owned, scale, count, *refs):
-    in_refs, (out_ref, u_all, g_all, turned_all) = refs[:count], refs[-4:]
+    )(*args, parts)
+
+
+def lag_kernel(shards, chans, groups, owned, scale, *refs):
+    in_refs, (out_ref, u_all, g_all, turned_all) = refs[:-4], refs[-4:]
     tok_rows = out_ref.shape[2]
     halves = tok_rows // LANES
     blocks = shards * halves
@@ -444,7 +468,7 @@
     lax.fori_loop(0, owned, one_filter, 0, unroll=min(owned, 4))
 
 
-def filter_lags(received, held, shards, chans, owned, scale):
+def filter_lags(received, shards, chans, owned, scale):
     tok_rows = received.shape[2]
     groups = received.shape[1] // (2 * owned)
     halves = tok_rows // LANES
@@ -456,10 +480,7 @@
         split = split.transpose(2, 4, 0, 5, 1, 3, 6).reshape(2, owned, full, LANES)
         args = (split[0], split[1])
     return pl.pallas_call(
-        functools.partial(lag_kernel, shards, chans, groups, owned, scale, len(args)),
-        in_specs=[pl.BlockSpec(memory_space=pltpu.VMEM)] * len(args)
-        + [pl.BlockSpec(memory_space=pl.ANY)] * len(held),
-        out_specs=pl.BlockSpec(memory_space=pltpu.VMEM),
+        functools.partial(lag_kernel, shards, chans, groups, owned, scale),
         out_shape=jax.ShapeDtypeStruct((shards, owned, tok_rows), F32),
         scratch_shapes=[
             pltpu.VMEM((owned, full, LANES), BF16),
@@ -471,7 +492,7 @@
             flops=4 * owned * LANES * full * full, bytes_accessed=8 * owned * full * LANES, transcendentals=0
         ),
         name="filter_lags",
-    )(*args, *held)
+    )(*args)
 
 
 def per_device(query_proj, key_proj, value_proj, out_grad, residues, decay_rate, skip_gain):
@@ -505,17 +526,17 @@
     *states, coefs = lax.optimization_barrier((*states, coefs))
     states = [along_column(state, pairs, 1 + i) for i, state in enumerate(states)]
     parts = local_parts(*signals, coefs, skip_gain[None, :])
-    kept, given = pair_states(seq_index, coefs, own, states)
+    kept, given = pair_states(seq_index, coefs, own, parts, states)
     received, kept, given = lax.optimization_barrier((received, kept, given))
     given = inside_pair(given, pairs)
 
     scale = 1.0 / math.sqrt(length * (CHANNELS // FILTERS))
-    lags = filter_lags(received, parts, shards, chans, owned, scale)
+    lags = filter_lags(received, shards, chans, owned, scale)
     lags, given = lax.optimization_barrier((lags, given))
     lags = lax.all_to_all(lags, "seq", split_axis=0, concat_axis=0, tiled=True)
     filter_grad = lags.reshape(shards * owned, tok_rows).T
     layer_out, key_grad, value_grad = final_outputs(
-        signals[:3], coefs, parts, kept, given
+        signals[:3], coefs, kept, given, parts
     )
     return (layer_out, key_grad, value_grad, filter_grad)
 

time: 65 us -> 58.4 us (0.90)
  waiting for transfers between devices: 20.8 us -> 14.7 us
  local copies, waits for them, and re-layouts: 5.04 us -> 1.42 us
  Pallas kernels: 20.2 us -> 23.2 us
    ppermute x3, waiting for transfers between devices: 19.8 us -> 13.2 us  [along_column(): return lax.ppermute(state, 'seq', route)]
    unnamed x29 -> x27, local copies, waits for them, and re-layouts: 4.96 us -> 1.34 us
    pallas_call x2, Pallas kernels: 10.2 us -> 11.8 us  [the longest x1 6.46 us: local_parts(): pl.pallas_call(local_kernel, out_shape=jax.ShapeDtypeStruct((2, *token_sh...]
    pallas_call x1, Pallas kernels: 4.02 us -> 5.23 us  [filter_lags(): pl.pallas_call(functools.partial(lag_kernel, shards, chans, groups, owned...]
  transfers between devices with their start and end apart: 6 -> 6, of which waited for: 3 -> 3; matrix products, arithmetic and copies ran while one was open for 0% -> 0% of each run, Pallas kernels for 27% -> 35%
where the time goes in v9:
time: 58.4 us; the launch traced here: 58.1 us
  Pallas kernels  23.2 us (40%)
  starting transfers between devices  17.8 us (30%)
  waiting for transfers between devices  14.7 us (25%)
  local copies, waits for them, and re-layouts  1.42 us (2%)
  between operations  0.88 us (2%)
    ppermute x3, waiting for transfers between devices, along_column(): return lax.ppermute(state, 'seq', route)  13.2 us
    all_to_all x1, starting transfers between devices, per_device(): lax.all_to_all(send, ('seq', 'chan'), split_axis=0, concat_axis=0, tiled=...  7.43 us
    pallas_call x1, Pallas kernels, local_parts(): pl.pallas_call(local_kernel, out_shape=jax.ShapeDtypeStruct((2, *token_sh...  6.46 us
    ppermute x3, starting transfers between devices, along_column(): return lax.ppermute(state, 'seq', route)  5.58 us
    pallas_call x1, Pallas kernels, final_outputs(): pl.pallas_call(final_kernel, in_specs=[whole] * len(args) + [away], out_s...  5.33 us
    pallas_call x1, Pallas kernels, filter_lags(): pl.pallas_call(functools.partial(lag_kernel, shards, chans, groups, owned...  5.23 us
    all_to_all x1, starting transfers between devices, per_device(): lags = lax.all_to_all(lags, 'seq', split_axis=0, concat_axis=0, tiled=True)  3.35 us
    pallas_call x1, Pallas kernels, pack_signals(): pl.pallas_call(functools.partial(pack_kernel, shards, chans, owned), in_s...  3.05 us
  transfers between devices with their start and end apart: 6, of which 3 were waited for; matrix products, arithmetic and copies ran while one was open for 0% of the time, Pallas kernels for 35%

profile of v9, /device:TPU:0, one launch (start us, length us, event | category | flops | bytes accessed | tf_op | source)
XLA Modules:
  0.0 58.1 jit_solution(2160026234446091061)
XLA Ops:
  0.6 0.0 copy-start.3
  0.6 0.0 copy-start.2
  0.7 0.0 copy-start.1
  0.7 0.0 copy-start.11
  0.7 0.0 copy-start.12
  0.7 3.1 %pack_signals.1 = bf16[32,64,256]{2,1,0:T(8,128)(2,1)} custom-call(bf16[256,1024]{1,0:T(8,128)(2,1)} %k_ref.2, bf16[256,1024]{1,0:T(8,128)(2,1)} %v_ref.2, bf16[256,1024]{1,0:T(8,128)(2,1)} %o_ref.1, bf16[256,1024]{1,0:T(8,128)(2,1)} %q_ref.2), custom_call_target="tpu_custom_call" | custom-call | tf_op jit(solution)/shard_map/pack_signals/pallas_call | solution.py:98
  3.7 0.0 copy-start.6
  3.8 0.0 copy-start.9
  3.8 7.4 %all-to-all-start = ((bf16[32,64,256]{2,1,0:T(8,128)(2,1)}), bf16[32,64,256]{2,1,0:T(8,128)(2,1)}, u32[]{:S(2)}, u32[]{:S(2)}) async-start(bf16[32,64,256]{2,1,0:T(8,128)(2,1)} %pack_signals.1), calls=%async_computation | async-start | bytes 2097152 | tf_op jit(solution)/shard_map/all_to_all | solution.py:511
  11.2 0.0 copy-done.11
  11.2 0.0 copy-done.12
  11.3 0.0 copy-start.4
  11.3 0.0 copy-start.7
  11.3 0.1 broadcast_in_dim.11
  11.4 0.0 copy-start.5
  11.4 0.0 copy-done.3
  11.4 0.0 copy-done.2
  11.4 0.0 copy-done.1
  11.4 0.0 copy-done.6
  11.4 3.0 %block_states.1 = (bf16[128,128]{1,0:T(8,128)(2,1)S(1)}, bf16[128,128]{1,0:T(8,128)(2,1)S(1)}, bf16[128,128]{1,0:T(8,128)(2,1)S(1)}, f32[2,128,128]{2,1,0:T(8,128)S(1)}) custom-call(s32[1]{0:T(128)} %bitcast.seq_ref, bf16[256,1024]{1,0:T(8,128)(2,1)S(1)} %copy-done.1, bf16[256,1024]{1,0:T(8,128)(2,1)S(1)} %copy-done.2, bf16[256,1024]{1,0:T(8,128)(2,1)S(1)} %copy-done.3, ...), custom_call_target="tpu_custom_call" | custom-call | flops 16777216 | bytes 2097152 | tf_op jit(solution)/shard_map/block_states/pallas_call | solution.py:199
  14.5 1.8 %collective-permute-start = (bf16[128,128]{1,0:T(8,128)(2,1)S(1)}, bf16[128,128]{1,0:T(8,128)(2,1)S(1)}, u32[]{:S(2)}, u32[]{:S(2)}) collective-permute-start(bf16[128,128]{1,0:T(8,128)(2,1)S(1)} %get-tuple-element.41), channel_id=1, source_target_pairs={{0,8},{4,12},{8,16},{12,20},{16,24},{20,28},{24,0},{28,4},{1,9},{5... | collective-permute-start | bytes 98312 | tf_op jit(solution)/shard_map/ppermute | solution.py:293
  16.2 2.4 %collective-permute-start.1 = (bf16[128,128]{1,0:T(8,128)(2,1)S(1)}, bf16[128,128]{1,0:T(8,128)(2,1)S(1)}, u32[]{:S(2)}, u32[]{:S(2)}) collective-permute-start(bf16[128,128]{1,0:T(8,128)(2,1)S(1)} %get-tuple-element.42), channel_id=1, source_target_pairs={{0,16},{4,20},{8,24},{12,28},{16,0},{20,4},{24,8},{28,12},{1,17},{... | collective-permute-start | bytes 98312 | tf_op jit(solution)/shard_map/ppermute | solution.py:293
  18.6 1.4 %collective-permute-start.2 = (bf16[128,128]{1,0:T(8,128)(2,1)S(1)}, bf16[128,128]{1,0:T(8,128)(2,1)S(1)}, u32[]{:S(2)}, u32[]{:S(2)}) collective-permute-start(bf16[128,128]{1,0:T(8,128)(2,1)S(1)} %get-tuple-element.43), channel_id=1, source_target_pairs={{0,24},{4,28},{8,0},{12,4},{16,8},{20,12},{24,16},{28,20},{1,25},{... | collective-permute-start | bytes 98312 | tf_op jit(solution)/shard_map/ppermute | solution.py:293
  20.1 0.0 copy-done.9
  20.1 0.0 copy-done.4
  20.1 0.0 copy-done.7
  20.1 6.5 %local_parts.1._.part_ref = f32[2,2112,128]{2,1,0:T(8,128)S(1)} custom-call(bf16[256,1024]{1,0:T(8,128)(2,1)S(1)} %copy-done.1, bf16[256,1024]{1,0:T(8,128)(2,1)S(1)} %copy-done.2, bf16[256,1024]{1,0:T(8,128)(2,1)S(1)} %copy-done.4, bf16[256,1024]{1,0:T(8,128)(2,1)S(1)} %copy-done.7, f32[3,16,8,128]{3,2,1,0:T(8,128)S(1)} %bitcast.15, f32[1,1024]{1,0:T(1,128)S(1)} %bitcast.18), custom_call_target="tpu_custom_call" | custom-call | flops 33554432 | bytes 2097152 | tf_op jit(solution)/shard_map/local_parts/pallas_call | solution.py:280
  26.5 0.0 copy-start
  26.5 7.3 %collective-permute-done.refs_0_ = bf16[128,128]{1,0:T(8,128)(2,1)S(1)} collective-permute-done((bf16[128,128]{1,0:T(8,128)(2,1)S(1)}, bf16[128,128]{1,0:T(8,128)(2,1)S(1)}, u32[]{:S(2)}, u32[]{:S(2)}) %collective-permute-start) | collective-permute-done | bytes 32800 | tf_op jit(solution)/shard_map/ppermute | solution.py:293
  33.8 6.0 %collective-permute-done.1.refs_1_ = bf16[128,128]{1,0:T(8,128)(2,1)S(1)} collective-permute-done((bf16[128,128]{1,0:T(8,128)(2,1)S(1)}, bf16[128,128]{1,0:T(8,128)(2,1)S(1)}, u32[]{:S(2)}, u32[]{:S(2)}) %collective-permute-start.1) | collective-permute-done | bytes 32800 | tf_op jit(solution)/shard_map/ppermute | solution.py:293
  39.8 0.0 collective-permute-done.2.refs_2_
  39.8 0.0 copy-done.5
  39.8 0.1 pair_states.1
  39.9 0.0 copy-start.8
  39.9 0.6 %copy-done.8 = f32[2,128,128]{2,1,0:T(8,128)} copy-done((f32[2,128,128]{2,1,0:T(8,128)}, f32[2,128,128]{2,1,0:T(8,128)S(1)}, u32[]{:S(2)}) %copy-start.8) | copy-done | bytes 131096
  40.5 0.0 all-to-all-done.refs_0_
  40.5 1.5 %collective-permute-start.3 = (bf16[2,128,128]{2,1,0:T(8,128)(2,1)S(1)}, bf16[2,128,128]{2,1,0:T(8,128)(2,1)S(1)}, u32[]{:S(2)}, u32[]{:S(2)}) collective-permute-start(bf16[2,128,128]{2,1,0:T(8,128)(2,1)S(1)} %get-tuple-element.48), channel_id=1, source_target_pairs={{0,4},{4,0},{8,12},{12,8},{16,20},{20,16},{24,28},{28,24},{1,5},{5... | collective-permute-start | bytes 196616 | tf_op jit(solution)/shard_map/ppermute | solution.py:297
  42.0 5.2 %filter_lags.1 = f32[8,8,256]{2,1,0:T(8,128)} custom-call(bf16[32,64,256]{2,1,0:T(8,128)(2,1)} %all-to-all-done.refs_0_), custom_call_target="tpu_custom_call" | custom-call | flops 268435456 | bytes 2097152 | tf_op jit(solution)/shard_map/filter_lags/pallas_call | solution.py:482
  47.2 0.0 collective-permute-done.3.given_ref
  47.2 0.0 copy-start.10
  47.3 3.4 %all-to-all-start.1 = ((f32[8,8,256]{2,1,0:T(8,128)}), f32[8,8,256]{2,1,0:T(8,128)S(1)}, u32[]{:S(2)}, u32[]{:S(2)}) async-start(f32[8,8,256]{2,1,0:T(8,128)} %filter_lags.1), calls=%async_computation.1 | async-start | bytes 131072 | tf_op jit(solution)/shard_map/all_to_all | solution.py:536
  50.6 0.0 copy-done
  50.6 0.0 copy-done.10
  50.6 5.3 %final_outputs.1 = (bf16[256,1024]{1,0:T(8,128)(2,1)}, bf16[256,1024]{1,0:T(8,128)(2,1)}, bf16[256,1024]{1,0:T(8,128)(2,1)}) custom-call(bf16[256,1024]{1,0:T(8,128)(2,1)} %q_ref.2, bf16[256,1024]{1,0:T(8,128)(2,1)} %k_ref.2, bf16[256,1024]{1,0:T(8,128)(2,1)} %v_ref.2, f32[3,16,8,128]{3,2,1,0:T(8,128)} %bitcast.17, f32[2,128,128]{2,1,0:T(8,128)} %copy-done.8, ...), custom_call_target="tpu_custom_call" | custom-call | flops 33554432 | bytes 3670016 | tf_op jit(solution)/shard_map/final_outputs/pallas_call | solution.py:371
  56.0 1.5 %all-to-all-done.1 = f32[8,8,256]{2,1,0:T(8,128)S(1)} async-done(((f32[8,8,256]{2,1,0:T(8,128)}), f32[8,8,256]{2,1,0:T(8,128)S(1)}, u32[]{:S(2)}, u32[]{:S(2)}) %all-to-all-start.1) | async-done | bytes 65568 | tf_op jit(solution)/shard_map/all_to_all | solution.py:536
  57.5 0.6 %copy.12 = f32[256,64]{0,1:T(8,128)} copy(f32[256,64]{0,1:T(8,128)S(1)} %bitcast.19) | data formatting | bytes 131072
  (3 shorter events, 0.1 us)
Async XLA Ops:
  0.6 10.8 %copy-start.3 = (bf16[256,1024]{1,0:T(8,128)(2,1)S(1)}, bf16[256,1024]{1,0:T(8,128)(2,1)}, u32[]{:S(2)}) copy-start(bf16[256,1024]{1,0:T(8,128)(2,1)} %v_ref.2) | copy-start | bytes 1572868
  0.6 10.8 %copy-start.2 = (bf16[256,1024]{1,0:T(8,128)(2,1)S(1)}, bf16[256,1024]{1,0:T(8,128)(2,1)}, u32[]{:S(2)}) copy-start(bf16[256,1024]{1,0:T(8,128)(2,1)} %k_ref.2) | copy-start | bytes 1572868
  0.7 10.8 %copy-start.1 = (bf16[256,1024]{1,0:T(8,128)(2,1)S(1)}, bf16[256,1024]{1,0:T(8,128)(2,1)}, u32[]{:S(2)}) copy-start(bf16[256,1024]{1,0:T(8,128)(2,1)} %q_ref.2) | copy-start | bytes 1572868
  0.7 10.6 %copy-start.11 = (f32[256,16]{0,1:T(8,128)S(1)}, f32[256,16]{0,1:T(8,128)}, u32[]{:S(2)}) copy-start(f32[256,16]{0,1:T(8,128)} %param.12) | copy-start | bytes 49156
  0.7 10.6 %copy-start.12 = (f32[256,16]{0,1:T(8,128)S(1)}, f32[256,16]{0,1:T(8,128)}, u32[]{:S(2)}) copy-start(f32[256,16]{0,1:T(8,128)} %param.11) | copy-start | bytes 49156
  3.7 7.7 %copy-start.6 = (bf16[256,1024]{1,0:T(8,128)(2,1)S(1)}, bf16[256,1024]{1,0:T(8,128)(2,1)}, u32[]{:S(2)}) copy-start(bf16[256,1024]{1,0:T(8,128)(2,1)} %o_ref.1) | copy-start | bytes 1572868
  3.8 16.3 %copy-start.9 = (f32[1024]{0:T(1024)S(1)}, f32[1024]{0:T(1024)}, u32[]{:S(2)}) copy-start(f32[1024]{0:T(1024)} %param.13) | copy-start | bytes 12292
  3.8 36.8 %all-to-all-start = ((bf16[32,64,256]{2,1,0:T(8,128)(2,1)}), bf16[32,64,256]{2,1,0:T(8,128)(2,1)}, u32[]{:S(2)}, u32[]{:S(2)}) async-start(bf16[32,64,256]{2,1,0:T(8,128)(2,1)} %pack_signals.1), calls=%async_computation | async-start | bytes 2097152 | tf_op jit(solution)/shard_map/all_to_all | solution.py:511
  11.3 8.8 %copy-start.4 = (bf16[256,1024]{1,0:T(8,128)(2,1)S(1)}, bf16[256,1024]{1,0:T(8,128)(2,1)}, u32[]{:S(2)}) copy-start(bf16[256,1024]{1,0:T(8,128)(2,1)} %v_ref.2) | copy-start | bytes 1572868
  11.3 8.7 %copy-start.7 = (bf16[256,1024]{1,0:T(8,128)(2,1)S(1)}, bf16[256,1024]{1,0:T(8,128)(2,1)}, u32[]{:S(2)}) copy-start(bf16[256,1024]{1,0:T(8,128)(2,1)} %o_ref.1) | copy-start | bytes 1572868
  11.4 28.4 %copy-start.5 = (f32[3,16,4,2,128]{4,3,2,1,0:T(2,128)}, f32[3,16,4,2,128]{4,3,2,1,0:T(2,128)S(1)}, u32[]{:S(2)}) copy-start(f32[3,16,4,2,128]{4,3,2,1,0:T(2,128)S(1)} %broadcast_in_dim.11) | copy-start | bytes 589828
  14.5 19.3 %collective-permute-start = (bf16[128,128]{1,0:T(8,128)(2,1)S(1)}, bf16[128,128]{1,0:T(8,128)(2,1)S(1)}, u32[]{:S(2)}, u32[]{:S(2)}) collective-permute-start(bf16[128,128]{1,0:T(8,128)(2,1)S(1)} %get-tuple-element.41), channel_id=1, source_target_pairs={{0,8},{4,12},{8,16},{12,20},{16,24},{20,28},{24,0},{28,4},{1,9},{5... | collective-permute-start | bytes 98312 | tf_op jit(solution)/shard_map/ppermute | solution.py:293
  16.2 23.5 %collective-permute-start.1 = (bf16[128,128]{1,0:T(8,128)(2,1)S(1)}, bf16[128,128]{1,0:T(8,128)(2,1)S(1)}, u32[]{:S(2)}, u32[]{:S(2)}) collective-permute-start(bf16[128,128]{1,0:T(8,128)(2,1)S(1)} %get-tuple-element.42), channel_id=1, source_target_pairs={{0,16},{4,20},{8,24},{12,28},{16,0},{20,4},{24,8},{28,12},{1,17},{... | collective-permute-start | bytes 98312 | tf_op jit(solution)/shard_map/ppermute | solution.py:293
  18.6 21.1 %collective-permute-start.2 = (bf16[128,128]{1,0:T(8,128)(2,1)S(1)}, bf16[128,128]{1,0:T(8,128)(2,1)S(1)}, u32[]{:S(2)}, u32[]{:S(2)}) collective-permute-start(bf16[128,128]{1,0:T(8,128)(2,1)S(1)} %get-tuple-element.43), channel_id=1, source_target_pairs={{0,24},{4,28},{8,0},{12,4},{16,8},{20,12},{24,16},{28,20},{1,25},{... | collective-permute-start | bytes 98312 | tf_op jit(solution)/shard_map/ppermute | solution.py:293
  26.5 24.1 %copy-start = (f32[2,2112,128]{2,1,0:T(8,128)}, f32[2,2112,128]{2,1,0:T(8,128)S(1)}, u32[]{:S(2)}) copy-start(f32[2,2112,128]{2,1,0:T(8,128)S(1)} %local_parts.1._.part_ref) | copy-start | bytes 6488068
  39.9 0.7 %copy-start.8 = (f32[2,128,128]{2,1,0:T(8,128)}, f32[2,128,128]{2,1,0:T(8,128)S(1)}, u32[]{:S(2)}) copy-start(f32[2,128,128]{2,1,0:T(8,128)S(1)} %get-tuple-element.46.kept_ref) | copy-start | bytes 393220
  40.5 6.7 %collective-permute-start.3 = (bf16[2,128,128]{2,1,0:T(8,128)(2,1)S(1)}, bf16[2,128,128]{2,1,0:T(8,128)(2,1)S(1)}, u32[]{:S(2)}, u32[]{:S(2)}) collective-permute-start(bf16[2,128,128]{2,1,0:T(8,128)(2,1)S(1)} %get-tuple-element.48), channel_id=1, source_target_pairs={{0,4},{4,0},{8,12},{12,8},{16,20},{20,16},{24,28},{28,24},{1,5},{5... | collective-permute-start | bytes 196616 | tf_op jit(solution)/shard_map/ppermute | solution.py:297
  47.2 3.4 %copy-start.10 = (bf16[2,128,128]{2,1,0:T(8,128)(2,1)}, bf16[2,128,128]{2,1,0:T(8,128)(2,1)S(1)}, u32[]{:S(2)}) copy-start(bf16[2,128,128]{2,1,0:T(8,128)(2,1)S(1)} %collective-permute-done.3.given_ref) | copy-start | bytes 196612
  47.3 10.2 %all-to-all-start.1 = ((f32[8,8,256]{2,1,0:T(8,128)}), f32[8,8,256]{2,1,0:T(8,128)S(1)}, u32[]{:S(2)}, u32[]{:S(2)}) async-start(f32[8,8,256]{2,1,0:T(8,128)} %filter_lags.1), calls=%async_computation.1 | async-start | bytes 131072 | tf_op jit(solution)/shard_map/all_to_all | solution.py:536

commit v10 on v8

--- a/solution.py
+++ b/solution.py
@@ -14,10 +14,14 @@
 SUBLANES = 8
 GAP = 8
 VMEM_BYTES = 16 * 1024 * 1024
-PACK_VMEM_BYTES = 62 * 1024 * 1024
+FULL_VMEM_BYTES = 62 * 1024 * 1024
 F32 = jnp.float32
 BF16 = jnp.bfloat16
 LINK = jnp.bfloat16
+
+
+def takes(micros):
+    return pl.CostEstimate(flops=0, bytes_accessed=int(micros * 3.6e6), transcendentals=0)
 
 
 def product(first, second):
@@ -105,7 +109,8 @@
             pltpu.SemaphoreType.DMA((4, groups // 2)),
             pltpu.SemaphoreType.DMA((2, groups // 2)),
         ],
-        compiler_params=pltpu.CompilerParams(vmem_limit_bytes=PACK_VMEM_BYTES),
+        compiler_params=pltpu.CompilerParams(vmem_limit_bytes=FULL_VMEM_BYTES),
+        cost_estimate=takes(3.0),
         name="pack_signals",
     )(key_proj, value_proj, out_grad, query_proj)
     if owned % SUBLANES:
@@ -203,15 +208,13 @@
         + [jax.ShapeDtypeStruct((2, modes * tiles, LANES), F32)],
         scratch_shapes=[pltpu.VMEM(token_shape(tok_rows, tiles), F32)] * 2,
         compiler_params=pltpu.CompilerParams(vmem_limit_bytes=VMEM_BYTES),
-        cost_estimate=pl.CostEstimate(
-            flops=4 * modes * tok_rows * width, bytes_accessed=8 * tok_rows * width, transcendentals=0
-        ),
+        cost_estimate=takes(3.0),
         name="block_states",
     )(seq_index, query_proj, key_proj, value_proj, out_grad, coefs)
     return states, own
 
 
-def pair_kernel(seq_ref, coef_ref, own_ref, *refs):
+def pair_kernel(seq_ref, coef_ref, own_ref, _, *refs):
     state_refs, kept_ref, given_ref = refs[:-2], *refs[-2:]
     pairs = len(state_refs) + 1
     modes, tiles = coef_ref.shape[1:3]
@@ -238,22 +241,26 @@
         given_ref[1, rows] = jnp.where(second, decay * after + own, after).astype(LINK)
 
 
-def pair_states(seq_index, coefs, own, states):
+def pair_states(seq_index, coefs, own, lags, states):
     whole = pl.BlockSpec(memory_space=pltpu.VMEM)
     return pl.pallas_call(
         pair_kernel,
-        in_specs=[pl.BlockSpec(memory_space=pltpu.SMEM)] + [whole] * (2 + len(states)),
+        in_specs=[pl.BlockSpec(memory_space=pltpu.SMEM), whole, whole]
+        + [pl.BlockSpec(memory_space=pl.ANY)]
+        + [whole] * len(states),
         out_specs=[whole] * 2,
         out_shape=[
             jax.ShapeDtypeStruct(own.shape, F32),
             jax.ShapeDtypeStruct(own.shape, LINK),
         ],
-        compiler_params=pltpu.CompilerParams(vmem_limit_bytes=VMEM_BYTES),
+        compiler_params=pltpu.CompilerParams(vmem_limit_bytes=FULL_VMEM_BYTES),
+        cost_estimate=takes(0.1),
         name="pair_states",
-    )(seq_index, coefs, own, *states)
-
-
-def local_kernel(q_ref, k_ref, v_ref, o_ref, coef_ref, gain_ref, conv_ref, grad_ref):
+    )(seq_index, coefs, own, lags, *states)
+
+
+def local_kernel(q_ref, k_ref, v_ref, o_ref, coef_ref, gain_ref, part_ref):
+    conv_ref, grad_ref = part_ref.at[0], part_ref.at[1]
     tok_rows, width = k_ref.shape
     tiles = width // LANES
     spread_tokens(k_ref, v_ref, conv_ref)
@@ -275,11 +282,9 @@
     modes, tiles = coefs.shape[1:3]
     return pl.pallas_call(
         local_kernel,
-        out_shape=[jax.ShapeDtypeStruct(token_shape(tok_rows, tiles), F32)] * 2,
+        out_shape=jax.ShapeDtypeStruct((2, *token_shape(tok_rows, tiles)), F32),
         compiler_params=pltpu.CompilerParams(vmem_limit_bytes=VMEM_BYTES),
-        cost_estimate=pl.CostEstimate(
-            flops=8 * modes * tok_rows * width, bytes_accessed=8 * tok_rows * width, transcendentals=0
-        ),
+        cost_estimate=takes(6.5),
         name="local_parts",
     )(query_proj, key_proj, value_proj, out_grad, coefs, gain)
 
@@ -307,35 +312,61 @@
 
 
 def final_kernel(
-    q_ref, k_ref, v_ref, coef_ref, x_ref, g_ref, kept_ref, given_ref, *refs
+    coef_hbm, kept_hbm, given_hbm, part_hbm, q_hbm, v_hbm, k_hbm, layer_hbm, key_hbm, value_hbm,
+    coef_ref, kept_ref, given_ref, part_ref, q_ref, v_ref, k_ref, edge_ref,
+    layer_ref, key_ref, value_ref, in_sems, out_sems,
 ):
-    hbm_refs, (edge_ref, layer_ref, key_ref, value_ref, sems) = refs[:3], refs[3:]
     tok_rows, width = k_ref.shape
     tiles = width // LANES
     modes = coef_ref.shape[1]
+    arrivals = [
+        pltpu.make_async_copy(source, target, in_sems.at[i])
+        for i, (source, target) in enumerate(
+            (
+                (kept_hbm, kept_ref),
+                (given_hbm, given_ref),
+                (coef_hbm, coef_ref),
+                (part_hbm.at[0], part_ref.at[0]),
+                (q_hbm, q_ref),
+                (part_hbm.at[1], part_ref.at[1]),
+                (v_hbm, v_ref),
+                (k_hbm, k_ref),
+            )
+        )
+    ]
 
     def departure(i, tile):
         place = (slice(None), pl.ds(tile * LANES, LANES))
         return pltpu.make_async_copy(
-            (layer_ref, key_ref, value_ref)[i].at[place], hbm_refs[i].at[place], sems.at[i, tile]
+            (layer_ref, key_ref, value_ref)[i].at[place],
+            (layer_hbm, key_hbm, value_hbm)[i].at[place],
+            out_sems.at[i, tile],
         )
 
     def edge(side):
         total = kept_ref[side] + given_ref[side].astype(F32)
         return [total[m * tiles : (m + 1) * tiles] for m in range(modes)]
 
+    for copy in arrivals:
+        copy.start()
+    for copy in arrivals[:3]:
+        copy.wait()
     fill_edge(edge_ref, edge(0), coef_ref, tok_rows, tiles, 0, 1)
+    for copy in arrivals[3:5]:
+        copy.wait()
     for tile in range(tiles):
         cols = slice(tile * LANES, (tile + 1) * LANES)
         rows = tile_rows(tok_rows, tile)
-        long_conv = x_ref[rows, :] + edge_ref[rows, :]
+        long_conv = part_ref[0, rows, :] + edge_ref[rows, :]
         layer_ref[:, cols] = (q_ref[:, cols].astype(F32) * long_conv).astype(BF16)
         departure(0, tile).start()
     fill_edge(edge_ref, edge(1), coef_ref, tok_rows, tiles, tok_rows - 1, -1)
+    for copy in arrivals[5:]:
+        copy.wait()
     for tile in range(tiles):
         cols = slice(tile * LANES, (tile + 1) * LANES)
         rows = tile_rows(tok_rows, tile)
-        conv_grad = g_ref[rows, :] + edge_ref[rows, :]
+        conv_grad = part_ref[1, rows, :] + edge_ref[rows, :]
         key_ref[:, cols] = (conv_grad * v_ref[:, cols].astype(F32)).astype(BF16)
         departure(1, tile).start()
         value_ref[:, cols] = (conv_grad * k_ref[:, cols].astype(F32)).astype(BF16)
@@ -345,29 +376,28 @@
             departure(i, tile).wait()
 
 
-def final_outputs(signals, coefs, parts, kept, given):
-    tok_rows, width = signals[0].shape
-    modes, tiles = coefs.shape[1:3]
-    args = (*signals, coefs, *parts, kept, given)
-    whole = pl.BlockSpec(memory_space=pltpu.VMEM)
+def final_outputs(query_proj, key_proj, value_proj, coefs, kept, given, parts):
+    tok_rows, width = key_proj.shape
+    tiles = coefs.shape[2]
+    args = (coefs, kept, given, parts, query_proj, value_proj, key_proj)
+    away = pl.BlockSpec(memory_space=pl.ANY)
     return pl.pallas_call(
         final_kernel,
-        in_specs=[whole] * len(args),
-        out_specs=[pl.BlockSpec(memory_space=pl.ANY)] * 3,
+        in_specs=[away] * len(args),
+        out_specs=[away] * 3,
         out_shape=[jax.ShapeDtypeStruct((tok_rows, width), BF16)] * 3,
-        scratch_shapes=[pltpu.VMEM(token_shape(tok_rows, tiles), F32)]
+        scratch_shapes=[pltpu.VMEM(arg.shape, arg.dtype) for arg in args]
+        + [pltpu.VMEM(parts.shape[1:], F32)]
         + [pltpu.VMEM((tok_rows, width), BF16)] * 3
-        + [pltpu.SemaphoreType.DMA((3, tiles))],
-        compiler_params=pltpu.CompilerParams(vmem_limit_bytes=VMEM_BYTES),
-        cost_estimate=pl.CostEstimate(
-            flops=8 * modes * tok_rows * width, bytes_accessed=14 * tok_rows * width, transcendentals=0
-        ),
+        + [pltpu.SemaphoreType.DMA((len(args) + 1,)), pltpu.SemaphoreType.DMA((3, tiles))],
+        compiler_params=pltpu.CompilerParams(vmem_limit_bytes=FULL_VMEM_BYTES),
+        cost_estimate=takes(5.0),
         name="final_outputs",
     )(*args)
 
 
-def lag_kernel(shards, chans, groups, owned, scale, count, *refs):
-    in_refs, (out_ref, u_all, g_all, turned_all) = refs[:count], refs[-4:]
+def lag_kernel(shards, chans, groups, owned, scale, *refs):
+    in_refs, (out_ref, held, sems, u_all, g_all, turned_all) = refs[1:-6], refs[-6:]
     tok_rows = out_ref.shape[2]
     halves = tok_rows // LANES
     blocks = shards * halves
@@ -379,19 +409,32 @@
         def by_filter(row):
             return row % depth * owned + row // depth
 
+        def arrival(s):
+            place = pl.ds(s * chans, chans)
+            return pltpu.make_async_copy(in_refs[0].at[place], held.at[place], sems.at[s])
+
+        for s in range(shards):
+            arrival(s).start()
         order = one_hot(take, take, by_filter)
-        for which, kept in enumerate((u_all, g_all)):
-            rows = slice(which * groups * owned, (which + 1) * groups * owned)
-            for s in range(shards):
-                piece = in_refs[0][s * chans : (s + 1) * chans, rows, :].reshape(take, tok_rows)
+        for s in range(shards):
+            arrival(s).wait()
+            for which, kept in enumerate((u_all, g_all)):
+                rows = slice(which * groups * owned, (which + 1) * groups * owned)
+                piece = held[s * chans : (s + 1) * chans, rows, :].reshape(take, tok_rows)
                 piece = jnp.dot(order, piece, preferred_element_type=F32).astype(BF16)
                 piece = piece.reshape(owned, depth, tok_rows)
                 for h in range(halves):
                     first = (s * halves + h) * depth
                     kept[:, first : first + depth, :] = piece[:, :, h * LANES : (h + 1) * LANES]
     else:
-        u_all[...] = in_refs[0][...]
-        g_all[:, :full, :] = in_refs[1][...]
+        copies = [
+            pltpu.make_async_copy(in_refs[0], u_all, sems.at[0]),
+            pltpu.make_async_copy(in_refs[1], g_all.at[:, pl.ds(0, full), :], sems.at[1]),
+        ]
+        for copy in copies:
+            copy.start()
+        for copy in copies:
+            copy.wait()
     g_all[:, full:, :] = jnp.zeros((owned, g_all.shape[1] - full, LANES), BF16)
     mirror = one_hot(LANES, LANES, lambda row: LANES - 1 - row)
     row = lax.broadcasted_iota(jnp.int32, (LANES, LANES), 0)
@@ -444,7 +487,7 @@
     lax.fori_loop(0, owned, one_filter, 0, unroll=min(owned, 4))
 
 
-def filter_lags(received, held, shards, chans, owned, scale):
+def filter_lags(received, parts, shards, chans, owned, scale):
     tok_rows = received.shape[2]
     groups = received.shape[1] // (2 * owned)
     halves = tok_rows // LANES
@@ -455,23 +498,23 @@
         split = received.reshape(shards, chans, 2, groups, owned, halves, LANES)
         split = split.transpose(2, 4, 0, 5, 1, 3, 6).reshape(2, owned, full, LANES)
         args = (split[0], split[1])
+    away = pl.BlockSpec(memory_space=pl.ANY)
     return pl.pallas_call(
-        functools.partial(lag_kernel, shards, chans, groups, owned, scale, len(args)),
-        in_specs=[pl.BlockSpec(memory_space=pltpu.VMEM)] * len(args)
-        + [pl.BlockSpec(memory_space=pl.ANY)] * len(held),
+        functools.partial(lag_kernel, shards, chans, groups, owned, scale),
+        in_specs=[away] * (len(args) + 1),
         out_specs=pl.BlockSpec(memory_space=pltpu.VMEM),
         out_shape=jax.ShapeDtypeStruct((shards, owned, tok_rows), F32),
         scratch_shapes=[
+            pltpu.VMEM(received.shape if len(args) == 1 else (SUBLANES, LANES), BF16),
+            pltpu.SemaphoreType.DMA((max(shards, 2),)),
             pltpu.VMEM((owned, full, LANES), BF16),
             pltpu.VMEM((owned, 2 * full + depth, LANES), BF16),
             pltpu.VMEM((owned, LANES, full), BF16),
         ],
         compiler_params=pltpu.CompilerParams(vmem_limit_bytes=VMEM_BYTES),
-        cost_estimate=pl.CostEstimate(
-            flops=4 * owned * LANES * full * full, bytes_accessed=8 * owned * full * LANES, transcendentals=0
-        ),
+        cost_estimate=takes(0.1),
         name="filter_lags",
-    )(*args, *held)
+    )(parts, *args)
 
 
 def per_device(query_proj, key_proj, value_proj, out_grad, residues, decay_rate, skip_gain):
@@ -505,17 +548,14 @@
     *states, coefs = lax.optimization_barrier((*states, coefs))
     states = [along_column(state, pairs, 1 + i) for i, state in enumerate(states)]
     parts = local_parts(*signals, coefs, skip_gain[None, :])
-    kept, given = pair_states(seq_index, coefs, own, states)
-    received, kept, given = lax.optimization_barrier((received, kept, given))
-    given = inside_pair(given, pairs)
-
     scale = 1.0 / math.sqrt(length * (CHANNELS // FILTERS))
     lags = filter_lags(received, parts, shards, chans, owned, scale)
-    lags, given = lax.optimization_barrier((lags, given))
+    kept, given = pair_states(seq_index, coefs, own, lags, states)
+    given = inside_pair(given, pairs)
     lags = lax.all_to_all(lags, "seq", split_axis=0, concat_axis=0, tiled=True)
     filter_grad = lags.reshape(shards * owned, tok_rows).T
     layer_out, key_grad, value_grad = final_outputs(
-        signals[:3], coefs, parts, kept, given
+        *signals[:3], coefs, kept, given, parts
     )
     return (layer_out, key_grad, value_grad, filter_grad)
 

time: 65 us -> 70.2 us (1.080)
  Pallas kernels: 20.2 us -> 25.3 us
  local copies, waits for them, and re-layouts: 5.04 us -> 4 us
    ppermute x3, waiting for transfers between devices: 19.8 us -> 2.51 us  [along_column(): return lax.ppermute(state, 'seq', route)]
    all_to_all x1, waiting for transfers between devices: 0.01 us -> 15.8 us  [per_device(): lax.all_to_all(send, ('seq', 'chan'), split_axis=0, concat_axis=0, tiled=...]
    ppermute x1, waiting for transfers between devices: 0.01 us -> 3.07 us  [inside_pair(): return lax.ppermute(state, 'seq', [(i, i ^ 1) for i in range(2 * pairs)])]
    pallas_call x1, Pallas kernels: 4.02 us -> 6.04 us  [filter_lags(): pl.pallas_call(functools.partial(lag_kernel, shards, chans, groups, owned...]
    pallas_call x1, Pallas kernels: 0.1 us -> 1.77 us  [pair_states(): pl.pallas_call(pair_kernel, in_specs=[pl.BlockSpec(memory_space=pltpu.SME...]
    pallas_call x2, Pallas kernels: 10.2 us -> 11.4 us  [the longest x1 6.46 us: local_parts(): pl.pallas_call(local_kernel, out_shape=jax.ShapeDtypeStruct((2, *token_sh...]
    unnamed x29 -> x33, local copies, waits for them, and re-layouts: 4.96 us -> 3.92 us
    all_to_all x1, waiting for transfers between devices: 0.94 us -> 0.01 us  [per_device(): lags = lax.all_to_all(lags, 'seq', split_axis=0, concat_axis=0, tiled=True)]
  transfers between devices with their start and end apart: 6 -> 6, of which waited for: 3 -> 5; matrix products, arithmetic and copies ran while one was open for 0% -> 0% of each run, Pallas kernels for 27% -> 23%
where the time goes in v10:
time: 70.2 us; the launch traced here: 69.9 us
  Pallas kernels  25.3 us (36%)
  waiting for transfers between devices  21.4 us (30%)
  starting transfers between devices  18.4 us (26%)
  local copies, waits for them, and re-layouts  4 us (6%)
  between operations  0.88 us (1%)
    all_to_all x1, waiting for transfers between devices, per_device(): lax.all_to_all(send, ('seq', 'chan'), split_axis=0, concat_axis=0, tiled=...  15.8 us
    all_to_all x1, starting transfers between devices, per_device(): lax.all_to_all(send, ('seq', 'chan'), split_axis=0, concat_axis=0, tiled=...  7.43 us
    pallas_call x1, Pallas kernels, local_parts(): pl.pallas_call(local_kernel, out_shape=jax.ShapeDtypeStruct((2, *token_sh...  6.46 us
    pallas_call x1, Pallas kernels, filter_lags(): pl.pallas_call(functools.partial(lag_kernel, shards, chans, groups, owned...  6.04 us
    ppermute x3, starting transfers between devices, along_column(): return lax.ppermute(state, 'seq', route)  5.85 us
    pallas_call x1, Pallas kernels, final_outputs(): pl.pallas_call(final_kernel, in_specs=[away] * len(args), out_specs=[away...  4.93 us
    unnamed x33, local copies, waits for them, and re-layouts  3.92 us
    all_to_all x1, starting transfers between devices, per_device(): lags = lax.all_to_all(lags, 'seq', split_axis=0, concat_axis=0, tiled=True)  3.68 us
  transfers between devices with their start and end apart: 6, of which 5 were waited for; matrix products, arithmetic and copies ran while one was open for 0% of the time, Pallas kernels for 23%

profile of v10, /device:TPU:0, one launch (start us, length us, event | category | flops | bytes accessed | tf_op | source)
XLA Modules:
  0.0 69.9 jit_solution(10616855409091975433)
XLA Ops:
  0.6 0.0 copy-start.3
  0.6 0.0 copy-start.2
  0.7 0.0 copy-start.1
  0.7 0.0 copy-start.14
  0.7 0.0 copy-start.15
  0.7 3.1 %pack_signals.1 = bf16[32,64,256]{2,1,0:T(8,128)(2,1)} custom-call(bf16[256,1024]{1,0:T(8,128)(2,1)} %k_hbm, bf16[256,1024]{1,0:T(8,128)(2,1)} %v_hbm, bf16[256,1024]{1,0:T(8,128)(2,1)} %o_ref.1, bf16[256,1024]{1,0:T(8,128)(2,1)} %q_hbm), custom_call_target="tpu_custom_call" | custom-call | bytes 10800000 | tf_op jit(solution)/shard_map/pack_signals/pallas_call | solution.py:101
  3.8 0.0 copy-start.6
  3.8 0.0 copy-start.9
  3.8 7.4 %all-to-all-start = ((bf16[32,64,256]{2,1,0:T(8,128)(2,1)}), bf16[32,64,256]{2,1,0:T(8,128)(2,1)}, u32[]{:S(2)}, u32[]{:S(2)}) async-start(bf16[32,64,256]{2,1,0:T(8,128)(2,1)} %pack_signals.1), calls=%async_computation | async-start | bytes 2097152 | tf_op jit(solution)/shard_map/all_to_all | solution.py:533
  11.2 0.0 copy-done.14
  11.2 0.0 copy-done.15
  11.3 0.0 copy-start.4
  11.3 0.0 copy-start.7
  11.3 0.1 broadcast_in_dim.11
  11.4 0.0 copy-start.5
  11.4 0.0 copy-done.3
  11.4 0.0 copy-done.2
  11.4 0.0 copy-done.1
  11.4 0.0 copy-done.6
  11.4 3.0 %block_states.1 = (bf16[128,128]{1,0:T(8,128)(2,1)S(1)}, bf16[128,128]{1,0:T(8,128)(2,1)S(1)}, bf16[128,128]{1,0:T(8,128)(2,1)S(1)}, f32[2,128,128]{2,1,0:T(8,128)S(1)}) custom-call(s32[1]{0:T(128)} %bitcast.seq_ref, bf16[256,1024]{1,0:T(8,128)(2,1)S(1)} %copy-done.1, bf16[256,1024]{1,0:T(8,128)(2,1)S(1)} %copy-done.2, bf16[256,1024]{1,0:T(8,128)(2,1)S(1)} %copy-done.3, ...), custom_call_target="tpu_custom_call" | custom-call | bytes 10800000 | tf_op jit(solution)/shard_map/block_states/pallas_call | solution.py:203
  14.5 0.0 copy-start.8
  14.5 0.6 copy-done.8
  15.1 0.0 copy-done.9
  15.1 0.0 copy-done.4
  15.1 0.0 copy-done.7
  15.1 6.5 %local_parts.1.refs_0_.part_hbm = f32[2,2112,128]{2,1,0:T(8,128)S(1)} custom-call(bf16[256,1024]{1,0:T(8,128)(2,1)S(1)} %copy-done.1, bf16[256,1024]{1,0:T(8,128)(2,1)S(1)} %copy-done.2, bf16[256,1024]{1,0:T(8,128)(2,1)S(1)} %copy-done.4, bf16[256,1024]{1,0:T(8,128)(2,1)S(1)} %copy-done.7, f32[3,16,8,128]{3,2,1,0:T(8,128)S(1)} %bitcast.15, ...), custom_call_target="tpu_custom_call" | custom-call | bytes 23400000 | tf_op jit(solution)/shard_map/local_parts/pallas_call | solution.py:283
  21.6 0.0 copy-done.5
  21.6 15.8 %all-to-all-done.refs_1_ = bf16[32,64,256]{2,1,0:T(8,128)(2,1)} async-done(((bf16[32,64,256]{2,1,0:T(8,128)(2,1)}), bf16[32,64,256]{2,1,0:T(8,128)(2,1)}, u32[]{:S(2)}, u32[]{:S(2)}) %all-to-all-start) | async-done | bytes 1048608 | tf_op jit(solution)/shard_map/all_to_all | solution.py:533
  37.4 6.0 %filter_lags.1._ = f32[8,8,256]{2,1,0:T(8,128)} custom-call(f32[2,2112,128]{2,1,0:T(8,128)S(1)} %local_parts.1.refs_0_.part_hbm, bf16[32,64,256]{2,1,0:T(8,128)(2,1)} %all-to-all-done.refs_1_), custom_call_target="tpu_custom_call" | custom-call | bytes 360000 | tf_op jit(solution)/shard_map/filter_lags/pallas_call | solution.py:502
  43.5 0.0 copy-start
  43.5 1.4 %copy-done = f32[2,2112,128]{2,1,0:T(8,128)} copy-done((f32[2,2112,128]{2,1,0:T(8,128)}, f32[2,2112,128]{2,1,0:T(8,128)S(1)}, u32[]{:S(2)}) %copy-start) | copy-done | bytes 2162712
  44.8 3.7 %all-to-all-start.1 = ((f32[8,8,256]{2,1,0:T(8,128)}), f32[8,8,256]{2,1,0:T(8,128)S(1)}, u32[]{:S(2)}, u32[]{:S(2)}) async-start(f32[8,8,256]{2,1,0:T(8,128)} %filter_lags.1._), calls=%async_computation.1 | async-start | bytes 131072 | tf_op jit(solution)/shard_map/all_to_all | solution.py:555
  48.5 2.0 %collective-permute-start = (bf16[128,128]{1,0:T(8,128)(2,1)S(1)}, bf16[128,128]{1,0:T(8,128)(2,1)S(1)}, u32[]{:S(2)}, u32[]{:S(2)}) collective-permute-start(bf16[128,128]{1,0:T(8,128)(2,1)S(1)} %get-tuple-element.36), channel_id=1, source_target_pairs={{0,8},{4,12},{8,16},{12,20},{16,24},{20,28},{24,0},{28,4},{1,9},{5... | collective-permute-start | bytes 98312 | tf_op jit(solution)/shard_map/ppermute | solution.py:294
  50.5 2.4 %collective-permute-start.1 = (bf16[128,128]{1,0:T(8,128)(2,1)S(1)}, bf16[128,128]{1,0:T(8,128)(2,1)S(1)}, u32[]{:S(2)}, u32[]{:S(2)}) collective-permute-start(bf16[128,128]{1,0:T(8,128)(2,1)S(1)} %get-tuple-element.37), channel_id=1, source_target_pairs={{0,16},{4,20},{8,24},{12,28},{16,0},{20,4},{24,8},{28,12},{1,17},{... | collective-permute-start | bytes 98312 | tf_op jit(solution)/shard_map/ppermute | solution.py:294
  52.9 1.5 %collective-permute-start.2 = (bf16[128,128]{1,0:T(8,128)(2,1)S(1)}, bf16[128,128]{1,0:T(8,128)(2,1)S(1)}, u32[]{:S(2)}, u32[]{:S(2)}) collective-permute-start(bf16[128,128]{1,0:T(8,128)(2,1)S(1)} %get-tuple-element.38), channel_id=1, source_target_pairs={{0,24},{4,28},{8,0},{12,4},{16,8},{20,12},{24,16},{28,20},{1,25},{... | collective-permute-start | bytes 98312 | tf_op jit(solution)/shard_map/ppermute | solution.py:294
  54.4 1.3 %collective-permute-done.refs_0_ = bf16[128,128]{1,0:T(8,128)(2,1)S(1)} collective-permute-done((bf16[128,128]{1,0:T(8,128)(2,1)S(1)}, bf16[128,128]{1,0:T(8,128)(2,1)S(1)}, u32[]{:S(2)}, u32[]{:S(2)}) %collective-permute-start) | collective-permute-done | bytes 32800 | tf_op jit(solution)/shard_map/ppermute | solution.py:294
  55.7 0.0 copy-start.11
  55.7 0.9 %collective-permute-done.1.refs_1_ = bf16[128,128]{1,0:T(8,128)(2,1)S(1)} collective-permute-done((bf16[128,128]{1,0:T(8,128)(2,1)S(1)}, bf16[128,128]{1,0:T(8,128)(2,1)S(1)}, u32[]{:S(2)}, u32[]{:S(2)}) %collective-permute-start.1) | collective-permute-done | bytes 32800 | tf_op jit(solution)/shard_map/ppermute | solution.py:294
  56.6 0.0 copy-start.12
  56.6 0.3 collective-permute-done.2.refs_2_
  56.9 0.0 copy-start.13
  56.9 0.0 copy-done.11
  56.9 0.3 copy-done.12
  57.2 0.3 copy-done.13
  57.5 1.8 %pair_states.1 = (f32[2,128,128]{2,1,0:T(8,128)}, bf16[2,128,128]{2,1,0:T(8,128)(2,1)}) custom-call(s32[1]{0:T(128)} %bitcast.seq_ref, f32[3,16,8,128]{3,2,1,0:T(8,128)} %bitcast.16, f32[2,128,128]{2,1,0:T(8,128)} %copy-done.8, f32[8,8,256]{2,1,0:T(8,128)} %filter_lags.1._, bf16[128,128]{1,0:T(8,128)(2,1)} %copy-done.11, bf16[128,128]{1,0:T(8,128)(2,1)} %copy-done.12, ...), custom_call_target="tpu_custom_call" | custom-call | bytes 360000 | tf_op jit(solution)/shard_map/pair_states/pallas_call | solution.py:246
  59.3 1.4 %collective-permute-start.3 = (bf16[2,128,128]{2,1,0:T(8,128)(2,1)}, bf16[2,128,128]{2,1,0:T(8,128)(2,1)S(1)}, u32[]{:S(2)}, u32[]{:S(2)}) collective-permute-start(bf16[2,128,128]{2,1,0:T(8,128)(2,1)} %get-tuple-element.40), channel_id=1, source_target_pairs={{0,4},{4,0},{8,12},{12,8},{16,20},{20,16},{24,28},{28,24},{1,5},{5... | collective-permute-start | bytes 196616 | tf_op jit(solution)/shard_map/ppermute | solution.py:298
  60.7 3.1 %collective-permute-done.3.given_hbm = bf16[2,128,128]{2,1,0:T(8,128)(2,1)S(1)} collective-permute-done((bf16[2,128,128]{2,1,0:T(8,128)(2,1)}, bf16[2,128,128]{2,1,0:T(8,128)(2,1)S(1)}, u32[]{:S(2)}, u32[]{:S(2)}) %collective-permute-start.3) | collective-permute-done | bytes 65568 | tf_op jit(solution)/shard_map/ppermute | solution.py:298
  63.7 0.0 copy-start.10
  63.7 0.6 copy-done.10
  64.3 4.9 %final_outputs.1 = (bf16[256,1024]{1,0:T(8,128)(2,1)}, bf16[256,1024]{1,0:T(8,128)(2,1)}, bf16[256,1024]{1,0:T(8,128)(2,1)}) custom-call(f32[3,16,8,128]{3,2,1,0:T(8,128)} %bitcast.17, f32[2,128,128]{2,1,0:T(8,128)} %get-tuple-element.39.kept_hbm, bf16[2,128,128]{2,1,0:T(8,128)(2,1)} %copy-done.10, f32[2,2112,128]{2,1,0:T(8,128)} %copy-done, ...), custom_call_target="tpu_custom_call" | custom-call | bytes 18000000 | tf_op jit(solution)/shard_map/final_outputs/pallas_call | solution.py:384
  69.3 0.0 all-to-all-done.1
  69.3 0.6 copy.12
  (3 shorter events, 0.1 us)
Async XLA Ops:
  0.6 10.8 %copy-start.3 = (bf16[256,1024]{1,0:T(8,128)(2,1)S(1)}, bf16[256,1024]{1,0:T(8,128)(2,1)}, u32[]{:S(2)}) copy-start(bf16[256,1024]{1,0:T(8,128)(2,1)} %v_hbm) | copy-start | bytes 1572868
  0.6 10.8 %copy-start.2 = (bf16[256,1024]{1,0:T(8,128)(2,1)S(1)}, bf16[256,1024]{1,0:T(8,128)(2,1)}, u32[]{:S(2)}) copy-start(bf16[256,1024]{1,0:T(8,128)(2,1)} %k_hbm) | copy-start | bytes 1572868
  0.7 10.8 %copy-start.1 = (bf16[256,1024]{1,0:T(8,128)(2,1)S(1)}, bf16[256,1024]{1,0:T(8,128)(2,1)}, u32[]{:S(2)}) copy-start(bf16[256,1024]{1,0:T(8,128)(2,1)} %q_hbm) | copy-start | bytes 1572868
  0.7 10.6 %copy-start.14 = (f32[256,16]{0,1:T(8,128)S(1)}, f32[256,16]{0,1:T(8,128)}, u32[]{:S(2)}) copy-start(f32[256,16]{0,1:T(8,128)} %param.12) | copy-start | bytes 49156
  0.7 10.6 %copy-start.15 = (f32[256,16]{0,1:T(8,128)S(1)}, f32[256,16]{0,1:T(8,128)}, u32[]{:S(2)}) copy-start(f32[256,16]{0,1:T(8,128)} %param.11) | copy-start | bytes 49156
  3.8 7.7 %copy-start.6 = (bf16[256,1024]{1,0:T(8,128)(2,1)S(1)}, bf16[256,1024]{1,0:T(8,128)(2,1)}, u32[]{:S(2)}) copy-start(bf16[256,1024]{1,0:T(8,128)(2,1)} %o_ref.1) | copy-start | bytes 1572868
  3.8 11.4 %copy-start.9 = (f32[1024]{0:T(1024)S(1)}, f32[1024]{0:T(1024)}, u32[]{:S(2)}) copy-start(f32[1024]{0:T(1024)} %param.13) | copy-start | bytes 12292
  3.8 33.7 %all-to-all-start = ((bf16[32,64,256]{2,1,0:T(8,128)(2,1)}), bf16[32,64,256]{2,1,0:T(8,128)(2,1)}, u32[]{:S(2)}, u32[]{:S(2)}) async-start(bf16[32,64,256]{2,1,0:T(8,128)(2,1)} %pack_signals.1), calls=%async_computation | async-start | bytes 2097152 | tf_op jit(solution)/shard_map/all_to_all | solution.py:533
  11.3 3.8 %copy-start.4 = (bf16[256,1024]{1,0:T(8,128)(2,1)S(1)}, bf16[256,1024]{1,0:T(8,128)(2,1)}, u32[]{:S(2)}) copy-start(bf16[256,1024]{1,0:T(8,128)(2,1)} %v_hbm) | copy-start | bytes 1572868
  11.3 3.8 %copy-start.7 = (bf16[256,1024]{1,0:T(8,128)(2,1)S(1)}, bf16[256,1024]{1,0:T(8,128)(2,1)}, u32[]{:S(2)}) copy-start(bf16[256,1024]{1,0:T(8,128)(2,1)} %o_ref.1) | copy-start | bytes 1572868
  11.4 10.2 %copy-start.5 = (f32[3,16,4,2,128]{4,3,2,1,0:T(2,128)}, f32[3,16,4,2,128]{4,3,2,1,0:T(2,128)S(1)}, u32[]{:S(2)}) copy-start(f32[3,16,4,2,128]{4,3,2,1,0:T(2,128)S(1)} %broadcast_in_dim.11) | copy-start | bytes 589828
  14.5 0.7 copy-start.8
  43.5 1.4 %copy-start = (f32[2,2112,128]{2,1,0:T(8,128)}, f32[2,2112,128]{2,1,0:T(8,128)S(1)}, u32[]{:S(2)}) copy-start(f32[2,2112,128]{2,1,0:T(8,128)S(1)} %local_parts.1.refs_0_.part_hbm) | copy-start | bytes 6488068
  44.8 24.4 %all-to-all-start.1 = ((f32[8,8,256]{2,1,0:T(8,128)}), f32[8,8,256]{2,1,0:T(8,128)S(1)}, u32[]{:S(2)}, u32[]{:S(2)}) async-start(f32[8,8,256]{2,1,0:T(8,128)} %filter_lags.1._), calls=%async_computation.1 | async-start | bytes 131072 | tf_op jit(solution)/shard_map/all_to_all | solution.py:555
  48.5 7.2 %collective-permute-start = (bf16[128,128]{1,0:T(8,128)(2,1)S(1)}, bf16[128,128]{1,0:T(8,128)(2,1)S(1)}, u32[]{:S(2)}, u32[]{:S(2)}) collective-permute-start(bf16[128,128]{1,0:T(8,128)(2,1)S(1)} %get-tuple-element.36), channel_id=1, source_target_pairs={{0,8},{4,12},{8,16},{12,20},{16,24},{20,28},{24,0},{28,4},{1,9},{5... | collective-permute-start | bytes 98312 | tf_op jit(solution)/shard_map/ppermute | solution.py:294
  50.5 6.0 %collective-permute-start.1 = (bf16[128,128]{1,0:T(8,128)(2,1)S(1)}, bf16[128,128]{1,0:T(8,128)(2,1)S(1)}, u32[]{:S(2)}, u32[]{:S(2)}) collective-permute-start(bf16[128,128]{1,0:T(8,128)(2,1)S(1)} %get-tuple-element.37), channel_id=1, source_target_pairs={{0,16},{4,20},{8,24},{12,28},{16,0},{20,4},{24,8},{28,12},{1,17},{... | collective-permute-start | bytes 98312 | tf_op jit(solution)/shard_map/ppermute | solution.py:294
  52.9 4.0 %collective-permute-start.2 = (bf16[128,128]{1,0:T(8,128)(2,1)S(1)}, bf16[128,128]{1,0:T(8,128)(2,1)S(1)}, u32[]{:S(2)}, u32[]{:S(2)}) collective-permute-start(bf16[128,128]{1,0:T(8,128)(2,1)S(1)} %get-tuple-element.38), channel_id=1, source_target_pairs={{0,24},{4,28},{8,0},{12,4},{16,8},{20,12},{24,16},{28,20},{1,25},{... | collective-permute-start | bytes 98312 | tf_op jit(solution)/shard_map/ppermute | solution.py:294
  55.7 1.2 %copy-start.11 = (bf16[128,128]{1,0:T(8,128)(2,1)}, bf16[128,128]{1,0:T(8,128)(2,1)S(1)}, u32[]{:S(2)}) copy-start(bf16[128,128]{1,0:T(8,128)(2,1)S(1)} %collective-permute-done.refs_0_) | copy-start | bytes 98308
  56.6 0.6 copy-start.12
  56.9 0.6 copy-start.13
  59.3 4.5 %collective-permute-start.3 = (bf16[2,128,128]{2,1,0:T(8,128)(2,1)}, bf16[2,128,128]{2,1,0:T(8,128)(2,1)S(1)}, u32[]{:S(2)}, u32[]{:S(2)}) collective-permute-start(bf16[2,128,128]{2,1,0:T(8,128)(2,1)} %get-tuple-element.40), channel_id=1, source_target_pairs={{0,4},{4,0},{8,12},{12,8},{16,20},{20,16},{24,28},{28,24},{1,5},{5... | collective-permute-start | bytes 196616 | tf_op jit(solution)/shard_map/ppermute | solution.py:298
  63.7 0.6 copy-start.10

commit v11 on v8

--- a/solution.py
+++ b/solution.py
@@ -18,6 +18,10 @@
 F32 = jnp.float32
 BF16 = jnp.bfloat16
 LINK = jnp.bfloat16
+
+
+def takes(micros):
+    return pl.CostEstimate(flops=0, bytes_accessed=int(micros * 3.6e6), transcendentals=0)
 
 
 def product(first, second):
@@ -106,6 +110,7 @@
             pltpu.SemaphoreType.DMA((2, groups // 2)),
         ],
         compiler_params=pltpu.CompilerParams(vmem_limit_bytes=PACK_VMEM_BYTES),
+        cost_estimate=takes(3.0),
         name="pack_signals",
     )(key_proj, value_proj, out_grad, query_proj)
     if owned % SUBLANES:
@@ -203,16 +208,14 @@
         + [jax.ShapeDtypeStruct((2, modes * tiles, LANES), F32)],
         scratch_shapes=[pltpu.VMEM(token_shape(tok_rows, tiles), F32)] * 2,
         compiler_params=pltpu.CompilerParams(vmem_limit_bytes=VMEM_BYTES),
-        cost_estimate=pl.CostEstimate(
-            flops=4 * modes * tok_rows * width, bytes_accessed=8 * tok_rows * width, transcendentals=0
-        ),
+        cost_estimate=takes(3.0),
         name="block_states",
     )(seq_index, query_proj, key_proj, value_proj, out_grad, coefs)
     return states, own
 
 
 def pair_kernel(seq_ref, coef_ref, own_ref, *refs):
-    state_refs, kept_ref, given_ref = refs[:-2], *refs[-2:]
+    state_refs, kept_ref, given_ref = refs[2:-2], *refs[-2:]
     pairs = len(state_refs) + 1
     modes, tiles = coef_ref.shape[1:3]
     pair = seq_ref[0] // 2
@@ -238,48 +241,52 @@
         given_ref[1, rows] = jnp.where(second, decay * after + own, after).astype(LINK)
 
 
-def pair_states(seq_index, coefs, own, states):
+def pair_states(seq_index, coefs, own, parts, states):
     whole = pl.BlockSpec(memory_space=pltpu.VMEM)
     return pl.pallas_call(
         pair_kernel,
-        in_specs=[pl.BlockSpec(memory_space=pltpu.SMEM)] + [whole] * (2 + len(states)),
+        in_specs=[pl.BlockSpec(memory_space=pltpu.SMEM), whole, whole]
+        + [pl.BlockSpec(memory_space=pl.ANY)] * len(parts)
+        + [whole] * len(states),
         out_specs=[whole] * 2,
         out_shape=[
             jax.ShapeDtypeStruct(own.shape, F32),
             jax.ShapeDtypeStruct(own.shape, LINK),
         ],
         compiler_params=pltpu.CompilerParams(vmem_limit_bytes=VMEM_BYTES),
+        cost_estimate=takes(0.1),
         name="pair_states",
-    )(seq_index, coefs, own, *states)
-
-
-def local_kernel(q_ref, k_ref, v_ref, o_ref, coef_ref, gain_ref, conv_ref, grad_ref):
+    )(seq_index, coefs, own, *parts, *states)
+
+
+def local_kernel(
+    q_ref, k_ref, v_ref, o_ref, coef_ref, gain_ref, conv_ref, grad_ref, x_ref, g_ref
+):
     tok_rows, width = k_ref.shape
     tiles = width // LANES
-    spread_tokens(k_ref, v_ref, conv_ref)
-    spread_tokens(o_ref, q_ref, grad_ref)
-    walk_tokens(conv_ref, coef_ref, tok_rows, tiles, 0, 1)
-    walk_tokens(grad_ref, coef_ref, tok_rows, tiles, tok_rows - 1, -1)
+    spread_tokens(k_ref, v_ref, x_ref)
+    spread_tokens(o_ref, q_ref, g_ref)
+    walk_tokens(x_ref, coef_ref, tok_rows, tiles, 0, 1)
+    walk_tokens(g_ref, coef_ref, tok_rows, tiles, tok_rows - 1, -1)
     for tile in range(tiles):
         cols = slice(tile * LANES, (tile + 1) * LANES)
         rows = tile_rows(tok_rows, tile)
         gain = gain_ref[:, cols]
         conv_in = product(k_ref[:, cols], v_ref[:, cols]).astype(F32)
-        conv_ref[rows, :] = conv_ref[rows, :] + gain * conv_in
+        conv_ref[:, cols] = (x_ref[rows, :] + gain * conv_in).astype(BF16)
         mid_grad = product(o_ref[:, cols], q_ref[:, cols]).astype(F32)
-        grad_ref[rows, :] = grad_ref[rows, :] + gain * mid_grad
+        grad_ref[:, cols] = (g_ref[rows, :] + gain * mid_grad).astype(BF16)
 
 
 def local_parts(query_proj, key_proj, value_proj, out_grad, coefs, gain):
     tok_rows, width = key_proj.shape
-    modes, tiles = coefs.shape[1:3]
+    tiles = coefs.shape[2]
     return pl.pallas_call(
         local_kernel,
-        out_shape=[jax.ShapeDtypeStruct(token_shape(tok_rows, tiles), F32)] * 2,
+        out_shape=[jax.ShapeDtypeStruct((tok_rows, width), BF16)] * 2,
+        scratch_shapes=[pltpu.VMEM(token_shape(tok_rows, tiles), F32)] * 2,
         compiler_params=pltpu.CompilerParams(vmem_limit_bytes=VMEM_BYTES),
-        cost_estimate=pl.CostEstimate(
-            flops=8 * modes * tok_rows * width, bytes_accessed=8 * tok_rows * width, transcendentals=0
-        ),
+        cost_estimate=takes(6.5),
         name="local_parts",
     )(query_proj, key_proj, value_proj, out_grad, coefs, gain)
 
@@ -307,9 +314,9 @@
 
 
 def final_kernel(
-    q_ref, k_ref, v_ref, coef_ref, x_ref, g_ref, kept_ref, given_ref, *refs
+    q_ref, k_ref, v_ref, conv_ref, grad_ref, coef_ref, kept_ref, given_ref,
+    layer_hbm, key_hbm, value_hbm, edge_ref, layer_ref, key_ref, value_ref, sems,
 ):
-    hbm_refs, (edge_ref, layer_ref, key_ref, value_ref, sems) = refs[:3], refs[3:]
     tok_rows, width = k_ref.shape
     tiles = width // LANES
     modes = coef_ref.shape[1]
@@ -317,7 +324,9 @@
     def departure(i, tile):
         place = (slice(None), pl.ds(tile * LANES, LANES))
         return pltpu.make_async_copy(
-            (layer_ref, key_ref, value_ref)[i].at[place], hbm_refs[i].at[place], sems.at[i, tile]
+            (layer_ref, key_ref, value_ref)[i].at[place],
+            (layer_hbm, key_hbm, value_hbm)[i].at[place],
+            sems.at[i, tile],
         )
 
     def edge(side):
@@ -327,15 +336,13 @@
     fill_edge(edge_ref, edge(0), coef_ref, tok_rows, tiles, 0, 1)
     for tile in range(tiles):
         cols = slice(tile * LANES, (tile + 1) * LANES)
-        rows = tile_rows(tok_rows, tile)
-        long_conv = x_ref[rows, :] + edge_ref[rows, :]
+        long_conv = conv_ref[:, cols].astype(F32) + edge_ref[tile_rows(tok_rows, tile), :]
         layer_ref[:, cols] = (q_ref[:, cols].astype(F32) * long_conv).astype(BF16)
         departure(0, tile).start()
     fill_edge(edge_ref, edge(1), coef_ref, tok_rows, tiles, tok_rows - 1, -1)
     for tile in range(tiles):
         cols = slice(tile * LANES, (tile + 1) * LANES)
-        rows = tile_rows(tok_rows, tile)
-        conv_grad = g_ref[rows, :] + edge_ref[rows, :]
+        conv_grad = grad_ref[:, cols].astype(F32) + edge_ref[tile_rows(tok_rows, tile), :]
         key_ref[:, cols] = (conv_grad * v_ref[:, cols].astype(F32)).astype(BF16)
         departure(1, tile).start()
         value_ref[:, cols] = (conv_grad * k_ref[:, cols].astype(F32)).astype(BF16)
@@ -345,29 +352,26 @@
             departure(i, tile).wait()
 
 
-def final_outputs(signals, coefs, parts, kept, given):
+def final_outputs(signals, parts, coefs, kept, given):
     tok_rows, width = signals[0].shape
-    modes, tiles = coefs.shape[1:3]
-    args = (*signals, coefs, *parts, kept, given)
-    whole = pl.BlockSpec(memory_space=pltpu.VMEM)
+    tiles = coefs.shape[2]
+    args = (*signals, *parts, coefs, kept, given)
     return pl.pallas_call(
         final_kernel,
-        in_specs=[whole] * len(args),
+        in_specs=[pl.BlockSpec(memory_space=pltpu.VMEM)] * len(args),
         out_specs=[pl.BlockSpec(memory_space=pl.ANY)] * 3,
         out_shape=[jax.ShapeDtypeStruct((tok_rows, width), BF16)] * 3,
         scratch_shapes=[pltpu.VMEM(token_shape(tok_rows, tiles), F32)]
         + [pltpu.VMEM((tok_rows, width), BF16)] * 3
         + [pltpu.SemaphoreType.DMA((3, tiles))],
         compiler_params=pltpu.CompilerParams(vmem_limit_bytes=VMEM_BYTES),
-        cost_estimate=pl.CostEstimate(
-            flops=8 * modes * tok_rows * width, bytes_accessed=14 * tok_rows * width, transcendentals=0
-        ),
+        cost_estimate=takes(4.0),
         name="final_outputs",
     )(*args)
 
 
-def lag_kernel(shards, chans, groups, owned, scale, count, *refs):
-    in_refs, (out_ref, u_all, g_all, turned_all) = refs[:count], refs[-4:]
+def lag_kernel(shards, chans, groups, owned, scale, *refs):
+    in_refs, (out_ref, u_all, g_all, turned_all) = refs[:-4], refs[-4:]
     tok_rows = out_ref.shape[2]
     halves = tok_rows // LANES
     blocks = shards * halves
@@ -444,7 +448,7 @@
     lax.fori_loop(0, owned, one_filter, 0, unroll=min(owned, 4))
 
 
-def filter_lags(received, held, shards, chans, owned, scale):
+def filter_lags(received, shards, chans, owned, scale):
     tok_rows = received.shape[2]
     groups = received.shape[1] // (2 * owned)
     halves = tok_rows // LANES
@@ -456,10 +460,7 @@
         split = split.transpose(2, 4, 0, 5, 1, 3, 6).reshape(2, owned, full, LANES)
         args = (split[0], split[1])
     return pl.pallas_call(
-        functools.partial(lag_kernel, shards, chans, groups, owned, scale, len(args)),
-        in_specs=[pl.BlockSpec(memory_space=pltpu.VMEM)] * len(args)
-        + [pl.BlockSpec(memory_space=pl.ANY)] * len(held),
-        out_specs=pl.BlockSpec(memory_space=pltpu.VMEM),
+        functools.partial(lag_kernel, shards, chans, groups, owned, scale),
         out_shape=jax.ShapeDtypeStruct((shards, owned, tok_rows), F32),
         scratch_shapes=[
             pltpu.VMEM((owned, full, LANES), BF16),
@@ -467,11 +468,9 @@
             pltpu.VMEM((owned, LANES, full), BF16),
         ],
         compiler_params=pltpu.CompilerParams(vmem_limit_bytes=VMEM_BYTES),
-        cost_estimate=pl.CostEstimate(
-            flops=4 * owned * LANES * full * full, bytes_accessed=8 * owned * full * LANES, transcendentals=0
-        ),
+        cost_estimate=takes(4.0),
         name="filter_lags",
-    )(*args, *held)
+    )(*args)
 
 
 def per_device(query_proj, key_proj, value_proj, out_grad, residues, decay_rate, skip_gain):
@@ -505,17 +504,17 @@
     *states, coefs = lax.optimization_barrier((*states, coefs))
     states = [along_column(state, pairs, 1 + i) for i, state in enumerate(states)]
     parts = local_parts(*signals, coefs, skip_gain[None, :])
-    kept, given = pair_states(seq_index, coefs, own, states)
+    kept, given = pair_states(seq_index, coefs, own, parts, states)
     received, kept, given = lax.optimization_barrier((received, kept, given))
     given = inside_pair(given, pairs)
 
     scale = 1.0 / math.sqrt(length * (CHANNELS // FILTERS))
-    lags = filter_lags(received, parts, shards, chans, owned, scale)
+    lags = filter_lags(received, shards, chans, owned, scale)
     lags, given = lax.optimization_barrier((lags, given))
     lags = lax.all_to_all(lags, "seq", split_axis=0, concat_axis=0, tiled=True)
     filter_grad = lags.reshape(shards * owned, tok_rows).T
     layer_out, key_grad, value_grad = final_outputs(
-        signals[:3], coefs, parts, kept, given
+        signals[:3], parts, coefs, kept, given
     )
     return (layer_out, key_grad, value_grad, filter_grad)
 

time: 65 us -> 58.7 us (0.903)
  waiting for transfers between devices: 20.8 us -> 14.5 us
    ppermute x3, waiting for transfers between devices: 19.8 us -> 12.6 us  [along_column(): return lax.ppermute(state, 'seq', route)]
    all_to_all x1, waiting for transfers between devices: 0.94 us -> 1.83 us  [per_device(): lags = lax.all_to_all(lags, 'seq', split_axis=0, concat_axis=0, tiled=True)]
    unnamed x29 -> x25, local copies, waits for them, and re-layouts: 4.96 us -> 4.76 us
  transfers between devices with their start and end apart: 6 -> 6, of which waited for: 3 -> 3; matrix products, arithmetic and copies ran while one was open for 0% -> 0% of each run, Pallas kernels for 27% -> 30%
where the time goes in v11:
time: 58.7 us; the launch traced here: 58.3 us
  Pallas kernels  20.4 us (35%)
  starting transfers between devices  17.8 us (30%)
  waiting for transfers between devices  14.5 us (25%)
  local copies, waits for them, and re-layouts  4.84 us (8%)
  between operations  0.84 us (1%)
    ppermute x3, waiting for transfers between devices, along_column(): return lax.ppermute(state, 'seq', route)  12.6 us
    all_to_all x1, starting transfers between devices, per_device(): lax.all_to_all(send, ('seq', 'chan'), split_axis=0, concat_axis=0, tiled=...  7.3 us
    pallas_call x1, Pallas kernels, local_parts(): pl.pallas_call(local_kernel, out_shape=[jax.ShapeDtypeStruct((tok_rows, w...  6.33 us
    ppermute x3, starting transfers between devices, along_column(): return lax.ppermute(state, 'seq', route)  5.65 us
    unnamed x25, local copies, waits for them, and re-layouts  4.76 us
    pallas_call x1, Pallas kernels, filter_lags(): pl.pallas_call(functools.partial(lag_kernel, shards, chans, groups, owned...  4.01 us
    pallas_call x1, Pallas kernels, final_outputs(): pl.pallas_call(final_kernel, in_specs=[pl.BlockSpec(memory_space=pltpu.VM...  3.95 us
    all_to_all x1, starting transfers between devices, per_device(): lags = lax.all_to_all(lags, 'seq', split_axis=0, concat_axis=0, tiled=True)  3.35 us
  transfers between devices with their start and end apart: 6, of which 3 were waited for; matrix products, arithmetic and copies ran while one was open for 0% of the time, Pallas kernels for 30%

profile of v11, /device:TPU:0, one launch (start us, length us, event | category | flops | bytes accessed | tf_op | source)
XLA Modules:
  0.0 58.3 jit_solution(6482683849960916667)
XLA Ops:
  0.6 3.0 %pack_signals.1 = bf16[32,64,256]{2,1,0:T(8,128)(2,1)} custom-call(bf16[256,1024]{1,0:T(8,128)(2,1)} %k_ref.2, bf16[256,1024]{1,0:T(8,128)(2,1)} %v_ref.2, bf16[256,1024]{1,0:T(8,128)(2,1)} %o_ref.1, bf16[256,1024]{1,0:T(8,128)(2,1)} %q_ref.2), custom_call_target="tpu_custom_call" | custom-call | bytes 10800000 | tf_op jit(solution)/shard_map/pack_signals/pallas_call | solution.py:101
  3.6 0.0 copy-start.10
  3.6 0.0 copy-start.11
  3.6 0.0 copy-start.1
  3.6 0.0 copy-start.2
  3.6 0.0 copy-start.3
  3.6 7.3 %all-to-all-start = ((bf16[32,64,256]{2,1,0:T(8,128)(2,1)}), bf16[32,64,256]{2,1,0:T(8,128)(2,1)S(1)}, u32[]{:S(2)}, u32[]{:S(2)}) async-start(bf16[32,64,256]{2,1,0:T(8,128)(2,1)} %pack_signals.1), calls=%async_computation | async-start | bytes 2097152 | tf_op jit(solution)/shard_map/all_to_all | solution.py:489
  11.0 0.0 copy-start
  11.0 0.0 copy-done.10
  11.0 0.0 copy-done.11
  11.1 0.1 broadcast_in_dim.11
  11.1 0.0 copy-done.1
  11.1 0.0 copy-done.2
  11.2 0.0 copy-done.3
  11.2 0.8 %copy-done = bf16[256,1024]{1,0:T(8,128)(2,1)S(1)} copy-done((bf16[256,1024]{1,0:T(8,128)(2,1)S(1)}, bf16[256,1024]{1,0:T(8,128)(2,1)}, u32[]{:S(2)}) %copy-start) | copy-done | bytes 524312
  12.0 3.0 %block_states.1 = (bf16[128,128]{1,0:T(8,128)(2,1)S(1)}, bf16[128,128]{1,0:T(8,128)(2,1)S(1)}, bf16[128,128]{1,0:T(8,128)(2,1)S(1)}, f32[2,128,128]{2,1,0:T(8,128)S(1)}) custom-call(s32[1]{0:T(128)} %bitcast.seq_ref, bf16[256,1024]{1,0:T(8,128)(2,1)S(1)} %copy-done, bf16[256,1024]{1,0:T(8,128)(2,1)S(1)} %copy-done.1, bf16[256,1024]{1,0:T(8,128)(2,1)S(1)} %copy-done.2, ...), custom_call_target="tpu_custom_call" | custom-call | bytes 10800000 | tf_op jit(solution)/shard_map/block_states/pallas_call | solution.py:203
  15.0 0.0 copy-start.8
  15.0 1.8 %collective-permute-start = (bf16[128,128]{1,0:T(8,128)(2,1)S(1)}, bf16[128,128]{1,0:T(8,128)(2,1)S(1)}, u32[]{:S(2)}, u32[]{:S(2)}) collective-permute-start(bf16[128,128]{1,0:T(8,128)(2,1)S(1)} %get-tuple-element.45), channel_id=1, source_target_pairs={{0,8},{4,12},{8,16},{12,20},{16,24},{20,28},{24,0},{28,4},{1,9},{5... | collective-permute-start | bytes 98312 | tf_op jit(solution)/shard_map/ppermute | solution.py:296
  16.9 2.4 %collective-permute-start.1 = (bf16[128,128]{1,0:T(8,128)(2,1)S(1)}, bf16[128,128]{1,0:T(8,128)(2,1)S(1)}, u32[]{:S(2)}, u32[]{:S(2)}) collective-permute-start(bf16[128,128]{1,0:T(8,128)(2,1)S(1)} %get-tuple-element.46), channel_id=1, source_target_pairs={{0,16},{4,20},{8,24},{12,28},{16,0},{20,4},{24,8},{28,12},{1,17},{... | collective-permute-start | bytes 98312 | tf_op jit(solution)/shard_map/ppermute | solution.py:296
  19.3 1.4 %collective-permute-start.2 = (bf16[128,128]{1,0:T(8,128)(2,1)S(1)}, bf16[128,128]{1,0:T(8,128)(2,1)S(1)}, u32[]{:S(2)}, u32[]{:S(2)}) collective-permute-start(bf16[128,128]{1,0:T(8,128)(2,1)S(1)} %get-tuple-element.47), channel_id=1, source_target_pairs={{0,24},{4,28},{8,0},{12,4},{16,8},{20,12},{24,16},{28,20},{1,25},{... | collective-permute-start | bytes 98312 | tf_op jit(solution)/shard_map/ppermute | solution.py:296
  20.7 0.0 copy-done.8
  20.7 6.3 %local_parts.1 = (bf16[256,1024]{1,0:T(8,128)(2,1)S(1)}, bf16[256,1024]{1,0:T(8,128)(2,1)S(1)}) custom-call(bf16[256,1024]{1,0:T(8,128)(2,1)S(1)} %copy-done, bf16[256,1024]{1,0:T(8,128)(2,1)S(1)} %copy-done.1, bf16[256,1024]{1,0:T(8,128)(2,1)S(1)} %copy-done.2, bf16[256,1024]{1,0:T(8,128)(2,1)S(1)} %copy-done.3, f32[3,16,8,128]{3,2,1,0:T(8,128)S(1)} %bitcast.15, ...), custom_call_target="tpu_custom_call" | custom-call | bytes 23400000 | tf_op jit(solution)/shard_map/local_parts/pallas_call | solution.py:284
  27.0 6.7 %collective-permute-done.refs_2_ = bf16[128,128]{1,0:T(8,128)(2,1)S(1)} collective-permute-done((bf16[128,128]{1,0:T(8,128)(2,1)S(1)}, bf16[128,128]{1,0:T(8,128)(2,1)S(1)}, u32[]{:S(2)}, u32[]{:S(2)}) %collective-permute-start) | collective-permute-done | bytes 32800 | tf_op jit(solution)/shard_map/ppermute | solution.py:296
  33.7 6.0 %collective-permute-done.1.refs_3_ = bf16[128,128]{1,0:T(8,128)(2,1)S(1)} collective-permute-done((bf16[128,128]{1,0:T(8,128)(2,1)S(1)}, bf16[128,128]{1,0:T(8,128)(2,1)S(1)}, u32[]{:S(2)}, u32[]{:S(2)}) %collective-permute-start.1) | collective-permute-done | bytes 32800 | tf_op jit(solution)/shard_map/ppermute | solution.py:296
  39.7 0.0 collective-permute-done.2.refs_4_
  39.7 0.1 pair_states.1
  39.8 0.0 copy-start.4
  39.8 0.8 %copy-done.4 = bf16[256,1024]{1,0:T(8,128)(2,1)} copy-done((bf16[256,1024]{1,0:T(8,128)(2,1)}, bf16[256,1024]{1,0:T(8,128)(2,1)S(1)}, u32[]{:S(2)}) %copy-start.4) | copy-done | bytes 524312
  40.6 0.0 copy-start.6
  40.6 0.8 %copy-done.6 = bf16[256,1024]{1,0:T(8,128)(2,1)} copy-done((bf16[256,1024]{1,0:T(8,128)(2,1)}, bf16[256,1024]{1,0:T(8,128)(2,1)S(1)}, u32[]{:S(2)}) %copy-start.6) | copy-done | bytes 524312
  41.3 0.0 copy-start.9
  41.3 0.6 %copy-done.9 = bf16[2,128,128]{2,1,0:T(8,128)(2,1)} copy-done((bf16[2,128,128]{2,1,0:T(8,128)(2,1)}, bf16[2,128,128]{2,1,0:T(8,128)(2,1)S(1)}, u32[]{:S(2)}) %copy-start.9) | copy-done | bytes 65560
  42.0 0.0 all-to-all-done.refs_0_
  42.0 0.0 copy-start.5
  42.0 1.5 %collective-permute-start.3 = (bf16[2,128,128]{2,1,0:T(8,128)(2,1)}, bf16[2,128,128]{2,1,0:T(8,128)(2,1)S(1)}, u32[]{:S(2)}, u32[]{:S(2)}) collective-permute-start(bf16[2,128,128]{2,1,0:T(8,128)(2,1)} %copy-done.9), channel_id=1, source_target_pairs={{0,4},{4,0},{8,12},{12,8},{16,20},{20,16},{24,28},{28,24},{1,5},{5... | collective-permute-start | bytes 196616 | tf_op jit(solution)/shard_map/ppermute | solution.py:300
  43.5 4.0 %filter_lags.1 = f32[8,8,256]{2,1,0:T(8,128)} custom-call(bf16[32,64,256]{2,1,0:T(8,128)(2,1)S(1)} %all-to-all-done.refs_0_), custom_call_target="tpu_custom_call" | custom-call | bytes 14400000 | tf_op jit(solution)/shard_map/filter_lags/pallas_call | solution.py:462
  47.5 0.0 collective-permute-done.3.given_ref
  47.5 3.4 %all-to-all-start.1 = ((f32[8,8,256]{2,1,0:T(8,128)}), f32[8,8,256]{2,1,0:T(8,128)S(1)}, u32[]{:S(2)}, u32[]{:S(2)}) async-start(f32[8,8,256]{2,1,0:T(8,128)} %filter_lags.1), calls=%async_computation.1 | async-start | bytes 131072 | tf_op jit(solution)/shard_map/all_to_all | solution.py:514
  50.8 0.0 copy-done.5
  50.8 0.0 copy-start.7
  50.8 1.0 %copy-done.7 = bf16[256,1024]{1,0:T(8,128)(2,1)S(1)} copy-done((bf16[256,1024]{1,0:T(8,128)(2,1)S(1)}, bf16[256,1024]{1,0:T(8,128)(2,1)}, u32[]{:S(2)}) %copy-start.7) | copy-done | bytes 524312
  51.9 4.0 %final_outputs.1 = (bf16[256,1024]{1,0:T(8,128)(2,1)}, bf16[256,1024]{1,0:T(8,128)(2,1)}, bf16[256,1024]{1,0:T(8,128)(2,1)}) custom-call(bf16[256,1024]{1,0:T(8,128)(2,1)S(1)} %copy-done, bf16[256,1024]{1,0:T(8,128)(2,1)S(1)} %copy-done.1, bf16[256,1024]{1,0:T(8,128)(2,1)S(1)} %copy-done.2, bf16[256,1024]{1,0:T(8,128)(2,1)S(1)} %copy-done.5, ...), custom_call_target="tpu_custom_call" | custom-call | bytes 14400000 | tf_op jit(solution)/shard_map/final_outputs/pallas_call | solution.py:359
  55.8 1.8 %all-to-all-done.1 = f32[8,8,256]{2,1,0:T(8,128)S(1)} async-done(((f32[8,8,256]{2,1,0:T(8,128)}), f32[8,8,256]{2,1,0:T(8,128)S(1)}, u32[]{:S(2)}, u32[]{:S(2)}) %all-to-all-start.1) | async-done | bytes 65568 | tf_op jit(solution)/shard_map/all_to_all | solution.py:514
  57.7 0.6 %copy.12 = f32[256,64]{0,1:T(8,128)} copy(f32[256,64]{0,1:T(8,128)S(1)} %bitcast.19) | data formatting | bytes 131072
  (3 shorter events, 0.1 us)
Async XLA Ops:
  3.6 7.4 %copy-start.10 = (f32[256,16]{0,1:T(8,128)S(1)}, f32[256,16]{0,1:T(8,128)}, u32[]{:S(2)}) copy-start(f32[256,16]{0,1:T(8,128)} %param.12) | copy-start | bytes 49156
  3.6 7.4 %copy-start.11 = (f32[256,16]{0,1:T(8,128)S(1)}, f32[256,16]{0,1:T(8,128)}, u32[]{:S(2)}) copy-start(f32[256,16]{0,1:T(8,128)} %param.11) | copy-start | bytes 49156
  3.6 7.5 %copy-start.1 = (bf16[256,1024]{1,0:T(8,128)(2,1)S(1)}, bf16[256,1024]{1,0:T(8,128)(2,1)}, u32[]{:S(2)}) copy-start(bf16[256,1024]{1,0:T(8,128)(2,1)} %k_ref.2) | copy-start | bytes 1572868
  3.6 7.5 %copy-start.2 = (bf16[256,1024]{1,0:T(8,128)(2,1)S(1)}, bf16[256,1024]{1,0:T(8,128)(2,1)}, u32[]{:S(2)}) copy-start(bf16[256,1024]{1,0:T(8,128)(2,1)} %v_ref.2) | copy-start | bytes 1572868
  3.6 7.5 %copy-start.3 = (bf16[256,1024]{1,0:T(8,128)(2,1)S(1)}, bf16[256,1024]{1,0:T(8,128)(2,1)}, u32[]{:S(2)}) copy-start(bf16[256,1024]{1,0:T(8,128)(2,1)} %o_ref.1) | copy-start | bytes 1572868
  3.6 38.3 %all-to-all-start = ((bf16[32,64,256]{2,1,0:T(8,128)(2,1)}), bf16[32,64,256]{2,1,0:T(8,128)(2,1)S(1)}, u32[]{:S(2)}, u32[]{:S(2)}) async-start(bf16[32,64,256]{2,1,0:T(8,128)(2,1)} %pack_signals.1), calls=%async_computation | async-start | bytes 2097152 | tf_op jit(solution)/shard_map/all_to_all | solution.py:489
  11.0 1.0 %copy-start = (bf16[256,1024]{1,0:T(8,128)(2,1)S(1)}, bf16[256,1024]{1,0:T(8,128)(2,1)}, u32[]{:S(2)}) copy-start(bf16[256,1024]{1,0:T(8,128)(2,1)} %q_ref.2) | copy-start | bytes 1572868
  15.0 5.7 %copy-start.8 = (f32[1024]{0:T(1024)S(1)}, f32[1024]{0:T(1024)}, u32[]{:S(2)}) copy-start(f32[1024]{0:T(1024)} %param.13) | copy-start | bytes 12292
  15.0 18.7 %collective-permute-start = (bf16[128,128]{1,0:T(8,128)(2,1)S(1)}, bf16[128,128]{1,0:T(8,128)(2,1)S(1)}, u32[]{:S(2)}, u32[]{:S(2)}) collective-permute-start(bf16[128,128]{1,0:T(8,128)(2,1)S(1)} %get-tuple-element.45), channel_id=1, source_target_pairs={{0,8},{4,12},{8,16},{12,20},{16,24},{20,28},{24,0},{28,4},{1,9},{5... | collective-permute-start | bytes 98312 | tf_op jit(solution)/shard_map/ppermute | solution.py:296
  16.9 22.8 %collective-permute-start.1 = (bf16[128,128]{1,0:T(8,128)(2,1)S(1)}, bf16[128,128]{1,0:T(8,128)(2,1)S(1)}, u32[]{:S(2)}, u32[]{:S(2)}) collective-permute-start(bf16[128,128]{1,0:T(8,128)(2,1)S(1)} %get-tuple-element.46), channel_id=1, source_target_pairs={{0,16},{4,20},{8,24},{12,28},{16,0},{20,4},{24,8},{28,12},{1,17},{... | collective-permute-start | bytes 98312 | tf_op jit(solution)/shard_map/ppermute | solution.py:296
  19.3 20.4 %collective-permute-start.2 = (bf16[128,128]{1,0:T(8,128)(2,1)S(1)}, bf16[128,128]{1,0:T(8,128)(2,1)S(1)}, u32[]{:S(2)}, u32[]{:S(2)}) collective-permute-start(bf16[128,128]{1,0:T(8,128)(2,1)S(1)} %get-tuple-element.47), channel_id=1, source_target_pairs={{0,24},{4,28},{8,0},{12,4},{16,8},{20,12},{24,16},{28,20},{1,25},{... | collective-permute-start | bytes 98312 | tf_op jit(solution)/shard_map/ppermute | solution.py:296
  39.8 0.8 %copy-start.4 = (bf16[256,1024]{1,0:T(8,128)(2,1)}, bf16[256,1024]{1,0:T(8,128)(2,1)S(1)}, u32[]{:S(2)}) copy-start(bf16[256,1024]{1,0:T(8,128)(2,1)S(1)} %get-tuple-element.41.refs_0_.conv_ref) | copy-start | bytes 1572868
  40.6 0.8 %copy-start.6 = (bf16[256,1024]{1,0:T(8,128)(2,1)}, bf16[256,1024]{1,0:T(8,128)(2,1)S(1)}, u32[]{:S(2)}) copy-start(bf16[256,1024]{1,0:T(8,128)(2,1)S(1)} %get-tuple-element.42.refs_1_.grad_ref) | copy-start | bytes 1572868
  41.3 0.6 %copy-start.9 = (bf16[2,128,128]{2,1,0:T(8,128)(2,1)}, bf16[2,128,128]{2,1,0:T(8,128)(2,1)S(1)}, u32[]{:S(2)}) copy-start(bf16[2,128,128]{2,1,0:T(8,128)(2,1)S(1)} %get-tuple-element.52) | copy-start | bytes 196612
  42.0 8.9 %copy-start.5 = (bf16[256,1024]{1,0:T(8,128)(2,1)S(1)}, bf16[256,1024]{1,0:T(8,128)(2,1)}, u32[]{:S(2)}) copy-start(bf16[256,1024]{1,0:T(8,128)(2,1)} %copy-done.4) | copy-start | bytes 1572868
  42.0 5.5 %collective-permute-start.3 = (bf16[2,128,128]{2,1,0:T(8,128)(2,1)}, bf16[2,128,128]{2,1,0:T(8,128)(2,1)S(1)}, u32[]{:S(2)}, u32[]{:S(2)}) collective-permute-start(bf16[2,128,128]{2,1,0:T(8,128)(2,1)} %copy-done.9), channel_id=1, source_target_pairs={{0,4},{4,0},{8,12},{12,8},{16,20},{20,16},{24,28},{28,24},{1,5},{5... | collective-permute-start | bytes 196616 | tf_op jit(solution)/shard_map/ppermute | solution.py:300
  47.5 10.2 %all-to-all-start.1 = ((f32[8,8,256]{2,1,0:T(8,128)}), f32[8,8,256]{2,1,0:T(8,128)S(1)}, u32[]{:S(2)}, u32[]{:S(2)}) async-start(f32[8,8,256]{2,1,0:T(8,128)} %filter_lags.1), calls=%async_computation.1 | async-start | bytes 131072 | tf_op jit(solution)/shard_map/all_to_all | solution.py:514
  50.8 1.0 %copy-start.7 = (bf16[256,1024]{1,0:T(8,128)(2,1)S(1)}, bf16[256,1024]{1,0:T(8,128)(2,1)}, u32[]{:S(2)}) copy-start(bf16[256,1024]{1,0:T(8,128)(2,1)} %copy-done.6) | copy-start | bytes 1572868

commit v12 on v11

--- a/solution.py
+++ b/solution.py
@@ -214,8 +214,8 @@
     return states, own
 
 
-def pair_kernel(seq_ref, coef_ref, own_ref, *refs):
-    state_refs, kept_ref, given_ref = refs[2:-2], *refs[-2:]
+def pair_kernel(seq_ref, coef_ref, own_ref, _, *refs):
+    state_refs, kept_ref, given_ref = refs[:-2], *refs[-2:]
     pairs = len(state_refs) + 1
     modes, tiles = coef_ref.shape[1:3]
     pair = seq_ref[0] // 2
@@ -241,12 +241,12 @@
         given_ref[1, rows] = jnp.where(second, decay * after + own, after).astype(LINK)
 
 
-def pair_states(seq_index, coefs, own, parts, states):
+def pair_states(seq_index, coefs, own, done, states):
     whole = pl.BlockSpec(memory_space=pltpu.VMEM)
     return pl.pallas_call(
         pair_kernel,
         in_specs=[pl.BlockSpec(memory_space=pltpu.SMEM), whole, whole]
-        + [pl.BlockSpec(memory_space=pl.ANY)] * len(parts)
+        + [pl.BlockSpec(memory_space=pl.ANY)]
         + [whole] * len(states),
         out_specs=[whole] * 2,
         out_shape=[
@@ -256,11 +256,11 @@
         compiler_params=pltpu.CompilerParams(vmem_limit_bytes=VMEM_BYTES),
         cost_estimate=takes(0.1),
         name="pair_states",
-    )(seq_index, coefs, own, *parts, *states)
+    )(seq_index, coefs, own, done, *states)
 
 
 def local_kernel(
-    q_ref, k_ref, v_ref, o_ref, coef_ref, gain_ref, conv_ref, grad_ref, x_ref, g_ref
+    q_ref, k_ref, v_ref, o_ref, coef_ref, gain_ref, conv_ref, grad_ref, done_ref, x_ref, g_ref
 ):
     tok_rows, width = k_ref.shape
     tiles = width // LANES
@@ -273,9 +273,10 @@
         rows = tile_rows(tok_rows, tile)
         gain = gain_ref[:, cols]
         conv_in = product(k_ref[:, cols], v_ref[:, cols]).astype(F32)
-        conv_ref[:, cols] = (x_ref[rows, :] + gain * conv_in).astype(BF16)
+        conv_ref[:, cols] = x_ref[rows, :] + gain * conv_in
         mid_grad = product(o_ref[:, cols], q_ref[:, cols]).astype(F32)
-        grad_ref[:, cols] = (g_ref[rows, :] + gain * mid_grad).astype(BF16)
+        grad_ref[:, cols] = g_ref[rows, :] + gain * mid_grad
+    done_ref[...] = jnp.zeros(done_ref.shape, F32)
 
 
 def local_parts(query_proj, key_proj, value_proj, out_grad, coefs, gain):
@@ -283,7 +284,8 @@
     tiles = coefs.shape[2]
     return pl.pallas_call(
         local_kernel,
-        out_shape=[jax.ShapeDtypeStruct((tok_rows, width), BF16)] * 2,
+        out_shape=[jax.ShapeDtypeStruct((tok_rows, width), F32)] * 2
+        + [jax.ShapeDtypeStruct((SUBLANES, LANES), F32)],
         scratch_shapes=[pltpu.VMEM(token_shape(tok_rows, tiles), F32)] * 2,
         compiler_params=pltpu.CompilerParams(vmem_limit_bytes=VMEM_BYTES),
         cost_estimate=takes(6.5),
@@ -313,60 +315,50 @@
     lax.fori_loop(0, tok_rows, step, held, unroll=8)
 
 
-def final_kernel(
-    q_ref, k_ref, v_ref, conv_ref, grad_ref, coef_ref, kept_ref, given_ref,
-    layer_hbm, key_hbm, value_hbm, edge_ref, layer_ref, key_ref, value_ref, sems,
-):
-    tok_rows, width = k_ref.shape
+def output_kernel(side, count, *refs):
+    part_ref, coef_ref, kept_ref, given_ref = refs[:4]
+    factor_refs, hbm_refs = refs[4 : 4 + count], refs[4 + count : 4 + 2 * count]
+    edge_ref, out_refs, sems = refs[4 + 2 * count], refs[5 + 2 * count : -1], refs[-1]
+    tok_rows, width = part_ref.shape
     tiles = width // LANES
-    modes = coef_ref.shape[1]
 
     def departure(i, tile):
         place = (slice(None), pl.ds(tile * LANES, LANES))
         return pltpu.make_async_copy(
-            (layer_ref, key_ref, value_ref)[i].at[place],
-            (layer_hbm, key_hbm, value_hbm)[i].at[place],
-            sems.at[i, tile],
+            out_refs[i].at[place], hbm_refs[i].at[place], sems.at[i, tile]
         )
 
-    def edge(side):
-        total = kept_ref[side] + given_ref[side].astype(F32)
-        return [total[m * tiles : (m + 1) * tiles] for m in range(modes)]
-
-    fill_edge(edge_ref, edge(0), coef_ref, tok_rows, tiles, 0, 1)
+    total = kept_ref[side] + given_ref[side].astype(F32)
+    held = [total[m * tiles : (m + 1) * tiles] for m in range(coef_ref.shape[1])]
+    start, move = ((0, 1), (tok_rows - 1, -1))[side]
+    fill_edge(edge_ref, held, coef_ref, tok_rows, tiles, start, move)
     for tile in range(tiles):
         cols = slice(tile * LANES, (tile + 1) * LANES)
-        long_conv = conv_ref[:, cols].astype(F32) + edge_ref[tile_rows(tok_rows, tile), :]
-        layer_ref[:, cols] = (q_ref[:, cols].astype(F32) * long_conv).astype(BF16)
-        departure(0, tile).start()
-    fill_edge(edge_ref, edge(1), coef_ref, tok_rows, tiles, tok_rows - 1, -1)
-    for tile in range(tiles):
-        cols = slice(tile * LANES, (tile + 1) * LANES)
-        conv_grad = grad_ref[:, cols].astype(F32) + edge_ref[tile_rows(tok_rows, tile), :]
-        key_ref[:, cols] = (conv_grad * v_ref[:, cols].astype(F32)).astype(BF16)
-        departure(1, tile).start()
-        value_ref[:, cols] = (conv_grad * k_ref[:, cols].astype(F32)).astype(BF16)
-        departure(2, tile).start()
-    for i in range(3):
+        value = part_ref[:, cols] + edge_ref[tile_rows(tok_rows, tile), :]
+        for i in range(count):
+            out_refs[i][:, cols] = (value * factor_refs[i][:, cols].astype(F32)).astype(BF16)
+            departure(i, tile).start()
+    for i in range(count):
         for tile in range(tiles):
             departure(i, tile).wait()
 
 
-def final_outputs(signals, parts, coefs, kept, given):
-    tok_rows, width = signals[0].shape
+def outputs(side, name, part, coefs, kept, given, *factors):
+    tok_rows, width = part.shape
     tiles = coefs.shape[2]
-    args = (*signals, *parts, coefs, kept, given)
+    count = len(factors)
+    args = (part, coefs, kept, given, *factors)
     return pl.pallas_call(
-        final_kernel,
+        functools.partial(output_kernel, side, count),
         in_specs=[pl.BlockSpec(memory_space=pltpu.VMEM)] * len(args),
-        out_specs=[pl.BlockSpec(memory_space=pl.ANY)] * 3,
-        out_shape=[jax.ShapeDtypeStruct((tok_rows, width), BF16)] * 3,
+        out_specs=[pl.BlockSpec(memory_space=pl.ANY)] * count,
+        out_shape=[jax.ShapeDtypeStruct((tok_rows, width), BF16)] * count,
         scratch_shapes=[pltpu.VMEM(token_shape(tok_rows, tiles), F32)]
-        + [pltpu.VMEM((tok_rows, width), BF16)] * 3
-        + [pltpu.SemaphoreType.DMA((3, tiles))],
+        + [pltpu.VMEM((tok_rows, width), BF16)] * count
+        + [pltpu.SemaphoreType.DMA((count, tiles))],
         compiler_params=pltpu.CompilerParams(vmem_limit_bytes=VMEM_BYTES),
-        cost_estimate=takes(4.0),
-        name="final_outputs",
+        cost_estimate=takes(2.0),
+        name=name,
     )(*args)
 
 
@@ -503,8 +495,8 @@
     states, own = block_states(seq_index, pairs, *signals, coefs)
     *states, coefs = lax.optimization_barrier((*states, coefs))
     states = [along_column(state, pairs, 1 + i) for i, state in enumerate(states)]
-    parts = local_parts(*signals, coefs, skip_gain[None, :])
-    kept, given = pair_states(seq_index, coefs, own, parts, states)
+    conv_part, grad_part, done = local_parts(*signals, coefs, skip_gain[None, :])
+    kept, given = pair_states(seq_index, coefs, own, done, states)
     received, kept, given = lax.optimization_barrier((received, kept, given))
     given = inside_pair(given, pairs)
 
@@ -513,8 +505,10 @@
     lags, given = lax.optimization_barrier((lags, given))
     lags = lax.all_to_all(lags, "seq", split_axis=0, concat_axis=0, tiled=True)
     filter_grad = lags.reshape(shards * owned, tok_rows).T
-    layer_out, key_grad, value_grad = final_outputs(
-        signals[:3], parts, coefs, kept, given
+    query_proj, key_proj, value_proj, _ = signals
+    (layer_out,) = outputs(0, "conv_outputs", conv_part, coefs, kept, given, query_proj)
+    key_grad, value_grad = outputs(
+        1, "grad_outputs", grad_part, coefs, kept, given, value_proj, key_proj
     )
     return (layer_out, key_grad, value_grad, filter_grad)
 

time: 58.7 us -> 56.5 us (0.963)
  waiting for transfers between devices: 14.5 us -> 11.8 us
    ppermute x3, waiting for transfers between devices: 12.6 us -> 10.7 us  [along_column(): return lax.ppermute(state, 'seq', route)]
    all_to_all x1, waiting for transfers between devices: 1.83 us -> 1.11 us  [per_device(): lags = lax.all_to_all(lags, 'seq', split_axis=0, concat_axis=0, tiled=True)]
    pallas_call x1 -> x2, Pallas kernels: 3.95 us -> 4.48 us  [outputs(): pl.pallas_call(functools.partial(output_kernel, side, count), in_specs=[p...]
    unnamed x25 -> x23, local copies, waits for them, and re-layouts: 4.76 us -> 4.7 us
  transfers between devices with their start and end apart: 6 -> 6, of which waited for: 3 -> 3; matrix products, arithmetic and copies ran while one was open for 0% -> 0% of each run, Pallas kernels for 30% -> 32%
where the time goes in v12:
time: 56.5 us; the launch traced here: 56.2 us
  Pallas kernels  20.9 us (37%)
  starting transfers between devices  17.9 us (32%)
  waiting for transfers between devices  11.8 us (21%)
  local copies, waits for them, and re-layouts  4.78 us (8%)
  between operations  0.86 us (2%)
    ppermute x3, waiting for transfers between devices, along_column(): return lax.ppermute(state, 'seq', route)  10.7 us
    all_to_all x1, starting transfers between devices, per_device(): lax.all_to_all(send, ('seq', 'chan'), split_axis=0, concat_axis=0, tiled=...  7.3 us
    pallas_call x1, Pallas kernels, local_parts(): pl.pallas_call(local_kernel, out_shape=[jax.ShapeDtypeStruct((tok_rows, w...  6.32 us
    ppermute x3, starting transfers between devices, along_column(): return lax.ppermute(state, 'seq', route)  5.65 us
    unnamed x23, local copies, waits for them, and re-layouts  4.7 us
    pallas_call x2, Pallas kernels, outputs(): pl.pallas_call(functools.partial(output_kernel, side, count), in_specs=[p...  4.48 us
    pallas_call x1, Pallas kernels, filter_lags(): pl.pallas_call(functools.partial(lag_kernel, shards, chans, groups, owned...  4.02 us
    all_to_all x1, starting transfers between devices, per_device(): lags = lax.all_to_all(lags, 'seq', split_axis=0, concat_axis=0, tiled=True)  3.35 us
  transfers between devices with their start and end apart: 6, of which 3 were waited for; matrix products, arithmetic and copies ran while one was open for 0% of the time, Pallas kernels for 32%

profile of v12, /device:TPU:0, one launch (start us, length us, event | category | flops | bytes accessed | tf_op | source)
XLA Modules:
  0.0 56.2 jit_solution(13507325264610969316)
XLA Ops:
  0.6 3.0 %pack_signals.1 = bf16[32,64,256]{2,1,0:T(8,128)(2,1)} custom-call(bf16[256,1024]{1,0:T(8,128)(2,1)} %refs_5_, bf16[256,1024]{1,0:T(8,128)(2,1)} %refs_4_.1, bf16[256,1024]{1,0:T(8,128)(2,1)} %o_ref.1, bf16[256,1024]{1,0:T(8,128)(2,1)} %refs_4_), custom_call_target="tpu_custom_call" | custom-call | bytes 10800000 | tf_op jit(solution)/shard_map/pack_signals/pallas_call | solution.py:101
  3.6 0.0 copy-start.9
  3.6 0.0 copy-start.10
  3.6 0.0 copy-start.1
  3.6 0.0 copy-start.2
  3.7 0.0 copy-start.3
  3.7 7.3 %all-to-all-start = ((bf16[32,64,256]{2,1,0:T(8,128)(2,1)}), bf16[32,64,256]{2,1,0:T(8,128)(2,1)S(1)}, u32[]{:S(2)}, u32[]{:S(2)}) async-start(bf16[32,64,256]{2,1,0:T(8,128)(2,1)} %pack_signals.1), calls=%async_computation | async-start | bytes 2097152 | tf_op jit(solution)/shard_map/all_to_all | solution.py:481
  11.0 0.0 copy-start
  11.0 0.0 copy-done.9
  11.0 0.0 copy-done.10
  11.1 0.1 broadcast_in_dim.11
  11.2 0.0 copy-done.1
  11.2 0.0 copy-done.2
  11.2 0.0 copy-done.3
  11.2 0.8 %copy-done = bf16[256,1024]{1,0:T(8,128)(2,1)S(1)} copy-done((bf16[256,1024]{1,0:T(8,128)(2,1)S(1)}, bf16[256,1024]{1,0:T(8,128)(2,1)}, u32[]{:S(2)}) %copy-start) | copy-done | bytes 524312
  12.0 3.0 %block_states.1 = (bf16[128,128]{1,0:T(8,128)(2,1)S(1)}, bf16[128,128]{1,0:T(8,128)(2,1)S(1)}, bf16[128,128]{1,0:T(8,128)(2,1)S(1)}, f32[2,128,128]{2,1,0:T(8,128)S(1)}) custom-call(s32[1]{0:T(128)} %bitcast.seq_ref, bf16[256,1024]{1,0:T(8,128)(2,1)S(1)} %copy-done, bf16[256,1024]{1,0:T(8,128)(2,1)S(1)} %copy-done.1, bf16[256,1024]{1,0:T(8,128)(2,1)S(1)} %copy-done.2, ...), custom_call_target="tpu_custom_call" | custom-call | bytes 10800000 | tf_op jit(solution)/shard_map/block_states/pallas_call | solution.py:203
  15.1 0.0 copy-start.8
  15.1 1.8 %collective-permute-start = (bf16[128,128]{1,0:T(8,128)(2,1)S(1)}, bf16[128,128]{1,0:T(8,128)(2,1)S(1)}, u32[]{:S(2)}, u32[]{:S(2)}) collective-permute-start(bf16[128,128]{1,0:T(8,128)(2,1)S(1)} %get-tuple-element.45), channel_id=1, source_target_pairs={{0,8},{4,12},{8,16},{12,20},{16,24},{20,28},{24,0},{28,4},{1,9},{5... | collective-permute-start | bytes 98312 | tf_op jit(solution)/shard_map/ppermute | solution.py:298
  16.9 2.4 %collective-permute-start.1 = (bf16[128,128]{1,0:T(8,128)(2,1)S(1)}, bf16[128,128]{1,0:T(8,128)(2,1)S(1)}, u32[]{:S(2)}, u32[]{:S(2)}) collective-permute-start(bf16[128,128]{1,0:T(8,128)(2,1)S(1)} %get-tuple-element.46), channel_id=1, source_target_pairs={{0,16},{4,20},{8,24},{12,28},{16,0},{20,4},{24,8},{28,12},{1,17},{... | collective-permute-start | bytes 98312 | tf_op jit(solution)/shard_map/ppermute | solution.py:298
  19.3 1.4 %collective-permute-start.2 = (bf16[128,128]{1,0:T(8,128)(2,1)S(1)}, bf16[128,128]{1,0:T(8,128)(2,1)S(1)}, u32[]{:S(2)}, u32[]{:S(2)}) collective-permute-start(bf16[128,128]{1,0:T(8,128)(2,1)S(1)} %get-tuple-element.47), channel_id=1, source_target_pairs={{0,24},{4,28},{8,0},{12,4},{16,8},{20,12},{24,16},{28,20},{1,25},{... | collective-permute-start | bytes 98312 | tf_op jit(solution)/shard_map/ppermute | solution.py:298
  20.7 0.0 copy-done.8
  20.7 6.3 %local_parts.1 = (f32[256,1024]{1,0:T(8,128)S(1)}, f32[256,1024]{1,0:T(8,128)S(1)}, f32[8,128]{1,0:T(8,128)S(1)}) custom-call(bf16[256,1024]{1,0:T(8,128)(2,1)S(1)} %copy-done, bf16[256,1024]{1,0:T(8,128)(2,1)S(1)} %copy-done.1, bf16[256,1024]{1,0:T(8,128)(2,1)S(1)} %copy-done.2, bf16[256,1024]{1,0:T(8,128)(2,1)S(1)} %copy-done.3, ...), custom_call_target="tpu_custom_call" | custom-call | bytes 23400000 | tf_op jit(solution)/shard_map/local_parts/pallas_call | solution.py:285
  27.0 0.0 copy-start.4
  27.1 1.0 %copy-done.4 = f32[256,1024]{1,0:T(8,128)} copy-done((f32[256,1024]{1,0:T(8,128)}, f32[256,1024]{1,0:T(8,128)S(1)}, u32[]{:S(2)}) %copy-start.4) | copy-done | bytes 1048600
  28.0 0.0 copy-start.6
  28.0 1.0 %copy-done.6 = f32[256,1024]{1,0:T(8,128)} copy-done((f32[256,1024]{1,0:T(8,128)}, f32[256,1024]{1,0:T(8,128)S(1)}, u32[]{:S(2)}) %copy-start.6) | copy-done | bytes 1048600
  29.0 4.7 %collective-permute-done.refs_0_ = bf16[128,128]{1,0:T(8,128)(2,1)S(1)} collective-permute-done((bf16[128,128]{1,0:T(8,128)(2,1)S(1)}, bf16[128,128]{1,0:T(8,128)(2,1)S(1)}, u32[]{:S(2)}, u32[]{:S(2)}) %collective-permute-start) | collective-permute-done | bytes 32800 | tf_op jit(solution)/shard_map/ppermute | solution.py:298
  33.7 6.0 %collective-permute-done.1.refs_1_ = bf16[128,128]{1,0:T(8,128)(2,1)S(1)} collective-permute-done((bf16[128,128]{1,0:T(8,128)(2,1)S(1)}, bf16[128,128]{1,0:T(8,128)(2,1)S(1)}, u32[]{:S(2)}, u32[]{:S(2)}) %collective-permute-start.1) | collective-permute-done | bytes 32800 | tf_op jit(solution)/shard_map/ppermute | solution.py:298
  39.7 0.0 collective-permute-done.2.refs_2_
  39.7 0.1 pair_states.1
  39.8 0.0 all-to-all-done.refs_0_
  39.8 1.5 %collective-permute-start.3 = (bf16[2,128,128]{2,1,0:T(8,128)(2,1)S(1)}, bf16[2,128,128]{2,1,0:T(8,128)(2,1)S(1)}, u32[]{:S(2)}, u32[]{:S(2)}) collective-permute-start(bf16[2,128,128]{2,1,0:T(8,128)(2,1)S(1)} %get-tuple-element.52), channel_id=1, source_target_pairs={{0,4},{4,0},{8,12},{12,8},{16,20},{20,16},{24,28},{28,24},{1,5},{5... | collective-permute-start | bytes 196616 | tf_op jit(solution)/shard_map/ppermute | solution.py:302
  41.3 4.0 %filter_lags.1 = f32[8,8,256]{2,1,0:T(8,128)} custom-call(bf16[32,64,256]{2,1,0:T(8,128)(2,1)S(1)} %all-to-all-done.refs_0_), custom_call_target="tpu_custom_call" | custom-call | bytes 14400000 | tf_op jit(solution)/shard_map/filter_lags/pallas_call | solution.py:454
  45.3 0.0 collective-permute-done.3.refs_3_
  45.4 3.4 %all-to-all-start.1 = ((f32[8,8,256]{2,1,0:T(8,128)}), f32[8,8,256]{2,1,0:T(8,128)S(1)}, u32[]{:S(2)}, u32[]{:S(2)}) async-start(f32[8,8,256]{2,1,0:T(8,128)} %filter_lags.1), calls=%async_computation.1 | async-start | bytes 131072 | tf_op jit(solution)/shard_map/all_to_all | solution.py:506
  48.7 0.0 copy-start.7
  48.7 1.2 %copy-done.7 = f32[256,1024]{1,0:T(8,128)S(1)} copy-done((f32[256,1024]{1,0:T(8,128)S(1)}, f32[256,1024]{1,0:T(8,128)}, u32[]{:S(2)}) %copy-start.7) | copy-done | bytes 1048600
  49.9 0.0 copy-start.5
  49.9 2.1 %conv_outputs.1 = bf16[256,1024]{1,0:T(8,128)(2,1)} custom-call(f32[256,1024]{1,0:T(8,128)S(1)} %copy-done.7, f32[3,16,8,128]{3,2,1,0:T(8,128)S(1)} %bitcast.17, f32[2,128,128]{2,1,0:T(8,128)S(1)} %get-tuple-element.50.refs_2_, bf16[2,128,128]{2,1,0:T(8,128)(2,1)S(1)} %collective-permute-done.3.refs_3_, bf16[256,1024]{1,0:T(8,128)(2,1)S(1)} %copy-done), custom_call_target="tpu_custom_call" | custom-call | bytes 7200000 | tf_op jit(solution)/shard_map/conv_outputs/pallas_call | solution.py:351
  52.0 0.0 copy-done.5
  52.1 2.4 %grad_outputs.1 = (bf16[256,1024]{1,0:T(8,128)(2,1)}, bf16[256,1024]{1,0:T(8,128)(2,1)}) custom-call(f32[256,1024]{1,0:T(8,128)S(1)} %copy-done.5, f32[3,16,8,128]{3,2,1,0:T(8,128)S(1)} %bitcast.18, f32[2,128,128]{2,1,0:T(8,128)S(1)} %get-tuple-element.50.refs_2_, bf16[2,128,128]{2,1,0:T(8,128)(2,1)S(1)} %collective-permute-done.3.refs_3_, ...), custom_call_target="tpu_custom_call" | custom-call | bytes 7200000 | tf_op jit(solution)/shard_map/grad_outputs/pallas_call | solution.py:351
  54.4 1.1 %all-to-all-done.1 = f32[8,8,256]{2,1,0:T(8,128)S(1)} async-done(((f32[8,8,256]{2,1,0:T(8,128)}), f32[8,8,256]{2,1,0:T(8,128)S(1)}, u32[]{:S(2)}, u32[]{:S(2)}) %all-to-all-start.1) | async-done | bytes 65568 | tf_op jit(solution)/shard_map/all_to_all | solution.py:506
  55.6 0.6 %copy.12 = f32[256,64]{0,1:T(8,128)} copy(f32[256,64]{0,1:T(8,128)S(1)} %bitcast.20) | data formatting | bytes 131072
  (3 shorter events, 0.1 us)
Async XLA Ops:
  3.6 7.4 %copy-start.9 = (f32[256,16]{0,1:T(8,128)S(1)}, f32[256,16]{0,1:T(8,128)}, u32[]{:S(2)}) copy-start(f32[256,16]{0,1:T(8,128)} %param.12) | copy-start | bytes 49156
  3.6 7.4 %copy-start.10 = (f32[256,16]{0,1:T(8,128)S(1)}, f32[256,16]{0,1:T(8,128)}, u32[]{:S(2)}) copy-start(f32[256,16]{0,1:T(8,128)} %param.11) | copy-start | bytes 49156
  3.6 7.5 %copy-start.1 = (bf16[256,1024]{1,0:T(8,128)(2,1)S(1)}, bf16[256,1024]{1,0:T(8,128)(2,1)}, u32[]{:S(2)}) copy-start(bf16[256,1024]{1,0:T(8,128)(2,1)} %refs_5_) | copy-start | bytes 1572868
  3.6 7.5 %copy-start.2 = (bf16[256,1024]{1,0:T(8,128)(2,1)S(1)}, bf16[256,1024]{1,0:T(8,128)(2,1)}, u32[]{:S(2)}) copy-start(bf16[256,1024]{1,0:T(8,128)(2,1)} %refs_4_.1) | copy-start | bytes 1572868
  3.7 7.5 %copy-start.3 = (bf16[256,1024]{1,0:T(8,128)(2,1)S(1)}, bf16[256,1024]{1,0:T(8,128)(2,1)}, u32[]{:S(2)}) copy-start(bf16[256,1024]{1,0:T(8,128)(2,1)} %o_ref.1) | copy-start | bytes 1572868
  3.7 36.1 %all-to-all-start = ((bf16[32,64,256]{2,1,0:T(8,128)(2,1)}), bf16[32,64,256]{2,1,0:T(8,128)(2,1)S(1)}, u32[]{:S(2)}, u32[]{:S(2)}) async-start(bf16[32,64,256]{2,1,0:T(8,128)(2,1)} %pack_signals.1), calls=%async_computation | async-start | bytes 2097152 | tf_op jit(solution)/shard_map/all_to_all | solution.py:481
  11.0 1.0 %copy-start = (bf16[256,1024]{1,0:T(8,128)(2,1)S(1)}, bf16[256,1024]{1,0:T(8,128)(2,1)}, u32[]{:S(2)}) copy-start(bf16[256,1024]{1,0:T(8,128)(2,1)} %refs_4_) | copy-start | bytes 1572868
  15.1 5.7 %copy-start.8 = (f32[1024]{0:T(1024)S(1)}, f32[1024]{0:T(1024)}, u32[]{:S(2)}) copy-start(f32[1024]{0:T(1024)} %param.13) | copy-start | bytes 12292
  15.1 18.7 %collective-permute-start = (bf16[128,128]{1,0:T(8,128)(2,1)S(1)}, bf16[128,128]{1,0:T(8,128)(2,1)S(1)}, u32[]{:S(2)}, u32[]{:S(2)}) collective-permute-start(bf16[128,128]{1,0:T(8,128)(2,1)S(1)} %get-tuple-element.45), channel_id=1, source_target_pairs={{0,8},{4,12},{8,16},{12,20},{16,24},{20,28},{24,0},{28,4},{1,9},{5... | collective-permute-start | bytes 98312 | tf_op jit(solution)/shard_map/ppermute | solution.py:298
  16.9 22.8 %collective-permute-start.1 = (bf16[128,128]{1,0:T(8,128)(2,1)S(1)}, bf16[128,128]{1,0:T(8,128)(2,1)S(1)}, u32[]{:S(2)}, u32[]{:S(2)}) collective-permute-start(bf16[128,128]{1,0:T(8,128)(2,1)S(1)} %get-tuple-element.46), channel_id=1, source_target_pairs={{0,16},{4,20},{8,24},{12,28},{16,0},{20,4},{24,8},{28,12},{1,17},{... | collective-permute-start | bytes 98312 | tf_op jit(solution)/shard_map/ppermute | solution.py:298
  19.3 20.4 %collective-permute-start.2 = (bf16[128,128]{1,0:T(8,128)(2,1)S(1)}, bf16[128,128]{1,0:T(8,128)(2,1)S(1)}, u32[]{:S(2)}, u32[]{:S(2)}) collective-permute-start(bf16[128,128]{1,0:T(8,128)(2,1)S(1)} %get-tuple-element.47), channel_id=1, source_target_pairs={{0,24},{4,28},{8,0},{12,4},{16,8},{20,12},{24,16},{28,20},{1,25},{... | collective-permute-start | bytes 98312 | tf_op jit(solution)/shard_map/ppermute | solution.py:298
  27.0 1.0 %copy-start.4 = (f32[256,1024]{1,0:T(8,128)}, f32[256,1024]{1,0:T(8,128)S(1)}, u32[]{:S(2)}) copy-start(f32[256,1024]{1,0:T(8,128)S(1)} %get-tuple-element.54.refs_0_) | copy-start | bytes 3145732
  28.0 1.0 %copy-start.6 = (f32[256,1024]{1,0:T(8,128)}, f32[256,1024]{1,0:T(8,128)S(1)}, u32[]{:S(2)}) copy-start(f32[256,1024]{1,0:T(8,128)S(1)} %get-tuple-element.41.refs_0_) | copy-start | bytes 3145732
  39.8 5.6 %collective-permute-start.3 = (bf16[2,128,128]{2,1,0:T(8,128)(2,1)S(1)}, bf16[2,128,128]{2,1,0:T(8,128)(2,1)S(1)}, u32[]{:S(2)}, u32[]{:S(2)}) collective-permute-start(bf16[2,128,128]{2,1,0:T(8,128)(2,1)S(1)} %get-tuple-element.52), channel_id=1, source_target_pairs={{0,4},{4,0},{8,12},{12,8},{16,20},{20,16},{24,28},{28,24},{1,5},{5... | collective-permute-start | bytes 196616 | tf_op jit(solution)/shard_map/ppermute | solution.py:302
  45.4 10.2 %all-to-all-start.1 = ((f32[8,8,256]{2,1,0:T(8,128)}), f32[8,8,256]{2,1,0:T(8,128)S(1)}, u32[]{:S(2)}, u32[]{:S(2)}) async-start(f32[8,8,256]{2,1,0:T(8,128)} %filter_lags.1), calls=%async_computation.1 | async-start | bytes 131072 | tf_op jit(solution)/shard_map/all_to_all | solution.py:506
  48.7 1.2 %copy-start.7 = (f32[256,1024]{1,0:T(8,128)S(1)}, f32[256,1024]{1,0:T(8,128)}, u32[]{:S(2)}) copy-start(f32[256,1024]{1,0:T(8,128)} %copy-done.6) | copy-start | bytes 3145732
  49.9 2.1 %copy-start.5 = (f32[256,1024]{1,0:T(8,128)S(1)}, f32[256,1024]{1,0:T(8,128)}, u32[]{:S(2)}) copy-start(f32[256,1024]{1,0:T(8,128)} %copy-done.4) | copy-start | bytes 3145732

commit v13 on v12

--- a/solution.py
+++ b/solution.py
@@ -25,7 +25,7 @@
 
 
 def product(first, second):
-    return (first.astype(F32) * second.astype(F32)).astype(BF16)
+    return first * second
 
 
 def one_hot(rows, cols, column_of):
@@ -315,51 +315,100 @@
     lax.fori_loop(0, tok_rows, step, held, unroll=8)
 
 
-def output_kernel(side, count, *refs):
-    part_ref, coef_ref, kept_ref, given_ref = refs[:4]
-    factor_refs, hbm_refs = refs[4 : 4 + count], refs[4 + count : 4 + 2 * count]
-    edge_ref, out_refs, sems = refs[4 + 2 * count], refs[5 + 2 * count : -1], refs[-1]
-    tok_rows, width = part_ref.shape
-    tiles = width // LANES
-
-    def departure(i, tile):
-        place = (slice(None), pl.ds(tile * LANES, LANES))
-        return pltpu.make_async_copy(
-            out_refs[i].at[place], hbm_refs[i].at[place], sems.at[i, tile]
-        )
-
+def edge_kernel(coef_ref, kept_ref, given_ref, edge_ref):
+    modes, tiles = coef_ref.shape[1:3]
+    tok_rows = edge_ref.shape[0] // tiles - GAP
+    fill_side(0, edge_ref, coef_ref, kept_ref, given_ref, tok_rows, tiles)
+
+
+def fill_side(side, edge_ref, coef_ref, kept_ref, given_ref, tok_rows, tiles):
     total = kept_ref[side] + given_ref[side].astype(F32)
     held = [total[m * tiles : (m + 1) * tiles] for m in range(coef_ref.shape[1])]
     start, move = ((0, 1), (tok_rows - 1, -1))[side]
     fill_edge(edge_ref, held, coef_ref, tok_rows, tiles, start, move)
-    for tile in range(tiles):
+
+
+def edge_terms(tok_rows, coefs, kept, given):
+    return pl.pallas_call(
+        edge_kernel,
+        out_shape=jax.ShapeDtypeStruct(token_shape(tok_rows, coefs.shape[2]), F32),
+        compiler_params=pltpu.CompilerParams(vmem_limit_bytes=VMEM_BYTES),
+        cost_estimate=takes(1.3),
+        name="edge_terms",
+    )(coefs, kept, given)
+
+
+def multiply_out(part_ref, edge_ref, factor_refs, out_refs, hbm_refs, sems):
+    tok_rows, width = part_ref.shape
+    copies = []
+    for tile in range(width // LANES):
         cols = slice(tile * LANES, (tile + 1) * LANES)
         value = part_ref[:, cols] + edge_ref[tile_rows(tok_rows, tile), :]
-        for i in range(count):
-            out_refs[i][:, cols] = (value * factor_refs[i][:, cols].astype(F32)).astype(BF16)
-            departure(i, tile).start()
-    for i in range(count):
-        for tile in range(tiles):
-            departure(i, tile).wait()
-
-
-def outputs(side, name, part, coefs, kept, given, *factors):
+        for i, (factor_ref, out_ref, hbm_ref) in enumerate(zip(factor_refs, out_refs, hbm_refs)):
+            out_ref[:, cols] = (value * factor_ref[:, cols].astype(F32)).astype(BF16)
+            place = (slice(None), pl.ds(tile * LANES, LANES))
+            copies.append(
+                pltpu.make_async_copy(out_ref.at[place], hbm_ref.at[place], sems.at[i, tile])
+            )
+            copies[-1].start()
+    return copies
+
+
+def conv_kernel(
+    part_ref, edge_ref, q_ref, coef_ref, kept_ref, given_ref,
+    layer_hbm, next_ref, layer_ref, sems,
+):
+    tok_rows, width = part_ref.shape
+    copies = multiply_out(part_ref, edge_ref, [q_ref], [layer_ref], [layer_hbm], sems)
+    fill_side(1, next_ref, coef_ref, kept_ref, given_ref, tok_rows, width // LANES)
+    for copy in copies:
+        copy.wait()
+
+
+def conv_outputs(part, edge, query_proj, coefs, kept, given):
     tok_rows, width = part.shape
-    tiles = coefs.shape[2]
-    count = len(factors)
-    args = (part, coefs, kept, given, *factors)
+    whole = pl.BlockSpec(memory_space=pltpu.VMEM)
     return pl.pallas_call(
-        functools.partial(output_kernel, side, count),
-        in_specs=[pl.BlockSpec(memory_space=pltpu.VMEM)] * len(args),
-        out_specs=[pl.BlockSpec(memory_space=pl.ANY)] * count,
-        out_shape=[jax.ShapeDtypeStruct((tok_rows, width), BF16)] * count,
-        scratch_shapes=[pltpu.VMEM(token_shape(tok_rows, tiles), F32)]
-        + [pltpu.VMEM((tok_rows, width), BF16)] * count
-        + [pltpu.SemaphoreType.DMA((count, tiles))],
+        conv_kernel,
+        in_specs=[whole] * 6,
+        out_specs=[pl.BlockSpec(memory_space=pl.ANY), whole],
+        out_shape=[
+            jax.ShapeDtypeStruct((tok_rows, width), BF16),
+            jax.ShapeDtypeStruct(edge.shape, F32),
+        ],
+        scratch_shapes=[
+            pltpu.VMEM((tok_rows, width), BF16),
+            pltpu.SemaphoreType.DMA((1, width // LANES)),
+        ],
         compiler_params=pltpu.CompilerParams(vmem_limit_bytes=VMEM_BYTES),
         cost_estimate=takes(2.0),
-        name=name,
-    )(*args)
+        name="conv_outputs",
+    )(part, edge, query_proj, coefs, kept, given)
+
+
+def grad_kernel(
+    part_ref, edge_ref, v_ref, k_ref, key_hbm, value_hbm, key_ref, value_ref, sems
+):
+    copies = multiply_out(
+        part_ref, edge_ref, [v_ref, k_ref], [key_ref, value_ref], [key_hbm, value_hbm], sems
+    )
+    for copy in copies:
+        copy.wait()
+
+
+def grad_outputs(part, edge, value_proj, key_proj):
+    tok_rows, width = part.shape
+    return pl.pallas_call(
+        grad_kernel,
+        in_specs=[pl.BlockSpec(memory_space=pltpu.VMEM)] * 4,
+        out_specs=[pl.BlockSpec(memory_space=pl.ANY)] * 2,
+        out_shape=[jax.ShapeDtypeStruct((tok_rows, width), BF16)] * 2,
+        scratch_shapes=[pltpu.VMEM((tok_rows, width), BF16)] * 2
+        + [pltpu.SemaphoreType.DMA((2, width // LANES))],
+        compiler_params=pltpu.CompilerParams(vmem_limit_bytes=VMEM_BYTES),
+        cost_estimate=takes(1.2),
+        name="grad_outputs",
+    )(part, edge, value_proj, key_proj)
 
 
 def lag_kernel(shards, chans, groups, owned, scale, *refs):
@@ -506,10 +555,9 @@
     lags = lax.all_to_all(lags, "seq", split_axis=0, concat_axis=0, tiled=True)
     filter_grad = lags.reshape(shards * owned, tok_rows).T
     query_proj, key_proj, value_proj, _ = signals
-    (layer_out,) = outputs(0, "conv_outputs", conv_part, coefs, kept, given, query_proj)
-    key_grad, value_grad = outputs(
-        1, "grad_outputs", grad_part, coefs, kept, given, value_proj, key_proj
-    )
+    edge = edge_terms(tok_rows, coefs, kept, given)
+    layer_out, edge = conv_outputs(conv_part, edge, query_proj, coefs, kept, given)
+    key_grad, value_grad = grad_outputs(grad_part, edge, value_proj, key_proj)
     return (layer_out, key_grad, value_grad, filter_grad)
 
 

time: 56.5 us -> 57.1 us (1.011)
  waiting for transfers between devices: 11.8 us -> 14.6 us
  local copies, waits for them, and re-layouts: 4.78 us -> 3.34 us
  Pallas kernels: 20.9 us -> 20.1 us
    all_to_all x1, waiting for transfers between devices: 1.11 us -> 2.94 us  [per_device(): lags = lax.all_to_all(lags, 'seq', split_axis=0, concat_axis=0, tiled=True)]
    unnamed x23 -> x25, local copies, waits for them, and re-layouts: 4.7 us -> 3.26 us
    ppermute x3, waiting for transfers between devices: 10.7 us -> 11.6 us  [along_column(): return lax.ppermute(state, 'seq', route)]
    pallas_call x1, Pallas kernels: 0.1 us -> 0.73 us  [pair_states(): pl.pallas_call(pair_kernel, in_specs=[pl.BlockSpec(memory_space=pltpu.SME...]
    pallas_call x2 -> x3, Pallas kernels: 4.48 us -> 3.85 us  [the longest x1 1.52 us: conv_outputs(): pl.pallas_call(conv_kernel, in_specs=[whole] * 6, out_specs=[pl.BlockSpec...]
    pallas_call x1, Pallas kernels: 4.02 us -> 3.4 us  [filter_lags(): pl.pallas_call(functools.partial(lag_kernel, shards, chans, groups, owned...]
  transfers between devices with their start and end apart: 6 -> 6, of which waited for: 3 -> 3; matrix products, arithmetic and copies ran while one was open for 0% -> 0% of each run, Pallas kernels for 32% -> 30%
where the time goes in v13:
time: 57.1 us; the launch traced here: 56.9 us
  Pallas kernels  20.1 us (35%)
  starting transfers between devices  17.9 us (31%)
  waiting for transfers between devices  14.6 us (26%)
  local copies, waits for them, and re-layouts  3.34 us (6%)
  between operations  0.89 us (2%)
    ppermute x3, waiting for transfers between devices, along_column(): return lax.ppermute(state, 'seq', route)  11.6 us
    all_to_all x1, starting transfers between devices, per_device(): lax.all_to_all(send, ('seq', 'chan'), split_axis=0, concat_axis=0, tiled=...  7.31 us
    pallas_call x1, Pallas kernels, local_parts(): pl.pallas_call(local_kernel, out_shape=[jax.ShapeDtypeStruct((tok_rows, w...  6.22 us
    ppermute x3, starting transfers between devices, along_column(): return lax.ppermute(state, 'seq', route)  5.65 us
    all_to_all x1, starting transfers between devices, per_device(): lags = lax.all_to_all(lags, 'seq', split_axis=0, concat_axis=0, tiled=True)  3.48 us
    pallas_call x1, Pallas kernels, filter_lags(): pl.pallas_call(functools.partial(lag_kernel, shards, chans, groups, owned...  3.4 us
    unnamed x25, local copies, waits for them, and re-layouts  3.26 us
    pallas_call x1, Pallas kernels, block_states(): pl.pallas_call(state_kernel, in_specs=[pl.BlockSpec(memory_space=pltpu.SM...  2.98 us
  transfers between devices with their start and end apart: 6, of which 3 were waited for; matrix products, arithmetic and copies ran while one was open for 0% of the time, Pallas kernels for 30%

profile of v13, /device:TPU:0, one launch (start us, length us, event | category | flops | bytes accessed | tf_op | source)
XLA Modules:
  0.0 56.9 jit_solution(11907408488382302622)
XLA Ops:
  0.6 0.0 copy-start.10
  0.6 0.0 copy-start.11
  0.7 2.9 %pack_signals.1 = bf16[32,64,256]{2,1,0:T(8,128)(2,1)} custom-call(bf16[256,1024]{1,0:T(8,128)(2,1)} %k_ref.2, bf16[256,1024]{1,0:T(8,128)(2,1)} %v_ref.2, bf16[256,1024]{1,0:T(8,128)(2,1)} %o_ref.1, bf16[256,1024]{1,0:T(8,128)(2,1)} %q_ref.2), custom_call_target="tpu_custom_call" | custom-call | bytes 10800000 | tf_op jit(solution)/shard_map/pack_signals/pallas_call | solution.py:101
  3.6 0.0 copy-start
  3.6 0.0 copy-start.1
  3.6 0.0 copy-start.2
  3.6 0.0 copy-start.3
  3.7 7.3 %all-to-all-start = ((bf16[32,64,256]{2,1,0:T(8,128)(2,1)}), bf16[32,64,256]{2,1,0:T(8,128)(2,1)S(1)}, u32[]{:S(2)}, u32[]{:S(2)}) async-start(bf16[32,64,256]{2,1,0:T(8,128)(2,1)} %pack_signals.1), calls=%async_computation | async-start | bytes 2097152 | tf_op jit(solution)/shard_map/all_to_all | solution.py:530
  11.0 0.0 copy-done.10
  11.0 0.0 copy-done.11
  11.1 0.1 broadcast_in_dim.11
  11.1 0.0 copy-done
  11.1 0.0 copy-done.1
  11.2 0.0 copy-done.2
  11.2 0.0 copy-done.3
  11.2 0.0 copy-start.9
  11.2 3.0 %block_states.1 = (bf16[128,128]{1,0:T(8,128)(2,1)S(1)}, bf16[128,128]{1,0:T(8,128)(2,1)S(1)}, bf16[128,128]{1,0:T(8,128)(2,1)S(1)}, f32[2,128,128]{2,1,0:T(8,128)S(1)}) custom-call(s32[1]{0:T(128)} %bitcast.seq_ref, bf16[256,1024]{1,0:T(8,128)(2,1)S(1)} %copy-done.2, bf16[256,1024]{1,0:T(8,128)(2,1)S(1)} %copy-done, bf16[256,1024]{1,0:T(8,128)(2,1)S(1)} %copy-done.1, ...), custom_call_target="tpu_custom_call" | custom-call | bytes 10800000 | tf_op jit(solution)/shard_map/block_states/pallas_call | solution.py:203
  14.2 1.8 %collective-permute-start = (bf16[128,128]{1,0:T(8,128)(2,1)S(1)}, bf16[128,128]{1,0:T(8,128)(2,1)S(1)}, u32[]{:S(2)}, u32[]{:S(2)}) collective-permute-start(bf16[128,128]{1,0:T(8,128)(2,1)S(1)} %get-tuple-element.47), channel_id=1, source_target_pairs={{0,8},{4,12},{8,16},{12,20},{16,24},{20,28},{24,0},{28,4},{1,9},{5... | collective-permute-start | bytes 98312 | tf_op jit(solution)/shard_map/ppermute | solution.py:298
  16.0 2.4 %collective-permute-start.1 = (bf16[128,128]{1,0:T(8,128)(2,1)S(1)}, bf16[128,128]{1,0:T(8,128)(2,1)S(1)}, u32[]{:S(2)}, u32[]{:S(2)}) collective-permute-start(bf16[128,128]{1,0:T(8,128)(2,1)S(1)} %get-tuple-element.48), channel_id=1, source_target_pairs={{0,16},{4,20},{8,24},{12,28},{16,0},{20,4},{24,8},{28,12},{1,17},{... | collective-permute-start | bytes 98312 | tf_op jit(solution)/shard_map/ppermute | solution.py:298
  18.4 1.4 %collective-permute-start.2 = (bf16[128,128]{1,0:T(8,128)(2,1)S(1)}, bf16[128,128]{1,0:T(8,128)(2,1)S(1)}, u32[]{:S(2)}, u32[]{:S(2)}) collective-permute-start(bf16[128,128]{1,0:T(8,128)(2,1)S(1)} %get-tuple-element.49), channel_id=1, source_target_pairs={{0,24},{4,28},{8,0},{12,4},{16,8},{20,12},{24,16},{28,20},{1,25},{... | collective-permute-start | bytes 98312 | tf_op jit(solution)/shard_map/ppermute | solution.py:298
  19.8 0.0 copy-done.9
  19.8 6.2 %local_parts.1 = (f32[256,1024]{1,0:T(8,128)S(1)}, f32[256,1024]{1,0:T(8,128)S(1)}, f32[8,128]{1,0:T(8,128)S(1)}) custom-call(bf16[256,1024]{1,0:T(8,128)(2,1)S(1)} %copy-done.2, bf16[256,1024]{1,0:T(8,128)(2,1)S(1)} %copy-done, bf16[256,1024]{1,0:T(8,128)(2,1)S(1)} %copy-done.1, bf16[256,1024]{1,0:T(8,128)(2,1)S(1)} %copy-done.3, ...), custom_call_target="tpu_custom_call" | custom-call | bytes 23400000 | tf_op jit(solution)/shard_map/local_parts/pallas_call | solution.py:285
  26.1 0.0 copy-start.4
  26.1 1.0 %copy-done.4 = f32[256,1024]{1,0:T(8,128)} copy-done((f32[256,1024]{1,0:T(8,128)}, f32[256,1024]{1,0:T(8,128)S(1)}, u32[]{:S(2)}) %copy-start.4) | copy-done | bytes 1048600
  27.1 0.0 copy-start.6
  27.1 1.0 %copy-done.6 = f32[256,1024]{1,0:T(8,128)} copy-done((f32[256,1024]{1,0:T(8,128)}, f32[256,1024]{1,0:T(8,128)S(1)}, u32[]{:S(2)}) %copy-start.6) | copy-done | bytes 1048600
  28.0 5.7 %collective-permute-done.refs_0_ = bf16[128,128]{1,0:T(8,128)(2,1)S(1)} collective-permute-done((bf16[128,128]{1,0:T(8,128)(2,1)S(1)}, bf16[128,128]{1,0:T(8,128)(2,1)S(1)}, u32[]{:S(2)}, u32[]{:S(2)}) %collective-permute-start) | collective-permute-done | bytes 32800 | tf_op jit(solution)/shard_map/ppermute | solution.py:298
  33.7 6.0 %collective-permute-done.1.refs_1_ = bf16[128,128]{1,0:T(8,128)(2,1)S(1)} collective-permute-done((bf16[128,128]{1,0:T(8,128)(2,1)S(1)}, bf16[128,128]{1,0:T(8,128)(2,1)S(1)}, u32[]{:S(2)}, u32[]{:S(2)}) %collective-permute-start.1) | collective-permute-done | bytes 32800 | tf_op jit(solution)/shard_map/ppermute | solution.py:298
  39.7 0.0 collective-permute-done.2.refs_2_
  39.7 0.7 %pair_states.1 = (f32[2,128,128]{2,1,0:T(8,128)S(1)}, bf16[2,128,128]{2,1,0:T(8,128)(2,1)}) custom-call(s32[1]{0:T(128)} %bitcast.seq_ref, f32[3,16,8,128]{3,2,1,0:T(8,128)S(1)} %bitcast.16, f32[2,128,128]{2,1,0:T(8,128)S(1)} %get-tuple-element.45.own_ref, f32[8,128]{1,0:T(8,128)S(1)} %get-tuple-element.46._, ...), custom_call_target="tpu_custom_call" | custom-call | bytes 360000 | tf_op jit(solution)/shard_map/pair_states/pallas_call | solution.py:246
  40.4 0.0 all-to-all-done.refs_0_
  40.4 1.5 %collective-permute-start.3 = (bf16[2,128,128]{2,1,0:T(8,128)(2,1)}, bf16[2,128,128]{2,1,0:T(8,128)(2,1)S(1)}, u32[]{:S(2)}, u32[]{:S(2)}) collective-permute-start(bf16[2,128,128]{2,1,0:T(8,128)(2,1)} %get-tuple-element.54), channel_id=1, source_target_pairs={{0,4},{4,0},{8,12},{12,8},{16,20},{20,16},{24,28},{28,24},{1,5},{5... | collective-permute-start | bytes 196616 | tf_op jit(solution)/shard_map/ppermute | solution.py:302
  41.9 3.4 %filter_lags.1 = f32[8,8,256]{2,1,0:T(8,128)S(1)} custom-call(bf16[32,64,256]{2,1,0:T(8,128)(2,1)S(1)} %all-to-all-done.refs_0_), custom_call_target="tpu_custom_call" | custom-call | bytes 14400000 | tf_op jit(solution)/shard_map/filter_lags/pallas_call | solution.py:503
  45.3 0.0 copy-start.8
  45.3 0.6 %copy-done.8 = f32[8,8,256]{2,1,0:T(8,128)} copy-done((f32[8,8,256]{2,1,0:T(8,128)}, f32[8,8,256]{2,1,0:T(8,128)S(1)}, u32[]{:S(2)}) %copy-start.8) | copy-done | bytes 65560
  45.9 0.0 copy-start.7
  45.9 0.0 collective-permute-done.3.given_ref
  45.9 3.5 %all-to-all-start.1 = ((f32[8,8,256]{2,1,0:T(8,128)}), f32[8,8,256]{2,1,0:T(8,128)S(1)}, u32[]{:S(2)}, u32[]{:S(2)}) async-start(f32[8,8,256]{2,1,0:T(8,128)} %copy-done.8), calls=%async_computation.1 | async-start | bytes 131072 | tf_op jit(solution)/shard_map/all_to_all | solution.py:555
  49.4 1.2 %edge_terms.1.edge_ref = f32[2112,128]{1,0:T(8,128)S(1)} custom-call(f32[3,16,8,128]{3,2,1,0:T(8,128)S(1)} %bitcast.17, f32[2,128,128]{2,1,0:T(8,128)S(1)} %get-tuple-element.52.kept_ref, bf16[2,128,128]{2,1,0:T(8,128)(2,1)S(1)} %collective-permute-done.3.given_ref), custom_call_target="tpu_custom_call" | custom-call | bytes 4680000 | tf_op jit(solution)/shard_map/edge_terms/pallas_call | solution.py:332
  50.6 0.0 copy-done.7
  50.6 0.0 copy-start.5
  50.6 1.5 %conv_outputs.1 = (bf16[256,1024]{1,0:T(8,128)(2,1)}, f32[2112,128]{1,0:T(8,128)S(1)}) custom-call(f32[256,1024]{1,0:T(8,128)S(1)} %copy-done.7, f32[2112,128]{1,0:T(8,128)S(1)} %edge_terms.1.edge_ref, bf16[256,1024]{1,0:T(8,128)(2,1)S(1)} %copy-done.2, f32[3,16,8,128]{3,2,1,0:T(8,128)S(1)} %bitcast.18, f32[2,128,128]{2,1,0:T(8,128)S(1)} %get-tuple-element.52.kept_ref, ...), custom_call_target="tpu_custom_call" | custom-call | bytes 7200000 | tf_op jit(solution)/shard_map/conv_outputs/pallas_call | solution.py:371
  52.2 0.0 copy-done.5
  52.2 1.1 %grad_outputs.1 = (bf16[256,1024]{1,0:T(8,128)(2,1)}, bf16[256,1024]{1,0:T(8,128)(2,1)}) custom-call(f32[256,1024]{1,0:T(8,128)S(1)} %copy-done.5, f32[2112,128]{1,0:T(8,128)S(1)} %get-tuple-element.58.edge_ref, bf16[256,1024]{1,0:T(8,128)(2,1)S(1)} %copy-done.1, bf16[256,1024]{1,0:T(8,128)(2,1)S(1)} %copy-done), custom_call_target="tpu_custom_call" | custom-call | bytes 4320000 | tf_op jit(solution)/shard_map/grad_outputs/pallas_call | solution.py:401
  53.3 2.9 %all-to-all-done.1 = f32[8,8,256]{2,1,0:T(8,128)S(1)} async-done(((f32[8,8,256]{2,1,0:T(8,128)}), f32[8,8,256]{2,1,0:T(8,128)S(1)}, u32[]{:S(2)}, u32[]{:S(2)}) %all-to-all-start.1) | async-done | bytes 65568 | tf_op jit(solution)/shard_map/all_to_all | solution.py:555
  56.3 0.6 %copy.12 = f32[256,64]{0,1:T(8,128)} copy(f32[256,64]{0,1:T(8,128)S(1)} %bitcast.20) | data formatting | bytes 131072
  (3 shorter events, 0.1 us)
Async XLA Ops:
  0.6 10.3 %copy-start.10 = (f32[256,16]{0,1:T(8,128)S(1)}, f32[256,16]{0,1:T(8,128)}, u32[]{:S(2)}) copy-start(f32[256,16]{0,1:T(8,128)} %param.12) | copy-start | bytes 49156
  0.6 10.3 %copy-start.11 = (f32[256,16]{0,1:T(8,128)S(1)}, f32[256,16]{0,1:T(8,128)}, u32[]{:S(2)}) copy-start(f32[256,16]{0,1:T(8,128)} %param.11) | copy-start | bytes 49156
  3.6 7.5 %copy-start = (bf16[256,1024]{1,0:T(8,128)(2,1)S(1)}, bf16[256,1024]{1,0:T(8,128)(2,1)}, u32[]{:S(2)}) copy-start(bf16[256,1024]{1,0:T(8,128)(2,1)} %k_ref.2) | copy-start | bytes 1572868
  3.6 7.5 %copy-start.1 = (bf16[256,1024]{1,0:T(8,128)(2,1)S(1)}, bf16[256,1024]{1,0:T(8,128)(2,1)}, u32[]{:S(2)}) copy-start(bf16[256,1024]{1,0:T(8,128)(2,1)} %v_ref.2) | copy-start | bytes 1572868
  3.6 7.5 %copy-start.2 = (bf16[256,1024]{1,0:T(8,128)(2,1)S(1)}, bf16[256,1024]{1,0:T(8,128)(2,1)}, u32[]{:S(2)}) copy-start(bf16[256,1024]{1,0:T(8,128)(2,1)} %q_ref.2) | copy-start | bytes 1572868
  3.6 7.5 %copy-start.3 = (bf16[256,1024]{1,0:T(8,128)(2,1)S(1)}, bf16[256,1024]{1,0:T(8,128)(2,1)}, u32[]{:S(2)}) copy-start(bf16[256,1024]{1,0:T(8,128)(2,1)} %o_ref.1) | copy-start | bytes 1572868
  3.7 36.7 %all-to-all-start = ((bf16[32,64,256]{2,1,0:T(8,128)(2,1)}), bf16[32,64,256]{2,1,0:T(8,128)(2,1)S(1)}, u32[]{:S(2)}, u32[]{:S(2)}) async-start(bf16[32,64,256]{2,1,0:T(8,128)(2,1)} %pack_signals.1), calls=%async_computation | async-start | bytes 2097152 | tf_op jit(solution)/shard_map/all_to_all | solution.py:530
  11.2 8.7 %copy-start.9 = (f32[1024]{0:T(1024)S(1)}, f32[1024]{0:T(1024)}, u32[]{:S(2)}) copy-start(f32[1024]{0:T(1024)} %param.13) | copy-start | bytes 12292
  14.2 19.5 %collective-permute-start = (bf16[128,128]{1,0:T(8,128)(2,1)S(1)}, bf16[128,128]{1,0:T(8,128)(2,1)S(1)}, u32[]{:S(2)}, u32[]{:S(2)}) collective-permute-start(bf16[128,128]{1,0:T(8,128)(2,1)S(1)} %get-tuple-element.47), channel_id=1, source_target_pairs={{0,8},{4,12},{8,16},{12,20},{16,24},{20,28},{24,0},{28,4},{1,9},{5... | collective-permute-start | bytes 98312 | tf_op jit(solution)/shard_map/ppermute | solution.py:298
  16.0 23.7 %collective-permute-start.1 = (bf16[128,128]{1,0:T(8,128)(2,1)S(1)}, bf16[128,128]{1,0:T(8,128)(2,1)S(1)}, u32[]{:S(2)}, u32[]{:S(2)}) collective-permute-start(bf16[128,128]{1,0:T(8,128)(2,1)S(1)} %get-tuple-element.48), channel_id=1, source_target_pairs={{0,16},{4,20},{8,24},{12,28},{16,0},{20,4},{24,8},{28,12},{1,17},{... | collective-permute-start | bytes 98312 | tf_op jit(solution)/shard_map/ppermute | solution.py:298
  18.4 21.3 %collective-permute-start.2 = (bf16[128,128]{1,0:T(8,128)(2,1)S(1)}, bf16[128,128]{1,0:T(8,128)(2,1)S(1)}, u32[]{:S(2)}, u32[]{:S(2)}) collective-permute-start(bf16[128,128]{1,0:T(8,128)(2,1)S(1)} %get-tuple-element.49), channel_id=1, source_target_pairs={{0,24},{4,28},{8,0},{12,4},{16,8},{20,12},{24,16},{28,20},{1,25},{... | collective-permute-start | bytes 98312 | tf_op jit(solution)/shard_map/ppermute | solution.py:298
  26.1 1.0 %copy-start.4 = (f32[256,1024]{1,0:T(8,128)}, f32[256,1024]{1,0:T(8,128)S(1)}, u32[]{:S(2)}) copy-start(f32[256,1024]{1,0:T(8,128)S(1)} %get-tuple-element.57.part_ref) | copy-start | bytes 3145732
  27.1 1.0 %copy-start.6 = (f32[256,1024]{1,0:T(8,128)}, f32[256,1024]{1,0:T(8,128)S(1)}, u32[]{:S(2)}) copy-start(f32[256,1024]{1,0:T(8,128)S(1)} %get-tuple-element.43.part_ref) | copy-start | bytes 3145732
  40.4 5.5 %collective-permute-start.3 = (bf16[2,128,128]{2,1,0:T(8,128)(2,1)}, bf16[2,128,128]{2,1,0:T(8,128)(2,1)S(1)}, u32[]{:S(2)}, u32[]{:S(2)}) collective-permute-start(bf16[2,128,128]{2,1,0:T(8,128)(2,1)} %get-tuple-element.54), channel_id=1, source_target_pairs={{0,4},{4,0},{8,12},{12,8},{16,20},{20,16},{24,28},{28,24},{1,5},{5... | collective-permute-start | bytes 196616 | tf_op jit(solution)/shard_map/ppermute | solution.py:302
  45.3 0.6 %copy-start.8 = (f32[8,8,256]{2,1,0:T(8,128)}, f32[8,8,256]{2,1,0:T(8,128)S(1)}, u32[]{:S(2)}) copy-start(f32[8,8,256]{2,1,0:T(8,128)S(1)} %filter_lags.1) | copy-start | bytes 196612
  45.9 4.7 %copy-start.7 = (f32[256,1024]{1,0:T(8,128)S(1)}, f32[256,1024]{1,0:T(8,128)}, u32[]{:S(2)}) copy-start(f32[256,1024]{1,0:T(8,128)} %copy-done.6) | copy-start | bytes 3145732
  45.9 10.3 %all-to-all-start.1 = ((f32[8,8,256]{2,1,0:T(8,128)}), f32[8,8,256]{2,1,0:T(8,128)S(1)}, u32[]{:S(2)}, u32[]{:S(2)}) async-start(f32[8,8,256]{2,1,0:T(8,128)} %copy-done.8), calls=%async_computation.1 | async-start | bytes 131072 | tf_op jit(solution)/shard_map/all_to_all | solution.py:555
  50.6 1.5 %copy-start.5 = (f32[256,1024]{1,0:T(8,128)S(1)}, f32[256,1024]{1,0:T(8,128)}, u32[]{:S(2)}) copy-start(f32[256,1024]{1,0:T(8,128)} %copy-done.4) | copy-start | bytes 3145732

commit v14 on v11

--- a/solution.py
+++ b/solution.py
@@ -14,7 +14,7 @@
 SUBLANES = 8
 GAP = 8
 VMEM_BYTES = 16 * 1024 * 1024
-PACK_VMEM_BYTES = 62 * 1024 * 1024
+FULL_VMEM_BYTES = 62 * 1024 * 1024
 F32 = jnp.float32
 BF16 = jnp.bfloat16
 LINK = jnp.bfloat16
@@ -25,7 +25,7 @@
 
 
 def product(first, second):
-    return (first.astype(F32) * second.astype(F32)).astype(BF16)
+    return first * second
 
 
 def one_hot(rows, cols, column_of):
@@ -109,7 +109,7 @@
             pltpu.SemaphoreType.DMA((4, groups // 2)),
             pltpu.SemaphoreType.DMA((2, groups // 2)),
         ],
-        compiler_params=pltpu.CompilerParams(vmem_limit_bytes=PACK_VMEM_BYTES),
+        compiler_params=pltpu.CompilerParams(vmem_limit_bytes=FULL_VMEM_BYTES),
         cost_estimate=takes(3.0),
         name="pack_signals",
     )(key_proj, value_proj, out_grad, query_proj)
@@ -161,12 +161,10 @@
     return terms[0]
 
 
-def state_kernel(seq_ref, q_ref, k_ref, v_ref, o_ref, coef_ref, *refs):
-    state_refs, own_ref, x_ref, g_ref = refs[:-3], *refs[-3:]
+def state_kernel(q_ref, k_ref, v_ref, o_ref, coef_ref, own_ref, sent_ref, x_ref, g_ref):
     tok_rows, width = k_ref.shape
     tiles = width // LANES
     modes = coef_ref.shape[1]
-    pairs = len(state_refs) + 1
     spread_tokens(k_ref, v_ref, x_ref)
     spread_tokens(o_ref, q_ref, g_ref)
     decay = [coef_ref[0, m] for m in range(modes)]
@@ -179,43 +177,29 @@
         return (ahead, behind)
 
     zero = tuple(jnp.zeros((tiles, LANES), F32) for _ in range(modes))
-    ahead, behind = lax.fori_loop(0, tok_rows, step, (zero, zero), unroll=8)
-    ahead = jnp.concatenate(ahead, axis=0)
-    behind = jnp.concatenate(behind, axis=0)
-    own_ref[0] = ahead
-    own_ref[1] = behind
-    for k in range(1, pairs):
-        stays = seq_ref[0] // 2 + k < pairs
-
-        @pl.when(stays)
-        def _():
-            state_refs[k - 1][...] = ahead.astype(LINK)
-
-        @pl.when(jnp.logical_not(stays))
-        def _():
-            state_refs[k - 1][...] = behind.astype(LINK)
-
-
-def block_states(seq_index, pairs, query_proj, key_proj, value_proj, out_grad, coefs):
+    for side, held in enumerate(lax.fori_loop(0, tok_rows, step, (zero, zero), unroll=8)):
+        held = jnp.concatenate(held, axis=0)
+        own_ref[side] = held
+        sent_ref[side] = held.astype(LINK)
+
+
+def block_states(query_proj, key_proj, value_proj, out_grad, coefs):
     tok_rows, width = key_proj.shape
     modes, tiles = coefs.shape[1:3]
-    whole = pl.BlockSpec(memory_space=pltpu.VMEM)
-    *states, own = pl.pallas_call(
+    return pl.pallas_call(
         state_kernel,
-        in_specs=[pl.BlockSpec(memory_space=pltpu.SMEM)] + [whole] * 5,
-        out_specs=[whole] * pairs,
-        out_shape=[jax.ShapeDtypeStruct((modes * tiles, LANES), LINK)] * (pairs - 1)
-        + [jax.ShapeDtypeStruct((2, modes * tiles, LANES), F32)],
+        out_shape=[
+            jax.ShapeDtypeStruct((2, modes * tiles, LANES), F32),
+            jax.ShapeDtypeStruct((2, modes * tiles, LANES), LINK),
+        ],
         scratch_shapes=[pltpu.VMEM(token_shape(tok_rows, tiles), F32)] * 2,
         compiler_params=pltpu.CompilerParams(vmem_limit_bytes=VMEM_BYTES),
         cost_estimate=takes(3.0),
         name="block_states",
-    )(seq_index, query_proj, key_proj, value_proj, out_grad, coefs)
-    return states, own
-
-
-def pair_kernel(seq_ref, coef_ref, own_ref, *refs):
-    state_refs, kept_ref, given_ref = refs[2:-2], *refs[-2:]
+    )(query_proj, key_proj, value_proj, out_grad, coefs)
+
+
+def pair_kernel(seq_ref, coef_ref, own_ref, near_ref, *state_refs):
     pairs = len(state_refs) + 1
     modes, tiles = coef_ref.shape[1:3]
     pair = seq_ref[0] // 2
@@ -223,59 +207,66 @@
     for m in range(modes):
         rows = slice(m * tiles, (m + 1) * tiles)
         decay = coef_ref[1, m]
-        both = decay * decay
-        before = jnp.zeros((tiles, LANES), F32)
-        after = jnp.zeros((tiles, LANES), F32)
-        for k in range(pairs - 1, 0, -1):
-            block = state_refs[k - 1][...].astype(F32)[rows]
-            before = both * before + jnp.where(k <= pair, block, 0.0)
-            block = state_refs[pairs - k - 1][...].astype(F32)[rows]
-            after = both * after + jnp.where(k <= pairs - 1 - pair, block, 0.0)
-        before = jnp.where(second, before, decay * before)
-        after = jnp.where(second, decay * after, after)
-        kept_ref[0, rows] = jnp.where(second, decay * before, before)
-        kept_ref[1, rows] = jnp.where(second, after, decay * after)
-        own = own_ref[0, rows]
-        given_ref[0, rows] = jnp.where(second, before, decay * before + own).astype(LINK)
-        own = own_ref[1, rows]
-        given_ref[1, rows] = jnp.where(second, decay * after + own, after).astype(LINK)
-
-
-def pair_states(seq_index, coefs, own, parts, states):
+        own, near = own_ref[0, rows], near_ref[0].astype(F32)[rows]
+        ahead = jnp.where(second, own + decay * near, near + decay * own)
+        own, near = own_ref[1, rows], near_ref[1].astype(F32)[rows]
+        behind = jnp.where(second, near + decay * own, own + decay * near)
+        for k in range(1, pairs):
+            state_refs[k - 1][rows] = jnp.where(pair + k < pairs, ahead, behind)
+
+
+def pair_states(seq_index, pairs, coefs, own, near):
     whole = pl.BlockSpec(memory_space=pltpu.VMEM)
-    return pl.pallas_call(
+    states = pl.pallas_call(
         pair_kernel,
-        in_specs=[pl.BlockSpec(memory_space=pltpu.SMEM), whole, whole]
-        + [pl.BlockSpec(memory_space=pl.ANY)] * len(parts)
-        + [whole] * len(states),
-        out_specs=[whole] * 2,
-        out_shape=[
-            jax.ShapeDtypeStruct(own.shape, F32),
-            jax.ShapeDtypeStruct(own.shape, LINK),
-        ],
+        in_specs=[pl.BlockSpec(memory_space=pltpu.SMEM)] + [whole] * 3,
+        out_specs=[whole] * (pairs - 1),
+        out_shape=[jax.ShapeDtypeStruct(own.shape[1:], F32)] * (pairs - 1),
         compiler_params=pltpu.CompilerParams(vmem_limit_bytes=VMEM_BYTES),
         cost_estimate=takes(0.1),
         name="pair_states",
-    )(seq_index, coefs, own, *parts, *states)
+    )(seq_index, coefs, own, near)
+    return [state.astype(LINK) for state in states]
+
+
+def sum_pairs(side, seq, coef_ref, near_ref, state_refs):
+    pairs = len(state_refs) + 1
+    modes, tiles = coef_ref.shape[1:3]
+    pair, count = seq // 2, (seq // 2, pairs - 1 - seq // 2)[side]
+    beside = seq % 2 == 1 - side
+    held = []
+    for m in range(modes):
+        rows = slice(m * tiles, (m + 1) * tiles)
+        decay = coef_ref[1, m]
+        total = jnp.zeros((tiles, LANES), F32)
+        for k in range(pairs - 1, 0, -1):
+            state_ref = state_refs[k - 1 if side == 0 else pairs - k - 1]
+            block = state_ref[...].astype(F32)[rows]
+            total = decay * decay * total + jnp.where(k <= count, block, 0.0)
+        near = near_ref[side].astype(F32)[rows]
+        held.append(jnp.where(beside, decay * total + near, total))
+    return held
 
 
 def local_kernel(
-    q_ref, k_ref, v_ref, o_ref, coef_ref, gain_ref, conv_ref, grad_ref, x_ref, g_ref
+    q_ref, k_ref, v_ref, o_ref, coef_ref, gain_ref, part_ref, done_ref
 ):
+    conv_ref, grad_ref = part_ref.at[0], part_ref.at[1]
     tok_rows, width = k_ref.shape
     tiles = width // LANES
-    spread_tokens(k_ref, v_ref, x_ref)
-    spread_tokens(o_ref, q_ref, g_ref)
-    walk_tokens(x_ref, coef_ref, tok_rows, tiles, 0, 1)
-    walk_tokens(g_ref, coef_ref, tok_rows, tiles, tok_rows - 1, -1)
+    spread_tokens(k_ref, v_ref, conv_ref)
+    spread_tokens(o_ref, q_ref, grad_ref)
+    walk_tokens(conv_ref, coef_ref, tok_rows, tiles, 0, 1)
+    walk_tokens(grad_ref, coef_ref, tok_rows, tiles, tok_rows - 1, -1)
     for tile in range(tiles):
         cols = slice(tile * LANES, (tile + 1) * LANES)
         rows = tile_rows(tok_rows, tile)
         gain = gain_ref[:, cols]
         conv_in = product(k_ref[:, cols], v_ref[:, cols]).astype(F32)
-        conv_ref[:, cols] = (x_ref[rows, :] + gain * conv_in).astype(BF16)
+        conv_ref[rows, :] = conv_ref[rows, :] + gain * conv_in
         mid_grad = product(o_ref[:, cols], q_ref[:, cols]).astype(F32)
-        grad_ref[:, cols] = (g_ref[rows, :] + gain * mid_grad).astype(BF16)
+        grad_ref[rows, :] = grad_ref[rows, :] + gain * mid_grad
+    done_ref[...] = jnp.zeros(done_ref.shape, F32)
 
 
 def local_parts(query_proj, key_proj, value_proj, out_grad, coefs, gain):
@@ -283,8 +274,10 @@
     tiles = coefs.shape[2]
     return pl.pallas_call(
         local_kernel,
-        out_shape=[jax.ShapeDtypeStruct((tok_rows, width), BF16)] * 2,
-        scratch_shapes=[pltpu.VMEM(token_shape(tok_rows, tiles), F32)] * 2,
+        out_shape=[
+            jax.ShapeDtypeStruct((2, *token_shape(tok_rows, tiles)), F32),
+            jax.ShapeDtypeStruct((SUBLANES, LANES), F32),
+        ],
         compiler_params=pltpu.CompilerParams(vmem_limit_bytes=VMEM_BYTES),
         cost_estimate=takes(6.5),
         name="local_parts",
@@ -313,65 +306,78 @@
     lax.fori_loop(0, tok_rows, step, held, unroll=8)
 
 
-def final_kernel(
-    q_ref, k_ref, v_ref, conv_ref, grad_ref, coef_ref, kept_ref, given_ref,
-    layer_hbm, key_hbm, value_hbm, edge_ref, layer_ref, key_ref, value_ref, sems,
-):
+def final_kernel(count, *refs):
+    seq_ref, hbm_refs, refs = refs[0], refs[1 : 1 + count], refs[1 + count :]
+    out_hbm, held_refs, refs = refs[:3], refs[3 : 3 + count], refs[3 + count :]
+    edge_ref, out_refs, in_sems, out_sems = refs[0], refs[1:4], refs[4], refs[5]
+    coef_ref, near_ref, *state_refs = held_refs[:-4]
+    part_ref, q_ref, v_ref, k_ref = held_refs[-4:]
     tok_rows, width = k_ref.shape
     tiles = width // LANES
-    modes = coef_ref.shape[1]
-
-    def departure(i, tile):
-        place = (slice(None), pl.ds(tile * LANES, LANES))
-        return pltpu.make_async_copy(
-            (layer_ref, key_ref, value_ref)[i].at[place],
-            (layer_hbm, key_hbm, value_hbm)[i].at[place],
-            sems.at[i, tile],
-        )
-
-    def edge(side):
-        total = kept_ref[side] + given_ref[side].astype(F32)
-        return [total[m * tiles : (m + 1) * tiles] for m in range(modes)]
-
-    fill_edge(edge_ref, edge(0), coef_ref, tok_rows, tiles, 0, 1)
-    for tile in range(tiles):
-        cols = slice(tile * LANES, (tile + 1) * LANES)
-        long_conv = conv_ref[:, cols].astype(F32) + edge_ref[tile_rows(tok_rows, tile), :]
-        layer_ref[:, cols] = (q_ref[:, cols].astype(F32) * long_conv).astype(BF16)
-        departure(0, tile).start()
-    fill_edge(edge_ref, edge(1), coef_ref, tok_rows, tiles, tok_rows - 1, -1)
-    for tile in range(tiles):
-        cols = slice(tile * LANES, (tile + 1) * LANES)
-        conv_grad = grad_ref[:, cols].astype(F32) + edge_ref[tile_rows(tok_rows, tile), :]
-        key_ref[:, cols] = (conv_grad * v_ref[:, cols].astype(F32)).astype(BF16)
-        departure(1, tile).start()
-        value_ref[:, cols] = (conv_grad * k_ref[:, cols].astype(F32)).astype(BF16)
-        departure(2, tile).start()
-    for i in range(3):
+    pieces = list(zip(hbm_refs[:-4], held_refs[:-4]))
+    small = len(pieces)
+    pieces += [(hbm_refs[-4].at[0], part_ref.at[0]), (hbm_refs[-3], q_ref)]
+    pieces += [(hbm_refs[-4].at[1], part_ref.at[1])] + list(zip(hbm_refs[-2:], held_refs[-2:]))
+    arrivals = [
+        pltpu.make_async_copy(source, target, in_sems.at[i])
+        for i, (source, target) in enumerate(pieces)
+    ]
+    departures = []
+
+    def multiply_out(side, outs):
         for tile in range(tiles):
-            departure(i, tile).wait()
-
-
-def final_outputs(signals, parts, coefs, kept, given):
-    tok_rows, width = signals[0].shape
+            cols = slice(tile * LANES, (tile + 1) * LANES)
+            rows = tile_rows(tok_rows, tile)
+            value = part_ref[side, rows, :] + edge_ref[rows, :]
+            for i, factor_ref in outs:
+                out_refs[i][:, cols] = (value * factor_ref[:, cols].astype(F32)).astype(BF16)
+                place = (slice(None), pl.ds(tile * LANES, LANES))
+                copy = pltpu.make_async_copy(
+                    out_refs[i].at[place], out_hbm[i].at[place], out_sems.at[i, tile]
+                )
+                copy.start()
+                departures.append(copy)
+
+    for copy in arrivals:
+        copy.start()
+    for copy in arrivals[:small]:
+        copy.wait()
+    held = sum_pairs(0, seq_ref[0], coef_ref, near_ref, state_refs)
+    fill_edge(edge_ref, held, coef_ref, tok_rows, tiles, 0, 1)
+    for copy in arrivals[small : small + 2]:
+        copy.wait()
+    multiply_out(0, [(0, q_ref)])
+    held = sum_pairs(1, seq_ref[0], coef_ref, near_ref, state_refs)
+    fill_edge(edge_ref, held, coef_ref, tok_rows, tiles, tok_rows - 1, -1)
+    for copy in arrivals[small + 2 :]:
+        copy.wait()
+    multiply_out(1, [(1, v_ref), (2, k_ref)])
+    for copy in departures:
+        copy.wait()
+
+
+def final_outputs(seq_index, coefs, near, states, parts, query_proj, value_proj, key_proj):
+    tok_rows, width = key_proj.shape
     tiles = coefs.shape[2]
-    args = (*signals, *parts, coefs, kept, given)
+    args = (coefs, near, *states, parts, query_proj, value_proj, key_proj)
+    away = pl.BlockSpec(memory_space=pl.ANY)
     return pl.pallas_call(
-        final_kernel,
-        in_specs=[pl.BlockSpec(memory_space=pltpu.VMEM)] * len(args),
-        out_specs=[pl.BlockSpec(memory_space=pl.ANY)] * 3,
+        functools.partial(final_kernel, len(args)),
+        in_specs=[pl.BlockSpec(memory_space=pltpu.SMEM)] + [away] * len(args),
+        out_specs=[away] * 3,
         out_shape=[jax.ShapeDtypeStruct((tok_rows, width), BF16)] * 3,
-        scratch_shapes=[pltpu.VMEM(token_shape(tok_rows, tiles), F32)]
+        scratch_shapes=[pltpu.VMEM(arg.shape, arg.dtype) for arg in args]
+        + [pltpu.VMEM(token_shape(tok_rows, tiles), F32)]
         + [pltpu.VMEM((tok_rows, width), BF16)] * 3
-        + [pltpu.SemaphoreType.DMA((3, tiles))],
-        compiler_params=pltpu.CompilerParams(vmem_limit_bytes=VMEM_BYTES),
-        cost_estimate=takes(4.0),
+        + [pltpu.SemaphoreType.DMA((len(args) + 1,)), pltpu.SemaphoreType.DMA((3, tiles))],
+        compiler_params=pltpu.CompilerParams(vmem_limit_bytes=FULL_VMEM_BYTES),
+        cost_estimate=takes(100.0),
         name="final_outputs",
-    )(*args)
+    )(seq_index, *args)
 
 
 def lag_kernel(shards, chans, groups, owned, scale, *refs):
-    in_refs, (out_ref, u_all, g_all, turned_all) = refs[:-4], refs[-4:]
+    in_refs, (out_ref, u_all, g_all, turned_all) = refs[1:-4], refs[-4:]
     tok_rows = out_ref.shape[2]
     halves = tok_rows // LANES
     blocks = shards * halves
@@ -448,7 +454,7 @@
     lax.fori_loop(0, owned, one_filter, 0, unroll=min(owned, 4))
 
 
-def filter_lags(received, shards, chans, owned, scale):
+def filter_lags(received, done, shards, chans, owned, scale):
     tok_rows = received.shape[2]
     groups = received.shape[1] // (2 * owned)
     halves = tok_rows // LANES
@@ -459,8 +465,11 @@
         split = received.reshape(shards, chans, 2, groups, owned, halves, LANES)
         split = split.transpose(2, 4, 0, 5, 1, 3, 6).reshape(2, owned, full, LANES)
         args = (split[0], split[1])
+    whole = pl.BlockSpec(memory_space=pltpu.VMEM)
     return pl.pallas_call(
         functools.partial(lag_kernel, shards, chans, groups, owned, scale),
+        in_specs=[pl.BlockSpec(memory_space=pl.ANY)] + [whole] * len(args),
+        out_specs=whole,
         out_shape=jax.ShapeDtypeStruct((shards, owned, tok_rows), F32),
         scratch_shapes=[
             pltpu.VMEM((owned, full, LANES), BF16),
@@ -468,9 +477,9 @@
             pltpu.VMEM((owned, LANES, full), BF16),
         ],
         compiler_params=pltpu.CompilerParams(vmem_limit_bytes=VMEM_BYTES),
-        cost_estimate=takes(4.0),
+        cost_estimate=takes(0.1),
         name="filter_lags",
-    )(*args)
+    )(done, *args)
 
 
 def per_device(query_proj, key_proj, value_proj, out_grad, residues, decay_rate, skip_gain):
@@ -500,21 +509,20 @@
     coefs = coefs.reshape(3, modes, width // LANES, LANES)
     seq_index = lax.axis_index("seq").reshape(1)
     pairs = shards // 2
-    states, own = block_states(seq_index, pairs, *signals, coefs)
-    *states, coefs = lax.optimization_barrier((*states, coefs))
+    own, sent = block_states(*signals, coefs)
+    near = inside_pair(sent, pairs)
+    states = pair_states(seq_index, pairs, coefs, own, near)
+    *states, coefs, near = lax.optimization_barrier((*states, coefs, near))
     states = [along_column(state, pairs, 1 + i) for i, state in enumerate(states)]
-    parts = local_parts(*signals, coefs, skip_gain[None, :])
-    kept, given = pair_states(seq_index, coefs, own, parts, states)
-    received, kept, given = lax.optimization_barrier((received, kept, given))
-    given = inside_pair(given, pairs)
+    parts, done = local_parts(*signals, coefs, skip_gain[None, :])
 
     scale = 1.0 / math.sqrt(length * (CHANNELS // FILTERS))
-    lags = filter_lags(received, shards, chans, owned, scale)
-    lags, given = lax.optimization_barrier((lags, given))
+    lags = filter_lags(received, done, shards, chans, owned, scale)
     lags = lax.all_to_all(lags, "seq", split_axis=0, concat_axis=0, tiled=True)
     filter_grad = lags.reshape(shards * owned, tok_rows).T
+    query_proj, key_proj, value_proj, _ = signals
     layer_out, key_grad, value_grad = final_outputs(
-        signals[:3], parts, coefs, kept, given
+        seq_index, coefs, near, states, parts, query_proj, value_proj, key_proj
     )
     return (layer_out, key_grad, value_grad, filter_grad)
 

time: 58.7 us -> 61.2 us (1.043)
  Pallas kernels: 20.4 us -> 22.6 us
  local copies, waits for them, and re-layouts: 4.84 us -> 2.71 us
  waiting for transfers between devices: 14.5 us -> 15.9 us
  starting transfers between devices: 17.8 us -> 18.7 us
    ppermute x3, waiting for transfers between devices: 12.6 us -> 2.51 us  [along_column(): return lax.ppermute(state, 'seq', route)]
    all_to_all x1, waiting for transfers between devices: 0.01 us -> 8.98 us  [per_device(): lax.all_to_all(send, ('seq', 'chan'), split_axis=0, concat_axis=0, tiled=...]
    ppermute x1, waiting for transfers between devices: 0.01 us -> 4.45 us  [inside_pair(): return lax.ppermute(state, 'seq', [(i, i ^ 1) for i in range(2 * pairs)])]
    unnamed x25 -> x27, local copies, waits for them, and re-layouts: 4.76 us -> 2.63 us
    all_to_all x1, waiting for transfers between devices: 1.83 us -> 0.01 us  [per_device(): lags = lax.all_to_all(lags, 'seq', split_axis=0, concat_axis=0, tiled=True)]
    pallas_call x1, Pallas kernels: 4.01 us -> 5.23 us  [filter_lags(): pl.pallas_call(functools.partial(lag_kernel, shards, chans, groups, owned...]
    pallas_call x3, Pallas kernels: 13.3 us -> 14.3 us  [the longest x1 6.39 us: local_parts(): pl.pallas_call(local_kernel, out_shape=[jax.ShapeDtypeStruct((2, *token_s...]
  transfers between devices with their start and end apart: 6 -> 6, of which waited for: 3 -> 5; matrix products, arithmetic and copies ran while one was open for 0% -> 0% of each run, Pallas kernels for 30% -> 24%
where the time goes in v14:
time: 61.2 us; the launch traced here: 60.9 us
  Pallas kernels  22.6 us (37%)
  starting transfers between devices  18.7 us (31%)
  waiting for transfers between devices  15.9 us (26%)
  local copies, waits for them, and re-layouts  2.71 us (4%)
  between operations  0.87 us (1%)
    all_to_all x1, waiting for transfers between devices, per_device(): lax.all_to_all(send, ('seq', 'chan'), split_axis=0, concat_axis=0, tiled=...  8.98 us
    all_to_all x1, starting transfers between devices, per_device(): lax.all_to_all(send, ('seq', 'chan'), split_axis=0, concat_axis=0, tiled=...  7.44 us
    pallas_call x1, Pallas kernels, local_parts(): pl.pallas_call(local_kernel, out_shape=[jax.ShapeDtypeStruct((2, *token_s...  6.39 us
    ppermute x3, starting transfers between devices, along_column(): return lax.ppermute(state, 'seq', route)  5.85 us
    pallas_call x1, Pallas kernels, filter_lags(): pl.pallas_call(functools.partial(lag_kernel, shards, chans, groups, owned...  5.23 us
    pallas_call x1, Pallas kernels, final_outputs(): pl.pallas_call(functools.partial(final_kernel, len(args)), in_specs=[pl.B...  4.95 us
    ppermute x1, waiting for transfers between devices, inside_pair(): return lax.ppermute(state, 'seq', [(i, i ^ 1) for i in range(2 * pairs)])  4.45 us
    all_to_all x1, starting transfers between devices, per_device(): lags = lax.all_to_all(lags, 'seq', split_axis=0, concat_axis=0, tiled=True)  3.67 us
  transfers between devices with their start and end apart: 6, of which 5 were waited for; matrix products, arithmetic and copies ran while one was open for 0% of the time, Pallas kernels for 24%

profile of v14, /device:TPU:0, one launch (start us, length us, event | category | flops | bytes accessed | tf_op | source)
XLA Modules:
  0.0 60.9 jit_solution(119854562130479530)
XLA Ops:
  0.6 0.0 copy-start.2
  0.6 0.0 copy-start.1
  0.7 0.0 copy-start
  0.7 0.0 copy-start.11
  0.7 0.0 copy-start.12
  0.7 3.1 %pack_signals.1 = bf16[32,64,256]{2,1,0:T(8,128)(2,1)} custom-call(bf16[256,1024]{1,0:T(8,128)(2,1)} %refs_9_, bf16[256,1024]{1,0:T(8,128)(2,1)} %refs_8_, bf16[256,1024]{1,0:T(8,128)(2,1)} %o_ref.1, bf16[256,1024]{1,0:T(8,128)(2,1)} %refs_7_), custom_call_target="tpu_custom_call" | custom-call | bytes 10800000 | tf_op jit(solution)/shard_map/pack_signals/pallas_call | solution.py:101
  3.8 0.0 copy-start.4
  3.8 7.4 %all-to-all-start = ((bf16[32,64,256]{2,1,0:T(8,128)(2,1)}), bf16[32,64,256]{2,1,0:T(8,128)(2,1)}, u32[]{:S(2)}, u32[]{:S(2)}) async-start(bf16[32,64,256]{2,1,0:T(8,128)(2,1)} %pack_signals.1), calls=%async_computation | async-start | bytes 2097152 | tf_op jit(solution)/shard_map/all_to_all | solution.py:498
  11.2 0.0 copy-done.11
  11.2 0.0 copy-done.12
  11.2 0.0 copy-start.7
  11.3 0.1 broadcast_in_dim.11
  11.4 0.0 copy-start.3
  11.4 0.0 copy-done.2
  11.4 0.0 copy-done.1
  11.4 0.0 copy-done
  11.4 0.0 copy-done.4
  11.4 2.9 %block_states.1 = (f32[2,128,128]{2,1,0:T(8,128)S(1)}, bf16[2,128,128]{2,1,0:T(8,128)(2,1)S(1)}) custom-call(bf16[256,1024]{1,0:T(8,128)(2,1)S(1)} %copy-done, bf16[256,1024]{1,0:T(8,128)(2,1)S(1)} %copy-done.1, bf16[256,1024]{1,0:T(8,128)(2,1)S(1)} %copy-done.2, bf16[256,1024]{1,0:T(8,128)(2,1)S(1)} %copy-done.4, f32[3,16,8,128]{3,2,1,0:T(8,128)S(1)} %bitcast.14), custom_call_target="tpu_custom_call" | custom-call | bytes 10800000 | tf_op jit(solution)/shard_map/block_states/pallas_call | solution.py:189
  14.4 1.8 %collective-permute-start = (bf16[2,128,128]{2,1,0:T(8,128)(2,1)S(1)}, bf16[2,128,128]{2,1,0:T(8,128)(2,1)S(1)}, u32[]{:S(2)}, u32[]{:S(2)}) collective-permute-start(bf16[2,128,128]{2,1,0:T(8,128)(2,1)S(1)} %get-tuple-element.33), channel_id=1, source_target_pairs={{0,4},{4,0},{8,12},{12,8},{16,20},{20,16},{24,28},{28,24},{1,5},{5... | collective-permute-start | bytes 196616 | tf_op jit(solution)/shard_map/ppermute | solution.py:293
  16.1 4.4 %collective-permute-done.near_ref.refs_2_ = bf16[2,128,128]{2,1,0:T(8,128)(2,1)S(1)} collective-permute-done((bf16[2,128,128]{2,1,0:T(8,128)(2,1)S(1)}, bf16[2,128,128]{2,1,0:T(8,128)(2,1)S(1)}, u32[]{:S(2)}, u32[]{:S(2)}) %collective-permute-start) | collective-permute-done | bytes 65568 | tf_op jit(solution)/shard_map/ppermute | solution.py:293
  20.6 0.0 copy-start.6
  20.7 0.0 copy-done.7
  20.7 6.4 %local_parts.1 = (f32[2,2112,128]{2,1,0:T(8,128)S(1)}, f32[8,128]{1,0:T(8,128)S(1)}) custom-call(bf16[256,1024]{1,0:T(8,128)(2,1)S(1)} %copy-done, bf16[256,1024]{1,0:T(8,128)(2,1)S(1)} %copy-done.1, bf16[256,1024]{1,0:T(8,128)(2,1)S(1)} %copy-done.2, bf16[256,1024]{1,0:T(8,128)(2,1)S(1)} %copy-done.4, f32[3,16,8,128]{3,2,1,0:T(8,128)S(1)} %bitcast.16, ...), custom_call_target="tpu_custom_call" | custom-call | bytes 23400000 | tf_op jit(solution)/shard_map/local_parts/pallas_call | solution.py:275
  27.1 0.0 copy-done.3
  27.1 0.0 copy-start.5
  27.1 1.3 %copy-done.5 = f32[2,2112,128]{2,1,0:T(8,128)} copy-done((f32[2,2112,128]{2,1,0:T(8,128)}, f32[2,2112,128]{2,1,0:T(8,128)S(1)}, u32[]{:S(2)}) %copy-start.5) | copy-done | bytes 2162712
  28.4 9.0 %all-to-all-done.refs_1_ = bf16[32,64,256]{2,1,0:T(8,128)(2,1)} async-done(((bf16[32,64,256]{2,1,0:T(8,128)(2,1)}), bf16[32,64,256]{2,1,0:T(8,128)(2,1)}, u32[]{:S(2)}, u32[]{:S(2)}) %all-to-all-start) | async-done | bytes 1048608 | tf_op jit(solution)/shard_map/all_to_all | solution.py:498
  37.4 5.2 %filter_lags.1 = f32[8,8,256]{2,1,0:T(8,128)} custom-call(f32[8,128]{1,0:T(8,128)S(1)} %get-tuple-element.46.refs_0_, bf16[32,64,256]{2,1,0:T(8,128)(2,1)} %all-to-all-done.refs_1_), custom_call_target="tpu_custom_call" | custom-call | bytes 360000 | tf_op jit(solution)/shard_map/filter_lags/pallas_call | solution.py:469
  42.7 3.7 %all-to-all-start.1 = ((f32[8,8,256]{2,1,0:T(8,128)}), f32[8,8,256]{2,1,0:T(8,128)S(1)}, u32[]{:S(2)}, u32[]{:S(2)}) async-start(f32[8,8,256]{2,1,0:T(8,128)} %filter_lags.1), calls=%async_computation.1 | async-start | bytes 131072 | tf_op jit(solution)/shard_map/all_to_all | solution.py:521
  46.3 2.0 %collective-permute-start.1 = (bf16[128,128]{1,0:T(8,128)(2,1)S(1)}, bf16[128,128]{1,0:T(8,128)(2,1)S(1)}, u32[]{:S(2)}, u32[]{:S(2)}) collective-permute-start(bf16[128,128]{1,0:T(8,128)(2,1)S(1)} %convert_element_type.9), channel_id=1, source_target_pairs={{0,8},{4,12},{8,16},{12,20},{16,24},{20,28},{24,0},{28,4},{1,9},{5... | collective-permute-start | bytes 98312 | tf_op jit(solution)/shard_map/ppermute | solution.py:289
  48.3 2.4 %collective-permute-start.2 = (bf16[128,128]{1,0:T(8,128)(2,1)S(1)}, bf16[128,128]{1,0:T(8,128)(2,1)S(1)}, u32[]{:S(2)}, u32[]{:S(2)}) collective-permute-start(bf16[128,128]{1,0:T(8,128)(2,1)S(1)} %convert_element_type.10), channel_id=1, source_target_pairs={{0,16},{4,20},{8,24},{12,28},{16,0},{20,4},{24,8},{28,12},{1,17},{... | collective-permute-start | bytes 98312 | tf_op jit(solution)/shard_map/ppermute | solution.py:289
  50.7 1.5 %collective-permute-start.3 = (bf16[128,128]{1,0:T(8,128)(2,1)S(1)}, bf16[128,128]{1,0:T(8,128)(2,1)S(1)}, u32[]{:S(2)}, u32[]{:S(2)}) collective-permute-start(bf16[128,128]{1,0:T(8,128)(2,1)S(1)} %convert_element_type.11), channel_id=1, source_target_pairs={{0,24},{4,28},{8,0},{12,4},{16,8},{20,12},{24,16},{28,20},{1,25},{... | collective-permute-start | bytes 98312 | tf_op jit(solution)/shard_map/ppermute | solution.py:289
  52.2 1.3 %collective-permute-done.1.refs_3_ = bf16[128,128]{1,0:T(8,128)(2,1)S(1)} collective-permute-done((bf16[128,128]{1,0:T(8,128)(2,1)S(1)}, bf16[128,128]{1,0:T(8,128)(2,1)S(1)}, u32[]{:S(2)}, u32[]{:S(2)}) %collective-permute-start.1) | collective-permute-done | bytes 32800 | tf_op jit(solution)/shard_map/ppermute | solution.py:289
  53.5 0.0 copy-start.8
  53.5 0.9 %collective-permute-done.2.refs_4_ = bf16[128,128]{1,0:T(8,128)(2,1)S(1)} collective-permute-done((bf16[128,128]{1,0:T(8,128)(2,1)S(1)}, bf16[128,128]{1,0:T(8,128)(2,1)S(1)}, u32[]{:S(2)}, u32[]{:S(2)}) %collective-permute-start.2) | collective-permute-done | bytes 32800 | tf_op jit(solution)/shard_map/ppermute | solution.py:289
  54.4 0.0 copy-start.9
  54.4 0.3 collective-permute-done.3.refs_5_
  54.7 0.0 copy-start.10
  54.7 0.0 copy-done.6
  54.7 0.0 copy-done.8
  54.7 0.3 copy-done.9
  55.0 0.3 copy-done.10
  55.3 4.9 %final_outputs.1 = (bf16[256,1024]{1,0:T(8,128)(2,1)}, bf16[256,1024]{1,0:T(8,128)(2,1)}, bf16[256,1024]{1,0:T(8,128)(2,1)}) custom-call(s32[1]{0:T(128)} %bitcast.seq_ref.refs_0_, f32[3,16,8,128]{3,2,1,0:T(8,128)} %bitcast.17, bf16[2,128,128]{2,1,0:T(8,128)(2,1)} %copy-done.6, bf16[128,128]{1,0:T(8,128)(2,1)} %copy-done.8, bf16[128,128]{1,0:T(8,128)(2,1)} %copy-done.9, ...), custom_call_target="tpu_custom_call" | custom-call | bytes 360000000 | tf_op jit(solution)/shard_map/final_outputs/pallas_call | solution.py:364
  60.2 0.0 all-to-all-done.1
  60.3 0.6 %copy.12 = f32[256,64]{0,1:T(8,128)} copy(f32[256,64]{0,1:T(8,128)S(1)} %bitcast.19) | data formatting | bytes 131072
  (7 shorter events, 0.1 us)
Async XLA Ops:
  0.6 10.8 %copy-start.2 = (bf16[256,1024]{1,0:T(8,128)(2,1)S(1)}, bf16[256,1024]{1,0:T(8,128)(2,1)}, u32[]{:S(2)}) copy-start(bf16[256,1024]{1,0:T(8,128)(2,1)} %refs_8_) | copy-start | bytes 1572868
  0.6 10.8 %copy-start.1 = (bf16[256,1024]{1,0:T(8,128)(2,1)S(1)}, bf16[256,1024]{1,0:T(8,128)(2,1)}, u32[]{:S(2)}) copy-start(bf16[256,1024]{1,0:T(8,128)(2,1)} %refs_9_) | copy-start | bytes 1572868
  0.7 10.8 %copy-start = (bf16[256,1024]{1,0:T(8,128)(2,1)S(1)}, bf16[256,1024]{1,0:T(8,128)(2,1)}, u32[]{:S(2)}) copy-start(bf16[256,1024]{1,0:T(8,128)(2,1)} %refs_7_) | copy-start | bytes 1572868
  0.7 10.5 %copy-start.11 = (f32[256,16]{0,1:T(8,128)S(1)}, f32[256,16]{0,1:T(8,128)}, u32[]{:S(2)}) copy-start(f32[256,16]{0,1:T(8,128)} %param.12) | copy-start | bytes 49156
  0.7 10.5 %copy-start.12 = (f32[256,16]{0,1:T(8,128)S(1)}, f32[256,16]{0,1:T(8,128)}, u32[]{:S(2)}) copy-start(f32[256,16]{0,1:T(8,128)} %param.11) | copy-start | bytes 49156
  3.8 7.7 %copy-start.4 = (bf16[256,1024]{1,0:T(8,128)(2,1)S(1)}, bf16[256,1024]{1,0:T(8,128)(2,1)}, u32[]{:S(2)}) copy-start(bf16[256,1024]{1,0:T(8,128)(2,1)} %o_ref.1) | copy-start | bytes 1572868
  3.8 33.7 %all-to-all-start = ((bf16[32,64,256]{2,1,0:T(8,128)(2,1)}), bf16[32,64,256]{2,1,0:T(8,128)(2,1)}, u32[]{:S(2)}, u32[]{:S(2)}) async-start(bf16[32,64,256]{2,1,0:T(8,128)(2,1)} %pack_signals.1), calls=%async_computation | async-start | bytes 2097152 | tf_op jit(solution)/shard_map/all_to_all | solution.py:498
  11.2 9.4 %copy-start.7 = (f32[1024]{0:T(1024)S(1)}, f32[1024]{0:T(1024)}, u32[]{:S(2)}) copy-start(f32[1024]{0:T(1024)} %param.13) | copy-start | bytes 12292
  11.4 15.7 %copy-start.3 = (f32[3,16,4,2,128]{4,3,2,1,0:T(2,128)}, f32[3,16,4,2,128]{4,3,2,1,0:T(2,128)S(1)}, u32[]{:S(2)}) copy-start(f32[3,16,4,2,128]{4,3,2,1,0:T(2,128)S(1)} %broadcast_in_dim.11) | copy-start | bytes 589828
  14.4 6.2 %collective-permute-start = (bf16[2,128,128]{2,1,0:T(8,128)(2,1)S(1)}, bf16[2,128,128]{2,1,0:T(8,128)(2,1)S(1)}, u32[]{:S(2)}, u32[]{:S(2)}) collective-permute-start(bf16[2,128,128]{2,1,0:T(8,128)(2,1)S(1)} %get-tuple-element.33), channel_id=1, source_target_pairs={{0,4},{4,0},{8,12},{12,8},{16,20},{20,16},{24,28},{28,24},{1,5},{5... | collective-permute-start | bytes 196616 | tf_op jit(solution)/shard_map/ppermute | solution.py:293
  20.6 34.1 %copy-start.6 = (bf16[2,128,128]{2,1,0:T(8,128)(2,1)}, bf16[2,128,128]{2,1,0:T(8,128)(2,1)S(1)}, u32[]{:S(2)}) copy-start(bf16[2,128,128]{2,1,0:T(8,128)(2,1)S(1)} %collective-permute-done.near_ref.refs_2_) | copy-start | bytes 196612
  27.1 1.4 %copy-start.5 = (f32[2,2112,128]{2,1,0:T(8,128)}, f32[2,2112,128]{2,1,0:T(8,128)S(1)}, u32[]{:S(2)}) copy-start(f32[2,2112,128]{2,1,0:T(8,128)S(1)} %get-tuple-element.42.refs_6_) | copy-start | bytes 6488068
  42.7 17.6 %all-to-all-start.1 = ((f32[8,8,256]{2,1,0:T(8,128)}), f32[8,8,256]{2,1,0:T(8,128)S(1)}, u32[]{:S(2)}, u32[]{:S(2)}) async-start(f32[8,8,256]{2,1,0:T(8,128)} %filter_lags.1), calls=%async_computation.1 | async-start | bytes 131072 | tf_op jit(solution)/shard_map/all_to_all | solution.py:521
  46.3 7.1 %collective-permute-start.1 = (bf16[128,128]{1,0:T(8,128)(2,1)S(1)}, bf16[128,128]{1,0:T(8,128)(2,1)S(1)}, u32[]{:S(2)}, u32[]{:S(2)}) collective-permute-start(bf16[128,128]{1,0:T(8,128)(2,1)S(1)} %convert_element_type.9), channel_id=1, source_target_pairs={{0,8},{4,12},{8,16},{12,20},{16,24},{20,28},{24,0},{28,4},{1,9},{5... | collective-permute-start | bytes 98312 | tf_op jit(solution)/shard_map/ppermute | solution.py:289
  48.3 6.0 %collective-permute-start.2 = (bf16[128,128]{1,0:T(8,128)(2,1)S(1)}, bf16[128,128]{1,0:T(8,128)(2,1)S(1)}, u32[]{:S(2)}, u32[]{:S(2)}) collective-permute-start(bf16[128,128]{1,0:T(8,128)(2,1)S(1)} %convert_element_type.10), channel_id=1, source_target_pairs={{0,16},{4,20},{8,24},{12,28},{16,0},{20,4},{24,8},{28,12},{1,17},{... | collective-permute-start | bytes 98312 | tf_op jit(solution)/shard_map/ppermute | solution.py:289
  50.7 4.0 %collective-permute-start.3 = (bf16[128,128]{1,0:T(8,128)(2,1)S(1)}, bf16[128,128]{1,0:T(8,128)(2,1)S(1)}, u32[]{:S(2)}, u32[]{:S(2)}) collective-permute-start(bf16[128,128]{1,0:T(8,128)(2,1)S(1)} %convert_element_type.11), channel_id=1, source_target_pairs={{0,24},{4,28},{8,0},{12,4},{16,8},{20,12},{24,16},{28,20},{1,25},{... | collective-permute-start | bytes 98312 | tf_op jit(solution)/shard_map/ppermute | solution.py:289
  53.5 1.2 %copy-start.8 = (bf16[128,128]{1,0:T(8,128)(2,1)}, bf16[128,128]{1,0:T(8,128)(2,1)S(1)}, u32[]{:S(2)}) copy-start(bf16[128,128]{1,0:T(8,128)(2,1)S(1)} %collective-permute-done.1.refs_3_) | copy-start | bytes 98308
  54.4 0.6 copy-start.9
  54.7 0.6 copy-start.10

commit v15 on v14

--- a/solution.py
+++ b/solution.py
@@ -371,7 +371,7 @@
         + [pltpu.VMEM((tok_rows, width), BF16)] * 3
         + [pltpu.SemaphoreType.DMA((len(args) + 1,)), pltpu.SemaphoreType.DMA((3, tiles))],
         compiler_params=pltpu.CompilerParams(vmem_limit_bytes=FULL_VMEM_BYTES),
-        cost_estimate=takes(100.0),
+        cost_estimate=takes(5.0),
         name="final_outputs",
     )(seq_index, *args)
 
@@ -518,6 +518,7 @@
 
     scale = 1.0 / math.sqrt(length * (CHANNELS // FILTERS))
     lags = filter_lags(received, done, shards, chans, owned, scale)
+    lags, *states = lax.optimization_barrier((lags, *states))
     lags = lax.all_to_all(lags, "seq", split_axis=0, concat_axis=0, tiled=True)
     filter_grad = lags.reshape(shards * owned, tok_rows).T
     query_proj, key_proj, value_proj, _ = signals

time: 61.2 us -> 55.7 us (0.910)
  waiting for transfers between devices: 15.9 us -> 12.3 us
  starting transfers between devices: 18.7 us -> 17.4 us
    all_to_all x1, waiting for transfers between devices: 8.98 us -> 6.02 us  [per_device(): lax.all_to_all(send, ('seq', 'chan'), split_axis=0, concat_axis=0, tiled=...]
    ppermute x3, waiting for transfers between devices: 2.51 us -> 0.01 us  [along_column(): return lax.ppermute(state, 'seq', route)]
    all_to_all x1, waiting for transfers between devices: 0.01 us -> 1.84 us  [per_device(): lags = lax.all_to_all(lags, 'seq', split_axis=0, concat_axis=0, tiled=True)]
    ppermute x3, starting transfers between devices: 5.85 us -> 4.84 us  [along_column(): return lax.ppermute(state, 'seq', route)]
  transfers between devices with their start and end apart: 6 -> 6, of which waited for: 5 -> 3; matrix products, arithmetic and copies ran while one was open for 0% -> 0% of each run, Pallas kernels for 24% -> 35%
where the time goes in v15:
time: 55.7 us; the launch traced here: 55.4 us
  Pallas kernels  22.6 us (41%)
  starting transfers between devices  17.4 us (31%)
  waiting for transfers between devices  12.3 us (22%)
  local copies, waits for them, and re-layouts  2.12 us (4%)
  between operations  0.92 us (2%)
    all_to_all x1, starting transfers between devices, per_device(): lax.all_to_all(send, ('seq', 'chan'), split_axis=0, concat_axis=0, tiled=...  7.44 us
    pallas_call x1, Pallas kernels, local_parts(): pl.pallas_call(local_kernel, out_shape=[jax.ShapeDtypeStruct((2, *token_s...  6.39 us
    all_to_all x1, waiting for transfers between devices, per_device(): lax.all_to_all(send, ('seq', 'chan'), split_axis=0, concat_axis=0, tiled=...  6.02 us
    pallas_call x1, Pallas kernels, filter_lags(): pl.pallas_call(functools.partial(lag_kernel, shards, chans, groups, owned...  5.23 us
    pallas_call x1, Pallas kernels, final_outputs(): pl.pallas_call(functools.partial(final_kernel, len(args)), in_specs=[pl.B...  4.96 us
    ppermute x3, starting transfers between devices, along_column(): return lax.ppermute(state, 'seq', route)  4.84 us
    ppermute x1, waiting for transfers between devices, inside_pair(): return lax.ppermute(state, 'seq', [(i, i ^ 1) for i in range(2 * pairs)])  4.45 us
    all_to_all x1, starting transfers between devices, per_device(): lags = lax.all_to_all(lags, 'seq', split_axis=0, concat_axis=0, tiled=True)  3.36 us
  transfers between devices with their start and end apart: 6, of which 3 were waited for; matrix products, arithmetic and copies ran while one was open for 0% of the time, Pallas kernels for 35%

profile of v15, /device:TPU:0, one launch (start us, length us, event | category | flops | bytes accessed | tf_op | source)
XLA Modules:
  0.0 55.4 jit_solution(3344668476562963962)
XLA Ops:
  0.6 0.0 copy-start.2
  0.6 0.0 copy-start.1
  0.7 0.0 copy-start
  0.7 0.0 copy-start.11
  0.7 0.0 copy-start.12
  0.7 3.1 %pack_signals.1 = bf16[32,64,256]{2,1,0:T(8,128)(2,1)} custom-call(bf16[256,1024]{1,0:T(8,128)(2,1)} %refs_9_, bf16[256,1024]{1,0:T(8,128)(2,1)} %refs_8_, bf16[256,1024]{1,0:T(8,128)(2,1)} %o_ref.1, bf16[256,1024]{1,0:T(8,128)(2,1)} %refs_7_), custom_call_target="tpu_custom_call" | custom-call | bytes 10800000 | tf_op jit(solution)/shard_map/pack_signals/pallas_call | solution.py:101
  3.8 0.0 copy-start.4
  3.8 7.4 %all-to-all-start = ((bf16[32,64,256]{2,1,0:T(8,128)(2,1)}), bf16[32,64,256]{2,1,0:T(8,128)(2,1)}, u32[]{:S(2)}, u32[]{:S(2)}) async-start(bf16[32,64,256]{2,1,0:T(8,128)(2,1)} %pack_signals.1), calls=%async_computation | async-start | bytes 2097152 | tf_op jit(solution)/shard_map/all_to_all | solution.py:498
  11.2 0.0 copy-done.11
  11.2 0.0 copy-done.12
  11.2 0.0 copy-start.7
  11.3 0.1 broadcast_in_dim.11
  11.4 0.0 copy-start.3
  11.4 0.0 copy-done.2
  11.4 0.0 copy-done.1
  11.4 0.0 copy-done
  11.4 0.0 copy-done.4
  11.4 2.9 %block_states.1 = (f32[2,128,128]{2,1,0:T(8,128)S(1)}, bf16[2,128,128]{2,1,0:T(8,128)(2,1)S(1)}) custom-call(bf16[256,1024]{1,0:T(8,128)(2,1)S(1)} %copy-done, bf16[256,1024]{1,0:T(8,128)(2,1)S(1)} %copy-done.1, bf16[256,1024]{1,0:T(8,128)(2,1)S(1)} %copy-done.2, bf16[256,1024]{1,0:T(8,128)(2,1)S(1)} %copy-done.4, f32[3,16,8,128]{3,2,1,0:T(8,128)S(1)} %bitcast.14), custom_call_target="tpu_custom_call" | custom-call | bytes 10800000 | tf_op jit(solution)/shard_map/block_states/pallas_call | solution.py:189
  14.4 1.8 %collective-permute-start = (bf16[2,128,128]{2,1,0:T(8,128)(2,1)S(1)}, bf16[2,128,128]{2,1,0:T(8,128)(2,1)S(1)}, u32[]{:S(2)}, u32[]{:S(2)}) collective-permute-start(bf16[2,128,128]{2,1,0:T(8,128)(2,1)S(1)} %get-tuple-element.37), channel_id=1, source_target_pairs={{0,4},{4,0},{8,12},{12,8},{16,20},{20,16},{24,28},{28,24},{1,5},{5... | collective-permute-start | bytes 196616 | tf_op jit(solution)/shard_map/ppermute | solution.py:293
  16.1 4.4 %collective-permute-done.near_ref.refs_2_ = bf16[2,128,128]{2,1,0:T(8,128)(2,1)S(1)} collective-permute-done((bf16[2,128,128]{2,1,0:T(8,128)(2,1)S(1)}, bf16[2,128,128]{2,1,0:T(8,128)(2,1)S(1)}, u32[]{:S(2)}, u32[]{:S(2)}) %collective-permute-start) | collective-permute-done | bytes 65568 | tf_op jit(solution)/shard_map/ppermute | solution.py:293
  20.6 0.0 copy-start.6
  20.7 2.4 %collective-permute-start.1 = (bf16[128,128]{1,0:T(8,128)(2,1)S(1)}, bf16[128,128]{1,0:T(8,128)(2,1)S(1)}, u32[]{:S(2)}, u32[]{:S(2)}) collective-permute-start(bf16[128,128]{1,0:T(8,128)(2,1)S(1)} %convert_element_type.9), channel_id=1, source_target_pairs={{0,8},{4,12},{8,16},{12,20},{16,24},{20,28},{24,0},{28,4},{1,9},{5... | collective-permute-start | bytes 98312 | tf_op jit(solution)/shard_map/ppermute | solution.py:289
  23.1 1.9 %collective-permute-start.2 = (bf16[128,128]{1,0:T(8,128)(2,1)S(1)}, bf16[128,128]{1,0:T(8,128)(2,1)S(1)}, u32[]{:S(2)}, u32[]{:S(2)}) collective-permute-start(bf16[128,128]{1,0:T(8,128)(2,1)S(1)} %convert_element_type.10), channel_id=1, source_target_pairs={{0,16},{4,20},{8,24},{12,28},{16,0},{20,4},{24,8},{28,12},{1,17},{... | collective-permute-start | bytes 98312 | tf_op jit(solution)/shard_map/ppermute | solution.py:289
  24.9 0.6 %collective-permute-start.3 = (bf16[128,128]{1,0:T(8,128)(2,1)S(1)}, bf16[128,128]{1,0:T(8,128)(2,1)S(1)}, u32[]{:S(2)}, u32[]{:S(2)}) collective-permute-start(bf16[128,128]{1,0:T(8,128)(2,1)S(1)} %convert_element_type.11), channel_id=1, source_target_pairs={{0,24},{4,28},{8,0},{12,4},{16,8},{20,12},{24,16},{28,20},{1,25},{... | collective-permute-start | bytes 98312 | tf_op jit(solution)/shard_map/ppermute | solution.py:289
  25.5 0.0 copy-done.7
  25.5 6.4 %local_parts.1 = (f32[2,2112,128]{2,1,0:T(8,128)S(1)}, f32[8,128]{1,0:T(8,128)S(1)}) custom-call(bf16[256,1024]{1,0:T(8,128)(2,1)S(1)} %copy-done, bf16[256,1024]{1,0:T(8,128)(2,1)S(1)} %copy-done.1, bf16[256,1024]{1,0:T(8,128)(2,1)S(1)} %copy-done.2, bf16[256,1024]{1,0:T(8,128)(2,1)S(1)} %copy-done.4, f32[3,16,8,128]{3,2,1,0:T(8,128)S(1)} %bitcast.16, ...), custom_call_target="tpu_custom_call" | custom-call | bytes 23400000 | tf_op jit(solution)/shard_map/local_parts/pallas_call | solution.py:275
  31.9 0.0 copy-done.3
  31.9 0.0 copy-start.5
  31.9 1.3 %copy-done.5 = f32[2,2112,128]{2,1,0:T(8,128)} copy-done((f32[2,2112,128]{2,1,0:T(8,128)}, f32[2,2112,128]{2,1,0:T(8,128)S(1)}, u32[]{:S(2)}) %copy-start.5) | copy-done | bytes 2162712
  33.3 6.0 %all-to-all-done.refs_1_ = bf16[32,64,256]{2,1,0:T(8,128)(2,1)} async-done(((bf16[32,64,256]{2,1,0:T(8,128)(2,1)}), bf16[32,64,256]{2,1,0:T(8,128)(2,1)}, u32[]{:S(2)}, u32[]{:S(2)}) %all-to-all-start) | async-done | bytes 1048608 | tf_op jit(solution)/shard_map/all_to_all | solution.py:498
  39.3 5.2 %filter_lags.1 = f32[8,8,256]{2,1,0:T(8,128)} custom-call(f32[8,128]{1,0:T(8,128)S(1)} %get-tuple-element.43.refs_0_, bf16[32,64,256]{2,1,0:T(8,128)(2,1)} %all-to-all-done.refs_1_), custom_call_target="tpu_custom_call" | custom-call | bytes 360000 | tf_op jit(solution)/shard_map/filter_lags/pallas_call | solution.py:469
  44.5 0.0 collective-permute-done.1.refs_3_
  44.5 0.0 copy-start.8
  44.5 0.0 collective-permute-done.2.refs_4_
  44.5 0.0 copy-start.9
  44.5 0.0 collective-permute-done.3.refs_5_
  44.6 0.0 copy-start.10
  44.6 3.4 %all-to-all-start.1 = ((f32[8,8,256]{2,1,0:T(8,128)}), f32[8,8,256]{2,1,0:T(8,128)S(1)}, u32[]{:S(2)}, u32[]{:S(2)}) async-start(f32[8,8,256]{2,1,0:T(8,128)} %filter_lags.1), calls=%async_computation.1 | async-start | bytes 131072 | tf_op jit(solution)/shard_map/all_to_all | solution.py:522
  47.9 0.0 copy-done.6
  47.9 0.0 copy-done.8
  48.0 0.0 copy-done.9
  48.0 0.0 copy-done.10
  48.0 5.0 %final_outputs.1 = (bf16[256,1024]{1,0:T(8,128)(2,1)}, bf16[256,1024]{1,0:T(8,128)(2,1)}, bf16[256,1024]{1,0:T(8,128)(2,1)}) custom-call(s32[1]{0:T(128)} %bitcast.seq_ref.refs_0_, f32[3,16,8,128]{3,2,1,0:T(8,128)} %bitcast.17, bf16[2,128,128]{2,1,0:T(8,128)(2,1)} %copy-done.6, bf16[128,128]{1,0:T(8,128)(2,1)} %copy-done.8, bf16[128,128]{1,0:T(8,128)(2,1)} %copy-done.9, ...), custom_call_target="tpu_custom_call" | custom-call | bytes 18000000 | tf_op jit(solution)/shard_map/final_outputs/pallas_call | solution.py:364
  52.9 1.8 %all-to-all-done.1 = f32[8,8,256]{2,1,0:T(8,128)S(1)} async-done(((f32[8,8,256]{2,1,0:T(8,128)}), f32[8,8,256]{2,1,0:T(8,128)S(1)}, u32[]{:S(2)}, u32[]{:S(2)}) %all-to-all-start.1) | async-done | bytes 65568 | tf_op jit(solution)/shard_map/all_to_all | solution.py:522
  54.8 0.6 %copy.12 = f32[256,64]{0,1:T(8,128)} copy(f32[256,64]{0,1:T(8,128)S(1)} %bitcast.19) | data formatting | bytes 131072
  (7 shorter events, 0.1 us)
Async XLA Ops:
  0.6 10.8 %copy-start.2 = (bf16[256,1024]{1,0:T(8,128)(2,1)S(1)}, bf16[256,1024]{1,0:T(8,128)(2,1)}, u32[]{:S(2)}) copy-start(bf16[256,1024]{1,0:T(8,128)(2,1)} %refs_8_) | copy-start | bytes 1572868
  0.6 10.8 %copy-start.1 = (bf16[256,1024]{1,0:T(8,128)(2,1)S(1)}, bf16[256,1024]{1,0:T(8,128)(2,1)}, u32[]{:S(2)}) copy-start(bf16[256,1024]{1,0:T(8,128)(2,1)} %refs_9_) | copy-start | bytes 1572868
  0.7 10.8 %copy-start = (bf16[256,1024]{1,0:T(8,128)(2,1)S(1)}, bf16[256,1024]{1,0:T(8,128)(2,1)}, u32[]{:S(2)}) copy-start(bf16[256,1024]{1,0:T(8,128)(2,1)} %refs_7_) | copy-start | bytes 1572868
  0.7 10.5 %copy-start.11 = (f32[256,16]{0,1:T(8,128)S(1)}, f32[256,16]{0,1:T(8,128)}, u32[]{:S(2)}) copy-start(f32[256,16]{0,1:T(8,128)} %param.12) | copy-start | bytes 49156
  0.7 10.5 %copy-start.12 = (f32[256,16]{0,1:T(8,128)S(1)}, f32[256,16]{0,1:T(8,128)}, u32[]{:S(2)}) copy-start(f32[256,16]{0,1:T(8,128)} %param.11) | copy-start | bytes 49156
  3.8 7.7 %copy-start.4 = (bf16[256,1024]{1,0:T(8,128)(2,1)S(1)}, bf16[256,1024]{1,0:T(8,128)(2,1)}, u32[]{:S(2)}) copy-start(bf16[256,1024]{1,0:T(8,128)(2,1)} %o_ref.1) | copy-start | bytes 1572868
  3.8 35.5 %all-to-all-start = ((bf16[32,64,256]{2,1,0:T(8,128)(2,1)}), bf16[32,64,256]{2,1,0:T(8,128)(2,1)}, u32[]{:S(2)}, u32[]{:S(2)}) async-start(bf16[32,64,256]{2,1,0:T(8,128)(2,1)} %pack_signals.1), calls=%async_computation | async-start | bytes 2097152 | tf_op jit(solution)/shard_map/all_to_all | solution.py:498
  11.2 14.3 %copy-start.7 = (f32[1024]{0:T(1024)S(1)}, f32[1024]{0:T(1024)}, u32[]{:S(2)}) copy-start(f32[1024]{0:T(1024)} %param.13) | copy-start | bytes 12292
  11.4 20.5 %copy-start.3 = (f32[3,16,4,2,128]{4,3,2,1,0:T(2,128)}, f32[3,16,4,2,128]{4,3,2,1,0:T(2,128)S(1)}, u32[]{:S(2)}) copy-start(f32[3,16,4,2,128]{4,3,2,1,0:T(2,128)S(1)} %broadcast_in_dim.11) | copy-start | bytes 589828
  14.4 6.2 %collective-permute-start = (bf16[2,128,128]{2,1,0:T(8,128)(2,1)S(1)}, bf16[2,128,128]{2,1,0:T(8,128)(2,1)S(1)}, u32[]{:S(2)}, u32[]{:S(2)}) collective-permute-start(bf16[2,128,128]{2,1,0:T(8,128)(2,1)S(1)} %get-tuple-element.37), channel_id=1, source_target_pairs={{0,4},{4,0},{8,12},{12,8},{16,20},{20,16},{24,28},{28,24},{1,5},{5... | collective-permute-start | bytes 196616 | tf_op jit(solution)/shard_map/ppermute | solution.py:293
  20.6 27.4 %copy-start.6 = (bf16[2,128,128]{2,1,0:T(8,128)(2,1)}, bf16[2,128,128]{2,1,0:T(8,128)(2,1)S(1)}, u32[]{:S(2)}) copy-start(bf16[2,128,128]{2,1,0:T(8,128)(2,1)S(1)} %collective-permute-done.near_ref.refs_2_) | copy-start | bytes 196612
  20.7 23.9 %collective-permute-start.1 = (bf16[128,128]{1,0:T(8,128)(2,1)S(1)}, bf16[128,128]{1,0:T(8,128)(2,1)S(1)}, u32[]{:S(2)}, u32[]{:S(2)}) collective-permute-start(bf16[128,128]{1,0:T(8,128)(2,1)S(1)} %convert_element_type.9), channel_id=1, source_target_pairs={{0,8},{4,12},{8,16},{12,20},{16,24},{20,28},{24,0},{28,4},{1,9},{5... | collective-permute-start | bytes 98312 | tf_op jit(solution)/shard_map/ppermute | solution.py:289
  23.1 21.5 %collective-permute-start.2 = (bf16[128,128]{1,0:T(8,128)(2,1)S(1)}, bf16[128,128]{1,0:T(8,128)(2,1)S(1)}, u32[]{:S(2)}, u32[]{:S(2)}) collective-permute-start(bf16[128,128]{1,0:T(8,128)(2,1)S(1)} %convert_element_type.10), channel_id=1, source_target_pairs={{0,16},{4,20},{8,24},{12,28},{16,0},{20,4},{24,8},{28,12},{1,17},{... | collective-permute-start | bytes 98312 | tf_op jit(solution)/shard_map/ppermute | solution.py:289
  24.9 19.6 %collective-permute-start.3 = (bf16[128,128]{1,0:T(8,128)(2,1)S(1)}, bf16[128,128]{1,0:T(8,128)(2,1)S(1)}, u32[]{:S(2)}, u32[]{:S(2)}) collective-permute-start(bf16[128,128]{1,0:T(8,128)(2,1)S(1)} %convert_element_type.11), channel_id=1, source_target_pairs={{0,24},{4,28},{8,0},{12,4},{16,8},{20,12},{24,16},{28,20},{1,25},{... | collective-permute-start | bytes 98312 | tf_op jit(solution)/shard_map/ppermute | solution.py:289
  31.9 1.4 %copy-start.5 = (f32[2,2112,128]{2,1,0:T(8,128)}, f32[2,2112,128]{2,1,0:T(8,128)S(1)}, u32[]{:S(2)}) copy-start(f32[2,2112,128]{2,1,0:T(8,128)S(1)} %get-tuple-element.51.refs_6_) | copy-start | bytes 6488068
  44.5 3.4 %copy-start.8 = (bf16[128,128]{1,0:T(8,128)(2,1)}, bf16[128,128]{1,0:T(8,128)(2,1)S(1)}, u32[]{:S(2)}) copy-start(bf16[128,128]{1,0:T(8,128)(2,1)S(1)} %collective-permute-done.1.refs_3_) | copy-start | bytes 98308
  44.5 3.4 %copy-start.9 = (bf16[128,128]{1,0:T(8,128)(2,1)}, bf16[128,128]{1,0:T(8,128)(2,1)S(1)}, u32[]{:S(2)}) copy-start(bf16[128,128]{1,0:T(8,128)(2,1)S(1)} %collective-permute-done.2.refs_4_) | copy-start | bytes 98308
  44.6 3.4 %copy-start.10 = (bf16[128,128]{1,0:T(8,128)(2,1)}, bf16[128,128]{1,0:T(8,128)(2,1)S(1)}, u32[]{:S(2)}) copy-start(bf16[128,128]{1,0:T(8,128)(2,1)S(1)} %collective-permute-done.3.refs_5_) | copy-start | bytes 98308
  44.6 10.2 %all-to-all-start.1 = ((f32[8,8,256]{2,1,0:T(8,128)}), f32[8,8,256]{2,1,0:T(8,128)S(1)}, u32[]{:S(2)}, u32[]{:S(2)}) async-start(f32[8,8,256]{2,1,0:T(8,128)} %filter_lags.1), calls=%async_computation.1 | async-start | bytes 131072 | tf_op jit(solution)/shard_map/all_to_all | solution.py:522

commit v16 on v15

--- a/solution.py
+++ b/solution.py
@@ -278,7 +278,7 @@
             jax.ShapeDtypeStruct((2, *token_shape(tok_rows, tiles)), F32),
             jax.ShapeDtypeStruct((SUBLANES, LANES), F32),
         ],
-        compiler_params=pltpu.CompilerParams(vmem_limit_bytes=VMEM_BYTES),
+        compiler_params=pltpu.CompilerParams(vmem_limit_bytes=FULL_VMEM_BYTES),
         cost_estimate=takes(6.5),
         name="local_parts",
     )(query_proj, key_proj, value_proj, out_grad, coefs, gain)
@@ -451,7 +451,7 @@
         turned_all[f] = lax.dot_general(
             mirror, u_all[f], (((1,), (1,)), ((), ())), preferred_element_type=F32
         ).astype(BF16)
-    lax.fori_loop(0, owned, one_filter, 0, unroll=min(owned, 4))
+    lax.fori_loop(0, owned, one_filter, 0, unroll=min(owned, 8))
 
 
 def filter_lags(received, done, shards, chans, owned, scale):

time: 55.7 us -> 55.9 us (level)
  Pallas kernels: 22.6 us -> 25.1 us
  waiting for transfers between devices: 12.3 us -> 10.6 us
  local copies, waits for them, and re-layouts: 2.12 us -> 1.45 us
    pallas_call x1, Pallas kernels: 6.39 us -> 9.41 us  [local_parts(): pl.pallas_call(local_kernel, out_shape=[jax.ShapeDtypeStruct((2, *token_s...]
    all_to_all x1, waiting for transfers between devices: 6.02 us -> 4.38 us  [per_device(): lax.all_to_all(send, ('seq', 'chan'), split_axis=0, concat_axis=0, tiled=...]
    unnamed x27 -> x25, local copies, waits for them, and re-layouts: 2.04 us -> 1.37 us
  transfers between devices with their start and end apart: 6 -> 6, of which waited for: 3 -> 3; matrix products, arithmetic and copies ran while one was open for 0% -> 0% of each run, Pallas kernels for 35% -> 40%
where the time goes in v16:
time: 55.9 us; the launch traced here: 55.5 us
  Pallas kernels  25.1 us (45%)
  starting transfers between devices  17.4 us (31%)
  waiting for transfers between devices  10.6 us (19%)
  local copies, waits for them, and re-layouts  1.45 us (3%)
  between operations  0.89 us (2%)
    pallas_call x1, Pallas kernels, local_parts(): pl.pallas_call(local_kernel, out_shape=[jax.ShapeDtypeStruct((2, *token_s...  9.41 us
    all_to_all x1, starting transfers between devices, per_device(): lax.all_to_all(send, ('seq', 'chan'), split_axis=0, concat_axis=0, tiled=...  7.44 us
    pallas_call x1, Pallas kernels, final_outputs(): pl.pallas_call(functools.partial(final_kernel, len(args)), in_specs=[pl.B...  4.96 us
    ppermute x3, starting transfers between devices, along_column(): return lax.ppermute(state, 'seq', route)  4.89 us
    pallas_call x1, Pallas kernels, filter_lags(): pl.pallas_call(functools.partial(lag_kernel, shards, chans, groups, owned...  4.68 us
    ppermute x1, waiting for transfers between devices, inside_pair(): return lax.ppermute(state, 'seq', [(i, i ^ 1) for i in range(2 * pairs)])  4.42 us
    all_to_all x1, waiting for transfers between devices, per_device(): lax.all_to_all(send, ('seq', 'chan'), split_axis=0, concat_axis=0, tiled=...  4.38 us
    all_to_all x1, starting transfers between devices, per_device(): lags = lax.all_to_all(lags, 'seq', split_axis=0, concat_axis=0, tiled=True)  3.36 us
  transfers between devices with their start and end apart: 6, of which 3 were waited for; matrix products, arithmetic and copies ran while one was open for 0% of the time, Pallas kernels for 40%

profile of v16, /device:TPU:0, one launch (start us, length us, event | category | flops | bytes accessed | tf_op | source)
XLA Modules:
  0.0 55.5 jit_solution(10908501270482951489)
XLA Ops:
  0.6 0.0 copy-start.2
  0.6 0.0 copy-start.1
  0.7 0.0 copy-start
  0.7 0.0 copy-start.10
  0.7 0.0 copy-start.11
  0.7 3.0 %pack_signals.1 = bf16[32,64,256]{2,1,0:T(8,128)(2,1)} custom-call(bf16[256,1024]{1,0:T(8,128)(2,1)} %refs_9_, bf16[256,1024]{1,0:T(8,128)(2,1)} %refs_8_, bf16[256,1024]{1,0:T(8,128)(2,1)} %o_ref.1, bf16[256,1024]{1,0:T(8,128)(2,1)} %refs_7_), custom_call_target="tpu_custom_call" | custom-call | bytes 10800000 | tf_op jit(solution)/shard_map/pack_signals/pallas_call | solution.py:101
  3.7 0.0 copy-start.4
  3.7 7.4 %all-to-all-start = ((bf16[32,64,256]{2,1,0:T(8,128)(2,1)}), bf16[32,64,256]{2,1,0:T(8,128)(2,1)}, u32[]{:S(2)}, u32[]{:S(2)}) async-start(bf16[32,64,256]{2,1,0:T(8,128)(2,1)} %pack_signals.1), calls=%async_computation | async-start | bytes 2097152 | tf_op jit(solution)/shard_map/all_to_all | solution.py:498
  11.2 0.0 copy-done.10
  11.2 0.0 copy-done.11
  11.3 0.1 broadcast_in_dim.11
  11.3 0.0 copy-start.3
  11.3 0.0 copy-done.2
  11.4 0.0 copy-done.1
  11.4 0.0 copy-done
  11.4 0.0 copy-done.4
  11.4 2.9 %block_states.1 = (f32[2,128,128]{2,1,0:T(8,128)S(1)}, bf16[2,128,128]{2,1,0:T(8,128)(2,1)S(1)}) custom-call(bf16[256,1024]{1,0:T(8,128)(2,1)S(1)} %copy-done, bf16[256,1024]{1,0:T(8,128)(2,1)S(1)} %copy-done.1, bf16[256,1024]{1,0:T(8,128)(2,1)S(1)} %copy-done.2, bf16[256,1024]{1,0:T(8,128)(2,1)S(1)} %copy-done.4, f32[3,16,8,128]{3,2,1,0:T(8,128)S(1)} %bitcast.14), custom_call_target="tpu_custom_call" | custom-call | bytes 10800000 | tf_op jit(solution)/shard_map/block_states/pallas_call | solution.py:189
  14.3 1.8 %collective-permute-start = (bf16[2,128,128]{2,1,0:T(8,128)(2,1)S(1)}, bf16[2,128,128]{2,1,0:T(8,128)(2,1)S(1)}, u32[]{:S(2)}, u32[]{:S(2)}) collective-permute-start(bf16[2,128,128]{2,1,0:T(8,128)(2,1)S(1)} %get-tuple-element.37), channel_id=1, source_target_pairs={{0,4},{4,0},{8,12},{12,8},{16,20},{20,16},{24,28},{28,24},{1,5},{5... | collective-permute-start | bytes 196616 | tf_op jit(solution)/shard_map/ppermute | solution.py:293
  16.1 4.4 %collective-permute-done.near_ref.refs_2_ = bf16[2,128,128]{2,1,0:T(8,128)(2,1)S(1)} collective-permute-done((bf16[2,128,128]{2,1,0:T(8,128)(2,1)S(1)}, bf16[2,128,128]{2,1,0:T(8,128)(2,1)S(1)}, u32[]{:S(2)}, u32[]{:S(2)}) %collective-permute-start) | collective-permute-done | bytes 65568 | tf_op jit(solution)/shard_map/ppermute | solution.py:293
  20.5 0.0 copy-start.5
  20.6 2.4 %collective-permute-start.1 = (bf16[128,128]{1,0:T(8,128)(2,1)S(1)}, bf16[128,128]{1,0:T(8,128)(2,1)S(1)}, u32[]{:S(2)}, u32[]{:S(2)}) collective-permute-start(bf16[128,128]{1,0:T(8,128)(2,1)S(1)} %convert_element_type.9), channel_id=1, source_target_pairs={{0,8},{4,12},{8,16},{12,20},{16,24},{20,28},{24,0},{28,4},{1,9},{5... | collective-permute-start | bytes 98312 | tf_op jit(solution)/shard_map/ppermute | solution.py:289
  23.0 1.9 %collective-permute-start.2 = (bf16[128,128]{1,0:T(8,128)(2,1)S(1)}, bf16[128,128]{1,0:T(8,128)(2,1)S(1)}, u32[]{:S(2)}, u32[]{:S(2)}) collective-permute-start(bf16[128,128]{1,0:T(8,128)(2,1)S(1)} %convert_element_type.10), channel_id=1, source_target_pairs={{0,16},{4,20},{8,24},{12,28},{16,0},{20,4},{24,8},{28,12},{1,17},{... | collective-permute-start | bytes 98312 | tf_op jit(solution)/shard_map/ppermute | solution.py:289
  24.9 0.6 %collective-permute-start.3 = (bf16[128,128]{1,0:T(8,128)(2,1)S(1)}, bf16[128,128]{1,0:T(8,128)(2,1)S(1)}, u32[]{:S(2)}, u32[]{:S(2)}) collective-permute-start(bf16[128,128]{1,0:T(8,128)(2,1)S(1)} %convert_element_type.11), channel_id=1, source_target_pairs={{0,24},{4,28},{8,0},{12,4},{16,8},{20,12},{24,16},{28,20},{1,25},{... | collective-permute-start | bytes 98312 | tf_op jit(solution)/shard_map/ppermute | solution.py:289
  25.5 0.0 copy-done.3
  25.5 9.4 %local_parts.1 = (f32[2,2112,128]{2,1,0:T(8,128)}, f32[8,128]{1,0:T(8,128)}) custom-call(bf16[256,1024]{1,0:T(8,128)(2,1)} %refs_7_, bf16[256,1024]{1,0:T(8,128)(2,1)} %refs_9_, bf16[256,1024]{1,0:T(8,128)(2,1)} %refs_8_, bf16[256,1024]{1,0:T(8,128)(2,1)} %o_ref.1, f32[3,16,8,128]{3,2,1,0:T(8,128)} %bitcast.16, f32[1,1024]{1,0:T(1,128)} %bitcast.19), custom_call_target="tpu_custom_call" | custom-call | bytes 23400000 | tf_op jit(solution)/shard_map/local_parts/pallas_call | solution.py:275
  34.9 4.4 %all-to-all-done.refs_1_ = bf16[32,64,256]{2,1,0:T(8,128)(2,1)} async-done(((bf16[32,64,256]{2,1,0:T(8,128)(2,1)}), bf16[32,64,256]{2,1,0:T(8,128)(2,1)}, u32[]{:S(2)}, u32[]{:S(2)}) %all-to-all-start) | async-done | bytes 1048608 | tf_op jit(solution)/shard_map/all_to_all | solution.py:498
  39.3 0.0 copy-start.6
  39.3 0.7 %copy-done.6 = f32[8,128]{1,0:T(8,128)S(1)} copy-done((f32[8,128]{1,0:T(8,128)S(1)}, f32[8,128]{1,0:T(8,128)}, u32[]{:S(2)}) %copy-start.6) | copy-done | bytes 4120
  40.0 4.7 %filter_lags.1 = f32[8,8,256]{2,1,0:T(8,128)} custom-call(f32[8,128]{1,0:T(8,128)S(1)} %copy-done.6, bf16[32,64,256]{2,1,0:T(8,128)(2,1)} %all-to-all-done.refs_1_), custom_call_target="tpu_custom_call" | custom-call | bytes 360000 | tf_op jit(solution)/shard_map/filter_lags/pallas_call | solution.py:469
  44.6 0.0 collective-permute-done.1.refs_3_
  44.6 0.0 copy-start.7
  44.7 0.0 collective-permute-done.2.refs_4_
  44.7 0.0 copy-start.8
  44.7 0.0 collective-permute-done.3.refs_5_
  44.7 0.0 copy-start.9
  44.7 3.4 %all-to-all-start.1 = ((f32[8,8,256]{2,1,0:T(8,128)}), f32[8,8,256]{2,1,0:T(8,128)S(1)}, u32[]{:S(2)}, u32[]{:S(2)}) async-start(f32[8,8,256]{2,1,0:T(8,128)} %filter_lags.1), calls=%async_computation.1 | async-start | bytes 131072 | tf_op jit(solution)/shard_map/all_to_all | solution.py:522
  48.1 0.0 copy-done.5
  48.1 0.0 copy-done.7
  48.1 0.0 copy-done.8
  48.1 0.0 copy-done.9
  48.1 5.0 %final_outputs.1 = (bf16[256,1024]{1,0:T(8,128)(2,1)}, bf16[256,1024]{1,0:T(8,128)(2,1)}, bf16[256,1024]{1,0:T(8,128)(2,1)}) custom-call(s32[1]{0:T(128)} %bitcast.seq_ref.refs_0_, f32[3,16,8,128]{3,2,1,0:T(8,128)} %bitcast.17, bf16[2,128,128]{2,1,0:T(8,128)(2,1)} %copy-done.5, bf16[128,128]{1,0:T(8,128)(2,1)} %copy-done.7, bf16[128,128]{1,0:T(8,128)(2,1)} %copy-done.8, ...), custom_call_target="tpu_custom_call" | custom-call | bytes 18000000 | tf_op jit(solution)/shard_map/final_outputs/pallas_call | solution.py:364
  53.1 1.8 %all-to-all-done.1 = f32[8,8,256]{2,1,0:T(8,128)S(1)} async-done(((f32[8,8,256]{2,1,0:T(8,128)}), f32[8,8,256]{2,1,0:T(8,128)S(1)}, u32[]{:S(2)}, u32[]{:S(2)}) %all-to-all-start.1) | async-done | bytes 65568 | tf_op jit(solution)/shard_map/all_to_all | solution.py:522
  54.9 0.6 %copy.12 = f32[256,64]{0,1:T(8,128)} copy(f32[256,64]{0,1:T(8,128)S(1)} %bitcast.18) | data formatting | bytes 131072
  (7 shorter events, 0.1 us)
Async XLA Ops:
  0.6 10.7 %copy-start.2 = (bf16[256,1024]{1,0:T(8,128)(2,1)S(1)}, bf16[256,1024]{1,0:T(8,128)(2,1)}, u32[]{:S(2)}) copy-start(bf16[256,1024]{1,0:T(8,128)(2,1)} %refs_8_) | copy-start | bytes 1572868
  0.6 10.7 %copy-start.1 = (bf16[256,1024]{1,0:T(8,128)(2,1)S(1)}, bf16[256,1024]{1,0:T(8,128)(2,1)}, u32[]{:S(2)}) copy-start(bf16[256,1024]{1,0:T(8,128)(2,1)} %refs_9_) | copy-start | bytes 1572868
  0.7 10.7 %copy-start = (bf16[256,1024]{1,0:T(8,128)(2,1)S(1)}, bf16[256,1024]{1,0:T(8,128)(2,1)}, u32[]{:S(2)}) copy-start(bf16[256,1024]{1,0:T(8,128)(2,1)} %refs_7_) | copy-start | bytes 1572868
  0.7 10.5 %copy-start.10 = (f32[256,16]{0,1:T(8,128)S(1)}, f32[256,16]{0,1:T(8,128)}, u32[]{:S(2)}) copy-start(f32[256,16]{0,1:T(8,128)} %param.12) | copy-start | bytes 49156
  0.7 10.5 %copy-start.11 = (f32[256,16]{0,1:T(8,128)S(1)}, f32[256,16]{0,1:T(8,128)}, u32[]{:S(2)}) copy-start(f32[256,16]{0,1:T(8,128)} %param.11) | copy-start | bytes 49156
  3.7 7.7 %copy-start.4 = (bf16[256,1024]{1,0:T(8,128)(2,1)S(1)}, bf16[256,1024]{1,0:T(8,128)(2,1)}, u32[]{:S(2)}) copy-start(bf16[256,1024]{1,0:T(8,128)(2,1)} %o_ref.1) | copy-start | bytes 1572868
  3.7 35.5 %all-to-all-start = ((bf16[32,64,256]{2,1,0:T(8,128)(2,1)}), bf16[32,64,256]{2,1,0:T(8,128)(2,1)}, u32[]{:S(2)}, u32[]{:S(2)}) async-start(bf16[32,64,256]{2,1,0:T(8,128)(2,1)} %pack_signals.1), calls=%async_computation | async-start | bytes 2097152 | tf_op jit(solution)/shard_map/all_to_all | solution.py:498
  11.3 14.1 %copy-start.3 = (f32[3,16,4,2,128]{4,3,2,1,0:T(2,128)}, f32[3,16,4,2,128]{4,3,2,1,0:T(2,128)S(1)}, u32[]{:S(2)}) copy-start(f32[3,16,4,2,128]{4,3,2,1,0:T(2,128)S(1)} %broadcast_in_dim.11) | copy-start | bytes 589828
  14.3 6.2 %collective-permute-start = (bf16[2,128,128]{2,1,0:T(8,128)(2,1)S(1)}, bf16[2,128,128]{2,1,0:T(8,128)(2,1)S(1)}, u32[]{:S(2)}, u32[]{:S(2)}) collective-permute-start(bf16[2,128,128]{2,1,0:T(8,128)(2,1)S(1)} %get-tuple-element.37), channel_id=1, source_target_pairs={{0,4},{4,0},{8,12},{12,8},{16,20},{20,16},{24,28},{28,24},{1,5},{5... | collective-permute-start | bytes 196616 | tf_op jit(solution)/shard_map/ppermute | solution.py:293
  20.5 27.5 %copy-start.5 = (bf16[2,128,128]{2,1,0:T(8,128)(2,1)}, bf16[2,128,128]{2,1,0:T(8,128)(2,1)S(1)}, u32[]{:S(2)}) copy-start(bf16[2,128,128]{2,1,0:T(8,128)(2,1)S(1)} %collective-permute-done.near_ref.refs_2_) | copy-start | bytes 196612
  20.6 24.1 %collective-permute-start.1 = (bf16[128,128]{1,0:T(8,128)(2,1)S(1)}, bf16[128,128]{1,0:T(8,128)(2,1)S(1)}, u32[]{:S(2)}, u32[]{:S(2)}) collective-permute-start(bf16[128,128]{1,0:T(8,128)(2,1)S(1)} %convert_element_type.9), channel_id=1, source_target_pairs={{0,8},{4,12},{8,16},{12,20},{16,24},{20,28},{24,0},{28,4},{1,9},{5... | collective-permute-start | bytes 98312 | tf_op jit(solution)/shard_map/ppermute | solution.py:289
  23.0 21.6 %collective-permute-start.2 = (bf16[128,128]{1,0:T(8,128)(2,1)S(1)}, bf16[128,128]{1,0:T(8,128)(2,1)S(1)}, u32[]{:S(2)}, u32[]{:S(2)}) collective-permute-start(bf16[128,128]{1,0:T(8,128)(2,1)S(1)} %convert_element_type.10), channel_id=1, source_target_pairs={{0,16},{4,20},{8,24},{12,28},{16,0},{20,4},{24,8},{28,12},{1,17},{... | collective-permute-start | bytes 98312 | tf_op jit(solution)/shard_map/ppermute | solution.py:289
  24.9 19.7 %collective-permute-start.3 = (bf16[128,128]{1,0:T(8,128)(2,1)S(1)}, bf16[128,128]{1,0:T(8,128)(2,1)S(1)}, u32[]{:S(2)}, u32[]{:S(2)}) collective-permute-start(bf16[128,128]{1,0:T(8,128)(2,1)S(1)} %convert_element_type.11), channel_id=1, source_target_pairs={{0,24},{4,28},{8,0},{12,4},{16,8},{20,12},{24,16},{28,20},{1,25},{... | collective-permute-start | bytes 98312 | tf_op jit(solution)/shard_map/ppermute | solution.py:289
  39.3 0.7 %copy-start.6 = (f32[8,128]{1,0:T(8,128)S(1)}, f32[8,128]{1,0:T(8,128)}, u32[]{:S(2)}) copy-start(f32[8,128]{1,0:T(8,128)} %get-tuple-element.43.refs_0_) | copy-start | bytes 12292
  44.6 3.4 %copy-start.7 = (bf16[128,128]{1,0:T(8,128)(2,1)}, bf16[128,128]{1,0:T(8,128)(2,1)S(1)}, u32[]{:S(2)}) copy-start(bf16[128,128]{1,0:T(8,128)(2,1)S(1)} %collective-permute-done.1.refs_3_) | copy-start | bytes 98308
  44.7 3.4 %copy-start.8 = (bf16[128,128]{1,0:T(8,128)(2,1)}, bf16[128,128]{1,0:T(8,128)(2,1)S(1)}, u32[]{:S(2)}) copy-start(bf16[128,128]{1,0:T(8,128)(2,1)S(1)} %collective-permute-done.2.refs_4_) | copy-start | bytes 98308
  44.7 3.4 %copy-start.9 = (bf16[128,128]{1,0:T(8,128)(2,1)}, bf16[128,128]{1,0:T(8,128)(2,1)S(1)}, u32[]{:S(2)}) copy-start(bf16[128,128]{1,0:T(8,128)(2,1)S(1)} %collective-permute-done.3.refs_5_) | copy-start | bytes 98308
  44.7 10.2 %all-to-all-start.1 = ((f32[8,8,256]{2,1,0:T(8,128)}), f32[8,8,256]{2,1,0:T(8,128)S(1)}, u32[]{:S(2)}, u32[]{:S(2)}) async-start(f32[8,8,256]{2,1,0:T(8,128)} %filter_lags.1), calls=%async_computation.1 | async-start | bytes 131072 | tf_op jit(solution)/shard_map/all_to_all | solution.py:522

commit v17 on v16

--- a/solution.py
+++ b/solution.py
@@ -249,9 +249,8 @@
 
 
 def local_kernel(
-    q_ref, k_ref, v_ref, o_ref, coef_ref, gain_ref, part_ref, done_ref
+    q_ref, k_ref, v_ref, o_ref, coef_ref, gain_ref, conv_ref, grad_ref, done_ref
 ):
-    conv_ref, grad_ref = part_ref.at[0], part_ref.at[1]
     tok_rows, width = k_ref.shape
     tiles = width // LANES
     spread_tokens(k_ref, v_ref, conv_ref)
@@ -274,11 +273,9 @@
     tiles = coefs.shape[2]
     return pl.pallas_call(
         local_kernel,
-        out_shape=[
-            jax.ShapeDtypeStruct((2, *token_shape(tok_rows, tiles)), F32),
-            jax.ShapeDtypeStruct((SUBLANES, LANES), F32),
-        ],
-        compiler_params=pltpu.CompilerParams(vmem_limit_bytes=FULL_VMEM_BYTES),
+        out_shape=[jax.ShapeDtypeStruct(token_shape(tok_rows, tiles), F32)] * 2
+        + [jax.ShapeDtypeStruct((SUBLANES, LANES), F32)],
+        compiler_params=pltpu.CompilerParams(vmem_limit_bytes=VMEM_BYTES),
         cost_estimate=takes(6.5),
         name="local_parts",
     )(query_proj, key_proj, value_proj, out_grad, coefs, gain)
@@ -310,25 +307,22 @@
     seq_ref, hbm_refs, refs = refs[0], refs[1 : 1 + count], refs[1 + count :]
     out_hbm, held_refs, refs = refs[:3], refs[3 : 3 + count], refs[3 + count :]
     edge_ref, out_refs, in_sems, out_sems = refs[0], refs[1:4], refs[4], refs[5]
-    coef_ref, near_ref, *state_refs = held_refs[:-4]
-    part_ref, q_ref, v_ref, k_ref = held_refs[-4:]
+    coef_ref, near_ref, *state_refs = held_refs[:-5]
+    conv_ref, q_ref, grad_ref, v_ref, k_ref = held_refs[-5:]
     tok_rows, width = k_ref.shape
     tiles = width // LANES
-    pieces = list(zip(hbm_refs[:-4], held_refs[:-4]))
-    small = len(pieces)
-    pieces += [(hbm_refs[-4].at[0], part_ref.at[0]), (hbm_refs[-3], q_ref)]
-    pieces += [(hbm_refs[-4].at[1], part_ref.at[1])] + list(zip(hbm_refs[-2:], held_refs[-2:]))
+    small = count - 5
     arrivals = [
         pltpu.make_async_copy(source, target, in_sems.at[i])
-        for i, (source, target) in enumerate(pieces)
+        for i, (source, target) in enumerate(zip(hbm_refs, held_refs))
     ]
     departures = []
 
-    def multiply_out(side, outs):
+    def multiply_out(part_ref, outs):
         for tile in range(tiles):
             cols = slice(tile * LANES, (tile + 1) * LANES)
             rows = tile_rows(tok_rows, tile)
-            value = part_ref[side, rows, :] + edge_ref[rows, :]
+            value = part_ref[rows, :] + edge_ref[rows, :]
             for i, factor_ref in outs:
                 out_refs[i][:, cols] = (value * factor_ref[:, cols].astype(F32)).astype(BF16)
                 place = (slice(None), pl.ds(tile * LANES, LANES))
@@ -346,20 +340,22 @@
     fill_edge(edge_ref, held, coef_ref, tok_rows, tiles, 0, 1)
     for copy in arrivals[small : small + 2]:
         copy.wait()
-    multiply_out(0, [(0, q_ref)])
+    multiply_out(conv_ref, [(0, q_ref)])
     held = sum_pairs(1, seq_ref[0], coef_ref, near_ref, state_refs)
     fill_edge(edge_ref, held, coef_ref, tok_rows, tiles, tok_rows - 1, -1)
     for copy in arrivals[small + 2 :]:
         copy.wait()
-    multiply_out(1, [(1, v_ref), (2, k_ref)])
+    multiply_out(grad_ref, [(1, v_ref), (2, k_ref)])
     for copy in departures:
         copy.wait()
 
 
-def final_outputs(seq_index, coefs, near, states, parts, query_proj, value_proj, key_proj):
+def final_outputs(
+    seq_index, coefs, near, states, conv_part, grad_part, query_proj, value_proj, key_proj
+):
     tok_rows, width = key_proj.shape
     tiles = coefs.shape[2]
-    args = (coefs, near, *states, parts, query_proj, value_proj, key_proj)
+    args = (coefs, near, *states, conv_part, query_proj, grad_part, value_proj, key_proj)
     away = pl.BlockSpec(memory_space=pl.ANY)
     return pl.pallas_call(
         functools.partial(final_kernel, len(args)),
@@ -369,7 +365,7 @@
         scratch_shapes=[pltpu.VMEM(arg.shape, arg.dtype) for arg in args]
         + [pltpu.VMEM(token_shape(tok_rows, tiles), F32)]
         + [pltpu.VMEM((tok_rows, width), BF16)] * 3
-        + [pltpu.SemaphoreType.DMA((len(args) + 1,)), pltpu.SemaphoreType.DMA((3, tiles))],
+        + [pltpu.SemaphoreType.DMA((len(args),)), pltpu.SemaphoreType.DMA((3, tiles))],
         compiler_params=pltpu.CompilerParams(vmem_limit_bytes=FULL_VMEM_BYTES),
         cost_estimate=takes(5.0),
         name="final_outputs",
@@ -514,7 +510,7 @@
     states = pair_states(seq_index, pairs, coefs, own, near)
     *states, coefs, near = lax.optimization_barrier((*states, coefs, near))
     states = [along_column(state, pairs, 1 + i) for i, state in enumerate(states)]
-    parts, done = local_parts(*signals, coefs, skip_gain[None, :])
+    conv_part, grad_part, done = local_parts(*signals, coefs, skip_gain[None, :])
 
     scale = 1.0 / math.sqrt(length * (CHANNELS // FILTERS))
     lags = filter_lags(received, done, shards, chans, owned, scale)
@@ -523,7 +519,7 @@
     filter_grad = lags.reshape(shards * owned, tok_rows).T
     query_proj, key_proj, value_proj, _ = signals
     layer_out, key_grad, value_grad = final_outputs(
-        seq_index, coefs, near, states, parts, query_proj, value_proj, key_proj
+        seq_index, coefs, near, states, conv_part, grad_part, query_proj, value_proj, key_proj
     )
     return (layer_out, key_grad, value_grad, filter_grad)
 

time: 55.9 us -> 55.1 us (0.986)
  Pallas kernels: 25.1 us -> 21.9 us
  local copies, waits for them, and re-layouts: 1.45 us -> 2.76 us
  waiting for transfers between devices: 10.6 us -> 11.8 us
    pallas_call x1, Pallas kernels: 9.41 us -> 6.29 us  [local_parts(): pl.pallas_call(local_kernel, out_shape=[jax.ShapeDtypeStruct(token_shape(...]
    unnamed x25 -> x29, local copies, waits for them, and re-layouts: 1.37 us -> 2.68 us
    all_to_all x1, waiting for transfers between devices: 4.38 us -> 5.48 us  [per_device(): lax.all_to_all(send, ('seq', 'chan'), split_axis=0, concat_axis=0, tiled=...]
  transfers between devices with their start and end apart: 6 -> 6, of which waited for: 3 -> 3; matrix products, arithmetic and copies ran while one was open for 0% -> 0% of each run, Pallas kernels for 40% -> 35%
where the time goes in v17:
time: 55.1 us; the launch traced here: 54.8 us
  Pallas kernels  21.9 us (40%)
  starting transfers between devices  17.4 us (32%)
  waiting for transfers between devices  11.8 us (21%)
  local copies, waits for them, and re-layouts  2.76 us (5%)
  between operations  0.91 us (2%)
    all_to_all x1, starting transfers between devices, per_device(): lax.all_to_all(send, ('seq', 'chan'), split_axis=0, concat_axis=0, tiled=...  7.44 us
    pallas_call x1, Pallas kernels, local_parts(): pl.pallas_call(local_kernel, out_shape=[jax.ShapeDtypeStruct(token_shape(...  6.29 us
    all_to_all x1, waiting for transfers between devices, per_device(): lax.all_to_all(send, ('seq', 'chan'), split_axis=0, concat_axis=0, tiled=...  5.48 us
    pallas_call x1, Pallas kernels, final_outputs(): pl.pallas_call(functools.partial(final_kernel, len(args)), in_specs=[pl.B...  4.96 us
    ppermute x3, starting transfers between devices, along_column(): return lax.ppermute(state, 'seq', route)  4.86 us
    pallas_call x1, Pallas kernels, filter_lags(): pl.pallas_call(functools.partial(lag_kernel, shards, chans, groups, owned...  4.7 us
    ppermute x1, waiting for transfers between devices, inside_pair(): return lax.ppermute(state, 'seq', [(i, i ^ 1) for i in range(2 * pairs)])  4.43 us
    all_to_all x1, starting transfers between devices, per_device(): lags = lax.all_to_all(lags, 'seq', split_axis=0, concat_axis=0, tiled=True)  3.36 us
  transfers between devices with their start and end apart: 6, of which 3 were waited for; matrix products, arithmetic and copies ran while one was open for 0% of the time, Pallas kernels for 35%

profile of v17, /device:TPU:0, one launch (start us, length us, event | category | flops | bytes accessed | tf_op | source)
XLA Modules:
  0.0 54.8 jit_solution(13192581576094409254)
XLA Ops:
  0.6 0.0 copy-start.12
  0.6 0.0 copy-start.13
  0.7 2.9 %pack_signals.1 = bf16[32,64,256]{2,1,0:T(8,128)(2,1)} custom-call(bf16[256,1024]{1,0:T(8,128)(2,1)} %refs_10_, bf16[256,1024]{1,0:T(8,128)(2,1)} %refs_9_, bf16[256,1024]{1,0:T(8,128)(2,1)} %o_ref.1, bf16[256,1024]{1,0:T(8,128)(2,1)} %refs_7_), custom_call_target="tpu_custom_call" | custom-call | bytes 10800000 | tf_op jit(solution)/shard_map/pack_signals/pallas_call | solution.py:101
  3.6 0.0 copy-start
  3.6 0.0 copy-start.1
  3.6 0.0 copy-start.2
  3.6 0.0 copy-start.4
  3.6 7.4 %all-to-all-start = ((bf16[32,64,256]{2,1,0:T(8,128)(2,1)}), bf16[32,64,256]{2,1,0:T(8,128)(2,1)}, u32[]{:S(2)}, u32[]{:S(2)}) async-start(bf16[32,64,256]{2,1,0:T(8,128)(2,1)} %pack_signals.1), calls=%async_computation | async-start | bytes 2097152 | tf_op jit(solution)/shard_map/all_to_all | solution.py:494
  11.1 0.0 copy-done.12
  11.1 0.0 copy-done.13
  11.2 0.1 broadcast_in_dim.11
  11.2 0.0 copy-start.3
  11.2 0.0 copy-done
  11.3 0.0 copy-done.1
  11.3 0.0 copy-done.2
  11.3 0.0 copy-done.4
  11.3 0.0 copy-start.8
  11.3 2.9 %block_states.1 = (f32[2,128,128]{2,1,0:T(8,128)S(1)}, bf16[2,128,128]{2,1,0:T(8,128)(2,1)S(1)}) custom-call(bf16[256,1024]{1,0:T(8,128)(2,1)S(1)} %copy-done, bf16[256,1024]{1,0:T(8,128)(2,1)S(1)} %copy-done.1, bf16[256,1024]{1,0:T(8,128)(2,1)S(1)} %copy-done.2, bf16[256,1024]{1,0:T(8,128)(2,1)S(1)} %copy-done.4, f32[3,16,8,128]{3,2,1,0:T(8,128)S(1)} %bitcast.14), custom_call_target="tpu_custom_call" | custom-call | bytes 10800000 | tf_op jit(solution)/shard_map/block_states/pallas_call | solution.py:189
  14.2 1.8 %collective-permute-start = (bf16[2,128,128]{2,1,0:T(8,128)(2,1)S(1)}, bf16[2,128,128]{2,1,0:T(8,128)(2,1)S(1)}, u32[]{:S(2)}, u32[]{:S(2)}) collective-permute-start(bf16[2,128,128]{2,1,0:T(8,128)(2,1)S(1)} %get-tuple-element.38), channel_id=1, source_target_pairs={{0,4},{4,0},{8,12},{12,8},{16,20},{20,16},{24,28},{28,24},{1,5},{5... | collective-permute-start | bytes 196616 | tf_op jit(solution)/shard_map/ppermute | solution.py:290
  16.0 4.4 %collective-permute-done.near_ref.refs_2_ = bf16[2,128,128]{2,1,0:T(8,128)(2,1)S(1)} collective-permute-done((bf16[2,128,128]{2,1,0:T(8,128)(2,1)S(1)}, bf16[2,128,128]{2,1,0:T(8,128)(2,1)S(1)}, u32[]{:S(2)}, u32[]{:S(2)}) %collective-permute-start) | collective-permute-done | bytes 65568 | tf_op jit(solution)/shard_map/ppermute | solution.py:290
  20.4 0.0 copy-start.7
  20.5 2.4 %collective-permute-start.1 = (bf16[128,128]{1,0:T(8,128)(2,1)S(1)}, bf16[128,128]{1,0:T(8,128)(2,1)S(1)}, u32[]{:S(2)}, u32[]{:S(2)}) collective-permute-start(bf16[128,128]{1,0:T(8,128)(2,1)S(1)} %convert_element_type.9), channel_id=1, source_target_pairs={{0,8},{4,12},{8,16},{12,20},{16,24},{20,28},{24,0},{28,4},{1,9},{5... | collective-permute-start | bytes 98312 | tf_op jit(solution)/shard_map/ppermute | solution.py:286
  22.9 1.9 %collective-permute-start.2 = (bf16[128,128]{1,0:T(8,128)(2,1)S(1)}, bf16[128,128]{1,0:T(8,128)(2,1)S(1)}, u32[]{:S(2)}, u32[]{:S(2)}) collective-permute-start(bf16[128,128]{1,0:T(8,128)(2,1)S(1)} %convert_element_type.10), channel_id=1, source_target_pairs={{0,16},{4,20},{8,24},{12,28},{16,0},{20,4},{24,8},{28,12},{1,17},{... | collective-permute-start | bytes 98312 | tf_op jit(solution)/shard_map/ppermute | solution.py:286
  24.8 0.6 %collective-permute-start.3 = (bf16[128,128]{1,0:T(8,128)(2,1)S(1)}, bf16[128,128]{1,0:T(8,128)(2,1)S(1)}, u32[]{:S(2)}, u32[]{:S(2)}) collective-permute-start(bf16[128,128]{1,0:T(8,128)(2,1)S(1)} %convert_element_type.11), channel_id=1, source_target_pairs={{0,24},{4,28},{8,0},{12,4},{16,8},{20,12},{24,16},{28,20},{1,25},{... | collective-permute-start | bytes 98312 | tf_op jit(solution)/shard_map/ppermute | solution.py:286
  25.4 0.0 copy-done.3
  25.4 0.0 copy-done.8
  25.4 6.3 %local_parts.1 = (f32[2112,128]{1,0:T(8,128)S(1)}, f32[2112,128]{1,0:T(8,128)S(1)}, f32[8,128]{1,0:T(8,128)S(1)}) custom-call(bf16[256,1024]{1,0:T(8,128)(2,1)S(1)} %copy-done, bf16[256,1024]{1,0:T(8,128)(2,1)S(1)} %copy-done.1, bf16[256,1024]{1,0:T(8,128)(2,1)S(1)} %copy-done.2, bf16[256,1024]{1,0:T(8,128)(2,1)S(1)} %copy-done.4, ...), custom_call_target="tpu_custom_call" | custom-call | bytes 23400000 | tf_op jit(solution)/shard_map/local_parts/pallas_call | solution.py:274
  31.7 0.0 copy-done.7
  31.7 0.0 copy-start.5
  31.7 1.0 %copy-done.5 = f32[2112,128]{1,0:T(8,128)} copy-done((f32[2112,128]{1,0:T(8,128)}, f32[2112,128]{1,0:T(8,128)S(1)}, u32[]{:S(2)}) %copy-start.5) | copy-done | bytes 1081368
  32.7 0.0 copy-start.6
  32.7 1.0 %copy-done.6 = f32[2112,128]{1,0:T(8,128)} copy-done((f32[2112,128]{1,0:T(8,128)}, f32[2112,128]{1,0:T(8,128)S(1)}, u32[]{:S(2)}) %copy-start.6) | copy-done | bytes 1081368
  33.7 5.5 %all-to-all-done.refs_1_ = bf16[32,64,256]{2,1,0:T(8,128)(2,1)} async-done(((bf16[32,64,256]{2,1,0:T(8,128)(2,1)}), bf16[32,64,256]{2,1,0:T(8,128)(2,1)}, u32[]{:S(2)}, u32[]{:S(2)}) %all-to-all-start) | async-done | bytes 1048608 | tf_op jit(solution)/shard_map/all_to_all | solution.py:494
  39.2 4.7 %filter_lags.1 = f32[8,8,256]{2,1,0:T(8,128)} custom-call(f32[8,128]{1,0:T(8,128)S(1)} %get-tuple-element.44.refs_0_, bf16[32,64,256]{2,1,0:T(8,128)(2,1)} %all-to-all-done.refs_1_), custom_call_target="tpu_custom_call" | custom-call | bytes 360000 | tf_op jit(solution)/shard_map/filter_lags/pallas_call | solution.py:465
  43.9 0.0 collective-permute-done.1.refs_3_
  43.9 0.0 copy-start.9
  43.9 0.0 collective-permute-done.2.refs_4_
  43.9 0.0 copy-start.10
  43.9 0.0 collective-permute-done.3.refs_5_
  43.9 0.0 copy-start.11
  43.9 3.4 %all-to-all-start.1 = ((f32[8,8,256]{2,1,0:T(8,128)}), f32[8,8,256]{2,1,0:T(8,128)S(1)}, u32[]{:S(2)}, u32[]{:S(2)}) async-start(f32[8,8,256]{2,1,0:T(8,128)} %filter_lags.1), calls=%async_computation.1 | async-start | bytes 131072 | tf_op jit(solution)/shard_map/all_to_all | solution.py:518
  47.3 0.0 copy-done.9
  47.3 0.0 copy-done.10
  47.3 0.0 copy-done.11
  47.3 5.0 %final_outputs.1 = (bf16[256,1024]{1,0:T(8,128)(2,1)}, bf16[256,1024]{1,0:T(8,128)(2,1)}, bf16[256,1024]{1,0:T(8,128)(2,1)}) custom-call(s32[1]{0:T(128)} %bitcast.seq_ref.refs_0_, f32[3,16,8,128]{3,2,1,0:T(8,128)} %bitcast.17, bf16[2,128,128]{2,1,0:T(8,128)(2,1)} %copy-done.7, bf16[128,128]{1,0:T(8,128)(2,1)} %copy-done.9, bf16[128,128]{1,0:T(8,128)(2,1)} %copy-done.10, ...), custom_call_target="tpu_custom_call" | custom-call | bytes 18000000 | tf_op jit(solution)/shard_map/final_outputs/pallas_call | solution.py:360
  52.3 1.8 %all-to-all-done.1 = f32[8,8,256]{2,1,0:T(8,128)S(1)} async-done(((f32[8,8,256]{2,1,0:T(8,128)}), f32[8,8,256]{2,1,0:T(8,128)S(1)}, u32[]{:S(2)}, u32[]{:S(2)}) %all-to-all-start.1) | async-done | bytes 65568 | tf_op jit(solution)/shard_map/all_to_all | solution.py:518
  54.1 0.6 %copy.12 = f32[256,64]{0,1:T(8,128)} copy(f32[256,64]{0,1:T(8,128)S(1)} %bitcast.19) | data formatting | bytes 131072
  (7 shorter events, 0.1 us)
Async XLA Ops:
  0.6 10.5 %copy-start.12 = (f32[256,16]{0,1:T(8,128)S(1)}, f32[256,16]{0,1:T(8,128)}, u32[]{:S(2)}) copy-start(f32[256,16]{0,1:T(8,128)} %param.12) | copy-start | bytes 49156
  0.6 10.5 %copy-start.13 = (f32[256,16]{0,1:T(8,128)S(1)}, f32[256,16]{0,1:T(8,128)}, u32[]{:S(2)}) copy-start(f32[256,16]{0,1:T(8,128)} %param.11) | copy-start | bytes 49156
  3.6 7.7 %copy-start = (bf16[256,1024]{1,0:T(8,128)(2,1)S(1)}, bf16[256,1024]{1,0:T(8,128)(2,1)}, u32[]{:S(2)}) copy-start(bf16[256,1024]{1,0:T(8,128)(2,1)} %refs_7_) | copy-start | bytes 1572868
  3.6 7.7 %copy-start.1 = (bf16[256,1024]{1,0:T(8,128)(2,1)S(1)}, bf16[256,1024]{1,0:T(8,128)(2,1)}, u32[]{:S(2)}) copy-start(bf16[256,1024]{1,0:T(8,128)(2,1)} %refs_10_) | copy-start | bytes 1572868
  3.6 7.7 %copy-start.2 = (bf16[256,1024]{1,0:T(8,128)(2,1)S(1)}, bf16[256,1024]{1,0:T(8,128)(2,1)}, u32[]{:S(2)}) copy-start(bf16[256,1024]{1,0:T(8,128)(2,1)} %refs_9_) | copy-start | bytes 1572868
  3.6 7.7 %copy-start.4 = (bf16[256,1024]{1,0:T(8,128)(2,1)S(1)}, bf16[256,1024]{1,0:T(8,128)(2,1)}, u32[]{:S(2)}) copy-start(bf16[256,1024]{1,0:T(8,128)(2,1)} %o_ref.1) | copy-start | bytes 1572868
  3.6 35.5 %all-to-all-start = ((bf16[32,64,256]{2,1,0:T(8,128)(2,1)}), bf16[32,64,256]{2,1,0:T(8,128)(2,1)}, u32[]{:S(2)}, u32[]{:S(2)}) async-start(bf16[32,64,256]{2,1,0:T(8,128)(2,1)} %pack_signals.1), calls=%async_computation | async-start | bytes 2097152 | tf_op jit(solution)/shard_map/all_to_all | solution.py:494
  11.2 14.1 %copy-start.3 = (f32[3,16,4,2,128]{4,3,2,1,0:T(2,128)}, f32[3,16,4,2,128]{4,3,2,1,0:T(2,128)S(1)}, u32[]{:S(2)}) copy-start(f32[3,16,4,2,128]{4,3,2,1,0:T(2,128)S(1)} %broadcast_in_dim.11) | copy-start | bytes 589828
  11.3 14.1 %copy-start.8 = (f32[1024]{0:T(1024)S(1)}, f32[1024]{0:T(1024)}, u32[]{:S(2)}) copy-start(f32[1024]{0:T(1024)} %param.13) | copy-start | bytes 12292
  14.2 6.2 %collective-permute-start = (bf16[2,128,128]{2,1,0:T(8,128)(2,1)S(1)}, bf16[2,128,128]{2,1,0:T(8,128)(2,1)S(1)}, u32[]{:S(2)}, u32[]{:S(2)}) collective-permute-start(bf16[2,128,128]{2,1,0:T(8,128)(2,1)S(1)} %get-tuple-element.38), channel_id=1, source_target_pairs={{0,4},{4,0},{8,12},{12,8},{16,20},{20,16},{24,28},{28,24},{1,5},{5... | collective-permute-start | bytes 196616 | tf_op jit(solution)/shard_map/ppermute | solution.py:290
  20.4 11.3 %copy-start.7 = (bf16[2,128,128]{2,1,0:T(8,128)(2,1)}, bf16[2,128,128]{2,1,0:T(8,128)(2,1)S(1)}, u32[]{:S(2)}) copy-start(bf16[2,128,128]{2,1,0:T(8,128)(2,1)S(1)} %collective-permute-done.near_ref.refs_2_) | copy-start | bytes 196612
  20.5 23.4 %collective-permute-start.1 = (bf16[128,128]{1,0:T(8,128)(2,1)S(1)}, bf16[128,128]{1,0:T(8,128)(2,1)S(1)}, u32[]{:S(2)}, u32[]{:S(2)}) collective-permute-start(bf16[128,128]{1,0:T(8,128)(2,1)S(1)} %convert_element_type.9), channel_id=1, source_target_pairs={{0,8},{4,12},{8,16},{12,20},{16,24},{20,28},{24,0},{28,4},{1,9},{5... | collective-permute-start | bytes 98312 | tf_op jit(solution)/shard_map/ppermute | solution.py:286
  22.9 20.9 %collective-permute-start.2 = (bf16[128,128]{1,0:T(8,128)(2,1)S(1)}, bf16[128,128]{1,0:T(8,128)(2,1)S(1)}, u32[]{:S(2)}, u32[]{:S(2)}) collective-permute-start(bf16[128,128]{1,0:T(8,128)(2,1)S(1)} %convert_element_type.10), channel_id=1, source_target_pairs={{0,16},{4,20},{8,24},{12,28},{16,0},{20,4},{24,8},{28,12},{1,17},{... | collective-permute-start | bytes 98312 | tf_op jit(solution)/shard_map/ppermute | solution.py:286
  24.8 19.1 %collective-permute-start.3 = (bf16[128,128]{1,0:T(8,128)(2,1)S(1)}, bf16[128,128]{1,0:T(8,128)(2,1)S(1)}, u32[]{:S(2)}, u32[]{:S(2)}) collective-permute-start(bf16[128,128]{1,0:T(8,128)(2,1)S(1)} %convert_element_type.11), channel_id=1, source_target_pairs={{0,24},{4,28},{8,0},{12,4},{16,8},{20,12},{24,16},{28,20},{1,25},{... | collective-permute-start | bytes 98312 | tf_op jit(solution)/shard_map/ppermute | solution.py:286
  31.7 1.0 %copy-start.5 = (f32[2112,128]{1,0:T(8,128)}, f32[2112,128]{1,0:T(8,128)S(1)}, u32[]{:S(2)}) copy-start(f32[2112,128]{1,0:T(8,128)S(1)} %get-tuple-element.52.refs_6_) | copy-start | bytes 3244036
  32.7 1.0 %copy-start.6 = (f32[2112,128]{1,0:T(8,128)}, f32[2112,128]{1,0:T(8,128)S(1)}, u32[]{:S(2)}) copy-start(f32[2112,128]{1,0:T(8,128)S(1)} %get-tuple-element.53.refs_8_) | copy-start | bytes 3244036
  43.9 3.4 %copy-start.9 = (bf16[128,128]{1,0:T(8,128)(2,1)}, bf16[128,128]{1,0:T(8,128)(2,1)S(1)}, u32[]{:S(2)}) copy-start(bf16[128,128]{1,0:T(8,128)(2,1)S(1)} %collective-permute-done.1.refs_3_) | copy-start | bytes 98308
  43.9 3.4 %copy-start.10 = (bf16[128,128]{1,0:T(8,128)(2,1)}, bf16[128,128]{1,0:T(8,128)(2,1)S(1)}, u32[]{:S(2)}) copy-start(bf16[128,128]{1,0:T(8,128)(2,1)S(1)} %collective-permute-done.2.refs_4_) | copy-start | bytes 98308
  43.9 3.4 %copy-start.11 = (bf16[128,128]{1,0:T(8,128)(2,1)}, bf16[128,128]{1,0:T(8,128)(2,1)S(1)}, u32[]{:S(2)}) copy-start(bf16[128,128]{1,0:T(8,128)(2,1)S(1)} %collective-permute-done.3.refs_5_) | copy-start | bytes 98308
  43.9 10.2 %all-to-all-start.1 = ((f32[8,8,256]{2,1,0:T(8,128)}), f32[8,8,256]{2,1,0:T(8,128)S(1)}, u32[]{:S(2)}, u32[]{:S(2)}) async-start(f32[8,8,256]{2,1,0:T(8,128)} %filter_lags.1), calls=%async_computation.1 | async-start | bytes 131072 | tf_op jit(solution)/shard_map/all_to_all | solution.py:518

commit v18 on v17

--- a/solution.py
+++ b/solution.py
@@ -61,8 +61,8 @@
             arrival(i, first).start()
 
     def owned_filter(row):
-        seq = row // (chans * owned)
-        chan = row // owned % chans
+        chan = row // (shards * owned)
+        seq = row // owned % shards
         return chan * per_chan + seq * owned + row % owned
 
     order = one_hot(FILTERS, FILTERS, owned_filter)
@@ -373,7 +373,7 @@
 
 
 def lag_kernel(shards, chans, groups, owned, scale, *refs):
-    in_refs, (out_ref, u_all, g_all, turned_all) = refs[1:-4], refs[-4:]
+    in_refs, (out_ref, held, sems, u_all, g_all, turned_all) = refs[1:-6], refs[-6:]
     tok_rows = out_ref.shape[2]
     halves = tok_rows // LANES
     blocks = shards * halves
@@ -385,20 +385,31 @@
         def by_filter(row):
             return row % depth * owned + row // depth
 
+        half = shards // 2
+        copies = []
+        for i in range(2):
+            place = (slice(None), pl.ds(i * half, half))
+            copies.append(
+                pltpu.make_async_copy(in_refs[0].at[place], held.at[place], sems.at[i])
+            )
+            copies[i].start()
         order = one_hot(take, take, by_filter)
-        for which, kept in enumerate((u_all, g_all)):
-            rows = slice(which * groups * owned, (which + 1) * groups * owned)
-            for s in range(shards):
-                piece = in_refs[0][s * chans : (s + 1) * chans, rows, :].reshape(take, tok_rows)
-                piece = jnp.dot(order, piece, preferred_element_type=F32).astype(BF16)
-                piece = piece.reshape(owned, depth, tok_rows)
-                for h in range(halves):
-                    first = (s * halves + h) * depth
-                    kept[:, first : first + depth, :] = piece[:, :, h * LANES : (h + 1) * LANES]
+        g_all[:, full:, :] = jnp.zeros((owned, g_all.shape[1] - full, LANES), BF16)
+        for i in range(2):
+            copies[i].wait()
+            for which, kept in enumerate((u_all, g_all)):
+                rows = slice(which * groups * owned, (which + 1) * groups * owned)
+                for s in range(i * half, (i + 1) * half):
+                    piece = held[:, s, rows, :].reshape(take, tok_rows)
+                    piece = jnp.dot(order, piece, preferred_element_type=F32).astype(BF16)
+                    piece = piece.reshape(owned, depth, tok_rows)
+                    for h in range(halves):
+                        first = (s * halves + h) * depth
+                        kept[:, first : first + depth, :] = piece[:, :, h * LANES : (h + 1) * LANES]
     else:
         u_all[...] = in_refs[0][...]
         g_all[:, :full, :] = in_refs[1][...]
-    g_all[:, full:, :] = jnp.zeros((owned, g_all.shape[1] - full, LANES), BF16)
+        g_all[:, full:, :] = jnp.zeros((owned, g_all.shape[1] - full, LANES), BF16)
     mirror = one_hot(LANES, LANES, lambda row: LANES - 1 - row)
     row = lax.broadcasted_iota(jnp.int32, (LANES, LANES), 0)
     col = lax.broadcasted_iota(jnp.int32, (LANES, LANES), 1)
@@ -456,18 +467,21 @@
     halves = tok_rows // LANES
     depth = chans * groups
     full = shards * halves * depth
-    args = (received,)
+    args = (received.reshape(chans, shards, *received.shape[1:]),)
     if owned % SUBLANES:
-        split = received.reshape(shards, chans, 2, groups, owned, halves, LANES)
-        split = split.transpose(2, 4, 0, 5, 1, 3, 6).reshape(2, owned, full, LANES)
+        split = received.reshape(chans, shards, 2, groups, owned, halves, LANES)
+        split = split.transpose(2, 4, 1, 5, 0, 3, 6).reshape(2, owned, full, LANES)
         args = (split[0], split[1])
-    whole = pl.BlockSpec(memory_space=pltpu.VMEM)
+    away, whole = pl.BlockSpec(memory_space=pl.ANY), pl.BlockSpec(memory_space=pltpu.VMEM)
+    fetched = len(args) == 1
     return pl.pallas_call(
         functools.partial(lag_kernel, shards, chans, groups, owned, scale),
-        in_specs=[pl.BlockSpec(memory_space=pl.ANY)] + [whole] * len(args),
+        in_specs=[away] + [away if fetched else whole] * len(args),
         out_specs=whole,
         out_shape=jax.ShapeDtypeStruct((shards, owned, tok_rows), F32),
         scratch_shapes=[
+            pltpu.VMEM(args[0].shape if fetched else (2 * SUBLANES, LANES), BF16),
+            pltpu.SemaphoreType.DMA((2,)),
             pltpu.VMEM((owned, full, LANES), BF16),
             pltpu.VMEM((owned, 2 * full + depth, LANES), BF16),
             pltpu.VMEM((owned, LANES, full), BF16),
@@ -491,7 +505,7 @@
     send, *signals, residues, decay_rate = lax.optimization_barrier(
         (send, *signals, residues, decay_rate)
     )
-    received = lax.all_to_all(send, ("seq", "chan"), split_axis=0, concat_axis=0, tiled=True)
+    received = lax.all_to_all(send, ("chan", "seq"), split_axis=0, concat_axis=0, tiled=True)
 
     coefs = jnp.stack(
         [

time: 55.1 us -> 56 us (1.016)
  starting transfers between devices: 17.4 us -> 18 us
    ppermute x1, waiting for transfers between devices: 4.43 us -> 5.88 us  [inside_pair(): return lax.ppermute(state, 'seq', [(i, i ^ 1) for i in range(2 * pairs)])]
    all_to_all x1, waiting for transfers between devices: 5.48 us -> 4.35 us  [per_device(): lax.all_to_all(send, ('chan', 'seq'), split_axis=0, concat_axis=0, tiled=...]
    ppermute x3, starting transfers between devices: 4.86 us -> 5.43 us  [along_column(): return lax.ppermute(state, 'seq', route)]
  transfers between devices with their start and end apart: 6 -> 6, of which waited for: 3 -> 3; matrix products, arithmetic and copies ran while one was open for 0% -> 0% of each run, Pallas kernels for 35% -> 34%
where the time goes in v18:
time: 56 us; the launch traced here: 55.7 us
  Pallas kernels  21.9 us (39%)
  starting transfers between devices  18 us (32%)
  waiting for transfers between devices  12.1 us (22%)
  local copies, waits for them, and re-layouts  2.76 us (5%)
  between operations  0.94 us (2%)
    all_to_all x1, starting transfers between devices, per_device(): lax.all_to_all(send, ('chan', 'seq'), split_axis=0, concat_axis=0, tiled=...  7.44 us
    pallas_call x1, Pallas kernels, local_parts(): pl.pallas_call(local_kernel, out_shape=[jax.ShapeDtypeStruct(token_shape(...  6.29 us
    ppermute x1, waiting for transfers between devices, inside_pair(): return lax.ppermute(state, 'seq', [(i, i ^ 1) for i in range(2 * pairs)])  5.88 us
    ppermute x3, starting transfers between devices, along_column(): return lax.ppermute(state, 'seq', route)  5.43 us
    pallas_call x1, Pallas kernels, final_outputs(): pl.pallas_call(functools.partial(final_kernel, len(args)), in_specs=[pl.B...  4.96 us
    pallas_call x1, Pallas kernels, filter_lags(): pl.pallas_call(functools.partial(lag_kernel, shards, chans, groups, owned...  4.76 us
    all_to_all x1, waiting for transfers between devices, per_device(): lax.all_to_all(send, ('chan', 'seq'), split_axis=0, concat_axis=0, tiled=...  4.35 us
    all_to_all x1, starting transfers between devices, per_device(): lags = lax.all_to_all(lags, 'seq', split_axis=0, concat_axis=0, tiled=True)  3.36 us
  transfers between devices with their start and end apart: 6, of which 3 were waited for; matrix products, arithmetic and copies ran while one was open for 0% of the time, Pallas kernels for 34%

profile of v18, /device:TPU:0, one launch (start us, length us, event | category | flops | bytes accessed | tf_op | source)
XLA Modules:
  0.0 55.7 jit_solution(8106137966470289955)
XLA Ops:
  0.6 0.0 copy-start.12
  0.6 0.0 copy-start.13
  0.7 2.9 %pack_signals.1 = bf16[32,64,256]{2,1,0:T(8,128)(2,1)} custom-call(bf16[256,1024]{1,0:T(8,128)(2,1)} %refs_10_, bf16[256,1024]{1,0:T(8,128)(2,1)} %refs_9_, bf16[256,1024]{1,0:T(8,128)(2,1)} %o_ref.1, bf16[256,1024]{1,0:T(8,128)(2,1)} %refs_7_), custom_call_target="tpu_custom_call" | custom-call | bytes 10800000 | tf_op jit(solution)/shard_map/pack_signals/pallas_call | solution.py:101
  3.6 0.0 copy-start
  3.6 0.0 copy-start.1
  3.6 0.0 copy-start.2
  3.6 0.0 copy-start.4
  3.6 7.4 %all-to-all-start = ((bf16[32,64,256]{2,1,0:T(8,128)(2,1)}), bf16[32,64,256]{2,1,0:T(8,128)(2,1)}, u32[]{:S(2)}, u32[]{:S(2)}) async-start(bf16[32,64,256]{2,1,0:T(8,128)(2,1)} %pack_signals.1), calls=%async_computation | async-start | bytes 2097152 | tf_op jit(solution)/shard_map/all_to_all | solution.py:508
  11.1 0.0 copy-done.12
  11.1 0.0 copy-done.13
  11.2 0.1 broadcast_in_dim.11
  11.2 0.0 copy-start.3
  11.2 0.0 copy-done
  11.3 0.0 copy-done.1
  11.3 0.0 copy-done.2
  11.3 0.0 copy-done.4
  11.3 0.0 copy-start.8
  11.3 2.9 %block_states.1 = (f32[2,128,128]{2,1,0:T(8,128)S(1)}, bf16[2,128,128]{2,1,0:T(8,128)(2,1)S(1)}) custom-call(bf16[256,1024]{1,0:T(8,128)(2,1)S(1)} %copy-done, bf16[256,1024]{1,0:T(8,128)(2,1)S(1)} %copy-done.1, bf16[256,1024]{1,0:T(8,128)(2,1)S(1)} %copy-done.2, bf16[256,1024]{1,0:T(8,128)(2,1)S(1)} %copy-done.4, f32[3,16,8,128]{3,2,1,0:T(8,128)S(1)} %bitcast.15), custom_call_target="tpu_custom_call" | custom-call | bytes 10800000 | tf_op jit(solution)/shard_map/block_states/pallas_call | solution.py:189
  14.2 1.8 %collective-permute-start = (bf16[2,128,128]{2,1,0:T(8,128)(2,1)S(1)}, bf16[2,128,128]{2,1,0:T(8,128)(2,1)S(1)}, u32[]{:S(2)}, u32[]{:S(2)}) collective-permute-start(bf16[2,128,128]{2,1,0:T(8,128)(2,1)S(1)} %get-tuple-element.38), channel_id=1, source_target_pairs={{0,4},{4,0},{8,12},{12,8},{16,20},{20,16},{24,28},{28,24},{1,5},{5... | collective-permute-start | bytes 196616 | tf_op jit(solution)/shard_map/ppermute | solution.py:290
  16.0 5.9 %collective-permute-done.near_ref.refs_2_ = bf16[2,128,128]{2,1,0:T(8,128)(2,1)S(1)} collective-permute-done((bf16[2,128,128]{2,1,0:T(8,128)(2,1)S(1)}, bf16[2,128,128]{2,1,0:T(8,128)(2,1)S(1)}, u32[]{:S(2)}, u32[]{:S(2)}) %collective-permute-start) | collective-permute-done | bytes 65568 | tf_op jit(solution)/shard_map/ppermute | solution.py:290
  21.9 0.0 copy-start.7
  22.0 3.0 %collective-permute-start.1 = (bf16[128,128]{1,0:T(8,128)(2,1)S(1)}, bf16[128,128]{1,0:T(8,128)(2,1)S(1)}, u32[]{:S(2)}, u32[]{:S(2)}) collective-permute-start(bf16[128,128]{1,0:T(8,128)(2,1)S(1)} %convert_element_type.9), channel_id=1, source_target_pairs={{0,8},{4,12},{8,16},{12,20},{16,24},{20,28},{24,0},{28,4},{1,9},{5... | collective-permute-start | bytes 98312 | tf_op jit(solution)/shard_map/ppermute | solution.py:286
  25.0 2.2 %collective-permute-start.2 = (bf16[128,128]{1,0:T(8,128)(2,1)S(1)}, bf16[128,128]{1,0:T(8,128)(2,1)S(1)}, u32[]{:S(2)}, u32[]{:S(2)}) collective-permute-start(bf16[128,128]{1,0:T(8,128)(2,1)S(1)} %convert_element_type.10), channel_id=1, source_target_pairs={{0,16},{4,20},{8,24},{12,28},{16,0},{20,4},{24,8},{28,12},{1,17},{... | collective-permute-start | bytes 98312 | tf_op jit(solution)/shard_map/ppermute | solution.py:286
  27.1 0.3 collective-permute-start.3
  27.4 0.0 copy-done.3
  27.4 0.0 copy-done.8
  27.4 6.3 %local_parts.1 = (f32[2112,128]{1,0:T(8,128)S(1)}, f32[2112,128]{1,0:T(8,128)S(1)}, f32[8,128]{1,0:T(8,128)S(1)}) custom-call(bf16[256,1024]{1,0:T(8,128)(2,1)S(1)} %copy-done, bf16[256,1024]{1,0:T(8,128)(2,1)S(1)} %copy-done.1, bf16[256,1024]{1,0:T(8,128)(2,1)S(1)} %copy-done.2, bf16[256,1024]{1,0:T(8,128)(2,1)S(1)} %copy-done.4, ...), custom_call_target="tpu_custom_call" | custom-call | bytes 23400000 | tf_op jit(solution)/shard_map/local_parts/pallas_call | solution.py:274
  33.7 0.0 copy-done.7
  33.7 0.0 copy-start.5
  33.7 1.0 %copy-done.5 = f32[2112,128]{1,0:T(8,128)} copy-done((f32[2112,128]{1,0:T(8,128)}, f32[2112,128]{1,0:T(8,128)S(1)}, u32[]{:S(2)}) %copy-start.5) | copy-done | bytes 1081368
  34.7 0.0 copy-start.6
  34.7 1.0 %copy-done.6 = f32[2112,128]{1,0:T(8,128)} copy-done((f32[2112,128]{1,0:T(8,128)}, f32[2112,128]{1,0:T(8,128)S(1)}, u32[]{:S(2)}) %copy-start.6) | copy-done | bytes 1081368
  35.7 4.3 %all-to-all-done = bf16[32,64,256]{2,1,0:T(8,128)(2,1)} async-done(((bf16[32,64,256]{2,1,0:T(8,128)(2,1)}), bf16[32,64,256]{2,1,0:T(8,128)(2,1)}, u32[]{:S(2)}, u32[]{:S(2)}) %all-to-all-start) | async-done | bytes 1048608 | tf_op jit(solution)/shard_map/all_to_all | solution.py:508
  40.1 4.8 %filter_lags.1 = f32[8,8,256]{2,1,0:T(8,128)} custom-call(f32[8,128]{1,0:T(8,128)S(1)} %get-tuple-element.44.refs_0_, bf16[4,8,64,256]{3,2,1,0:T(8,128)(2,1)} %bitcast.7.refs_1_), custom_call_target="tpu_custom_call" | custom-call | bytes 360000 | tf_op jit(solution)/shard_map/filter_lags/pallas_call | solution.py:477
  44.8 0.0 collective-permute-done.1.refs_3_
  44.8 0.0 copy-start.9
  44.8 0.0 collective-permute-done.2.refs_4_
  44.8 0.0 copy-start.10
  44.9 0.0 collective-permute-done.3.refs_5_
  44.9 0.0 copy-start.11
  44.9 3.4 %all-to-all-start.1 = ((f32[8,8,256]{2,1,0:T(8,128)}), f32[8,8,256]{2,1,0:T(8,128)S(1)}, u32[]{:S(2)}, u32[]{:S(2)}) async-start(f32[8,8,256]{2,1,0:T(8,128)} %filter_lags.1), calls=%async_computation.1 | async-start | bytes 131072 | tf_op jit(solution)/shard_map/all_to_all | solution.py:532
  48.2 0.0 copy-done.9
  48.3 0.0 copy-done.10
  48.3 0.0 copy-done.11
  48.3 5.0 %final_outputs.1 = (bf16[256,1024]{1,0:T(8,128)(2,1)}, bf16[256,1024]{1,0:T(8,128)(2,1)}, bf16[256,1024]{1,0:T(8,128)(2,1)}) custom-call(s32[1]{0:T(128)} %bitcast.seq_ref.refs_0_, f32[3,16,8,128]{3,2,1,0:T(8,128)} %bitcast.18, bf16[2,128,128]{2,1,0:T(8,128)(2,1)} %copy-done.7, bf16[128,128]{1,0:T(8,128)(2,1)} %copy-done.9, bf16[128,128]{1,0:T(8,128)(2,1)} %copy-done.10, ...), custom_call_target="tpu_custom_call" | custom-call | bytes 18000000 | tf_op jit(solution)/shard_map/final_outputs/pallas_call | solution.py:360
  53.2 1.8 %all-to-all-done.1 = f32[8,8,256]{2,1,0:T(8,128)S(1)} async-done(((f32[8,8,256]{2,1,0:T(8,128)}), f32[8,8,256]{2,1,0:T(8,128)S(1)}, u32[]{:S(2)}, u32[]{:S(2)}) %all-to-all-start.1) | async-done | bytes 65568 | tf_op jit(solution)/shard_map/all_to_all | solution.py:532
  55.1 0.6 %copy.12 = f32[256,64]{0,1:T(8,128)} copy(f32[256,64]{0,1:T(8,128)S(1)} %bitcast.20) | data formatting | bytes 131072
  (7 shorter events, 0.1 us)
Async XLA Ops:
  0.6 10.5 %copy-start.12 = (f32[256,16]{0,1:T(8,128)S(1)}, f32[256,16]{0,1:T(8,128)}, u32[]{:S(2)}) copy-start(f32[256,16]{0,1:T(8,128)} %param.12) | copy-start | bytes 49156
  0.6 10.5 %copy-start.13 = (f32[256,16]{0,1:T(8,128)S(1)}, f32[256,16]{0,1:T(8,128)}, u32[]{:S(2)}) copy-start(f32[256,16]{0,1:T(8,128)} %param.11) | copy-start | bytes 49156
  3.6 7.7 %copy-start = (bf16[256,1024]{1,0:T(8,128)(2,1)S(1)}, bf16[256,1024]{1,0:T(8,128)(2,1)}, u32[]{:S(2)}) copy-start(bf16[256,1024]{1,0:T(8,128)(2,1)} %refs_7_) | copy-start | bytes 1572868
  3.6 7.7 %copy-start.1 = (bf16[256,1024]{1,0:T(8,128)(2,1)S(1)}, bf16[256,1024]{1,0:T(8,128)(2,1)}, u32[]{:S(2)}) copy-start(bf16[256,1024]{1,0:T(8,128)(2,1)} %refs_10_) | copy-start | bytes 1572868
  3.6 7.7 %copy-start.2 = (bf16[256,1024]{1,0:T(8,128)(2,1)S(1)}, bf16[256,1024]{1,0:T(8,128)(2,1)}, u32[]{:S(2)}) copy-start(bf16[256,1024]{1,0:T(8,128)(2,1)} %refs_9_) | copy-start | bytes 1572868
  3.6 7.7 %copy-start.4 = (bf16[256,1024]{1,0:T(8,128)(2,1)S(1)}, bf16[256,1024]{1,0:T(8,128)(2,1)}, u32[]{:S(2)}) copy-start(bf16[256,1024]{1,0:T(8,128)(2,1)} %o_ref.1) | copy-start | bytes 1572868
  3.6 36.4 %all-to-all-start = ((bf16[32,64,256]{2,1,0:T(8,128)(2,1)}), bf16[32,64,256]{2,1,0:T(8,128)(2,1)}, u32[]{:S(2)}, u32[]{:S(2)}) async-start(bf16[32,64,256]{2,1,0:T(8,128)(2,1)} %pack_signals.1), calls=%async_computation | async-start | bytes 2097152 | tf_op jit(solution)/shard_map/all_to_all | solution.py:508
  11.2 16.2 %copy-start.3 = (f32[3,16,4,2,128]{4,3,2,1,0:T(2,128)}, f32[3,16,4,2,128]{4,3,2,1,0:T(2,128)S(1)}, u32[]{:S(2)}) copy-start(f32[3,16,4,2,128]{4,3,2,1,0:T(2,128)S(1)} %broadcast_in_dim.11) | copy-start | bytes 589828
  11.3 16.1 %copy-start.8 = (f32[1024]{0:T(1024)S(1)}, f32[1024]{0:T(1024)}, u32[]{:S(2)}) copy-start(f32[1024]{0:T(1024)} %param.13) | copy-start | bytes 12292
  14.2 7.6 %collective-permute-start = (bf16[2,128,128]{2,1,0:T(8,128)(2,1)S(1)}, bf16[2,128,128]{2,1,0:T(8,128)(2,1)S(1)}, u32[]{:S(2)}, u32[]{:S(2)}) collective-permute-start(bf16[2,128,128]{2,1,0:T(8,128)(2,1)S(1)} %get-tuple-element.38), channel_id=1, source_target_pairs={{0,4},{4,0},{8,12},{12,8},{16,20},{20,16},{24,28},{28,24},{1,5},{5... | collective-permute-start | bytes 196616 | tf_op jit(solution)/shard_map/ppermute | solution.py:290
  21.9 11.8 %copy-start.7 = (bf16[2,128,128]{2,1,0:T(8,128)(2,1)}, bf16[2,128,128]{2,1,0:T(8,128)(2,1)S(1)}, u32[]{:S(2)}) copy-start(bf16[2,128,128]{2,1,0:T(8,128)(2,1)S(1)} %collective-permute-done.near_ref.refs_2_) | copy-start | bytes 196612
  22.0 22.9 %collective-permute-start.1 = (bf16[128,128]{1,0:T(8,128)(2,1)S(1)}, bf16[128,128]{1,0:T(8,128)(2,1)S(1)}, u32[]{:S(2)}, u32[]{:S(2)}) collective-permute-start(bf16[128,128]{1,0:T(8,128)(2,1)S(1)} %convert_element_type.9), channel_id=1, source_target_pairs={{0,8},{4,12},{8,16},{12,20},{16,24},{20,28},{24,0},{28,4},{1,9},{5... | collective-permute-start | bytes 98312 | tf_op jit(solution)/shard_map/ppermute | solution.py:286
  25.0 19.9 %collective-permute-start.2 = (bf16[128,128]{1,0:T(8,128)(2,1)S(1)}, bf16[128,128]{1,0:T(8,128)(2,1)S(1)}, u32[]{:S(2)}, u32[]{:S(2)}) collective-permute-start(bf16[128,128]{1,0:T(8,128)(2,1)S(1)} %convert_element_type.10), channel_id=1, source_target_pairs={{0,16},{4,20},{8,24},{12,28},{16,0},{20,4},{24,8},{28,12},{1,17},{... | collective-permute-start | bytes 98312 | tf_op jit(solution)/shard_map/ppermute | solution.py:286
  27.1 17.7 %collective-permute-start.3 = (bf16[128,128]{1,0:T(8,128)(2,1)S(1)}, bf16[128,128]{1,0:T(8,128)(2,1)S(1)}, u32[]{:S(2)}, u32[]{:S(2)}) collective-permute-start(bf16[128,128]{1,0:T(8,128)(2,1)S(1)} %convert_element_type.11), channel_id=1, source_target_pairs={{0,24},{4,28},{8,0},{12,4},{16,8},{20,12},{24,16},{28,20},{1,25},{... | collective-permute-start | bytes 98312 | tf_op jit(solution)/shard_map/ppermute | solution.py:286
  33.7 1.0 %copy-start.5 = (f32[2112,128]{1,0:T(8,128)}, f32[2112,128]{1,0:T(8,128)S(1)}, u32[]{:S(2)}) copy-start(f32[2112,128]{1,0:T(8,128)S(1)} %get-tuple-element.52.refs_6_) | copy-start | bytes 3244036
  34.7 1.0 %copy-start.6 = (f32[2112,128]{1,0:T(8,128)}, f32[2112,128]{1,0:T(8,128)S(1)}, u32[]{:S(2)}) copy-start(f32[2112,128]{1,0:T(8,128)S(1)} %get-tuple-element.53.refs_8_) | copy-start | bytes 3244036
  44.8 3.4 %copy-start.9 = (bf16[128,128]{1,0:T(8,128)(2,1)}, bf16[128,128]{1,0:T(8,128)(2,1)S(1)}, u32[]{:S(2)}) copy-start(bf16[128,128]{1,0:T(8,128)(2,1)S(1)} %collective-permute-done.1.refs_3_) | copy-start | bytes 98308
  44.8 3.4 %copy-start.10 = (bf16[128,128]{1,0:T(8,128)(2,1)}, bf16[128,128]{1,0:T(8,128)(2,1)S(1)}, u32[]{:S(2)}) copy-start(bf16[128,128]{1,0:T(8,128)(2,1)S(1)} %collective-permute-done.2.refs_4_) | copy-start | bytes 98308
  44.9 3.4 %copy-start.11 = (bf16[128,128]{1,0:T(8,128)(2,1)}, bf16[128,128]{1,0:T(8,128)(2,1)S(1)}, u32[]{:S(2)}) copy-start(bf16[128,128]{1,0:T(8,128)(2,1)S(1)} %collective-permute-done.3.refs_5_) | copy-start | bytes 98308
  44.9 10.2 %all-to-all-start.1 = ((f32[8,8,256]{2,1,0:T(8,128)}), f32[8,8,256]{2,1,0:T(8,128)S(1)}, u32[]{:S(2)}, u32[]{:S(2)}) async-start(f32[8,8,256]{2,1,0:T(8,128)} %filter_lags.1), calls=%async_computation.1 | async-start | bytes 131072 | tf_op jit(solution)/shard_map/all_to_all | solution.py:532

commit v19 on v17

--- a/solution.py
+++ b/solution.py
@@ -473,7 +473,7 @@
             pltpu.VMEM((owned, LANES, full), BF16),
         ],
         compiler_params=pltpu.CompilerParams(vmem_limit_bytes=VMEM_BYTES),
-        cost_estimate=takes(0.1),
+        cost_estimate=takes(2.5),
         name="filter_lags",
     )(done, *args)
 

time: 55.1 us -> 55.1 us (level)
  no operation moved by 1% of the time
where the time goes in v19:
time: 55.1 us; the launch traced here: 54.8 us
  Pallas kernels  21.9 us (40%)
  starting transfers between devices  17.4 us (32%)
  waiting for transfers between devices  11.8 us (21%)
  local copies, waits for them, and re-layouts  2.76 us (5%)
  between operations  0.91 us (2%)
    all_to_all x1, starting transfers between devices, per_device(): lax.all_to_all(send, ('seq', 'chan'), split_axis=0, concat_axis=0, tiled=...  7.44 us
    pallas_call x1, Pallas kernels, local_parts(): pl.pallas_call(local_kernel, out_shape=[jax.ShapeDtypeStruct(token_shape(...  6.29 us
    all_to_all x1, waiting for transfers between devices, per_device(): lax.all_to_all(send, ('seq', 'chan'), split_axis=0, concat_axis=0, tiled=...  5.48 us
    pallas_call x1, Pallas kernels, final_outputs(): pl.pallas_call(functools.partial(final_kernel, len(args)), in_specs=[pl.B...  4.96 us
    ppermute x3, starting transfers between devices, along_column(): return lax.ppermute(state, 'seq', route)  4.86 us
    pallas_call x1, Pallas kernels, filter_lags(): pl.pallas_call(functools.partial(lag_kernel, shards, chans, groups, owned...  4.7 us
    ppermute x1, waiting for transfers between devices, inside_pair(): return lax.ppermute(state, 'seq', [(i, i ^ 1) for i in range(2 * pairs)])  4.43 us
    all_to_all x1, starting transfers between devices, per_device(): lags = lax.all_to_all(lags, 'seq', split_axis=0, concat_axis=0, tiled=True)  3.36 us
  transfers between devices with their start and end apart: 6, of which 3 were waited for; matrix products, arithmetic and copies ran while one was open for 0% of the time, Pallas kernels for 35%

profile of v19, /device:TPU:0, one launch (start us, length us, event | category | flops | bytes accessed | tf_op | source)
XLA Modules:
  0.0 54.8 jit_solution(13192581576094409254)
XLA Ops:
  0.6 0.0 copy-start.12
  0.6 0.0 copy-start.13
  0.7 2.9 %pack_signals.1 = bf16[32,64,256]{2,1,0:T(8,128)(2,1)} custom-call(bf16[256,1024]{1,0:T(8,128)(2,1)} %refs_10_, bf16[256,1024]{1,0:T(8,128)(2,1)} %refs_9_, bf16[256,1024]{1,0:T(8,128)(2,1)} %o_ref.1, bf16[256,1024]{1,0:T(8,128)(2,1)} %refs_7_), custom_call_target="tpu_custom_call" | custom-call | bytes 10800000 | tf_op jit(solution)/shard_map/pack_signals/pallas_call | solution.py:101
  3.6 0.0 copy-start
  3.6 0.0 copy-start.1
  3.6 0.0 copy-start.2
  3.6 0.0 copy-start.4
  3.6 7.4 %all-to-all-start = ((bf16[32,64,256]{2,1,0:T(8,128)(2,1)}), bf16[32,64,256]{2,1,0:T(8,128)(2,1)}, u32[]{:S(2)}, u32[]{:S(2)}) async-start(bf16[32,64,256]{2,1,0:T(8,128)(2,1)} %pack_signals.1), calls=%async_computation | async-start | bytes 2097152 | tf_op jit(solution)/shard_map/all_to_all | solution.py:494
  11.1 0.0 copy-done.12
  11.1 0.0 copy-done.13
  11.2 0.1 broadcast_in_dim.11
  11.2 0.0 copy-start.3
  11.2 0.0 copy-done
  11.3 0.0 copy-done.1
  11.3 0.0 copy-done.2
  11.3 0.0 copy-done.4
  11.3 0.0 copy-start.8
  11.3 2.9 %block_states.1 = (f32[2,128,128]{2,1,0:T(8,128)S(1)}, bf16[2,128,128]{2,1,0:T(8,128)(2,1)S(1)}) custom-call(bf16[256,1024]{1,0:T(8,128)(2,1)S(1)} %copy-done, bf16[256,1024]{1,0:T(8,128)(2,1)S(1)} %copy-done.1, bf16[256,1024]{1,0:T(8,128)(2,1)S(1)} %copy-done.2, bf16[256,1024]{1,0:T(8,128)(2,1)S(1)} %copy-done.4, f32[3,16,8,128]{3,2,1,0:T(8,128)S(1)} %bitcast.14), custom_call_target="tpu_custom_call" | custom-call | bytes 10800000 | tf_op jit(solution)/shard_map/block_states/pallas_call | solution.py:189
  14.2 1.8 %collective-permute-start = (bf16[2,128,128]{2,1,0:T(8,128)(2,1)S(1)}, bf16[2,128,128]{2,1,0:T(8,128)(2,1)S(1)}, u32[]{:S(2)}, u32[]{:S(2)}) collective-permute-start(bf16[2,128,128]{2,1,0:T(8,128)(2,1)S(1)} %get-tuple-element.38), channel_id=1, source_target_pairs={{0,4},{4,0},{8,12},{12,8},{16,20},{20,16},{24,28},{28,24},{1,5},{5... | collective-permute-start | bytes 196616 | tf_op jit(solution)/shard_map/ppermute | solution.py:290
  16.0 4.4 %collective-permute-done.near_ref.refs_2_ = bf16[2,128,128]{2,1,0:T(8,128)(2,1)S(1)} collective-permute-done((bf16[2,128,128]{2,1,0:T(8,128)(2,1)S(1)}, bf16[2,128,128]{2,1,0:T(8,128)(2,1)S(1)}, u32[]{:S(2)}, u32[]{:S(2)}) %collective-permute-start) | collective-permute-done | bytes 65568 | tf_op jit(solution)/shard_map/ppermute | solution.py:290
  20.4 0.0 copy-start.7
  20.5 2.4 %collective-permute-start.1 = (bf16[128,128]{1,0:T(8,128)(2,1)S(1)}, bf16[128,128]{1,0:T(8,128)(2,1)S(1)}, u32[]{:S(2)}, u32[]{:S(2)}) collective-permute-start(bf16[128,128]{1,0:T(8,128)(2,1)S(1)} %convert_element_type.9), channel_id=1, source_target_pairs={{0,8},{4,12},{8,16},{12,20},{16,24},{20,28},{24,0},{28,4},{1,9},{5... | collective-permute-start | bytes 98312 | tf_op jit(solution)/shard_map/ppermute | solution.py:286
  22.9 1.9 %collective-permute-start.2 = (bf16[128,128]{1,0:T(8,128)(2,1)S(1)}, bf16[128,128]{1,0:T(8,128)(2,1)S(1)}, u32[]{:S(2)}, u32[]{:S(2)}) collective-permute-start(bf16[128,128]{1,0:T(8,128)(2,1)S(1)} %convert_element_type.10), channel_id=1, source_target_pairs={{0,16},{4,20},{8,24},{12,28},{16,0},{20,4},{24,8},{28,12},{1,17},{... | collective-permute-start | bytes 98312 | tf_op jit(solution)/shard_map/ppermute | solution.py:286
  24.8 0.6 %collective-permute-start.3 = (bf16[128,128]{1,0:T(8,128)(2,1)S(1)}, bf16[128,128]{1,0:T(8,128)(2,1)S(1)}, u32[]{:S(2)}, u32[]{:S(2)}) collective-permute-start(bf16[128,128]{1,0:T(8,128)(2,1)S(1)} %convert_element_type.11), channel_id=1, source_target_pairs={{0,24},{4,28},{8,0},{12,4},{16,8},{20,12},{24,16},{28,20},{1,25},{... | collective-permute-start | bytes 98312 | tf_op jit(solution)/shard_map/ppermute | solution.py:286
  25.4 0.0 copy-done.3
  25.4 0.0 copy-done.8
  25.4 6.3 %local_parts.1 = (f32[2112,128]{1,0:T(8,128)S(1)}, f32[2112,128]{1,0:T(8,128)S(1)}, f32[8,128]{1,0:T(8,128)S(1)}) custom-call(bf16[256,1024]{1,0:T(8,128)(2,1)S(1)} %copy-done, bf16[256,1024]{1,0:T(8,128)(2,1)S(1)} %copy-done.1, bf16[256,1024]{1,0:T(8,128)(2,1)S(1)} %copy-done.2, bf16[256,1024]{1,0:T(8,128)(2,1)S(1)} %copy-done.4, ...), custom_call_target="tpu_custom_call" | custom-call | bytes 23400000 | tf_op jit(solution)/shard_map/local_parts/pallas_call | solution.py:274
  31.7 0.0 copy-done.7
  31.7 0.0 copy-start.5
  31.7 1.0 %copy-done.5 = f32[2112,128]{1,0:T(8,128)} copy-done((f32[2112,128]{1,0:T(8,128)}, f32[2112,128]{1,0:T(8,128)S(1)}, u32[]{:S(2)}) %copy-start.5) | copy-done | bytes 1081368
  32.7 0.0 copy-start.6
  32.7 1.0 %copy-done.6 = f32[2112,128]{1,0:T(8,128)} copy-done((f32[2112,128]{1,0:T(8,128)}, f32[2112,128]{1,0:T(8,128)S(1)}, u32[]{:S(2)}) %copy-start.6) | copy-done | bytes 1081368
  33.7 5.5 %all-to-all-done.refs_1_ = bf16[32,64,256]{2,1,0:T(8,128)(2,1)} async-done(((bf16[32,64,256]{2,1,0:T(8,128)(2,1)}), bf16[32,64,256]{2,1,0:T(8,128)(2,1)}, u32[]{:S(2)}, u32[]{:S(2)}) %all-to-all-start) | async-done | bytes 1048608 | tf_op jit(solution)/shard_map/all_to_all | solution.py:494
  39.2 4.7 %filter_lags.1 = f32[8,8,256]{2,1,0:T(8,128)} custom-call(f32[8,128]{1,0:T(8,128)S(1)} %get-tuple-element.44.refs_0_, bf16[32,64,256]{2,1,0:T(8,128)(2,1)} %all-to-all-done.refs_1_), custom_call_target="tpu_custom_call" | custom-call | bytes 9000000 | tf_op jit(solution)/shard_map/filter_lags/pallas_call | solution.py:465
  43.9 0.0 collective-permute-done.1.refs_3_
  43.9 0.0 copy-start.9
  43.9 0.0 collective-permute-done.2.refs_4_
  43.9 0.0 copy-start.10
  43.9 0.0 collective-permute-done.3.refs_5_
  43.9 0.0 copy-start.11
  43.9 3.4 %all-to-all-start.1 = ((f32[8,8,256]{2,1,0:T(8,128)}), f32[8,8,256]{2,1,0:T(8,128)S(1)}, u32[]{:S(2)}, u32[]{:S(2)}) async-start(f32[8,8,256]{2,1,0:T(8,128)} %filter_lags.1), calls=%async_computation.1 | async-start | bytes 131072 | tf_op jit(solution)/shard_map/all_to_all | solution.py:518
  47.3 0.0 copy-done.9
  47.3 0.0 copy-done.10
  47.3 0.0 copy-done.11
  47.3 5.0 %final_outputs.1 = (bf16[256,1024]{1,0:T(8,128)(2,1)}, bf16[256,1024]{1,0:T(8,128)(2,1)}, bf16[256,1024]{1,0:T(8,128)(2,1)}) custom-call(s32[1]{0:T(128)} %bitcast.seq_ref.refs_0_, f32[3,16,8,128]{3,2,1,0:T(8,128)} %bitcast.17, bf16[2,128,128]{2,1,0:T(8,128)(2,1)} %copy-done.7, bf16[128,128]{1,0:T(8,128)(2,1)} %copy-done.9, bf16[128,128]{1,0:T(8,128)(2,1)} %copy-done.10, ...), custom_call_target="tpu_custom_call" | custom-call | bytes 18000000 | tf_op jit(solution)/shard_map/final_outputs/pallas_call | solution.py:360
  52.3 1.8 %all-to-all-done.1 = f32[8,8,256]{2,1,0:T(8,128)S(1)} async-done(((f32[8,8,256]{2,1,0:T(8,128)}), f32[8,8,256]{2,1,0:T(8,128)S(1)}, u32[]{:S(2)}, u32[]{:S(2)}) %all-to-all-start.1) | async-done | bytes 65568 | tf_op jit(solution)/shard_map/all_to_all | solution.py:518
  54.1 0.6 %copy.12 = f32[256,64]{0,1:T(8,128)} copy(f32[256,64]{0,1:T(8,128)S(1)} %bitcast.19) | data formatting | bytes 131072
  (7 shorter events, 0.1 us)
Async XLA Ops:
  0.6 10.5 %copy-start.12 = (f32[256,16]{0,1:T(8,128)S(1)}, f32[256,16]{0,1:T(8,128)}, u32[]{:S(2)}) copy-start(f32[256,16]{0,1:T(8,128)} %param.12) | copy-start | bytes 49156
  0.6 10.5 %copy-start.13 = (f32[256,16]{0,1:T(8,128)S(1)}, f32[256,16]{0,1:T(8,128)}, u32[]{:S(2)}) copy-start(f32[256,16]{0,1:T(8,128)} %param.11) | copy-start | bytes 49156
  3.6 7.7 %copy-start = (bf16[256,1024]{1,0:T(8,128)(2,1)S(1)}, bf16[256,1024]{1,0:T(8,128)(2,1)}, u32[]{:S(2)}) copy-start(bf16[256,1024]{1,0:T(8,128)(2,1)} %refs_7_) | copy-start | bytes 1572868
  3.6 7.7 %copy-start.1 = (bf16[256,1024]{1,0:T(8,128)(2,1)S(1)}, bf16[256,1024]{1,0:T(8,128)(2,1)}, u32[]{:S(2)}) copy-start(bf16[256,1024]{1,0:T(8,128)(2,1)} %refs_10_) | copy-start | bytes 1572868
  3.6 7.7 %copy-start.2 = (bf16[256,1024]{1,0:T(8,128)(2,1)S(1)}, bf16[256,1024]{1,0:T(8,128)(2,1)}, u32[]{:S(2)}) copy-start(bf16[256,1024]{1,0:T(8,128)(2,1)} %refs_9_) | copy-start | bytes 1572868
  3.6 7.7 %copy-start.4 = (bf16[256,1024]{1,0:T(8,128)(2,1)S(1)}, bf16[256,1024]{1,0:T(8,128)(2,1)}, u32[]{:S(2)}) copy-start(bf16[256,1024]{1,0:T(8,128)(2,1)} %o_ref.1) | copy-start | bytes 1572868
  3.6 35.5 %all-to-all-start = ((bf16[32,64,256]{2,1,0:T(8,128)(2,1)}), bf16[32,64,256]{2,1,0:T(8,128)(2,1)}, u32[]{:S(2)}, u32[]{:S(2)}) async-start(bf16[32,64,256]{2,1,0:T(8,128)(2,1)} %pack_signals.1), calls=%async_computation | async-start | bytes 2097152 | tf_op jit(solution)/shard_map/all_to_all | solution.py:494
  11.2 14.1 %copy-start.3 = (f32[3,16,4,2,128]{4,3,2,1,0:T(2,128)}, f32[3,16,4,2,128]{4,3,2,1,0:T(2,128)S(1)}, u32[]{:S(2)}) copy-start(f32[3,16,4,2,128]{4,3,2,1,0:T(2,128)S(1)} %broadcast_in_dim.11) | copy-start | bytes 589828
  11.3 14.1 %copy-start.8 = (f32[1024]{0:T(1024)S(1)}, f32[1024]{0:T(1024)}, u32[]{:S(2)}) copy-start(f32[1024]{0:T(1024)} %param.13) | copy-start | bytes 12292
  14.2 6.2 %collective-permute-start = (bf16[2,128,128]{2,1,0:T(8,128)(2,1)S(1)}, bf16[2,128,128]{2,1,0:T(8,128)(2,1)S(1)}, u32[]{:S(2)}, u32[]{:S(2)}) collective-permute-start(bf16[2,128,128]{2,1,0:T(8,128)(2,1)S(1)} %get-tuple-element.38), channel_id=1, source_target_pairs={{0,4},{4,0},{8,12},{12,8},{16,20},{20,16},{24,28},{28,24},{1,5},{5... | collective-permute-start | bytes 196616 | tf_op jit(solution)/shard_map/ppermute | solution.py:290
  20.4 11.3 %copy-start.7 = (bf16[2,128,128]{2,1,0:T(8,128)(2,1)}, bf16[2,128,128]{2,1,0:T(8,128)(2,1)S(1)}, u32[]{:S(2)}) copy-start(bf16[2,128,128]{2,1,0:T(8,128)(2,1)S(1)} %collective-permute-done.near_ref.refs_2_) | copy-start | bytes 196612
  20.5 23.4 %collective-permute-start.1 = (bf16[128,128]{1,0:T(8,128)(2,1)S(1)}, bf16[128,128]{1,0:T(8,128)(2,1)S(1)}, u32[]{:S(2)}, u32[]{:S(2)}) collective-permute-start(bf16[128,128]{1,0:T(8,128)(2,1)S(1)} %convert_element_type.9), channel_id=1, source_target_pairs={{0,8},{4,12},{8,16},{12,20},{16,24},{20,28},{24,0},{28,4},{1,9},{5... | collective-permute-start | bytes 98312 | tf_op jit(solution)/shard_map/ppermute | solution.py:286
  22.9 20.9 %collective-permute-start.2 = (bf16[128,128]{1,0:T(8,128)(2,1)S(1)}, bf16[128,128]{1,0:T(8,128)(2,1)S(1)}, u32[]{:S(2)}, u32[]{:S(2)}) collective-permute-start(bf16[128,128]{1,0:T(8,128)(2,1)S(1)} %convert_element_type.10), channel_id=1, source_target_pairs={{0,16},{4,20},{8,24},{12,28},{16,0},{20,4},{24,8},{28,12},{1,17},{... | collective-permute-start | bytes 98312 | tf_op jit(solution)/shard_map/ppermute | solution.py:286
  24.8 19.1 %collective-permute-start.3 = (bf16[128,128]{1,0:T(8,128)(2,1)S(1)}, bf16[128,128]{1,0:T(8,128)(2,1)S(1)}, u32[]{:S(2)}, u32[]{:S(2)}) collective-permute-start(bf16[128,128]{1,0:T(8,128)(2,1)S(1)} %convert_element_type.11), channel_id=1, source_target_pairs={{0,24},{4,28},{8,0},{12,4},{16,8},{20,12},{24,16},{28,20},{1,25},{... | collective-permute-start | bytes 98312 | tf_op jit(solution)/shard_map/ppermute | solution.py:286
  31.7 1.0 %copy-start.5 = (f32[2112,128]{1,0:T(8,128)}, f32[2112,128]{1,0:T(8,128)S(1)}, u32[]{:S(2)}) copy-start(f32[2112,128]{1,0:T(8,128)S(1)} %get-tuple-element.52.refs_6_) | copy-start | bytes 3244036
  32.7 1.0 %copy-start.6 = (f32[2112,128]{1,0:T(8,128)}, f32[2112,128]{1,0:T(8,128)S(1)}, u32[]{:S(2)}) copy-start(f32[2112,128]{1,0:T(8,128)S(1)} %get-tuple-element.53.refs_8_) | copy-start | bytes 3244036
  43.9 3.4 %copy-start.9 = (bf16[128,128]{1,0:T(8,128)(2,1)}, bf16[128,128]{1,0:T(8,128)(2,1)S(1)}, u32[]{:S(2)}) copy-start(bf16[128,128]{1,0:T(8,128)(2,1)S(1)} %collective-permute-done.1.refs_3_) | copy-start | bytes 98308
  43.9 3.4 %copy-start.10 = (bf16[128,128]{1,0:T(8,128)(2,1)}, bf16[128,128]{1,0:T(8,128)(2,1)S(1)}, u32[]{:S(2)}) copy-start(bf16[128,128]{1,0:T(8,128)(2,1)S(1)} %collective-permute-done.2.refs_4_) | copy-start | bytes 98308
  43.9 3.4 %copy-start.11 = (bf16[128,128]{1,0:T(8,128)(2,1)}, bf16[128,128]{1,0:T(8,128)(2,1)S(1)}, u32[]{:S(2)}) copy-start(bf16[128,128]{1,0:T(8,128)(2,1)S(1)} %collective-permute-done.3.refs_5_) | copy-start | bytes 98308
  43.9 10.2 %all-to-all-start.1 = ((f32[8,8,256]{2,1,0:T(8,128)}), f32[8,8,256]{2,1,0:T(8,128)S(1)}, u32[]{:S(2)}, u32[]{:S(2)}) async-start(f32[8,8,256]{2,1,0:T(8,128)} %filter_lags.1), calls=%async_computation.1 | async-start | bytes 131072 | tf_op jit(solution)/shard_map/all_to_all | solution.py:518

commit v20 on v19

--- a/solution.py
+++ b/solution.py
@@ -18,10 +18,6 @@
 F32 = jnp.float32
 BF16 = jnp.bfloat16
 LINK = jnp.bfloat16
-
-
-def takes(micros):
-    return pl.CostEstimate(flops=0, bytes_accessed=int(micros * 3.6e6), transcendentals=0)
 
 
 def product(first, second):
@@ -110,7 +106,6 @@
             pltpu.SemaphoreType.DMA((2, groups // 2)),
         ],
         compiler_params=pltpu.CompilerParams(vmem_limit_bytes=FULL_VMEM_BYTES),
-        cost_estimate=takes(3.0),
         name="pack_signals",
     )(key_proj, value_proj, out_grad, query_proj)
     if owned % SUBLANES:
@@ -194,7 +189,6 @@
         ],
         scratch_shapes=[pltpu.VMEM(token_shape(tok_rows, tiles), F32)] * 2,
         compiler_params=pltpu.CompilerParams(vmem_limit_bytes=VMEM_BYTES),
-        cost_estimate=takes(3.0),
         name="block_states",
     )(query_proj, key_proj, value_proj, out_grad, coefs)
 
@@ -223,7 +217,6 @@
         out_specs=[whole] * (pairs - 1),
         out_shape=[jax.ShapeDtypeStruct(own.shape[1:], F32)] * (pairs - 1),
         compiler_params=pltpu.CompilerParams(vmem_limit_bytes=VMEM_BYTES),
-        cost_estimate=takes(0.1),
         name="pair_states",
     )(seq_index, coefs, own, near)
     return [state.astype(LINK) for state in states]
@@ -249,22 +242,22 @@
 
 
 def local_kernel(
-    q_ref, k_ref, v_ref, o_ref, coef_ref, gain_ref, conv_ref, grad_ref, done_ref
+    q_ref, k_ref, v_ref, o_ref, coef_ref, gain_ref, conv_ref, grad_ref, done_ref, x_ref, g_ref
 ):
     tok_rows, width = k_ref.shape
     tiles = width // LANES
-    spread_tokens(k_ref, v_ref, conv_ref)
-    spread_tokens(o_ref, q_ref, grad_ref)
-    walk_tokens(conv_ref, coef_ref, tok_rows, tiles, 0, 1)
-    walk_tokens(grad_ref, coef_ref, tok_rows, tiles, tok_rows - 1, -1)
+    spread_tokens(k_ref, v_ref, x_ref)
+    spread_tokens(o_ref, q_ref, g_ref)
+    walk_tokens(x_ref, coef_ref, tok_rows, tiles, 0, 1)
+    walk_tokens(g_ref, coef_ref, tok_rows, tiles, tok_rows - 1, -1)
     for tile in range(tiles):
         cols = slice(tile * LANES, (tile + 1) * LANES)
         rows = tile_rows(tok_rows, tile)
         gain = gain_ref[:, cols]
         conv_in = product(k_ref[:, cols], v_ref[:, cols]).astype(F32)
-        conv_ref[rows, :] = conv_ref[rows, :] + gain * conv_in
+        conv_ref[:, cols] = x_ref[rows, :] + gain * conv_in
         mid_grad = product(o_ref[:, cols], q_ref[:, cols]).astype(F32)
-        grad_ref[rows, :] = grad_ref[rows, :] + gain * mid_grad
+        grad_ref[:, cols] = g_ref[rows, :] + gain * mid_grad
     done_ref[...] = jnp.zeros(done_ref.shape, F32)
 
 
@@ -273,10 +266,10 @@
     tiles = coefs.shape[2]
     return pl.pallas_call(
         local_kernel,
-        out_shape=[jax.ShapeDtypeStruct(token_shape(tok_rows, tiles), F32)] * 2
+        out_shape=[jax.ShapeDtypeStruct((tok_rows, width), F32)] * 2
         + [jax.ShapeDtypeStruct((SUBLANES, LANES), F32)],
-        compiler_params=pltpu.CompilerParams(vmem_limit_bytes=VMEM_BYTES),
-        cost_estimate=takes(6.5),
+        scratch_shapes=[pltpu.VMEM(token_shape(tok_rows, tiles), F32)] * 2,
+        compiler_params=pltpu.CompilerParams(vmem_limit_bytes=VMEM_BYTES),
         name="local_parts",
     )(query_proj, key_proj, value_proj, out_grad, coefs, gain)
 
@@ -303,73 +296,96 @@
     lax.fori_loop(0, tok_rows, step, held, unroll=8)
 
 
-def final_kernel(count, *refs):
-    seq_ref, hbm_refs, refs = refs[0], refs[1 : 1 + count], refs[1 + count :]
-    out_hbm, held_refs, refs = refs[:3], refs[3 : 3 + count], refs[3 + count :]
-    edge_ref, out_refs, in_sems, out_sems = refs[0], refs[1:4], refs[4], refs[5]
-    coef_ref, near_ref, *state_refs = held_refs[:-5]
-    conv_ref, q_ref, grad_ref, v_ref, k_ref = held_refs[-5:]
-    tok_rows, width = k_ref.shape
-    tiles = width // LANES
-    small = count - 5
-    arrivals = [
-        pltpu.make_async_copy(source, target, in_sems.at[i])
-        for i, (source, target) in enumerate(zip(hbm_refs, held_refs))
-    ]
-    departures = []
-
-    def multiply_out(part_ref, outs):
-        for tile in range(tiles):
-            cols = slice(tile * LANES, (tile + 1) * LANES)
-            rows = tile_rows(tok_rows, tile)
-            value = part_ref[rows, :] + edge_ref[rows, :]
-            for i, factor_ref in outs:
-                out_refs[i][:, cols] = (value * factor_ref[:, cols].astype(F32)).astype(BF16)
-                place = (slice(None), pl.ds(tile * LANES, LANES))
-                copy = pltpu.make_async_copy(
-                    out_refs[i].at[place], out_hbm[i].at[place], out_sems.at[i, tile]
-                )
-                copy.start()
-                departures.append(copy)
-
-    for copy in arrivals:
-        copy.start()
-    for copy in arrivals[:small]:
+def edge_kernel(seq_ref, coef_ref, near_ref, *refs):
+    state_refs, edge_ref = refs[:-1], refs[-1]
+    fill_side(0, edge_ref, seq_ref, coef_ref, near_ref, state_refs)
+
+
+def fill_side(side, edge_ref, seq_ref, coef_ref, near_ref, state_refs):
+    tiles = coef_ref.shape[2]
+    tok_rows = edge_ref.shape[0] // tiles - GAP
+    held = sum_pairs(side, seq_ref[0], coef_ref, near_ref, state_refs)
+    start, move = ((0, 1), (tok_rows - 1, -1))[side]
+    fill_edge(edge_ref, held, coef_ref, tok_rows, tiles, start, move)
+
+
+def edge_terms(tok_rows, seq_index, coefs, near, states):
+    whole = pl.BlockSpec(memory_space=pltpu.VMEM)
+    return pl.pallas_call(
+        edge_kernel,
+        in_specs=[pl.BlockSpec(memory_space=pltpu.SMEM)] + [whole] * (2 + len(states)),
+        out_shape=jax.ShapeDtypeStruct(token_shape(tok_rows, coefs.shape[2]), F32),
+        compiler_params=pltpu.CompilerParams(vmem_limit_bytes=VMEM_BYTES),
+        name="edge_terms",
+    )(seq_index, coefs, near, *states)
+
+
+def multiply_out(part_ref, edge_ref, factor_refs, out_refs, hbm_refs, sems):
+    tok_rows, width = part_ref.shape
+    copies = []
+    for tile in range(width // LANES):
+        cols = slice(tile * LANES, (tile + 1) * LANES)
+        value = part_ref[:, cols] + edge_ref[tile_rows(tok_rows, tile), :]
+        for i, (factor_ref, out_ref, hbm_ref) in enumerate(zip(factor_refs, out_refs, hbm_refs)):
+            out_ref[:, cols] = (value * factor_ref[:, cols].astype(F32)).astype(BF16)
+            place = (slice(None), pl.ds(tile * LANES, LANES))
+            copies.append(
+                pltpu.make_async_copy(out_ref.at[place], hbm_ref.at[place], sems.at[i, tile])
+            )
+            copies[-1].start()
+    return copies
+
+
+def conv_kernel(seq_ref, part_ref, edge_ref, q_ref, coef_ref, near_ref, *refs):
+    state_refs, (layer_hbm, next_ref, layer_ref, sems) = refs[:-4], refs[-4:]
+    copies = multiply_out(part_ref, edge_ref, [q_ref], [layer_ref], [layer_hbm], sems)
+    fill_side(1, next_ref, seq_ref, coef_ref, near_ref, state_refs)
+    for copy in copies:
         copy.wait()
-    held = sum_pairs(0, seq_ref[0], coef_ref, near_ref, state_refs)
-    fill_edge(edge_ref, held, coef_ref, tok_rows, tiles, 0, 1)
-    for copy in arrivals[small : small + 2]:
+
+
+def conv_outputs(seq_index, part, edge, query_proj, coefs, near, states):
+    tok_rows, width = part.shape
+    whole = pl.BlockSpec(memory_space=pltpu.VMEM)
+    return pl.pallas_call(
+        conv_kernel,
+        in_specs=[pl.BlockSpec(memory_space=pltpu.SMEM)] + [whole] * (5 + len(states)),
+        out_specs=[pl.BlockSpec(memory_space=pl.ANY), whole],
+        out_shape=[
+            jax.ShapeDtypeStruct((tok_rows, width), BF16),
+            jax.ShapeDtypeStruct(edge.shape, F32),
+        ],
+        scratch_shapes=[
+            pltpu.VMEM((tok_rows, width), BF16),
+            pltpu.SemaphoreType.DMA((1, width // LANES)),
+        ],
+        compiler_params=pltpu.CompilerParams(vmem_limit_bytes=VMEM_BYTES),
+        name="conv_outputs",
+    )(seq_index, part, edge, query_proj, coefs, near, *states)
+
+
+def grad_kernel(
+    part_ref, edge_ref, v_ref, k_ref, key_hbm, value_hbm, key_ref, value_ref, sems
+):
+    copies = multiply_out(
+        part_ref, edge_ref, [v_ref, k_ref], [key_ref, value_ref], [key_hbm, value_hbm], sems
+    )
+    for copy in copies:
         copy.wait()
-    multiply_out(conv_ref, [(0, q_ref)])
-    held = sum_pairs(1, seq_ref[0], coef_ref, near_ref, state_refs)
-    fill_edge(edge_ref, held, coef_ref, tok_rows, tiles, tok_rows - 1, -1)
-    for copy in arrivals[small + 2 :]:
-        copy.wait()
-    multiply_out(grad_ref, [(1, v_ref), (2, k_ref)])
-    for copy in departures:
-        copy.wait()
-
-
-def final_outputs(
-    seq_index, coefs, near, states, conv_part, grad_part, query_proj, value_proj, key_proj
-):
-    tok_rows, width = key_proj.shape
-    tiles = coefs.shape[2]
-    args = (coefs, near, *states, conv_part, query_proj, grad_part, value_proj, key_proj)
-    away = pl.BlockSpec(memory_space=pl.ANY)
+
+
+def grad_outputs(part, edge, value_proj, key_proj):
+    tok_rows, width = part.shape
     return pl.pallas_call(
-        functools.partial(final_kernel, len(args)),
-        in_specs=[pl.BlockSpec(memory_space=pltpu.SMEM)] + [away] * len(args),
-        out_specs=[away] * 3,
-        out_shape=[jax.ShapeDtypeStruct((tok_rows, width), BF16)] * 3,
-        scratch_shapes=[pltpu.VMEM(arg.shape, arg.dtype) for arg in args]
-        + [pltpu.VMEM(token_shape(tok_rows, tiles), F32)]
-        + [pltpu.VMEM((tok_rows, width), BF16)] * 3
-        + [pltpu.SemaphoreType.DMA((len(args),)), pltpu.SemaphoreType.DMA((3, tiles))],
-        compiler_params=pltpu.CompilerParams(vmem_limit_bytes=FULL_VMEM_BYTES),
-        cost_estimate=takes(5.0),
-        name="final_outputs",
-    )(seq_index, *args)
+        grad_kernel,
+        in_specs=[pl.BlockSpec(memory_space=pltpu.VMEM)] * 4,
+        out_specs=[pl.BlockSpec(memory_space=pl.ANY)] * 2,
+        out_shape=[jax.ShapeDtypeStruct((tok_rows, width), BF16)] * 2,
+        scratch_shapes=[pltpu.VMEM((tok_rows, width), BF16)] * 2
+        + [pltpu.SemaphoreType.DMA((2, width // LANES))],
+        compiler_params=pltpu.CompilerParams(vmem_limit_bytes=VMEM_BYTES),
+        name="grad_outputs",
+    )(part, edge, value_proj, key_proj)
 
 
 def lag_kernel(shards, chans, groups, owned, scale, *refs):
@@ -473,7 +489,6 @@
             pltpu.VMEM((owned, LANES, full), BF16),
         ],
         compiler_params=pltpu.CompilerParams(vmem_limit_bytes=VMEM_BYTES),
-        cost_estimate=takes(2.5),
         name="filter_lags",
     )(done, *args)
 
@@ -518,9 +533,9 @@
     lags = lax.all_to_all(lags, "seq", split_axis=0, concat_axis=0, tiled=True)
     filter_grad = lags.reshape(shards * owned, tok_rows).T
     query_proj, key_proj, value_proj, _ = signals
-    layer_out, key_grad, value_grad = final_outputs(
-        seq_index, coefs, near, states, conv_part, grad_part, query_proj, value_proj, key_proj
-    )
+    edge = edge_terms(tok_rows, seq_index, coefs, near, states)
+    layer_out, edge = conv_outputs(seq_index, conv_part, edge, query_proj, coefs, near, states)
+    key_grad, value_grad = grad_outputs(grad_part, edge, value_proj, key_proj)
     return (layer_out, key_grad, value_grad, filter_grad)
 
 

time: 55.1 us -> 53.8 us (0.976)
  waiting for transfers between devices: 11.8 us -> 9.69 us
  other arithmetic: 0.04 us -> 1.88 us
  Pallas kernels: 21.9 us -> 20.3 us
  starting transfers between devices: 17.4 us -> 18.1 us
    all_to_all x1, waiting for transfers between devices: 5.48 us -> 2.51 us  [per_device(): lax.all_to_all(send, ('seq', 'chan'), split_axis=0, concat_axis=0, tiled=...]
    convert_element_type x3, other arithmetic: 0.02 us -> 1.86 us  [pair_states(): return [state.astype(LINK) for state in states]]
    pallas_call x1, Pallas kernels: 4.7 us -> 3.47 us  [filter_lags(): pl.pallas_call(functools.partial(lag_kernel, shards, chans, groups, owned...]
    pallas_call x2 -> x4, Pallas kernels: 11.2 us -> 10.3 us  [the longest x1 6.22 us: local_parts(): pl.pallas_call(local_kernel, out_shape=[jax.ShapeDtypeStruct((tok_rows, w...]
    all_to_all x1, waiting for transfers between devices: 1.85 us -> 2.71 us  [per_device(): lags = lax.all_to_all(lags, 'seq', split_axis=0, concat_axis=0, tiled=True)]
    pallas_call x1, Pallas kernels: 2.94 us -> 3.57 us  [block_states(): pl.pallas_call(state_kernel, out_shape=[jax.ShapeDtypeStruct((2, modes *...]
    ppermute x3, starting transfers between devices: 4.86 us -> 5.49 us  [along_column(): return lax.ppermute(state, 'seq', route)]
    unnamed x29 -> x23, local copies, waits for them, and re-layouts: 2.68 us -> 2.65 us
  transfers between devices with their start and end apart: 6 -> 6, of which waited for: 3 -> 3; matrix products, arithmetic and copies ran while one was open for 0% -> 4% of each run, Pallas kernels for 35% -> 32%
where the time goes in v20:
time: 53.8 us; the launch traced here: 53.6 us
  Pallas kernels  20.3 us (38%)
  starting transfers between devices  18.1 us (34%)
  waiting for transfers between devices  9.69 us (18%)
  local copies, waits for them, and re-layouts  2.73 us (5%)
  other arithmetic  1.88 us (3%)
  between operations  0.87 us (2%)
    all_to_all x1, starting transfers between devices, per_device(): lax.all_to_all(send, ('seq', 'chan'), split_axis=0, concat_axis=0, tiled=...  7.31 us
    pallas_call x1, Pallas kernels, local_parts(): pl.pallas_call(local_kernel, out_shape=[jax.ShapeDtypeStruct((tok_rows, w...  6.22 us
    ppermute x3, starting transfers between devices, along_column(): return lax.ppermute(state, 'seq', route)  5.49 us
    ppermute x1, waiting for transfers between devices, inside_pair(): return lax.ppermute(state, 'seq', [(i, i ^ 1) for i in range(2 * pairs)])  4.46 us
    pallas_call x1, Pallas kernels, block_states(): pl.pallas_call(state_kernel, out_shape=[jax.ShapeDtypeStruct((2, modes *...  3.57 us
    all_to_all x1, starting transfers between devices, per_device(): lags = lax.all_to_all(lags, 'seq', split_axis=0, concat_axis=0, tiled=True)  3.5 us
    pallas_call x1, Pallas kernels, filter_lags(): pl.pallas_call(functools.partial(lag_kernel, shards, chans, groups, owned...  3.47 us
    pallas_call x1, Pallas kernels, pack_signals(): pl.pallas_call(functools.partial(pack_kernel, shards, chans, owned), in_s...  2.97 us
  transfers between devices with their start and end apart: 6, of which 3 were waited for; matrix products, arithmetic and copies ran while one was open for 4% of the time, Pallas kernels for 32%

profile of v20, /device:TPU:0, one launch (start us, length us, event | category | flops | bytes accessed | tf_op | source)
XLA Modules:
  0.0 53.6 jit_solution(13869565995980658855)
XLA Ops:
  0.6 0.0 copy-start.9
  0.6 0.0 copy-start.10
  0.7 3.0 %pack_signals.1 = bf16[32,64,256]{2,1,0:T(8,128)(2,1)} custom-call(bf16[256,1024]{1,0:T(8,128)(2,1)} %k_ref.2, bf16[256,1024]{1,0:T(8,128)(2,1)} %v_ref.2, bf16[256,1024]{1,0:T(8,128)(2,1)} %o_ref.1, bf16[256,1024]{1,0:T(8,128)(2,1)} %q_ref.2), custom_call_target="tpu_custom_call" | custom-call | tf_op jit(solution)/shard_map/pack_signals/pallas_call | solution.py:97
  3.6 0.0 copy-start
  3.6 0.0 copy-start.1
  3.7 0.0 copy-start.2
  3.7 0.0 copy-start.3
  3.7 7.3 %all-to-all-start = ((bf16[32,64,256]{2,1,0:T(8,128)(2,1)}), bf16[32,64,256]{2,1,0:T(8,128)(2,1)S(1)}, u32[]{:S(2)}, u32[]{:S(2)}) async-start(bf16[32,64,256]{2,1,0:T(8,128)(2,1)} %pack_signals.1), calls=%async_computation | async-start | bytes 2097152 | tf_op jit(solution)/shard_map/all_to_all | solution.py:509
  11.0 0.0 copy-done.9
  11.0 0.0 copy-done.10
  11.1 0.1 broadcast_in_dim.11
  11.1 0.0 copy-done
  11.2 0.0 copy-done.1
  11.2 0.0 copy-done.2
  11.2 0.0 copy-done.3
  11.2 0.0 copy-start.8
  11.2 3.6 %block_states.1 = (f32[2,128,128]{2,1,0:T(8,128)S(1)}, bf16[2,128,128]{2,1,0:T(8,128)(2,1)}) custom-call(bf16[256,1024]{1,0:T(8,128)(2,1)S(1)} %copy-done, bf16[256,1024]{1,0:T(8,128)(2,1)S(1)} %copy-done.1, bf16[256,1024]{1,0:T(8,128)(2,1)S(1)} %copy-done.2, bf16[256,1024]{1,0:T(8,128)(2,1)S(1)} %copy-done.3, f32[3,16,8,128]{3,2,1,0:T(8,128)S(1)} %bitcast.14), custom_call_target="tpu_custom_call" | custom-call | tf_op jit(solution)/shard_map/block_states/pallas_call | solution.py:184
  14.8 1.8 %collective-permute-start = (bf16[2,128,128]{2,1,0:T(8,128)(2,1)}, bf16[2,128,128]{2,1,0:T(8,128)(2,1)S(1)}, u32[]{:S(2)}, u32[]{:S(2)}) collective-permute-start(bf16[2,128,128]{2,1,0:T(8,128)(2,1)} %get-tuple-element.39), channel_id=1, source_target_pairs={{0,4},{4,0},{8,12},{12,8},{16,20},{20,16},{24,28},{28,24},{1,5},{5... | collective-permute-start | bytes 196616 | tf_op jit(solution)/shard_map/ppermute | solution.py:283
  16.5 4.5 %collective-permute-done.near_ref = bf16[2,128,128]{2,1,0:T(8,128)(2,1)S(1)} collective-permute-done((bf16[2,128,128]{2,1,0:T(8,128)(2,1)}, bf16[2,128,128]{2,1,0:T(8,128)(2,1)S(1)}, u32[]{:S(2)}, u32[]{:S(2)}) %collective-permute-start) | collective-permute-done | bytes 65568 | tf_op jit(solution)/shard_map/ppermute | solution.py:283
  21.0 0.6 %convert_element_type.9 = bf16[128,128]{1,0:T(8,128)(2,1)} convert(f32[128,128]{1,0:T(8,128)S(1)} %get-tuple-element.40) | non-fusion elementwise | flops 16384 | bytes 98304 | tf_op jit(solution)/shard_map/convert_element_type | solution.py:222
  21.7 0.6 %convert_element_type.10 = bf16[128,128]{1,0:T(8,128)(2,1)} convert(f32[128,128]{1,0:T(8,128)S(1)} %get-tuple-element.41) | non-fusion elementwise | flops 16384 | bytes 98304 | tf_op jit(solution)/shard_map/convert_element_type | solution.py:222
  22.3 0.6 %convert_element_type.11 = bf16[128,128]{1,0:T(8,128)(2,1)} convert(f32[128,128]{1,0:T(8,128)S(1)} %get-tuple-element.42) | non-fusion elementwise | flops 16384 | bytes 98304 | tf_op jit(solution)/shard_map/convert_element_type | solution.py:222
  22.9 1.9 %collective-permute-start.1 = (bf16[128,128]{1,0:T(8,128)(2,1)}, bf16[128,128]{1,0:T(8,128)(2,1)S(1)}, u32[]{:S(2)}, u32[]{:S(2)}) collective-permute-start(bf16[128,128]{1,0:T(8,128)(2,1)} %convert_element_type.9), channel_id=1, source_target_pairs={{0,8},{4,12},{8,16},{12,20},{16,24},{20,28},{24,0},{28,4},{1,9},{5... | collective-permute-start | bytes 98312 | tf_op jit(solution)/shard_map/ppermute | solution.py:279
  24.8 2.1 %collective-permute-start.2 = (bf16[128,128]{1,0:T(8,128)(2,1)}, bf16[128,128]{1,0:T(8,128)(2,1)S(1)}, u32[]{:S(2)}, u32[]{:S(2)}) collective-permute-start(bf16[128,128]{1,0:T(8,128)(2,1)} %convert_element_type.10), channel_id=1, source_target_pairs={{0,16},{4,20},{8,24},{12,28},{16,0},{20,4},{24,8},{28,12},{1,17},{... | collective-permute-start | bytes 98312 | tf_op jit(solution)/shard_map/ppermute | solution.py:279
  26.8 1.6 %collective-permute-start.3 = (bf16[128,128]{1,0:T(8,128)(2,1)}, bf16[128,128]{1,0:T(8,128)(2,1)S(1)}, u32[]{:S(2)}, u32[]{:S(2)}) collective-permute-start(bf16[128,128]{1,0:T(8,128)(2,1)} %convert_element_type.11), channel_id=1, source_target_pairs={{0,24},{4,28},{8,0},{12,4},{16,8},{20,12},{24,16},{28,20},{1,25},{... | collective-permute-start | bytes 98312 | tf_op jit(solution)/shard_map/ppermute | solution.py:279
  28.4 0.0 copy-done.8
  28.4 6.2 %local_parts.1 = (f32[256,1024]{1,0:T(8,128)S(1)}, f32[256,1024]{1,0:T(8,128)S(1)}, f32[8,128]{1,0:T(8,128)S(1)}) custom-call(bf16[256,1024]{1,0:T(8,128)(2,1)S(1)} %copy-done, bf16[256,1024]{1,0:T(8,128)(2,1)S(1)} %copy-done.1, bf16[256,1024]{1,0:T(8,128)(2,1)S(1)} %copy-done.2, bf16[256,1024]{1,0:T(8,128)(2,1)S(1)} %copy-done.3, ...), custom_call_target="tpu_custom_call" | custom-call | tf_op jit(solution)/shard_map/local_parts/pallas_call | solution.py:267
  34.6 0.0 copy-start.4
  34.6 1.0 %copy-done.4 = f32[256,1024]{1,0:T(8,128)} copy-done((f32[256,1024]{1,0:T(8,128)}, f32[256,1024]{1,0:T(8,128)S(1)}, u32[]{:S(2)}) %copy-start.4) | copy-done | bytes 1048600
  35.6 0.0 copy-start.6
  35.6 1.0 %copy-done.6 = f32[256,1024]{1,0:T(8,128)} copy-done((f32[256,1024]{1,0:T(8,128)}, f32[256,1024]{1,0:T(8,128)S(1)}, u32[]{:S(2)}) %copy-start.6) | copy-done | bytes 1048600
  36.6 2.5 %all-to-all-done.refs_1_ = bf16[32,64,256]{2,1,0:T(8,128)(2,1)S(1)} async-done(((bf16[32,64,256]{2,1,0:T(8,128)(2,1)}), bf16[32,64,256]{2,1,0:T(8,128)(2,1)S(1)}, u32[]{:S(2)}, u32[]{:S(2)}) %all-to-all-start) | async-done | bytes 1048608 | tf_op jit(solution)/shard_map/all_to_all | solution.py:509
  39.1 3.5 %filter_lags.1 = f32[8,8,256]{2,1,0:T(8,128)} custom-call(f32[8,128]{1,0:T(8,128)S(1)} %get-tuple-element.46.refs_0_, bf16[32,64,256]{2,1,0:T(8,128)(2,1)S(1)} %all-to-all-done.refs_1_), custom_call_target="tpu_custom_call" | custom-call | tf_op jit(solution)/shard_map/filter_lags/pallas_call | solution.py:481
  42.6 0.0 copy-start.7
  42.6 0.0 collective-permute-done.1.refs_0_
  42.6 0.0 collective-permute-done.2.refs_1_
  42.6 0.0 collective-permute-done.3.refs_2_
  42.6 3.5 %all-to-all-start.1 = ((f32[8,8,256]{2,1,0:T(8,128)}), f32[8,8,256]{2,1,0:T(8,128)S(1)}, u32[]{:S(2)}, u32[]{:S(2)}) async-start(f32[8,8,256]{2,1,0:T(8,128)} %filter_lags.1), calls=%async_computation.1 | async-start | bytes 131072 | tf_op jit(solution)/shard_map/all_to_all | solution.py:533
  46.1 1.3 %edge_terms.1.edge_ref = f32[2112,128]{1,0:T(8,128)S(1)} custom-call(s32[1]{0:T(128)} %bitcast.seq_ref, f32[3,16,8,128]{3,2,1,0:T(8,128)S(1)} %bitcast.17, bf16[2,128,128]{2,1,0:T(8,128)(2,1)S(1)} %collective-permute-done.near_ref, bf16[128,128]{1,0:T(8,128)(2,1)S(1)} %collective-permute-done.1.refs_0_, bf16[128,128]{1,0:T(8,128)(2,1)S(1)} %collective-permute-done.2.refs_1_, ...), custom_call_target="tpu_custom_call" | custom-call | tf_op jit(solution)/shard_map/edge_terms/pallas_call | solution.py:314
  47.4 0.0 copy-done.7
  47.4 0.0 copy-start.5
  47.4 1.6 %conv_outputs.1 = (bf16[256,1024]{1,0:T(8,128)(2,1)}, f32[2112,128]{1,0:T(8,128)S(1)}) custom-call(s32[1]{0:T(128)} %bitcast.seq_ref, f32[256,1024]{1,0:T(8,128)S(1)} %copy-done.7, f32[2112,128]{1,0:T(8,128)S(1)} %edge_terms.1.edge_ref, bf16[256,1024]{1,0:T(8,128)(2,1)S(1)} %copy-done, f32[3,16,8,128]{3,2,1,0:T(8,128)S(1)} %bitcast.18, ...), custom_call_target="tpu_custom_call" | custom-call | tf_op jit(solution)/shard_map/conv_outputs/pallas_call | solution.py:350
  49.0 0.0 copy-done.5
  49.1 1.2 %grad_outputs.1 = (bf16[256,1024]{1,0:T(8,128)(2,1)}, bf16[256,1024]{1,0:T(8,128)(2,1)}) custom-call(f32[256,1024]{1,0:T(8,128)S(1)} %copy-done.5, f32[2112,128]{1,0:T(8,128)S(1)} %get-tuple-element.56.edge_ref, bf16[256,1024]{1,0:T(8,128)(2,1)S(1)} %copy-done.2, bf16[256,1024]{1,0:T(8,128)(2,1)S(1)} %copy-done.1), custom_call_target="tpu_custom_call" | custom-call | tf_op jit(solution)/shard_map/grad_outputs/pallas_call | solution.py:379
  50.2 2.7 %all-to-all-done.1 = f32[8,8,256]{2,1,0:T(8,128)S(1)} async-done(((f32[8,8,256]{2,1,0:T(8,128)}), f32[8,8,256]{2,1,0:T(8,128)S(1)}, u32[]{:S(2)}, u32[]{:S(2)}) %all-to-all-start.1) | async-done | bytes 65568 | tf_op jit(solution)/shard_map/all_to_all | solution.py:533
  52.9 0.6 %copy.12 = f32[256,64]{0,1:T(8,128)} copy(f32[256,64]{0,1:T(8,128)S(1)} %bitcast.20) | data formatting | bytes 131072
  (4 shorter events, 0.1 us)
Async XLA Ops:
  0.6 10.4 %copy-start.9 = (f32[256,16]{0,1:T(8,128)S(1)}, f32[256,16]{0,1:T(8,128)}, u32[]{:S(2)}) copy-start(f32[256,16]{0,1:T(8,128)} %param.12) | copy-start | bytes 49156
  0.6 10.4 %copy-start.10 = (f32[256,16]{0,1:T(8,128)S(1)}, f32[256,16]{0,1:T(8,128)}, u32[]{:S(2)}) copy-start(f32[256,16]{0,1:T(8,128)} %param.11) | copy-start | bytes 49156
  3.6 7.5 %copy-start = (bf16[256,1024]{1,0:T(8,128)(2,1)S(1)}, bf16[256,1024]{1,0:T(8,128)(2,1)}, u32[]{:S(2)}) copy-start(bf16[256,1024]{1,0:T(8,128)(2,1)} %q_ref.2) | copy-start | bytes 1572868
  3.6 7.5 %copy-start.1 = (bf16[256,1024]{1,0:T(8,128)(2,1)S(1)}, bf16[256,1024]{1,0:T(8,128)(2,1)}, u32[]{:S(2)}) copy-start(bf16[256,1024]{1,0:T(8,128)(2,1)} %k_ref.2) | copy-start | bytes 1572868
  3.7 7.5 %copy-start.2 = (bf16[256,1024]{1,0:T(8,128)(2,1)S(1)}, bf16[256,1024]{1,0:T(8,128)(2,1)}, u32[]{:S(2)}) copy-start(bf16[256,1024]{1,0:T(8,128)(2,1)} %v_ref.2) | copy-start | bytes 1572868
  3.7 7.5 %copy-start.3 = (bf16[256,1024]{1,0:T(8,128)(2,1)S(1)}, bf16[256,1024]{1,0:T(8,128)(2,1)}, u32[]{:S(2)}) copy-start(bf16[256,1024]{1,0:T(8,128)(2,1)} %o_ref.1) | copy-start | bytes 1572868
  3.7 35.4 %all-to-all-start = ((bf16[32,64,256]{2,1,0:T(8,128)(2,1)}), bf16[32,64,256]{2,1,0:T(8,128)(2,1)S(1)}, u32[]{:S(2)}, u32[]{:S(2)}) async-start(bf16[32,64,256]{2,1,0:T(8,128)(2,1)} %pack_signals.1), calls=%async_computation | async-start | bytes 2097152 | tf_op jit(solution)/shard_map/all_to_all | solution.py:509
  11.2 17.2 %copy-start.8 = (f32[1024]{0:T(1024)S(1)}, f32[1024]{0:T(1024)}, u32[]{:S(2)}) copy-start(f32[1024]{0:T(1024)} %param.13) | copy-start | bytes 12292
  14.8 6.2 %collective-permute-start = (bf16[2,128,128]{2,1,0:T(8,128)(2,1)}, bf16[2,128,128]{2,1,0:T(8,128)(2,1)S(1)}, u32[]{:S(2)}, u32[]{:S(2)}) collective-permute-start(bf16[2,128,128]{2,1,0:T(8,128)(2,1)} %get-tuple-element.39), channel_id=1, source_target_pairs={{0,4},{4,0},{8,12},{12,8},{16,20},{20,16},{24,28},{28,24},{1,5},{5... | collective-permute-start | bytes 196616 | tf_op jit(solution)/shard_map/ppermute | solution.py:283
  22.9 19.7 %collective-permute-start.1 = (bf16[128,128]{1,0:T(8,128)(2,1)}, bf16[128,128]{1,0:T(8,128)(2,1)S(1)}, u32[]{:S(2)}, u32[]{:S(2)}) collective-permute-start(bf16[128,128]{1,0:T(8,128)(2,1)} %convert_element_type.9), channel_id=1, source_target_pairs={{0,8},{4,12},{8,16},{12,20},{16,24},{20,28},{24,0},{28,4},{1,9},{5... | collective-permute-start | bytes 98312 | tf_op jit(solution)/shard_map/ppermute | solution.py:279
  24.8 17.8 %collective-permute-start.2 = (bf16[128,128]{1,0:T(8,128)(2,1)}, bf16[128,128]{1,0:T(8,128)(2,1)S(1)}, u32[]{:S(2)}, u32[]{:S(2)}) collective-permute-start(bf16[128,128]{1,0:T(8,128)(2,1)} %convert_element_type.10), channel_id=1, source_target_pairs={{0,16},{4,20},{8,24},{12,28},{16,0},{20,4},{24,8},{28,12},{1,17},{... | collective-permute-start | bytes 98312 | tf_op jit(solution)/shard_map/ppermute | solution.py:279
  26.8 15.8 %collective-permute-start.3 = (bf16[128,128]{1,0:T(8,128)(2,1)}, bf16[128,128]{1,0:T(8,128)(2,1)S(1)}, u32[]{:S(2)}, u32[]{:S(2)}) collective-permute-start(bf16[128,128]{1,0:T(8,128)(2,1)} %convert_element_type.11), channel_id=1, source_target_pairs={{0,24},{4,28},{8,0},{12,4},{16,8},{20,12},{24,16},{28,20},{1,25},{... | collective-permute-start | bytes 98312 | tf_op jit(solution)/shard_map/ppermute | solution.py:279
  34.6 1.0 %copy-start.4 = (f32[256,1024]{1,0:T(8,128)}, f32[256,1024]{1,0:T(8,128)S(1)}, u32[]{:S(2)}) copy-start(f32[256,1024]{1,0:T(8,128)S(1)} %get-tuple-element.55.part_ref) | copy-start | bytes 3145732
  35.6 1.0 %copy-start.6 = (f32[256,1024]{1,0:T(8,128)}, f32[256,1024]{1,0:T(8,128)S(1)}, u32[]{:S(2)}) copy-start(f32[256,1024]{1,0:T(8,128)S(1)} %get-tuple-element.44.part_ref) | copy-start | bytes 3145732
  42.6 4.8 %copy-start.7 = (f32[256,1024]{1,0:T(8,128)S(1)}, f32[256,1024]{1,0:T(8,128)}, u32[]{:S(2)}) copy-start(f32[256,1024]{1,0:T(8,128)} %copy-done.6) | copy-start | bytes 3145732
  42.6 10.3 %all-to-all-start.1 = ((f32[8,8,256]{2,1,0:T(8,128)}), f32[8,8,256]{2,1,0:T(8,128)S(1)}, u32[]{:S(2)}, u32[]{:S(2)}) async-start(f32[8,8,256]{2,1,0:T(8,128)} %filter_lags.1), calls=%async_computation.1 | async-start | bytes 131072 | tf_op jit(solution)/shard_map/all_to_all | solution.py:533
  47.4 1.7 %copy-start.5 = (f32[256,1024]{1,0:T(8,128)S(1)}, f32[256,1024]{1,0:T(8,128)}, u32[]{:S(2)}) copy-start(f32[256,1024]{1,0:T(8,128)} %copy-done.4) | copy-start | bytes 3145732

commit v21 on v20

--- a/solution.py
+++ b/solution.py
@@ -35,26 +35,28 @@
     tok_rows, width = held.shape[1:]
     groups = width // FILTERS
     per_chan = FILTERS // chans
-    units = [(which, first) for which in range(2) for first in range(0, groups, 2)]
-
-    def arrival(i, first):
-        place = (slice(None), pl.ds(first * FILTERS, 2 * FILTERS))
+    units = [(w, first, 0, tok_rows) for w in range(2) for first in range(0, groups, 2)]
+    which, first, _, _ = units.pop()
+    units += [(which, first, 0, tok_rows // 2), (which, first, tok_rows // 2, tok_rows // 2)]
+
+    def arrival(i, unit, n):
+        place = (pl.ds(unit[2], unit[3]), pl.ds(unit[1] * FILTERS, 2 * FILTERS))
         return pltpu.make_async_copy(
-            hbm_refs[i].at[place], held.at[(i, *place)], in_sems.at[i, first // 2]
+            hbm_refs[i].at[place], held.at[(i, *place)], in_sems.at[i % 2, n]
         )
 
-    def departure(which, first):
+    def departure(unit, n):
+        which, first, token, count = unit
+        lanes = pl.ds(token, count)
         if owned % SUBLANES:
-            place = (which, pl.ds(first, 2))
+            place = (which, pl.ds(first, 2), slice(None), lanes)
         else:
-            place = (slice(None), pl.ds((which * groups + first) * owned, 2 * owned))
-        return pltpu.make_async_copy(
-            packed.at[place], send_ref.at[place], out_sems.at[which, first // 2]
-        )
-
-    for which, first in units:
-        for i in (2 * which, 2 * which + 1):
-            arrival(i, first).start()
+            place = (slice(None), pl.ds((which * groups + first) * owned, 2 * owned), lanes)
+        return pltpu.make_async_copy(packed.at[place], send_ref.at[place], out_sems.at[n])
+
+    for n, unit in enumerate(units):
+        for i in (2 * unit[0], 2 * unit[0] + 1):
+            arrival(i, unit, n).start()
 
     def owned_filter(row):
         seq = row // (chans * owned)
@@ -62,28 +64,30 @@
         return chan * per_chan + seq * owned + row % owned
 
     order = one_hot(FILTERS, FILTERS, owned_filter)
-    for which, first in units:
+    for n, unit in enumerate(units):
+        which, first, token, count = unit
+        rows = slice(token, token + count)
         for i in (2 * which, 2 * which + 1):
-            arrival(i, first).wait()
+            arrival(i, unit, n).wait()
         pieces = []
         for group in (first, first + 1):
             cols = slice(group * FILTERS, (group + 1) * FILTERS)
             piece = lax.dot_general(
                 order,
-                product(held[2 * which, :, cols], held[2 * which + 1, :, cols]),
+                product(held[2 * which, rows, cols], held[2 * which + 1, rows, cols]),
                 (((1,), (1,)), ((), ())),
                 preferred_element_type=F32,
             )
             if owned % SUBLANES:
-                packed[which, group] = piece.astype(BF16)
+                packed[which, group, :, rows] = piece.astype(BF16)
             else:
-                pieces.append(piece.reshape(shards * chans, owned, tok_rows))
+                pieces.append(piece.reshape(shards * chans, owned, count))
         if pieces:
             row = (which * groups + first) * owned
-            packed[:, row : row + 2 * owned, :] = jnp.concatenate(pieces, axis=1).astype(BF16)
-        departure(which, first).start()
-    for which, first in units:
-        departure(which, first).wait()
+            packed[:, row : row + 2 * owned, rows] = jnp.concatenate(pieces, axis=1).astype(BF16)
+        departure(unit, n).start()
+    for n, unit in enumerate(units):
+        departure(unit, n).wait()
 
 
 def pack_signals(shards, chans, owned, query_proj, key_proj, value_proj, out_grad):
@@ -102,8 +106,8 @@
         scratch_shapes=[
             pltpu.VMEM((4, tok_rows, width), BF16),
             pltpu.VMEM(shape, BF16),
-            pltpu.SemaphoreType.DMA((4, groups // 2)),
-            pltpu.SemaphoreType.DMA((2, groups // 2)),
+            pltpu.SemaphoreType.DMA((2, groups + 1)),
+            pltpu.SemaphoreType.DMA((groups + 1,)),
         ],
         compiler_params=pltpu.CompilerParams(vmem_limit_bytes=FULL_VMEM_BYTES),
         name="pack_signals",
@@ -447,7 +451,13 @@
                 tables.append(jnp.zeros((LANES, LANES), F32))
             for d in range(batch):
                 joined = jnp.where(same_block, tables[d], tables[d + 1])
-                skewed = pltpu.roll(joined, 1, 1, stride=1, stride_axis=0)
+                folded = tree_sum(
+                    [
+                        pltpu.roll(joined[r : r + SUBLANES], r, 1) if r else joined[:SUBLANES]
+                        for r in range(0, LANES, SUBLANES)
+                    ]
+                )
+                skewed = pltpu.roll(folded, 1, 1, stride=1, stride_axis=0)
                 sums = jnp.sum(skewed, axis=0, keepdims=True) * scale
                 lane = d % halves * LANES
                 place = ((first + d) // halves, slice(None), slice(lane, lane + LANES))

time: 53.8 us -> 57.7 us (1.072)
  Pallas kernels: 20.3 us -> 24.2 us
    pallas_call x1, Pallas kernels: 3.47 us -> 7.12 us  [filter_lags(): pl.pallas_call(functools.partial(lag_kernel, shards, chans, groups, owned...]
  transfers between devices with their start and end apart: 6 -> 6, of which waited for: 3 -> 3; matrix products, arithmetic and copies ran while one was open for 4% -> 3% of each run, Pallas kernels for 32% -> 37%
where the time goes in v21:
time: 57.7 us; the launch traced here: 57.4 us
  Pallas kernels  24.2 us (42%)
  starting transfers between devices  18.1 us (31%)
  waiting for transfers between devices  9.69 us (17%)
  local copies, waits for them, and re-layouts  2.73 us (5%)
  other arithmetic  1.88 us (3%)
  between operations  0.87 us (2%)
    all_to_all x1, starting transfers between devices, per_device(): lax.all_to_all(send, ('seq', 'chan'), split_axis=0, concat_axis=0, tiled=...  7.3 us
    pallas_call x1, Pallas kernels, filter_lags(): pl.pallas_call(functools.partial(lag_kernel, shards, chans, groups, owned...  7.12 us
    pallas_call x1, Pallas kernels, local_parts(): pl.pallas_call(local_kernel, out_shape=[jax.ShapeDtypeStruct((tok_rows, w...  6.22 us
    ppermute x3, starting transfers between devices, along_column(): return lax.ppermute(state, 'seq', route)  5.49 us
    ppermute x1, waiting for transfers between devices, inside_pair(): return lax.ppermute(state, 'seq', [(i, i ^ 1) for i in range(2 * pairs)])  4.46 us
    pallas_call x1, Pallas kernels, block_states(): pl.pallas_call(state_kernel, out_shape=[jax.ShapeDtypeStruct((2, modes *...  3.57 us
    all_to_all x1, starting transfers between devices, per_device(): lags = lax.all_to_all(lags, 'seq', split_axis=0, concat_axis=0, tiled=True)  3.5 us
    pallas_call x1, Pallas kernels, pack_signals(): pl.pallas_call(functools.partial(pack_kernel, shards, chans, owned), in_s...  3.16 us
  transfers between devices with their start and end apart: 6, of which 3 were waited for; matrix products, arithmetic and copies ran while one was open for 3% of the time, Pallas kernels for 37%

profile of v21, /device:TPU:0, one launch (start us, length us, event | category | flops | bytes accessed | tf_op | source)
XLA Modules:
  0.0 57.4 jit_solution(13905400259978406661)
XLA Ops:
  0.6 0.0 copy-start.9
  0.6 0.0 copy-start.10
  0.7 3.2 %pack_signals.1 = bf16[32,64,256]{2,1,0:T(8,128)(2,1)} custom-call(bf16[256,1024]{1,0:T(8,128)(2,1)} %k_ref.2, bf16[256,1024]{1,0:T(8,128)(2,1)} %v_ref.2, bf16[256,1024]{1,0:T(8,128)(2,1)} %o_ref.1, bf16[256,1024]{1,0:T(8,128)(2,1)} %q_ref.2), custom_call_target="tpu_custom_call" | custom-call | tf_op jit(solution)/shard_map/pack_signals/pallas_call | solution.py:101
  3.8 0.0 copy-start
  3.8 0.0 copy-start.1
  3.8 0.0 copy-start.2
  3.9 0.0 copy-start.3
  3.9 7.3 %all-to-all-start = ((bf16[32,64,256]{2,1,0:T(8,128)(2,1)}), bf16[32,64,256]{2,1,0:T(8,128)(2,1)S(1)}, u32[]{:S(2)}, u32[]{:S(2)}) async-start(bf16[32,64,256]{2,1,0:T(8,128)(2,1)} %pack_signals.1), calls=%async_computation | async-start | bytes 2097152 | tf_op jit(solution)/shard_map/all_to_all | solution.py:519
  11.2 0.0 copy-done.9
  11.2 0.0 copy-done.10
  11.3 0.1 broadcast_in_dim.11
  11.3 0.0 copy-done
  11.3 0.0 copy-done.1
  11.3 0.0 copy-done.2
  11.4 0.0 copy-done.3
  11.4 0.0 copy-start.8
  11.4 3.6 %block_states.1 = (f32[2,128,128]{2,1,0:T(8,128)S(1)}, bf16[2,128,128]{2,1,0:T(8,128)(2,1)}) custom-call(bf16[256,1024]{1,0:T(8,128)(2,1)S(1)} %copy-done, bf16[256,1024]{1,0:T(8,128)(2,1)S(1)} %copy-done.1, bf16[256,1024]{1,0:T(8,128)(2,1)S(1)} %copy-done.2, bf16[256,1024]{1,0:T(8,128)(2,1)S(1)} %copy-done.3, f32[3,16,8,128]{3,2,1,0:T(8,128)S(1)} %bitcast.14), custom_call_target="tpu_custom_call" | custom-call | tf_op jit(solution)/shard_map/block_states/pallas_call | solution.py:188
  15.0 1.8 %collective-permute-start = (bf16[2,128,128]{2,1,0:T(8,128)(2,1)}, bf16[2,128,128]{2,1,0:T(8,128)(2,1)S(1)}, u32[]{:S(2)}, u32[]{:S(2)}) collective-permute-start(bf16[2,128,128]{2,1,0:T(8,128)(2,1)} %get-tuple-element.39), channel_id=1, source_target_pairs={{0,4},{4,0},{8,12},{12,8},{16,20},{20,16},{24,28},{28,24},{1,5},{5... | collective-permute-start | bytes 196616 | tf_op jit(solution)/shard_map/ppermute | solution.py:287
  16.7 4.5 %collective-permute-done.near_ref = bf16[2,128,128]{2,1,0:T(8,128)(2,1)S(1)} collective-permute-done((bf16[2,128,128]{2,1,0:T(8,128)(2,1)}, bf16[2,128,128]{2,1,0:T(8,128)(2,1)S(1)}, u32[]{:S(2)}, u32[]{:S(2)}) %collective-permute-start) | collective-permute-done | bytes 65568 | tf_op jit(solution)/shard_map/ppermute | solution.py:287
  21.2 0.6 %convert_element_type.9 = bf16[128,128]{1,0:T(8,128)(2,1)} convert(f32[128,128]{1,0:T(8,128)S(1)} %get-tuple-element.40) | non-fusion elementwise | flops 16384 | bytes 98304 | tf_op jit(solution)/shard_map/convert_element_type | solution.py:226
  21.8 0.6 %convert_element_type.10 = bf16[128,128]{1,0:T(8,128)(2,1)} convert(f32[128,128]{1,0:T(8,128)S(1)} %get-tuple-element.41) | non-fusion elementwise | flops 16384 | bytes 98304 | tf_op jit(solution)/shard_map/convert_element_type | solution.py:226
  22.5 0.6 %convert_element_type.11 = bf16[128,128]{1,0:T(8,128)(2,1)} convert(f32[128,128]{1,0:T(8,128)S(1)} %get-tuple-element.42) | non-fusion elementwise | flops 16384 | bytes 98304 | tf_op jit(solution)/shard_map/convert_element_type | solution.py:226
  23.1 1.9 %collective-permute-start.1 = (bf16[128,128]{1,0:T(8,128)(2,1)}, bf16[128,128]{1,0:T(8,128)(2,1)S(1)}, u32[]{:S(2)}, u32[]{:S(2)}) collective-permute-start(bf16[128,128]{1,0:T(8,128)(2,1)} %convert_element_type.9), channel_id=1, source_target_pairs={{0,8},{4,12},{8,16},{12,20},{16,24},{20,28},{24,0},{28,4},{1,9},{5... | collective-permute-start | bytes 98312 | tf_op jit(solution)/shard_map/ppermute | solution.py:283
  25.0 2.1 %collective-permute-start.2 = (bf16[128,128]{1,0:T(8,128)(2,1)}, bf16[128,128]{1,0:T(8,128)(2,1)S(1)}, u32[]{:S(2)}, u32[]{:S(2)}) collective-permute-start(bf16[128,128]{1,0:T(8,128)(2,1)} %convert_element_type.10), channel_id=1, source_target_pairs={{0,16},{4,20},{8,24},{12,28},{16,0},{20,4},{24,8},{28,12},{1,17},{... | collective-permute-start | bytes 98312 | tf_op jit(solution)/shard_map/ppermute | solution.py:283
  27.0 1.6 %collective-permute-start.3 = (bf16[128,128]{1,0:T(8,128)(2,1)}, bf16[128,128]{1,0:T(8,128)(2,1)S(1)}, u32[]{:S(2)}, u32[]{:S(2)}) collective-permute-start(bf16[128,128]{1,0:T(8,128)(2,1)} %convert_element_type.11), channel_id=1, source_target_pairs={{0,24},{4,28},{8,0},{12,4},{16,8},{20,12},{24,16},{28,20},{1,25},{... | collective-permute-start | bytes 98312 | tf_op jit(solution)/shard_map/ppermute | solution.py:283
  28.6 0.0 copy-done.8
  28.6 6.2 %local_parts.1 = (f32[256,1024]{1,0:T(8,128)S(1)}, f32[256,1024]{1,0:T(8,128)S(1)}, f32[8,128]{1,0:T(8,128)S(1)}) custom-call(bf16[256,1024]{1,0:T(8,128)(2,1)S(1)} %copy-done, bf16[256,1024]{1,0:T(8,128)(2,1)S(1)} %copy-done.1, bf16[256,1024]{1,0:T(8,128)(2,1)S(1)} %copy-done.2, bf16[256,1024]{1,0:T(8,128)(2,1)S(1)} %copy-done.3, ...), custom_call_target="tpu_custom_call" | custom-call | tf_op jit(solution)/shard_map/local_parts/pallas_call | solution.py:271
  34.8 0.0 copy-start.4
  34.8 1.0 %copy-done.4 = f32[256,1024]{1,0:T(8,128)} copy-done((f32[256,1024]{1,0:T(8,128)}, f32[256,1024]{1,0:T(8,128)S(1)}, u32[]{:S(2)}) %copy-start.4) | copy-done | bytes 1048600
  35.8 0.0 copy-start.6
  35.8 1.0 %copy-done.6 = f32[256,1024]{1,0:T(8,128)} copy-done((f32[256,1024]{1,0:T(8,128)}, f32[256,1024]{1,0:T(8,128)S(1)}, u32[]{:S(2)}) %copy-start.6) | copy-done | bytes 1048600
  36.8 2.5 %all-to-all-done.refs_1_ = bf16[32,64,256]{2,1,0:T(8,128)(2,1)S(1)} async-done(((bf16[32,64,256]{2,1,0:T(8,128)(2,1)}), bf16[32,64,256]{2,1,0:T(8,128)(2,1)S(1)}, u32[]{:S(2)}, u32[]{:S(2)}) %all-to-all-start) | async-done | bytes 1048608 | tf_op jit(solution)/shard_map/all_to_all | solution.py:519
  39.3 7.1 %filter_lags.1 = f32[8,8,256]{2,1,0:T(8,128)} custom-call(f32[8,128]{1,0:T(8,128)S(1)} %get-tuple-element.46.refs_0_, bf16[32,64,256]{2,1,0:T(8,128)(2,1)S(1)} %all-to-all-done.refs_1_), custom_call_target="tpu_custom_call" | custom-call | tf_op jit(solution)/shard_map/filter_lags/pallas_call | solution.py:491
  46.4 0.0 copy-start.7
  46.4 0.0 collective-permute-done.1.refs_0_
  46.4 0.0 collective-permute-done.2.refs_1_
  46.4 0.0 collective-permute-done.3.refs_2_
  46.4 3.5 %all-to-all-start.1 = ((f32[8,8,256]{2,1,0:T(8,128)}), f32[8,8,256]{2,1,0:T(8,128)S(1)}, u32[]{:S(2)}, u32[]{:S(2)}) async-start(f32[8,8,256]{2,1,0:T(8,128)} %filter_lags.1), calls=%async_computation.1 | async-start | bytes 131072 | tf_op jit(solution)/shard_map/all_to_all | solution.py:543
  49.9 1.3 %edge_terms.1.edge_ref = f32[2112,128]{1,0:T(8,128)S(1)} custom-call(s32[1]{0:T(128)} %bitcast.seq_ref, f32[3,16,8,128]{3,2,1,0:T(8,128)S(1)} %bitcast.17, bf16[2,128,128]{2,1,0:T(8,128)(2,1)S(1)} %collective-permute-done.near_ref, bf16[128,128]{1,0:T(8,128)(2,1)S(1)} %collective-permute-done.1.refs_0_, bf16[128,128]{1,0:T(8,128)(2,1)S(1)} %collective-permute-done.2.refs_1_, ...), custom_call_target="tpu_custom_call" | custom-call | tf_op jit(solution)/shard_map/edge_terms/pallas_call | solution.py:318
  51.2 0.0 copy-done.7
  51.2 0.0 copy-start.5
  51.2 1.6 %conv_outputs.1 = (bf16[256,1024]{1,0:T(8,128)(2,1)}, f32[2112,128]{1,0:T(8,128)S(1)}) custom-call(s32[1]{0:T(128)} %bitcast.seq_ref, f32[256,1024]{1,0:T(8,128)S(1)} %copy-done.7, f32[2112,128]{1,0:T(8,128)S(1)} %edge_terms.1.edge_ref, bf16[256,1024]{1,0:T(8,128)(2,1)S(1)} %copy-done, f32[3,16,8,128]{3,2,1,0:T(8,128)S(1)} %bitcast.18, ...), custom_call_target="tpu_custom_call" | custom-call | tf_op jit(solution)/shard_map/conv_outputs/pallas_call | solution.py:354
  52.9 0.0 copy-done.5
  52.9 1.2 %grad_outputs.1 = (bf16[256,1024]{1,0:T(8,128)(2,1)}, bf16[256,1024]{1,0:T(8,128)(2,1)}) custom-call(f32[256,1024]{1,0:T(8,128)S(1)} %copy-done.5, f32[2112,128]{1,0:T(8,128)S(1)} %get-tuple-element.56.edge_ref, bf16[256,1024]{1,0:T(8,128)(2,1)S(1)} %copy-done.2, bf16[256,1024]{1,0:T(8,128)(2,1)S(1)} %copy-done.1), custom_call_target="tpu_custom_call" | custom-call | tf_op jit(solution)/shard_map/grad_outputs/pallas_call | solution.py:383
  54.1 2.7 %all-to-all-done.1 = f32[8,8,256]{2,1,0:T(8,128)S(1)} async-done(((f32[8,8,256]{2,1,0:T(8,128)}), f32[8,8,256]{2,1,0:T(8,128)S(1)}, u32[]{:S(2)}, u32[]{:S(2)}) %all-to-all-start.1) | async-done | bytes 65568 | tf_op jit(solution)/shard_map/all_to_all | solution.py:543
  56.8 0.6 %copy.12 = f32[256,64]{0,1:T(8,128)} copy(f32[256,64]{0,1:T(8,128)S(1)} %bitcast.20) | data formatting | bytes 131072
  (4 shorter events, 0.1 us)
Async XLA Ops:
  0.6 10.5 %copy-start.9 = (f32[256,16]{0,1:T(8,128)S(1)}, f32[256,16]{0,1:T(8,128)}, u32[]{:S(2)}) copy-start(f32[256,16]{0,1:T(8,128)} %param.12) | copy-start | bytes 49156
  0.6 10.5 %copy-start.10 = (f32[256,16]{0,1:T(8,128)S(1)}, f32[256,16]{0,1:T(8,128)}, u32[]{:S(2)}) copy-start(f32[256,16]{0,1:T(8,128)} %param.11) | copy-start | bytes 49156
  3.8 7.5 %copy-start = (bf16[256,1024]{1,0:T(8,128)(2,1)S(1)}, bf16[256,1024]{1,0:T(8,128)(2,1)}, u32[]{:S(2)}) copy-start(bf16[256,1024]{1,0:T(8,128)(2,1)} %q_ref.2) | copy-start | bytes 1572868
  3.8 7.5 %copy-start.1 = (bf16[256,1024]{1,0:T(8,128)(2,1)S(1)}, bf16[256,1024]{1,0:T(8,128)(2,1)}, u32[]{:S(2)}) copy-start(bf16[256,1024]{1,0:T(8,128)(2,1)} %k_ref.2) | copy-start | bytes 1572868
  3.8 7.5 %copy-start.2 = (bf16[256,1024]{1,0:T(8,128)(2,1)S(1)}, bf16[256,1024]{1,0:T(8,128)(2,1)}, u32[]{:S(2)}) copy-start(bf16[256,1024]{1,0:T(8,128)(2,1)} %v_ref.2) | copy-start | bytes 1572868
  3.9 7.5 %copy-start.3 = (bf16[256,1024]{1,0:T(8,128)(2,1)S(1)}, bf16[256,1024]{1,0:T(8,128)(2,1)}, u32[]{:S(2)}) copy-start(bf16[256,1024]{1,0:T(8,128)(2,1)} %o_ref.1) | copy-start | bytes 1572868
  3.9 35.4 %all-to-all-start = ((bf16[32,64,256]{2,1,0:T(8,128)(2,1)}), bf16[32,64,256]{2,1,0:T(8,128)(2,1)S(1)}, u32[]{:S(2)}, u32[]{:S(2)}) async-start(bf16[32,64,256]{2,1,0:T(8,128)(2,1)} %pack_signals.1), calls=%async_computation | async-start | bytes 2097152 | tf_op jit(solution)/shard_map/all_to_all | solution.py:519
  11.4 17.2 %copy-start.8 = (f32[1024]{0:T(1024)S(1)}, f32[1024]{0:T(1024)}, u32[]{:S(2)}) copy-start(f32[1024]{0:T(1024)} %param.13) | copy-start | bytes 12292
  15.0 6.2 %collective-permute-start = (bf16[2,128,128]{2,1,0:T(8,128)(2,1)}, bf16[2,128,128]{2,1,0:T(8,128)(2,1)S(1)}, u32[]{:S(2)}, u32[]{:S(2)}) collective-permute-start(bf16[2,128,128]{2,1,0:T(8,128)(2,1)} %get-tuple-element.39), channel_id=1, source_target_pairs={{0,4},{4,0},{8,12},{12,8},{16,20},{20,16},{24,28},{28,24},{1,5},{5... | collective-permute-start | bytes 196616 | tf_op jit(solution)/shard_map/ppermute | solution.py:287
  23.1 23.3 %collective-permute-start.1 = (bf16[128,128]{1,0:T(8,128)(2,1)}, bf16[128,128]{1,0:T(8,128)(2,1)S(1)}, u32[]{:S(2)}, u32[]{:S(2)}) collective-permute-start(bf16[128,128]{1,0:T(8,128)(2,1)} %convert_element_type.9), channel_id=1, source_target_pairs={{0,8},{4,12},{8,16},{12,20},{16,24},{20,28},{24,0},{28,4},{1,9},{5... | collective-permute-start | bytes 98312 | tf_op jit(solution)/shard_map/ppermute | solution.py:283
  25.0 21.5 %collective-permute-start.2 = (bf16[128,128]{1,0:T(8,128)(2,1)}, bf16[128,128]{1,0:T(8,128)(2,1)S(1)}, u32[]{:S(2)}, u32[]{:S(2)}) collective-permute-start(bf16[128,128]{1,0:T(8,128)(2,1)} %convert_element_type.10), channel_id=1, source_target_pairs={{0,16},{4,20},{8,24},{12,28},{16,0},{20,4},{24,8},{28,12},{1,17},{... | collective-permute-start | bytes 98312 | tf_op jit(solution)/shard_map/ppermute | solution.py:283
  27.0 19.4 %collective-permute-start.3 = (bf16[128,128]{1,0:T(8,128)(2,1)}, bf16[128,128]{1,0:T(8,128)(2,1)S(1)}, u32[]{:S(2)}, u32[]{:S(2)}) collective-permute-start(bf16[128,128]{1,0:T(8,128)(2,1)} %convert_element_type.11), channel_id=1, source_target_pairs={{0,24},{4,28},{8,0},{12,4},{16,8},{20,12},{24,16},{28,20},{1,25},{... | collective-permute-start | bytes 98312 | tf_op jit(solution)/shard_map/ppermute | solution.py:283
  34.8 1.0 %copy-start.4 = (f32[256,1024]{1,0:T(8,128)}, f32[256,1024]{1,0:T(8,128)S(1)}, u32[]{:S(2)}) copy-start(f32[256,1024]{1,0:T(8,128)S(1)} %get-tuple-element.55.part_ref) | copy-start | bytes 3145732
  35.8 1.0 %copy-start.6 = (f32[256,1024]{1,0:T(8,128)}, f32[256,1024]{1,0:T(8,128)S(1)}, u32[]{:S(2)}) copy-start(f32[256,1024]{1,0:T(8,128)S(1)} %get-tuple-element.44.part_ref) | copy-start | bytes 3145732
  46.4 4.8 %copy-start.7 = (f32[256,1024]{1,0:T(8,128)S(1)}, f32[256,1024]{1,0:T(8,128)}, u32[]{:S(2)}) copy-start(f32[256,1024]{1,0:T(8,128)} %copy-done.6) | copy-start | bytes 3145732
  46.4 10.3 %all-to-all-start.1 = ((f32[8,8,256]{2,1,0:T(8,128)}), f32[8,8,256]{2,1,0:T(8,128)S(1)}, u32[]{:S(2)}, u32[]{:S(2)}) async-start(f32[8,8,256]{2,1,0:T(8,128)} %filter_lags.1), calls=%async_computation.1 | async-start | bytes 131072 | tf_op jit(solution)/shard_map/all_to_all | solution.py:543
  51.2 1.7 %copy-start.5 = (f32[256,1024]{1,0:T(8,128)S(1)}, f32[256,1024]{1,0:T(8,128)}, u32[]{:S(2)}) copy-start(f32[256,1024]{1,0:T(8,128)} %copy-done.4) | copy-start | bytes 3145732

commit v22 on v20

--- a/solution.py
+++ b/solution.py
@@ -388,10 +388,10 @@
     )(part, edge, value_proj, key_proj)
 
 
-def lag_kernel(shards, chans, groups, owned, scale, *refs):
-    in_refs, (out_ref, u_all, g_all, turned_all) = refs[1:-4], refs[-4:]
-    tok_rows = out_ref.shape[2]
-    halves = tok_rows // LANES
+def lag_kernel(shards, chans, groups, owned, *refs):
+    in_refs, (out_ref, lag_sums, u_all, g_all, turned_all) = refs[1:-5], refs[-5:]
+    halves = out_ref.shape[1] // owned
+    tok_rows = halves * LANES
     blocks = shards * halves
     depth = chans * groups
     full = blocks * depth
@@ -448,10 +448,10 @@
             for d in range(batch):
                 joined = jnp.where(same_block, tables[d], tables[d + 1])
                 skewed = pltpu.roll(joined, 1, 1, stride=1, stride_axis=0)
-                sums = jnp.sum(skewed, axis=0, keepdims=True) * scale
-                lane = d % halves * LANES
-                place = ((first + d) // halves, slice(None), slice(lane, lane + LANES))
-                out_ref[place] = jnp.where(filter_row == f, sums, out_ref[place])
+                sums = jnp.sum(skewed, axis=0, keepdims=True)
+                row = d % halves * owned
+                place = ((first + d) // halves, slice(row, row + owned), slice(None))
+                lag_sums[place] = jnp.where(filter_row == f, sums, lag_sums[place])
 
         if batch == blocks:
             some_lags(0)
@@ -464,9 +464,10 @@
             mirror, u_all[f], (((1,), (1,)), ((), ())), preferred_element_type=F32
         ).astype(BF16)
     lax.fori_loop(0, owned, one_filter, 0, unroll=min(owned, 8))
-
-
-def filter_lags(received, done, shards, chans, owned, scale):
+    out_ref[...] = lag_sums[...].astype(LINK)
+
+
+def filter_lags(received, done, shards, chans, owned):
     tok_rows = received.shape[2]
     groups = received.shape[1] // (2 * owned)
     halves = tok_rows // LANES
@@ -479,11 +480,12 @@
         args = (split[0], split[1])
     whole = pl.BlockSpec(memory_space=pltpu.VMEM)
     return pl.pallas_call(
-        functools.partial(lag_kernel, shards, chans, groups, owned, scale),
+        functools.partial(lag_kernel, shards, chans, groups, owned),
         in_specs=[pl.BlockSpec(memory_space=pl.ANY)] + [whole] * len(args),
         out_specs=whole,
-        out_shape=jax.ShapeDtypeStruct((shards, owned, tok_rows), F32),
+        out_shape=jax.ShapeDtypeStruct((shards, halves * owned, LANES), LINK),
         scratch_shapes=[
+            pltpu.VMEM((shards, halves * owned, LANES), F32),
             pltpu.VMEM((owned, full, LANES), BF16),
             pltpu.VMEM((owned, 2 * full + depth, LANES), BF16),
             pltpu.VMEM((owned, LANES, full), BF16),
@@ -528,10 +530,11 @@
     conv_part, grad_part, done = local_parts(*signals, coefs, skip_gain[None, :])
 
     scale = 1.0 / math.sqrt(length * (CHANNELS // FILTERS))
-    lags = filter_lags(received, done, shards, chans, owned, scale)
+    lags = filter_lags(received, done, shards, chans, owned)
     lags, *states = lax.optimization_barrier((lags, *states))
     lags = lax.all_to_all(lags, "seq", split_axis=0, concat_axis=0, tiled=True)
-    filter_grad = lags.reshape(shards * owned, tok_rows).T
+    lags = lags.reshape(shards, tok_rows // LANES, owned, LANES).transpose(0, 2, 1, 3)
+    filter_grad = lags.reshape(shards * owned, tok_rows).T.astype(F32) * scale
     query_proj, key_proj, value_proj, _ = signals
     edge = edge_terms(tok_rows, seq_index, coefs, near, states)
     layer_out, edge = conv_outputs(seq_index, conv_part, edge, query_proj, coefs, near, states)

time: 53.8 us -> 53.6 us (level)
  other arithmetic: 1.88 us -> 2.52 us
  local copies, waits for them, and re-layouts: 2.73 us -> 2.1 us
    mul x0 -> x1, other arithmetic: none -> 0.64 us  [per_device(): filter_grad = lags.reshape(shards * owned, tok_rows).T.astype(F32) * scale]
    unnamed x23 -> x22, local copies, waits for them, and re-layouts: 2.65 us -> 2.02 us
  transfers between devices with their start and end apart: 6 -> 6, of which waited for: 3 -> 3; matrix products, arithmetic and copies ran while one was open for 4% -> 4% of each run, Pallas kernels for 32% -> 33%
where the time goes in v22:
time: 53.6 us; the launch traced here: 53.3 us
  Pallas kernels  20.3 us (38%)
  starting transfers between devices  18 us (34%)
  waiting for transfers between devices  9.47 us (18%)
  other arithmetic  2.52 us (5%)
  local copies, waits for them, and re-layouts  2.1 us (4%)
  between operations  0.87 us (2%)
    all_to_all x1, starting transfers between devices, per_device(): lax.all_to_all(send, ('seq', 'chan'), split_axis=0, concat_axis=0, tiled=...  7.31 us
    pallas_call x1, Pallas kernels, local_parts(): pl.pallas_call(local_kernel, out_shape=[jax.ShapeDtypeStruct((tok_rows, w...  6.22 us
    ppermute x3, starting transfers between devices, along_column(): return lax.ppermute(state, 'seq', route)  5.49 us
    ppermute x1, waiting for transfers between devices, inside_pair(): return lax.ppermute(state, 'seq', [(i, i ^ 1) for i in range(2 * pairs)])  4.46 us
    pallas_call x1, Pallas kernels, block_states(): pl.pallas_call(state_kernel, out_shape=[jax.ShapeDtypeStruct((2, modes *...  3.57 us
    all_to_all x1, starting transfers between devices, per_device(): lags = lax.all_to_all(lags, 'seq', split_axis=0, concat_axis=0, tiled=True)  3.48 us
    pallas_call x1, Pallas kernels, filter_lags(): pl.pallas_call(functools.partial(lag_kernel, shards, chans, groups, owned...  3.45 us
    pallas_call x1, Pallas kernels, pack_signals(): pl.pallas_call(functools.partial(pack_kernel, shards, chans, owned), in_s...  2.97 us
  transfers between devices with their start and end apart: 6, of which 3 were waited for; matrix products, arithmetic and copies ran while one was open for 4% of the time, Pallas kernels for 33%

profile of v22, /device:TPU:0, one launch (start us, length us, event | category | flops | bytes accessed | tf_op | source)
XLA Modules:
  0.0 53.3 jit_solution(7676293298108420380)
XLA Ops:
  0.6 0.0 copy-start.9
  0.6 0.0 copy-start.10
  0.7 3.0 %pack_signals.1 = bf16[32,64,256]{2,1,0:T(8,128)(2,1)} custom-call(bf16[256,1024]{1,0:T(8,128)(2,1)} %k_ref.2, bf16[256,1024]{1,0:T(8,128)(2,1)} %v_ref.2, bf16[256,1024]{1,0:T(8,128)(2,1)} %o_ref.1, bf16[256,1024]{1,0:T(8,128)(2,1)} %q_ref.2), custom_call_target="tpu_custom_call" | custom-call | tf_op jit(solution)/shard_map/pack_signals/pallas_call | solution.py:97
  3.6 0.0 copy-start
  3.6 0.0 copy-start.1
  3.7 0.0 copy-start.2
  3.7 0.0 copy-start.3
  3.7 7.3 %all-to-all-start = ((bf16[32,64,256]{2,1,0:T(8,128)(2,1)}), bf16[32,64,256]{2,1,0:T(8,128)(2,1)S(1)}, u32[]{:S(2)}, u32[]{:S(2)}) async-start(bf16[32,64,256]{2,1,0:T(8,128)(2,1)} %pack_signals.1), calls=%async_computation | async-start | bytes 2097152 | tf_op jit(solution)/shard_map/all_to_all | solution.py:511
  11.0 0.0 copy-done.9
  11.0 0.0 copy-done.10
  11.1 0.1 broadcast_in_dim.11
  11.1 0.0 copy-done
  11.2 0.0 copy-done.1
  11.2 0.0 copy-done.2
  11.2 0.0 copy-done.3
  11.2 0.0 copy-start.8
  11.2 3.6 %block_states.1 = (f32[2,128,128]{2,1,0:T(8,128)S(1)}, bf16[2,128,128]{2,1,0:T(8,128)(2,1)}) custom-call(bf16[256,1024]{1,0:T(8,128)(2,1)S(1)} %copy-done, bf16[256,1024]{1,0:T(8,128)(2,1)S(1)} %copy-done.1, bf16[256,1024]{1,0:T(8,128)(2,1)S(1)} %copy-done.2, bf16[256,1024]{1,0:T(8,128)(2,1)S(1)} %copy-done.3, f32[3,16,8,128]{3,2,1,0:T(8,128)S(1)} %bitcast.19), custom_call_target="tpu_custom_call" | custom-call | tf_op jit(solution)/shard_map/block_states/pallas_call | solution.py:184
  14.8 1.8 %collective-permute-start = (bf16[2,128,128]{2,1,0:T(8,128)(2,1)}, bf16[2,128,128]{2,1,0:T(8,128)(2,1)S(1)}, u32[]{:S(2)}, u32[]{:S(2)}) collective-permute-start(bf16[2,128,128]{2,1,0:T(8,128)(2,1)} %get-tuple-element.39), channel_id=1, source_target_pairs={{0,4},{4,0},{8,12},{12,8},{16,20},{20,16},{24,28},{28,24},{1,5},{5... | collective-permute-start | bytes 196616 | tf_op jit(solution)/shard_map/ppermute | solution.py:283
  16.5 4.5 %collective-permute-done.near_ref = bf16[2,128,128]{2,1,0:T(8,128)(2,1)S(1)} collective-permute-done((bf16[2,128,128]{2,1,0:T(8,128)(2,1)}, bf16[2,128,128]{2,1,0:T(8,128)(2,1)S(1)}, u32[]{:S(2)}, u32[]{:S(2)}) %collective-permute-start) | collective-permute-done | bytes 65568 | tf_op jit(solution)/shard_map/ppermute | solution.py:283
  21.0 0.6 %convert_element_type.18 = bf16[128,128]{1,0:T(8,128)(2,1)} convert(f32[128,128]{1,0:T(8,128)S(1)} %get-tuple-element.40) | non-fusion elementwise | flops 16384 | bytes 98304 | tf_op jit(solution)/shard_map/convert_element_type | solution.py:222
  21.7 0.6 %convert_element_type.19 = bf16[128,128]{1,0:T(8,128)(2,1)} convert(f32[128,128]{1,0:T(8,128)S(1)} %get-tuple-element.41) | non-fusion elementwise | flops 16384 | bytes 98304 | tf_op jit(solution)/shard_map/convert_element_type | solution.py:222
  22.3 0.6 %convert_element_type.20 = bf16[128,128]{1,0:T(8,128)(2,1)} convert(f32[128,128]{1,0:T(8,128)S(1)} %get-tuple-element.42) | non-fusion elementwise | flops 16384 | bytes 98304 | tf_op jit(solution)/shard_map/convert_element_type | solution.py:222
  22.9 1.9 %collective-permute-start.1 = (bf16[128,128]{1,0:T(8,128)(2,1)}, bf16[128,128]{1,0:T(8,128)(2,1)S(1)}, u32[]{:S(2)}, u32[]{:S(2)}) collective-permute-start(bf16[128,128]{1,0:T(8,128)(2,1)} %convert_element_type.18), channel_id=1, source_target_pairs={{0,8},{4,12},{8,16},{12,20},{16,24},{20,28},{24,0},{28,4},{1,9},{5... | collective-permute-start | bytes 98312 | tf_op jit(solution)/shard_map/ppermute | solution.py:279
  24.8 2.1 %collective-permute-start.2 = (bf16[128,128]{1,0:T(8,128)(2,1)}, bf16[128,128]{1,0:T(8,128)(2,1)S(1)}, u32[]{:S(2)}, u32[]{:S(2)}) collective-permute-start(bf16[128,128]{1,0:T(8,128)(2,1)} %convert_element_type.19), channel_id=1, source_target_pairs={{0,16},{4,20},{8,24},{12,28},{16,0},{20,4},{24,8},{28,12},{1,17},{... | collective-permute-start | bytes 98312 | tf_op jit(solution)/shard_map/ppermute | solution.py:279
  26.8 1.6 %collective-permute-start.3 = (bf16[128,128]{1,0:T(8,128)(2,1)}, bf16[128,128]{1,0:T(8,128)(2,1)S(1)}, u32[]{:S(2)}, u32[]{:S(2)}) collective-permute-start(bf16[128,128]{1,0:T(8,128)(2,1)} %convert_element_type.20), channel_id=1, source_target_pairs={{0,24},{4,28},{8,0},{12,4},{16,8},{20,12},{24,16},{28,20},{1,25},{... | collective-permute-start | bytes 98312 | tf_op jit(solution)/shard_map/ppermute | solution.py:279
  28.4 0.0 copy-done.8
  28.4 6.2 %local_parts.1 = (f32[256,1024]{1,0:T(8,128)S(1)}, f32[256,1024]{1,0:T(8,128)S(1)}, f32[8,128]{1,0:T(8,128)S(1)}) custom-call(bf16[256,1024]{1,0:T(8,128)(2,1)S(1)} %copy-done, bf16[256,1024]{1,0:T(8,128)(2,1)S(1)} %copy-done.1, bf16[256,1024]{1,0:T(8,128)(2,1)S(1)} %copy-done.2, bf16[256,1024]{1,0:T(8,128)(2,1)S(1)} %copy-done.3, ...), custom_call_target="tpu_custom_call" | custom-call | tf_op jit(solution)/shard_map/local_parts/pallas_call | solution.py:267
  34.6 0.0 copy-start.4
  34.6 1.0 %copy-done.4 = f32[256,1024]{1,0:T(8,128)} copy-done((f32[256,1024]{1,0:T(8,128)}, f32[256,1024]{1,0:T(8,128)S(1)}, u32[]{:S(2)}) %copy-start.4) | copy-done | bytes 1048600
  35.6 0.0 copy-start.6
  35.6 1.0 %copy-done.6 = f32[256,1024]{1,0:T(8,128)} copy-done((f32[256,1024]{1,0:T(8,128)}, f32[256,1024]{1,0:T(8,128)S(1)}, u32[]{:S(2)}) %copy-start.6) | copy-done | bytes 1048600
  36.6 2.5 %all-to-all-done.refs_1_ = bf16[32,64,256]{2,1,0:T(8,128)(2,1)S(1)} async-done(((bf16[32,64,256]{2,1,0:T(8,128)(2,1)}), bf16[32,64,256]{2,1,0:T(8,128)(2,1)S(1)}, u32[]{:S(2)}, u32[]{:S(2)}) %all-to-all-start) | async-done | bytes 1048608 | tf_op jit(solution)/shard_map/all_to_all | solution.py:511
  39.1 3.5 %filter_lags.1 = bf16[8,16,128]{2,1,0:T(8,128)(2,1)} custom-call(f32[8,128]{1,0:T(8,128)S(1)} %get-tuple-element.46.refs_0_, bf16[32,64,256]{2,1,0:T(8,128)(2,1)S(1)} %all-to-all-done.refs_1_), custom_call_target="tpu_custom_call" | custom-call | tf_op jit(solution)/shard_map/filter_lags/pallas_call | solution.py:482
  42.6 0.0 copy-start.7
  42.6 0.0 collective-permute-done.1.refs_0_
  42.6 0.0 collective-permute-done.2.refs_1_
  42.6 0.0 collective-permute-done.3.refs_2_
  42.6 3.5 %all-to-all-start.1 = ((bf16[8,16,128]{2,1,0:T(8,128)(2,1)}), bf16[8,16,128]{2,1,0:T(8,128)(2,1)S(1)}, u32[]{:S(2)}, u32[]{:S(2)}) async-start(bf16[8,16,128]{2,1,0:T(8,128)(2,1)} %filter_lags.1), calls=%async_computation.1 | async-start | bytes 65536 | tf_op jit(solution)/shard_map/all_to_all | solution.py:535
  46.1 1.3 %edge_terms.1.edge_ref = f32[2112,128]{1,0:T(8,128)S(1)} custom-call(s32[1]{0:T(128)} %bitcast.seq_ref, f32[3,16,8,128]{3,2,1,0:T(8,128)S(1)} %bitcast.22, bf16[2,128,128]{2,1,0:T(8,128)(2,1)S(1)} %collective-permute-done.near_ref, bf16[128,128]{1,0:T(8,128)(2,1)S(1)} %collective-permute-done.1.refs_0_, bf16[128,128]{1,0:T(8,128)(2,1)S(1)} %collective-permute-done.2.refs_1_, ...), custom_call_target="tpu_custom_call" | custom-call | tf_op jit(solution)/shard_map/edge_terms/pallas_call | solution.py:314
  47.3 0.0 copy-done.7
  47.3 0.0 copy-start.5
  47.4 1.6 %conv_outputs.1 = (bf16[256,1024]{1,0:T(8,128)(2,1)}, f32[2112,128]{1,0:T(8,128)S(1)}) custom-call(s32[1]{0:T(128)} %bitcast.seq_ref, f32[256,1024]{1,0:T(8,128)S(1)} %copy-done.7, f32[2112,128]{1,0:T(8,128)S(1)} %edge_terms.1.edge_ref, bf16[256,1024]{1,0:T(8,128)(2,1)S(1)} %copy-done, f32[3,16,8,128]{3,2,1,0:T(8,128)S(1)} %bitcast.23, ...), custom_call_target="tpu_custom_call" | custom-call | tf_op jit(solution)/shard_map/conv_outputs/pallas_call | solution.py:350
  49.0 0.0 copy-done.5
  49.0 1.2 %grad_outputs.1 = (bf16[256,1024]{1,0:T(8,128)(2,1)}, bf16[256,1024]{1,0:T(8,128)(2,1)}) custom-call(f32[256,1024]{1,0:T(8,128)S(1)} %copy-done.5, f32[2112,128]{1,0:T(8,128)S(1)} %get-tuple-element.56.edge_ref, bf16[256,1024]{1,0:T(8,128)(2,1)S(1)} %copy-done.2, bf16[256,1024]{1,0:T(8,128)(2,1)S(1)} %copy-done.1), custom_call_target="tpu_custom_call" | custom-call | tf_op jit(solution)/shard_map/grad_outputs/pallas_call | solution.py:379
  50.2 2.5 %all-to-all-done.1 = bf16[8,16,128]{2,1,0:T(8,128)(2,1)S(1)} async-done(((bf16[8,16,128]{2,1,0:T(8,128)(2,1)}), bf16[8,16,128]{2,1,0:T(8,128)(2,1)S(1)}, u32[]{:S(2)}, u32[]{:S(2)}) %all-to-all-start.1) | async-done | bytes 32800 | tf_op jit(solution)/shard_map/all_to_all | solution.py:535
  52.7 0.6 %multiply_bitcast_fusion = f32[256,64]{0,1:T(8,128)} fusion(bf16[8,16,128]{2,1,0:T(8,128)(2,1)S(1)} %all-to-all-done.1), kind=kLoop, calls=%fused_computation | loop fusion | flops 32768 | bytes 98304 | tf_op jit(solution)/shard_map/mul | solution.py:537
  (4 shorter events, 0.1 us)
Async XLA Ops:
  0.6 10.4 %copy-start.9 = (f32[256,16]{0,1:T(8,128)S(1)}, f32[256,16]{0,1:T(8,128)}, u32[]{:S(2)}) copy-start(f32[256,16]{0,1:T(8,128)} %param.12) | copy-start | bytes 49156
  0.6 10.4 %copy-start.10 = (f32[256,16]{0,1:T(8,128)S(1)}, f32[256,16]{0,1:T(8,128)}, u32[]{:S(2)}) copy-start(f32[256,16]{0,1:T(8,128)} %param.11) | copy-start | bytes 49156
  3.6 7.5 %copy-start = (bf16[256,1024]{1,0:T(8,128)(2,1)S(1)}, bf16[256,1024]{1,0:T(8,128)(2,1)}, u32[]{:S(2)}) copy-start(bf16[256,1024]{1,0:T(8,128)(2,1)} %q_ref.2) | copy-start | bytes 1572868
  3.6 7.5 %copy-start.1 = (bf16[256,1024]{1,0:T(8,128)(2,1)S(1)}, bf16[256,1024]{1,0:T(8,128)(2,1)}, u32[]{:S(2)}) copy-start(bf16[256,1024]{1,0:T(8,128)(2,1)} %k_ref.2) | copy-start | bytes 1572868
  3.7 7.5 %copy-start.2 = (bf16[256,1024]{1,0:T(8,128)(2,1)S(1)}, bf16[256,1024]{1,0:T(8,128)(2,1)}, u32[]{:S(2)}) copy-start(bf16[256,1024]{1,0:T(8,128)(2,1)} %v_ref.2) | copy-start | bytes 1572868
  3.7 7.5 %copy-start.3 = (bf16[256,1024]{1,0:T(8,128)(2,1)S(1)}, bf16[256,1024]{1,0:T(8,128)(2,1)}, u32[]{:S(2)}) copy-start(bf16[256,1024]{1,0:T(8,128)(2,1)} %o_ref.1) | copy-start | bytes 1572868
  3.7 35.4 %all-to-all-start = ((bf16[32,64,256]{2,1,0:T(8,128)(2,1)}), bf16[32,64,256]{2,1,0:T(8,128)(2,1)S(1)}, u32[]{:S(2)}, u32[]{:S(2)}) async-start(bf16[32,64,256]{2,1,0:T(8,128)(2,1)} %pack_signals.1), calls=%async_computation | async-start | bytes 2097152 | tf_op jit(solution)/shard_map/all_to_all | solution.py:511
  11.2 17.2 %copy-start.8 = (f32[1024]{0:T(1024)S(1)}, f32[1024]{0:T(1024)}, u32[]{:S(2)}) copy-start(f32[1024]{0:T(1024)} %param.13) | copy-start | bytes 12292
  14.8 6.2 %collective-permute-start = (bf16[2,128,128]{2,1,0:T(8,128)(2,1)}, bf16[2,128,128]{2,1,0:T(8,128)(2,1)S(1)}, u32[]{:S(2)}, u32[]{:S(2)}) collective-permute-start(bf16[2,128,128]{2,1,0:T(8,128)(2,1)} %get-tuple-element.39), channel_id=1, source_target_pairs={{0,4},{4,0},{8,12},{12,8},{16,20},{20,16},{24,28},{28,24},{1,5},{5... | collective-permute-start | bytes 196616 | tf_op jit(solution)/shard_map/ppermute | solution.py:283
  22.9 19.7 %collective-permute-start.1 = (bf16[128,128]{1,0:T(8,128)(2,1)}, bf16[128,128]{1,0:T(8,128)(2,1)S(1)}, u32[]{:S(2)}, u32[]{:S(2)}) collective-permute-start(bf16[128,128]{1,0:T(8,128)(2,1)} %convert_element_type.18), channel_id=1, source_target_pairs={{0,8},{4,12},{8,16},{12,20},{16,24},{20,28},{24,0},{28,4},{1,9},{5... | collective-permute-start | bytes 98312 | tf_op jit(solution)/shard_map/ppermute | solution.py:279
  24.8 17.8 %collective-permute-start.2 = (bf16[128,128]{1,0:T(8,128)(2,1)}, bf16[128,128]{1,0:T(8,128)(2,1)S(1)}, u32[]{:S(2)}, u32[]{:S(2)}) collective-permute-start(bf16[128,128]{1,0:T(8,128)(2,1)} %convert_element_type.19), channel_id=1, source_target_pairs={{0,16},{4,20},{8,24},{12,28},{16,0},{20,4},{24,8},{28,12},{1,17},{... | collective-permute-start | bytes 98312 | tf_op jit(solution)/shard_map/ppermute | solution.py:279
  26.8 15.7 %collective-permute-start.3 = (bf16[128,128]{1,0:T(8,128)(2,1)}, bf16[128,128]{1,0:T(8,128)(2,1)S(1)}, u32[]{:S(2)}, u32[]{:S(2)}) collective-permute-start(bf16[128,128]{1,0:T(8,128)(2,1)} %convert_element_type.20), channel_id=1, source_target_pairs={{0,24},{4,28},{8,0},{12,4},{16,8},{20,12},{24,16},{28,20},{1,25},{... | collective-permute-start | bytes 98312 | tf_op jit(solution)/shard_map/ppermute | solution.py:279
  34.6 1.0 %copy-start.4 = (f32[256,1024]{1,0:T(8,128)}, f32[256,1024]{1,0:T(8,128)S(1)}, u32[]{:S(2)}) copy-start(f32[256,1024]{1,0:T(8,128)S(1)} %get-tuple-element.55.part_ref) | copy-start | bytes 3145732
  35.6 1.0 %copy-start.6 = (f32[256,1024]{1,0:T(8,128)}, f32[256,1024]{1,0:T(8,128)S(1)}, u32[]{:S(2)}) copy-start(f32[256,1024]{1,0:T(8,128)S(1)} %get-tuple-element.44.part_ref) | copy-start | bytes 3145732
  42.6 4.8 %copy-start.7 = (f32[256,1024]{1,0:T(8,128)S(1)}, f32[256,1024]{1,0:T(8,128)}, u32[]{:S(2)}) copy-start(f32[256,1024]{1,0:T(8,128)} %copy-done.6) | copy-start | bytes 3145732
  42.6 10.1 %all-to-all-start.1 = ((bf16[8,16,128]{2,1,0:T(8,128)(2,1)}), bf16[8,16,128]{2,1,0:T(8,128)(2,1)S(1)}, u32[]{:S(2)}, u32[]{:S(2)}) async-start(bf16[8,16,128]{2,1,0:T(8,128)(2,1)} %filter_lags.1), calls=%async_computation.1 | async-start | bytes 65536 | tf_op jit(solution)/shard_map/all_to_all | solution.py:535
  47.3 1.7 %copy-start.5 = (f32[256,1024]{1,0:T(8,128)S(1)}, f32[256,1024]{1,0:T(8,128)}, u32[]{:S(2)}) copy-start(f32[256,1024]{1,0:T(8,128)} %copy-done.4) | copy-start | bytes 3145732

commit v23 on v22

--- a/solution.py
+++ b/solution.py
@@ -198,28 +198,30 @@
     modes, tiles = coef_ref.shape[1:3]
     pair = seq_ref[0] // 2
     second = seq_ref[0] % 2 == 1
+    ahead, behind = [], []
     for m in range(modes):
         rows = slice(m * tiles, (m + 1) * tiles)
         decay = coef_ref[1, m]
         own, near = own_ref[0, rows], near_ref[0].astype(F32)[rows]
-        ahead = jnp.where(second, own + decay * near, near + decay * own)
+        ahead.append(jnp.where(second, own + decay * near, near + decay * own))
         own, near = own_ref[1, rows], near_ref[1].astype(F32)[rows]
-        behind = jnp.where(second, near + decay * own, own + decay * near)
-        for k in range(1, pairs):
-            state_refs[k - 1][rows] = jnp.where(pair + k < pairs, ahead, behind)
+        behind.append(jnp.where(second, near + decay * own, own + decay * near))
+    ahead = jnp.concatenate(ahead, axis=0)
+    behind = jnp.concatenate(behind, axis=0)
+    for k in range(1, pairs):
+        state_refs[k - 1][...] = jnp.where(pair + k < pairs, ahead, behind).astype(LINK)
 
 
 def pair_states(seq_index, pairs, coefs, own, near):
     whole = pl.BlockSpec(memory_space=pltpu.VMEM)
-    states = pl.pallas_call(
+    return pl.pallas_call(
         pair_kernel,
         in_specs=[pl.BlockSpec(memory_space=pltpu.SMEM)] + [whole] * 3,
         out_specs=[whole] * (pairs - 1),
-        out_shape=[jax.ShapeDtypeStruct(own.shape[1:], F32)] * (pairs - 1),
+        out_shape=[jax.ShapeDtypeStruct(own.shape[1:], LINK)] * (pairs - 1),
         compiler_params=pltpu.CompilerParams(vmem_limit_bytes=VMEM_BYTES),
         name="pair_states",
     )(seq_index, coefs, own, near)
-    return [state.astype(LINK) for state in states]
 
 
 def sum_pairs(side, seq, coef_ref, near_ref, state_refs):
@@ -523,11 +525,11 @@
     seq_index = lax.axis_index("seq").reshape(1)
     pairs = shards // 2
     own, sent = block_states(*signals, coefs)
+    conv_part, grad_part, done = local_parts(*signals, coefs, skip_gain[None, :])
+    sent, done = lax.optimization_barrier((sent, done))
     near = inside_pair(sent, pairs)
     states = pair_states(seq_index, pairs, coefs, own, near)
-    *states, coefs, near = lax.optimization_barrier((*states, coefs, near))
     states = [along_column(state, pairs, 1 + i) for i, state in enumerate(states)]
-    conv_part, grad_part, done = local_parts(*signals, coefs, skip_gain[None, :])
 
     scale = 1.0 / math.sqrt(length * (CHANNELS // FILTERS))
     lags = filter_lags(received, done, shards, chans, owned)

time: 53.6 us -> 53.5 us (level)
  other arithmetic: 2.52 us -> 0.66 us
  waiting for transfers between devices: 9.47 us -> 11.3 us
  Pallas kernels: 20.3 us -> 20.9 us
    all_to_all x1, waiting for transfers between devices: 2.51 us -> 5.2 us  [per_device(): lax.all_to_all(send, ('seq', 'chan'), split_axis=0, concat_axis=0, tiled=...]
    convert_element_type x3 -> x0, other arithmetic: 1.86 us -> none  [pair_states(): return [state.astype(LINK) for state in states]]
    ppermute x1, waiting for transfers between devices: 4.46 us -> 3.57 us  [inside_pair(): return lax.ppermute(state, 'seq', [(i, i ^ 1) for i in range(2 * pairs)])]
    pallas_call x1, Pallas kernels: 0.04 us -> 0.67 us  [pair_states(): pl.pallas_call(pair_kernel, in_specs=[pl.BlockSpec(memory_space=pltpu.SME...]
    ppermute x3, starting transfers between devices: 5.49 us -> 4.93 us  [along_column(): return lax.ppermute(state, 'seq', route)]
  transfers between devices with their start and end apart: 6 -> 6, of which waited for: 3 -> 3; matrix products, arithmetic and copies ran while one was open for 4% -> 0% of each run, Pallas kernels for 33% -> 34%
where the time goes in v23:
time: 53.5 us; the launch traced here: 53.3 us
  Pallas kernels  20.9 us (39%)
  starting transfers between devices  17.5 us (33%)
  waiting for transfers between devices  11.3 us (21%)
  local copies, waits for them, and re-layouts  2.08 us (4%)
  between operations  0.87 us (2%)
  other arithmetic  0.66 us (1%)
    all_to_all x1, starting transfers between devices, per_device(): lax.all_to_all(send, ('seq', 'chan'), split_axis=0, concat_axis=0, tiled=...  7.31 us
    pallas_call x1, Pallas kernels, local_parts(): pl.pallas_call(local_kernel, out_shape=[jax.ShapeDtypeStruct((tok_rows, w...  6.22 us
    all_to_all x1, waiting for transfers between devices, per_device(): lax.all_to_all(send, ('seq', 'chan'), split_axis=0, concat_axis=0, tiled=...  5.2 us
    ppermute x3, starting transfers between devices, along_column(): return lax.ppermute(state, 'seq', route)  4.93 us
    pallas_call x1, Pallas kernels, block_states(): pl.pallas_call(state_kernel, out_shape=[jax.ShapeDtypeStruct((2, modes *...  3.57 us
    ppermute x1, waiting for transfers between devices, inside_pair(): return lax.ppermute(state, 'seq', [(i, i ^ 1) for i in range(2 * pairs)])  3.57 us
    all_to_all x1, starting transfers between devices, per_device(): lags = lax.all_to_all(lags, 'seq', split_axis=0, concat_axis=0, tiled=True)  3.48 us
    pallas_call x1, Pallas kernels, filter_lags(): pl.pallas_call(functools.partial(lag_kernel, shards, chans, groups, owned...  3.45 us
  transfers between devices with their start and end apart: 6, of which 3 were waited for; matrix products, arithmetic and copies ran while one was open for 0% of the time, Pallas kernels for 34%

profile of v23, /device:TPU:0, one launch (start us, length us, event | category | flops | bytes accessed | tf_op | source)
XLA Modules:
  0.0 53.3 jit_solution(8690658932762354277)
XLA Ops:
  0.6 0.0 copy-start.9
  0.6 0.0 copy-start.10
  0.7 2.9 %pack_signals.1 = bf16[32,64,256]{2,1,0:T(8,128)(2,1)} custom-call(bf16[256,1024]{1,0:T(8,128)(2,1)} %k_ref.2, bf16[256,1024]{1,0:T(8,128)(2,1)} %v_ref.2, bf16[256,1024]{1,0:T(8,128)(2,1)} %o_ref.1, bf16[256,1024]{1,0:T(8,128)(2,1)} %q_ref.2), custom_call_target="tpu_custom_call" | custom-call | tf_op jit(solution)/shard_map/pack_signals/pallas_call | solution.py:97
  3.6 0.0 copy-start
  3.6 0.0 copy-start.1
  3.6 0.0 copy-start.2
  3.6 0.0 copy-start.3
  3.6 7.3 %all-to-all-start = ((bf16[32,64,256]{2,1,0:T(8,128)(2,1)}), bf16[32,64,256]{2,1,0:T(8,128)(2,1)S(1)}, u32[]{:S(2)}, u32[]{:S(2)}) async-start(bf16[32,64,256]{2,1,0:T(8,128)(2,1)} %pack_signals.1), calls=%async_computation | async-start | bytes 2097152 | tf_op jit(solution)/shard_map/all_to_all | solution.py:513
  11.0 0.0 copy-done.9
  11.0 0.0 copy-done.10
  11.1 0.1 broadcast_in_dim.11
  11.1 0.0 copy-done
  11.1 0.0 copy-done.1
  11.1 0.0 copy-done.2
  11.1 0.0 copy-done.3
  11.2 0.0 copy-start.8
  11.2 3.6 %block_states.1 = (f32[2,128,128]{2,1,0:T(8,128)S(1)}, bf16[2,128,128]{2,1,0:T(8,128)(2,1)}) custom-call(bf16[256,1024]{1,0:T(8,128)(2,1)S(1)} %copy-done, bf16[256,1024]{1,0:T(8,128)(2,1)S(1)} %copy-done.1, bf16[256,1024]{1,0:T(8,128)(2,1)S(1)} %copy-done.2, bf16[256,1024]{1,0:T(8,128)(2,1)S(1)} %copy-done.3, f32[3,16,8,128]{3,2,1,0:T(8,128)S(1)} %bitcast.19), custom_call_target="tpu_custom_call" | custom-call | tf_op jit(solution)/shard_map/block_states/pallas_call | solution.py:184
  14.7 0.0 copy-done.8
  14.7 6.2 %local_parts.1 = (f32[256,1024]{1,0:T(8,128)S(1)}, f32[256,1024]{1,0:T(8,128)S(1)}, f32[8,128]{1,0:T(8,128)S(1)}) custom-call(bf16[256,1024]{1,0:T(8,128)(2,1)S(1)} %copy-done, bf16[256,1024]{1,0:T(8,128)(2,1)S(1)} %copy-done.1, bf16[256,1024]{1,0:T(8,128)(2,1)S(1)} %copy-done.2, bf16[256,1024]{1,0:T(8,128)(2,1)S(1)} %copy-done.3, ...), custom_call_target="tpu_custom_call" | custom-call | tf_op jit(solution)/shard_map/local_parts/pallas_call | solution.py:269
  21.0 0.0 copy-start.4
  21.0 1.0 %copy-done.4 = f32[256,1024]{1,0:T(8,128)} copy-done((f32[256,1024]{1,0:T(8,128)}, f32[256,1024]{1,0:T(8,128)S(1)}, u32[]{:S(2)}) %copy-start.4) | copy-done | bytes 1048600
  22.0 0.0 copy-start.6
  22.0 1.0 %copy-done.6 = f32[256,1024]{1,0:T(8,128)} copy-done((f32[256,1024]{1,0:T(8,128)}, f32[256,1024]{1,0:T(8,128)S(1)}, u32[]{:S(2)}) %copy-start.6) | copy-done | bytes 1048600
  22.9 1.8 %collective-permute-start = (bf16[2,128,128]{2,1,0:T(8,128)(2,1)}, bf16[2,128,128]{2,1,0:T(8,128)(2,1)S(1)}, u32[]{:S(2)}, u32[]{:S(2)}) collective-permute-start(bf16[2,128,128]{2,1,0:T(8,128)(2,1)} %get-tuple-element.38), channel_id=1, source_target_pairs={{0,4},{4,0},{8,12},{12,8},{16,20},{20,16},{24,28},{28,24},{1,5},{5... | collective-permute-start | bytes 196616 | tf_op jit(solution)/shard_map/ppermute | solution.py:285
  24.7 3.6 %collective-permute-done.near_ref = bf16[2,128,128]{2,1,0:T(8,128)(2,1)S(1)} collective-permute-done((bf16[2,128,128]{2,1,0:T(8,128)(2,1)}, bf16[2,128,128]{2,1,0:T(8,128)(2,1)S(1)}, u32[]{:S(2)}, u32[]{:S(2)}) %collective-permute-start) | collective-permute-done | bytes 65568 | tf_op jit(solution)/shard_map/ppermute | solution.py:285
  28.3 0.7 %pair_states.1 = (bf16[128,128]{1,0:T(8,128)(2,1)}, bf16[128,128]{1,0:T(8,128)(2,1)}, bf16[128,128]{1,0:T(8,128)(2,1)}) custom-call(s32[1]{0:T(128)} %bitcast.seq_ref, f32[3,16,8,128]{3,2,1,0:T(8,128)S(1)} %bitcast.21, f32[2,128,128]{2,1,0:T(8,128)S(1)} %get-tuple-element.41.own_ref, bf16[2,128,128]{2,1,0:T(8,128)(2,1)S(1)} %collective-permute-done.near_ref), custom_call_target="tpu_custom_call" | custom-call | tf_op jit(solution)/shard_map/pair_states/pallas_call | solution.py:217
  28.9 1.9 %collective-permute-start.1 = (bf16[128,128]{1,0:T(8,128)(2,1)}, bf16[128,128]{1,0:T(8,128)(2,1)S(1)}, u32[]{:S(2)}, u32[]{:S(2)}) collective-permute-start(bf16[128,128]{1,0:T(8,128)(2,1)} %get-tuple-element.42), channel_id=1, source_target_pairs={{0,8},{4,12},{8,16},{12,20},{16,24},{20,28},{24,0},{28,4},{1,9},{5... | collective-permute-start | bytes 98312 | tf_op jit(solution)/shard_map/ppermute | solution.py:281
  30.8 2.3 %collective-permute-start.2 = (bf16[128,128]{1,0:T(8,128)(2,1)}, bf16[128,128]{1,0:T(8,128)(2,1)S(1)}, u32[]{:S(2)}, u32[]{:S(2)}) collective-permute-start(bf16[128,128]{1,0:T(8,128)(2,1)} %get-tuple-element.43), channel_id=1, source_target_pairs={{0,16},{4,20},{8,24},{12,28},{16,0},{20,4},{24,8},{28,12},{1,17},{... | collective-permute-start | bytes 98312 | tf_op jit(solution)/shard_map/ppermute | solution.py:281
  33.1 0.7 %collective-permute-start.3 = (bf16[128,128]{1,0:T(8,128)(2,1)}, bf16[128,128]{1,0:T(8,128)(2,1)S(1)}, u32[]{:S(2)}, u32[]{:S(2)}) collective-permute-start(bf16[128,128]{1,0:T(8,128)(2,1)} %get-tuple-element.44), channel_id=1, source_target_pairs={{0,24},{4,28},{8,0},{12,4},{16,8},{20,12},{24,16},{28,20},{1,25},{... | collective-permute-start | bytes 98312 | tf_op jit(solution)/shard_map/ppermute | solution.py:281
  33.9 5.2 %all-to-all-done.refs_1_ = bf16[32,64,256]{2,1,0:T(8,128)(2,1)S(1)} async-done(((bf16[32,64,256]{2,1,0:T(8,128)(2,1)}), bf16[32,64,256]{2,1,0:T(8,128)(2,1)S(1)}, u32[]{:S(2)}, u32[]{:S(2)}) %all-to-all-start) | async-done | bytes 1048608 | tf_op jit(solution)/shard_map/all_to_all | solution.py:513
  39.1 3.4 %filter_lags.1 = bf16[8,16,128]{2,1,0:T(8,128)(2,1)} custom-call(f32[8,128]{1,0:T(8,128)S(1)} %get-tuple-element.39.refs_0_, bf16[32,64,256]{2,1,0:T(8,128)(2,1)S(1)} %all-to-all-done.refs_1_), custom_call_target="tpu_custom_call" | custom-call | tf_op jit(solution)/shard_map/filter_lags/pallas_call | solution.py:484
  42.5 0.0 copy-start.7
  42.5 0.0 collective-permute-done.1.refs_0_
  42.5 0.0 collective-permute-done.2.refs_1_
  42.5 0.0 collective-permute-done.3.refs_2_
  42.5 3.5 %all-to-all-start.1 = ((bf16[8,16,128]{2,1,0:T(8,128)(2,1)}), bf16[8,16,128]{2,1,0:T(8,128)(2,1)S(1)}, u32[]{:S(2)}, u32[]{:S(2)}) async-start(bf16[8,16,128]{2,1,0:T(8,128)(2,1)} %filter_lags.1), calls=%async_computation.1 | async-start | bytes 65536 | tf_op jit(solution)/shard_map/all_to_all | solution.py:537
  46.0 1.3 %edge_terms.1.edge_ref = f32[2112,128]{1,0:T(8,128)S(1)} custom-call(s32[1]{0:T(128)} %bitcast.seq_ref, f32[3,16,8,128]{3,2,1,0:T(8,128)S(1)} %bitcast.22, bf16[2,128,128]{2,1,0:T(8,128)(2,1)S(1)} %collective-permute-done.near_ref, bf16[128,128]{1,0:T(8,128)(2,1)S(1)} %collective-permute-done.1.refs_0_, bf16[128,128]{1,0:T(8,128)(2,1)S(1)} %collective-permute-done.2.refs_1_, ...), custom_call_target="tpu_custom_call" | custom-call | tf_op jit(solution)/shard_map/edge_terms/pallas_call | solution.py:316
  47.3 0.0 copy-done.7
  47.3 0.0 copy-start.5
  47.3 1.6 %conv_outputs.1 = (bf16[256,1024]{1,0:T(8,128)(2,1)}, f32[2112,128]{1,0:T(8,128)S(1)}) custom-call(s32[1]{0:T(128)} %bitcast.seq_ref, f32[256,1024]{1,0:T(8,128)S(1)} %copy-done.7, f32[2112,128]{1,0:T(8,128)S(1)} %edge_terms.1.edge_ref, bf16[256,1024]{1,0:T(8,128)(2,1)S(1)} %copy-done, f32[3,16,8,128]{3,2,1,0:T(8,128)S(1)} %bitcast.23, ...), custom_call_target="tpu_custom_call" | custom-call | tf_op jit(solution)/shard_map/conv_outputs/pallas_call | solution.py:352
  49.0 0.0 copy-done.5
  49.0 1.2 %grad_outputs.1 = (bf16[256,1024]{1,0:T(8,128)(2,1)}, bf16[256,1024]{1,0:T(8,128)(2,1)}) custom-call(f32[256,1024]{1,0:T(8,128)S(1)} %copy-done.5, f32[2112,128]{1,0:T(8,128)S(1)} %get-tuple-element.50.edge_ref, bf16[256,1024]{1,0:T(8,128)(2,1)S(1)} %copy-done.2, bf16[256,1024]{1,0:T(8,128)(2,1)S(1)} %copy-done.1), custom_call_target="tpu_custom_call" | custom-call | tf_op jit(solution)/shard_map/grad_outputs/pallas_call | solution.py:381
  50.2 2.5 %all-to-all-done.1 = bf16[8,16,128]{2,1,0:T(8,128)(2,1)S(1)} async-done(((bf16[8,16,128]{2,1,0:T(8,128)(2,1)}), bf16[8,16,128]{2,1,0:T(8,128)(2,1)S(1)}, u32[]{:S(2)}, u32[]{:S(2)}) %all-to-all-start.1) | async-done | bytes 32800 | tf_op jit(solution)/shard_map/all_to_all | solution.py:537
  52.7 0.6 %multiply_bitcast_fusion = f32[256,64]{0,1:T(8,128)} fusion(bf16[8,16,128]{2,1,0:T(8,128)(2,1)S(1)} %all-to-all-done.1), kind=kLoop, calls=%fused_computation | loop fusion | flops 32768 | bytes 98304 | tf_op jit(solution)/shard_map/mul | solution.py:539
  (3 shorter events, 0.1 us)
Async XLA Ops:
  0.6 10.3 %copy-start.9 = (f32[256,16]{0,1:T(8,128)S(1)}, f32[256,16]{0,1:T(8,128)}, u32[]{:S(2)}) copy-start(f32[256,16]{0,1:T(8,128)} %param.12) | copy-start | bytes 49156
  0.6 10.3 %copy-start.10 = (f32[256,16]{0,1:T(8,128)S(1)}, f32[256,16]{0,1:T(8,128)}, u32[]{:S(2)}) copy-start(f32[256,16]{0,1:T(8,128)} %param.11) | copy-start | bytes 49156
  3.6 7.5 %copy-start = (bf16[256,1024]{1,0:T(8,128)(2,1)S(1)}, bf16[256,1024]{1,0:T(8,128)(2,1)}, u32[]{:S(2)}) copy-start(bf16[256,1024]{1,0:T(8,128)(2,1)} %q_ref.2) | copy-start | bytes 1572868
  3.6 7.5 %copy-start.1 = (bf16[256,1024]{1,0:T(8,128)(2,1)S(1)}, bf16[256,1024]{1,0:T(8,128)(2,1)}, u32[]{:S(2)}) copy-start(bf16[256,1024]{1,0:T(8,128)(2,1)} %k_ref.2) | copy-start | bytes 1572868
  3.6 7.5 %copy-start.2 = (bf16[256,1024]{1,0:T(8,128)(2,1)S(1)}, bf16[256,1024]{1,0:T(8,128)(2,1)}, u32[]{:S(2)}) copy-start(bf16[256,1024]{1,0:T(8,128)(2,1)} %v_ref.2) | copy-start | bytes 1572868
  3.6 7.5 %copy-start.3 = (bf16[256,1024]{1,0:T(8,128)(2,1)S(1)}, bf16[256,1024]{1,0:T(8,128)(2,1)}, u32[]{:S(2)}) copy-start(bf16[256,1024]{1,0:T(8,128)(2,1)} %o_ref.1) | copy-start | bytes 1572868
  3.6 35.4 %all-to-all-start = ((bf16[32,64,256]{2,1,0:T(8,128)(2,1)}), bf16[32,64,256]{2,1,0:T(8,128)(2,1)S(1)}, u32[]{:S(2)}, u32[]{:S(2)}) async-start(bf16[32,64,256]{2,1,0:T(8,128)(2,1)} %pack_signals.1), calls=%async_computation | async-start | bytes 2097152 | tf_op jit(solution)/shard_map/all_to_all | solution.py:513
  11.2 3.6 %copy-start.8 = (f32[1024]{0:T(1024)S(1)}, f32[1024]{0:T(1024)}, u32[]{:S(2)}) copy-start(f32[1024]{0:T(1024)} %param.13) | copy-start | bytes 12292
  21.0 1.0 %copy-start.4 = (f32[256,1024]{1,0:T(8,128)}, f32[256,1024]{1,0:T(8,128)S(1)}, u32[]{:S(2)}) copy-start(f32[256,1024]{1,0:T(8,128)S(1)} %get-tuple-element.49.part_ref) | copy-start | bytes 3145732
  22.0 1.0 %copy-start.6 = (f32[256,1024]{1,0:T(8,128)}, f32[256,1024]{1,0:T(8,128)S(1)}, u32[]{:S(2)}) copy-start(f32[256,1024]{1,0:T(8,128)S(1)} %get-tuple-element.35.part_ref) | copy-start | bytes 3145732
  22.9 5.3 %collective-permute-start = (bf16[2,128,128]{2,1,0:T(8,128)(2,1)}, bf16[2,128,128]{2,1,0:T(8,128)(2,1)S(1)}, u32[]{:S(2)}, u32[]{:S(2)}) collective-permute-start(bf16[2,128,128]{2,1,0:T(8,128)(2,1)} %get-tuple-element.38), channel_id=1, source_target_pairs={{0,4},{4,0},{8,12},{12,8},{16,20},{20,16},{24,28},{28,24},{1,5},{5... | collective-permute-start | bytes 196616 | tf_op jit(solution)/shard_map/ppermute | solution.py:285
  28.9 13.6 %collective-permute-start.1 = (bf16[128,128]{1,0:T(8,128)(2,1)}, bf16[128,128]{1,0:T(8,128)(2,1)S(1)}, u32[]{:S(2)}, u32[]{:S(2)}) collective-permute-start(bf16[128,128]{1,0:T(8,128)(2,1)} %get-tuple-element.42), channel_id=1, source_target_pairs={{0,8},{4,12},{8,16},{12,20},{16,24},{20,28},{24,0},{28,4},{1,9},{5... | collective-permute-start | bytes 98312 | tf_op jit(solution)/shard_map/ppermute | solution.py:281
  30.8 11.7 %collective-permute-start.2 = (bf16[128,128]{1,0:T(8,128)(2,1)}, bf16[128,128]{1,0:T(8,128)(2,1)S(1)}, u32[]{:S(2)}, u32[]{:S(2)}) collective-permute-start(bf16[128,128]{1,0:T(8,128)(2,1)} %get-tuple-element.43), channel_id=1, source_target_pairs={{0,16},{4,20},{8,24},{12,28},{16,0},{20,4},{24,8},{28,12},{1,17},{... | collective-permute-start | bytes 98312 | tf_op jit(solution)/shard_map/ppermute | solution.py:281
  33.1 9.4 %collective-permute-start.3 = (bf16[128,128]{1,0:T(8,128)(2,1)}, bf16[128,128]{1,0:T(8,128)(2,1)S(1)}, u32[]{:S(2)}, u32[]{:S(2)}) collective-permute-start(bf16[128,128]{1,0:T(8,128)(2,1)} %get-tuple-element.44), channel_id=1, source_target_pairs={{0,24},{4,28},{8,0},{12,4},{16,8},{20,12},{24,16},{28,20},{1,25},{... | collective-permute-start | bytes 98312 | tf_op jit(solution)/shard_map/ppermute | solution.py:281
  42.5 4.8 %copy-start.7 = (f32[256,1024]{1,0:T(8,128)S(1)}, f32[256,1024]{1,0:T(8,128)}, u32[]{:S(2)}) copy-start(f32[256,1024]{1,0:T(8,128)} %copy-done.6) | copy-start | bytes 3145732
  42.5 10.1 %all-to-all-start.1 = ((bf16[8,16,128]{2,1,0:T(8,128)(2,1)}), bf16[8,16,128]{2,1,0:T(8,128)(2,1)S(1)}, u32[]{:S(2)}, u32[]{:S(2)}) async-start(bf16[8,16,128]{2,1,0:T(8,128)(2,1)} %filter_lags.1), calls=%async_computation.1 | async-start | bytes 65536 | tf_op jit(solution)/shard_map/all_to_all | solution.py:537
  47.3 1.7 %copy-start.5 = (f32[256,1024]{1,0:T(8,128)S(1)}, f32[256,1024]{1,0:T(8,128)}, u32[]{:S(2)}) copy-start(f32[256,1024]{1,0:T(8,128)} %copy-done.4) | copy-start | bytes 3145732

commit v24 on v23

--- a/solution.py
+++ b/solution.py
@@ -421,10 +421,9 @@
     row = lax.broadcasted_iota(jnp.int32, (LANES, LANES), 0)
     col = lax.broadcasted_iota(jnp.int32, (LANES, LANES), 1)
     same_block = row + col >= LANES - 1
-    filter_row = lax.broadcasted_iota(jnp.int32, (owned, LANES), 0)
     batch = min(blocks, 16)
 
-    def one_filter(f, _):
+    def one_filter(f):
         turned = turned_all[f]
 
         def some_lags(first):
@@ -451,21 +450,20 @@
                 joined = jnp.where(same_block, tables[d], tables[d + 1])
                 skewed = pltpu.roll(joined, 1, 1, stride=1, stride_axis=0)
                 sums = jnp.sum(skewed, axis=0, keepdims=True)
-                row = d % halves * owned
-                place = ((first + d) // halves, slice(row, row + owned), slice(None))
-                lag_sums[place] = jnp.where(filter_row == f, sums, lag_sums[place])
+                row = d % halves * owned + f
+                lag_sums[(first + d) // halves, row : row + 1, :] = sums
 
         if batch == blocks:
             some_lags(0)
         else:
             lax.fori_loop(0, blocks // batch, lambda i, c: (some_lags(i * batch), c)[1], 0)
-        return 0
 
     for f in range(owned):
         turned_all[f] = lax.dot_general(
             mirror, u_all[f], (((1,), (1,)), ((), ())), preferred_element_type=F32
         ).astype(BF16)
-    lax.fori_loop(0, owned, one_filter, 0, unroll=min(owned, 8))
+    for f in range(owned):
+        one_filter(f)
     out_ref[...] = lag_sums[...].astype(LINK)
 
 

time: 53.5 us -> 53.6 us (level)
  no operation moved by 1% of the time
where the time goes in v24:
time: 53.6 us; the launch traced here: 53.3 us
  Pallas kernels  20.9 us (39%)
  starting transfers between devices  17.5 us (33%)
  waiting for transfers between devices  11.3 us (21%)
  local copies, waits for them, and re-layouts  2.08 us (4%)
  between operations  0.87 us (2%)
  other arithmetic  0.66 us (1%)
    all_to_all x1, starting transfers between devices, per_device(): lax.all_to_all(send, ('seq', 'chan'), split_axis=0, concat_axis=0, tiled=...  7.31 us
    pallas_call x1, Pallas kernels, local_parts(): pl.pallas_call(local_kernel, out_shape=[jax.ShapeDtypeStruct((tok_rows, w...  6.22 us
    all_to_all x1, waiting for transfers between devices, per_device(): lax.all_to_all(send, ('seq', 'chan'), split_axis=0, concat_axis=0, tiled=...  5.2 us
    ppermute x3, starting transfers between devices, along_column(): return lax.ppermute(state, 'seq', route)  4.93 us
    pallas_call x1, Pallas kernels, block_states(): pl.pallas_call(state_kernel, out_shape=[jax.ShapeDtypeStruct((2, modes *...  3.57 us
    ppermute x1, waiting for transfers between devices, inside_pair(): return lax.ppermute(state, 'seq', [(i, i ^ 1) for i in range(2 * pairs)])  3.57 us
    all_to_all x1, starting transfers between devices, per_device(): lags = lax.all_to_all(lags, 'seq', split_axis=0, concat_axis=0, tiled=True)  3.48 us
    pallas_call x1, Pallas kernels, filter_lags(): pl.pallas_call(functools.partial(lag_kernel, shards, chans, groups, owned...  3.45 us
  transfers between devices with their start and end apart: 6, of which 3 were waited for; matrix products, arithmetic and copies ran while one was open for 0% of the time, Pallas kernels for 34%

profile of v24, /device:TPU:0, one launch (start us, length us, event | category | flops | bytes accessed | tf_op | source)
XLA Modules:
  0.0 53.3 jit_solution(4182024467415347675)
XLA Ops:
  0.6 0.0 copy-start.9
  0.6 0.0 copy-start.10
  0.7 2.9 %pack_signals.1 = bf16[32,64,256]{2,1,0:T(8,128)(2,1)} custom-call(bf16[256,1024]{1,0:T(8,128)(2,1)} %k_ref.2, bf16[256,1024]{1,0:T(8,128)(2,1)} %v_ref.2, bf16[256,1024]{1,0:T(8,128)(2,1)} %o_ref.1, bf16[256,1024]{1,0:T(8,128)(2,1)} %q_ref.2), custom_call_target="tpu_custom_call" | custom-call | tf_op jit(solution)/shard_map/pack_signals/pallas_call | solution.py:97
  3.6 0.0 copy-start
  3.6 0.0 copy-start.1
  3.6 0.0 copy-start.2
  3.6 0.0 copy-start.3
  3.6 7.3 %all-to-all-start = ((bf16[32,64,256]{2,1,0:T(8,128)(2,1)}), bf16[32,64,256]{2,1,0:T(8,128)(2,1)S(1)}, u32[]{:S(2)}, u32[]{:S(2)}) async-start(bf16[32,64,256]{2,1,0:T(8,128)(2,1)} %pack_signals.1), calls=%async_computation | async-start | bytes 2097152 | tf_op jit(solution)/shard_map/all_to_all | solution.py:511
  11.0 0.0 copy-done.9
  11.0 0.0 copy-done.10
  11.1 0.1 broadcast_in_dim.11
  11.1 0.0 copy-done
  11.1 0.0 copy-done.1
  11.1 0.0 copy-done.2
  11.1 0.0 copy-done.3
  11.2 0.0 copy-start.8
  11.2 3.6 %block_states.1 = (f32[2,128,128]{2,1,0:T(8,128)S(1)}, bf16[2,128,128]{2,1,0:T(8,128)(2,1)}) custom-call(bf16[256,1024]{1,0:T(8,128)(2,1)S(1)} %copy-done, bf16[256,1024]{1,0:T(8,128)(2,1)S(1)} %copy-done.1, bf16[256,1024]{1,0:T(8,128)(2,1)S(1)} %copy-done.2, bf16[256,1024]{1,0:T(8,128)(2,1)S(1)} %copy-done.3, f32[3,16,8,128]{3,2,1,0:T(8,128)S(1)} %bitcast.19), custom_call_target="tpu_custom_call" | custom-call | tf_op jit(solution)/shard_map/block_states/pallas_call | solution.py:184
  14.7 0.0 copy-done.8
  14.7 6.2 %local_parts.1 = (f32[256,1024]{1,0:T(8,128)S(1)}, f32[256,1024]{1,0:T(8,128)S(1)}, f32[8,128]{1,0:T(8,128)S(1)}) custom-call(bf16[256,1024]{1,0:T(8,128)(2,1)S(1)} %copy-done, bf16[256,1024]{1,0:T(8,128)(2,1)S(1)} %copy-done.1, bf16[256,1024]{1,0:T(8,128)(2,1)S(1)} %copy-done.2, bf16[256,1024]{1,0:T(8,128)(2,1)S(1)} %copy-done.3, ...), custom_call_target="tpu_custom_call" | custom-call | tf_op jit(solution)/shard_map/local_parts/pallas_call | solution.py:269
  21.0 0.0 copy-start.4
  21.0 1.0 %copy-done.4 = f32[256,1024]{1,0:T(8,128)} copy-done((f32[256,1024]{1,0:T(8,128)}, f32[256,1024]{1,0:T(8,128)S(1)}, u32[]{:S(2)}) %copy-start.4) | copy-done | bytes 1048600
  22.0 0.0 copy-start.6
  22.0 1.0 %copy-done.6 = f32[256,1024]{1,0:T(8,128)} copy-done((f32[256,1024]{1,0:T(8,128)}, f32[256,1024]{1,0:T(8,128)S(1)}, u32[]{:S(2)}) %copy-start.6) | copy-done | bytes 1048600
  22.9 1.8 %collective-permute-start = (bf16[2,128,128]{2,1,0:T(8,128)(2,1)}, bf16[2,128,128]{2,1,0:T(8,128)(2,1)S(1)}, u32[]{:S(2)}, u32[]{:S(2)}) collective-permute-start(bf16[2,128,128]{2,1,0:T(8,128)(2,1)} %get-tuple-element.38), channel_id=1, source_target_pairs={{0,4},{4,0},{8,12},{12,8},{16,20},{20,16},{24,28},{28,24},{1,5},{5... | collective-permute-start | bytes 196616 | tf_op jit(solution)/shard_map/ppermute | solution.py:285
  24.7 3.6 %collective-permute-done.near_ref = bf16[2,128,128]{2,1,0:T(8,128)(2,1)S(1)} collective-permute-done((bf16[2,128,128]{2,1,0:T(8,128)(2,1)}, bf16[2,128,128]{2,1,0:T(8,128)(2,1)S(1)}, u32[]{:S(2)}, u32[]{:S(2)}) %collective-permute-start) | collective-permute-done | bytes 65568 | tf_op jit(solution)/shard_map/ppermute | solution.py:285
  28.3 0.7 %pair_states.1 = (bf16[128,128]{1,0:T(8,128)(2,1)}, bf16[128,128]{1,0:T(8,128)(2,1)}, bf16[128,128]{1,0:T(8,128)(2,1)}) custom-call(s32[1]{0:T(128)} %bitcast.seq_ref, f32[3,16,8,128]{3,2,1,0:T(8,128)S(1)} %bitcast.21, f32[2,128,128]{2,1,0:T(8,128)S(1)} %get-tuple-element.41.own_ref, bf16[2,128,128]{2,1,0:T(8,128)(2,1)S(1)} %collective-permute-done.near_ref), custom_call_target="tpu_custom_call" | custom-call | tf_op jit(solution)/shard_map/pair_states/pallas_call | solution.py:217
  28.9 1.9 %collective-permute-start.1 = (bf16[128,128]{1,0:T(8,128)(2,1)}, bf16[128,128]{1,0:T(8,128)(2,1)S(1)}, u32[]{:S(2)}, u32[]{:S(2)}) collective-permute-start(bf16[128,128]{1,0:T(8,128)(2,1)} %get-tuple-element.42), channel_id=1, source_target_pairs={{0,8},{4,12},{8,16},{12,20},{16,24},{20,28},{24,0},{28,4},{1,9},{5... | collective-permute-start | bytes 98312 | tf_op jit(solution)/shard_map/ppermute | solution.py:281
  30.8 2.3 %collective-permute-start.2 = (bf16[128,128]{1,0:T(8,128)(2,1)}, bf16[128,128]{1,0:T(8,128)(2,1)S(1)}, u32[]{:S(2)}, u32[]{:S(2)}) collective-permute-start(bf16[128,128]{1,0:T(8,128)(2,1)} %get-tuple-element.43), channel_id=1, source_target_pairs={{0,16},{4,20},{8,24},{12,28},{16,0},{20,4},{24,8},{28,12},{1,17},{... | collective-permute-start | bytes 98312 | tf_op jit(solution)/shard_map/ppermute | solution.py:281
  33.1 0.7 %collective-permute-start.3 = (bf16[128,128]{1,0:T(8,128)(2,1)}, bf16[128,128]{1,0:T(8,128)(2,1)S(1)}, u32[]{:S(2)}, u32[]{:S(2)}) collective-permute-start(bf16[128,128]{1,0:T(8,128)(2,1)} %get-tuple-element.44), channel_id=1, source_target_pairs={{0,24},{4,28},{8,0},{12,4},{16,8},{20,12},{24,16},{28,20},{1,25},{... | collective-permute-start | bytes 98312 | tf_op jit(solution)/shard_map/ppermute | solution.py:281
  33.9 5.2 %all-to-all-done.refs_1_ = bf16[32,64,256]{2,1,0:T(8,128)(2,1)S(1)} async-done(((bf16[32,64,256]{2,1,0:T(8,128)(2,1)}), bf16[32,64,256]{2,1,0:T(8,128)(2,1)S(1)}, u32[]{:S(2)}, u32[]{:S(2)}) %all-to-all-start) | async-done | bytes 1048608 | tf_op jit(solution)/shard_map/all_to_all | solution.py:511
  39.1 3.5 %filter_lags.1 = bf16[8,16,128]{2,1,0:T(8,128)(2,1)} custom-call(f32[8,128]{1,0:T(8,128)S(1)} %get-tuple-element.39.refs_0_, bf16[32,64,256]{2,1,0:T(8,128)(2,1)S(1)} %all-to-all-done.refs_1_), custom_call_target="tpu_custom_call" | custom-call | tf_op jit(solution)/shard_map/filter_lags/pallas_call | solution.py:482
  42.5 0.0 copy-start.7
  42.5 0.0 collective-permute-done.1.refs_0_
  42.5 0.0 collective-permute-done.2.refs_1_
  42.5 0.0 collective-permute-done.3.refs_2_
  42.6 3.5 %all-to-all-start.1 = ((bf16[8,16,128]{2,1,0:T(8,128)(2,1)}), bf16[8,16,128]{2,1,0:T(8,128)(2,1)S(1)}, u32[]{:S(2)}, u32[]{:S(2)}) async-start(bf16[8,16,128]{2,1,0:T(8,128)(2,1)} %filter_lags.1), calls=%async_computation.1 | async-start | bytes 65536 | tf_op jit(solution)/shard_map/all_to_all | solution.py:535
  46.0 1.3 %edge_terms.1.edge_ref = f32[2112,128]{1,0:T(8,128)S(1)} custom-call(s32[1]{0:T(128)} %bitcast.seq_ref, f32[3,16,8,128]{3,2,1,0:T(8,128)S(1)} %bitcast.22, bf16[2,128,128]{2,1,0:T(8,128)(2,1)S(1)} %collective-permute-done.near_ref, bf16[128,128]{1,0:T(8,128)(2,1)S(1)} %collective-permute-done.1.refs_0_, bf16[128,128]{1,0:T(8,128)(2,1)S(1)} %collective-permute-done.2.refs_1_, ...), custom_call_target="tpu_custom_call" | custom-call | tf_op jit(solution)/shard_map/edge_terms/pallas_call | solution.py:316
  47.3 0.0 copy-done.7
  47.3 0.0 copy-start.5
  47.3 1.6 %conv_outputs.1 = (bf16[256,1024]{1,0:T(8,128)(2,1)}, f32[2112,128]{1,0:T(8,128)S(1)}) custom-call(s32[1]{0:T(128)} %bitcast.seq_ref, f32[256,1024]{1,0:T(8,128)S(1)} %copy-done.7, f32[2112,128]{1,0:T(8,128)S(1)} %edge_terms.1.edge_ref, bf16[256,1024]{1,0:T(8,128)(2,1)S(1)} %copy-done, f32[3,16,8,128]{3,2,1,0:T(8,128)S(1)} %bitcast.23, ...), custom_call_target="tpu_custom_call" | custom-call | tf_op jit(solution)/shard_map/conv_outputs/pallas_call | solution.py:352
  49.0 0.0 copy-done.5
  49.0 1.2 %grad_outputs.1 = (bf16[256,1024]{1,0:T(8,128)(2,1)}, bf16[256,1024]{1,0:T(8,128)(2,1)}) custom-call(f32[256,1024]{1,0:T(8,128)S(1)} %copy-done.5, f32[2112,128]{1,0:T(8,128)S(1)} %get-tuple-element.50.edge_ref, bf16[256,1024]{1,0:T(8,128)(2,1)S(1)} %copy-done.2, bf16[256,1024]{1,0:T(8,128)(2,1)S(1)} %copy-done.1), custom_call_target="tpu_custom_call" | custom-call | tf_op jit(solution)/shard_map/grad_outputs/pallas_call | solution.py:381
  50.2 2.5 %all-to-all-done.1 = bf16[8,16,128]{2,1,0:T(8,128)(2,1)S(1)} async-done(((bf16[8,16,128]{2,1,0:T(8,128)(2,1)}), bf16[8,16,128]{2,1,0:T(8,128)(2,1)S(1)}, u32[]{:S(2)}, u32[]{:S(2)}) %all-to-all-start.1) | async-done | bytes 32800 | tf_op jit(solution)/shard_map/all_to_all | solution.py:535
  52.7 0.6 %multiply_bitcast_fusion = f32[256,64]{0,1:T(8,128)} fusion(bf16[8,16,128]{2,1,0:T(8,128)(2,1)S(1)} %all-to-all-done.1), kind=kLoop, calls=%fused_computation | loop fusion | flops 32768 | bytes 98304 | tf_op jit(solution)/shard_map/mul | solution.py:537
  (3 shorter events, 0.1 us)
Async XLA Ops:
  0.6 10.3 %copy-start.9 = (f32[256,16]{0,1:T(8,128)S(1)}, f32[256,16]{0,1:T(8,128)}, u32[]{:S(2)}) copy-start(f32[256,16]{0,1:T(8,128)} %param.12) | copy-start | bytes 49156
  0.6 10.3 %copy-start.10 = (f32[256,16]{0,1:T(8,128)S(1)}, f32[256,16]{0,1:T(8,128)}, u32[]{:S(2)}) copy-start(f32[256,16]{0,1:T(8,128)} %param.11) | copy-start | bytes 49156
  3.6 7.5 %copy-start = (bf16[256,1024]{1,0:T(8,128)(2,1)S(1)}, bf16[256,1024]{1,0:T(8,128)(2,1)}, u32[]{:S(2)}) copy-start(bf16[256,1024]{1,0:T(8,128)(2,1)} %q_ref.2) | copy-start | bytes 1572868
  3.6 7.5 %copy-start.1 = (bf16[256,1024]{1,0:T(8,128)(2,1)S(1)}, bf16[256,1024]{1,0:T(8,128)(2,1)}, u32[]{:S(2)}) copy-start(bf16[256,1024]{1,0:T(8,128)(2,1)} %k_ref.2) | copy-start | bytes 1572868
  3.6 7.5 %copy-start.2 = (bf16[256,1024]{1,0:T(8,128)(2,1)S(1)}, bf16[256,1024]{1,0:T(8,128)(2,1)}, u32[]{:S(2)}) copy-start(bf16[256,1024]{1,0:T(8,128)(2,1)} %v_ref.2) | copy-start | bytes 1572868
  3.6 7.5 %copy-start.3 = (bf16[256,1024]{1,0:T(8,128)(2,1)S(1)}, bf16[256,1024]{1,0:T(8,128)(2,1)}, u32[]{:S(2)}) copy-start(bf16[256,1024]{1,0:T(8,128)(2,1)} %o_ref.1) | copy-start | bytes 1572868
  3.6 35.4 %all-to-all-start = ((bf16[32,64,256]{2,1,0:T(8,128)(2,1)}), bf16[32,64,256]{2,1,0:T(8,128)(2,1)S(1)}, u32[]{:S(2)}, u32[]{:S(2)}) async-start(bf16[32,64,256]{2,1,0:T(8,128)(2,1)} %pack_signals.1), calls=%async_computation | async-start | bytes 2097152 | tf_op jit(solution)/shard_map/all_to_all | solution.py:511
  11.2 3.6 %copy-start.8 = (f32[1024]{0:T(1024)S(1)}, f32[1024]{0:T(1024)}, u32[]{:S(2)}) copy-start(f32[1024]{0:T(1024)} %param.13) | copy-start | bytes 12292
  21.0 1.0 %copy-start.4 = (f32[256,1024]{1,0:T(8,128)}, f32[256,1024]{1,0:T(8,128)S(1)}, u32[]{:S(2)}) copy-start(f32[256,1024]{1,0:T(8,128)S(1)} %get-tuple-element.49.part_ref) | copy-start | bytes 3145732
  22.0 1.0 %copy-start.6 = (f32[256,1024]{1,0:T(8,128)}, f32[256,1024]{1,0:T(8,128)S(1)}, u32[]{:S(2)}) copy-start(f32[256,1024]{1,0:T(8,128)S(1)} %get-tuple-element.35.part_ref) | copy-start | bytes 3145732
  22.9 5.3 %collective-permute-start = (bf16[2,128,128]{2,1,0:T(8,128)(2,1)}, bf16[2,128,128]{2,1,0:T(8,128)(2,1)S(1)}, u32[]{:S(2)}, u32[]{:S(2)}) collective-permute-start(bf16[2,128,128]{2,1,0:T(8,128)(2,1)} %get-tuple-element.38), channel_id=1, source_target_pairs={{0,4},{4,0},{8,12},{12,8},{16,20},{20,16},{24,28},{28,24},{1,5},{5... | collective-permute-start | bytes 196616 | tf_op jit(solution)/shard_map/ppermute | solution.py:285
  28.9 13.6 %collective-permute-start.1 = (bf16[128,128]{1,0:T(8,128)(2,1)}, bf16[128,128]{1,0:T(8,128)(2,1)S(1)}, u32[]{:S(2)}, u32[]{:S(2)}) collective-permute-start(bf16[128,128]{1,0:T(8,128)(2,1)} %get-tuple-element.42), channel_id=1, source_target_pairs={{0,8},{4,12},{8,16},{12,20},{16,24},{20,28},{24,0},{28,4},{1,9},{5... | collective-permute-start | bytes 98312 | tf_op jit(solution)/shard_map/ppermute | solution.py:281
  30.8 11.7 %collective-permute-start.2 = (bf16[128,128]{1,0:T(8,128)(2,1)}, bf16[128,128]{1,0:T(8,128)(2,1)S(1)}, u32[]{:S(2)}, u32[]{:S(2)}) collective-permute-start(bf16[128,128]{1,0:T(8,128)(2,1)} %get-tuple-element.43), channel_id=1, source_target_pairs={{0,16},{4,20},{8,24},{12,28},{16,0},{20,4},{24,8},{28,12},{1,17},{... | collective-permute-start | bytes 98312 | tf_op jit(solution)/shard_map/ppermute | solution.py:281
  33.1 9.4 %collective-permute-start.3 = (bf16[128,128]{1,0:T(8,128)(2,1)}, bf16[128,128]{1,0:T(8,128)(2,1)S(1)}, u32[]{:S(2)}, u32[]{:S(2)}) collective-permute-start(bf16[128,128]{1,0:T(8,128)(2,1)} %get-tuple-element.44), channel_id=1, source_target_pairs={{0,24},{4,28},{8,0},{12,4},{16,8},{20,12},{24,16},{28,20},{1,25},{... | collective-permute-start | bytes 98312 | tf_op jit(solution)/shard_map/ppermute | solution.py:281
  42.5 4.8 %copy-start.7 = (f32[256,1024]{1,0:T(8,128)S(1)}, f32[256,1024]{1,0:T(8,128)}, u32[]{:S(2)}) copy-start(f32[256,1024]{1,0:T(8,128)} %copy-done.6) | copy-start | bytes 3145732
  42.6 10.1 %all-to-all-start.1 = ((bf16[8,16,128]{2,1,0:T(8,128)(2,1)}), bf16[8,16,128]{2,1,0:T(8,128)(2,1)S(1)}, u32[]{:S(2)}, u32[]{:S(2)}) async-start(bf16[8,16,128]{2,1,0:T(8,128)(2,1)} %filter_lags.1), calls=%async_computation.1 | async-start | bytes 65536 | tf_op jit(solution)/shard_map/all_to_all | solution.py:535
  47.3 1.7 %copy-start.5 = (f32[256,1024]{1,0:T(8,128)S(1)}, f32[256,1024]{1,0:T(8,128)}, u32[]{:S(2)}) copy-start(f32[256,1024]{1,0:T(8,128)} %copy-done.4) | copy-start | bytes 3145732

commit v25 on v23

--- a/solution.py
+++ b/solution.py
@@ -37,10 +37,10 @@
     per_chan = FILTERS // chans
     units = [(which, first) for which in range(2) for first in range(0, groups, 2)]
 
-    def arrival(i, first):
-        place = (slice(None), pl.ds(first * FILTERS, 2 * FILTERS))
+    def arrival(i, group):
+        place = (slice(None), pl.ds(group * FILTERS, FILTERS))
         return pltpu.make_async_copy(
-            hbm_refs[i].at[place], held.at[(i, *place)], in_sems.at[i, first // 2]
+            hbm_refs[i].at[place], held.at[(i, *place)], in_sems.at[i, group]
         )
 
     def departure(which, first):
@@ -52,9 +52,10 @@
             packed.at[place], send_ref.at[place], out_sems.at[which, first // 2]
         )
 
-    for which, first in units:
-        for i in (2 * which, 2 * which + 1):
-            arrival(i, first).start()
+    for which in range(2):
+        for group in range(groups):
+            for i in (2 * which, 2 * which + 1):
+                arrival(i, group).start()
 
     def owned_filter(row):
         seq = row // (chans * owned)
@@ -63,10 +64,10 @@
 
     order = one_hot(FILTERS, FILTERS, owned_filter)
     for which, first in units:
-        for i in (2 * which, 2 * which + 1):
-            arrival(i, first).wait()
         pieces = []
         for group in (first, first + 1):
+            for i in (2 * which, 2 * which + 1):
+                arrival(i, group).wait()
             cols = slice(group * FILTERS, (group + 1) * FILTERS)
             piece = lax.dot_general(
                 order,
@@ -102,7 +103,7 @@
         scratch_shapes=[
             pltpu.VMEM((4, tok_rows, width), BF16),
             pltpu.VMEM(shape, BF16),
-            pltpu.SemaphoreType.DMA((4, groups // 2)),
+            pltpu.SemaphoreType.DMA((4, groups)),
             pltpu.SemaphoreType.DMA((2, groups // 2)),
         ],
         compiler_params=pltpu.CompilerParams(vmem_limit_bytes=FULL_VMEM_BYTES),

time: 53.5 us -> 54.5 us (1.019)
  Pallas kernels: 20.9 us -> 21.9 us
    pallas_call x1, Pallas kernels: 2.94 us -> 3.94 us  [pack_signals(): pl.pallas_call(functools.partial(pack_kernel, shards, chans, owned), in_s...]
  transfers between devices with their start and end apart: 6 -> 6, of which waited for: 3 -> 3; matrix products, arithmetic and copies ran while one was open for 0% -> 0% of each run, Pallas kernels for 34% -> 33%
where the time goes in v25:
time: 54.5 us; the launch traced here: 54.3 us
  Pallas kernels  21.9 us (40%)
  starting transfers between devices  17.5 us (32%)
  waiting for transfers between devices  11.3 us (21%)
  local copies, waits for them, and re-layouts  2.08 us (4%)
  between operations  0.87 us (2%)
  other arithmetic  0.66 us (1%)
    all_to_all x1, starting transfers between devices, per_device(): lax.all_to_all(send, ('seq', 'chan'), split_axis=0, concat_axis=0, tiled=...  7.3 us
    pallas_call x1, Pallas kernels, local_parts(): pl.pallas_call(local_kernel, out_shape=[jax.ShapeDtypeStruct((tok_rows, w...  6.22 us
    all_to_all x1, waiting for transfers between devices, per_device(): lax.all_to_all(send, ('seq', 'chan'), split_axis=0, concat_axis=0, tiled=...  5.2 us
    ppermute x3, starting transfers between devices, along_column(): return lax.ppermute(state, 'seq', route)  4.93 us
    pallas_call x1, Pallas kernels, pack_signals(): pl.pallas_call(functools.partial(pack_kernel, shards, chans, owned), in_s...  3.94 us
    pallas_call x1, Pallas kernels, block_states(): pl.pallas_call(state_kernel, out_shape=[jax.ShapeDtypeStruct((2, modes *...  3.57 us
    ppermute x1, waiting for transfers between devices, inside_pair(): return lax.ppermute(state, 'seq', [(i, i ^ 1) for i in range(2 * pairs)])  3.57 us
    all_to_all x1, starting transfers between devices, per_device(): lags = lax.all_to_all(lags, 'seq', split_axis=0, concat_axis=0, tiled=True)  3.48 us
  transfers between devices with their start and end apart: 6, of which 3 were waited for; matrix products, arithmetic and copies ran while one was open for 0% of the time, Pallas kernels for 33%

profile of v25, /device:TPU:0, one launch (start us, length us, event | category | flops | bytes accessed | tf_op | source)
XLA Modules:
  0.0 54.3 jit_solution(7529922380626325547)
XLA Ops:
  0.6 0.0 copy-start.9
  0.6 0.0 copy-start.10
  0.7 3.9 %pack_signals.1 = bf16[32,64,256]{2,1,0:T(8,128)(2,1)} custom-call(bf16[256,1024]{1,0:T(8,128)(2,1)} %k_ref.2, bf16[256,1024]{1,0:T(8,128)(2,1)} %v_ref.2, bf16[256,1024]{1,0:T(8,128)(2,1)} %o_ref.1, bf16[256,1024]{1,0:T(8,128)(2,1)} %q_ref.2), custom_call_target="tpu_custom_call" | custom-call | tf_op jit(solution)/shard_map/pack_signals/pallas_call | solution.py:98
  4.6 0.0 copy-start
  4.6 0.0 copy-start.1
  4.6 0.0 copy-start.2
  4.6 0.0 copy-start.3
  4.6 7.3 %all-to-all-start = ((bf16[32,64,256]{2,1,0:T(8,128)(2,1)}), bf16[32,64,256]{2,1,0:T(8,128)(2,1)S(1)}, u32[]{:S(2)}, u32[]{:S(2)}) async-start(bf16[32,64,256]{2,1,0:T(8,128)(2,1)} %pack_signals.1), calls=%async_computation | async-start | bytes 2097152 | tf_op jit(solution)/shard_map/all_to_all | solution.py:514
  12.0 0.0 copy-done.9
  12.0 0.0 copy-done.10
  12.0 0.1 broadcast_in_dim.11
  12.1 0.0 copy-done
  12.1 0.0 copy-done.1
  12.1 0.0 copy-done.2
  12.1 0.0 copy-done.3
  12.2 0.0 copy-start.8
  12.2 3.6 %block_states.1 = (f32[2,128,128]{2,1,0:T(8,128)S(1)}, bf16[2,128,128]{2,1,0:T(8,128)(2,1)}) custom-call(bf16[256,1024]{1,0:T(8,128)(2,1)S(1)} %copy-done, bf16[256,1024]{1,0:T(8,128)(2,1)S(1)} %copy-done.1, bf16[256,1024]{1,0:T(8,128)(2,1)S(1)} %copy-done.2, bf16[256,1024]{1,0:T(8,128)(2,1)S(1)} %copy-done.3, f32[3,16,8,128]{3,2,1,0:T(8,128)S(1)} %bitcast.19), custom_call_target="tpu_custom_call" | custom-call | tf_op jit(solution)/shard_map/block_states/pallas_call | solution.py:185
  15.7 0.0 copy-done.8
  15.7 6.2 %local_parts.1 = (f32[256,1024]{1,0:T(8,128)S(1)}, f32[256,1024]{1,0:T(8,128)S(1)}, f32[8,128]{1,0:T(8,128)S(1)}) custom-call(bf16[256,1024]{1,0:T(8,128)(2,1)S(1)} %copy-done, bf16[256,1024]{1,0:T(8,128)(2,1)S(1)} %copy-done.1, bf16[256,1024]{1,0:T(8,128)(2,1)S(1)} %copy-done.2, bf16[256,1024]{1,0:T(8,128)(2,1)S(1)} %copy-done.3, ...), custom_call_target="tpu_custom_call" | custom-call | tf_op jit(solution)/shard_map/local_parts/pallas_call | solution.py:270
  22.0 0.0 copy-start.4
  22.0 1.0 %copy-done.4 = f32[256,1024]{1,0:T(8,128)} copy-done((f32[256,1024]{1,0:T(8,128)}, f32[256,1024]{1,0:T(8,128)S(1)}, u32[]{:S(2)}) %copy-start.4) | copy-done | bytes 1048600
  23.0 0.0 copy-start.6
  23.0 1.0 %copy-done.6 = f32[256,1024]{1,0:T(8,128)} copy-done((f32[256,1024]{1,0:T(8,128)}, f32[256,1024]{1,0:T(8,128)S(1)}, u32[]{:S(2)}) %copy-start.6) | copy-done | bytes 1048600
  23.9 1.8 %collective-permute-start = (bf16[2,128,128]{2,1,0:T(8,128)(2,1)}, bf16[2,128,128]{2,1,0:T(8,128)(2,1)S(1)}, u32[]{:S(2)}, u32[]{:S(2)}) collective-permute-start(bf16[2,128,128]{2,1,0:T(8,128)(2,1)} %get-tuple-element.38), channel_id=1, source_target_pairs={{0,4},{4,0},{8,12},{12,8},{16,20},{20,16},{24,28},{28,24},{1,5},{5... | collective-permute-start | bytes 196616 | tf_op jit(solution)/shard_map/ppermute | solution.py:286
  25.7 3.6 %collective-permute-done.near_ref = bf16[2,128,128]{2,1,0:T(8,128)(2,1)S(1)} collective-permute-done((bf16[2,128,128]{2,1,0:T(8,128)(2,1)}, bf16[2,128,128]{2,1,0:T(8,128)(2,1)S(1)}, u32[]{:S(2)}, u32[]{:S(2)}) %collective-permute-start) | collective-permute-done | bytes 65568 | tf_op jit(solution)/shard_map/ppermute | solution.py:286
  29.3 0.7 %pair_states.1 = (bf16[128,128]{1,0:T(8,128)(2,1)}, bf16[128,128]{1,0:T(8,128)(2,1)}, bf16[128,128]{1,0:T(8,128)(2,1)}) custom-call(s32[1]{0:T(128)} %bitcast.seq_ref, f32[3,16,8,128]{3,2,1,0:T(8,128)S(1)} %bitcast.21, f32[2,128,128]{2,1,0:T(8,128)S(1)} %get-tuple-element.41.own_ref, bf16[2,128,128]{2,1,0:T(8,128)(2,1)S(1)} %collective-permute-done.near_ref), custom_call_target="tpu_custom_call" | custom-call | tf_op jit(solution)/shard_map/pair_states/pallas_call | solution.py:218
  29.9 1.9 %collective-permute-start.1 = (bf16[128,128]{1,0:T(8,128)(2,1)}, bf16[128,128]{1,0:T(8,128)(2,1)S(1)}, u32[]{:S(2)}, u32[]{:S(2)}) collective-permute-start(bf16[128,128]{1,0:T(8,128)(2,1)} %get-tuple-element.42), channel_id=1, source_target_pairs={{0,8},{4,12},{8,16},{12,20},{16,24},{20,28},{24,0},{28,4},{1,9},{5... | collective-permute-start | bytes 98312 | tf_op jit(solution)/shard_map/ppermute | solution.py:282
  31.8 2.3 %collective-permute-start.2 = (bf16[128,128]{1,0:T(8,128)(2,1)}, bf16[128,128]{1,0:T(8,128)(2,1)S(1)}, u32[]{:S(2)}, u32[]{:S(2)}) collective-permute-start(bf16[128,128]{1,0:T(8,128)(2,1)} %get-tuple-element.43), channel_id=1, source_target_pairs={{0,16},{4,20},{8,24},{12,28},{16,0},{20,4},{24,8},{28,12},{1,17},{... | collective-permute-start | bytes 98312 | tf_op jit(solution)/shard_map/ppermute | solution.py:282
  34.1 0.7 %collective-permute-start.3 = (bf16[128,128]{1,0:T(8,128)(2,1)}, bf16[128,128]{1,0:T(8,128)(2,1)S(1)}, u32[]{:S(2)}, u32[]{:S(2)}) collective-permute-start(bf16[128,128]{1,0:T(8,128)(2,1)} %get-tuple-element.44), channel_id=1, source_target_pairs={{0,24},{4,28},{8,0},{12,4},{16,8},{20,12},{24,16},{28,20},{1,25},{... | collective-permute-start | bytes 98312 | tf_op jit(solution)/shard_map/ppermute | solution.py:282
  34.9 5.2 %all-to-all-done.refs_1_ = bf16[32,64,256]{2,1,0:T(8,128)(2,1)S(1)} async-done(((bf16[32,64,256]{2,1,0:T(8,128)(2,1)}), bf16[32,64,256]{2,1,0:T(8,128)(2,1)S(1)}, u32[]{:S(2)}, u32[]{:S(2)}) %all-to-all-start) | async-done | bytes 1048608 | tf_op jit(solution)/shard_map/all_to_all | solution.py:514
  40.1 3.5 %filter_lags.1 = bf16[8,16,128]{2,1,0:T(8,128)(2,1)} custom-call(f32[8,128]{1,0:T(8,128)S(1)} %get-tuple-element.39.refs_0_, bf16[32,64,256]{2,1,0:T(8,128)(2,1)S(1)} %all-to-all-done.refs_1_), custom_call_target="tpu_custom_call" | custom-call | tf_op jit(solution)/shard_map/filter_lags/pallas_call | solution.py:485
  43.5 0.0 copy-start.7
  43.5 0.0 collective-permute-done.1.refs_0_
  43.5 0.0 collective-permute-done.2.refs_1_
  43.5 0.0 collective-permute-done.3.refs_2_
  43.5 3.5 %all-to-all-start.1 = ((bf16[8,16,128]{2,1,0:T(8,128)(2,1)}), bf16[8,16,128]{2,1,0:T(8,128)(2,1)S(1)}, u32[]{:S(2)}, u32[]{:S(2)}) async-start(bf16[8,16,128]{2,1,0:T(8,128)(2,1)} %filter_lags.1), calls=%async_computation.1 | async-start | bytes 65536 | tf_op jit(solution)/shard_map/all_to_all | solution.py:538
  47.0 1.3 %edge_terms.1.edge_ref = f32[2112,128]{1,0:T(8,128)S(1)} custom-call(s32[1]{0:T(128)} %bitcast.seq_ref, f32[3,16,8,128]{3,2,1,0:T(8,128)S(1)} %bitcast.22, bf16[2,128,128]{2,1,0:T(8,128)(2,1)S(1)} %collective-permute-done.near_ref, bf16[128,128]{1,0:T(8,128)(2,1)S(1)} %collective-permute-done.1.refs_0_, bf16[128,128]{1,0:T(8,128)(2,1)S(1)} %collective-permute-done.2.refs_1_, ...), custom_call_target="tpu_custom_call" | custom-call | tf_op jit(solution)/shard_map/edge_terms/pallas_call | solution.py:317
  48.3 0.0 copy-done.7
  48.3 0.0 copy-start.5
  48.3 1.6 %conv_outputs.1 = (bf16[256,1024]{1,0:T(8,128)(2,1)}, f32[2112,128]{1,0:T(8,128)S(1)}) custom-call(s32[1]{0:T(128)} %bitcast.seq_ref, f32[256,1024]{1,0:T(8,128)S(1)} %copy-done.7, f32[2112,128]{1,0:T(8,128)S(1)} %edge_terms.1.edge_ref, bf16[256,1024]{1,0:T(8,128)(2,1)S(1)} %copy-done, f32[3,16,8,128]{3,2,1,0:T(8,128)S(1)} %bitcast.23, ...), custom_call_target="tpu_custom_call" | custom-call | tf_op jit(solution)/shard_map/conv_outputs/pallas_call | solution.py:353
  50.0 0.0 copy-done.5
  50.0 1.2 %grad_outputs.1 = (bf16[256,1024]{1,0:T(8,128)(2,1)}, bf16[256,1024]{1,0:T(8,128)(2,1)}) custom-call(f32[256,1024]{1,0:T(8,128)S(1)} %copy-done.5, f32[2112,128]{1,0:T(8,128)S(1)} %get-tuple-element.50.edge_ref, bf16[256,1024]{1,0:T(8,128)(2,1)S(1)} %copy-done.2, bf16[256,1024]{1,0:T(8,128)(2,1)S(1)} %copy-done.1), custom_call_target="tpu_custom_call" | custom-call | tf_op jit(solution)/shard_map/grad_outputs/pallas_call | solution.py:382
  51.2 2.5 %all-to-all-done.1 = bf16[8,16,128]{2,1,0:T(8,128)(2,1)S(1)} async-done(((bf16[8,16,128]{2,1,0:T(8,128)(2,1)}), bf16[8,16,128]{2,1,0:T(8,128)(2,1)S(1)}, u32[]{:S(2)}, u32[]{:S(2)}) %all-to-all-start.1) | async-done | bytes 32800 | tf_op jit(solution)/shard_map/all_to_all | solution.py:538
  53.7 0.6 %multiply_bitcast_fusion = f32[256,64]{0,1:T(8,128)} fusion(bf16[8,16,128]{2,1,0:T(8,128)(2,1)S(1)} %all-to-all-done.1), kind=kLoop, calls=%fused_computation | loop fusion | flops 32768 | bytes 98304 | tf_op jit(solution)/shard_map/mul | solution.py:540
  (3 shorter events, 0.1 us)
Async XLA Ops:
  0.6 11.3 %copy-start.9 = (f32[256,16]{0,1:T(8,128)S(1)}, f32[256,16]{0,1:T(8,128)}, u32[]{:S(2)}) copy-start(f32[256,16]{0,1:T(8,128)} %param.12) | copy-start | bytes 49156
  0.6 11.3 %copy-start.10 = (f32[256,16]{0,1:T(8,128)S(1)}, f32[256,16]{0,1:T(8,128)}, u32[]{:S(2)}) copy-start(f32[256,16]{0,1:T(8,128)} %param.11) | copy-start | bytes 49156
  4.6 7.5 %copy-start = (bf16[256,1024]{1,0:T(8,128)(2,1)S(1)}, bf16[256,1024]{1,0:T(8,128)(2,1)}, u32[]{:S(2)}) copy-start(bf16[256,1024]{1,0:T(8,128)(2,1)} %q_ref.2) | copy-start | bytes 1572868
  4.6 7.5 %copy-start.1 = (bf16[256,1024]{1,0:T(8,128)(2,1)S(1)}, bf16[256,1024]{1,0:T(8,128)(2,1)}, u32[]{:S(2)}) copy-start(bf16[256,1024]{1,0:T(8,128)(2,1)} %k_ref.2) | copy-start | bytes 1572868
  4.6 7.5 %copy-start.2 = (bf16[256,1024]{1,0:T(8,128)(2,1)S(1)}, bf16[256,1024]{1,0:T(8,128)(2,1)}, u32[]{:S(2)}) copy-start(bf16[256,1024]{1,0:T(8,128)(2,1)} %v_ref.2) | copy-start | bytes 1572868
  4.6 7.5 %copy-start.3 = (bf16[256,1024]{1,0:T(8,128)(2,1)S(1)}, bf16[256,1024]{1,0:T(8,128)(2,1)}, u32[]{:S(2)}) copy-start(bf16[256,1024]{1,0:T(8,128)(2,1)} %o_ref.1) | copy-start | bytes 1572868
  4.6 35.4 %all-to-all-start = ((bf16[32,64,256]{2,1,0:T(8,128)(2,1)}), bf16[32,64,256]{2,1,0:T(8,128)(2,1)S(1)}, u32[]{:S(2)}, u32[]{:S(2)}) async-start(bf16[32,64,256]{2,1,0:T(8,128)(2,1)} %pack_signals.1), calls=%async_computation | async-start | bytes 2097152 | tf_op jit(solution)/shard_map/all_to_all | solution.py:514
  12.2 3.6 %copy-start.8 = (f32[1024]{0:T(1024)S(1)}, f32[1024]{0:T(1024)}, u32[]{:S(2)}) copy-start(f32[1024]{0:T(1024)} %param.13) | copy-start | bytes 12292
  22.0 1.0 %copy-start.4 = (f32[256,1024]{1,0:T(8,128)}, f32[256,1024]{1,0:T(8,128)S(1)}, u32[]{:S(2)}) copy-start(f32[256,1024]{1,0:T(8,128)S(1)} %get-tuple-element.49.part_ref) | copy-start | bytes 3145732
  23.0 1.0 %copy-start.6 = (f32[256,1024]{1,0:T(8,128)}, f32[256,1024]{1,0:T(8,128)S(1)}, u32[]{:S(2)}) copy-start(f32[256,1024]{1,0:T(8,128)S(1)} %get-tuple-element.35.part_ref) | copy-start | bytes 3145732
  23.9 5.3 %collective-permute-start = (bf16[2,128,128]{2,1,0:T(8,128)(2,1)}, bf16[2,128,128]{2,1,0:T(8,128)(2,1)S(1)}, u32[]{:S(2)}, u32[]{:S(2)}) collective-permute-start(bf16[2,128,128]{2,1,0:T(8,128)(2,1)} %get-tuple-element.38), channel_id=1, source_target_pairs={{0,4},{4,0},{8,12},{12,8},{16,20},{20,16},{24,28},{28,24},{1,5},{5... | collective-permute-start | bytes 196616 | tf_op jit(solution)/shard_map/ppermute | solution.py:286
  29.9 13.6 %collective-permute-start.1 = (bf16[128,128]{1,0:T(8,128)(2,1)}, bf16[128,128]{1,0:T(8,128)(2,1)S(1)}, u32[]{:S(2)}, u32[]{:S(2)}) collective-permute-start(bf16[128,128]{1,0:T(8,128)(2,1)} %get-tuple-element.42), channel_id=1, source_target_pairs={{0,8},{4,12},{8,16},{12,20},{16,24},{20,28},{24,0},{28,4},{1,9},{5... | collective-permute-start | bytes 98312 | tf_op jit(solution)/shard_map/ppermute | solution.py:282
  31.8 11.7 %collective-permute-start.2 = (bf16[128,128]{1,0:T(8,128)(2,1)}, bf16[128,128]{1,0:T(8,128)(2,1)S(1)}, u32[]{:S(2)}, u32[]{:S(2)}) collective-permute-start(bf16[128,128]{1,0:T(8,128)(2,1)} %get-tuple-element.43), channel_id=1, source_target_pairs={{0,16},{4,20},{8,24},{12,28},{16,0},{20,4},{24,8},{28,12},{1,17},{... | collective-permute-start | bytes 98312 | tf_op jit(solution)/shard_map/ppermute | solution.py:282
  34.1 9.4 %collective-permute-start.3 = (bf16[128,128]{1,0:T(8,128)(2,1)}, bf16[128,128]{1,0:T(8,128)(2,1)S(1)}, u32[]{:S(2)}, u32[]{:S(2)}) collective-permute-start(bf16[128,128]{1,0:T(8,128)(2,1)} %get-tuple-element.44), channel_id=1, source_target_pairs={{0,24},{4,28},{8,0},{12,4},{16,8},{20,12},{24,16},{28,20},{1,25},{... | collective-permute-start | bytes 98312 | tf_op jit(solution)/shard_map/ppermute | solution.py:282
  43.5 4.8 %copy-start.7 = (f32[256,1024]{1,0:T(8,128)S(1)}, f32[256,1024]{1,0:T(8,128)}, u32[]{:S(2)}) copy-start(f32[256,1024]{1,0:T(8,128)} %copy-done.6) | copy-start | bytes 3145732
  43.5 10.1 %all-to-all-start.1 = ((bf16[8,16,128]{2,1,0:T(8,128)(2,1)}), bf16[8,16,128]{2,1,0:T(8,128)(2,1)S(1)}, u32[]{:S(2)}, u32[]{:S(2)}) async-start(bf16[8,16,128]{2,1,0:T(8,128)(2,1)} %filter_lags.1), calls=%async_computation.1 | async-start | bytes 65536 | tf_op jit(solution)/shard_map/all_to_all | solution.py:538
  48.3 1.7 %copy-start.5 = (f32[256,1024]{1,0:T(8,128)S(1)}, f32[256,1024]{1,0:T(8,128)}, u32[]{:S(2)}) copy-start(f32[256,1024]{1,0:T(8,128)} %copy-done.4) | copy-start | bytes 3145732

commit v26 on v23

--- a/solution.py
+++ b/solution.py
@@ -35,26 +35,24 @@
     tok_rows, width = held.shape[1:]
     groups = width // FILTERS
     per_chan = FILTERS // chans
-    units = [(which, first) for which in range(2) for first in range(0, groups, 2)]
-
-    def arrival(i, first):
-        place = (slice(None), pl.ds(first * FILTERS, 2 * FILTERS))
+    half = tok_rows // 2
+
+    def arrival(i, part):
+        place = (pl.ds(part * half, half), slice(None))
         return pltpu.make_async_copy(
-            hbm_refs[i].at[place], held.at[(i, *place)], in_sems.at[i, first // 2]
+            hbm_refs[i].at[place], held.at[(i, *place)], in_sems.at[i, part]
         )
 
-    def departure(which, first):
+    def departure(which):
         if owned % SUBLANES:
-            place = (which, pl.ds(first, 2))
+            place = (which,)
         else:
-            place = (slice(None), pl.ds((which * groups + first) * owned, 2 * owned))
-        return pltpu.make_async_copy(
-            packed.at[place], send_ref.at[place], out_sems.at[which, first // 2]
-        )
-
-    for which, first in units:
-        for i in (2 * which, 2 * which + 1):
-            arrival(i, first).start()
+            place = (slice(None), pl.ds(which * groups * owned, groups * owned))
+        return pltpu.make_async_copy(packed.at[place], send_ref.at[place], out_sems.at[which])
+
+    for i in range(len(hbm_refs)):
+        for part in range(2):
+            arrival(i, part).start()
 
     def owned_filter(row):
         seq = row // (chans * owned)
@@ -62,11 +60,12 @@
         return chan * per_chan + seq * owned + row % owned
 
     order = one_hot(FILTERS, FILTERS, owned_filter)
-    for which, first in units:
+    for which in range(2):
         for i in (2 * which, 2 * which + 1):
-            arrival(i, first).wait()
+            for part in range(2):
+                arrival(i, part).wait()
         pieces = []
-        for group in (first, first + 1):
+        for group in range(groups):
             cols = slice(group * FILTERS, (group + 1) * FILTERS)
             piece = lax.dot_general(
                 order,
@@ -79,11 +78,11 @@
             else:
                 pieces.append(piece.reshape(shards * chans, owned, tok_rows))
         if pieces:
-            row = (which * groups + first) * owned
-            packed[:, row : row + 2 * owned, :] = jnp.concatenate(pieces, axis=1).astype(BF16)
-        departure(which, first).start()
-    for which, first in units:
-        departure(which, first).wait()
+            rows = slice(which * groups * owned, (which + 1) * groups * owned)
+            packed[:, rows, :] = jnp.concatenate(pieces, axis=1).astype(BF16)
+        departure(which).start()
+    for which in range(2):
+        departure(which).wait()
 
 
 def pack_signals(shards, chans, owned, query_proj, key_proj, value_proj, out_grad):
@@ -102,8 +101,8 @@
         scratch_shapes=[
             pltpu.VMEM((4, tok_rows, width), BF16),
             pltpu.VMEM(shape, BF16),
-            pltpu.SemaphoreType.DMA((4, groups // 2)),
-            pltpu.SemaphoreType.DMA((2, groups // 2)),
+            pltpu.SemaphoreType.DMA((4, 2)),
+            pltpu.SemaphoreType.DMA((2,)),
         ],
         compiler_params=pltpu.CompilerParams(vmem_limit_bytes=FULL_VMEM_BYTES),
         name="pack_signals",

time: 53.5 us -> 53.4 us (level)
  no operation moved by 1% of the time
where the time goes in v26:
time: 53.4 us; the launch traced here: 53.1 us
  Pallas kernels  20.8 us (39%)
  starting transfers between devices  17.5 us (33%)
  waiting for transfers between devices  11.3 us (21%)
  local copies, waits for them, and re-layouts  2.08 us (4%)
  between operations  0.87 us (2%)
  other arithmetic  0.66 us (1%)
    all_to_all x1, starting transfers between devices, per_device(): lax.all_to_all(send, ('seq', 'chan'), split_axis=0, concat_axis=0, tiled=...  7.3 us
    pallas_call x1, Pallas kernels, local_parts(): pl.pallas_call(local_kernel, out_shape=[jax.ShapeDtypeStruct((tok_rows, w...  6.22 us
    all_to_all x1, waiting for transfers between devices, per_device(): lax.all_to_all(send, ('seq', 'chan'), split_axis=0, concat_axis=0, tiled=...  5.2 us
    ppermute x3, starting transfers between devices, along_column(): return lax.ppermute(state, 'seq', route)  4.93 us
    pallas_call x1, Pallas kernels, block_states(): pl.pallas_call(state_kernel, out_shape=[jax.ShapeDtypeStruct((2, modes *...  3.57 us
    ppermute x1, waiting for transfers between devices, inside_pair(): return lax.ppermute(state, 'seq', [(i, i ^ 1) for i in range(2 * pairs)])  3.57 us
    all_to_all x1, starting transfers between devices, per_device(): lags = lax.all_to_all(lags, 'seq', split_axis=0, concat_axis=0, tiled=True)  3.48 us
    pallas_call x1, Pallas kernels, filter_lags(): pl.pallas_call(functools.partial(lag_kernel, shards, chans, groups, owned...  3.45 us
  transfers between devices with their start and end apart: 6, of which 3 were waited for; matrix products, arithmetic and copies ran while one was open for 0% of the time, Pallas kernels for 34%

profile of v26, /device:TPU:0, one launch (start us, length us, event | category | flops | bytes accessed | tf_op | source)
XLA Modules:
  0.0 53.1 jit_solution(216885567427716927)
XLA Ops:
  0.6 0.0 copy-start.9
  0.6 0.0 copy-start.10
  0.7 2.8 %pack_signals.1 = bf16[32,64,256]{2,1,0:T(8,128)(2,1)} custom-call(bf16[256,1024]{1,0:T(8,128)(2,1)} %k_ref.2, bf16[256,1024]{1,0:T(8,128)(2,1)} %v_ref.2, bf16[256,1024]{1,0:T(8,128)(2,1)} %o_ref.1, bf16[256,1024]{1,0:T(8,128)(2,1)} %q_ref.2), custom_call_target="tpu_custom_call" | custom-call | tf_op jit(solution)/shard_map/pack_signals/pallas_call | solution.py:96
  3.4 0.0 copy-start
  3.5 0.0 copy-start.1
  3.5 0.0 copy-start.2
  3.5 0.0 copy-start.3
  3.5 7.3 %all-to-all-start = ((bf16[32,64,256]{2,1,0:T(8,128)(2,1)}), bf16[32,64,256]{2,1,0:T(8,128)(2,1)S(1)}, u32[]{:S(2)}, u32[]{:S(2)}) async-start(bf16[32,64,256]{2,1,0:T(8,128)(2,1)} %pack_signals.1), calls=%async_computation | async-start | bytes 2097152 | tf_op jit(solution)/shard_map/all_to_all | solution.py:512
  10.8 0.0 copy-done.9
  10.8 0.0 copy-done.10
  10.9 0.1 broadcast_in_dim.11
  11.0 0.0 copy-done
  11.0 0.0 copy-done.1
  11.0 0.0 copy-done.2
  11.0 0.0 copy-done.3
  11.0 0.0 copy-start.8
  11.0 3.6 %block_states.1 = (f32[2,128,128]{2,1,0:T(8,128)S(1)}, bf16[2,128,128]{2,1,0:T(8,128)(2,1)}) custom-call(bf16[256,1024]{1,0:T(8,128)(2,1)S(1)} %copy-done, bf16[256,1024]{1,0:T(8,128)(2,1)S(1)} %copy-done.1, bf16[256,1024]{1,0:T(8,128)(2,1)S(1)} %copy-done.2, bf16[256,1024]{1,0:T(8,128)(2,1)S(1)} %copy-done.3, f32[3,16,8,128]{3,2,1,0:T(8,128)S(1)} %bitcast.19), custom_call_target="tpu_custom_call" | custom-call | tf_op jit(solution)/shard_map/block_states/pallas_call | solution.py:183
  14.6 0.0 copy-done.8
  14.6 6.2 %local_parts.1 = (f32[256,1024]{1,0:T(8,128)S(1)}, f32[256,1024]{1,0:T(8,128)S(1)}, f32[8,128]{1,0:T(8,128)S(1)}) custom-call(bf16[256,1024]{1,0:T(8,128)(2,1)S(1)} %copy-done, bf16[256,1024]{1,0:T(8,128)(2,1)S(1)} %copy-done.1, bf16[256,1024]{1,0:T(8,128)(2,1)S(1)} %copy-done.2, bf16[256,1024]{1,0:T(8,128)(2,1)S(1)} %copy-done.3, ...), custom_call_target="tpu_custom_call" | custom-call | tf_op jit(solution)/shard_map/local_parts/pallas_call | solution.py:268
  20.8 0.0 copy-start.4
  20.8 1.0 %copy-done.4 = f32[256,1024]{1,0:T(8,128)} copy-done((f32[256,1024]{1,0:T(8,128)}, f32[256,1024]{1,0:T(8,128)S(1)}, u32[]{:S(2)}) %copy-start.4) | copy-done | bytes 1048600
  21.8 0.0 copy-start.6
  21.8 1.0 %copy-done.6 = f32[256,1024]{1,0:T(8,128)} copy-done((f32[256,1024]{1,0:T(8,128)}, f32[256,1024]{1,0:T(8,128)S(1)}, u32[]{:S(2)}) %copy-start.6) | copy-done | bytes 1048600
  22.8 1.8 %collective-permute-start = (bf16[2,128,128]{2,1,0:T(8,128)(2,1)}, bf16[2,128,128]{2,1,0:T(8,128)(2,1)S(1)}, u32[]{:S(2)}, u32[]{:S(2)}) collective-permute-start(bf16[2,128,128]{2,1,0:T(8,128)(2,1)} %get-tuple-element.38), channel_id=1, source_target_pairs={{0,4},{4,0},{8,12},{12,8},{16,20},{20,16},{24,28},{28,24},{1,5},{5... | collective-permute-start | bytes 196616 | tf_op jit(solution)/shard_map/ppermute | solution.py:284
  24.5 3.6 %collective-permute-done.near_ref = bf16[2,128,128]{2,1,0:T(8,128)(2,1)S(1)} collective-permute-done((bf16[2,128,128]{2,1,0:T(8,128)(2,1)}, bf16[2,128,128]{2,1,0:T(8,128)(2,1)S(1)}, u32[]{:S(2)}, u32[]{:S(2)}) %collective-permute-start) | collective-permute-done | bytes 65568 | tf_op jit(solution)/shard_map/ppermute | solution.py:284
  28.1 0.7 %pair_states.1 = (bf16[128,128]{1,0:T(8,128)(2,1)}, bf16[128,128]{1,0:T(8,128)(2,1)}, bf16[128,128]{1,0:T(8,128)(2,1)}) custom-call(s32[1]{0:T(128)} %bitcast.seq_ref, f32[3,16,8,128]{3,2,1,0:T(8,128)S(1)} %bitcast.21, f32[2,128,128]{2,1,0:T(8,128)S(1)} %get-tuple-element.41.own_ref, bf16[2,128,128]{2,1,0:T(8,128)(2,1)S(1)} %collective-permute-done.near_ref), custom_call_target="tpu_custom_call" | custom-call | tf_op jit(solution)/shard_map/pair_states/pallas_call | solution.py:216
  28.8 1.9 %collective-permute-start.1 = (bf16[128,128]{1,0:T(8,128)(2,1)}, bf16[128,128]{1,0:T(8,128)(2,1)S(1)}, u32[]{:S(2)}, u32[]{:S(2)}) collective-permute-start(bf16[128,128]{1,0:T(8,128)(2,1)} %get-tuple-element.42), channel_id=1, source_target_pairs={{0,8},{4,12},{8,16},{12,20},{16,24},{20,28},{24,0},{28,4},{1,9},{5... | collective-permute-start | bytes 98312 | tf_op jit(solution)/shard_map/ppermute | solution.py:280
  30.7 2.3 %collective-permute-start.2 = (bf16[128,128]{1,0:T(8,128)(2,1)}, bf16[128,128]{1,0:T(8,128)(2,1)S(1)}, u32[]{:S(2)}, u32[]{:S(2)}) collective-permute-start(bf16[128,128]{1,0:T(8,128)(2,1)} %get-tuple-element.43), channel_id=1, source_target_pairs={{0,16},{4,20},{8,24},{12,28},{16,0},{20,4},{24,8},{28,12},{1,17},{... | collective-permute-start | bytes 98312 | tf_op jit(solution)/shard_map/ppermute | solution.py:280
  33.0 0.7 %collective-permute-start.3 = (bf16[128,128]{1,0:T(8,128)(2,1)}, bf16[128,128]{1,0:T(8,128)(2,1)S(1)}, u32[]{:S(2)}, u32[]{:S(2)}) collective-permute-start(bf16[128,128]{1,0:T(8,128)(2,1)} %get-tuple-element.44), channel_id=1, source_target_pairs={{0,24},{4,28},{8,0},{12,4},{16,8},{20,12},{24,16},{28,20},{1,25},{... | collective-permute-start | bytes 98312 | tf_op jit(solution)/shard_map/ppermute | solution.py:280
  33.7 5.2 %all-to-all-done.refs_1_ = bf16[32,64,256]{2,1,0:T(8,128)(2,1)S(1)} async-done(((bf16[32,64,256]{2,1,0:T(8,128)(2,1)}), bf16[32,64,256]{2,1,0:T(8,128)(2,1)S(1)}, u32[]{:S(2)}, u32[]{:S(2)}) %all-to-all-start) | async-done | bytes 1048608 | tf_op jit(solution)/shard_map/all_to_all | solution.py:512
  38.9 3.4 %filter_lags.1 = bf16[8,16,128]{2,1,0:T(8,128)(2,1)} custom-call(f32[8,128]{1,0:T(8,128)S(1)} %get-tuple-element.39.refs_0_, bf16[32,64,256]{2,1,0:T(8,128)(2,1)S(1)} %all-to-all-done.refs_1_), custom_call_target="tpu_custom_call" | custom-call | tf_op jit(solution)/shard_map/filter_lags/pallas_call | solution.py:483
  42.4 0.0 copy-start.7
  42.4 0.0 collective-permute-done.1.refs_0_
  42.4 0.0 collective-permute-done.2.refs_1_
  42.4 0.0 collective-permute-done.3.refs_2_
  42.4 3.5 %all-to-all-start.1 = ((bf16[8,16,128]{2,1,0:T(8,128)(2,1)}), bf16[8,16,128]{2,1,0:T(8,128)(2,1)S(1)}, u32[]{:S(2)}, u32[]{:S(2)}) async-start(bf16[8,16,128]{2,1,0:T(8,128)(2,1)} %filter_lags.1), calls=%async_computation.1 | async-start | bytes 65536 | tf_op jit(solution)/shard_map/all_to_all | solution.py:536
  45.9 1.3 %edge_terms.1.edge_ref = f32[2112,128]{1,0:T(8,128)S(1)} custom-call(s32[1]{0:T(128)} %bitcast.seq_ref, f32[3,16,8,128]{3,2,1,0:T(8,128)S(1)} %bitcast.22, bf16[2,128,128]{2,1,0:T(8,128)(2,1)S(1)} %collective-permute-done.near_ref, bf16[128,128]{1,0:T(8,128)(2,1)S(1)} %collective-permute-done.1.refs_0_, bf16[128,128]{1,0:T(8,128)(2,1)S(1)} %collective-permute-done.2.refs_1_, ...), custom_call_target="tpu_custom_call" | custom-call | tf_op jit(solution)/shard_map/edge_terms/pallas_call | solution.py:315
  47.1 0.0 copy-done.7
  47.2 0.0 copy-start.5
  47.2 1.6 %conv_outputs.1 = (bf16[256,1024]{1,0:T(8,128)(2,1)}, f32[2112,128]{1,0:T(8,128)S(1)}) custom-call(s32[1]{0:T(128)} %bitcast.seq_ref, f32[256,1024]{1,0:T(8,128)S(1)} %copy-done.7, f32[2112,128]{1,0:T(8,128)S(1)} %edge_terms.1.edge_ref, bf16[256,1024]{1,0:T(8,128)(2,1)S(1)} %copy-done, f32[3,16,8,128]{3,2,1,0:T(8,128)S(1)} %bitcast.23, ...), custom_call_target="tpu_custom_call" | custom-call | tf_op jit(solution)/shard_map/conv_outputs/pallas_call | solution.py:351
  48.8 0.0 copy-done.5
  48.8 1.2 %grad_outputs.1 = (bf16[256,1024]{1,0:T(8,128)(2,1)}, bf16[256,1024]{1,0:T(8,128)(2,1)}) custom-call(f32[256,1024]{1,0:T(8,128)S(1)} %copy-done.5, f32[2112,128]{1,0:T(8,128)S(1)} %get-tuple-element.50.edge_ref, bf16[256,1024]{1,0:T(8,128)(2,1)S(1)} %copy-done.2, bf16[256,1024]{1,0:T(8,128)(2,1)S(1)} %copy-done.1), custom_call_target="tpu_custom_call" | custom-call | tf_op jit(solution)/shard_map/grad_outputs/pallas_call | solution.py:380
  50.0 2.5 %all-to-all-done.1 = bf16[8,16,128]{2,1,0:T(8,128)(2,1)S(1)} async-done(((bf16[8,16,128]{2,1,0:T(8,128)(2,1)}), bf16[8,16,128]{2,1,0:T(8,128)(2,1)S(1)}, u32[]{:S(2)}, u32[]{:S(2)}) %all-to-all-start.1) | async-done | bytes 32800 | tf_op jit(solution)/shard_map/all_to_all | solution.py:536
  52.5 0.6 %multiply_bitcast_fusion = f32[256,64]{0,1:T(8,128)} fusion(bf16[8,16,128]{2,1,0:T(8,128)(2,1)S(1)} %all-to-all-done.1), kind=kLoop, calls=%fused_computation | loop fusion | flops 32768 | bytes 98304 | tf_op jit(solution)/shard_map/mul | solution.py:538
  (3 shorter events, 0.1 us)
Async XLA Ops:
  0.6 10.2 %copy-start.9 = (f32[256,16]{0,1:T(8,128)S(1)}, f32[256,16]{0,1:T(8,128)}, u32[]{:S(2)}) copy-start(f32[256,16]{0,1:T(8,128)} %param.12) | copy-start | bytes 49156
  0.6 10.2 %copy-start.10 = (f32[256,16]{0,1:T(8,128)S(1)}, f32[256,16]{0,1:T(8,128)}, u32[]{:S(2)}) copy-start(f32[256,16]{0,1:T(8,128)} %param.11) | copy-start | bytes 49156
  3.4 7.5 %copy-start = (bf16[256,1024]{1,0:T(8,128)(2,1)S(1)}, bf16[256,1024]{1,0:T(8,128)(2,1)}, u32[]{:S(2)}) copy-start(bf16[256,1024]{1,0:T(8,128)(2,1)} %q_ref.2) | copy-start | bytes 1572868
  3.5 7.5 %copy-start.1 = (bf16[256,1024]{1,0:T(8,128)(2,1)S(1)}, bf16[256,1024]{1,0:T(8,128)(2,1)}, u32[]{:S(2)}) copy-start(bf16[256,1024]{1,0:T(8,128)(2,1)} %k_ref.2) | copy-start | bytes 1572868
  3.5 7.5 %copy-start.2 = (bf16[256,1024]{1,0:T(8,128)(2,1)S(1)}, bf16[256,1024]{1,0:T(8,128)(2,1)}, u32[]{:S(2)}) copy-start(bf16[256,1024]{1,0:T(8,128)(2,1)} %v_ref.2) | copy-start | bytes 1572868
  3.5 7.5 %copy-start.3 = (bf16[256,1024]{1,0:T(8,128)(2,1)S(1)}, bf16[256,1024]{1,0:T(8,128)(2,1)}, u32[]{:S(2)}) copy-start(bf16[256,1024]{1,0:T(8,128)(2,1)} %o_ref.1) | copy-start | bytes 1572868
  3.5 35.4 %all-to-all-start = ((bf16[32,64,256]{2,1,0:T(8,128)(2,1)}), bf16[32,64,256]{2,1,0:T(8,128)(2,1)S(1)}, u32[]{:S(2)}, u32[]{:S(2)}) async-start(bf16[32,64,256]{2,1,0:T(8,128)(2,1)} %pack_signals.1), calls=%async_computation | async-start | bytes 2097152 | tf_op jit(solution)/shard_map/all_to_all | solution.py:512
  11.0 3.6 %copy-start.8 = (f32[1024]{0:T(1024)S(1)}, f32[1024]{0:T(1024)}, u32[]{:S(2)}) copy-start(f32[1024]{0:T(1024)} %param.13) | copy-start | bytes 12292
  20.8 1.0 %copy-start.4 = (f32[256,1024]{1,0:T(8,128)}, f32[256,1024]{1,0:T(8,128)S(1)}, u32[]{:S(2)}) copy-start(f32[256,1024]{1,0:T(8,128)S(1)} %get-tuple-element.49.part_ref) | copy-start | bytes 3145732
  21.8 1.0 %copy-start.6 = (f32[256,1024]{1,0:T(8,128)}, f32[256,1024]{1,0:T(8,128)S(1)}, u32[]{:S(2)}) copy-start(f32[256,1024]{1,0:T(8,128)S(1)} %get-tuple-element.35.part_ref) | copy-start | bytes 3145732
  22.8 5.3 %collective-permute-start = (bf16[2,128,128]{2,1,0:T(8,128)(2,1)}, bf16[2,128,128]{2,1,0:T(8,128)(2,1)S(1)}, u32[]{:S(2)}, u32[]{:S(2)}) collective-permute-start(bf16[2,128,128]{2,1,0:T(8,128)(2,1)} %get-tuple-element.38), channel_id=1, source_target_pairs={{0,4},{4,0},{8,12},{12,8},{16,20},{20,16},{24,28},{28,24},{1,5},{5... | collective-permute-start | bytes 196616 | tf_op jit(solution)/shard_map/ppermute | solution.py:284
  28.8 13.6 %collective-permute-start.1 = (bf16[128,128]{1,0:T(8,128)(2,1)}, bf16[128,128]{1,0:T(8,128)(2,1)S(1)}, u32[]{:S(2)}, u32[]{:S(2)}) collective-permute-start(bf16[128,128]{1,0:T(8,128)(2,1)} %get-tuple-element.42), channel_id=1, source_target_pairs={{0,8},{4,12},{8,16},{12,20},{16,24},{20,28},{24,0},{28,4},{1,9},{5... | collective-permute-start | bytes 98312 | tf_op jit(solution)/shard_map/ppermute | solution.py:280
  30.7 11.7 %collective-permute-start.2 = (bf16[128,128]{1,0:T(8,128)(2,1)}, bf16[128,128]{1,0:T(8,128)(2,1)S(1)}, u32[]{:S(2)}, u32[]{:S(2)}) collective-permute-start(bf16[128,128]{1,0:T(8,128)(2,1)} %get-tuple-element.43), channel_id=1, source_target_pairs={{0,16},{4,20},{8,24},{12,28},{16,0},{20,4},{24,8},{28,12},{1,17},{... | collective-permute-start | bytes 98312 | tf_op jit(solution)/shard_map/ppermute | solution.py:280
  33.0 9.4 %collective-permute-start.3 = (bf16[128,128]{1,0:T(8,128)(2,1)}, bf16[128,128]{1,0:T(8,128)(2,1)S(1)}, u32[]{:S(2)}, u32[]{:S(2)}) collective-permute-start(bf16[128,128]{1,0:T(8,128)(2,1)} %get-tuple-element.44), channel_id=1, source_target_pairs={{0,24},{4,28},{8,0},{12,4},{16,8},{20,12},{24,16},{28,20},{1,25},{... | collective-permute-start | bytes 98312 | tf_op jit(solution)/shard_map/ppermute | solution.py:280
  42.4 4.8 %copy-start.7 = (f32[256,1024]{1,0:T(8,128)S(1)}, f32[256,1024]{1,0:T(8,128)}, u32[]{:S(2)}) copy-start(f32[256,1024]{1,0:T(8,128)} %copy-done.6) | copy-start | bytes 3145732
  42.4 10.1 %all-to-all-start.1 = ((bf16[8,16,128]{2,1,0:T(8,128)(2,1)}), bf16[8,16,128]{2,1,0:T(8,128)(2,1)S(1)}, u32[]{:S(2)}, u32[]{:S(2)}) async-start(bf16[8,16,128]{2,1,0:T(8,128)(2,1)} %filter_lags.1), calls=%async_computation.1 | async-start | bytes 65536 | tf_op jit(solution)/shard_map/all_to_all | solution.py:536
  47.2 1.7 %copy-start.5 = (f32[256,1024]{1,0:T(8,128)S(1)}, f32[256,1024]{1,0:T(8,128)}, u32[]{:S(2)}) copy-start(f32[256,1024]{1,0:T(8,128)} %copy-done.4) | copy-start | bytes 3145732

commit v27 on v26

--- a/solution.py
+++ b/solution.py
@@ -397,21 +397,23 @@
     depth = chans * groups
     full = blocks * depth
     if len(in_refs) == 1:
-        take = chans * groups * owned
+        take = 2 * chans * groups * owned
 
         def by_filter(row):
-            return row % depth * owned + row // depth
+            return row % (2 * depth) * owned + row // (2 * depth)
 
         order = one_hot(take, take, by_filter)
         for which, kept in enumerate((u_all, g_all)):
             rows = slice(which * groups * owned, (which + 1) * groups * owned)
-            for s in range(shards):
-                piece = in_refs[0][s * chans : (s + 1) * chans, rows, :].reshape(take, tok_rows)
+            for s in range(0, shards, 2):
+                piece = in_refs[0][s * chans : (s + 2) * chans, rows, :].reshape(take, tok_rows)
                 piece = jnp.dot(order, piece, preferred_element_type=F32).astype(BF16)
-                piece = piece.reshape(owned, depth, tok_rows)
-                for h in range(halves):
-                    first = (s * halves + h) * depth
-                    kept[:, first : first + depth, :] = piece[:, :, h * LANES : (h + 1) * LANES]
+                piece = piece.reshape(owned, 2 * depth, tok_rows)
+                for e in range(2):
+                    part = piece[:, e * depth : (e + 1) * depth, :]
+                    for h in range(halves):
+                        first = ((s + e) * halves + h) * depth
+                        kept[:, first : first + depth, :] = part[:, :, h * LANES : (h + 1) * LANES]
     else:
         u_all[...] = in_refs[0][...]
         g_all[:, :full, :] = in_refs[1][...]

time: 53.4 us -> 53.4 us (level)
  no operation moved by 1% of the time
where the time goes in v27:
time: 53.4 us; the launch traced here: 53.1 us
  Pallas kernels  20.8 us (39%)
  starting transfers between devices  17.5 us (33%)
  waiting for transfers between devices  11.3 us (21%)
  local copies, waits for them, and re-layouts  2.08 us (4%)
  between operations  0.87 us (2%)
  other arithmetic  0.66 us (1%)
    all_to_all x1, starting transfers between devices, per_device(): lax.all_to_all(send, ('seq', 'chan'), split_axis=0, concat_axis=0, tiled=...  7.3 us
    pallas_call x1, Pallas kernels, local_parts(): pl.pallas_call(local_kernel, out_shape=[jax.ShapeDtypeStruct((tok_rows, w...  6.22 us
    all_to_all x1, waiting for transfers between devices, per_device(): lax.all_to_all(send, ('seq', 'chan'), split_axis=0, concat_axis=0, tiled=...  5.2 us
    ppermute x3, starting transfers between devices, along_column(): return lax.ppermute(state, 'seq', route)  4.93 us
    pallas_call x1, Pallas kernels, block_states(): pl.pallas_call(state_kernel, out_shape=[jax.ShapeDtypeStruct((2, modes *...  3.57 us
    ppermute x1, waiting for transfers between devices, inside_pair(): return lax.ppermute(state, 'seq', [(i, i ^ 1) for i in range(2 * pairs)])  3.57 us
    all_to_all x1, starting transfers between devices, per_device(): lags = lax.all_to_all(lags, 'seq', split_axis=0, concat_axis=0, tiled=True)  3.48 us
    pallas_call x1, Pallas kernels, filter_lags(): pl.pallas_call(functools.partial(lag_kernel, shards, chans, groups, owned...  3.47 us
  transfers between devices with their start and end apart: 6, of which 3 were waited for; matrix products, arithmetic and copies ran while one was open for 0% of the time, Pallas kernels for 34%

profile of v27, /device:TPU:0, one launch (start us, length us, event | category | flops | bytes accessed | tf_op | source)
XLA Modules:
  0.0 53.1 jit_solution(479150100009768118)
XLA Ops:
  0.6 0.0 copy-start.9
  0.6 0.0 copy-start.10
  0.7 2.8 %pack_signals.1 = bf16[32,64,256]{2,1,0:T(8,128)(2,1)} custom-call(bf16[256,1024]{1,0:T(8,128)(2,1)} %k_ref.2, bf16[256,1024]{1,0:T(8,128)(2,1)} %v_ref.2, bf16[256,1024]{1,0:T(8,128)(2,1)} %o_ref.1, bf16[256,1024]{1,0:T(8,128)(2,1)} %q_ref.2), custom_call_target="tpu_custom_call" | custom-call | tf_op jit(solution)/shard_map/pack_signals/pallas_call | solution.py:96
  3.4 0.0 copy-start
  3.5 0.0 copy-start.1
  3.5 0.0 copy-start.2
  3.5 0.0 copy-start.3
  3.5 7.3 %all-to-all-start = ((bf16[32,64,256]{2,1,0:T(8,128)(2,1)}), bf16[32,64,256]{2,1,0:T(8,128)(2,1)S(1)}, u32[]{:S(2)}, u32[]{:S(2)}) async-start(bf16[32,64,256]{2,1,0:T(8,128)(2,1)} %pack_signals.1), calls=%async_computation | async-start | bytes 2097152 | tf_op jit(solution)/shard_map/all_to_all | solution.py:514
  10.8 0.0 copy-done.9
  10.8 0.0 copy-done.10
  10.9 0.1 broadcast_in_dim.11
  11.0 0.0 copy-done
  11.0 0.0 copy-done.1
  11.0 0.0 copy-done.2
  11.0 0.0 copy-done.3
  11.0 0.0 copy-start.8
  11.0 3.6 %block_states.1 = (f32[2,128,128]{2,1,0:T(8,128)S(1)}, bf16[2,128,128]{2,1,0:T(8,128)(2,1)}) custom-call(bf16[256,1024]{1,0:T(8,128)(2,1)S(1)} %copy-done, bf16[256,1024]{1,0:T(8,128)(2,1)S(1)} %copy-done.1, bf16[256,1024]{1,0:T(8,128)(2,1)S(1)} %copy-done.2, bf16[256,1024]{1,0:T(8,128)(2,1)S(1)} %copy-done.3, f32[3,16,8,128]{3,2,1,0:T(8,128)S(1)} %bitcast.19), custom_call_target="tpu_custom_call" | custom-call | tf_op jit(solution)/shard_map/block_states/pallas_call | solution.py:183
  14.6 0.0 copy-done.8
  14.6 6.2 %local_parts.1 = (f32[256,1024]{1,0:T(8,128)S(1)}, f32[256,1024]{1,0:T(8,128)S(1)}, f32[8,128]{1,0:T(8,128)S(1)}) custom-call(bf16[256,1024]{1,0:T(8,128)(2,1)S(1)} %copy-done, bf16[256,1024]{1,0:T(8,128)(2,1)S(1)} %copy-done.1, bf16[256,1024]{1,0:T(8,128)(2,1)S(1)} %copy-done.2, bf16[256,1024]{1,0:T(8,128)(2,1)S(1)} %copy-done.3, ...), custom_call_target="tpu_custom_call" | custom-call | tf_op jit(solution)/shard_map/local_parts/pallas_call | solution.py:268
  20.8 0.0 copy-start.4
  20.8 1.0 %copy-done.4 = f32[256,1024]{1,0:T(8,128)} copy-done((f32[256,1024]{1,0:T(8,128)}, f32[256,1024]{1,0:T(8,128)S(1)}, u32[]{:S(2)}) %copy-start.4) | copy-done | bytes 1048600
  21.8 0.0 copy-start.6
  21.8 1.0 %copy-done.6 = f32[256,1024]{1,0:T(8,128)} copy-done((f32[256,1024]{1,0:T(8,128)}, f32[256,1024]{1,0:T(8,128)S(1)}, u32[]{:S(2)}) %copy-start.6) | copy-done | bytes 1048600
  22.8 1.8 %collective-permute-start = (bf16[2,128,128]{2,1,0:T(8,128)(2,1)}, bf16[2,128,128]{2,1,0:T(8,128)(2,1)S(1)}, u32[]{:S(2)}, u32[]{:S(2)}) collective-permute-start(bf16[2,128,128]{2,1,0:T(8,128)(2,1)} %get-tuple-element.38), channel_id=1, source_target_pairs={{0,4},{4,0},{8,12},{12,8},{16,20},{20,16},{24,28},{28,24},{1,5},{5... | collective-permute-start | bytes 196616 | tf_op jit(solution)/shard_map/ppermute | solution.py:284
  24.5 3.6 %collective-permute-done.near_ref = bf16[2,128,128]{2,1,0:T(8,128)(2,1)S(1)} collective-permute-done((bf16[2,128,128]{2,1,0:T(8,128)(2,1)}, bf16[2,128,128]{2,1,0:T(8,128)(2,1)S(1)}, u32[]{:S(2)}, u32[]{:S(2)}) %collective-permute-start) | collective-permute-done | bytes 65568 | tf_op jit(solution)/shard_map/ppermute | solution.py:284
  28.1 0.7 %pair_states.1 = (bf16[128,128]{1,0:T(8,128)(2,1)}, bf16[128,128]{1,0:T(8,128)(2,1)}, bf16[128,128]{1,0:T(8,128)(2,1)}) custom-call(s32[1]{0:T(128)} %bitcast.seq_ref, f32[3,16,8,128]{3,2,1,0:T(8,128)S(1)} %bitcast.21, f32[2,128,128]{2,1,0:T(8,128)S(1)} %get-tuple-element.41.own_ref, bf16[2,128,128]{2,1,0:T(8,128)(2,1)S(1)} %collective-permute-done.near_ref), custom_call_target="tpu_custom_call" | custom-call | tf_op jit(solution)/shard_map/pair_states/pallas_call | solution.py:216
  28.8 1.9 %collective-permute-start.1 = (bf16[128,128]{1,0:T(8,128)(2,1)}, bf16[128,128]{1,0:T(8,128)(2,1)S(1)}, u32[]{:S(2)}, u32[]{:S(2)}) collective-permute-start(bf16[128,128]{1,0:T(8,128)(2,1)} %get-tuple-element.42), channel_id=1, source_target_pairs={{0,8},{4,12},{8,16},{12,20},{16,24},{20,28},{24,0},{28,4},{1,9},{5... | collective-permute-start | bytes 98312 | tf_op jit(solution)/shard_map/ppermute | solution.py:280
  30.7 2.3 %collective-permute-start.2 = (bf16[128,128]{1,0:T(8,128)(2,1)}, bf16[128,128]{1,0:T(8,128)(2,1)S(1)}, u32[]{:S(2)}, u32[]{:S(2)}) collective-permute-start(bf16[128,128]{1,0:T(8,128)(2,1)} %get-tuple-element.43), channel_id=1, source_target_pairs={{0,16},{4,20},{8,24},{12,28},{16,0},{20,4},{24,8},{28,12},{1,17},{... | collective-permute-start | bytes 98312 | tf_op jit(solution)/shard_map/ppermute | solution.py:280
  33.0 0.7 %collective-permute-start.3 = (bf16[128,128]{1,0:T(8,128)(2,1)}, bf16[128,128]{1,0:T(8,128)(2,1)S(1)}, u32[]{:S(2)}, u32[]{:S(2)}) collective-permute-start(bf16[128,128]{1,0:T(8,128)(2,1)} %get-tuple-element.44), channel_id=1, source_target_pairs={{0,24},{4,28},{8,0},{12,4},{16,8},{20,12},{24,16},{28,20},{1,25},{... | collective-permute-start | bytes 98312 | tf_op jit(solution)/shard_map/ppermute | solution.py:280
  33.7 5.2 %all-to-all-done.refs_1_ = bf16[32,64,256]{2,1,0:T(8,128)(2,1)S(1)} async-done(((bf16[32,64,256]{2,1,0:T(8,128)(2,1)}), bf16[32,64,256]{2,1,0:T(8,128)(2,1)S(1)}, u32[]{:S(2)}, u32[]{:S(2)}) %all-to-all-start) | async-done | bytes 1048608 | tf_op jit(solution)/shard_map/all_to_all | solution.py:514
  38.9 3.5 %filter_lags.1 = bf16[8,16,128]{2,1,0:T(8,128)(2,1)} custom-call(f32[8,128]{1,0:T(8,128)S(1)} %get-tuple-element.39.refs_0_, bf16[32,64,256]{2,1,0:T(8,128)(2,1)S(1)} %all-to-all-done.refs_1_), custom_call_target="tpu_custom_call" | custom-call | tf_op jit(solution)/shard_map/filter_lags/pallas_call | solution.py:485
  42.4 0.0 copy-start.7
  42.4 0.0 collective-permute-done.1.refs_0_
  42.4 0.0 collective-permute-done.2.refs_1_
  42.4 0.0 collective-permute-done.3.refs_2_
  42.4 3.5 %all-to-all-start.1 = ((bf16[8,16,128]{2,1,0:T(8,128)(2,1)}), bf16[8,16,128]{2,1,0:T(8,128)(2,1)S(1)}, u32[]{:S(2)}, u32[]{:S(2)}) async-start(bf16[8,16,128]{2,1,0:T(8,128)(2,1)} %filter_lags.1), calls=%async_computation.1 | async-start | bytes 65536 | tf_op jit(solution)/shard_map/all_to_all | solution.py:538
  45.9 1.3 %edge_terms.1.edge_ref = f32[2112,128]{1,0:T(8,128)S(1)} custom-call(s32[1]{0:T(128)} %bitcast.seq_ref, f32[3,16,8,128]{3,2,1,0:T(8,128)S(1)} %bitcast.22, bf16[2,128,128]{2,1,0:T(8,128)(2,1)S(1)} %collective-permute-done.near_ref, bf16[128,128]{1,0:T(8,128)(2,1)S(1)} %collective-permute-done.1.refs_0_, bf16[128,128]{1,0:T(8,128)(2,1)S(1)} %collective-permute-done.2.refs_1_, ...), custom_call_target="tpu_custom_call" | custom-call | tf_op jit(solution)/shard_map/edge_terms/pallas_call | solution.py:315
  47.2 0.0 copy-done.7
  47.2 0.0 copy-start.5
  47.2 1.6 %conv_outputs.1 = (bf16[256,1024]{1,0:T(8,128)(2,1)}, f32[2112,128]{1,0:T(8,128)S(1)}) custom-call(s32[1]{0:T(128)} %bitcast.seq_ref, f32[256,1024]{1,0:T(8,128)S(1)} %copy-done.7, f32[2112,128]{1,0:T(8,128)S(1)} %edge_terms.1.edge_ref, bf16[256,1024]{1,0:T(8,128)(2,1)S(1)} %copy-done, f32[3,16,8,128]{3,2,1,0:T(8,128)S(1)} %bitcast.23, ...), custom_call_target="tpu_custom_call" | custom-call | tf_op jit(solution)/shard_map/conv_outputs/pallas_call | solution.py:351
  48.8 0.0 copy-done.5
  48.8 1.2 %grad_outputs.1 = (bf16[256,1024]{1,0:T(8,128)(2,1)}, bf16[256,1024]{1,0:T(8,128)(2,1)}) custom-call(f32[256,1024]{1,0:T(8,128)S(1)} %copy-done.5, f32[2112,128]{1,0:T(8,128)S(1)} %get-tuple-element.50.edge_ref, bf16[256,1024]{1,0:T(8,128)(2,1)S(1)} %copy-done.2, bf16[256,1024]{1,0:T(8,128)(2,1)S(1)} %copy-done.1), custom_call_target="tpu_custom_call" | custom-call | tf_op jit(solution)/shard_map/grad_outputs/pallas_call | solution.py:380
  50.0 2.5 %all-to-all-done.1 = bf16[8,16,128]{2,1,0:T(8,128)(2,1)S(1)} async-done(((bf16[8,16,128]{2,1,0:T(8,128)(2,1)}), bf16[8,16,128]{2,1,0:T(8,128)(2,1)S(1)}, u32[]{:S(2)}, u32[]{:S(2)}) %all-to-all-start.1) | async-done | bytes 32800 | tf_op jit(solution)/shard_map/all_to_all | solution.py:538
  52.5 0.6 %multiply_bitcast_fusion = f32[256,64]{0,1:T(8,128)} fusion(bf16[8,16,128]{2,1,0:T(8,128)(2,1)S(1)} %all-to-all-done.1), kind=kLoop, calls=%fused_computation | loop fusion | flops 32768 | bytes 98304 | tf_op jit(solution)/shard_map/mul | solution.py:540
  (3 shorter events, 0.1 us)
Async XLA Ops:
  0.6 10.2 %copy-start.9 = (f32[256,16]{0,1:T(8,128)S(1)}, f32[256,16]{0,1:T(8,128)}, u32[]{:S(2)}) copy-start(f32[256,16]{0,1:T(8,128)} %param.12) | copy-start | bytes 49156
  0.6 10.2 %copy-start.10 = (f32[256,16]{0,1:T(8,128)S(1)}, f32[256,16]{0,1:T(8,128)}, u32[]{:S(2)}) copy-start(f32[256,16]{0,1:T(8,128)} %param.11) | copy-start | bytes 49156
  3.4 7.5 %copy-start = (bf16[256,1024]{1,0:T(8,128)(2,1)S(1)}, bf16[256,1024]{1,0:T(8,128)(2,1)}, u32[]{:S(2)}) copy-start(bf16[256,1024]{1,0:T(8,128)(2,1)} %q_ref.2) | copy-start | bytes 1572868
  3.5 7.5 %copy-start.1 = (bf16[256,1024]{1,0:T(8,128)(2,1)S(1)}, bf16[256,1024]{1,0:T(8,128)(2,1)}, u32[]{:S(2)}) copy-start(bf16[256,1024]{1,0:T(8,128)(2,1)} %k_ref.2) | copy-start | bytes 1572868
  3.5 7.5 %copy-start.2 = (bf16[256,1024]{1,0:T(8,128)(2,1)S(1)}, bf16[256,1024]{1,0:T(8,128)(2,1)}, u32[]{:S(2)}) copy-start(bf16[256,1024]{1,0:T(8,128)(2,1)} %v_ref.2) | copy-start | bytes 1572868
  3.5 7.5 %copy-start.3 = (bf16[256,1024]{1,0:T(8,128)(2,1)S(1)}, bf16[256,1024]{1,0:T(8,128)(2,1)}, u32[]{:S(2)}) copy-start(bf16[256,1024]{1,0:T(8,128)(2,1)} %o_ref.1) | copy-start | bytes 1572868
  3.5 35.4 %all-to-all-start = ((bf16[32,64,256]{2,1,0:T(8,128)(2,1)}), bf16[32,64,256]{2,1,0:T(8,128)(2,1)S(1)}, u32[]{:S(2)}, u32[]{:S(2)}) async-start(bf16[32,64,256]{2,1,0:T(8,128)(2,1)} %pack_signals.1), calls=%async_computation | async-start | bytes 2097152 | tf_op jit(solution)/shard_map/all_to_all | solution.py:514
  11.0 3.6 %copy-start.8 = (f32[1024]{0:T(1024)S(1)}, f32[1024]{0:T(1024)}, u32[]{:S(2)}) copy-start(f32[1024]{0:T(1024)} %param.13) | copy-start | bytes 12292
  20.8 1.0 %copy-start.4 = (f32[256,1024]{1,0:T(8,128)}, f32[256,1024]{1,0:T(8,128)S(1)}, u32[]{:S(2)}) copy-start(f32[256,1024]{1,0:T(8,128)S(1)} %get-tuple-element.49.part_ref) | copy-start | bytes 3145732
  21.8 1.0 %copy-start.6 = (f32[256,1024]{1,0:T(8,128)}, f32[256,1024]{1,0:T(8,128)S(1)}, u32[]{:S(2)}) copy-start(f32[256,1024]{1,0:T(8,128)S(1)} %get-tuple-element.35.part_ref) | copy-start | bytes 3145732
  22.8 5.3 %collective-permute-start = (bf16[2,128,128]{2,1,0:T(8,128)(2,1)}, bf16[2,128,128]{2,1,0:T(8,128)(2,1)S(1)}, u32[]{:S(2)}, u32[]{:S(2)}) collective-permute-start(bf16[2,128,128]{2,1,0:T(8,128)(2,1)} %get-tuple-element.38), channel_id=1, source_target_pairs={{0,4},{4,0},{8,12},{12,8},{16,20},{20,16},{24,28},{28,24},{1,5},{5... | collective-permute-start | bytes 196616 | tf_op jit(solution)/shard_map/ppermute | solution.py:284
  28.8 13.6 %collective-permute-start.1 = (bf16[128,128]{1,0:T(8,128)(2,1)}, bf16[128,128]{1,0:T(8,128)(2,1)S(1)}, u32[]{:S(2)}, u32[]{:S(2)}) collective-permute-start(bf16[128,128]{1,0:T(8,128)(2,1)} %get-tuple-element.42), channel_id=1, source_target_pairs={{0,8},{4,12},{8,16},{12,20},{16,24},{20,28},{24,0},{28,4},{1,9},{5... | collective-permute-start | bytes 98312 | tf_op jit(solution)/shard_map/ppermute | solution.py:280
  30.7 11.7 %collective-permute-start.2 = (bf16[128,128]{1,0:T(8,128)(2,1)}, bf16[128,128]{1,0:T(8,128)(2,1)S(1)}, u32[]{:S(2)}, u32[]{:S(2)}) collective-permute-start(bf16[128,128]{1,0:T(8,128)(2,1)} %get-tuple-element.43), channel_id=1, source_target_pairs={{0,16},{4,20},{8,24},{12,28},{16,0},{20,4},{24,8},{28,12},{1,17},{... | collective-permute-start | bytes 98312 | tf_op jit(solution)/shard_map/ppermute | solution.py:280
  33.0 9.4 %collective-permute-start.3 = (bf16[128,128]{1,0:T(8,128)(2,1)}, bf16[128,128]{1,0:T(8,128)(2,1)S(1)}, u32[]{:S(2)}, u32[]{:S(2)}) collective-permute-start(bf16[128,128]{1,0:T(8,128)(2,1)} %get-tuple-element.44), channel_id=1, source_target_pairs={{0,24},{4,28},{8,0},{12,4},{16,8},{20,12},{24,16},{28,20},{1,25},{... | collective-permute-start | bytes 98312 | tf_op jit(solution)/shard_map/ppermute | solution.py:280
  42.4 4.8 %copy-start.7 = (f32[256,1024]{1,0:T(8,128)S(1)}, f32[256,1024]{1,0:T(8,128)}, u32[]{:S(2)}) copy-start(f32[256,1024]{1,0:T(8,128)} %copy-done.6) | copy-start | bytes 3145732
  42.4 10.1 %all-to-all-start.1 = ((bf16[8,16,128]{2,1,0:T(8,128)(2,1)}), bf16[8,16,128]{2,1,0:T(8,128)(2,1)S(1)}, u32[]{:S(2)}, u32[]{:S(2)}) async-start(bf16[8,16,128]{2,1,0:T(8,128)(2,1)} %filter_lags.1), calls=%async_computation.1 | async-start | bytes 65536 | tf_op jit(solution)/shard_map/all_to_all | solution.py:538
  47.2 1.7 %copy-start.5 = (f32[256,1024]{1,0:T(8,128)S(1)}, f32[256,1024]{1,0:T(8,128)}, u32[]{:S(2)}) copy-start(f32[256,1024]{1,0:T(8,128)} %copy-done.4) | copy-start | bytes 3145732
